TPU v7x, 32 devices: a whole 2x2x4 slice. The times are simulated.
32 devices in a mesh: groups: 2 (over x), row: 16 (over z, y, core).
Axes of the slice: x: 2, y: 2, z: 4, core: 2. Of those that a mesh axis runs over, the one named last changes fastest.
Arguments:
- object_field: float32 [2, 1280, 32768], P(None, ('groups', 'row')), parts along dimension 1, may hold values from -5 to 5
- probe: bfloat16 [4, 512, 512], P('groups'), parts along dimension 0, may hold values from -5 to 5
- amplitude: bfloat16 [32, 512, 512], P(('groups', 'row')), parts along dimension 0, may hold values from 0.25 to 2.5
- row_offsets: int32 [32], P('groups'), parts along dimension 0, may hold values from 0 to 128
- col_offsets: int32 [32], P('groups'), parts along dimension 0, may hold values from 0 to 32256
- dealing: int32 [32], P('groups'), parts along dimension 0, may hold values from 0 to 15, each once
Outputs:
- object_grad: float32 [2, 1280, 32768], P(None, ('groups', 'row')), parts along dimension 1
- probe_grad: float32 [4, 512, 512], P('groups'), parts along dimension 0
There are 2 independent parts, one for each index of `groups`. A program takes and returns all parts, laid end to end along the dimension named above; each array names one. Nothing has to cross between parts.
Inputs may be any that keep to these rules, and one draw needn't show every extreme that they name: dealing holds every scan position exactly once.
All inputs are finite; a program needn't handle non-finite values.
Results may differ from a plain program's by a relative error of at most 0.012.
The roundings to bfloat16 on the way count: a program that leaves them out, or rounds other values in their place, can miss the bound.
Values may be sent and summed in bfloat16 or wider, within the bound.
No kernel may reach another device: no remote copies, remote signals or barrier semaphores. Data moves between devices by JAX's collectives and lax.ppermute only.
A program may use at most 128 MiB of HBM per device.

v0:
```python
import math

import jax
import jax.numpy as jnp
from jax import lax
from jax.sharding import PartitionSpec as P

MAG_FLOOR = 0.25


def as_sent(x):

    def short(part):
        return part.astype(jnp.bfloat16) if part.dtype == jnp.float32 else part

    return jax.tree.map(short, x)


def dft_tables(order):
    indices = jnp.arange(order, dtype=jnp.int32)
    phases = indices[:, None] * indices[None, :] % order
    angles = phases.astype(jnp.float32) * (2.0 * math.pi / order)
    factor = 1.0 / math.sqrt(order)
    real_part = jnp.cos(angles) * factor
    imag_part = -jnp.sin(angles) * factor
    right_table = jnp.block([[real_part, imag_part], [-imag_part, real_part]]).astype(jnp.bfloat16)
    left_table = jnp.block([[real_part, -imag_part], [imag_part, real_part]]).astype(jnp.bfloat16)
    return (right_table, left_table)


def slot_terms(patch_cells, probe, measured, right_table, left_table):
    order = probe.shape[1]
    patch_wide = patch_cells.astype(jnp.float32)
    probe_wide = probe.astype(jnp.float32)
    wave_real = probe_wide[0] * patch_wide[0] - probe_wide[1] * patch_wide[1]
    wave_imag = probe_wide[0] * patch_wide[1] + probe_wide[1] * patch_wide[0]
    wave_cells = jnp.concatenate([wave_real, wave_imag], axis=1).astype(jnp.bfloat16)
    half_done = jnp.dot(wave_cells, right_table, preferred_element_type=jnp.float32).astype(
        jnp.bfloat16
    )
    stacked = jnp.concatenate([half_done[:, :order], half_done[:, order:]], axis=0)
    far_field = jnp.dot(left_table, stacked, preferred_element_type=jnp.float32)
    far_real = far_field[:order]
    far_imag = far_field[order:]
    magnitude = jnp.sqrt(far_real * far_real + far_imag * far_imag)
    shrink = 1.0 - measured.astype(jnp.float32) / jnp.maximum(magnitude, MAG_FLOOR)
    resid_cells = jnp.concatenate([far_real * shrink, far_imag * shrink], axis=1).astype(
        jnp.bfloat16
    )
    turned = jnp.dot(resid_cells, left_table, preferred_element_type=jnp.float32).astype(
        jnp.bfloat16
    )
    turned_rows = jnp.concatenate([turned[:, :order], turned[:, order:]], axis=0)
    back_field = jnp.dot(right_table, turned_rows, preferred_element_type=jnp.float32)
    back_real = back_field[:order]
    back_imag = back_field[order:]
    object_term = jnp.stack(
        [
            probe_wide[0] * back_real + probe_wide[1] * back_imag,
            probe_wide[0] * back_imag - probe_wide[1] * back_real,
        ]
    )
    probe_term = jnp.stack(
        [
            patch_wide[0] * back_real + patch_wide[1] * back_imag,
            patch_wide[0] * back_imag - patch_wide[1] * back_real,
        ]
    )
    return (object_term, probe_term)


def fetch_windows(tile, starts, order):
    numbers = lax.GatherDimensionNumbers(
        offset_dims=(0, 1, 3), collapsed_slice_dims=(), start_index_map=(2,)
    )
    return lax.gather(tile, starts[:, None], numbers, (tile.shape[0], tile.shape[1], order))


def add_windows(total, starts, updates):
    numbers = lax.ScatterDimensionNumbers(
        update_window_dims=(0, 1, 3), inserted_window_dims=(), scatter_dims_to_operand_dims=(2,)
    )
    return lax.scatter_add(total, starts[:, None], updates, numbers)


def body(object_field, probe, amplitude, row_offsets, col_offsets, dealing):
    order = probe.shape[1]
    device_count = lax.axis_size("row")
    own_index = lax.axis_index("row")
    slot_count = amplitude.shape[0]
    tile_rows = object_field.shape[1]
    tile_cols = object_field.shape[2]
    total_rows = tile_rows * device_count
    total_slots = dealing.shape[0]
    right_table, left_table = dft_tables(order)
    slot_rows = row_offsets[dealing]
    slot_cols = col_offsets[dealing]
    own_rows = lax.dynamic_slice_in_dim(slot_rows, own_index * slot_count, slot_count)
    tile_low = object_field.astype(jnp.bfloat16)
    pieces = fetch_windows(tile_low, slot_cols, order)
    strips = lax.all_to_all(as_sent(pieces), "row", split_axis=2, concat_axis=1, tiled=True).astype(
        pieces.dtype
    )
    object_grad = jnp.zeros((2, tile_rows, tile_cols), jnp.float32)
    probe_total = jnp.zeros((2, order, order), jnp.float32)
    first_row = own_rows[0]
    patch_cells = lax.dynamic_slice(strips[:, :, 0, :], (0, first_row, 0), (2, order, order))
    object_term, probe_term = slot_terms(patch_cells, probe, amplitude[0], right_table, left_table)
    empty_strip = jnp.zeros((2, total_rows, order), jnp.float32)
    filled_strip = lax.dynamic_update_slice(empty_strip, object_term, (0, first_row, 0))
    back_strips = [filled_strip]
    probe_total = probe_total + lax.psum(probe_term, "row")
    outgoing = jnp.stack(back_strips, axis=2)
    arrived = lax.all_to_all(outgoing, "row", split_axis=1, concat_axis=2, tiled=True)
    object_grad = add_windows(object_grad, slot_cols, arrived)
    probe_grad = probe_total * (1.0 / total_slots)
    return (object_grad, probe_grad)


def solution(mesh):
    return jax.shard_map(
        body,
        mesh=mesh,
        in_specs=(
            P(None, ("groups", "row"), None),
            P("groups", None, None),
            P(("groups", "row"), None, None),
            P("groups"),
            P("groups"),
            P("groups"),
        ),
        out_specs=(P(None, ("groups", "row"), None), P("groups", None, None)),
        check_vma=False,
    )
```

profile of v0, /device:TPU:15, one launch (start us, length us, event | category | flops | bytes accessed | tf_op | source)
XLA Modules:
  0.0 392.7 jit_solution(3644933805374672318)
XLA Ops:
  8.5 6.9 %convert_element_type.44 = bf16[2,40,32768]{2,1,0:T(8,128)(2,1)} convert(f32[2,40,32768]{2,1,0:T(8,128)} %param.6) | non-fusion elementwise | flops 2621440 | bytes 15728640 | tf_op jit(solution)/shard_map/convert_element_type | solution.py:99
  15.4 33.3 %copy.15 = bf16[2,40,32768]{1,0,2:T(2,128)(2,1)} copy(bf16[2,40,32768]{2,1,0:T(8,128)(2,1)} %convert_element_type.44) | data formatting | bytes 10485760 | tf_op jit(solution)/shard_map/convert_element_type | solution.py:99
  48.8 15.7 %gather_fusion.1 = bf16[16,2,40,512]{2,1,3,0:T(2,128)(2,1)} fusion(bf16[2,40,32768]{1,0,2:T(2,128)(2,1)} %copy.15, s32[1024]{0:T(1024)S(1)} %pad_clamp_fusion), kind=kCustom, calls=%fused_computation.1 | custom fusion | bytes 2621504 | tf_op jit(solution)/shard_map/gather | solution.py:76
  64.5 10.4 %copy.16 = bf16[2,40,16,512]{3,1,0,2:T(8,128)(2,1)} copy(bf16[2,40,16,512]{1,0,3,2:T(2,128)(2,1)} %bitcast.76) | data formatting | bytes 2621440 | tf_op jit(solution)/shard_map/gather | solution.py:76
  74.9 6.7 %all-to-all-start = ((bf16[2,40,16,512]{3,1,0,2:T(8,128)(2,1)}), bf16[2,40,16,512]{3,1,0,2:T(8,128)(2,1)S(1)}, u32[]{:S(2)}, u32[]{:S(2)}) async-start(bf16[2,40,16,512]{3,1,0,2:T(8,128)(2,1)} %copy.16), calls=%async_computation | async-start | bytes 2621440 | tf_op jit(solution)/shard_map/all_to_all | solution.py:101
  84.1 1.5 convert_element_type.42
  85.7 2.1 copy.18
  88.4 4.7 %fusion.23 = bf16[512,512]{1,0:T(8,128)(2,1)} fusion(), kind=kLoop, calls=%fused_computation.58 | loop fusion | flops 4456448 | bytes 524288 | tf_op jit(solution)/shard_map/convert.16
  93.0 5.3 %negate_convert_fusion = (bf16[512,512]{1,0:T(8,128)(2,1)}, bf16[512,512]{1,0:T(8,128)(2,1)}) fusion(), kind=kLoop, calls=%fused_computation.52 | loop fusion | flops 5242880 | bytes 1048576 | tf_op jit(solution)/shard_map/convert.13
  98.4 13.8 %all-to-all-done = bf16[2,40,16,512]{3,1,0,2:T(8,128)(2,1)S(1)} async-done(((bf16[2,40,16,512]{3,1,0,2:T(8,128)(2,1)}), bf16[2,40,16,512]{3,1,0,2:T(8,128)(2,1)S(1)}, u32[]{:S(2)}, u32[]{:S(2)}) %all-to-all-start) | async-done | bytes 1310752 | tf_op jit(solution)/shard_map/all_to_all | solution.py:101
  119.9 2.1 add_bitcast_fusion
  122.2 2.2 broadcast_in_dim.19
  124.3 2.9 copy_dynamic-update-slice_fusion
  127.3 4.9 %all-to-all-start.1 = ((f32[2,640,1,512]{3,0,2,1:T(2,128)}), f32[2,640,1,512]{3,0,2,1:T(2,128)S(1)}, u32[]{:S(2)}, u32[]{:S(2)}) async-start(f32[2,640,1,512]{3,0,2,1:T(2,128)} %copy_dynamic-update-slice_fusion), calls=%async_computation.1 | async-start | bytes 5242880 | tf_op jit(solution)/shard_map/all_to_all | solution.py:114
  132.2 3.0 pad_maximum_fusion.4
  135.2 128.7 %all-reduce.2.cloned.1.call-done = f32[2,512,512]{2,1,0:T(8,128)} async-done(((f32[2,512,512]{2,1,0:T(8,128)}), f32[2,512,512]{2,1,0:T(8,128)}) %all-reduce.2.cloned.1.call-update) | async-done | bytes 2097168 | tf_op jit(solution)/shard_map/psum | solution.py:112
  263.9 3.1 broadcast_multiply_fusion
  267.1 2.0 copy.20
  269.1 5.0 %broadcast_in_dim.16 = f32[2,40,32768]{2,1,0:T(8,128)} broadcast(f32[]{:T(128)} %constant.12.clone.1), dimensions={} | broadcast | bytes 10485764 | tf_op jit(solution)/shard_map/broadcast_in_dim | solution.py:104
  274.1 111.7 %while.1 = (s32[]{:T(128)}, f32[2,40,32768]{2,1,0:T(8,128)}, s32[16]{0:T(128)S(1)}, f32[16,2,40,512]{3,2,0,1:T(8,128)}, s32[]{:T(128)}, /*index=5*/s32[3]{0:T(128)S(1)}, s32[1]{0:T(128)}, s32[]{:T(128)}) while((s32[]{:T(128)}, f32[2,40,32768]{2,1,0:T(8,128)}, s32[16]{0:T(128)S(1)}, f32[16,2,40,512]{3,2,0,1:T(8,128)}, s32[]{:T(128)}, ...), condition=%wide.while_cond, body=%wide.while_body.sunk | while | flops 81939 | bytes 819331 | solution.py:83
  274.7 1.3 and_reduce_fusion.2
  276.1 2.4 add_select_fusion.3
  278.4 2.2 dynamic-update-slice.3
  281.3 1.3 and_reduce_fusion.2
  282.7 2.4 add_select_fusion.3
  285.1 2.7 dynamic-update-slice.3
  288.4 1.3 and_reduce_fusion.2
  289.7 2.4 add_select_fusion.3
  292.1 2.7 dynamic-update-slice.3
  295.4 1.3 and_reduce_fusion.2
  296.7 2.4 add_select_fusion.3
  299.1 2.7 dynamic-update-slice.3
  302.4 1.3 and_reduce_fusion.2
  303.8 2.4 add_select_fusion.3
  306.2 2.7 dynamic-update-slice.3
  309.4 1.3 and_reduce_fusion.2
  310.8 2.4 add_select_fusion.3
  313.2 2.7 dynamic-update-slice.3
  316.5 1.3 and_reduce_fusion.2
  317.8 2.4 add_select_fusion.3
  320.2 2.7 dynamic-update-slice.3
  323.5 1.3 and_reduce_fusion.2
  324.9 2.4 add_select_fusion.3
  327.2 2.7 dynamic-update-slice.3
  330.5 1.3 and_reduce_fusion.2
  331.9 2.4 add_select_fusion.3
  334.3 2.7 dynamic-update-slice.3
  337.6 1.3 and_reduce_fusion.2
  338.9 2.4 add_select_fusion.3
  341.3 2.7 dynamic-update-slice.3
  344.6 1.3 and_reduce_fusion.2
  345.9 2.4 add_select_fusion.3
  348.3 2.7 dynamic-update-slice.3
  353.0 2.4 add_select_fusion.3
  355.4 2.7 dynamic-update-slice.3
  360.0 2.4 add_select_fusion.3
  362.4 2.7 dynamic-update-slice.3
  367.0 2.4 add_select_fusion.3
  369.4 2.7 dynamic-update-slice.3
  372.7 1.3 and_reduce_fusion.2
  374.1 2.4 add_select_fusion.3
  376.4 2.7 dynamic-update-slice.3
  381.1 2.4 add_select_fusion.3
  383.5 2.3 dynamic-update-slice.3
  (56 shorter events, 26.1 us)
Async XLA Ops:
  7.2 0.7 copy-start
  74.9 6.7 %copy-start.2 = (s32[16]{0:T(128)S(1)}, s32[16]{0:T(128)}, u32[]{:S(2)}) copy-start(s32[16]{0:T(128)} %param.9) | copy-start | bytes 196
  74.9 37.3 %all-to-all-start = ((bf16[2,40,16,512]{3,1,0,2:T(8,128)(2,1)}), bf16[2,40,16,512]{3,1,0,2:T(8,128)(2,1)S(1)}, u32[]{:S(2)}, u32[]{:S(2)}) async-start(bf16[2,40,16,512]{3,1,0,2:T(8,128)(2,1)} %copy.16), calls=%async_computation | async-start | bytes 2621440 | tf_op jit(solution)/shard_map/all_to_all | solution.py:101
  112.6 1.0 copy-start.4
  112.6 1.2 copy-start.5
  112.6 1.3 copy-start.6
  115.3 1.3 copy-start.3
  127.3 139.8 %all-to-all-start.1 = ((f32[2,640,1,512]{3,0,2,1:T(2,128)}), f32[2,640,1,512]{3,0,2,1:T(2,128)S(1)}, u32[]{:S(2)}, u32[]{:S(2)}) async-start(f32[2,640,1,512]{3,0,2,1:T(2,128)} %copy_dynamic-update-slice_fusion), calls=%async_computation.1 | async-start | bytes 5242880 | tf_op jit(solution)/shard_map/all_to_all | solution.py:114
  132.1 131.8 %all-reduce.2.cloned.1.call-start = ((), (), s32[]{:S(2)}) async-start(), calls=%async_computation.2 | async-start | bytes 4194304 | tf_op jit(solution)/shard_map/psum | solution.py:112
  269.1 5.0 %copy-start.7 = (s32[3]{0:T(128)S(1)}, s32[3]{0:T(128)}, u32[]{:S(2)}) copy-start(s32[3]{0:T(128)} %constant.167) | copy-start | bytes 40
  274.1 111.7 %copy-start.1 = (s32[16]{0:T(128)S(1)}, s32[16]{0:T(128)}, u32[]{:S(2)}) copy-start(s32[16]{0:T(128)} %param.10) | copy-start | bytes 196
Sparse Core Ops, SparseCore 0:
  137.1 126.8 all-reduce.1
where the time goes:
time: 400 us; the launch traced here: 393 us
  waiting for transfers between devices  143 us (36%)
  local copies, waits for them, and re-layouts  129 us (32%)
  other arithmetic  88.7 us (22%)
  between operations  16.1 us (4%)
  starting transfers between devices  11.6 us (3%)
  matrix products  5.07 us (1%)
    psum x1, waiting for transfers between devices, body(): probe_total = probe_total + lax.psum(probe_term, 'row')  129 us
    scatter-add x32, other arithmetic  59.5 us
    scatter-add x32, local copies, waits for them, and re-layouts  52 us
    convert_element_type x1, local copies, waits for them, and re-layouts, body(): tile_low = object_field.astype(jnp.bfloat16)  33.3 us
    gather x2, local copies, waits for them, and re-layouts, fetch_windows(): lax.gather(tile, starts[:, None], numbers, (tile.shape[0], tile.shape[1],...  26.1 us
    all_to_all x1, waiting for transfers between devices, body(): lax.all_to_all(as_sent(pieces), 'row', split_axis=2, concat_axis=1, tiled...  13.8 us
    another operation x4, other arithmetic  11.2 us
  transfers between devices with their start and end apart: 3, of which 2 were waited for; matrix products, arithmetic and copies ran while one was open for 5% of the time, Pallas kernels for 0%

commit v1 on v0

v1 whole, which is shorter than its diff:
```python
import functools
import math

import jax
import jax.numpy as jnp
import numpy as np
from jax import lax
from jax.experimental import pallas as pl
from jax.experimental.pallas import tpu as pltpu
from jax.sharding import PartitionSpec as P

MAG_FLOOR = 0.25
LANES = 128
SUBLANES = 8
SMEM = pl.BlockSpec(memory_space=pltpu.SMEM)
VMEM = pl.BlockSpec(memory_space=pltpu.VMEM)
ANY = pl.BlockSpec(memory_space=pl.ANY)


def dft_tables(order):
    indices = np.arange(order, dtype=np.int32)
    phases = indices[:, None] * indices[None, :] % order
    angles = phases.astype(np.float32) * np.float32(2.0 * math.pi / order)
    factor = np.float32(1.0 / math.sqrt(order))
    real_part = np.cos(angles) * factor
    imag_part = -np.sin(angles) * factor
    right_table = np.block([[real_part, imag_part], [-imag_part, real_part]])
    left_table = np.block([[real_part, -imag_part], [imag_part, real_part]])
    return right_table.astype(jnp.bfloat16), left_table.astype(jnp.bfloat16)


def window_start(column, order, tile_cols):
    span = order + LANES
    base = jnp.minimum(column // LANES, (tile_cols - span) // LANES) * LANES
    return pl.multiple_of(base, LANES), column - base


def rows_from(ref, start, count):
    aligned = pl.multiple_of(start // SUBLANES * SUBLANES, SUBLANES)
    rest = start - aligned
    width = ref.shape[-1]
    blocks = ref[pl.ds(aligned, count + SUBLANES), :].reshape(-1, SUBLANES, width)
    turned = pltpu.roll(blocks, lax.rem(SUBLANES - rest, SUBLANES), 1)
    sub = lax.broadcasted_iota(jnp.int32, (1, SUBLANES, width), 1)
    picked = jnp.where(sub < SUBLANES - rest, turned[:-1], turned[1:])
    return picked.reshape(count, width)


def fetch_kernel(order, dealing, cols, tile, out, held, sems):
    slots, tile_rows = out.shape[0], out.shape[1]
    tile_cols = tile.shape[2]
    span = order + LANES

    def copy(slot):
        base, _ = window_start(cols[dealing[slot]], order, tile_cols)
        return pltpu.make_async_copy(tile.at[:, :, pl.ds(base, span)], held.at[slot], sems.at[slot])

    @pl.loop(0, slots)
    def _(slot):
        copy(slot).start()

    lane = lax.broadcasted_iota(jnp.int32, (tile_rows, LANES), 1)

    @pl.loop(0, slots)
    def _(slot):
        copy(slot).wait()
        _, offset = window_start(cols[dealing[slot]], order, tile_cols)
        shift = lax.rem(LANES - lax.rem(offset, LANES), LANES)
        for part in range(2):
            turned = [
                pltpu.roll(held[slot, part, :, b * LANES : (b + 1) * LANES], shift, 1)
                for b in range(span // LANES)
            ]
            for b in range(order // LANES):
                first = part * order + b * LANES
                cells = jnp.where(lane < LANES - offset, turned[b], turned[b + 1])
                out[slot, :, first : first + LANES] = cells.astype(out.dtype)


def fetch_windows(tile, dealing, cols, order):
    slots, tile_rows, tile_cols = dealing.shape[0], tile.shape[1], tile.shape[2]
    span = order + LANES

    return pl.pallas_call(
        functools.partial(fetch_kernel, order),
        out_shape=jax.ShapeDtypeStruct((slots, tile_rows, 2 * order), jnp.bfloat16),
        in_specs=[SMEM, SMEM, ANY],
        out_specs=VMEM,
        scratch_shapes=[
            pltpu.VMEM((slots, 2, tile_rows, span), jnp.float32),
            pltpu.SemaphoreType.DMA((slots,)),
        ],
        compiler_params=pltpu.CompilerParams(vmem_limit_bytes=24 * 2**20),
        cost_estimate=pl.CostEstimate(flops=0, bytes_accessed=6 * 2**20, transcendentals=0),
        name="fetch",
    )(dealing, cols, tile)


def slot_kernel(
    dealing, rows, cells, probe, measured, right, left,
    terms, kept, sent, empty,
    wide, patch, wave, half, resid, turned, padded, mine, zeros, sem,
):
    order = probe.shape[1]
    total_rows = cells.shape[0]
    reach = total_rows - order
    me = lax.axis_index("row")
    first_row = rows[dealing[me]]
    step = 64
    tile = 256

    zeros[...] = jnp.zeros_like(zeros)
    fills = []
    for b in range(empty.shape[2] // zeros.shape[2]):
        fill = pltpu.make_async_copy(
            zeros, empty.at[:, :, b * zeros.shape[2] : (b + 1) * zeros.shape[2]], sem.at[b]
        )
        fill.start()
        fills.append(fill)

    wide[0:total_rows, :] = cells[...].astype(jnp.float32)
    wide[total_rows:, :] = jnp.zeros((SUBLANES, 2 * order), jnp.float32)
    padded[0:reach, :] = jnp.zeros((reach, 2 * order), jnp.float32)
    padded[reach + order :, :] = jnp.zeros((reach + SUBLANES, 2 * order), jnp.float32)

    @pl.loop(0, order // step)
    def _(i):
        place = pl.ds(pl.multiple_of(i * step, step), step)
        found = rows_from(wide, first_row + i * step, step)
        patch[place, :] = found.astype(patch.dtype)
        real, imag = found[:, :order], found[:, order:]
        probe_real = probe[0, place, :].astype(jnp.float32)
        probe_imag = probe[1, place, :].astype(jnp.float32)
        wave[place, :order] = (probe_real * real - probe_imag * imag).astype(wave.dtype)
        wave[place, order:] = (probe_real * imag + probe_imag * real).astype(wave.dtype)

    def dot(a, b):
        return jnp.dot(a, b, preferred_element_type=jnp.float32)

    for first in range(0, order, tile):
        here = slice(first, first + tile)
        there = slice(order + first, order + first + tile)
        half[:order, here] = dot(wave[...], right[:, here]).astype(half.dtype)
        half[order:, here] = dot(wave[...], right[:, there]).astype(half.dtype)
    for first in range(0, order, tile):
        here = slice(first, first + tile)
        there = slice(order + first, order + first + tile)
        for top in range(0, order, tile):
            line = slice(top, top + tile)
            real = dot(left[line, :], half[:, here])
            imag = dot(left[order + top : order + top + tile, :], half[:, here])
            inverse = jnp.minimum(lax.rsqrt(real * real + imag * imag), 1.0 / MAG_FLOOR)
            shrink = 1.0 - measured[0, line, here].astype(jnp.float32) * inverse
            resid[line, here] = (real * shrink).astype(resid.dtype)
            resid[line, there] = (imag * shrink).astype(resid.dtype)
    for first in range(0, order, tile):
        here = slice(first, first + tile)
        there = slice(order + first, order + first + tile)
        turned[:order, here] = dot(resid[...], left[:, here]).astype(turned.dtype)
        turned[order:, here] = dot(resid[...], left[:, there]).astype(turned.dtype)
    for first in range(0, order, tile):
        here = slice(first, first + tile)
        there = slice(order + first, order + first + tile)
        for top in range(0, order, tile):
            line = slice(top, top + tile)
            real = dot(right[line, :], turned[:, here])
            imag = dot(right[order + top : order + top + tile, :], turned[:, here])
            probe_real = probe[0, line, here].astype(jnp.float32)
            probe_imag = probe[1, line, here].astype(jnp.float32)
            down = slice(reach + top, reach + top + tile)
            padded[down, here] = probe_real * real + probe_imag * imag
            padded[down, there] = probe_real * imag - probe_imag * real
            patch_real = patch[line, here].astype(jnp.float32)
            patch_imag = patch[line, there].astype(jnp.float32)
            mine[line, here] = patch_real * real + patch_imag * imag
            mine[line, there] = patch_real * imag - patch_imag * real

    @pl.loop(0, total_rows // step)
    def _(i):
        place = pl.ds(pl.multiple_of(i * step, step), step)
        terms[place, :] = rows_from(padded, reach - first_row + i * step, step).astype(terms.dtype)

    count = kept.shape[0]
    side = lax.rem(me, 2)
    kept[...] = mine[pl.ds(pl.multiple_of(side * count, count), count), :]
    sent[...] = mine[pl.ds(pl.multiple_of((1 - side) * count, count), count), :].astype(sent.dtype)
    for fill in fills:
        fill.wait()


def slot_terms(cells, probe, measured, dealing, rows, tile_rows, tile_cols):
    order = probe.shape[1]
    total_rows = cells.shape[0]
    right, left = dft_tables(order)
    wide_cols = 2 * order
    fill_cols = 2048
    bf16, f32 = jnp.bfloat16, jnp.float32
    return pl.pallas_call(
        slot_kernel,
        out_shape=(
            jax.ShapeDtypeStruct((total_rows, wide_cols), bf16),
            jax.ShapeDtypeStruct((order // 2, wide_cols), f32),
            jax.ShapeDtypeStruct((order // 2, wide_cols), bf16),
            jax.ShapeDtypeStruct((2, tile_rows, tile_cols), f32),
        ),
        in_specs=[SMEM, SMEM, VMEM, VMEM, VMEM, VMEM, VMEM],
        out_specs=(VMEM, VMEM, VMEM, ANY),
        scratch_shapes=[
            pltpu.VMEM((total_rows + SUBLANES, wide_cols), f32),
            pltpu.VMEM((order, wide_cols), bf16),
            pltpu.VMEM((order, wide_cols), bf16),
            pltpu.VMEM((wide_cols, order), bf16),
            pltpu.VMEM((order, wide_cols), bf16),
            pltpu.VMEM((wide_cols, order), bf16),
            pltpu.VMEM((2 * total_rows - order + SUBLANES, wide_cols), f32),
            pltpu.VMEM((order, wide_cols), f32),
            pltpu.VMEM((2, tile_rows, fill_cols), f32),
            pltpu.SemaphoreType.DMA((tile_cols // fill_cols,)),
        ],
        compiler_params=pltpu.CompilerParams(vmem_limit_bytes=40 * 2**20),
        cost_estimate=pl.CostEstimate(
            flops=8 * 2 * order**3 * 2, bytes_accessed=20 * 2**20, transcendentals=order * order
        ),
        name="slot",
    )(dealing, rows, cells, probe, measured, jnp.asarray(right), jnp.asarray(left))


def block_places(dealing, cols, order, tile_cols):
    base, _ = window_start(cols[dealing], order, tile_cols)
    count = (order + LANES) // LANES
    blocks = (base[:, None] // LANES + jnp.arange(count, dtype=jnp.int32)[None, :]).reshape(-1)
    same = blocks[:, None] == blocks[None, :]
    return blocks, jnp.argmax(same, axis=1).astype(jnp.int32)


def place_kernel(order, dealing, cols, blocks, owners, terms, empty, out, totals, sems):
    del empty
    slots, tile_rows = terms.shape[0], terms.shape[1]
    tile_cols = out.shape[2]
    count = (order + LANES) // LANES
    totals[...] = jnp.zeros_like(totals)
    lane = lax.broadcasted_iota(jnp.int32, (tile_rows, LANES), 1)

    @pl.loop(0, slots)
    def _(slot):
        _, offset = window_start(cols[dealing[slot]], order, tile_cols)
        shift = lax.rem(offset, LANES)
        for part in range(2):
            turned = []
            for b in range(count - 1):
                first = part * order + b * LANES
                turned.append(pltpu.roll(terms[slot, :, first : first + LANES].astype(jnp.float32), shift, 1))
            nothing = jnp.zeros_like(turned[0])
            for b in range(count):
                before = turned[b - 1] if b else nothing
                after = turned[b] if b < count - 1 else nothing
                owner = owners[slot * count + b]
                totals[owner, part] += jnp.where(lane < offset, before, after)

    def copy(number):
        place = pl.multiple_of(blocks[number] * LANES, LANES)
        return pltpu.make_async_copy(totals.at[number], out.at[:, :, pl.ds(place, LANES)], sems.at[number])

    @pl.loop(0, slots * count)
    def _(number):
        @pl.when(owners[number] == number)
        def _():
            copy(number).start()

    @pl.loop(0, slots * count)
    def _(number):
        @pl.when(owners[number] == number)
        def _():
            copy(number).wait()


def place_windows(terms, empty, dealing, cols, order):

    slots, tile_rows = terms.shape[0], terms.shape[1]
    tile_cols = empty.shape[2]
    count = (order + LANES) // LANES
    blocks, owners = block_places(dealing, cols, order, tile_cols)
    return pl.pallas_call(
        functools.partial(place_kernel, order),
        out_shape=jax.ShapeDtypeStruct(empty.shape, empty.dtype),
        in_specs=[SMEM, SMEM, SMEM, SMEM, VMEM, ANY],
        out_specs=ANY,
        scratch_shapes=[
            pltpu.VMEM((slots * count, 2, tile_rows, LANES), jnp.float32),
            pltpu.SemaphoreType.DMA((slots * count,)),
        ],
        input_output_aliases={5: 0},
        compiler_params=pltpu.CompilerParams(vmem_limit_bytes=24 * 2**20),
        cost_estimate=pl.CostEstimate(flops=0, bytes_accessed=6 * 2**20, transcendentals=0),
        name="place",
    )(dealing, cols, blocks, owners, terms, empty)


def strides(devices):
    steps, stride = [], 1
    while stride < devices:
        radix = 4 if len(steps) >= 2 and (devices // stride) % 4 == 0 else 2
        steps.append((stride, radix))
        stride *= radix
    return steps


def turn(x, stride, radix, distance, devices):
    pairs = []
    for d in range(devices):
        digit = d // stride % radix
        pairs.append((d, d + ((digit + distance) % radix - digit) * stride))
    return lax.ppermute(x, "row", pairs)


def sum_probe(kept, sent, devices, scale):
    me = lax.axis_index("row")
    steps = strides(devices)
    total = kept + turn(sent, 1, 2, 1, devices).astype(jnp.float32)
    for stride, radix in steps[1:]:
        digit = me // stride % radix
        count = total.shape[0] // radix
        own = lax.dynamic_slice_in_dim(total, digit * count, count)
        for distance in range(1, radix):
            other = lax.rem(digit + distance, radix)
            share = lax.dynamic_slice_in_dim(total, other * count, count).astype(jnp.bfloat16)
            own = own + turn(share, stride, radix, distance, devices).astype(jnp.float32)
        total = own
    whole = (total * scale).astype(jnp.bfloat16)
    for stride, radix in reversed(steps):
        digit = me // stride % radix
        shares = [whole] + [turn(whole, stride, radix, distance, devices) for distance in range(1, radix)]
        order = [lax.rem(digit - k + radix, radix) for k in range(radix)]
        rows = []
        for k in range(radix):
            piece = shares[0]
            for d in range(1, radix):
                piece = jnp.where(order[k] == d, shares[d], piece)
            rows.append(piece)
        whole = jnp.concatenate(rows, axis=0)
    return whole


def body(object_field, probe, amplitude, row_offsets, col_offsets, dealing):
    order = probe.shape[1]
    devices = lax.axis_size("row")
    own_rows, tile_cols = object_field.shape[1], object_field.shape[2]
    tile_rows = -(-own_rows // SUBLANES) * SUBLANES
    spare = tile_rows - own_rows
    if spare:
        object_field = jnp.pad(object_field, ((0, 0), (0, spare), (0, 0)))
    pieces = fetch_windows(object_field, dealing, col_offsets, order)
    strips = lax.all_to_all(pieces, "row", split_axis=0, concat_axis=0, tiled=True)
    cells = strips[:, :own_rows].reshape(devices * own_rows, 2 * order)
    terms, kept, sent, empty = slot_terms(
        cells, probe, amplitude, dealing, row_offsets, tile_rows, tile_cols
    )
    outgoing = terms.reshape(devices, own_rows, 2 * order)
    if spare:
        outgoing = jnp.pad(outgoing, ((0, 0), (0, spare), (0, 0)))
    arrived = lax.all_to_all(outgoing, "row", split_axis=0, concat_axis=0, tiled=True)
    whole = sum_probe(kept, sent, devices, 1.0 / dealing.shape[0]).astype(jnp.float32)
    probe_grad = jnp.stack([whole[:, :order], whole[:, order:]])
    object_grad = place_windows(arrived, empty, dealing, col_offsets, order)
    if spare:
        object_grad = object_grad[:, :own_rows]
    return (object_grad, probe_grad)


def solution(mesh):
    return jax.shard_map(
        body,
        mesh=mesh,
        in_specs=(
            P(None, ("groups", "row"), None),
            P("groups", None, None),
            P(("groups", "row"), None, None),
            P("groups"),
            P("groups"),
            P("groups"),
        ),
        out_specs=(P(None, ("groups", "row"), None), P("groups", None, None)),
        check_vma=False,
    )
```

time: 400 us -> 119 us (0.30); the launches traced: 393 us -> 119 us
  local copies, waits for them, and re-layouts: 129 us -> 6.35 us
  waiting for transfers between devices: 143 us -> 35.3 us
  other arithmetic: 88.7 us -> 3.23 us
  blocking collectives: 0 us -> 36.9 us
  Pallas kernels: 0 us -> 16.8 us
  between operations: 16.1 us -> 0.87 us
  starting transfers between devices: 11.6 us -> 19.2 us
  matrix products: 5.07 us -> 0 us
    psum x1 -> x0, waiting for transfers between devices: 129 us -> none  [body(): probe_total = probe_total + lax.psum(probe_term, 'row')]
    scatter-add x32 -> x0, other arithmetic: 59.5 us -> none
    scatter-add x32 -> x0, local copies, waits for them, and re-layouts: 52 us -> none
    all_to_all x0 -> x1, blocking collectives: none -> 36.9 us  [body(): lax.all_to_all(pieces, 'row', split_axis=0, concat_axis=0, tiled=True)]
    convert_element_type x1 -> x2, local copies, waits for them, and re-layouts: 33.3 us -> 0.07 us  [sum_probe(): lax.dynamic_slice_in_dim(total, other * count, count).astype(jnp.bfloat16)]
    gather x4 -> x1, local copies, waits for them, and re-layouts: 27.4 us -> 0.66 us  [block_places(): base, _ = window_start(cols[dealing], order, tile_cols)]
    ppermute x0 -> x10, waiting for transfers between devices: none -> 25.2 us  [turn(): return lax.ppermute(x, 'row', pairs)]
    pallas_call x0 -> x3, Pallas kernels: none -> 16.8 us  [the longest x1 8.38 us: slot_terms(): pl.pallas_call(slot_kernel, out_shape=(jax.ShapeDtypeStruct((total_rows,...]
  transfers between devices with their start and end apart: 3 -> 11, of which waited for: 2 -> 7; matrix products, arithmetic and copies ran while one was open for 5% -> 3% of each run, Pallas kernels for 0% -> 0%
where the time goes in v1:
time: 119 us
  blocking collectives  36.9 us (31%)
  waiting for transfers between devices  35.3 us (30%)
  starting transfers between devices  19.2 us (16%)
  Pallas kernels  16.8 us (14%)
  local copies, waits for them, and re-layouts  6.35 us (5%)
  other arithmetic  3.23 us (3%)
    all_to_all x1, blocking collectives, body(): lax.all_to_all(pieces, 'row', split_axis=0, concat_axis=0, tiled=True)  36.9 us
    ppermute x10, waiting for transfers between devices, turn(): return lax.ppermute(x, 'row', pairs)  25.2 us
    ppermute x10, starting transfers between devices, turn(): return lax.ppermute(x, 'row', pairs)  11.5 us
    all_to_all x1, waiting for transfers between devices, body(): lax.all_to_all(outgoing, 'row', split_axis=0, concat_axis=0, tiled=True)  10.1 us
    pallas_call x1, Pallas kernels, slot_terms(): pl.pallas_call(slot_kernel, out_shape=(jax.ShapeDtypeStruct((total_rows,...  8.38 us
    all_to_all x1, starting transfers between devices, body(): lax.all_to_all(outgoing, 'row', split_axis=0, concat_axis=0, tiled=True)  7.72 us
    unnamed x20, local copies, waits for them, and re-layouts  5.32 us
    pallas_call x1, Pallas kernels, place_windows(): pl.pallas_call(functools.partial(place_kernel, order), out_shape=jax.Shap...  5.12 us
  transfers between devices with their start and end apart: 11, of which 7 were waited for; matrix products, arithmetic and copies ran while one was open for 3% of the time, Pallas kernels for 0%

profile of v1, /device:TPU:15, one launch (start us, length us, event | category | flops | bytes accessed | tf_op | source)
XLA Modules:
  0.0 118.7 jit_solution(7821597992364067227)
XLA Ops:
  0.6 0.0 copy-start
  0.6 0.6 copy-done
  1.3 0.0 copy-start.2
  1.3 4.0 %copy-done.2 = f32[2,40,32768]{2,1,0:T(8,128)S(1)} copy-done((f32[2,40,32768]{2,1,0:T(8,128)S(1)}, f32[2,40,32768]{2,1,0:T(8,128)}, u32[]{:S(2)}) %copy-start.2) | copy-done | bytes 10485784
  5.3 0.0 copy-start.3
  5.3 0.7 copy-done.3
  5.9 0.0 copy-start.8
  5.9 0.0 copy-start.9
  5.9 3.3 %fetch.1 = bf16[16,40,1024]{2,1,0:T(8,128)(2,1)S(1)} custom-call(s32[16]{0:T(128)S(1)} %copy-done.3, s32[16]{0:T(128)S(1)} %copy-done, f32[2,40,32768]{2,1,0:T(8,128)S(1)} %copy-done.2), custom_call_target="tpu_custom_call" | custom-call | bytes 6291456 | tf_op jit(solution)/shard_map/fetch/pallas_call | solution.py:84
  9.3 0.0 copy-start.4
  9.3 0.0 copy-start.5
  9.3 0.0 copy-start.6
  9.3 0.0 copy-start.7
  9.3 36.9 %all_to_all.10 = bf16[16,40,1024]{2,1,0:T(8,128)(2,1)S(1)} all-to-all(bf16[16,40,1024]{2,1,0:T(8,128)(2,1)S(1)} %fetch.1), channel_id=1, replica_groups=mesh['groups'=2,'row'=16] {'row'}, dimensions={0} | all-to-all | bytes 2621440 | tf_op jit(solution)/shard_map/all_to_all | solution.py:353
  46.3 0.0 copy-done.8
  46.3 0.0 copy-done.9
  46.3 0.0 copy-done.4
  46.3 0.0 copy-done.5
  46.3 0.0 copy-done.6
  46.3 0.0 copy-done.7
  46.3 8.4 %slot.1 = (bf16[640,1024]{1,0:T(8,128)(2,1)}, f32[256,1024]{1,0:T(8,128)S(1)}, bf16[256,1024]{1,0:T(8,128)(2,1)S(1)}, f32[2,40,32768]{2,1,0:T(8,128)}) custom-call(s32[16]{0:T(128)S(1)} %copy-done.4, s32[16]{0:T(128)S(1)} %copy-done.7, bf16[640,1024]{1,0:T(8,128)(2,1)S(1)} %bitcast.6, bf16[2,512,512]{2,1,0:T(8,128)(2,1)S(1)} %copy-done.5, ...), custom_call_target="tpu_custom_call" | custom-call | flops 4294967296 | bytes 20971520 | tf_op jit(solution)/shard_map/slot/pallas_call | solution.py:198
  54.7 0.3 collective-permute-start
  55.0 1.7 %collective-permute-done = bf16[256,1024]{1,0:T(8,128)(2,1)S(1)} collective-permute-done((bf16[256,1024]{1,0:T(8,128)(2,1)S(1)}, bf16[256,1024]{1,0:T(8,128)(2,1)S(1)}, u32[]{:S(2)}, u32[]{:S(2)}) %collective-permute-start) | collective-permute-done | bytes 524320 | tf_op jit(solution)/shard_map/ppermute | solution.py:313
  56.7 0.1 convert_add_fusion
  56.9 1.1 collective-permute-start.1
  57.9 6.7 %collective-permute-done.1 = bf16[128,1024]{1,0:T(8,128)(2,1)S(1)} collective-permute-done((bf16[128,1024]{1,0:T(8,128)(2,1)S(1)}, bf16[128,1024]{1,0:T(8,128)(2,1)S(1)}, u32[]{:S(2)}, u32[]{:S(2)}) %collective-permute-start.1) | collective-permute-done | bytes 262176 | tf_op jit(solution)/shard_map/ppermute | solution.py:313
  64.6 0.1 convert_add_fusion.1
  64.7 0.0 copy-start.1
  64.7 0.9 collective-permute-start.4
  65.7 0.7 collective-permute-start.3
  66.4 2.0 %collective-permute-start.2 = (bf16[32,1024]{1,0:T(8,128)(2,1)S(1)}, bf16[32,1024]{1,0:T(8,128)(2,1)S(1)}, u32[]{:S(2)}, u32[]{:S(2)}) collective-permute-start(bf16[32,1024]{1,0:T(8,128)(2,1)S(1)} %get-tuple-element.18), channel_id=1, source_target_pairs={{0,4},{1,5},{2,6},{3,7},{4,8},{5,9},{6,10},{7,11},{8,12},{9,13},{1... | collective-permute-start | bytes 196616 | tf_op jit(solution)/shard_map/ppermute | solution.py:313
  68.4 0.0 collective-permute-done.4
  68.5 1.8 %collective-permute-done.3 = bf16[32,1024]{1,0:T(8,128)(2,1)S(1)} collective-permute-done((bf16[32,1024]{1,0:T(8,128)(2,1)S(1)}, bf16[32,1024]{1,0:T(8,128)(2,1)S(1)}, u32[]{:S(2)}, u32[]{:S(2)}) %collective-permute-start.3) | collective-permute-done | bytes 65568 | tf_op jit(solution)/shard_map/ppermute | solution.py:313
  70.2 1.4 %collective-permute-done.2 = bf16[32,1024]{1,0:T(8,128)(2,1)S(1)} collective-permute-done((bf16[32,1024]{1,0:T(8,128)(2,1)S(1)}, bf16[32,1024]{1,0:T(8,128)(2,1)S(1)}, u32[]{:S(2)}, u32[]{:S(2)}) %collective-permute-start.2) | collective-permute-done | bytes 65568 | tf_op jit(solution)/shard_map/ppermute | solution.py:313
  71.7 2.4 %collective-permute-start.5 = (bf16[32,1024]{1,0:T(8,128)(2,1)S(1)}, bf16[32,1024]{1,0:T(8,128)(2,1)S(1)}, u32[]{:S(2)}, u32[]{:S(2)}) collective-permute-start(bf16[32,1024]{1,0:T(8,128)(2,1)S(1)} %multiply_convert_fusion), channel_id=1, source_target_pairs={{0,12},{1,13},{2,14},{3,15},{4,0},{5,1},{6,2},{7,3},{8,4},{9,5},{1... | collective-permute-start | bytes 196616 | tf_op jit(solution)/shard_map/ppermute | solution.py:313
  74.0 0.9 collective-permute-start.6
  75.0 0.3 collective-permute-start.7
  75.3 7.7 %all-to-all-start.1 = ((bf16[16,40,1024]{2,1,0:T(8,128)(2,1)}), bf16[16,40,1024]{2,1,0:T(8,128)(2,1)S(1)}, u32[]{:S(2)}, u32[]{:S(2)}) async-start(bf16[16,40,1024]{2,1,0:T(8,128)(2,1)} %bitcast.1), calls=%async_computation.1 | async-start | bytes 2621440 | tf_op jit(solution)/shard_map/all_to_all | solution.py:361
  83.0 0.0 collective-permute-done.5
  83.0 0.0 collective-permute-done.6
  83.0 0.0 collective-permute-done.7
  83.1 0.3 collective-permute-start.8
  83.5 0.0 copy-done.1
  83.5 0.7 gather_fusion
  84.2 13.0 %collective-permute-done.8 = bf16[128,1024]{1,0:T(8,128)(2,1)S(1)} collective-permute-done((bf16[128,1024]{1,0:T(8,128)(2,1)S(1)}, bf16[128,1024]{1,0:T(8,128)(2,1)S(1)}, u32[]{:S(2)}, u32[]{:S(2)}) %collective-permute-start.8) | collective-permute-done | bytes 262176 | tf_op jit(solution)/shard_map/ppermute | solution.py:313
  97.1 0.1 broadcast_select_fusion.3
  97.3 2.5 %collective-permute-start.9 = (bf16[256,1024]{1,0:T(8,128)(2,1)S(1)}, bf16[256,1024]{1,0:T(8,128)(2,1)S(1)}, u32[]{:S(2)}, u32[]{:S(2)}) collective-permute-start(bf16[256,1024]{1,0:T(8,128)(2,1)S(1)} %pad_maximum_fusion.1), channel_id=1, source_target_pairs={{0,1},{1,0},{2,3},{3,2},{4,5},{5,4},{6,7},{7,6},{8,9},{9,8},{10,11... | collective-permute-start | bytes 1572872 | tf_op jit(solution)/shard_map/ppermute | solution.py:313
  99.8 0.1 iota_add_fusion
  99.9 0.1 add.134.blocks
  100.0 0.7 iota_reduce_fusion
  100.7 0.6 collective-permute-done.9
  101.3 0.2 broadcast_select_fusion.1
  101.6 0.2 maximum_convert_fusion
  101.8 0.2 slice_bitcast_fusion.1
  102.0 1.5 %pad_maximum_fusion = f32[2,512,512]{2,1,0:T(8,128)} fusion(f32[1,512,512]{2,1,0:T(8,128)S(1)} %get-tuple-element.13, f32[1,512,512]{2,1,0:T(8,128)S(1)} %get-tuple-element.12), kind=kLoop, calls=%fused_computation.1 | loop fusion | flops 524288 | bytes 4194304 | tf_op jit(solution)/shard_map/stack | solution.py:363
  103.5 10.1 %all-to-all-done.1.terms = bf16[16,40,1024]{2,1,0:T(8,128)(2,1)S(1)} async-done(((bf16[16,40,1024]{2,1,0:T(8,128)(2,1)}), bf16[16,40,1024]{2,1,0:T(8,128)(2,1)S(1)}, u32[]{:S(2)}, u32[]{:S(2)}) %all-to-all-start.1) | async-done | bytes 1310752 | tf_op jit(solution)/shard_map/all_to_all | solution.py:361
  113.6 5.1 %place.1 = f32[2,40,32768]{2,1,0:T(8,128)} custom-call(s32[16]{0:T(128)S(1)} %copy-done.4, s32[16]{0:T(128)S(1)} %copy-done.1, s32[80]{0:T(128)S(1)} %add.134.blocks, s32[80]{0:T(128)S(1)} %get-tuple-element.7.owners, bf16[16,40,1024]{2,1,0:T(8,128)(2,1)S(1)} %all-to-all-done.1.terms, ...), custom_call_target="tpu_custom_call", output_to_operand_aliasing={{}: (5, {})} | custom-call | bytes 6291456 | tf_op jit(solution)/shard_map/place/pallas_call | solution.py:283
  (9 shorter events, 0.2 us)
Async XLA Ops:
  0.6 0.7 copy-start
  1.3 4.0 %copy-start.2 = (f32[2,40,32768]{2,1,0:T(8,128)S(1)}, f32[2,40,32768]{2,1,0:T(8,128)}, u32[]{:S(2)}) copy-start(f32[2,40,32768]{2,1,0:T(8,128)} %tile.1) | copy-start | bytes 31457284
  5.3 0.7 copy-start.3
  5.9 40.3 %copy-start.8 = (bf16[1024,1024]{1,0:T(8,128)(2,1)S(1)}, bf16[1024,1024]{1,0:T(8,128)(2,1)}, u32[]{:S(2)}) copy-start(bf16[1024,1024]{1,0:T(8,128)(2,1)} %constant.147.clone.right) | copy-start | bytes 6291460
  5.9 40.3 %copy-start.9 = (bf16[1024,1024]{1,0:T(8,128)(2,1)S(1)}, bf16[1024,1024]{1,0:T(8,128)(2,1)}, u32[]{:S(2)}) copy-start(bf16[1024,1024]{1,0:T(8,128)(2,1)} %constant.148.clone.left) | copy-start | bytes 6291460
  9.3 37.0 %copy-start.4 = (s32[16]{0:T(128)S(1)}, s32[16]{0:T(128)}, u32[]{:S(2)}) copy-start(s32[16]{0:T(128)} %dealing.5) | copy-start | bytes 196
  9.3 37.0 %copy-start.5 = (bf16[2,512,512]{2,1,0:T(8,128)(2,1)S(1)}, bf16[2,512,512]{2,1,0:T(8,128)(2,1)}, u32[]{:S(2)}) copy-start(bf16[2,512,512]{2,1,0:T(8,128)(2,1)} %probe.1) | copy-start | bytes 3145732
  9.3 37.0 %copy-start.6 = (bf16[1,512,512]{2,1,0:T(8,128)(2,1)S(1)}, bf16[1,512,512]{2,1,0:T(8,128)(2,1)}, u32[]{:S(2)}) copy-start(bf16[1,512,512]{2,1,0:T(8,128)(2,1)} %measured.1) | copy-start | bytes 1572868
  9.3 37.0 %copy-start.7 = (s32[16]{0:T(128)S(1)}, s32[16]{0:T(128)}, u32[]{:S(2)}) copy-start(s32[16]{0:T(128)} %rows.1) | copy-start | bytes 196
  54.7 2.0 %collective-permute-start = (bf16[256,1024]{1,0:T(8,128)(2,1)S(1)}, bf16[256,1024]{1,0:T(8,128)(2,1)S(1)}, u32[]{:S(2)}, u32[]{:S(2)}) collective-permute-start(bf16[256,1024]{1,0:T(8,128)(2,1)S(1)} %get-tuple-element.11), channel_id=1, source_target_pairs={{0,1},{1,0},{2,3},{3,2},{4,5},{5,4},{6,7},{7,6},{8,9},{9,8},{10,11... | collective-permute-start | bytes 1572872 | tf_op jit(solution)/shard_map/ppermute | solution.py:313
  56.9 7.8 %collective-permute-start.1 = (bf16[128,1024]{1,0:T(8,128)(2,1)S(1)}, bf16[128,1024]{1,0:T(8,128)(2,1)S(1)}, u32[]{:S(2)}, u32[]{:S(2)}) collective-permute-start(bf16[128,1024]{1,0:T(8,128)(2,1)S(1)} %dynamic-slice_convert_fusion), channel_id=1, source_target_pairs={{0,2},{1,3},{2,0},{3,1},{4,6},{5,7},{6,4},{7,5},{8,10},{9,11},{10,... | collective-permute-start | bytes 786440 | tf_op jit(solution)/shard_map/ppermute | solution.py:313
  64.7 18.8 %copy-start.1 = (s32[16]{0:T(128)S(1)}, s32[16]{0:T(128)}, u32[]{:S(2)}) copy-start(s32[16]{0:T(128)} %cols.3) | copy-start | bytes 196
  64.7 3.7 %collective-permute-start.4 = (bf16[32,1024]{1,0:T(8,128)(2,1)S(1)}, bf16[32,1024]{1,0:T(8,128)(2,1)S(1)}, u32[]{:S(2)}, u32[]{:S(2)}) collective-permute-start(bf16[32,1024]{1,0:T(8,128)(2,1)S(1)} %get-tuple-element.19), channel_id=1, source_target_pairs={{0,12},{1,13},{2,14},{3,15},{4,0},{5,1},{6,2},{7,3},{8,4},{9,5},{1... | collective-permute-start | bytes 196616 | tf_op jit(solution)/shard_map/ppermute | solution.py:313
  65.7 4.5 %collective-permute-start.3 = (bf16[32,1024]{1,0:T(8,128)(2,1)S(1)}, bf16[32,1024]{1,0:T(8,128)(2,1)S(1)}, u32[]{:S(2)}, u32[]{:S(2)}) collective-permute-start(bf16[32,1024]{1,0:T(8,128)(2,1)S(1)} %get-tuple-element.20), channel_id=1, source_target_pairs={{0,8},{1,9},{2,10},{3,11},{4,12},{5,13},{6,14},{7,15},{8,0},{9,1},... | collective-permute-start | bytes 196616 | tf_op jit(solution)/shard_map/ppermute | solution.py:313
  66.4 5.2 %collective-permute-start.2 = (bf16[32,1024]{1,0:T(8,128)(2,1)S(1)}, bf16[32,1024]{1,0:T(8,128)(2,1)S(1)}, u32[]{:S(2)}, u32[]{:S(2)}) collective-permute-start(bf16[32,1024]{1,0:T(8,128)(2,1)S(1)} %get-tuple-element.18), channel_id=1, source_target_pairs={{0,4},{1,5},{2,6},{3,7},{4,8},{5,9},{6,10},{7,11},{8,12},{9,13},{1... | collective-permute-start | bytes 196616 | tf_op jit(solution)/shard_map/ppermute | solution.py:313
  71.7 11.3 %collective-permute-start.5 = (bf16[32,1024]{1,0:T(8,128)(2,1)S(1)}, bf16[32,1024]{1,0:T(8,128)(2,1)S(1)}, u32[]{:S(2)}, u32[]{:S(2)}) collective-permute-start(bf16[32,1024]{1,0:T(8,128)(2,1)S(1)} %multiply_convert_fusion), channel_id=1, source_target_pairs={{0,12},{1,13},{2,14},{3,15},{4,0},{5,1},{6,2},{7,3},{8,4},{9,5},{1... | collective-permute-start | bytes 196616 | tf_op jit(solution)/shard_map/ppermute | solution.py:313
  74.0 9.0 %collective-permute-start.6 = (bf16[32,1024]{1,0:T(8,128)(2,1)S(1)}, bf16[32,1024]{1,0:T(8,128)(2,1)S(1)}, u32[]{:S(2)}, u32[]{:S(2)}) collective-permute-start(bf16[32,1024]{1,0:T(8,128)(2,1)S(1)} %multiply_convert_fusion), channel_id=1, source_target_pairs={{0,8},{1,9},{2,10},{3,11},{4,12},{5,13},{6,14},{7,15},{8,0},{9,1},... | collective-permute-start | bytes 196616 | tf_op jit(solution)/shard_map/ppermute | solution.py:313
  75.0 8.1 %collective-permute-start.7 = (bf16[32,1024]{1,0:T(8,128)(2,1)S(1)}, bf16[32,1024]{1,0:T(8,128)(2,1)S(1)}, u32[]{:S(2)}, u32[]{:S(2)}) collective-permute-start(bf16[32,1024]{1,0:T(8,128)(2,1)S(1)} %multiply_convert_fusion), channel_id=1, source_target_pairs={{0,4},{1,5},{2,6},{3,7},{4,8},{5,9},{6,10},{7,11},{8,12},{9,13},{1... | collective-permute-start | bytes 196616 | tf_op jit(solution)/shard_map/ppermute | solution.py:313
  75.3 38.3 %all-to-all-start.1 = ((bf16[16,40,1024]{2,1,0:T(8,128)(2,1)}), bf16[16,40,1024]{2,1,0:T(8,128)(2,1)S(1)}, u32[]{:S(2)}, u32[]{:S(2)}) async-start(bf16[16,40,1024]{2,1,0:T(8,128)(2,1)} %bitcast.1), calls=%async_computation.1 | async-start | bytes 2621440 | tf_op jit(solution)/shard_map/all_to_all | solution.py:361
  83.1 14.0 %collective-permute-start.8 = (bf16[128,1024]{1,0:T(8,128)(2,1)S(1)}, bf16[128,1024]{1,0:T(8,128)(2,1)S(1)}, u32[]{:S(2)}, u32[]{:S(2)}) collective-permute-start(bf16[128,1024]{1,0:T(8,128)(2,1)S(1)} %pad_maximum_fusion.2), channel_id=1, source_target_pairs={{0,2},{1,3},{2,0},{3,1},{4,6},{5,7},{6,4},{7,5},{8,10},{9,11},{10,... | collective-permute-start | bytes 786440 | tf_op jit(solution)/shard_map/ppermute | solution.py:313
  97.3 4.0 %collective-permute-start.9 = (bf16[256,1024]{1,0:T(8,128)(2,1)S(1)}, bf16[256,1024]{1,0:T(8,128)(2,1)S(1)}, u32[]{:S(2)}, u32[]{:S(2)}) collective-permute-start(bf16[256,1024]{1,0:T(8,128)(2,1)S(1)} %pad_maximum_fusion.1), channel_id=1, source_target_pairs={{0,1},{1,0},{2,3},{3,2},{4,5},{5,4},{6,7},{7,6},{8,9},{9,8},{10,11... | collective-permute-start | bytes 1572872 | tf_op jit(solution)/shard_map/ppermute | solution.py:313

commit v2 on v1

--- a/solution.py
+++ b/solution.py
@@ -61,7 +61,7 @@
 
     lane = lax.broadcasted_iota(jnp.int32, (tile_rows, LANES), 1)
 
-    @pl.loop(0, slots)
+    @pl.loop(0, slots, unroll=2)
     def _(slot):
         copy(slot).wait()
         _, offset = window_start(cols[dealing[slot]], order, tile_cols)
@@ -90,7 +90,7 @@
             pltpu.VMEM((slots, 2, tile_rows, span), jnp.float32),
             pltpu.SemaphoreType.DMA((slots,)),
         ],
-        compiler_params=pltpu.CompilerParams(vmem_limit_bytes=24 * 2**20),
+        compiler_params=pltpu.CompilerParams(vmem_limit_bytes=56 * 2**20),
         cost_estimate=pl.CostEstimate(flops=0, bytes_accessed=6 * 2**20, transcendentals=0),
         name="fetch",
     )(dealing, cols, tile)
@@ -241,7 +241,7 @@
     totals[...] = jnp.zeros_like(totals)
     lane = lax.broadcasted_iota(jnp.int32, (tile_rows, LANES), 1)
 
-    @pl.loop(0, slots)
+    @pl.loop(0, slots, unroll=2)
     def _(slot):
         _, offset = window_start(cols[dealing[slot]], order, tile_cols)
         shift = lax.rem(offset, LANES)
@@ -359,7 +359,13 @@
     if spare:
         outgoing = jnp.pad(outgoing, ((0, 0), (0, spare), (0, 0)))
     arrived = lax.all_to_all(outgoing, "row", split_axis=0, concat_axis=0, tiled=True)
-    whole = sum_probe(kept, sent, devices, 1.0 / dealing.shape[0]).astype(jnp.float32)
+    rounds = jnp.minimum(dealing[0] + 1, 1)
+    _, whole = lax.while_loop(
+        lambda state: state[0] < rounds,
+        lambda state: (state[0] + 1, sum_probe(kept, sent, devices, 1.0 / dealing.shape[0])),
+        (jnp.zeros((), jnp.int32), jnp.zeros((order, 2 * order), jnp.bfloat16)),
+    )
+    whole = whole.astype(jnp.float32)
     probe_grad = jnp.stack([whole[:, :order], whole[:, order:]])
     object_grad = place_windows(arrived, empty, dealing, col_offsets, order)
     if spare:

time: 119 us -> 125 us (1.050); the launches traced: 119 us -> 123 us
  blocking collectives: 36.9 us -> 0 us
  waiting for transfers between devices: 35.3 us -> 66.4 us
  starting transfers between devices: 19.2 us -> 25.8 us
  other arithmetic: 3.23 us -> 6.9 us
    all_to_all x1 -> x0, blocking collectives: 36.9 us -> none  [body(): lax.all_to_all(pieces, 'row', split_axis=0, concat_axis=0, tiled=True)]
    all_to_all x0 -> x1, waiting for transfers between devices: none -> 29.9 us  [body(): lax.all_to_all(pieces, 'row', split_axis=0, concat_axis=0, tiled=True)]
    ppermute x10, waiting for transfers between devices: 25.2 us -> 36.5 us  [turn(): return lax.ppermute(x, 'row', pairs)]
    all_to_all x1, waiting for transfers between devices: 10.1 us -> 0.01 us  [body(): lax.all_to_all(outgoing, 'row', split_axis=0, concat_axis=0, tiled=True)]
    all_to_all x0 -> x1, starting transfers between devices: none -> 6.7 us  [body(): lax.all_to_all(pieces, 'row', split_axis=0, concat_axis=0, tiled=True)]
    all_to_all x1, starting transfers between devices: 7.72 us -> 4.95 us  [body(): lax.all_to_all(outgoing, 'row', split_axis=0, concat_axis=0, tiled=True)]
    ppermute x10, starting transfers between devices: 11.5 us -> 14.1 us  [turn(): return lax.ppermute(x, 'row', pairs)]
    unnamed x20 -> x14, local copies, waits for them, and re-layouts: 5.32 us -> 3.21 us
  transfers between devices with their start and end apart: 11 -> 12, of which waited for: 7 -> 8; matrix products, arithmetic and copies ran while one was open for 3% -> 7% of each run, Pallas kernels for 0% -> 0%
where the time goes in v2:
time: 125 us; the launch traced here: 123 us
  waiting for transfers between devices  66.4 us (53%)
  starting transfers between devices  25.8 us (21%)
  Pallas kernels  17.7 us (14%)
  other arithmetic  6.9 us (6%)
  local copies, waits for them, and re-layouts  5.33 us (4%)
    ppermute x10, waiting for transfers between devices, turn(): return lax.ppermute(x, 'row', pairs)  36.5 us
    all_to_all x1, waiting for transfers between devices, body(): lax.all_to_all(pieces, 'row', split_axis=0, concat_axis=0, tiled=True)  29.9 us
    ppermute x10, starting transfers between devices, turn(): return lax.ppermute(x, 'row', pairs)  14.1 us
    pallas_call x1, Pallas kernels, slot_terms(): pl.pallas_call(slot_kernel, out_shape=(jax.ShapeDtypeStruct((total_rows,...  8.56 us
    all_to_all x1, starting transfers between devices, body(): lax.all_to_all(pieces, 'row', split_axis=0, concat_axis=0, tiled=True)  6.7 us
    all_to_all x1, starting transfers between devices, body(): lax.all_to_all(outgoing, 'row', split_axis=0, concat_axis=0, tiled=True)  4.95 us
    pallas_call x1, Pallas kernels, fetch_windows(): pl.pallas_call(functools.partial(fetch_kernel, order), out_shape=jax.Shap...  4.6 us
    pallas_call x1, Pallas kernels, place_windows(): pl.pallas_call(functools.partial(place_kernel, order), out_shape=jax.Shap...  4.52 us
  transfers between devices with their start and end apart: 12, of which 8 were waited for; matrix products, arithmetic and copies ran while one was open for 7% of the time, Pallas kernels for 0%

profile of v2, /device:TPU:15, one launch (start us, length us, event | category | flops | bytes accessed | tf_op | source)
XLA Modules:
  0.0 123.0 jit_solution(3903645042297623992)
XLA Ops:
  0.6 4.6 %fetch.1 = bf16[16,40,1024]{2,1,0:T(8,128)(2,1)} custom-call(s32[16]{0:T(128)} %dealing.5, s32[16]{0:T(128)} %cols.3, f32[2,40,32768]{2,1,0:T(8,128)} %tile.1), custom_call_target="tpu_custom_call" | custom-call | bytes 6291456 | tf_op jit(solution)/shard_map/fetch/pallas_call | solution.py:84
  5.2 0.0 copy-start.1
  5.3 0.0 copy-start
  5.3 0.0 copy-start.2
  5.3 0.0 copy-start.3
  5.3 0.0 copy-start.4
  5.3 6.7 %all-to-all-start = ((bf16[16,40,1024]{2,1,0:T(8,128)(2,1)}), bf16[16,40,1024]{2,1,0:T(8,128)(2,1)S(1)}, u32[]{:S(2)}, u32[]{:S(2)}) async-start(bf16[16,40,1024]{2,1,0:T(8,128)(2,1)} %fetch.1), calls=%async_computation | async-start | bytes 2621440 | tf_op jit(solution)/shard_map/all_to_all | solution.py:353
  12.0 0.0 copy-done.1
  12.0 0.0 copy-done
  12.0 0.7 gather_fusion
  12.7 29.9 %all-to-all-done = bf16[16,40,1024]{2,1,0:T(8,128)(2,1)S(1)} async-done(((bf16[16,40,1024]{2,1,0:T(8,128)(2,1)}), bf16[16,40,1024]{2,1,0:T(8,128)(2,1)S(1)}, u32[]{:S(2)}, u32[]{:S(2)}) %all-to-all-start) | async-done | bytes 1310752 | tf_op jit(solution)/shard_map/all_to_all | solution.py:353
  42.6 0.0 copy-done.2
  42.6 0.0 copy-done.3
  42.6 0.0 copy-done.4
  42.6 0.0 copy-start.5
  42.6 1.6 %copy-done.5 = bf16[1024,1024]{1,0:T(8,128)(2,1)S(1)} copy-done((bf16[1024,1024]{1,0:T(8,128)(2,1)S(1)}, bf16[1024,1024]{1,0:T(8,128)(2,1)}, u32[]{:S(2)}) %copy-start.5) | copy-done | bytes 2097176
  44.2 0.0 copy-start.6
  44.2 1.6 %copy-done.6 = bf16[1024,1024]{1,0:T(8,128)(2,1)S(1)} copy-done((bf16[1024,1024]{1,0:T(8,128)(2,1)S(1)}, bf16[1024,1024]{1,0:T(8,128)(2,1)}, u32[]{:S(2)}) %copy-start.6) | copy-done | bytes 2097176
  45.8 8.6 %slot.1 = (bf16[640,1024]{1,0:T(8,128)(2,1)}, f32[256,1024]{1,0:T(8,128)}, bf16[256,1024]{1,0:T(8,128)(2,1)S(1)}, f32[2,40,32768]{2,1,0:T(8,128)}) custom-call(s32[16]{0:T(128)S(1)} %copy-done.1, s32[16]{0:T(128)S(1)} %copy-done.4, bf16[640,1024]{1,0:T(8,128)(2,1)S(1)} %bitcast.8, bf16[2,512,512]{2,1,0:T(8,128)(2,1)S(1)} %copy-done.2, ...), custom_call_target="tpu_custom_call" | custom-call | flops 4294967296 | bytes 20971520 | tf_op jit(solution)/shard_map/slot/pallas_call | solution.py:198
  54.3 0.3 collective-permute-start.9
  54.6 0.1 iota_add_fusion
  54.7 0.1 add.377.blocks
  54.8 0.7 iota_reduce_fusion
  55.6 5.0 %all-to-all-start.1 = ((bf16[16,40,1024]{2,1,0:T(8,128)(2,1)}), bf16[16,40,1024]{2,1,0:T(8,128)(2,1)S(1)}, u32[]{:S(2)}, u32[]{:S(2)}) async-start(bf16[16,40,1024]{2,1,0:T(8,128)(2,1)} %bitcast.1), calls=%async_computation.1 | async-start | bytes 2621440 | tf_op jit(solution)/shard_map/all_to_all | solution.py:361
  60.5 0.0 collective-permute-done.9
  60.5 1.1 broadcast_in_dim.9
  61.6 53.6 %while.15 = (s32[]{:T(128)}, bf16[512,1024]{1,0:T(8,128)(2,1)}, s32[]{:T(128)}, bf16[256,1024]{1,0:T(8,128)(2,1)}, f32[256,1024]{1,0:T(8,128)}, /*index=5*/s32[]...) while((s32[]{:T(128)}, bf16[512,1024]{1,0:T(8,128)(2,1)}, ...), condition=%wide.region_2.3_spmd, body=%wide.region_1.2_spmd.sunk | while | flops 8519831 | bytes 18352168 | solution.py:363
  61.6 1.5 %convert_add_fusion.4 = f32[256,1024]{1,0:T(8,128)S(1)} fusion(f32[256,1024]{1,0:T(8,128)} %get-tuple-element.284, bf16[256,1024]{1,0:T(8,128)(2,1)} %get-tuple-element.283), kind=kLoop, calls=%fused_computation.2.clone.1 | loop fusion | flops 524288 | bytes 2621440 | tf_op jit(solution)/shard_map/while/body/add | solution.py:319
  63.2 0.3 collective-permute-start
  63.6 10.9 %collective-permute-done = bf16[128,1024]{1,0:T(8,128)(2,1)S(1)} collective-permute-done((bf16[128,1024]{1,0:T(8,128)(2,1)S(1)}, bf16[128,1024]{1,0:T(8,128)(2,1)S(1)}, u32[]{:S(2)}, u32[]{:S(2)}) %collective-permute-start) | collective-permute-done | bytes 262176 | tf_op jit(solution)/shard_map/while/body/ppermute | solution.py:313
  74.5 0.1 convert_add_fusion.5
  74.6 2.6 %collective-permute-start.1 = (bf16[32,1024]{1,0:T(8,128)(2,1)S(1)}, bf16[32,1024]{1,0:T(8,128)(2,1)S(1)}, u32[]{:S(2)}, u32[]{:S(2)}) collective-permute-start(bf16[32,1024]{1,0:T(8,128)(2,1)S(1)} %get-tuple-element.239), channel_id=1, source_target_pairs={{0,12},{1,13},{2,14},{3,15},{4,0},{5,1},{6,2},{7,3},{8,4},{9,5},{1... | collective-permute-start | bytes 196616 | tf_op jit(solution)/shard_map/while/body/ppermute | solution.py:313
  77.2 2.8 %collective-permute-start.2 = (bf16[32,1024]{1,0:T(8,128)(2,1)S(1)}, bf16[32,1024]{1,0:T(8,128)(2,1)S(1)}, u32[]{:S(2)}, u32[]{:S(2)}) collective-permute-start(bf16[32,1024]{1,0:T(8,128)(2,1)S(1)} %get-tuple-element.240), channel_id=1, source_target_pairs={{0,8},{1,9},{2,10},{3,11},{4,12},{5,13},{6,14},{7,15},{8,0},{9,1},... | collective-permute-start | bytes 196616 | tf_op jit(solution)/shard_map/while/body/ppermute | solution.py:313
  80.0 2.3 %collective-permute-start.3 = (bf16[32,1024]{1,0:T(8,128)(2,1)S(1)}, bf16[32,1024]{1,0:T(8,128)(2,1)S(1)}, u32[]{:S(2)}, u32[]{:S(2)}) collective-permute-start(bf16[32,1024]{1,0:T(8,128)(2,1)S(1)} %get-tuple-element.241), channel_id=1, source_target_pairs={{0,4},{1,5},{2,6},{3,7},{4,8},{5,9},{6,10},{7,11},{8,12},{9,13},{1... | collective-permute-start | bytes 196616 | tf_op jit(solution)/shard_map/while/body/ppermute | solution.py:313
  82.3 12.8 %collective-permute-done.1 = bf16[32,1024]{1,0:T(8,128)(2,1)S(1)} collective-permute-done((bf16[32,1024]{1,0:T(8,128)(2,1)S(1)}, bf16[32,1024]{1,0:T(8,128)(2,1)S(1)}, u32[]{:S(2)}, u32[]{:S(2)}) %collective-permute-start.1) | collective-permute-done | bytes 65568 | tf_op jit(solution)/shard_map/while/body/ppermute | solution.py:313
  95.1 0.0 collective-permute-done.2
  95.1 0.0 collective-permute-done.3
  95.2 2.6 %collective-permute-start.4 = (bf16[32,1024]{1,0:T(8,128)(2,1)S(1)}, bf16[32,1024]{1,0:T(8,128)(2,1)S(1)}, u32[]{:S(2)}, u32[]{:S(2)}) collective-permute-start(bf16[32,1024]{1,0:T(8,128)(2,1)S(1)} %multiply_convert_fusion.2), channel_id=1, source_target_pairs={{0,12},{1,13},{2,14},{3,15},{4,0},{5,1},{6,2},{7,3},{8,4},{9,5},{1... | collective-permute-start | bytes 196616 | tf_op jit(solution)/shard_map/while/body/ppermute | solution.py:313
  97.8 0.2 collective-permute-start.5
  98.0 1.1 collective-permute-start.6
  99.1 0.1 collective-permute-done.4
  99.1 2.7 %collective-permute-done.5 = bf16[32,1024]{1,0:T(8,128)(2,1)S(1)} collective-permute-done((bf16[32,1024]{1,0:T(8,128)(2,1)S(1)}, bf16[32,1024]{1,0:T(8,128)(2,1)S(1)}, u32[]{:S(2)}, u32[]{:S(2)}) %collective-permute-start.5) | collective-permute-done | bytes 65568 | tf_op jit(solution)/shard_map/while/body/ppermute | solution.py:313
  101.8 1.5 %collective-permute-done.6 = bf16[32,1024]{1,0:T(8,128)(2,1)S(1)} collective-permute-done((bf16[32,1024]{1,0:T(8,128)(2,1)S(1)}, bf16[32,1024]{1,0:T(8,128)(2,1)S(1)}, u32[]{:S(2)}, u32[]{:S(2)}) %collective-permute-start.6) | collective-permute-done | bytes 65568 | tf_op jit(solution)/shard_map/while/body/ppermute | solution.py:313
  103.4 0.1 collective-permute-start.7
  103.6 7.0 %collective-permute-done.7 = bf16[128,1024]{1,0:T(8,128)(2,1)S(1)} collective-permute-done((bf16[128,1024]{1,0:T(8,128)(2,1)S(1)}, bf16[128,1024]{1,0:T(8,128)(2,1)S(1)}, u32[]{:S(2)}, u32[]{:S(2)}) %collective-permute-start.7) | collective-permute-done | bytes 262176 | tf_op jit(solution)/shard_map/while/body/ppermute | solution.py:313
  110.6 0.1 broadcast_select_fusion.6
  110.7 1.7 %collective-permute-start.8 = (bf16[256,1024]{1,0:T(8,128)(2,1)S(1)}, bf16[256,1024]{1,0:T(8,128)(2,1)S(1)}, u32[]{:S(2)}, u32[]{:S(2)}) collective-permute-start(bf16[256,1024]{1,0:T(8,128)(2,1)S(1)} %pad_maximum_fusion.8), channel_id=1, source_target_pairs={{0,1},{1,0},{2,3},{3,2},{4,5},{5,4},{6,7},{7,6},{8,9},{9,8},{10,11... | collective-permute-start | bytes 1572872 | tf_op jit(solution)/shard_map/while/body/ppermute | solution.py:313
  112.4 1.5 %collective-permute-done.8 = bf16[256,1024]{1,0:T(8,128)(2,1)S(1)} collective-permute-done((bf16[256,1024]{1,0:T(8,128)(2,1)S(1)}, bf16[256,1024]{1,0:T(8,128)(2,1)S(1)}, u32[]{:S(2)}, u32[]{:S(2)}) %collective-permute-start.8) | collective-permute-done | bytes 524320 | tf_op jit(solution)/shard_map/while/body/ppermute | solution.py:313
  114.0 0.2 broadcast_select_fusion.7
  114.2 1.0 pad_maximum_fusion.9
  115.3 1.5 %convert_element_type.103 = f32[512,1024]{1,0:T(8,128)S(1)} convert(bf16[512,1024]{1,0:T(8,128)(2,1)} %get-tuple-element.174) | non-fusion elementwise | flops 524288 | bytes 3145728 | tf_op jit(solution)/shard_map/convert_element_type | solution.py:368
  116.7 0.2 slice_bitcast_fusion.1
  117.0 1.5 %pad_maximum_fusion.3 = f32[2,512,512]{2,1,0:T(8,128)} fusion(f32[1,512,512]{2,1,0:T(8,128)S(1)} %get-tuple-element.197, f32[1,512,512]{2,1,0:T(8,128)S(1)} %get-tuple-element.196), kind=kLoop, calls=%fused_computation.19 | loop fusion | flops 524288 | bytes 4194304 | tf_op jit(solution)/shard_map/stack | solution.py:369
  118.5 0.0 all-to-all-done.1.terms
  118.5 4.5 %place.1 = f32[2,40,32768]{2,1,0:T(8,128)} custom-call(s32[16]{0:T(128)S(1)} %copy-done.1, s32[16]{0:T(128)S(1)} %copy-done, s32[80]{0:T(128)S(1)} %add.377.blocks, s32[80]{0:T(128)S(1)} %get-tuple-element.169.owners, bf16[16,40,1024]{2,1,0:T(8,128)(2,1)S(1)} %all-to-all-done.1.terms, ...), custom_call_target="tpu_custom_call", output_to_operand_aliasing={{}: (5, {})} | custom-call | bytes 6291456 | tf_op jit(solution)/shard_map/place/pallas_call | solution.py:283
  (9 shorter events, 0.2 us)
Async XLA Ops:
  5.2 6.8 %copy-start.1 = (s32[16]{0:T(128)S(1)}, s32[16]{0:T(128)}, u32[]{:S(2)}) copy-start(s32[16]{0:T(128)} %dealing.5) | copy-start | bytes 196
  5.3 6.8 %copy-start = (s32[16]{0:T(128)S(1)}, s32[16]{0:T(128)}, u32[]{:S(2)}) copy-start(s32[16]{0:T(128)} %cols.3) | copy-start | bytes 196
  5.3 37.3 %copy-start.2 = (bf16[2,512,512]{2,1,0:T(8,128)(2,1)S(1)}, bf16[2,512,512]{2,1,0:T(8,128)(2,1)}, u32[]{:S(2)}) copy-start(bf16[2,512,512]{2,1,0:T(8,128)(2,1)} %probe.1) | copy-start | bytes 3145732
  5.3 37.3 %copy-start.3 = (bf16[1,512,512]{2,1,0:T(8,128)(2,1)S(1)}, bf16[1,512,512]{2,1,0:T(8,128)(2,1)}, u32[]{:S(2)}) copy-start(bf16[1,512,512]{2,1,0:T(8,128)(2,1)} %measured.1) | copy-start | bytes 1572868
  5.3 37.3 %copy-start.4 = (s32[16]{0:T(128)S(1)}, s32[16]{0:T(128)}, u32[]{:S(2)}) copy-start(s32[16]{0:T(128)} %rows.1) | copy-start | bytes 196
  5.3 37.3 %all-to-all-start = ((bf16[16,40,1024]{2,1,0:T(8,128)(2,1)}), bf16[16,40,1024]{2,1,0:T(8,128)(2,1)S(1)}, u32[]{:S(2)}, u32[]{:S(2)}) async-start(bf16[16,40,1024]{2,1,0:T(8,128)(2,1)} %fetch.1), calls=%async_computation | async-start | bytes 2621440 | tf_op jit(solution)/shard_map/all_to_all | solution.py:353
  42.6 1.6 %copy-start.5 = (bf16[1024,1024]{1,0:T(8,128)(2,1)S(1)}, bf16[1024,1024]{1,0:T(8,128)(2,1)}, u32[]{:S(2)}) copy-start(bf16[1024,1024]{1,0:T(8,128)(2,1)} %constant.285.clone.right) | copy-start | bytes 6291460
  44.2 1.6 %copy-start.6 = (bf16[1024,1024]{1,0:T(8,128)(2,1)S(1)}, bf16[1024,1024]{1,0:T(8,128)(2,1)}, u32[]{:S(2)}) copy-start(bf16[1024,1024]{1,0:T(8,128)(2,1)} %constant.286.clone.left) | copy-start | bytes 6291460
  54.3 6.2 %collective-permute-start.9 = (bf16[256,1024]{1,0:T(8,128)(2,1)S(1)}, bf16[256,1024]{1,0:T(8,128)(2,1)}, u32[]{:S(2)}, u32[]{:S(2)}) collective-permute-start(bf16[256,1024]{1,0:T(8,128)(2,1)S(1)} %get-tuple-element.172), channel_id=1, source_target_pairs={{0,1},{1,0},{2,3},{3,2},{4,5},{5,4},{6,7},{7,6},{8,9},{9,8},{10,11... | collective-permute-start | bytes 1572872 | tf_op jit(solution)/shard_map/while/body/ppermute | solution.py:313
  55.6 62.9 %all-to-all-start.1 = ((bf16[16,40,1024]{2,1,0:T(8,128)(2,1)}), bf16[16,40,1024]{2,1,0:T(8,128)(2,1)S(1)}, u32[]{:S(2)}, u32[]{:S(2)}) async-start(bf16[16,40,1024]{2,1,0:T(8,128)(2,1)} %bitcast.1), calls=%async_computation.1 | async-start | bytes 2621440 | tf_op jit(solution)/shard_map/all_to_all | solution.py:361
  63.2 11.3 %collective-permute-start = (bf16[128,1024]{1,0:T(8,128)(2,1)S(1)}, bf16[128,1024]{1,0:T(8,128)(2,1)S(1)}, u32[]{:S(2)}, u32[]{:S(2)}) collective-permute-start(bf16[128,1024]{1,0:T(8,128)(2,1)S(1)} %dynamic-slice_convert_fusion.6), channel_id=1, source_target_pairs={{0,2},{1,3},{2,0},{3,1},{4,6},{5,7},{6,4},{7,5},{8,10},{9,11},{10,... | collective-permute-start | bytes 786440 | tf_op jit(solution)/shard_map/while/body/ppermute | solution.py:313
  74.6 20.5 %collective-permute-start.1 = (bf16[32,1024]{1,0:T(8,128)(2,1)S(1)}, bf16[32,1024]{1,0:T(8,128)(2,1)S(1)}, u32[]{:S(2)}, u32[]{:S(2)}) collective-permute-start(bf16[32,1024]{1,0:T(8,128)(2,1)S(1)} %get-tuple-element.239), channel_id=1, source_target_pairs={{0,12},{1,13},{2,14},{3,15},{4,0},{5,1},{6,2},{7,3},{8,4},{9,5},{1... | collective-permute-start | bytes 196616 | tf_op jit(solution)/shard_map/while/body/ppermute | solution.py:313
  77.2 17.9 %collective-permute-start.2 = (bf16[32,1024]{1,0:T(8,128)(2,1)S(1)}, bf16[32,1024]{1,0:T(8,128)(2,1)S(1)}, u32[]{:S(2)}, u32[]{:S(2)}) collective-permute-start(bf16[32,1024]{1,0:T(8,128)(2,1)S(1)} %get-tuple-element.240), channel_id=1, source_target_pairs={{0,8},{1,9},{2,10},{3,11},{4,12},{5,13},{6,14},{7,15},{8,0},{9,1},... | collective-permute-start | bytes 196616 | tf_op jit(solution)/shard_map/while/body/ppermute | solution.py:313
  80.0 15.1 %collective-permute-start.3 = (bf16[32,1024]{1,0:T(8,128)(2,1)S(1)}, bf16[32,1024]{1,0:T(8,128)(2,1)S(1)}, u32[]{:S(2)}, u32[]{:S(2)}) collective-permute-start(bf16[32,1024]{1,0:T(8,128)(2,1)S(1)} %get-tuple-element.241), channel_id=1, source_target_pairs={{0,4},{1,5},{2,6},{3,7},{4,8},{5,9},{6,10},{7,11},{8,12},{9,13},{1... | collective-permute-start | bytes 196616 | tf_op jit(solution)/shard_map/while/body/ppermute | solution.py:313
  95.2 4.0 %collective-permute-start.4 = (bf16[32,1024]{1,0:T(8,128)(2,1)S(1)}, bf16[32,1024]{1,0:T(8,128)(2,1)S(1)}, u32[]{:S(2)}, u32[]{:S(2)}) collective-permute-start(bf16[32,1024]{1,0:T(8,128)(2,1)S(1)} %multiply_convert_fusion.2), channel_id=1, source_target_pairs={{0,12},{1,13},{2,14},{3,15},{4,0},{5,1},{6,2},{7,3},{8,4},{9,5},{1... | collective-permute-start | bytes 196616 | tf_op jit(solution)/shard_map/while/body/ppermute | solution.py:313
  97.8 4.0 %collective-permute-start.5 = (bf16[32,1024]{1,0:T(8,128)(2,1)S(1)}, bf16[32,1024]{1,0:T(8,128)(2,1)S(1)}, u32[]{:S(2)}, u32[]{:S(2)}) collective-permute-start(bf16[32,1024]{1,0:T(8,128)(2,1)S(1)} %multiply_convert_fusion.2), channel_id=1, source_target_pairs={{0,8},{1,9},{2,10},{3,11},{4,12},{5,13},{6,14},{7,15},{8,0},{9,1},... | collective-permute-start | bytes 196616 | tf_op jit(solution)/shard_map/while/body/ppermute | solution.py:313
  98.0 5.4 %collective-permute-start.6 = (bf16[32,1024]{1,0:T(8,128)(2,1)S(1)}, bf16[32,1024]{1,0:T(8,128)(2,1)S(1)}, u32[]{:S(2)}, u32[]{:S(2)}) collective-permute-start(bf16[32,1024]{1,0:T(8,128)(2,1)S(1)} %multiply_convert_fusion.2), channel_id=1, source_target_pairs={{0,4},{1,5},{2,6},{3,7},{4,8},{5,9},{6,10},{7,11},{8,12},{9,13},{1... | collective-permute-start | bytes 196616 | tf_op jit(solution)/shard_map/while/body/ppermute | solution.py:313
  103.4 7.1 %collective-permute-start.7 = (bf16[128,1024]{1,0:T(8,128)(2,1)S(1)}, bf16[128,1024]{1,0:T(8,128)(2,1)S(1)}, u32[]{:S(2)}, u32[]{:S(2)}) collective-permute-start(bf16[128,1024]{1,0:T(8,128)(2,1)S(1)} %pad_maximum_fusion.7), channel_id=1, source_target_pairs={{0,2},{1,3},{2,0},{3,1},{4,6},{5,7},{6,4},{7,5},{8,10},{9,11},{10,... | collective-permute-start | bytes 786440 | tf_op jit(solution)/shard_map/while/body/ppermute | solution.py:313
  110.7 3.3 %collective-permute-start.8 = (bf16[256,1024]{1,0:T(8,128)(2,1)S(1)}, bf16[256,1024]{1,0:T(8,128)(2,1)S(1)}, u32[]{:S(2)}, u32[]{:S(2)}) collective-permute-start(bf16[256,1024]{1,0:T(8,128)(2,1)S(1)} %pad_maximum_fusion.8), channel_id=1, source_target_pairs={{0,1},{1,0},{2,3},{3,2},{4,5},{5,4},{6,7},{7,6},{8,9},{9,8},{10,11... | collective-permute-start | bytes 1572872 | tf_op jit(solution)/shard_map/while/body/ppermute | solution.py:313

commit v3 on v2

--- a/solution.py
+++ b/solution.py
@@ -97,10 +97,12 @@
 
 
 def slot_kernel(
-    dealing, rows, cells, probe, measured, right, left,
-    terms, kept, sent, empty,
-    wide, patch, wave, half, resid, turned, padded, mine, zeros, sem,
+    chunks, dealing, rows, cells, probe, measured, right_table, left_table,
+    *rest,
 ):
+    backs, (empty, wide, wave, half, resid, turned, padded, zeros, right, left, sem, table_sem) = (
+        rest[: len(chunks)], rest[len(chunks) :]
+    )
     order = probe.shape[1]
     total_rows = cells.shape[0]
     reach = total_rows - order
@@ -109,6 +111,10 @@
     step = 64
     tile = 256
 
+    right_copy = pltpu.make_async_copy(right_table, right, table_sem.at[0])
+    left_copy = pltpu.make_async_copy(left_table, left, table_sem.at[1])
+    right_copy.start()
+    left_copy.start()
     zeros[...] = jnp.zeros_like(zeros)
     fills = []
     for b in range(empty.shape[2] // zeros.shape[2]):
@@ -127,7 +133,6 @@
     def _(i):
         place = pl.ds(pl.multiple_of(i * step, step), step)
         found = rows_from(wide, first_row + i * step, step)
-        patch[place, :] = found.astype(patch.dtype)
         real, imag = found[:, :order], found[:, order:]
         probe_real = probe[0, place, :].astype(jnp.float32)
         probe_imag = probe[1, place, :].astype(jnp.float32)
@@ -137,11 +142,13 @@
     def dot(a, b):
         return jnp.dot(a, b, preferred_element_type=jnp.float32)
 
+    right_copy.wait()
     for first in range(0, order, tile):
         here = slice(first, first + tile)
         there = slice(order + first, order + first + tile)
         half[:order, here] = dot(wave[...], right[:, here]).astype(half.dtype)
         half[order:, here] = dot(wave[...], right[:, there]).astype(half.dtype)
+    left_copy.wait()
     for first in range(0, order, tile):
         here = slice(first, first + tile)
         there = slice(order + first, order + first + tile)
@@ -161,61 +168,48 @@
     for first in range(0, order, tile):
         here = slice(first, first + tile)
         there = slice(order + first, order + first + tile)
-        for top in range(0, order, tile):
-            line = slice(top, top + tile)
-            real = dot(right[line, :], turned[:, here])
-            imag = dot(right[order + top : order + top + tile, :], turned[:, here])
-            probe_real = probe[0, line, here].astype(jnp.float32)
-            probe_imag = probe[1, line, here].astype(jnp.float32)
-            down = slice(reach + top, reach + top + tile)
-            padded[down, here] = probe_real * real + probe_imag * imag
-            padded[down, there] = probe_real * imag - probe_imag * real
-            patch_real = patch[line, here].astype(jnp.float32)
-            patch_imag = patch[line, there].astype(jnp.float32)
-            mine[line, here] = patch_real * real + patch_imag * imag
-            mine[line, there] = patch_real * imag - patch_imag * real
+        padded[reach : reach + order, here] = dot(right[:order, :], turned[:, here])
+        padded[reach : reach + order, there] = dot(right[order:, :], turned[:, here])
 
     @pl.loop(0, total_rows // step)
     def _(i):
         place = pl.ds(pl.multiple_of(i * step, step), step)
-        terms[place, :] = rows_from(padded, reach - first_row + i * step, step).astype(terms.dtype)
-
-    count = kept.shape[0]
-    side = lax.rem(me, 2)
-    kept[...] = mine[pl.ds(pl.multiple_of(side * count, count), count), :]
-    sent[...] = mine[pl.ds(pl.multiple_of((1 - side) * count, count), count), :].astype(sent.dtype)
+        moved = rows_from(padded, reach - first_row + i * step, step).astype(jnp.bfloat16)
+        for back, (low, high) in zip(backs, chunks):
+            back[place, : high - low] = moved[:, low:high]
+            back[place, high - low :] = moved[:, order + low : order + high]
+
     for fill in fills:
         fill.wait()
 
 
-def slot_terms(cells, probe, measured, dealing, rows, tile_rows, tile_cols):
+def slot_backs(cells, probe, measured, dealing, rows, tile_rows, tile_cols, chunks):
     order = probe.shape[1]
     total_rows = cells.shape[0]
     right, left = dft_tables(order)
     wide_cols = 2 * order
     fill_cols = 2048
     bf16, f32 = jnp.bfloat16, jnp.float32
-    return pl.pallas_call(
-        slot_kernel,
-        out_shape=(
-            jax.ShapeDtypeStruct((total_rows, wide_cols), bf16),
-            jax.ShapeDtypeStruct((order // 2, wide_cols), f32),
-            jax.ShapeDtypeStruct((order // 2, wide_cols), bf16),
-            jax.ShapeDtypeStruct((2, tile_rows, tile_cols), f32),
-        ),
-        in_specs=[SMEM, SMEM, VMEM, VMEM, VMEM, VMEM, VMEM],
-        out_specs=(VMEM, VMEM, VMEM, ANY),
+    *backs, empty = pl.pallas_call(
+        functools.partial(slot_kernel, chunks),
+        out_shape=tuple(
+            jax.ShapeDtypeStruct((total_rows, 2 * (high - low)), bf16) for low, high in chunks
+        )
+        + (jax.ShapeDtypeStruct((2, tile_rows, tile_cols), f32),),
+        in_specs=[SMEM, SMEM, VMEM, VMEM, VMEM, ANY, ANY],
+        out_specs=(VMEM,) * len(chunks) + (ANY,),
         scratch_shapes=[
             pltpu.VMEM((total_rows + SUBLANES, wide_cols), f32),
-            pltpu.VMEM((order, wide_cols), bf16),
             pltpu.VMEM((order, wide_cols), bf16),
             pltpu.VMEM((wide_cols, order), bf16),
             pltpu.VMEM((order, wide_cols), bf16),
             pltpu.VMEM((wide_cols, order), bf16),
             pltpu.VMEM((2 * total_rows - order + SUBLANES, wide_cols), f32),
-            pltpu.VMEM((order, wide_cols), f32),
             pltpu.VMEM((2, tile_rows, fill_cols), f32),
+            pltpu.VMEM((wide_cols, wide_cols), bf16),
+            pltpu.VMEM((wide_cols, wide_cols), bf16),
             pltpu.SemaphoreType.DMA((tile_cols // fill_cols,)),
+            pltpu.SemaphoreType.DMA((2,)),
         ],
         compiler_params=pltpu.CompilerParams(vmem_limit_bytes=40 * 2**20),
         cost_estimate=pl.CostEstimate(
@@ -223,6 +217,53 @@
         ),
         name="slot",
     )(dealing, rows, cells, probe, measured, jnp.asarray(right), jnp.asarray(left))
+    return backs, empty
+
+
+def partial_kernel(reach, own_rows, shifts, low, dealing, rows, pieces, back, *out):
+    *parts, total = out
+    slots, tile_rows = back.shape[0], back.shape[1]
+    width = back.shape[2] // 2
+    order = pieces.shape[2] // 2
+    count = tile_rows // SUBLANES
+    total[...] = jnp.zeros_like(total)
+    sub = lax.broadcasted_iota(jnp.int32, (1, SUBLANES, 2 * width), 1)
+    nothing = jnp.zeros((1, SUBLANES, 2 * width), jnp.float32)
+
+    @pl.loop(0, slots, unroll=2)
+    def _(slot):
+        start = (shifts - 1) * own_rows - rows[dealing[slot]]
+        aligned = pl.multiple_of(start // SUBLANES * SUBLANES, SUBLANES)
+        rest = start - aligned
+        patch_real = pieces[slot, :, low : low + width].astype(jnp.float32)
+        patch_imag = pieces[slot, :, order + low : order + low + width].astype(jnp.float32)
+        real = back[slot, :, :width].astype(jnp.float32)
+        imag = back[slot, :, width:].astype(jnp.float32)
+        terms = jnp.concatenate(
+            [patch_real * real + patch_imag * imag, patch_real * imag - patch_imag * real], axis=1
+        )
+        turned = pltpu.roll(terms.reshape(count, SUBLANES, 2 * width), rest, 1)
+        before = jnp.concatenate([nothing, turned], axis=0)
+        after = jnp.concatenate([turned, nothing], axis=0)
+        moved = jnp.where(sub < rest, before, after).reshape(tile_rows + SUBLANES, 2 * width)
+        total[pl.ds(aligned, tile_rows + SUBLANES), :] += moved
+
+    for e, part in enumerate(parts):
+        part[...] = total[e * own_rows : (e + 1) * own_rows, :].astype(part.dtype)
+
+
+def probe_partials(pieces, back, dealing, rows, own_rows, reach, shifts, low, dtypes):
+    tile_rows, wide = back.shape[1], back.shape[2]
+    return pl.pallas_call(
+        functools.partial(partial_kernel, reach, own_rows, shifts, low),
+        out_shape=tuple(jax.ShapeDtypeStruct((own_rows, wide), dtype) for dtype in dtypes),
+        in_specs=[SMEM, SMEM, VMEM, VMEM],
+        out_specs=(VMEM,) * len(dtypes),
+        scratch_shapes=[pltpu.VMEM((shifts * own_rows + tile_rows + SUBLANES, wide), jnp.float32)],
+        compiler_params=pltpu.CompilerParams(vmem_limit_bytes=16 * 2**20),
+        cost_estimate=pl.CostEstimate(flops=0, bytes_accessed=4 * 2**20, transcendentals=0),
+        name="partial",
+    )(dealing, rows, pieces, back)
 
 
 def block_places(dealing, cols, order, tile_cols):
@@ -233,28 +274,43 @@
     return blocks, jnp.argmax(same, axis=1).astype(jnp.int32)
 
 
-def place_kernel(order, dealing, cols, blocks, owners, terms, empty, out, totals, sems):
+def place_kernel(
+    order, own_rows, top, chunks, dealing, rows, cols, blocks, owners, probe, *rest
+):
+    backs, (empty, out, totals, spread, sems) = rest[: len(chunks)], rest[len(chunks) :]
     del empty
-    slots, tile_rows = terms.shape[0], terms.shape[1]
-    tile_cols = out.shape[2]
+    slots, tile_rows = backs[0].shape[0], backs[0].shape[1]
     count = (order + LANES) // LANES
+    me = lax.axis_index("row")
+    spread[0:top, :] = jnp.zeros((top, 2 * order), jnp.float32)
+    spread[top : top + order, :order] = probe[0].astype(jnp.float32)
+    spread[top : top + order, order:] = probe[1].astype(jnp.float32)
+    spread[top + order :, :] = jnp.zeros((spread.shape[0] - top - order, 2 * order), jnp.float32)
     totals[...] = jnp.zeros_like(totals)
     lane = lax.broadcasted_iota(jnp.int32, (tile_rows, LANES), 1)
 
     @pl.loop(0, slots, unroll=2)
     def _(slot):
-        _, offset = window_start(cols[dealing[slot]], order, tile_cols)
+        _, offset = window_start(cols[dealing[slot]], order, out.shape[2])
         shift = lax.rem(offset, LANES)
-        for part in range(2):
-            turned = []
-            for b in range(count - 1):
-                first = part * order + b * LANES
-                turned.append(pltpu.roll(terms[slot, :, first : first + LANES].astype(jnp.float32), shift, 1))
-            nothing = jnp.zeros_like(turned[0])
-            for b in range(count):
-                before = turned[b - 1] if b else nothing
-                after = turned[b] if b < count - 1 else nothing
-                owner = owners[slot * count + b]
+        around = rows_from(spread, top + me * own_rows - rows[dealing[slot]], tile_rows)
+        turned = [[], []]
+        for back, (low, high) in zip(backs, chunks):
+            for first in range(low, high, LANES):
+                here = slice(first - low, first - low + LANES)
+                there = slice(high - low + first - low, high - low + first - low + LANES)
+                real = back[slot, :, here].astype(jnp.float32)
+                imag = back[slot, :, there].astype(jnp.float32)
+                probe_real = around[:, first : first + LANES]
+                probe_imag = around[:, order + first : order + first + LANES]
+                turned[0].append(pltpu.roll(probe_real * real + probe_imag * imag, shift, 1))
+                turned[1].append(pltpu.roll(probe_real * imag - probe_imag * real, shift, 1))
+        nothing = jnp.zeros((tile_rows, LANES), jnp.float32)
+        for b in range(count):
+            owner = owners[slot * count + b]
+            for part in range(2):
+                before = turned[part][b - 1] if b else nothing
+                after = turned[part][b] if b < count - 1 else nothing
                 totals[owner, part] += jnp.where(lane < offset, before, after)
 
     def copy(number):
@@ -274,26 +330,29 @@
             copy(number).wait()
 
 
-def place_windows(terms, empty, dealing, cols, order):
-
-    slots, tile_rows = terms.shape[0], terms.shape[1]
+def place_windows(backs, empty, probe, dealing, rows, cols, own_rows, total_rows, chunks):
+    order = probe.shape[1]
+    slots, tile_rows = backs[0].shape[0], backs[0].shape[1]
     tile_cols = empty.shape[2]
     count = (order + LANES) // LANES
     blocks, owners = block_places(dealing, cols, order, tile_cols)
+    top = -(-(total_rows - order) // SUBLANES) * SUBLANES
+    spread_rows = -(-(top + total_rows) // SUBLANES) * SUBLANES + tile_rows + SUBLANES
     return pl.pallas_call(
-        functools.partial(place_kernel, order),
+        functools.partial(place_kernel, order, own_rows, top, chunks),
         out_shape=jax.ShapeDtypeStruct(empty.shape, empty.dtype),
-        in_specs=[SMEM, SMEM, SMEM, SMEM, VMEM, ANY],
+        in_specs=[SMEM, SMEM, SMEM, SMEM, SMEM, VMEM] + [VMEM] * len(backs) + [ANY],
         out_specs=ANY,
         scratch_shapes=[
             pltpu.VMEM((slots * count, 2, tile_rows, LANES), jnp.float32),
+            pltpu.VMEM((spread_rows, 2 * order), jnp.float32),
             pltpu.SemaphoreType.DMA((slots * count,)),
         ],
-        input_output_aliases={5: 0},
+        input_output_aliases={6 + len(backs): 0},
         compiler_params=pltpu.CompilerParams(vmem_limit_bytes=24 * 2**20),
         cost_estimate=pl.CostEstimate(flops=0, bytes_accessed=6 * 2**20, transcendentals=0),
         name="place",
-    )(dealing, cols, blocks, owners, terms, empty)
+    )(dealing, rows, cols, blocks, owners, probe, *backs, empty)
 
 
 def strides(devices):
@@ -313,61 +372,91 @@
     return lax.ppermute(x, "row", pairs)
 
 
-def sum_probe(kept, sent, devices, scale):
+def join(whole, devices):
     me = lax.axis_index("row")
-    steps = strides(devices)
-    total = kept + turn(sent, 1, 2, 1, devices).astype(jnp.float32)
-    for stride, radix in steps[1:]:
-        digit = me // stride % radix
-        count = total.shape[0] // radix
-        own = lax.dynamic_slice_in_dim(total, digit * count, count)
-        for distance in range(1, radix):
-            other = lax.rem(digit + distance, radix)
-            share = lax.dynamic_slice_in_dim(total, other * count, count).astype(jnp.bfloat16)
-            own = own + turn(share, stride, radix, distance, devices).astype(jnp.float32)
-        total = own
-    whole = (total * scale).astype(jnp.bfloat16)
-    for stride, radix in reversed(steps):
+    rows, width = whole.shape
+    for axis, (stride, radix) in enumerate(reversed(strides(devices))):
         digit = me // stride % radix
         shares = [whole] + [turn(whole, stride, radix, distance, devices) for distance in range(1, radix)]
-        order = [lax.rem(digit - k + radix, radix) for k in range(radix)]
-        rows = []
+        pieces = []
         for k in range(radix):
+            distance = lax.rem(digit - k + radix, radix)
             piece = shares[0]
             for d in range(1, radix):
-                piece = jnp.where(order[k] == d, shares[d], piece)
-            rows.append(piece)
-        whole = jnp.concatenate(rows, axis=0)
-    return whole
+                piece = jnp.where(distance == d, shares[d], piece)
+            pieces.append(piece)
+        whole = jnp.stack(pieces, axis=axis)
+    return whole.reshape(devices * rows, width)
+
+
+def sum_probe(pieces, back, dealing, rows, own_rows, reach, low, devices):
+    order = pieces.shape[2] // 2
+    scale = 1.0 / dealing.shape[0]
+    shifts = -(-reach // own_rows) + 1
+    held = -(-order // own_rows)
+    middle = (shifts - 1) // 2
+    own = shifts - 1 - middle
+    direct = shifts <= 8
+    dtypes = [jnp.bfloat16 if direct and e != own else jnp.float32 for e in range(shifts)]
+    parts = probe_partials(pieces, back, dealing, rows, own_rows, reach, shifts, low, dtypes)
+    if direct:
+        total = parts[own]
+        for e in range(shifts):
+            if e != own:
+                pairs = [
+                    (d, d - shifts + 1 + e + middle)
+                    for d in range(devices)
+                    if 0 <= d - shifts + 1 + e < held
+                ]
+                total = total + lax.ppermute(parts[e], "row", pairs).astype(jnp.float32)
+        whole = join((total * scale).astype(jnp.bfloat16), devices)
+        first = middle * own_rows
+    else:
+        spread = jnp.zeros(((devices + shifts) * own_rows, back.shape[2]), jnp.float32)
+        start = lax.axis_index("row") * own_rows
+        spread = lax.dynamic_update_slice(spread, jnp.concatenate(parts, axis=0), (start, 0))
+        first = (shifts - 1) * own_rows
+        whole = lax.psum(spread, "row") * scale
+    return whole[first : first + order].astype(jnp.float32)
 
 
 def body(object_field, probe, amplitude, row_offsets, col_offsets, dealing):
     order = probe.shape[1]
     devices = lax.axis_size("row")
     own_rows, tile_cols = object_field.shape[1], object_field.shape[2]
+    total_rows = devices * own_rows
     tile_rows = -(-own_rows // SUBLANES) * SUBLANES
     spare = tile_rows - own_rows
+    cut = order // LANES * 3 // 4 * LANES
+    chunks = ((0, cut), (cut, order))
     if spare:
         object_field = jnp.pad(object_field, ((0, 0), (0, spare), (0, 0)))
     pieces = fetch_windows(object_field, dealing, col_offsets, order)
     strips = lax.all_to_all(pieces, "row", split_axis=0, concat_axis=0, tiled=True)
-    cells = strips[:, :own_rows].reshape(devices * own_rows, 2 * order)
-    terms, kept, sent, empty = slot_terms(
-        cells, probe, amplitude, dealing, row_offsets, tile_rows, tile_cols
+    cells = strips[:, :own_rows].reshape(total_rows, 2 * order)
+    backs, empty = slot_backs(
+        cells, probe, amplitude, dealing, row_offsets, tile_rows, tile_cols, chunks
     )
-    outgoing = terms.reshape(devices, own_rows, 2 * order)
-    if spare:
-        outgoing = jnp.pad(outgoing, ((0, 0), (0, spare), (0, 0)))
-    arrived = lax.all_to_all(outgoing, "row", split_axis=0, concat_axis=0, tiled=True)
-    rounds = jnp.minimum(dealing[0] + 1, 1)
-    _, whole = lax.while_loop(
-        lambda state: state[0] < rounds,
-        lambda state: (state[0] + 1, sum_probe(kept, sent, devices, 1.0 / dealing.shape[0])),
-        (jnp.zeros((), jnp.int32), jnp.zeros((order, 2 * order), jnp.bfloat16)),
+    arrived, sums = [], []
+    for back, (low, high) in zip(backs, chunks):
+        outgoing = back.reshape(devices, own_rows, 2 * (high - low))
+        if spare:
+            outgoing = jnp.pad(outgoing, ((0, 0), (0, spare), (0, 0)))
+        arrived.append(lax.all_to_all(outgoing, "row", split_axis=0, concat_axis=0, tiled=True))
+    for here, (low, high) in zip(arrived, chunks):
+        sums.append(
+            sum_probe(pieces, here, dealing, row_offsets, own_rows, total_rows - order, low, devices)
+        )
+    widths = [high - low for low, high in chunks]
+    probe_grad = jnp.stack(
+        [
+            jnp.concatenate([total[:, :width] for total, width in zip(sums, widths)], axis=1),
+            jnp.concatenate([total[:, width:] for total, width in zip(sums, widths)], axis=1),
+        ]
     )
-    whole = whole.astype(jnp.float32)
-    probe_grad = jnp.stack([whole[:, :order], whole[:, order:]])
-    object_grad = place_windows(arrived, empty, dealing, col_offsets, order)
+    object_grad = place_windows(
+        arrived, empty, probe, dealing, row_offsets, col_offsets, own_rows, total_rows, chunks
+    )
     if spare:
         object_grad = object_grad[:, :own_rows]
     return (object_grad, probe_grad)

time: 125 us -> 146 us (1.17)
  the two profiles are of different devices: /device:TPU:15 before, /device:TPU:0 now
where the time goes in v3:
time: 146 us
  blocking collectives  54 us (37%)
  starting transfers between devices  50.8 us (35%)
  Pallas kernels  19.4 us (13%)
  waiting for transfers between devices  14.3 us (10%)
  other arithmetic  3.2 us (2%)
  local copies, waits for them, and re-layouts  2.91 us (2%)
    all_to_all x1, blocking collectives, body(): lax.all_to_all(pieces, 'row', split_axis=0, concat_axis=0, tiled=True)  39 us
    ppermute x10, starting transfers between devices, turn(): return lax.ppermute(x, 'row', pairs)  37 us
    all_to_all x1, blocking collectives, body(): lax.all_to_all(outgoing, 'row', split_axis=0, concat_axis=0, tiled=True)  15 us
    ppermute x10, waiting for transfers between devices, turn(): return lax.ppermute(x, 'row', pairs)  14.3 us
    ppermute x8, starting transfers between devices, sum_probe(): total = total + lax.ppermute(parts[e], 'row', pairs).astype(jnp.float32)  10.1 us
    pallas_call x1, Pallas kernels, slot_backs(): pl.pallas_call(functools.partial(slot_kernel, chunks), out_shape=tuple((j...  7.1 us
    pallas_call x1, Pallas kernels, fetch_windows(): pl.pallas_call(functools.partial(fetch_kernel, order), out_shape=jax.Shap...  5.14 us
    pallas_call x1, Pallas kernels, place_windows(): pl.pallas_call(functools.partial(place_kernel, order, own_rows, top, chun...  4.91 us
  transfers between devices with their start and end apart: 19, of which 6 were waited for; matrix products, arithmetic and copies ran while one was open for 1% of the time, Pallas kernels for 5%

profile of v3, /device:TPU:0, one launch (start us, length us, event | category | flops | bytes accessed | tf_op | source)
XLA Modules:
  0.0 145.8 jit_solution(4077789868840455912)
XLA Ops:
  0.6 0.0 copy-start.8
  0.6 0.0 copy-start.9
  0.7 5.1 %fetch.1.pieces = bf16[16,40,1024]{2,1,0:T(8,128)(2,1)} custom-call(s32[16]{0:T(128)} %dealing.9, s32[16]{0:T(128)} %cols.3, f32[2,40,32768]{2,1,0:T(8,128)} %tile.1), custom_call_target="tpu_custom_call" | custom-call | bytes 6291456 | tf_op jit(solution)/shard_map/fetch/pallas_call | solution.py:84
  5.8 0.0 copy-start.2
  5.8 0.0 copy-start.5
  5.8 0.0 copy-start.6
  5.8 0.0 copy-start.7
  5.9 39.0 %all_to_all.15 = bf16[16,40,1024]{2,1,0:T(8,128)(2,1)S(1)} all-to-all(bf16[16,40,1024]{2,1,0:T(8,128)(2,1)} %fetch.1.pieces), channel_id=1, replica_groups=mesh['groups'=2,'row'=16] {'row'}, dimensions={0} | all-to-all | bytes 2621440 | tf_op jit(solution)/shard_map/all_to_all | solution.py:435
  44.9 7.1 %slot.1 = (bf16[640,768]{1,0:T(8,128)(2,1)S(1)}, bf16[640,256]{1,0:T(8,128)(2,1)S(1)}, f32[2,40,32768]{2,1,0:T(8,128)}) custom-call(s32[16]{0:T(128)S(1)} %copy-done.5, s32[16]{0:T(128)S(1)} %copy-done.6, bf16[640,1024]{1,0:T(8,128)(2,1)S(1)} %bitcast.41, bf16[2,512,512]{2,1,0:T(8,128)(2,1)S(1)} %copy-done.2, bf16[1,512,512]{2,1,0:T(8,128)(2,1)S(1)} %copy-done.7, ...), custom_call_target="tpu_custom_call" | custom-call | flops 4294967296 | bytes 20971520 | tf_op jit(solution)/shard_map/slot/pallas_call | solution.py:193
  52.1 1.0 copy-done.4
  53.0 15.0 %all_to_all.16.rest_1_.back = bf16[16,40,256]{2,1,0:T(8,128)(2,1)S(1)} all-to-all(bf16[16,40,256]{2,1,0:T(8,128)(2,1)S(1)} %bitcast.43), channel_id=1, replica_groups=mesh['groups'=2,'row'=16] {'row'}, dimensions={0} | all-to-all | bytes 655360 | tf_op jit(solution)/shard_map/all_to_all | solution.py:445
  68.0 3.6 %all-to-all-start.1 = ((bf16[16,40,768]{2,1,0:T(8,128)(2,1)}), bf16[16,40,768]{2,1,0:T(8,128)(2,1)S(1)}, u32[]{:S(2)}, u32[]{:S(2)}) async-start(bf16[16,40,768]{2,1,0:T(8,128)(2,1)} %bitcast.42), calls=%async_computation.1 | async-start | bytes 1966080 | tf_op jit(solution)/shard_map/all_to_all | solution.py:445
  71.7 0.8 partial.3
  72.5 3.7 %collective-permute-start.12 = (bf16[40,256]{1,0:T(8,128)(2,1)S(1)}, bf16[40,256]{1,0:T(8,128)(2,1)S(1)}, u32[]{:S(2)}, u32[]{:S(2)}) collective-permute-start(bf16[40,256]{1,0:T(8,128)(2,1)S(1)} %get-tuple-element.29), channel_id=1, source_target_pairs={{0,2},{1,3},{2,4},{3,5},{4,6},{5,7},{6,8},{7,9},{8,10},{9,11},{10,... | collective-permute-start | bytes 61448 | tf_op jit(solution)/shard_map/ppermute | solution.py:411
  76.3 0.7 collective-permute-start.11
  76.9 0.7 collective-permute-start.10
  77.6 0.7 collective-permute-start.9
  78.3 0.7 gather_fusion
  78.9 0.0 collective-permute-done.12
  79.0 0.0 collective-permute-done.11
  79.0 0.0 collective-permute-done.10
  79.0 0.0 collective-permute-done.9
  79.0 13.8 %collective-permute-start.13 = (bf16[40,256]{1,0:T(8,128)(2,1)S(1)}, bf16[40,256]{1,0:T(8,128)(2,1)S(1)}, u32[]{:S(2)}, u32[]{:S(2)}) collective-permute-start(bf16[40,256]{1,0:T(8,128)(2,1)S(1)} %multiply_convert_fusion.1), channel_id=1, source_target_pairs={{0,12},{1,13},{2,14},{3,15},{4,0},{5,1},{6,2},{7,3},{8,4},{9,5},{1... | collective-permute-start | bytes 61448 | tf_op jit(solution)/shard_map/ppermute | solution.py:372
  92.8 6.7 %collective-permute-start.14 = (bf16[40,256]{1,0:T(8,128)(2,1)S(1)}, bf16[40,256]{1,0:T(8,128)(2,1)S(1)}, u32[]{:S(2)}, u32[]{:S(2)}) collective-permute-start(bf16[40,256]{1,0:T(8,128)(2,1)S(1)} %multiply_convert_fusion.1), channel_id=1, source_target_pairs={{0,8},{1,9},{2,10},{3,11},{4,12},{5,13},{6,14},{7,15},{8,0},{9,1},... | collective-permute-start | bytes 61448 | tf_op jit(solution)/shard_map/ppermute | solution.py:372
  99.5 1.9 %collective-permute-start.15 = (bf16[40,256]{1,0:T(8,128)(2,1)S(1)}, bf16[40,256]{1,0:T(8,128)(2,1)S(1)}, u32[]{:S(2)}, u32[]{:S(2)}) collective-permute-start(bf16[40,256]{1,0:T(8,128)(2,1)S(1)} %multiply_convert_fusion.1), channel_id=1, source_target_pairs={{0,4},{1,5},{2,6},{3,7},{4,8},{5,9},{6,10},{7,11},{8,12},{9,13},{1... | collective-permute-start | bytes 61448 | tf_op jit(solution)/shard_map/ppermute | solution.py:372
  101.5 0.0 collective-permute-done.13
  101.5 0.1 collective-permute-done.14
  101.6 3.5 %collective-permute-done.15 = bf16[40,256]{1,0:T(8,128)(2,1)S(1)} collective-permute-done((bf16[40,256]{1,0:T(8,128)(2,1)S(1)}, bf16[40,256]{1,0:T(8,128)(2,1)S(1)}, u32[]{:S(2)}, u32[]{:S(2)}) %collective-permute-start.15) | collective-permute-done | bytes 20512 | tf_op jit(solution)/shard_map/ppermute | solution.py:372
  105.1 1.6 %collective-permute-start.16 = (bf16[4,40,256]{2,1,0:T(8,128)(2,1)S(1)}, bf16[4,40,256]{2,1,0:T(8,128)(2,1)S(1)}, u32[]{:S(2)}, u32[]{:S(2)}) collective-permute-start(bf16[4,40,256]{2,1,0:T(8,128)(2,1)S(1)} %pad_maximum_fusion.6), channel_id=1, source_target_pairs={{0,2},{1,3},{2,0},{3,1},{4,6},{5,7},{6,4},{7,5},{8,10},{9,11},{10,... | collective-permute-start | bytes 245768 | tf_op jit(solution)/shard_map/ppermute | solution.py:372
  106.7 0.1 iota_add_fusion
  106.7 0.1 add.130.blocks
  106.8 0.0 all-to-all-done.1.rest_0_.back
  106.8 1.4 partial.2
  108.2 2.4 %collective-permute-start.3 = (bf16[40,768]{1,0:T(8,128)(2,1)S(1)}, bf16[40,768]{1,0:T(8,128)(2,1)S(1)}, u32[]{:S(2)}, u32[]{:S(2)}) collective-permute-start(bf16[40,768]{1,0:T(8,128)(2,1)S(1)} %get-tuple-element.24), channel_id=1, source_target_pairs={{0,2},{1,3},{2,4},{3,5},{4,6},{5,7},{6,8},{7,9},{8,10},{9,11},{10,... | collective-permute-start | bytes 184328 | tf_op jit(solution)/shard_map/ppermute | solution.py:411
  110.7 0.7 collective-permute-start.2
  111.3 0.7 collective-permute-start.1
  112.0 0.7 collective-permute-start
  112.7 0.0 collective-permute-done.16
  112.7 0.0 collective-permute-done.3
  112.7 0.0 collective-permute-done.2
  112.8 0.0 collective-permute-done.1
  112.8 0.0 collective-permute-done
  112.8 11.0 %collective-permute-start.4 = (bf16[40,768]{1,0:T(8,128)(2,1)S(1)}, bf16[40,768]{1,0:T(8,128)(2,1)S(1)}, u32[]{:S(2)}, u32[]{:S(2)}) collective-permute-start(bf16[40,768]{1,0:T(8,128)(2,1)S(1)} %multiply_convert_fusion), channel_id=1, source_target_pairs={{0,12},{1,13},{2,14},{3,15},{4,0},{5,1},{6,2},{7,3},{8,4},{9,5},{1... | collective-permute-start | bytes 184328 | tf_op jit(solution)/shard_map/ppermute | solution.py:372
  123.9 1.1 collective-permute-start.5
  125.0 0.2 collective-permute-start.6
  125.2 0.1 collective-permute-start.17
  125.3 0.4 collective-permute-done.4
  125.8 3.2 %collective-permute-done.5 = bf16[40,768]{1,0:T(8,128)(2,1)S(1)} collective-permute-done((bf16[40,768]{1,0:T(8,128)(2,1)S(1)}, bf16[40,768]{1,0:T(8,128)(2,1)S(1)}, u32[]{:S(2)}, u32[]{:S(2)}) %collective-permute-start.5) | collective-permute-done | bytes 61472 | tf_op jit(solution)/shard_map/ppermute | solution.py:372
  129.0 2.0 %collective-permute-done.6 = bf16[40,768]{1,0:T(8,128)(2,1)S(1)} collective-permute-done((bf16[40,768]{1,0:T(8,128)(2,1)S(1)}, bf16[40,768]{1,0:T(8,128)(2,1)S(1)}, u32[]{:S(2)}, u32[]{:S(2)}) %collective-permute-start.6) | collective-permute-done | bytes 61472 | tf_op jit(solution)/shard_map/ppermute | solution.py:372
  131.1 0.5 collective-permute-start.7
  131.6 0.7 iota_reduce_fusion
  132.3 5.0 %collective-permute-done.7 = bf16[4,40,768]{2,1,0:T(8,128)(2,1)S(1)} collective-permute-done((bf16[4,40,768]{2,1,0:T(8,128)(2,1)S(1)}, bf16[4,40,768]{2,1,0:T(8,128)(2,1)S(1)}, u32[]{:S(2)}, u32[]{:S(2)}) %collective-permute-start.7) | collective-permute-done | bytes 245792 | tf_op jit(solution)/shard_map/ppermute | solution.py:372
  137.4 0.1 select_bitcast_fusion.3
  137.4 0.0 copy-start.3
  137.5 0.1 collective-permute-start.8
  137.7 0.9 copy-done.3
  138.7 4.9 %place.1 = f32[2,40,32768]{2,1,0:T(8,128)} custom-call(s32[16]{0:T(128)S(1)} %copy-done.5, s32[16]{0:T(128)S(1)} %copy-done.6, s32[16]{0:T(128)S(1)} %copy-done, s32[80]{0:T(128)S(1)} %add.130.blocks, s32[80]{0:T(128)S(1)} %get-tuple-element.16.owners, bf16[2,512,512]{2,1,0:T(8,128)(2,1)S(1)} %copy-done.3, ...), custom_call_target="tpu_custom_call", output_to_operand_aliasing={{}: (8, {})} | custom-call | bytes 6291456 | tf_op jit(solution)/shard_map/place/pallas_call | solution.py:341
  143.6 0.1 select_bitcast_fusion.1
  143.7 0.1 pad_maximum_fusion.1
  143.8 0.1 copy.13
  143.8 0.1 slice_convert_fusion
  144.0 0.1 fusion
  144.1 0.2 maximum_bitcast_fusion
  144.3 1.5 %pad_maximum_fusion = f32[2,512,512]{2,1,0:T(8,128)} fusion(f32[1,512,512]{2,1,0:T(8,128)S(1)} %get-tuple-element.51, f32[1,512,512]{2,1,0:T(8,128)S(1)} %get-tuple-element.50), kind=kLoop, calls=%fused_computation.1 | loop fusion | flops 524288 | bytes 4194304 | tf_op jit(solution)/shard_map/stack | solution.py:451
  (30 shorter events, 0.5 us)
Async XLA Ops:
  0.6 44.3 %copy-start.8 = (bf16[1024,1024]{1,0:T(8,128)(2,1)S(1)}, bf16[1024,1024]{1,0:T(8,128)(2,1)}, u32[]{:S(2)}) copy-start(bf16[1024,1024]{1,0:T(8,128)(2,1)} %constant.139.clone.right_table) | copy-start | bytes 6291460
  0.6 44.3 %copy-start.9 = (bf16[1024,1024]{1,0:T(8,128)(2,1)S(1)}, bf16[1024,1024]{1,0:T(8,128)(2,1)}, u32[]{:S(2)}) copy-start(bf16[1024,1024]{1,0:T(8,128)(2,1)} %constant.140.clone.left_table) | copy-start | bytes 6291460
  5.8 39.1 %copy-start.2 = (bf16[2,512,512]{2,1,0:T(8,128)(2,1)S(1)}, bf16[2,512,512]{2,1,0:T(8,128)(2,1)}, u32[]{:S(2)}) copy-start(bf16[2,512,512]{2,1,0:T(8,128)(2,1)} %probe.3) | copy-start | bytes 3145732
  5.8 39.1 %copy-start.5 = (s32[16]{0:T(128)S(1)}, s32[16]{0:T(128)}, u32[]{:S(2)}) copy-start(s32[16]{0:T(128)} %dealing.9) | copy-start | bytes 196
  5.8 39.1 %copy-start.6 = (s32[16]{0:T(128)S(1)}, s32[16]{0:T(128)}, u32[]{:S(2)}) copy-start(s32[16]{0:T(128)} %rows.7) | copy-start | bytes 196
  5.8 39.1 %copy-start.7 = (bf16[1,512,512]{2,1,0:T(8,128)(2,1)S(1)}, bf16[1,512,512]{2,1,0:T(8,128)(2,1)}, u32[]{:S(2)}) copy-start(bf16[1,512,512]{2,1,0:T(8,128)(2,1)} %measured.1) | copy-start | bytes 1572868
  52.1 1.0 copy-start.4
  53.0 18.7 %copy-start.1 = (bf16[16,40,1024]{2,1,0:T(8,128)(2,1)S(1)}, bf16[16,40,1024]{2,1,0:T(8,128)(2,1)}, u32[]{:S(2)}) copy-start(bf16[16,40,1024]{2,1,0:T(8,128)(2,1)} %fetch.1.pieces) | copy-start | bytes 3932164
  53.0 25.3 %copy-start = (s32[16]{0:T(128)S(1)}, s32[16]{0:T(128)}, u32[]{:S(2)}) copy-start(s32[16]{0:T(128)} %cols.3) | copy-start | bytes 196
  68.0 38.8 %all-to-all-start.1 = ((bf16[16,40,768]{2,1,0:T(8,128)(2,1)}), bf16[16,40,768]{2,1,0:T(8,128)(2,1)S(1)}, u32[]{:S(2)}, u32[]{:S(2)}) async-start(bf16[16,40,768]{2,1,0:T(8,128)(2,1)} %bitcast.42), calls=%async_computation.1 | async-start | bytes 1966080 | tf_op jit(solution)/shard_map/all_to_all | solution.py:445
  72.5 6.4 %collective-permute-start.12 = (bf16[40,256]{1,0:T(8,128)(2,1)S(1)}, bf16[40,256]{1,0:T(8,128)(2,1)S(1)}, u32[]{:S(2)}, u32[]{:S(2)}) collective-permute-start(bf16[40,256]{1,0:T(8,128)(2,1)S(1)} %get-tuple-element.29), channel_id=1, source_target_pairs={{0,2},{1,3},{2,4},{3,5},{4,6},{5,7},{6,8},{7,9},{8,10},{9,11},{10,... | collective-permute-start | bytes 61448 | tf_op jit(solution)/shard_map/ppermute | solution.py:411
  76.3 2.7 %collective-permute-start.11 = (bf16[40,256]{1,0:T(8,128)(2,1)S(1)}, bf16[40,256]{1,0:T(8,128)(2,1)S(1)}, u32[]{:S(2)}, u32[]{:S(2)}) collective-permute-start(bf16[40,256]{1,0:T(8,128)(2,1)S(1)} %get-tuple-element.28), channel_id=1, source_target_pairs={{1,2},{2,3},{3,4},{4,5},{5,6},{6,7},{7,8},{8,9},{9,10},{10,11},{11... | collective-permute-start | bytes 61448 | tf_op jit(solution)/shard_map/ppermute | solution.py:411
  76.9 2.0 %collective-permute-start.10 = (bf16[40,256]{1,0:T(8,128)(2,1)S(1)}, bf16[40,256]{1,0:T(8,128)(2,1)S(1)}, u32[]{:S(2)}, u32[]{:S(2)}) collective-permute-start(bf16[40,256]{1,0:T(8,128)(2,1)S(1)} %get-tuple-element.27), channel_id=1, source_target_pairs={{3,2},{4,3},{5,4},{6,5},{7,6},{8,7},{9,8},{10,9},{11,10},{12,11},{... | collective-permute-start | bytes 61448 | tf_op jit(solution)/shard_map/ppermute | solution.py:411
  77.6 1.4 collective-permute-start.9
  79.0 22.5 %collective-permute-start.13 = (bf16[40,256]{1,0:T(8,128)(2,1)S(1)}, bf16[40,256]{1,0:T(8,128)(2,1)S(1)}, u32[]{:S(2)}, u32[]{:S(2)}) collective-permute-start(bf16[40,256]{1,0:T(8,128)(2,1)S(1)} %multiply_convert_fusion.1), channel_id=1, source_target_pairs={{0,12},{1,13},{2,14},{3,15},{4,0},{5,1},{6,2},{7,3},{8,4},{9,5},{1... | collective-permute-start | bytes 61448 | tf_op jit(solution)/shard_map/ppermute | solution.py:372
  92.8 8.8 %collective-permute-start.14 = (bf16[40,256]{1,0:T(8,128)(2,1)S(1)}, bf16[40,256]{1,0:T(8,128)(2,1)S(1)}, u32[]{:S(2)}, u32[]{:S(2)}) collective-permute-start(bf16[40,256]{1,0:T(8,128)(2,1)S(1)} %multiply_convert_fusion.1), channel_id=1, source_target_pairs={{0,8},{1,9},{2,10},{3,11},{4,12},{5,13},{6,14},{7,15},{8,0},{9,1},... | collective-permute-start | bytes 61448 | tf_op jit(solution)/shard_map/ppermute | solution.py:372
  99.5 5.6 %collective-permute-start.15 = (bf16[40,256]{1,0:T(8,128)(2,1)S(1)}, bf16[40,256]{1,0:T(8,128)(2,1)S(1)}, u32[]{:S(2)}, u32[]{:S(2)}) collective-permute-start(bf16[40,256]{1,0:T(8,128)(2,1)S(1)} %multiply_convert_fusion.1), channel_id=1, source_target_pairs={{0,4},{1,5},{2,6},{3,7},{4,8},{5,9},{6,10},{7,11},{8,12},{9,13},{1... | collective-permute-start | bytes 61448 | tf_op jit(solution)/shard_map/ppermute | solution.py:372
  105.1 7.6 %collective-permute-start.16 = (bf16[4,40,256]{2,1,0:T(8,128)(2,1)S(1)}, bf16[4,40,256]{2,1,0:T(8,128)(2,1)S(1)}, u32[]{:S(2)}, u32[]{:S(2)}) collective-permute-start(bf16[4,40,256]{2,1,0:T(8,128)(2,1)S(1)} %pad_maximum_fusion.6), channel_id=1, source_target_pairs={{0,2},{1,3},{2,0},{3,1},{4,6},{5,7},{6,4},{7,5},{8,10},{9,11},{10,... | collective-permute-start | bytes 245768 | tf_op jit(solution)/shard_map/ppermute | solution.py:372
  108.2 4.5 %collective-permute-start.3 = (bf16[40,768]{1,0:T(8,128)(2,1)S(1)}, bf16[40,768]{1,0:T(8,128)(2,1)S(1)}, u32[]{:S(2)}, u32[]{:S(2)}) collective-permute-start(bf16[40,768]{1,0:T(8,128)(2,1)S(1)} %get-tuple-element.24), channel_id=1, source_target_pairs={{0,2},{1,3},{2,4},{3,5},{4,6},{5,7},{6,8},{7,9},{8,10},{9,11},{10,... | collective-permute-start | bytes 184328 | tf_op jit(solution)/shard_map/ppermute | solution.py:411
  110.7 2.1 %collective-permute-start.2 = (bf16[40,768]{1,0:T(8,128)(2,1)S(1)}, bf16[40,768]{1,0:T(8,128)(2,1)S(1)}, u32[]{:S(2)}, u32[]{:S(2)}) collective-permute-start(bf16[40,768]{1,0:T(8,128)(2,1)S(1)} %get-tuple-element.23), channel_id=1, source_target_pairs={{1,2},{2,3},{3,4},{4,5},{5,6},{6,7},{7,8},{8,9},{9,10},{10,11},{11... | collective-permute-start | bytes 184328 | tf_op jit(solution)/shard_map/ppermute | solution.py:411
  111.3 1.4 collective-permute-start.1
  112.0 0.7 collective-permute-start
  112.8 12.9 %collective-permute-start.4 = (bf16[40,768]{1,0:T(8,128)(2,1)S(1)}, bf16[40,768]{1,0:T(8,128)(2,1)S(1)}, u32[]{:S(2)}, u32[]{:S(2)}) collective-permute-start(bf16[40,768]{1,0:T(8,128)(2,1)S(1)} %multiply_convert_fusion), channel_id=1, source_target_pairs={{0,12},{1,13},{2,14},{3,15},{4,0},{5,1},{6,2},{7,3},{8,4},{9,5},{1... | collective-permute-start | bytes 184328 | tf_op jit(solution)/shard_map/ppermute | solution.py:372
  123.9 5.1 %collective-permute-start.5 = (bf16[40,768]{1,0:T(8,128)(2,1)S(1)}, bf16[40,768]{1,0:T(8,128)(2,1)S(1)}, u32[]{:S(2)}, u32[]{:S(2)}) collective-permute-start(bf16[40,768]{1,0:T(8,128)(2,1)S(1)} %multiply_convert_fusion), channel_id=1, source_target_pairs={{0,8},{1,9},{2,10},{3,11},{4,12},{5,13},{6,14},{7,15},{8,0},{9,1},... | collective-permute-start | bytes 184328 | tf_op jit(solution)/shard_map/ppermute | solution.py:372
  125.0 6.0 %collective-permute-start.6 = (bf16[40,768]{1,0:T(8,128)(2,1)S(1)}, bf16[40,768]{1,0:T(8,128)(2,1)S(1)}, u32[]{:S(2)}, u32[]{:S(2)}) collective-permute-start(bf16[40,768]{1,0:T(8,128)(2,1)S(1)} %multiply_convert_fusion), channel_id=1, source_target_pairs={{0,4},{1,5},{2,6},{3,7},{4,8},{5,9},{6,10},{7,11},{8,12},{9,13},{1... | collective-permute-start | bytes 184328 | tf_op jit(solution)/shard_map/ppermute | solution.py:372
  125.2 7.1 %collective-permute-start.17 = (bf16[4,2,40,256]{3,2,0,1:T(8,128)(2,1)S(1)}, bf16[4,2,40,256]{3,2,0,1:T(8,128)(2,1)S(1)}, u32[]{:S(2)}, u32[]{:S(2)}) collective-permute-start(bf16[4,2,40,256]{3,2,0,1:T(8,128)(2,1)S(1)} %pad_maximum_fusion.5), channel_id=1, source_target_pairs={{0,1},{1,0},{2,3},{3,2},{4,5},{5,4},{6,7},{7,6},{8,9},{9,8},{10,11... | collective-permute-start | bytes 491528 | tf_op jit(solution)/shard_map/ppermute | solution.py:372
  131.1 6.3 %collective-permute-start.7 = (bf16[4,40,768]{2,1,0:T(8,128)(2,1)S(1)}, bf16[4,40,768]{2,1,0:T(8,128)(2,1)S(1)}, u32[]{:S(2)}, u32[]{:S(2)}) collective-permute-start(bf16[4,40,768]{2,1,0:T(8,128)(2,1)S(1)} %pad_maximum_fusion.4), channel_id=1, source_target_pairs={{0,2},{1,3},{2,0},{3,1},{4,6},{5,7},{6,4},{7,5},{8,10},{9,11},{10,... | collective-permute-start | bytes 737288 | tf_op jit(solution)/shard_map/ppermute | solution.py:372
  137.4 1.2 copy-start.3
  137.5 6.1 %collective-permute-start.8 = (bf16[4,2,40,768]{3,2,0,1:T(8,128)(2,1)S(1)}, bf16[4,2,40,768]{3,2,0,1:T(8,128)(2,1)S(1)}, u32[]{:S(2)}, u32[]{:S(2)}) collective-permute-start(bf16[4,2,40,768]{3,2,0,1:T(8,128)(2,1)S(1)} %pad_maximum_fusion.2), channel_id=1, source_target_pairs={{0,1},{1,0},{2,3},{3,2},{4,5},{5,4},{6,7},{7,6},{8,9},{9,8},{10,11... | collective-permute-start | bytes 1474568 | tf_op jit(solution)/shard_map/ppermute | solution.py:372

commit v4 on v3

--- a/solution.py
+++ b/solution.py
@@ -46,65 +46,71 @@
     return picked.reshape(count, width)
 
 
-def fetch_kernel(order, dealing, cols, tile, out, held, sems):
-    slots, tile_rows = out.shape[0], out.shape[1]
-    tile_cols = tile.shape[2]
+def partner(k, paired):
+    return lax.bitwise_xor(lax.axis_index("row"), k) if paired else k
+
+
+def fetch_kernel(order, paired, dealing, cols, tile, *rest):
+    *outs, held, sems = rest
+    tile_rows, tile_cols = tile.shape[1], tile.shape[2]
     span = order + LANES
-
-    def copy(slot):
-        base, _ = window_start(cols[dealing[slot]], order, tile_cols)
-        return pltpu.make_async_copy(tile.at[:, :, pl.ds(base, span)], held.at[slot], sems.at[slot])
-
-    @pl.loop(0, slots)
-    def _(slot):
-        copy(slot).start()
-
+    copies, offsets = [], []
+    for k in range(len(outs)):
+        base, offset = window_start(cols[dealing[partner(k, paired)]], order, tile_cols)
+        copy = pltpu.make_async_copy(tile.at[:, :, pl.ds(base, span)], held.at[k], sems.at[k])
+        copy.start()
+        copies.append(copy)
+        offsets.append(offset)
     lane = lax.broadcasted_iota(jnp.int32, (tile_rows, LANES), 1)
-
-    @pl.loop(0, slots, unroll=2)
-    def _(slot):
-        copy(slot).wait()
-        _, offset = window_start(cols[dealing[slot]], order, tile_cols)
+    for k, out in enumerate(outs):
+        copies[k].wait()
+        offset = offsets[k]
         shift = lax.rem(LANES - lax.rem(offset, LANES), LANES)
         for part in range(2):
             turned = [
-                pltpu.roll(held[slot, part, :, b * LANES : (b + 1) * LANES], shift, 1)
+                pltpu.roll(held[k, part, :, b * LANES : (b + 1) * LANES], shift, 1)
                 for b in range(span // LANES)
             ]
             for b in range(order // LANES):
                 first = part * order + b * LANES
                 cells = jnp.where(lane < LANES - offset, turned[b], turned[b + 1])
-                out[slot, :, first : first + LANES] = cells.astype(out.dtype)
-
-
-def fetch_windows(tile, dealing, cols, order):
-    slots, tile_rows, tile_cols = dealing.shape[0], tile.shape[1], tile.shape[2]
+                out[:, first : first + LANES] = cells.astype(out.dtype)
+
+
+def fetch_windows(tile, dealing, cols, order, paired):
+    slots, tile_rows = dealing.shape[0], tile.shape[1]
     span = order + LANES
-
     return pl.pallas_call(
-        functools.partial(fetch_kernel, order),
-        out_shape=jax.ShapeDtypeStruct((slots, tile_rows, 2 * order), jnp.bfloat16),
+        functools.partial(fetch_kernel, order, paired),
+        out_shape=(jax.ShapeDtypeStruct((tile_rows, 2 * order), jnp.bfloat16),) * slots,
         in_specs=[SMEM, SMEM, ANY],
-        out_specs=VMEM,
+        out_specs=(VMEM,) * slots,
         scratch_shapes=[
             pltpu.VMEM((slots, 2, tile_rows, span), jnp.float32),
             pltpu.SemaphoreType.DMA((slots,)),
         ],
-        compiler_params=pltpu.CompilerParams(vmem_limit_bytes=56 * 2**20),
+        compiler_params=pltpu.CompilerParams(vmem_limit_bytes=54 * 2**20),
         cost_estimate=pl.CostEstimate(flops=0, bytes_accessed=6 * 2**20, transcendentals=0),
         name="fetch",
     )(dealing, cols, tile)
 
 
-def slot_kernel(
-    chunks, dealing, rows, cells, probe, measured, right_table, left_table,
-    *rest,
-):
-    backs, (empty, wide, wave, half, resid, turned, padded, zeros, right, left, sem, table_sem) = (
-        rest[: len(chunks)], rest[len(chunks) :]
-    )
+def exchange(items, paired):
+    if paired:
+        devices = len(items)
+        return [items[0]] + [
+            lax.ppermute(items[k], "row", [(d, d ^ k) for d in range(devices)])
+            for k in range(1, devices)
+        ]
+    arrived = lax.all_to_all(jnp.stack(items), "row", split_axis=0, concat_axis=0, tiled=True)
+    return [arrived[k] for k in range(len(items))]
+
+
+def slot_kernel(slots, own_rows, paired, dealing, rows, probe, measured, right_table, left_table, *rest):
+    cells, backs = rest[:slots], rest[slots : 2 * slots]
+    empty, wide, wave, half, resid, turned, padded, zeros, right, left, sem, table_sem = rest[2 * slots :]
     order = probe.shape[1]
-    total_rows = cells.shape[0]
+    total_rows = slots * own_rows
     reach = total_rows - order
     me = lax.axis_index("row")
     first_row = rows[dealing[me]]
@@ -124,10 +130,15 @@
         fill.start()
         fills.append(fill)
 
-    wide[0:total_rows, :] = cells[...].astype(jnp.float32)
+    for k, cell in enumerate(cells):
+        place = partner(k, paired) * own_rows
+        if own_rows % SUBLANES == 0:
+            place = pl.multiple_of(place, SUBLANES)
+        wide[pl.ds(place, own_rows), :] = cell[:own_rows, :].astype(jnp.float32)
     wide[total_rows:, :] = jnp.zeros((SUBLANES, 2 * order), jnp.float32)
     padded[0:reach, :] = jnp.zeros((reach, 2 * order), jnp.float32)
-    padded[reach + order :, :] = jnp.zeros((reach + SUBLANES, 2 * order), jnp.float32)
+    below = padded.shape[0] - reach - order
+    padded[reach + order :, :] = jnp.zeros((below, 2 * order), jnp.float32)
 
     @pl.loop(0, order // step)
     def _(i):
@@ -171,40 +182,35 @@
         padded[reach : reach + order, here] = dot(right[:order, :], turned[:, here])
         padded[reach : reach + order, there] = dot(right[order:, :], turned[:, here])
 
-    @pl.loop(0, total_rows // step)
-    def _(i):
-        place = pl.ds(pl.multiple_of(i * step, step), step)
-        moved = rows_from(padded, reach - first_row + i * step, step).astype(jnp.bfloat16)
-        for back, (low, high) in zip(backs, chunks):
-            back[place, : high - low] = moved[:, low:high]
-            back[place, high - low :] = moved[:, order + low : order + high]
+    for k, back in enumerate(backs):
+        start = reach - first_row + partner(k, paired) * own_rows
+        back[...] = rows_from(padded, start, back.shape[0]).astype(back.dtype)
 
     for fill in fills:
         fill.wait()
 
 
-def slot_backs(cells, probe, measured, dealing, rows, tile_rows, tile_cols, chunks):
+def slot_backs(cells, probe, measured, dealing, rows, own_rows, tile_cols, paired):
     order = probe.shape[1]
-    total_rows = cells.shape[0]
+    slots, tile_rows = len(cells), cells[0].shape[0]
+    total_rows = slots * own_rows
     right, left = dft_tables(order)
     wide_cols = 2 * order
     fill_cols = 2048
     bf16, f32 = jnp.bfloat16, jnp.float32
     *backs, empty = pl.pallas_call(
-        functools.partial(slot_kernel, chunks),
-        out_shape=tuple(
-            jax.ShapeDtypeStruct((total_rows, 2 * (high - low)), bf16) for low, high in chunks
-        )
+        functools.partial(slot_kernel, slots, own_rows, paired),
+        out_shape=(jax.ShapeDtypeStruct((tile_rows, wide_cols), bf16),) * slots
         + (jax.ShapeDtypeStruct((2, tile_rows, tile_cols), f32),),
-        in_specs=[SMEM, SMEM, VMEM, VMEM, VMEM, ANY, ANY],
-        out_specs=(VMEM,) * len(chunks) + (ANY,),
+        in_specs=[SMEM, SMEM, VMEM, VMEM, ANY, ANY] + [VMEM] * slots,
+        out_specs=(VMEM,) * slots + (ANY,),
         scratch_shapes=[
             pltpu.VMEM((total_rows + SUBLANES, wide_cols), f32),
             pltpu.VMEM((order, wide_cols), bf16),
             pltpu.VMEM((wide_cols, order), bf16),
             pltpu.VMEM((order, wide_cols), bf16),
             pltpu.VMEM((wide_cols, order), bf16),
-            pltpu.VMEM((2 * total_rows - order + SUBLANES, wide_cols), f32),
+            pltpu.VMEM((2 * total_rows - order + tile_rows + SUBLANES, wide_cols), f32),
             pltpu.VMEM((2, tile_rows, fill_cols), f32),
             pltpu.VMEM((wide_cols, wide_cols), bf16),
             pltpu.VMEM((wide_cols, wide_cols), bf16),
@@ -216,54 +222,51 @@
             flops=8 * 2 * order**3 * 2, bytes_accessed=20 * 2**20, transcendentals=order * order
         ),
         name="slot",
-    )(dealing, rows, cells, probe, measured, jnp.asarray(right), jnp.asarray(left))
+    )(dealing, rows, probe, measured, jnp.asarray(right), jnp.asarray(left), *cells)
     return backs, empty
 
 
-def partial_kernel(reach, own_rows, shifts, low, dealing, rows, pieces, back, *out):
-    *parts, total = out
-    slots, tile_rows = back.shape[0], back.shape[1]
-    width = back.shape[2] // 2
-    order = pieces.shape[2] // 2
+def partial_kernel(slots, own_rows, shifts, paired, dealing, rows, *rest):
+    pieces, backs, (*parts, total) = rest[:slots], rest[slots : 2 * slots], rest[2 * slots :]
+    tile_rows, width = backs[0].shape
+    order = width // 2
     count = tile_rows // SUBLANES
     total[...] = jnp.zeros_like(total)
-    sub = lax.broadcasted_iota(jnp.int32, (1, SUBLANES, 2 * width), 1)
-    nothing = jnp.zeros((1, SUBLANES, 2 * width), jnp.float32)
-
-    @pl.loop(0, slots, unroll=2)
-    def _(slot):
-        start = (shifts - 1) * own_rows - rows[dealing[slot]]
+    sub = lax.broadcasted_iota(jnp.int32, (1, SUBLANES, width), 1)
+    nothing = jnp.zeros((1, SUBLANES, width), jnp.float32)
+    for k in range(slots):
+        start = (shifts - 1) * own_rows - rows[dealing[partner(k, paired)]]
         aligned = pl.multiple_of(start // SUBLANES * SUBLANES, SUBLANES)
-        rest = start - aligned
-        patch_real = pieces[slot, :, low : low + width].astype(jnp.float32)
-        patch_imag = pieces[slot, :, order + low : order + low + width].astype(jnp.float32)
-        real = back[slot, :, :width].astype(jnp.float32)
-        imag = back[slot, :, width:].astype(jnp.float32)
+        rest_rows = start - aligned
+        patch_real = pieces[k][:, :order].astype(jnp.float32)
+        patch_imag = pieces[k][:, order:].astype(jnp.float32)
+        real = backs[k][:, :order].astype(jnp.float32)
+        imag = backs[k][:, order:].astype(jnp.float32)
         terms = jnp.concatenate(
             [patch_real * real + patch_imag * imag, patch_real * imag - patch_imag * real], axis=1
         )
-        turned = pltpu.roll(terms.reshape(count, SUBLANES, 2 * width), rest, 1)
+        turned = pltpu.roll(terms.reshape(count, SUBLANES, width), rest_rows, 1)
         before = jnp.concatenate([nothing, turned], axis=0)
         after = jnp.concatenate([turned, nothing], axis=0)
-        moved = jnp.where(sub < rest, before, after).reshape(tile_rows + SUBLANES, 2 * width)
+        moved = jnp.where(sub < rest_rows, before, after).reshape(tile_rows + SUBLANES, width)
         total[pl.ds(aligned, tile_rows + SUBLANES), :] += moved
 
     for e, part in enumerate(parts):
         part[...] = total[e * own_rows : (e + 1) * own_rows, :].astype(part.dtype)
 
 
-def probe_partials(pieces, back, dealing, rows, own_rows, reach, shifts, low, dtypes):
-    tile_rows, wide = back.shape[1], back.shape[2]
+def probe_partials(pieces, backs, dealing, rows, own_rows, shifts, dtypes, paired):
+    slots, (tile_rows, width) = len(backs), backs[0].shape
     return pl.pallas_call(
-        functools.partial(partial_kernel, reach, own_rows, shifts, low),
-        out_shape=tuple(jax.ShapeDtypeStruct((own_rows, wide), dtype) for dtype in dtypes),
-        in_specs=[SMEM, SMEM, VMEM, VMEM],
+        functools.partial(partial_kernel, slots, own_rows, shifts, paired),
+        out_shape=tuple(jax.ShapeDtypeStruct((own_rows, width), dtype) for dtype in dtypes),
+        in_specs=[SMEM, SMEM] + [VMEM] * (2 * slots),
         out_specs=(VMEM,) * len(dtypes),
-        scratch_shapes=[pltpu.VMEM((shifts * own_rows + tile_rows + SUBLANES, wide), jnp.float32)],
+        scratch_shapes=[pltpu.VMEM((shifts * own_rows + tile_rows + SUBLANES, width), jnp.float32)],
         compiler_params=pltpu.CompilerParams(vmem_limit_bytes=16 * 2**20),
         cost_estimate=pl.CostEstimate(flops=0, bytes_accessed=4 * 2**20, transcendentals=0),
         name="partial",
-    )(dealing, rows, pieces, back)
+    )(dealing, rows, *pieces, *backs)
 
 
 def block_places(dealing, cols, order, tile_cols):
@@ -275,11 +278,11 @@
 
 
 def place_kernel(
-    order, own_rows, top, chunks, dealing, rows, cols, blocks, owners, probe, *rest
+    slots, order, own_rows, top, paired, dealing, rows, cols, blocks, owners, probe, *rest
 ):
-    backs, (empty, out, totals, spread, sems) = rest[: len(chunks)], rest[len(chunks) :]
+    backs, (empty, out, totals, spread, sems) = rest[:slots], rest[slots:]
     del empty
-    slots, tile_rows = backs[0].shape[0], backs[0].shape[1]
+    tile_rows = backs[0].shape[0]
     count = (order + LANES) // LANES
     me = lax.axis_index("row")
     spread[0:top, :] = jnp.zeros((top, 2 * order), jnp.float32)
@@ -288,24 +291,22 @@
     spread[top + order :, :] = jnp.zeros((spread.shape[0] - top - order, 2 * order), jnp.float32)
     totals[...] = jnp.zeros_like(totals)
     lane = lax.broadcasted_iota(jnp.int32, (tile_rows, LANES), 1)
-
-    @pl.loop(0, slots, unroll=2)
-    def _(slot):
+    nothing = jnp.zeros((tile_rows, LANES), jnp.float32)
+
+    for k, back in enumerate(backs):
+        slot = partner(k, paired)
         _, offset = window_start(cols[dealing[slot]], order, out.shape[2])
         shift = lax.rem(offset, LANES)
         around = rows_from(spread, top + me * own_rows - rows[dealing[slot]], tile_rows)
         turned = [[], []]
-        for back, (low, high) in zip(backs, chunks):
-            for first in range(low, high, LANES):
-                here = slice(first - low, first - low + LANES)
-                there = slice(high - low + first - low, high - low + first - low + LANES)
-                real = back[slot, :, here].astype(jnp.float32)
-                imag = back[slot, :, there].astype(jnp.float32)
-                probe_real = around[:, first : first + LANES]
-                probe_imag = around[:, order + first : order + first + LANES]
-                turned[0].append(pltpu.roll(probe_real * real + probe_imag * imag, shift, 1))
-                turned[1].append(pltpu.roll(probe_real * imag - probe_imag * real, shift, 1))
-        nothing = jnp.zeros((tile_rows, LANES), jnp.float32)
+        for first in range(0, order, LANES):
+            here = slice(first, first + LANES)
+            there = slice(order + first, order + first + LANES)
+            real = back[:, here].astype(jnp.float32)
+            imag = back[:, there].astype(jnp.float32)
+            probe_real, probe_imag = around[:, here], around[:, there]
+            turned[0].append(pltpu.roll(probe_real * real + probe_imag * imag, shift, 1))
+            turned[1].append(pltpu.roll(probe_real * imag - probe_imag * real, shift, 1))
         for b in range(count):
             owner = owners[slot * count + b]
             for part in range(2):
@@ -330,25 +331,26 @@
             copy(number).wait()
 
 
-def place_windows(backs, empty, probe, dealing, rows, cols, own_rows, total_rows, chunks):
+def place_windows(backs, empty, probe, dealing, rows, cols, own_rows, paired):
     order = probe.shape[1]
-    slots, tile_rows = backs[0].shape[0], backs[0].shape[1]
+    slots, tile_rows = len(backs), backs[0].shape[0]
+    total_rows = slots * own_rows
     tile_cols = empty.shape[2]
     count = (order + LANES) // LANES
     blocks, owners = block_places(dealing, cols, order, tile_cols)
     top = -(-(total_rows - order) // SUBLANES) * SUBLANES
     spread_rows = -(-(top + total_rows) // SUBLANES) * SUBLANES + tile_rows + SUBLANES
     return pl.pallas_call(
-        functools.partial(place_kernel, order, own_rows, top, chunks),
+        functools.partial(place_kernel, slots, order, own_rows, top, paired),
         out_shape=jax.ShapeDtypeStruct(empty.shape, empty.dtype),
-        in_specs=[SMEM, SMEM, SMEM, SMEM, SMEM, VMEM] + [VMEM] * len(backs) + [ANY],
+        in_specs=[SMEM, SMEM, SMEM, SMEM, SMEM, VMEM] + [VMEM] * slots + [ANY],
         out_specs=ANY,
         scratch_shapes=[
             pltpu.VMEM((slots * count, 2, tile_rows, LANES), jnp.float32),
             pltpu.VMEM((spread_rows, 2 * order), jnp.float32),
             pltpu.SemaphoreType.DMA((slots * count,)),
         ],
-        input_output_aliases={6 + len(backs): 0},
+        input_output_aliases={6 + slots: 0},
         compiler_params=pltpu.CompilerParams(vmem_limit_bytes=24 * 2**20),
         cost_estimate=pl.CostEstimate(flops=0, bytes_accessed=6 * 2**20, transcendentals=0),
         name="place",
@@ -389,8 +391,9 @@
     return whole.reshape(devices * rows, width)
 
 
-def sum_probe(pieces, back, dealing, rows, own_rows, reach, low, devices):
-    order = pieces.shape[2] // 2
+def sum_probe(pieces, backs, dealing, rows, own_rows, reach, paired):
+    devices, width = len(backs), backs[0].shape[1]
+    order = width // 2
     scale = 1.0 / dealing.shape[0]
     shifts = -(-reach // own_rows) + 1
     held = -(-order // own_rows)
@@ -398,7 +401,7 @@
     own = shifts - 1 - middle
     direct = shifts <= 8
     dtypes = [jnp.bfloat16 if direct and e != own else jnp.float32 for e in range(shifts)]
-    parts = probe_partials(pieces, back, dealing, rows, own_rows, reach, shifts, low, dtypes)
+    parts = probe_partials(pieces, backs, dealing, rows, own_rows, shifts, dtypes, paired)
     if direct:
         total = parts[own]
         for e in range(shifts):
@@ -412,7 +415,7 @@
         whole = join((total * scale).astype(jnp.bfloat16), devices)
         first = middle * own_rows
     else:
-        spread = jnp.zeros(((devices + shifts) * own_rows, back.shape[2]), jnp.float32)
+        spread = jnp.zeros(((devices + shifts) * own_rows, width), jnp.float32)
         start = lax.axis_index("row") * own_rows
         spread = lax.dynamic_update_slice(spread, jnp.concatenate(parts, axis=0), (start, 0))
         first = (shifts - 1) * own_rows
@@ -427,35 +430,19 @@
     total_rows = devices * own_rows
     tile_rows = -(-own_rows // SUBLANES) * SUBLANES
     spare = tile_rows - own_rows
-    cut = order // LANES * 3 // 4 * LANES
-    chunks = ((0, cut), (cut, order))
+    paired = devices <= 16 and devices & (devices - 1) == 0
     if spare:
         object_field = jnp.pad(object_field, ((0, 0), (0, spare), (0, 0)))
-    pieces = fetch_windows(object_field, dealing, col_offsets, order)
-    strips = lax.all_to_all(pieces, "row", split_axis=0, concat_axis=0, tiled=True)
-    cells = strips[:, :own_rows].reshape(total_rows, 2 * order)
+    pieces = fetch_windows(object_field, dealing, col_offsets, order, paired)
+    cells = exchange(pieces, paired)
     backs, empty = slot_backs(
-        cells, probe, amplitude, dealing, row_offsets, tile_rows, tile_cols, chunks
+        cells, probe, amplitude, dealing, row_offsets, own_rows, tile_cols, paired
     )
-    arrived, sums = [], []
-    for back, (low, high) in zip(backs, chunks):
-        outgoing = back.reshape(devices, own_rows, 2 * (high - low))
-        if spare:
-            outgoing = jnp.pad(outgoing, ((0, 0), (0, spare), (0, 0)))
-        arrived.append(lax.all_to_all(outgoing, "row", split_axis=0, concat_axis=0, tiled=True))
-    for here, (low, high) in zip(arrived, chunks):
-        sums.append(
-            sum_probe(pieces, here, dealing, row_offsets, own_rows, total_rows - order, low, devices)
-        )
-    widths = [high - low for low, high in chunks]
-    probe_grad = jnp.stack(
-        [
-            jnp.concatenate([total[:, :width] for total, width in zip(sums, widths)], axis=1),
-            jnp.concatenate([total[:, width:] for total, width in zip(sums, widths)], axis=1),
-        ]
-    )
+    backs = exchange(backs, paired)
+    whole = sum_probe(pieces, backs, dealing, row_offsets, own_rows, total_rows - order, paired)
+    probe_grad = jnp.stack([whole[:, :order], whole[:, order:]])
     object_grad = place_windows(
-        arrived, empty, probe, dealing, row_offsets, col_offsets, own_rows, total_rows, chunks
+        backs, empty, probe, dealing, row_offsets, col_offsets, own_rows, paired
     )
     if spare:
         object_grad = object_grad[:, :own_rows]

time: 146 us -> 141 us (0.966)
  the two profiles are of different devices: /device:TPU:0 before, /device:TPU:15 now
where the time goes in v4:
time: 141 us; the launch traced here: 139 us
  waiting for transfers between devices  57.8 us (41%)
  starting transfers between devices  54.1 us (38%)
  Pallas kernels  17.9 us (13%)
  other arithmetic  5.98 us (4%)
  local copies, waits for them, and re-layouts  2.06 us (1%)
    ppermute x30, waiting for transfers between devices, exchange(): lax.ppermute(items[k], 'row', [(d, d ^ k) for d in range(devices)])  42.8 us
    ppermute x30, starting transfers between devices, exchange(): lax.ppermute(items[k], 'row', [(d, d ^ k) for d in range(devices)])  34.8 us
    ppermute x5, waiting for transfers between devices, turn(): return lax.ppermute(x, 'row', pairs)  12.7 us
    ppermute x4, starting transfers between devices, sum_probe(): total = total + lax.ppermute(parts[e], 'row', pairs).astype(jnp.float32)  11.7 us
    ppermute x5, starting transfers between devices, turn(): return lax.ppermute(x, 'row', pairs)  7.61 us
    pallas_call x1, Pallas kernels, slot_backs(): pl.pallas_call(functools.partial(slot_kernel, slots, own_rows, paired), o...  7.03 us
    pallas_call x1, Pallas kernels, fetch_windows(): pl.pallas_call(functools.partial(fetch_kernel, order, paired), out_shape=...  4.97 us
    pallas_call x1, Pallas kernels, place_windows(): pl.pallas_call(functools.partial(place_kernel, slots, order, own_rows, to...  4.25 us
  transfers between devices with their start and end apart: 39, of which 20 were waited for; matrix products, arithmetic and copies ran while one was open for 1% of the time, Pallas kernels for 3%

profile of v4, /device:TPU:15, one launch (start us, length us, event | category | flops | bytes accessed | tf_op | source)
XLA Modules:
  0.0 139.0 jit_solution(12441376089310635443)
XLA Ops:
  0.7 5.0 %fetch.1 = (bf16[40,1024]{1,0:T(8,128)(2,1)}, bf16[40,1024]{1,0:T(8,128)(2,1)}, bf16[40,1024]{1,0:T(8,128)(2,1)}, bf16[40,1024]{1,0:T(8,128)(2,1)}, bf16[40,1024...) custom-call(s32[16]{0:T(128)} %dealing.7, ...), custom_call_target="tpu_custom_call" | custom-call | bytes 6291456 | tf_op jit(solution)/shard_map/fetch/pallas_call | solution.py:83
  5.7 0.7 collective-permute-start
  6.4 0.2 collective-permute-start.1
  6.7 1.5 %collective-permute-start.2 = (bf16[40,1024]{1,0:T(8,128)(2,1)}, bf16[40,1024]{1,0:T(8,128)(2,1)S(1)}, u32[]{:S(2)}, u32[]{:S(2)}) collective-permute-start(bf16[40,1024]{1,0:T(8,128)(2,1)} %get-tuple-element.45.rest_3_), channel_id=1, source_target_pairs={{0,3},{1,2},{2,1},{3,0},{4,7},{5,6},{6,5},{7,4},{8,11},{9,10},{10,... | collective-permute-start | bytes 245768 | tf_op jit(solution)/shard_map/ppermute | solution.py:102
  8.1 0.2 collective-permute-start.3
  8.3 1.6 %collective-permute-start.4 = (bf16[40,1024]{1,0:T(8,128)(2,1)}, bf16[40,1024]{1,0:T(8,128)(2,1)S(1)}, u32[]{:S(2)}, u32[]{:S(2)}) collective-permute-start(bf16[40,1024]{1,0:T(8,128)(2,1)} %get-tuple-element.47.rest_5_), channel_id=1, source_target_pairs={{0,5},{1,4},{2,7},{3,6},{4,1},{5,0},{6,3},{7,2},{8,13},{9,12},{10,... | collective-permute-start | bytes 245768 | tf_op jit(solution)/shard_map/ppermute | solution.py:102
  10.0 0.6 collective-permute-done.1.rest_2_
  10.7 1.9 %collective-permute-start.6 = (bf16[40,1024]{1,0:T(8,128)(2,1)}, bf16[40,1024]{1,0:T(8,128)(2,1)S(1)}, u32[]{:S(2)}, u32[]{:S(2)}) collective-permute-start(bf16[40,1024]{1,0:T(8,128)(2,1)} %get-tuple-element.49.rest_7_), channel_id=1, source_target_pairs={{0,7},{1,6},{2,5},{3,4},{4,3},{5,2},{6,1},{7,0},{8,15},{9,14},{10,... | collective-permute-start | bytes 245768 | tf_op jit(solution)/shard_map/ppermute | solution.py:102
  12.5 0.3 collective-permute-done.2.rest_3_
  12.9 2.3 %collective-permute-start.7 = (bf16[40,1024]{1,0:T(8,128)(2,1)}, bf16[40,1024]{1,0:T(8,128)(2,1)S(1)}, u32[]{:S(2)}, u32[]{:S(2)}) collective-permute-start(bf16[40,1024]{1,0:T(8,128)(2,1)} %get-tuple-element.50.rest_8_), channel_id=1, source_target_pairs={{0,8},{1,9},{2,10},{3,11},{4,12},{5,13},{6,14},{7,15},{8,0},{9,1},... | collective-permute-start | bytes 245768 | tf_op jit(solution)/shard_map/ppermute | solution.py:102
  15.2 0.8 collective-permute-start.8
  16.0 1.8 %collective-permute-start.9 = (bf16[40,1024]{1,0:T(8,128)(2,1)}, bf16[40,1024]{1,0:T(8,128)(2,1)S(1)}, u32[]{:S(2)}, u32[]{:S(2)}) collective-permute-start(bf16[40,1024]{1,0:T(8,128)(2,1)} %get-tuple-element.52.rest_10_), channel_id=1, source_target_pairs={{0,10},{1,11},{2,8},{3,9},{4,14},{5,15},{6,12},{7,13},{8,2},{9,3},... | collective-permute-start | bytes 245768 | tf_op jit(solution)/shard_map/ppermute | solution.py:102
  17.7 3.4 %collective-permute-start.10 = (bf16[40,1024]{1,0:T(8,128)(2,1)}, bf16[40,1024]{1,0:T(8,128)(2,1)S(1)}, u32[]{:S(2)}, u32[]{:S(2)}) collective-permute-start(bf16[40,1024]{1,0:T(8,128)(2,1)} %get-tuple-element.53.rest_11_), channel_id=1, source_target_pairs={{0,11},{1,10},{2,9},{3,8},{4,15},{5,14},{6,13},{7,12},{8,3},{9,2},... | collective-permute-start | bytes 245768 | tf_op jit(solution)/shard_map/ppermute | solution.py:102
  21.2 0.8 collective-permute-start.12
  22.0 6.0 %collective-permute-done.8.rest_9_ = bf16[40,1024]{1,0:T(8,128)(2,1)S(1)} collective-permute-done((bf16[40,1024]{1,0:T(8,128)(2,1)}, bf16[40,1024]{1,0:T(8,128)(2,1)S(1)}, u32[]{:S(2)}, u32[]{:S(2)}) %collective-permute-start.8) | collective-permute-done | bytes 81952 | tf_op jit(solution)/shard_map/ppermute | solution.py:102
  28.0 0.8 collective-permute-start.13
  28.7 1.0 collective-permute-done.9.rest_10_
  29.7 2.1 %collective-permute-start.14 = (bf16[40,1024]{1,0:T(8,128)(2,1)}, bf16[40,1024]{1,0:T(8,128)(2,1)S(1)}, u32[]{:S(2)}, u32[]{:S(2)}) collective-permute-start(bf16[40,1024]{1,0:T(8,128)(2,1)} %get-tuple-element.57.rest_15_), channel_id=1, source_target_pairs={{0,15},{1,14},{2,13},{3,12},{4,11},{5,10},{6,9},{7,8},{8,7},{9,6},... | collective-permute-start | bytes 245768 | tf_op jit(solution)/shard_map/ppermute | solution.py:102
  31.8 6.5 %collective-permute-done.11.rest_12_ = bf16[40,1024]{1,0:T(8,128)(2,1)S(1)} collective-permute-done((bf16[40,1024]{1,0:T(8,128)(2,1)}, bf16[40,1024]{1,0:T(8,128)(2,1)S(1)}, u32[]{:S(2)}, u32[]{:S(2)}) %collective-permute-start.11) | collective-permute-done | bytes 81952 | tf_op jit(solution)/shard_map/ppermute | solution.py:102
  38.4 2.7 %collective-permute-done.12.rest_13_ = bf16[40,1024]{1,0:T(8,128)(2,1)S(1)} collective-permute-done((bf16[40,1024]{1,0:T(8,128)(2,1)}, bf16[40,1024]{1,0:T(8,128)(2,1)S(1)}, u32[]{:S(2)}, u32[]{:S(2)}) %collective-permute-start.12) | collective-permute-done | bytes 81952 | tf_op jit(solution)/shard_map/ppermute | solution.py:102
  41.1 1.4 %collective-permute-done.13.rest_14_ = bf16[40,1024]{1,0:T(8,128)(2,1)S(1)} collective-permute-done((bf16[40,1024]{1,0:T(8,128)(2,1)}, bf16[40,1024]{1,0:T(8,128)(2,1)S(1)}, u32[]{:S(2)}, u32[]{:S(2)}) %collective-permute-start.13) | collective-permute-done | bytes 81952 | tf_op jit(solution)/shard_map/ppermute | solution.py:102
  42.5 2.1 %collective-permute-done.14.rest_15_ = bf16[40,1024]{1,0:T(8,128)(2,1)S(1)} collective-permute-done((bf16[40,1024]{1,0:T(8,128)(2,1)}, bf16[40,1024]{1,0:T(8,128)(2,1)S(1)}, u32[]{:S(2)}, u32[]{:S(2)}) %collective-permute-start.14) | collective-permute-done | bytes 81952 | tf_op jit(solution)/shard_map/ppermute | solution.py:102
  44.6 0.9 copy-done.2
  45.6 7.0 %slot.1 = (bf16[40,1024]{1,0:T(8,128)(2,1)S(1)}, bf16[40,1024]{1,0:T(8,128)(2,1)S(1)}, bf16[40,1024]{1,0:T(8,128)(2,1)S(1)}, bf16[40,1024]{1,0:T(8,128)(2,1)S(1)...) custom-call(s32[16]{0:T(128)S(1)} %copy-done.18, ...), custom_call_target="tpu_custom_call" | custom-call | flops 4294967296 | bytes 20971520 | tf_op jit(solution)/shard_map/slot/pallas_call | solution.py:201
  52.8 0.9 collective-permute-start.16
  53.7 1.2 collective-permute-start.17
  54.9 1.4 %collective-permute-start.19 = (bf16[40,1024]{1,0:T(8,128)(2,1)S(1)}, bf16[40,1024]{1,0:T(8,128)(2,1)S(1)}, u32[]{:S(2)}, u32[]{:S(2)}) collective-permute-start(bf16[40,1024]{1,0:T(8,128)(2,1)S(1)} %get-tuple-element.63), channel_id=1, source_target_pairs={{0,5},{1,4},{2,7},{3,6},{4,1},{5,0},{6,3},{7,2},{8,13},{9,12},{10,... | collective-permute-start | bytes 245768 | tf_op jit(solution)/shard_map/ppermute | solution.py:102
  56.3 0.5 collective-permute-start.20
  56.8 2.5 %collective-permute-start.21 = (bf16[40,1024]{1,0:T(8,128)(2,1)S(1)}, bf16[40,1024]{1,0:T(8,128)(2,1)S(1)}, u32[]{:S(2)}, u32[]{:S(2)}) collective-permute-start(bf16[40,1024]{1,0:T(8,128)(2,1)S(1)} %get-tuple-element.65), channel_id=1, source_target_pairs={{0,7},{1,6},{2,5},{3,4},{4,3},{5,2},{6,1},{7,0},{8,15},{9,14},{10,... | collective-permute-start | bytes 245768 | tf_op jit(solution)/shard_map/ppermute | solution.py:102
  59.3 2.5 %collective-permute-start.22 = (bf16[40,1024]{1,0:T(8,128)(2,1)S(1)}, bf16[40,1024]{1,0:T(8,128)(2,1)S(1)}, u32[]{:S(2)}, u32[]{:S(2)}) collective-permute-start(bf16[40,1024]{1,0:T(8,128)(2,1)S(1)} %get-tuple-element.66), channel_id=1, source_target_pairs={{0,8},{1,9},{2,10},{3,11},{4,12},{5,13},{6,14},{7,15},{8,0},{9,1},... | collective-permute-start | bytes 245768 | tf_op jit(solution)/shard_map/ppermute | solution.py:102
  61.8 1.8 %collective-permute-start.24 = (bf16[40,1024]{1,0:T(8,128)(2,1)S(1)}, bf16[40,1024]{1,0:T(8,128)(2,1)S(1)}, u32[]{:S(2)}, u32[]{:S(2)}) collective-permute-start(bf16[40,1024]{1,0:T(8,128)(2,1)S(1)} %get-tuple-element.68), channel_id=1, source_target_pairs={{0,10},{1,11},{2,8},{3,9},{4,14},{5,15},{6,12},{7,13},{8,2},{9,3},... | collective-permute-start | bytes 245768 | tf_op jit(solution)/shard_map/ppermute | solution.py:102
  63.6 2.1 %collective-permute-start.25 = (bf16[40,1024]{1,0:T(8,128)(2,1)S(1)}, bf16[40,1024]{1,0:T(8,128)(2,1)S(1)}, u32[]{:S(2)}, u32[]{:S(2)}) collective-permute-start(bf16[40,1024]{1,0:T(8,128)(2,1)S(1)} %get-tuple-element.69), channel_id=1, source_target_pairs={{0,11},{1,10},{2,9},{3,8},{4,15},{5,14},{6,13},{7,12},{8,3},{9,2},... | collective-permute-start | bytes 245768 | tf_op jit(solution)/shard_map/ppermute | solution.py:102
  65.7 1.6 %collective-permute-start.26 = (bf16[40,1024]{1,0:T(8,128)(2,1)S(1)}, bf16[40,1024]{1,0:T(8,128)(2,1)S(1)}, u32[]{:S(2)}, u32[]{:S(2)}) collective-permute-start(bf16[40,1024]{1,0:T(8,128)(2,1)S(1)} %get-tuple-element.70), channel_id=1, source_target_pairs={{0,12},{1,13},{2,14},{3,15},{4,8},{5,9},{6,10},{7,11},{8,4},{9,5},... | collective-permute-start | bytes 245768 | tf_op jit(solution)/shard_map/ppermute | solution.py:102
  67.3 6.3 %collective-permute-done.22.rest_8_.rest_24_ = bf16[40,1024]{1,0:T(8,128)(2,1)S(1)} collective-permute-done((bf16[40,1024]{1,0:T(8,128)(2,1)S(1)}, bf16[40,1024]{1,0:T(8,128)(2,1)S(1)}, u32[]{:S(2)}, u32[]{:S(2)}) %collective-permute-start.22) | collective-permute-done | bytes 81952 | tf_op jit(solution)/shard_map/ppermute | solution.py:102
  73.6 1.9 %collective-permute-done.23.rest_9_.rest_25_ = bf16[40,1024]{1,0:T(8,128)(2,1)S(1)} collective-permute-done((bf16[40,1024]{1,0:T(8,128)(2,1)S(1)}, bf16[40,1024]{1,0:T(8,128)(2,1)S(1)}, u32[]{:S(2)}, u32[]{:S(2)}) %collective-permute-start.23) | collective-permute-done | bytes 81952 | tf_op jit(solution)/shard_map/ppermute | solution.py:102
  75.5 1.8 %collective-permute-done.24.rest_10_.rest_26_ = bf16[40,1024]{1,0:T(8,128)(2,1)S(1)} collective-permute-done((bf16[40,1024]{1,0:T(8,128)(2,1)S(1)}, bf16[40,1024]{1,0:T(8,128)(2,1)S(1)}, u32[]{:S(2)}, u32[]{:S(2)}) %collective-permute-start.24) | collective-permute-done | bytes 81952 | tf_op jit(solution)/shard_map/ppermute | solution.py:102
  77.2 2.0 %collective-permute-start.29 = (bf16[40,1024]{1,0:T(8,128)(2,1)S(1)}, bf16[40,1024]{1,0:T(8,128)(2,1)S(1)}, u32[]{:S(2)}, u32[]{:S(2)}) collective-permute-start(bf16[40,1024]{1,0:T(8,128)(2,1)S(1)} %get-tuple-element.73), channel_id=1, source_target_pairs={{0,15},{1,14},{2,13},{3,12},{4,11},{5,10},{6,9},{7,8},{8,7},{9,6},... | collective-permute-start | bytes 245768 | tf_op jit(solution)/shard_map/ppermute | solution.py:102
  79.2 0.5 collective-permute-done.25.rest_11_.rest_27_
  79.7 5.3 %collective-permute-done.26.rest_12_.rest_28_ = bf16[40,1024]{1,0:T(8,128)(2,1)S(1)} collective-permute-done((bf16[40,1024]{1,0:T(8,128)(2,1)S(1)}, bf16[40,1024]{1,0:T(8,128)(2,1)S(1)}, u32[]{:S(2)}, u32[]{:S(2)}) %collective-permute-start.26) | collective-permute-done | bytes 81952 | tf_op jit(solution)/shard_map/ppermute | solution.py:102
  85.0 2.4 %collective-permute-done.27.rest_13_.rest_29_ = bf16[40,1024]{1,0:T(8,128)(2,1)S(1)} collective-permute-done((bf16[40,1024]{1,0:T(8,128)(2,1)S(1)}, bf16[40,1024]{1,0:T(8,128)(2,1)S(1)}, u32[]{:S(2)}, u32[]{:S(2)}) %collective-permute-start.27) | collective-permute-done | bytes 81952 | tf_op jit(solution)/shard_map/ppermute | solution.py:102
  87.4 2.3 %collective-permute-done.28.rest_14_.rest_30_ = bf16[40,1024]{1,0:T(8,128)(2,1)S(1)} collective-permute-done((bf16[40,1024]{1,0:T(8,128)(2,1)S(1)}, bf16[40,1024]{1,0:T(8,128)(2,1)S(1)}, u32[]{:S(2)}, u32[]{:S(2)}) %collective-permute-start.28) | collective-permute-done | bytes 81952 | tf_op jit(solution)/shard_map/ppermute | solution.py:102
  89.7 1.8 %collective-permute-done.29.rest_15_.rest_31_ = bf16[40,1024]{1,0:T(8,128)(2,1)S(1)} collective-permute-done((bf16[40,1024]{1,0:T(8,128)(2,1)S(1)}, bf16[40,1024]{1,0:T(8,128)(2,1)S(1)}, u32[]{:S(2)}, u32[]{:S(2)}) %collective-permute-start.29) | collective-permute-done | bytes 81952 | tf_op jit(solution)/shard_map/ppermute | solution.py:102
  91.6 1.7 %partial.1 = (bf16[40,1024]{1,0:T(8,128)(2,1)S(1)}, bf16[40,1024]{1,0:T(8,128)(2,1)S(1)}, f32[40,1024]{1,0:T(8,128)S(1)}, bf16[40,1024]{1,0:T(8,128)(2,1)S(1)}, bf16[40,1024]{1,0:T(8,128)(2,1)S(1)}) custom-call(s32[16]{0:T(128)S(1)} %copy-done.18, s32[16]{0:T(128)S(1)} %copy-done.19, bf16[40,1024]{1,0:T(8,128)(2,1)S(1)} %copy-done.2, ...), custom_call_target="tpu_custom_call" | custom-call | bytes 4194304 | tf_op jit(solution)/shard_map/partial/pallas_call | solution.py:260
  93.2 2.2 %collective-permute-start.30 = (bf16[40,1024]{1,0:T(8,128)(2,1)S(1)}, bf16[40,1024]{1,0:T(8,128)(2,1)S(1)}, u32[]{:S(2)}, u32[]{:S(2)}) collective-permute-start(bf16[40,1024]{1,0:T(8,128)(2,1)S(1)} %get-tuple-element.76), channel_id=1, source_target_pairs={{4,2},{5,3},{6,4},{7,5},{8,6},{9,7},{10,8},{11,9},{12,10},{13,11},... | collective-permute-start | bytes 245768 | tf_op jit(solution)/shard_map/ppermute | solution.py:414
  95.5 2.5 %collective-permute-start.31 = (bf16[40,1024]{1,0:T(8,128)(2,1)S(1)}, bf16[40,1024]{1,0:T(8,128)(2,1)S(1)}, u32[]{:S(2)}, u32[]{:S(2)}) collective-permute-start(bf16[40,1024]{1,0:T(8,128)(2,1)S(1)} %get-tuple-element.77), channel_id=1, source_target_pairs={{3,2},{4,3},{5,4},{6,5},{7,6},{8,7},{9,8},{10,9},{11,10},{12,11},{... | collective-permute-start | bytes 245768 | tf_op jit(solution)/shard_map/ppermute | solution.py:414
  98.0 3.9 %collective-permute-start.32 = (bf16[40,1024]{1,0:T(8,128)(2,1)S(1)}, bf16[40,1024]{1,0:T(8,128)(2,1)S(1)}, u32[]{:S(2)}, u32[]{:S(2)}) collective-permute-start(bf16[40,1024]{1,0:T(8,128)(2,1)S(1)} %get-tuple-element.78), channel_id=1, source_target_pairs={{1,2},{2,3},{3,4},{4,5},{5,6},{6,7},{7,8},{8,9},{9,10},{10,11},{11... | collective-permute-start | bytes 245768 | tf_op jit(solution)/shard_map/ppermute | solution.py:414
  102.0 3.0 %collective-permute-start.33 = (bf16[40,1024]{1,0:T(8,128)(2,1)S(1)}, bf16[40,1024]{1,0:T(8,128)(2,1)S(1)}, u32[]{:S(2)}, u32[]{:S(2)}) collective-permute-start(bf16[40,1024]{1,0:T(8,128)(2,1)S(1)} %get-tuple-element.79), channel_id=1, source_target_pairs={{0,2},{1,3},{2,4},{3,5},{4,6},{5,7},{6,8},{7,9},{8,10},{9,11},{10,... | collective-permute-start | bytes 245768 | tf_op jit(solution)/shard_map/ppermute | solution.py:414
  105.1 2.2 %collective-permute-done.33 = bf16[40,1024]{1,0:T(8,128)(2,1)S(1)} collective-permute-done((bf16[40,1024]{1,0:T(8,128)(2,1)S(1)}, bf16[40,1024]{1,0:T(8,128)(2,1)S(1)}, u32[]{:S(2)}, u32[]{:S(2)}) %collective-permute-start.33) | collective-permute-done | bytes 81952 | tf_op jit(solution)/shard_map/ppermute | solution.py:414
  107.3 1.4 collective-permute-start.36
  108.7 1.3 collective-permute-start.34
  110.0 1.3 collective-permute-done.36
  111.2 4.3 %collective-permute-done.35 = bf16[40,1024]{1,0:T(8,128)(2,1)S(1)} collective-permute-done((bf16[40,1024]{1,0:T(8,128)(2,1)S(1)}, bf16[40,1024]{1,0:T(8,128)(2,1)S(1)}, u32[]{:S(2)}, u32[]{:S(2)}) %collective-permute-start.35) | collective-permute-done | bytes 81952 | tf_op jit(solution)/shard_map/ppermute | solution.py:374
  115.7 4.0 %collective-permute-start.37 = (bf16[4,40,1024]{2,1,0:T(8,128)(2,1)S(1)}, bf16[4,40,1024]{2,1,0:T(8,128)(2,1)}, u32[]{:S(2)}, u32[]{:S(2)}) collective-permute-start(bf16[4,40,1024]{2,1,0:T(8,128)(2,1)S(1)} %pad_maximum_fusion.3), channel_id=1, source_target_pairs={{0,2},{1,3},{2,0},{3,1},{4,6},{5,7},{6,4},{7,5},{8,10},{9,11},{10,... | collective-permute-start | bytes 983048 | tf_op jit(solution)/shard_map/ppermute | solution.py:374
  119.7 0.7 gather_fusion
  120.3 7.1 %collective-permute-done.37 = bf16[4,40,1024]{2,1,0:T(8,128)(2,1)} collective-permute-done((bf16[4,40,1024]{2,1,0:T(8,128)(2,1)S(1)}, bf16[4,40,1024]{2,1,0:T(8,128)(2,1)}, u32[]{:S(2)}, u32[]{:S(2)}) %collective-permute-start.37) | collective-permute-done | bytes 327712 | tf_op jit(solution)/shard_map/ppermute | solution.py:374
  127.4 1.0 select_bitcast_fusion.3
  128.5 0.9 pad_maximum_fusion.2
  129.4 1.0 collective-permute-start.38
  130.5 0.8 iota_reduce_fusion
  131.3 4.2 %place.1 = f32[2,40,32768]{2,1,0:T(8,128)} custom-call(s32[16]{0:T(128)S(1)} %copy-done.18, s32[16]{0:T(128)S(1)} %copy-done.19, s32[16]{0:T(128)S(1)} %copy-done, s32[80]{0:T(128)S(1)} %add.107.blocks, s32[80]{0:T(128)S(1)} %get-tuple-element.41.owners, bf16[2,512,512]{2,1,0:T(8,128)(2,1)S(1)} %copy-done.1, ...), custom_call_target="tpu_custom_call", output_to_operand_aliasing={{}: (22, {})} | custom-call | bytes 6291456 | tf_op jit(solution)/shard_map/place/pallas_call | solution.py:343
  135.6 1.2 select_bitcast_fusion.1
  137.0 0.2 slice_convert_fusion
  137.3 0.2 slice_bitcast_fusion.1
  137.5 1.5 %pad_maximum_fusion = f32[2,512,512]{2,1,0:T(8,128)} fusion(f32[1,512,512]{2,1,0:T(8,128)S(1)} %get-tuple-element.81, f32[1,512,512]{2,1,0:T(8,128)S(1)} %get-tuple-element.80), kind=kLoop, calls=%fused_computation.1 | loop fusion | flops 524288 | bytes 4194304 | tf_op jit(solution)/shard_map/stack | solution.py:443
  (82 shorter events, 1.0 us)
Async XLA Ops:
  0.6 43.9 %copy-start.21 = (bf16[1024,1024]{1,0:T(8,128)(2,1)S(1)}, bf16[1024,1024]{1,0:T(8,128)(2,1)}, u32[]{:S(2)}) copy-start(bf16[1024,1024]{1,0:T(8,128)(2,1)} %constant.127.clone.left_table) | copy-start | bytes 6291460
  0.6 43.9 %copy-start.22 = (bf16[1024,1024]{1,0:T(8,128)(2,1)S(1)}, bf16[1024,1024]{1,0:T(8,128)(2,1)}, u32[]{:S(2)}) copy-start(bf16[1024,1024]{1,0:T(8,128)(2,1)} %constant.126.clone.right_table) | copy-start | bytes 6291460
  0.7 43.9 %copy-start.18 = (s32[16]{0:T(128)S(1)}, s32[16]{0:T(128)}, u32[]{:S(2)}) copy-start(s32[16]{0:T(128)} %dealing.7) | copy-start | bytes 196
  0.7 43.9 %copy-start.19 = (s32[16]{0:T(128)S(1)}, s32[16]{0:T(128)}, u32[]{:S(2)}) copy-start(s32[16]{0:T(128)} %rows.5) | copy-start | bytes 196
  0.7 43.9 %copy-start.1 = (bf16[2,512,512]{2,1,0:T(8,128)(2,1)S(1)}, bf16[2,512,512]{2,1,0:T(8,128)(2,1)}, u32[]{:S(2)}) copy-start(bf16[2,512,512]{2,1,0:T(8,128)(2,1)} %probe.3) | copy-start | bytes 3145732
  0.7 43.9 %copy-start.20 = (bf16[1,512,512]{2,1,0:T(8,128)(2,1)S(1)}, bf16[1,512,512]{2,1,0:T(8,128)(2,1)}, u32[]{:S(2)}) copy-start(bf16[1,512,512]{2,1,0:T(8,128)(2,1)} %measured.1) | copy-start | bytes 1572868
  5.7 4.3 %collective-permute-start = (bf16[40,1024]{1,0:T(8,128)(2,1)}, bf16[40,1024]{1,0:T(8,128)(2,1)S(1)}, u32[]{:S(2)}, u32[]{:S(2)}) collective-permute-start(bf16[40,1024]{1,0:T(8,128)(2,1)} %get-tuple-element.43.rest_1_), channel_id=1, source_target_pairs={{0,1},{1,0},{2,3},{3,2},{4,5},{5,4},{6,7},{7,6},{8,9},{9,8},{10,11... | collective-permute-start | bytes 245768 | tf_op jit(solution)/shard_map/ppermute | solution.py:102
  6.4 4.2 %collective-permute-start.1 = (bf16[40,1024]{1,0:T(8,128)(2,1)}, bf16[40,1024]{1,0:T(8,128)(2,1)S(1)}, u32[]{:S(2)}, u32[]{:S(2)}) collective-permute-start(bf16[40,1024]{1,0:T(8,128)(2,1)} %get-tuple-element.44.rest_2_), channel_id=1, source_target_pairs={{0,2},{1,3},{2,0},{3,1},{4,6},{5,7},{6,4},{7,5},{8,10},{9,11},{10,... | collective-permute-start | bytes 245768 | tf_op jit(solution)/shard_map/ppermute | solution.py:102
  6.7 6.2 %collective-permute-start.2 = (bf16[40,1024]{1,0:T(8,128)(2,1)}, bf16[40,1024]{1,0:T(8,128)(2,1)S(1)}, u32[]{:S(2)}, u32[]{:S(2)}) collective-permute-start(bf16[40,1024]{1,0:T(8,128)(2,1)} %get-tuple-element.45.rest_3_), channel_id=1, source_target_pairs={{0,3},{1,2},{2,1},{3,0},{4,7},{5,6},{6,5},{7,4},{8,11},{9,10},{10,... | collective-permute-start | bytes 245768 | tf_op jit(solution)/shard_map/ppermute | solution.py:102
  8.1 7.0 %collective-permute-start.3 = (bf16[40,1024]{1,0:T(8,128)(2,1)}, bf16[40,1024]{1,0:T(8,128)(2,1)S(1)}, u32[]{:S(2)}, u32[]{:S(2)}) collective-permute-start(bf16[40,1024]{1,0:T(8,128)(2,1)} %get-tuple-element.46.rest_4_), channel_id=1, source_target_pairs={{0,4},{1,5},{2,6},{3,7},{4,0},{5,1},{6,2},{7,3},{8,12},{9,13},{10,... | collective-permute-start | bytes 245768 | tf_op jit(solution)/shard_map/ppermute | solution.py:102
  8.3 7.7 %collective-permute-start.4 = (bf16[40,1024]{1,0:T(8,128)(2,1)}, bf16[40,1024]{1,0:T(8,128)(2,1)S(1)}, u32[]{:S(2)}, u32[]{:S(2)}) collective-permute-start(bf16[40,1024]{1,0:T(8,128)(2,1)} %get-tuple-element.47.rest_5_), channel_id=1, source_target_pairs={{0,5},{1,4},{2,7},{3,6},{4,1},{5,0},{6,3},{7,2},{8,13},{9,12},{10,... | collective-permute-start | bytes 245768 | tf_op jit(solution)/shard_map/ppermute | solution.py:102
  9.9 7.8 %collective-permute-start.5 = (bf16[40,1024]{1,0:T(8,128)(2,1)}, bf16[40,1024]{1,0:T(8,128)(2,1)S(1)}, u32[]{:S(2)}, u32[]{:S(2)}) collective-permute-start(bf16[40,1024]{1,0:T(8,128)(2,1)} %get-tuple-element.48.rest_6_), channel_id=1, source_target_pairs={{0,6},{1,7},{2,4},{3,5},{4,2},{5,3},{6,0},{7,1},{8,14},{9,15},{10,... | collective-permute-start | bytes 245768 | tf_op jit(solution)/shard_map/ppermute | solution.py:102
  10.7 10.5 %collective-permute-start.6 = (bf16[40,1024]{1,0:T(8,128)(2,1)}, bf16[40,1024]{1,0:T(8,128)(2,1)S(1)}, u32[]{:S(2)}, u32[]{:S(2)}) collective-permute-start(bf16[40,1024]{1,0:T(8,128)(2,1)} %get-tuple-element.49.rest_7_), channel_id=1, source_target_pairs={{0,7},{1,6},{2,5},{3,4},{4,3},{5,2},{6,1},{7,0},{8,15},{9,14},{10,... | collective-permute-start | bytes 245768 | tf_op jit(solution)/shard_map/ppermute | solution.py:102
  12.9 8.3 %collective-permute-start.7 = (bf16[40,1024]{1,0:T(8,128)(2,1)}, bf16[40,1024]{1,0:T(8,128)(2,1)S(1)}, u32[]{:S(2)}, u32[]{:S(2)}) collective-permute-start(bf16[40,1024]{1,0:T(8,128)(2,1)} %get-tuple-element.50.rest_8_), channel_id=1, source_target_pairs={{0,8},{1,9},{2,10},{3,11},{4,12},{5,13},{6,14},{7,15},{8,0},{9,1},... | collective-permute-start | bytes 245768 | tf_op jit(solution)/shard_map/ppermute | solution.py:102
  15.2 12.8 %collective-permute-start.8 = (bf16[40,1024]{1,0:T(8,128)(2,1)}, bf16[40,1024]{1,0:T(8,128)(2,1)S(1)}, u32[]{:S(2)}, u32[]{:S(2)}) collective-permute-start(bf16[40,1024]{1,0:T(8,128)(2,1)} %get-tuple-element.51.rest_9_), channel_id=1, source_target_pairs={{0,9},{1,8},{2,11},{3,10},{4,13},{5,12},{6,15},{7,14},{8,1},{9,0},... | collective-permute-start | bytes 245768 | tf_op jit(solution)/shard_map/ppermute | solution.py:102
  16.0 13.8 %collective-permute-start.9 = (bf16[40,1024]{1,0:T(8,128)(2,1)}, bf16[40,1024]{1,0:T(8,128)(2,1)S(1)}, u32[]{:S(2)}, u32[]{:S(2)}) collective-permute-start(bf16[40,1024]{1,0:T(8,128)(2,1)} %get-tuple-element.52.rest_10_), channel_id=1, source_target_pairs={{0,10},{1,11},{2,8},{3,9},{4,14},{5,15},{6,12},{7,13},{8,2},{9,3},... | collective-permute-start | bytes 245768 | tf_op jit(solution)/shard_map/ppermute | solution.py:102
  17.7 14.1 %collective-permute-start.10 = (bf16[40,1024]{1,0:T(8,128)(2,1)}, bf16[40,1024]{1,0:T(8,128)(2,1)S(1)}, u32[]{:S(2)}, u32[]{:S(2)}) collective-permute-start(bf16[40,1024]{1,0:T(8,128)(2,1)} %get-tuple-element.53.rest_11_), channel_id=1, source_target_pairs={{0,11},{1,10},{2,9},{3,8},{4,15},{5,14},{6,13},{7,12},{8,3},{9,2},... | collective-permute-start | bytes 245768 | tf_op jit(solution)/shard_map/ppermute | solution.py:102
  21.2 17.2 %collective-permute-start.11 = (bf16[40,1024]{1,0:T(8,128)(2,1)}, bf16[40,1024]{1,0:T(8,128)(2,1)S(1)}, u32[]{:S(2)}, u32[]{:S(2)}) collective-permute-start(bf16[40,1024]{1,0:T(8,128)(2,1)} %get-tuple-element.54.rest_12_), channel_id=1, source_target_pairs={{0,12},{1,13},{2,14},{3,15},{4,8},{5,9},{6,10},{7,11},{8,4},{9,5},... | collective-permute-start | bytes 245768 | tf_op jit(solution)/shard_map/ppermute | solution.py:102
  21.2 19.9 %collective-permute-start.12 = (bf16[40,1024]{1,0:T(8,128)(2,1)}, bf16[40,1024]{1,0:T(8,128)(2,1)S(1)}, u32[]{:S(2)}, u32[]{:S(2)}) collective-permute-start(bf16[40,1024]{1,0:T(8,128)(2,1)} %get-tuple-element.55.rest_13_), channel_id=1, source_target_pairs={{0,13},{1,12},{2,15},{3,14},{4,9},{5,8},{6,11},{7,10},{8,5},{9,4},... | collective-permute-start | bytes 245768 | tf_op jit(solution)/shard_map/ppermute | solution.py:102
  28.0 14.5 %collective-permute-start.13 = (bf16[40,1024]{1,0:T(8,128)(2,1)}, bf16[40,1024]{1,0:T(8,128)(2,1)S(1)}, u32[]{:S(2)}, u32[]{:S(2)}) collective-permute-start(bf16[40,1024]{1,0:T(8,128)(2,1)} %get-tuple-element.56.rest_14_), channel_id=1, source_target_pairs={{0,14},{1,15},{2,12},{3,13},{4,10},{5,11},{6,8},{7,9},{8,6},{9,7},... | collective-permute-start | bytes 245768 | tf_op jit(solution)/shard_map/ppermute | solution.py:102
  29.7 14.8 %collective-permute-start.14 = (bf16[40,1024]{1,0:T(8,128)(2,1)}, bf16[40,1024]{1,0:T(8,128)(2,1)S(1)}, u32[]{:S(2)}, u32[]{:S(2)}) collective-permute-start(bf16[40,1024]{1,0:T(8,128)(2,1)} %get-tuple-element.57.rest_15_), channel_id=1, source_target_pairs={{0,15},{1,14},{2,13},{3,12},{4,11},{5,10},{6,9},{7,8},{8,7},{9,6},... | collective-permute-start | bytes 245768 | tf_op jit(solution)/shard_map/ppermute | solution.py:102
  44.6 0.9 copy-start.2
  45.5 45.9 %copy-start.3 = (bf16[40,1024]{1,0:T(8,128)(2,1)S(1)}, bf16[40,1024]{1,0:T(8,128)(2,1)}, u32[]{:S(2)}) copy-start(bf16[40,1024]{1,0:T(8,128)(2,1)} %get-tuple-element.43.rest_1_) | copy-start | bytes 245764
  45.5 45.9 %copy-start.4 = (bf16[40,1024]{1,0:T(8,128)(2,1)S(1)}, bf16[40,1024]{1,0:T(8,128)(2,1)}, u32[]{:S(2)}) copy-start(bf16[40,1024]{1,0:T(8,128)(2,1)} %get-tuple-element.44.rest_2_) | copy-start | bytes 245764
  45.5 45.9 %copy-start.5 = (bf16[40,1024]{1,0:T(8,128)(2,1)S(1)}, bf16[40,1024]{1,0:T(8,128)(2,1)}, u32[]{:S(2)}) copy-start(bf16[40,1024]{1,0:T(8,128)(2,1)} %get-tuple-element.45.rest_3_) | copy-start | bytes 245764
  45.5 45.9 %copy-start.6 = (bf16[40,1024]{1,0:T(8,128)(2,1)S(1)}, bf16[40,1024]{1,0:T(8,128)(2,1)}, u32[]{:S(2)}) copy-start(bf16[40,1024]{1,0:T(8,128)(2,1)} %get-tuple-element.46.rest_4_) | copy-start | bytes 245764
  45.5 45.9 %copy-start.7 = (bf16[40,1024]{1,0:T(8,128)(2,1)S(1)}, bf16[40,1024]{1,0:T(8,128)(2,1)}, u32[]{:S(2)}) copy-start(bf16[40,1024]{1,0:T(8,128)(2,1)} %get-tuple-element.47.rest_5_) | copy-start | bytes 245764
  45.5 45.9 %copy-start.8 = (bf16[40,1024]{1,0:T(8,128)(2,1)S(1)}, bf16[40,1024]{1,0:T(8,128)(2,1)}, u32[]{:S(2)}) copy-start(bf16[40,1024]{1,0:T(8,128)(2,1)} %get-tuple-element.48.rest_6_) | copy-start | bytes 245764
  45.5 45.9 %copy-start.9 = (bf16[40,1024]{1,0:T(8,128)(2,1)S(1)}, bf16[40,1024]{1,0:T(8,128)(2,1)}, u32[]{:S(2)}) copy-start(bf16[40,1024]{1,0:T(8,128)(2,1)} %get-tuple-element.49.rest_7_) | copy-start | bytes 245764
  45.5 45.9 %copy-start.10 = (bf16[40,1024]{1,0:T(8,128)(2,1)S(1)}, bf16[40,1024]{1,0:T(8,128)(2,1)}, u32[]{:S(2)}) copy-start(bf16[40,1024]{1,0:T(8,128)(2,1)} %get-tuple-element.50.rest_8_) | copy-start | bytes 245764
  45.6 45.9 %copy-start.11 = (bf16[40,1024]{1,0:T(8,128)(2,1)S(1)}, bf16[40,1024]{1,0:T(8,128)(2,1)}, u32[]{:S(2)}) copy-start(bf16[40,1024]{1,0:T(8,128)(2,1)} %get-tuple-element.51.rest_9_) | copy-start | bytes 245764
  45.6 45.9 %copy-start.12 = (bf16[40,1024]{1,0:T(8,128)(2,1)S(1)}, bf16[40,1024]{1,0:T(8,128)(2,1)}, u32[]{:S(2)}) copy-start(bf16[40,1024]{1,0:T(8,128)(2,1)} %get-tuple-element.52.rest_10_) | copy-start | bytes 245764
  45.6 45.9 %copy-start.13 = (bf16[40,1024]{1,0:T(8,128)(2,1)S(1)}, bf16[40,1024]{1,0:T(8,128)(2,1)}, u32[]{:S(2)}) copy-start(bf16[40,1024]{1,0:T(8,128)(2,1)} %get-tuple-element.53.rest_11_) | copy-start | bytes 245764
  45.6 45.9 %copy-start.14 = (bf16[40,1024]{1,0:T(8,128)(2,1)S(1)}, bf16[40,1024]{1,0:T(8,128)(2,1)}, u32[]{:S(2)}) copy-start(bf16[40,1024]{1,0:T(8,128)(2,1)} %get-tuple-element.54.rest_12_) | copy-start | bytes 245764
  45.6 45.9 %copy-start.15 = (bf16[40,1024]{1,0:T(8,128)(2,1)S(1)}, bf16[40,1024]{1,0:T(8,128)(2,1)}, u32[]{:S(2)}) copy-start(bf16[40,1024]{1,0:T(8,128)(2,1)} %get-tuple-element.55.rest_13_) | copy-start | bytes 245764
  45.6 45.9 %copy-start.16 = (bf16[40,1024]{1,0:T(8,128)(2,1)S(1)}, bf16[40,1024]{1,0:T(8,128)(2,1)}, u32[]{:S(2)}) copy-start(bf16[40,1024]{1,0:T(8,128)(2,1)} %get-tuple-element.56.rest_14_) | copy-start | bytes 245764
  45.6 45.9 %copy-start.17 = (bf16[40,1024]{1,0:T(8,128)(2,1)S(1)}, bf16[40,1024]{1,0:T(8,128)(2,1)}, u32[]{:S(2)}) copy-start(bf16[40,1024]{1,0:T(8,128)(2,1)} %get-tuple-element.57.rest_15_) | copy-start | bytes 245764
  52.7 3.6 %collective-permute-start.15 = (bf16[40,1024]{1,0:T(8,128)(2,1)S(1)}, bf16[40,1024]{1,0:T(8,128)(2,1)S(1)}, u32[]{:S(2)}, u32[]{:S(2)}) collective-permute-start(bf16[40,1024]{1,0:T(8,128)(2,1)S(1)} %get-tuple-element.59), channel_id=1, source_target_pairs={{0,1},{1,0},{2,3},{3,2},{4,5},{5,4},{6,7},{7,6},{8,9},{9,8},{10,11... | collective-permute-start | bytes 245768 | tf_op jit(solution)/shard_map/ppermute | solution.py:102
  52.8 4.0 %collective-permute-start.16 = (bf16[40,1024]{1,0:T(8,128)(2,1)S(1)}, bf16[40,1024]{1,0:T(8,128)(2,1)S(1)}, u32[]{:S(2)}, u32[]{:S(2)}) collective-permute-start(bf16[40,1024]{1,0:T(8,128)(2,1)S(1)} %get-tuple-element.60), channel_id=1, source_target_pairs={{0,2},{1,3},{2,0},{3,1},{4,6},{5,7},{6,4},{7,5},{8,10},{9,11},{10,... | collective-permute-start | bytes 245768 | tf_op jit(solution)/shard_map/ppermute | solution.py:102
  53.7 5.6 %collective-permute-start.17 = (bf16[40,1024]{1,0:T(8,128)(2,1)S(1)}, bf16[40,1024]{1,0:T(8,128)(2,1)S(1)}, u32[]{:S(2)}, u32[]{:S(2)}) collective-permute-start(bf16[40,1024]{1,0:T(8,128)(2,1)S(1)} %get-tuple-element.61), channel_id=1, source_target_pairs={{0,3},{1,2},{2,1},{3,0},{4,7},{5,6},{6,5},{7,4},{8,11},{9,10},{10,... | collective-permute-start | bytes 245768 | tf_op jit(solution)/shard_map/ppermute | solution.py:102
  54.9 6.9 %collective-permute-start.18 = (bf16[40,1024]{1,0:T(8,128)(2,1)S(1)}, bf16[40,1024]{1,0:T(8,128)(2,1)S(1)}, u32[]{:S(2)}, u32[]{:S(2)}) collective-permute-start(bf16[40,1024]{1,0:T(8,128)(2,1)S(1)} %get-tuple-element.62), channel_id=1, source_target_pairs={{0,4},{1,5},{2,6},{3,7},{4,0},{5,1},{6,2},{7,3},{8,12},{9,13},{10,... | collective-permute-start | bytes 245768 | tf_op jit(solution)/shard_map/ppermute | solution.py:102
  54.9 6.9 %collective-permute-start.19 = (bf16[40,1024]{1,0:T(8,128)(2,1)S(1)}, bf16[40,1024]{1,0:T(8,128)(2,1)S(1)}, u32[]{:S(2)}, u32[]{:S(2)}) collective-permute-start(bf16[40,1024]{1,0:T(8,128)(2,1)S(1)} %get-tuple-element.63), channel_id=1, source_target_pairs={{0,5},{1,4},{2,7},{3,6},{4,1},{5,0},{6,3},{7,2},{8,13},{9,12},{10,... | collective-permute-start | bytes 245768 | tf_op jit(solution)/shard_map/ppermute | solution.py:102
  56.3 7.3 %collective-permute-start.20 = (bf16[40,1024]{1,0:T(8,128)(2,1)S(1)}, bf16[40,1024]{1,0:T(8,128)(2,1)S(1)}, u32[]{:S(2)}, u32[]{:S(2)}) collective-permute-start(bf16[40,1024]{1,0:T(8,128)(2,1)S(1)} %get-tuple-element.64), channel_id=1, source_target_pairs={{0,6},{1,7},{2,4},{3,5},{4,2},{5,3},{6,0},{7,1},{8,14},{9,15},{10,... | collective-permute-start | bytes 245768 | tf_op jit(solution)/shard_map/ppermute | solution.py:102
  56.8 8.9 %collective-permute-start.21 = (bf16[40,1024]{1,0:T(8,128)(2,1)S(1)}, bf16[40,1024]{1,0:T(8,128)(2,1)S(1)}, u32[]{:S(2)}, u32[]{:S(2)}) collective-permute-start(bf16[40,1024]{1,0:T(8,128)(2,1)S(1)} %get-tuple-element.65), channel_id=1, source_target_pairs={{0,7},{1,6},{2,5},{3,4},{4,3},{5,2},{6,1},{7,0},{8,15},{9,14},{10,... | collective-permute-start | bytes 245768 | tf_op jit(solution)/shard_map/ppermute | solution.py:102
  59.3 14.3 %collective-permute-start.22 = (bf16[40,1024]{1,0:T(8,128)(2,1)S(1)}, bf16[40,1024]{1,0:T(8,128)(2,1)S(1)}, u32[]{:S(2)}, u32[]{:S(2)}) collective-permute-start(bf16[40,1024]{1,0:T(8,128)(2,1)S(1)} %get-tuple-element.66), channel_id=1, source_target_pairs={{0,8},{1,9},{2,10},{3,11},{4,12},{5,13},{6,14},{7,15},{8,0},{9,1},... | collective-permute-start | bytes 245768 | tf_op jit(solution)/shard_map/ppermute | solution.py:102
  61.8 13.7 %collective-permute-start.23 = (bf16[40,1024]{1,0:T(8,128)(2,1)S(1)}, bf16[40,1024]{1,0:T(8,128)(2,1)S(1)}, u32[]{:S(2)}, u32[]{:S(2)}) collective-permute-start(bf16[40,1024]{1,0:T(8,128)(2,1)S(1)} %get-tuple-element.67), channel_id=1, source_target_pairs={{0,9},{1,8},{2,11},{3,10},{4,13},{5,12},{6,15},{7,14},{8,1},{9,0},... | collective-permute-start | bytes 245768 | tf_op jit(solution)/shard_map/ppermute | solution.py:102
  61.8 15.4 %collective-permute-start.24 = (bf16[40,1024]{1,0:T(8,128)(2,1)S(1)}, bf16[40,1024]{1,0:T(8,128)(2,1)S(1)}, u32[]{:S(2)}, u32[]{:S(2)}) collective-permute-start(bf16[40,1024]{1,0:T(8,128)(2,1)S(1)} %get-tuple-element.68), channel_id=1, source_target_pairs={{0,10},{1,11},{2,8},{3,9},{4,14},{5,15},{6,12},{7,13},{8,2},{9,3},... | collective-permute-start | bytes 245768 | tf_op jit(solution)/shard_map/ppermute | solution.py:102
  63.6 16.1 %collective-permute-start.25 = (bf16[40,1024]{1,0:T(8,128)(2,1)S(1)}, bf16[40,1024]{1,0:T(8,128)(2,1)S(1)}, u32[]{:S(2)}, u32[]{:S(2)}) collective-permute-start(bf16[40,1024]{1,0:T(8,128)(2,1)S(1)} %get-tuple-element.69), channel_id=1, source_target_pairs={{0,11},{1,10},{2,9},{3,8},{4,15},{5,14},{6,13},{7,12},{8,3},{9,2},... | collective-permute-start | bytes 245768 | tf_op jit(solution)/shard_map/ppermute | solution.py:102
  65.7 19.3 %collective-permute-start.26 = (bf16[40,1024]{1,0:T(8,128)(2,1)S(1)}, bf16[40,1024]{1,0:T(8,128)(2,1)S(1)}, u32[]{:S(2)}, u32[]{:S(2)}) collective-permute-start(bf16[40,1024]{1,0:T(8,128)(2,1)S(1)} %get-tuple-element.70), channel_id=1, source_target_pairs={{0,12},{1,13},{2,14},{3,15},{4,8},{5,9},{6,10},{7,11},{8,4},{9,5},... | collective-permute-start | bytes 245768 | tf_op jit(solution)/shard_map/ppermute | solution.py:102
  73.6 13.8 %collective-permute-start.27 = (bf16[40,1024]{1,0:T(8,128)(2,1)S(1)}, bf16[40,1024]{1,0:T(8,128)(2,1)S(1)}, u32[]{:S(2)}, u32[]{:S(2)}) collective-permute-start(bf16[40,1024]{1,0:T(8,128)(2,1)S(1)} %get-tuple-element.71), channel_id=1, source_target_pairs={{0,13},{1,12},{2,15},{3,14},{4,9},{5,8},{6,11},{7,10},{8,5},{9,4},... | collective-permute-start | bytes 245768 | tf_op jit(solution)/shard_map/ppermute | solution.py:102
  75.5 14.2 %collective-permute-start.28 = (bf16[40,1024]{1,0:T(8,128)(2,1)S(1)}, bf16[40,1024]{1,0:T(8,128)(2,1)S(1)}, u32[]{:S(2)}, u32[]{:S(2)}) collective-permute-start(bf16[40,1024]{1,0:T(8,128)(2,1)S(1)} %get-tuple-element.72), channel_id=1, source_target_pairs={{0,14},{1,15},{2,12},{3,13},{4,10},{5,11},{6,8},{7,9},{8,6},{9,7},... | collective-permute-start | bytes 245768 | tf_op jit(solution)/shard_map/ppermute | solution.py:102
  77.2 14.2 %collective-permute-start.29 = (bf16[40,1024]{1,0:T(8,128)(2,1)S(1)}, bf16[40,1024]{1,0:T(8,128)(2,1)S(1)}, u32[]{:S(2)}, u32[]{:S(2)}) collective-permute-start(bf16[40,1024]{1,0:T(8,128)(2,1)S(1)} %get-tuple-element.73), channel_id=1, source_target_pairs={{0,15},{1,14},{2,13},{3,12},{4,11},{5,10},{6,9},{7,8},{8,7},{9,6},... | collective-permute-start | bytes 245768 | tf_op jit(solution)/shard_map/ppermute | solution.py:102
  91.5 28.1 %copy-start = (s32[16]{0:T(128)S(1)}, s32[16]{0:T(128)}, u32[]{:S(2)}) copy-start(s32[16]{0:T(128)} %cols.3) | copy-start | bytes 196
  93.2 11.8 %collective-permute-start.30 = (bf16[40,1024]{1,0:T(8,128)(2,1)S(1)}, bf16[40,1024]{1,0:T(8,128)(2,1)S(1)}, u32[]{:S(2)}, u32[]{:S(2)}) collective-permute-start(bf16[40,1024]{1,0:T(8,128)(2,1)S(1)} %get-tuple-element.76), channel_id=1, source_target_pairs={{4,2},{5,3},{6,4},{7,5},{8,6},{9,7},{10,8},{11,9},{12,10},{13,11},... | collective-permute-start | bytes 245768 | tf_op jit(solution)/shard_map/ppermute | solution.py:414
  95.5 9.5 %collective-permute-start.31 = (bf16[40,1024]{1,0:T(8,128)(2,1)S(1)}, bf16[40,1024]{1,0:T(8,128)(2,1)S(1)}, u32[]{:S(2)}, u32[]{:S(2)}) collective-permute-start(bf16[40,1024]{1,0:T(8,128)(2,1)S(1)} %get-tuple-element.77), channel_id=1, source_target_pairs={{3,2},{4,3},{5,4},{6,5},{7,6},{8,7},{9,8},{10,9},{11,10},{12,11},{... | collective-permute-start | bytes 245768 | tf_op jit(solution)/shard_map/ppermute | solution.py:414
  98.0 7.0 %collective-permute-start.32 = (bf16[40,1024]{1,0:T(8,128)(2,1)S(1)}, bf16[40,1024]{1,0:T(8,128)(2,1)S(1)}, u32[]{:S(2)}, u32[]{:S(2)}) collective-permute-start(bf16[40,1024]{1,0:T(8,128)(2,1)S(1)} %get-tuple-element.78), channel_id=1, source_target_pairs={{1,2},{2,3},{3,4},{4,5},{5,6},{6,7},{7,8},{8,9},{9,10},{10,11},{11... | collective-permute-start | bytes 245768 | tf_op jit(solution)/shard_map/ppermute | solution.py:414
  102.0 5.3 %collective-permute-start.33 = (bf16[40,1024]{1,0:T(8,128)(2,1)S(1)}, bf16[40,1024]{1,0:T(8,128)(2,1)S(1)}, u32[]{:S(2)}, u32[]{:S(2)}) collective-permute-start(bf16[40,1024]{1,0:T(8,128)(2,1)S(1)} %get-tuple-element.79), channel_id=1, source_target_pairs={{0,2},{1,3},{2,4},{3,5},{4,6},{5,7},{6,8},{7,9},{8,10},{9,11},{10,... | collective-permute-start | bytes 245768 | tf_op jit(solution)/shard_map/ppermute | solution.py:414
  107.3 3.9 %collective-permute-start.36 = (bf16[40,1024]{1,0:T(8,128)(2,1)S(1)}, bf16[40,1024]{1,0:T(8,128)(2,1)S(1)}, u32[]{:S(2)}, u32[]{:S(2)}) collective-permute-start(bf16[40,1024]{1,0:T(8,128)(2,1)S(1)} %multiply_convert_fusion), channel_id=1, source_target_pairs={{0,4},{1,5},{2,6},{3,7},{4,8},{5,9},{6,10},{7,11},{8,12},{9,13},{1... | collective-permute-start | bytes 245768 | tf_op jit(solution)/shard_map/ppermute | solution.py:374
  108.7 6.9 %collective-permute-start.35 = (bf16[40,1024]{1,0:T(8,128)(2,1)S(1)}, bf16[40,1024]{1,0:T(8,128)(2,1)S(1)}, u32[]{:S(2)}, u32[]{:S(2)}) collective-permute-start(bf16[40,1024]{1,0:T(8,128)(2,1)S(1)} %multiply_convert_fusion), channel_id=1, source_target_pairs={{0,8},{1,9},{2,10},{3,11},{4,12},{5,13},{6,14},{7,15},{8,0},{9,1},... | collective-permute-start | bytes 245768 | tf_op jit(solution)/shard_map/ppermute | solution.py:374
  108.7 6.9 %collective-permute-start.34 = (bf16[40,1024]{1,0:T(8,128)(2,1)S(1)}, bf16[40,1024]{1,0:T(8,128)(2,1)S(1)}, u32[]{:S(2)}, u32[]{:S(2)}) collective-permute-start(bf16[40,1024]{1,0:T(8,128)(2,1)S(1)} %multiply_convert_fusion), channel_id=1, source_target_pairs={{0,12},{1,13},{2,14},{3,15},{4,0},{5,1},{6,2},{7,3},{8,4},{9,5},{1... | collective-permute-start | bytes 245768 | tf_op jit(solution)/shard_map/ppermute | solution.py:374
  115.7 11.7 %collective-permute-start.37 = (bf16[4,40,1024]{2,1,0:T(8,128)(2,1)S(1)}, bf16[4,40,1024]{2,1,0:T(8,128)(2,1)}, u32[]{:S(2)}, u32[]{:S(2)}) collective-permute-start(bf16[4,40,1024]{2,1,0:T(8,128)(2,1)S(1)} %pad_maximum_fusion.3), channel_id=1, source_target_pairs={{0,2},{1,3},{2,0},{3,1},{4,6},{5,7},{6,4},{7,5},{8,10},{9,11},{10,... | collective-permute-start | bytes 983048 | tf_op jit(solution)/shard_map/ppermute | solution.py:374
  129.4 6.2 %collective-permute-start.38 = (bf16[4,2,40,1024]{3,2,0,1:T(8,128)(2,1)}, bf16[4,2,40,1024]{3,2,0,1:T(8,128)(2,1)}, u32[]{:S(2)}, u32[]{:S(2)}) collective-permute-start(bf16[4,2,40,1024]{3,2,0,1:T(8,128)(2,1)} %pad_maximum_fusion.2), channel_id=1, source_target_pairs={{0,1},{1,0},{2,3},{3,2},{4,5},{5,4},{6,7},{7,6},{8,9},{9,8},{10,11... | collective-permute-start | bytes 1966088 | tf_op jit(solution)/shard_map/ppermute | solution.py:374

commit v5 on v2

--- a/solution.py
+++ b/solution.py
@@ -97,9 +97,9 @@
 
 
 def slot_kernel(
-    dealing, rows, cells, probe, measured, right, left,
+    dealing, rows, cells, probe, measured, right_table, left_table,
     terms, kept, sent, empty,
-    wide, patch, wave, half, resid, turned, padded, mine, zeros, sem,
+    wide, patch, wave, half, resid, turned, padded, mine, zeros, right, left, sem, table_sem,
 ):
     order = probe.shape[1]
     total_rows = cells.shape[0]
@@ -109,6 +109,10 @@
     step = 64
     tile = 256
 
+    right_copy = pltpu.make_async_copy(right_table, right, table_sem.at[0])
+    left_copy = pltpu.make_async_copy(left_table, left, table_sem.at[1])
+    right_copy.start()
+    left_copy.start()
     zeros[...] = jnp.zeros_like(zeros)
     fills = []
     for b in range(empty.shape[2] // zeros.shape[2]):
@@ -137,11 +141,13 @@
     def dot(a, b):
         return jnp.dot(a, b, preferred_element_type=jnp.float32)
 
+    right_copy.wait()
     for first in range(0, order, tile):
         here = slice(first, first + tile)
         there = slice(order + first, order + first + tile)
         half[:order, here] = dot(wave[...], right[:, here]).astype(half.dtype)
         half[order:, here] = dot(wave[...], right[:, there]).astype(half.dtype)
+    left_copy.wait()
     for first in range(0, order, tile):
         here = slice(first, first + tile)
         there = slice(order + first, order + first + tile)
@@ -203,7 +209,7 @@
             jax.ShapeDtypeStruct((order // 2, wide_cols), bf16),
             jax.ShapeDtypeStruct((2, tile_rows, tile_cols), f32),
         ),
-        in_specs=[SMEM, SMEM, VMEM, VMEM, VMEM, VMEM, VMEM],
+        in_specs=[SMEM, SMEM, VMEM, VMEM, VMEM, ANY, ANY],
         out_specs=(VMEM, VMEM, VMEM, ANY),
         scratch_shapes=[
             pltpu.VMEM((total_rows + SUBLANES, wide_cols), f32),
@@ -215,7 +221,10 @@
             pltpu.VMEM((2 * total_rows - order + SUBLANES, wide_cols), f32),
             pltpu.VMEM((order, wide_cols), f32),
             pltpu.VMEM((2, tile_rows, fill_cols), f32),
+            pltpu.VMEM((wide_cols, wide_cols), bf16),
+            pltpu.VMEM((wide_cols, wide_cols), bf16),
             pltpu.SemaphoreType.DMA((tile_cols // fill_cols,)),
+            pltpu.SemaphoreType.DMA((2,)),
         ],
         compiler_params=pltpu.CompilerParams(vmem_limit_bytes=40 * 2**20),
         cost_estimate=pl.CostEstimate(
@@ -296,49 +305,18 @@
     )(dealing, cols, blocks, owners, terms, empty)
 
 
-def strides(devices):
-    steps, stride = [], 1
-    while stride < devices:
-        radix = 4 if len(steps) >= 2 and (devices // stride) % 4 == 0 else 2
-        steps.append((stride, radix))
-        stride *= radix
-    return steps
-
-
-def turn(x, stride, radix, distance, devices):
-    pairs = []
-    for d in range(devices):
-        digit = d // stride % radix
-        pairs.append((d, d + ((digit + distance) % radix - digit) * stride))
-    return lax.ppermute(x, "row", pairs)
+def swap_sides(x, devices):
+    return lax.ppermute(x, "row", [(d, d ^ 1) for d in range(devices)])
 
 
 def sum_probe(kept, sent, devices, scale):
-    me = lax.axis_index("row")
-    steps = strides(devices)
-    total = kept + turn(sent, 1, 2, 1, devices).astype(jnp.float32)
-    for stride, radix in steps[1:]:
-        digit = me // stride % radix
-        count = total.shape[0] // radix
-        own = lax.dynamic_slice_in_dim(total, digit * count, count)
-        for distance in range(1, radix):
-            other = lax.rem(digit + distance, radix)
-            share = lax.dynamic_slice_in_dim(total, other * count, count).astype(jnp.bfloat16)
-            own = own + turn(share, stride, radix, distance, devices).astype(jnp.float32)
-        total = own
-    whole = (total * scale).astype(jnp.bfloat16)
-    for stride, radix in reversed(steps):
-        digit = me // stride % radix
-        shares = [whole] + [turn(whole, stride, radix, distance, devices) for distance in range(1, radix)]
-        order = [lax.rem(digit - k + radix, radix) for k in range(radix)]
-        rows = []
-        for k in range(radix):
-            piece = shares[0]
-            for d in range(1, radix):
-                piece = jnp.where(order[k] == d, shares[d], piece)
-            rows.append(piece)
-        whole = jnp.concatenate(rows, axis=0)
-    return whole
+    side = lax.rem(lax.axis_index("row"), 2)
+    total = (kept + swap_sides(sent, devices).astype(jnp.float32)).astype(jnp.bfloat16)
+    groups = [list(range(core, devices, 2)) for core in range(2)]
+    total = lax.psum(total, "row", axis_index_groups=groups)
+    mine = (total.astype(jnp.float32) * scale).astype(jnp.bfloat16)
+    other = swap_sides(mine, devices)
+    return jnp.where(side == 0, jnp.concatenate([mine, other]), jnp.concatenate([other, mine]))
 
 
 def body(object_field, probe, amplitude, row_offsets, col_offsets, dealing):
@@ -359,12 +337,7 @@
     if spare:
         outgoing = jnp.pad(outgoing, ((0, 0), (0, spare), (0, 0)))
     arrived = lax.all_to_all(outgoing, "row", split_axis=0, concat_axis=0, tiled=True)
-    rounds = jnp.minimum(dealing[0] + 1, 1)
-    _, whole = lax.while_loop(
-        lambda state: state[0] < rounds,
-        lambda state: (state[0] + 1, sum_probe(kept, sent, devices, 1.0 / dealing.shape[0])),
-        (jnp.zeros((), jnp.int32), jnp.zeros((order, 2 * order), jnp.bfloat16)),
-    )
+    whole = sum_probe(kept, sent, devices, 1.0 / dealing.shape[0])
     whole = whole.astype(jnp.float32)
     probe_grad = jnp.stack([whole[:, :order], whole[:, order:]])
     object_grad = place_windows(arrived, empty, dealing, col_offsets, order)

time: 125 us -> 169 us (1.35)
  blocking collectives: 0 us -> 37.1 us
  starting transfers between devices: 25.8 us -> 7.67 us
  waiting for transfers between devices: 66.4 us -> 83.5 us
  between operations: 0.8 us -> 14.2 us
  local copies, waits for them, and re-layouts: 5.33 us -> 0.99 us
  other arithmetic: 6.9 us -> 4.81 us
    psum x0 -> x1, waiting for transfers between devices: none -> 82.8 us  [sum_probe(): total = lax.psum(total, 'row', axis_index_groups=groups)]
    all_to_all x0 -> x1, blocking collectives: none -> 37.1 us  [body(): lax.all_to_all(pieces, 'row', split_axis=0, concat_axis=0, tiled=True)]
    ppermute x10 -> x2, waiting for transfers between devices: 36.5 us -> 0.65 us  [swap_sides(): return lax.ppermute(x, 'row', [(d, d ^ 1) for d in range(devices)])]
    all_to_all x1 -> x0, waiting for transfers between devices: 29.9 us -> none  [body(): lax.all_to_all(pieces, 'row', split_axis=0, concat_axis=0, tiled=True)]
    ppermute x10 -> x2, starting transfers between devices: 14.1 us -> 2.27 us  [swap_sides(): return lax.ppermute(x, 'row', [(d, d ^ 1) for d in range(devices)])]
    all_to_all x1 -> x0, starting transfers between devices: 6.7 us -> none  [body(): lax.all_to_all(pieces, 'row', split_axis=0, concat_axis=0, tiled=True)]
    unnamed x14, local copies, waits for them, and re-layouts: 3.21 us -> 0.04 us
    convert_element_type x1 -> x2, other arithmetic: 0.04 us -> 2.09 us  [the longest x1 1.14 us: sum_probe(): mine = (total.astype(jnp.float32) * scale).astype(jnp.bfloat16)]
  transfers between devices with their start and end apart: 12 -> 4, of which waited for: 8 -> 2; matrix products, arithmetic and copies ran while one was open for 7% -> 3% of each run, Pallas kernels for 0% -> 0%
where the time goes in v5:
time: 169 us; the launch traced here: 167 us
  waiting for transfers between devices  83.5 us (49%)
  blocking collectives  37.1 us (22%)
  Pallas kernels  18.4 us (11%)
  between operations  14.2 us (8%)
  starting transfers between devices  7.67 us (5%)
  other arithmetic  4.81 us (3%)
    psum x1, waiting for transfers between devices, sum_probe(): total = lax.psum(total, 'row', axis_index_groups=groups)  82.8 us
    all_to_all x1, blocking collectives, body(): lax.all_to_all(pieces, 'row', split_axis=0, concat_axis=0, tiled=True)  37.1 us
    pallas_call x1, Pallas kernels, slot_terms(): pl.pallas_call(slot_kernel, out_shape=(jax.ShapeDtypeStruct((total_rows,...  8.7 us
    all_to_all x1, starting transfers between devices, body(): lax.all_to_all(outgoing, 'row', split_axis=0, concat_axis=0, tiled=True)  5.37 us
    pallas_call x1, Pallas kernels, fetch_windows(): pl.pallas_call(functools.partial(fetch_kernel, order), out_shape=jax.Shap...  5.14 us
    pallas_call x1, Pallas kernels, place_windows(): pl.pallas_call(functools.partial(place_kernel, order), out_shape=jax.Shap...  4.52 us
  transfers between devices with their start and end apart: 4, of which 2 were waited for; matrix products, arithmetic and copies ran while one was open for 3% of the time, Pallas kernels for 0%

profile of v5, /device:TPU:15, one launch (start us, length us, event | category | flops | bytes accessed | tf_op | source)
XLA Modules:
  0.0 166.7 jit_solution(15356478102920397571)
XLA Ops:
  7.2 0.0 copy-start.5
  7.2 0.0 copy-start.6
  7.2 5.1 %fetch.1 = bf16[16,40,1024]{2,1,0:T(8,128)(2,1)} custom-call(s32[16]{0:T(128)} %dealing.5, s32[16]{0:T(128)} %cols.3, f32[2,40,32768]{2,1,0:T(8,128)} %tile.1), custom_call_target="tpu_custom_call" | custom-call | bytes 6291456 | tf_op jit(solution)/shard_map/fetch/pallas_call | solution.py:84
  12.3 0.0 copy-start.1
  12.4 0.0 copy-start.2
  12.4 0.0 copy-start.3
  12.4 0.0 copy-start.4
  12.4 37.1 %all_to_all.10 = bf16[16,40,1024]{2,1,0:T(8,128)(2,1)S(1)} all-to-all(bf16[16,40,1024]{2,1,0:T(8,128)(2,1)} %fetch.1), channel_id=1, replica_groups=mesh['groups'=2,'row'=16] {'row'}, dimensions={0} | all-to-all | bytes 2621440 | tf_op jit(solution)/shard_map/all_to_all | solution.py:331
  49.5 0.0 copy-done.5
  49.5 0.0 copy-done.6
  49.5 0.0 copy-done.1
  49.5 0.0 copy-done.2
  49.6 0.0 copy-done.3
  49.6 0.0 copy-done.4
  49.6 8.7 %slot.1 = (bf16[640,1024]{1,0:T(8,128)(2,1)}, f32[256,1024]{1,0:T(8,128)S(1)}, bf16[256,1024]{1,0:T(8,128)(2,1)S(1)}, f32[2,40,32768]{2,1,0:T(8,128)}) custom-call(s32[16]{0:T(128)S(1)} %copy-done.1, s32[16]{0:T(128)S(1)} %copy-done.4, bf16[640,1024]{1,0:T(8,128)(2,1)S(1)} %bitcast.6, bf16[2,512,512]{2,1,0:T(8,128)(2,1)S(1)} %copy-done.2, ...), custom_call_target="tpu_custom_call" | custom-call | flops 4294967296 | bytes 20971520 | tf_op jit(solution)/shard_map/slot/pallas_call | solution.py:204
  58.3 0.3 collective-permute-start
  58.6 0.0 copy-start
  58.6 5.4 %all-to-all-start.1 = ((bf16[16,40,1024]{2,1,0:T(8,128)(2,1)}), bf16[16,40,1024]{2,1,0:T(8,128)(2,1)S(1)}, u32[]{:S(2)}, u32[]{:S(2)}) async-start(bf16[16,40,1024]{2,1,0:T(8,128)(2,1)} %bitcast.1), calls=%async_computation.1 | async-start | bytes 2621440 | tf_op jit(solution)/shard_map/all_to_all | solution.py:339
  63.9 0.0 all-reduce.2.cloned.1.call-start
  64.0 0.0 collective-permute-done
  64.0 0.9 add_convert_fusion
  64.9 0.0 all-reduce.2.cloned.1.call-update
  65.0 0.0 copy-done
  65.0 0.7 gather_fusion
  65.7 82.8 %all-reduce.2.cloned.1.call-done = bf16[256,1024]{1,0:T(8,128)(2,1)} async-done(((bf16[256,1024]{1,0:T(8,128)(2,1)}), bf16[256,1024]{1,0:T(8,128)(2,1)}) %all-reduce.2.cloned.1.call-update) | async-done | bytes 524304 | tf_op jit(solution)/shard_map/psum | solution.py:316
  148.5 1.1 multiply_convert_fusion
  149.7 2.0 %collective-permute-start.1 = (bf16[256,1024]{1,0:T(8,128)(2,1)S(1)}, bf16[256,1024]{1,0:T(8,128)(2,1)S(1)}, u32[]{:S(2)}, u32[]{:S(2)}) collective-permute-start(bf16[256,1024]{1,0:T(8,128)(2,1)S(1)} %multiply_convert_fusion), channel_id=1, source_target_pairs={{0,1},{1,0},{2,3},{3,2},{4,5},{5,4},{6,7},{7,6},{8,9},{9,8},{10,11... | collective-permute-start | bytes 1572872 | tf_op jit(solution)/shard_map/ppermute | solution.py:309
  151.7 0.1 iota_add_fusion
  151.7 0.1 add.48.blocks
  151.8 0.7 iota_reduce_fusion
  152.5 0.6 collective-permute-done.1
  153.2 0.4 fusion
  153.6 0.2 slice_bitcast_fusion.1
  153.8 1.5 pad_maximum_fusion
  155.3 0.0 all-to-all-done.1.terms
  155.3 4.5 %place.1 = f32[2,40,32768]{2,1,0:T(8,128)} custom-call(s32[16]{0:T(128)S(1)} %copy-done.1, s32[16]{0:T(128)S(1)} %copy-done, s32[80]{0:T(128)S(1)} %add.48.blocks, s32[80]{0:T(128)S(1)} %get-tuple-element.7.owners, bf16[16,40,1024]{2,1,0:T(8,128)(2,1)S(1)} %all-to-all-done.1.terms, ...), custom_call_target="tpu_custom_call", output_to_operand_aliasing={{}: (5, {})} | custom-call | bytes 6291456 | tf_op jit(solution)/shard_map/place/pallas_call | solution.py:292
  (3 shorter events, 0.0 us)
Async XLA Ops:
  7.2 42.4 %copy-start.5 = (bf16[1024,1024]{1,0:T(8,128)(2,1)S(1)}, bf16[1024,1024]{1,0:T(8,128)(2,1)}, u32[]{:S(2)}) copy-start(bf16[1024,1024]{1,0:T(8,128)(2,1)} %constant.51.clone.right_table) | copy-start | bytes 6291460
  7.2 42.4 %copy-start.6 = (bf16[1024,1024]{1,0:T(8,128)(2,1)S(1)}, bf16[1024,1024]{1,0:T(8,128)(2,1)}, u32[]{:S(2)}) copy-start(bf16[1024,1024]{1,0:T(8,128)(2,1)} %constant.52.clone.left_table) | copy-start | bytes 6291460
  12.3 37.2 %copy-start.1 = (s32[16]{0:T(128)S(1)}, s32[16]{0:T(128)}, u32[]{:S(2)}) copy-start(s32[16]{0:T(128)} %dealing.5) | copy-start | bytes 196
  12.4 37.2 %copy-start.2 = (bf16[2,512,512]{2,1,0:T(8,128)(2,1)S(1)}, bf16[2,512,512]{2,1,0:T(8,128)(2,1)}, u32[]{:S(2)}) copy-start(bf16[2,512,512]{2,1,0:T(8,128)(2,1)} %probe.1) | copy-start | bytes 3145732
  12.4 37.2 %copy-start.3 = (bf16[1,512,512]{2,1,0:T(8,128)(2,1)S(1)}, bf16[1,512,512]{2,1,0:T(8,128)(2,1)}, u32[]{:S(2)}) copy-start(bf16[1,512,512]{2,1,0:T(8,128)(2,1)} %measured.1) | copy-start | bytes 1572868
  12.4 37.2 %copy-start.4 = (s32[16]{0:T(128)S(1)}, s32[16]{0:T(128)}, u32[]{:S(2)}) copy-start(s32[16]{0:T(128)} %rows.1) | copy-start | bytes 196
  58.3 5.7 %collective-permute-start = (bf16[256,1024]{1,0:T(8,128)(2,1)S(1)}, bf16[256,1024]{1,0:T(8,128)(2,1)S(1)}, u32[]{:S(2)}, u32[]{:S(2)}) collective-permute-start(bf16[256,1024]{1,0:T(8,128)(2,1)S(1)} %get-tuple-element.11), channel_id=1, source_target_pairs={{0,1},{1,0},{2,3},{3,2},{4,5},{5,4},{6,7},{7,6},{8,9},{9,8},{10,11... | collective-permute-start | bytes 1572872 | tf_op jit(solution)/shard_map/ppermute | solution.py:309
  58.6 6.4 %copy-start = (s32[16]{0:T(128)S(1)}, s32[16]{0:T(128)}, u32[]{:S(2)}) copy-start(s32[16]{0:T(128)} %cols.3) | copy-start | bytes 196
  58.6 96.8 %all-to-all-start.1 = ((bf16[16,40,1024]{2,1,0:T(8,128)(2,1)}), bf16[16,40,1024]{2,1,0:T(8,128)(2,1)S(1)}, u32[]{:S(2)}, u32[]{:S(2)}) async-start(bf16[16,40,1024]{2,1,0:T(8,128)(2,1)} %bitcast.1), calls=%async_computation.1 | async-start | bytes 2621440 | tf_op jit(solution)/shard_map/all_to_all | solution.py:339
  63.9 84.6 %all-reduce.2.cloned.1.call-start = ((), (), s32[]{:S(2)}) async-start(), calls=%async_computation.2 | async-start | bytes 1048576 | tf_op jit(solution)/shard_map/psum | solution.py:316
  149.7 3.5 %collective-permute-start.1 = (bf16[256,1024]{1,0:T(8,128)(2,1)S(1)}, bf16[256,1024]{1,0:T(8,128)(2,1)S(1)}, u32[]{:S(2)}, u32[]{:S(2)}) collective-permute-start(bf16[256,1024]{1,0:T(8,128)(2,1)S(1)} %multiply_convert_fusion), channel_id=1, source_target_pairs={{0,1},{1,0},{2,3},{3,2},{4,5},{5,4},{6,7},{7,6},{8,9},{9,8},{10,11... | collective-permute-start | bytes 1572872 | tf_op jit(solution)/shard_map/ppermute | solution.py:309
Sparse Core Ops, SparseCore 0:
  68.8 79.6 all-reduce.1

commit v6 on v1

--- a/solution.py
+++ b/solution.py
@@ -46,7 +46,12 @@
     return picked.reshape(count, width)
 
 
-def fetch_kernel(order, dealing, cols, tile, out, held, sems):
+def partner(k, paired):
+    return lax.bitwise_xor(lax.axis_index("row"), k) if paired else k
+
+
+def fetch_kernel(order, dealing, cols, tile, out, token, held, sems):
+    token[0] = dealing[0]
     slots, tile_rows = out.shape[0], out.shape[1]
     tile_cols = tile.shape[2]
     span = order + LANES
@@ -61,7 +66,7 @@
 
     lane = lax.broadcasted_iota(jnp.int32, (tile_rows, LANES), 1)
 
-    @pl.loop(0, slots)
+    @pl.loop(0, slots, unroll=4)
     def _(slot):
         copy(slot).wait()
         _, offset = window_start(cols[dealing[slot]], order, tile_cols)
@@ -83,24 +88,94 @@
 
     return pl.pallas_call(
         functools.partial(fetch_kernel, order),
-        out_shape=jax.ShapeDtypeStruct((slots, tile_rows, 2 * order), jnp.bfloat16),
+        out_shape=(
+            jax.ShapeDtypeStruct((slots, tile_rows, 2 * order), jnp.bfloat16),
+            jax.ShapeDtypeStruct((1,), jnp.int32),
+        ),
         in_specs=[SMEM, SMEM, ANY],
-        out_specs=VMEM,
+        out_specs=(VMEM, SMEM),
         scratch_shapes=[
             pltpu.VMEM((slots, 2, tile_rows, span), jnp.float32),
             pltpu.SemaphoreType.DMA((slots,)),
         ],
-        compiler_params=pltpu.CompilerParams(vmem_limit_bytes=24 * 2**20),
+        compiler_params=pltpu.CompilerParams(vmem_limit_bytes=56 * 2**20),
         cost_estimate=pl.CostEstimate(flops=0, bytes_accessed=6 * 2**20, transcendentals=0),
         name="fetch",
     )(dealing, cols, tile)
 
 
-def slot_kernel(
-    dealing, rows, cells, probe, measured, right, left,
-    terms, kept, sent, empty,
-    wide, patch, wave, half, resid, turned, padded, mine, zeros, sem,
-):
+def prepare_kernel(order, dealing, cols, token, empty, blocks, owners, table, zeros, sems):
+    del token
+    count = (order + LANES) // LANES
+    slots = dealing.shape[0]
+    tile_cols = empty.shape[2]
+    width = zeros.shape[2]
+    zeros[...] = jnp.zeros_like(zeros)
+    fills = []
+    for b in range(tile_cols // width):
+        fill = pltpu.make_async_copy(zeros, empty.at[:, :, b * width : (b + 1) * width], sems.at[b])
+        fill.start()
+        fills.append(fill)
+
+    @pl.loop(0, tile_cols // LANES)
+    def _(block):
+        table[block] = -1
+
+    @pl.loop(0, slots)
+    def _(slot):
+        base, _ = window_start(cols[dealing[slot]], order, tile_cols)
+        for b in range(count):
+            number = slot * count + b
+            block = base // LANES + b
+            blocks[number] = block
+            known = table[block]
+            owner = jnp.where(known < 0, number, known)
+            owners[number] = owner
+            table[block] = owner
+
+    for fill in fills:
+        fill.wait()
+
+
+def prepare(dealing, cols, token, tile_shape, order):
+    slots = dealing.shape[0]
+    numbers = slots * (order + LANES) // LANES
+    fill_cols = 2048
+    return pl.pallas_call(
+        functools.partial(prepare_kernel, order),
+        out_shape=(
+            jax.ShapeDtypeStruct(tile_shape, jnp.float32),
+            jax.ShapeDtypeStruct((numbers,), jnp.int32),
+            jax.ShapeDtypeStruct((numbers,), jnp.int32),
+        ),
+        in_specs=[SMEM, SMEM, SMEM],
+        out_specs=(ANY, SMEM, SMEM),
+        scratch_shapes=[
+            pltpu.SMEM((tile_shape[2] // LANES,), jnp.int32),
+            pltpu.VMEM(tile_shape[:2] + (fill_cols,), jnp.float32),
+            pltpu.SemaphoreType.DMA((tile_shape[2] // fill_cols,)),
+        ],
+        compiler_params=pltpu.CompilerParams(vmem_limit_bytes=8 * 2**20),
+        cost_estimate=pl.CostEstimate(flops=0, bytes_accessed=11 * 2**20, transcendentals=0),
+        name="prepare",
+    )(dealing, cols, token)
+
+
+def exchange(items, paired):
+    if paired:
+        devices = len(items)
+        return [items[0]] + [
+            lax.ppermute(items[k], "row", [(d, d ^ k) for d in range(devices)])
+            for k in range(1, devices)
+        ]
+    arrived = lax.all_to_all(jnp.stack(items), "row", split_axis=0, concat_axis=0, tiled=True)
+    return [arrived[k] for k in range(len(items))]
+
+
+def slot_kernel(own_rows, paired, dealing, rows, owners, cells, probe, measured, right_table, left_table, *rest):
+    del owners
+    *terms, kept, sent = rest[:-11]
+    wide, patch, wave, half, resid, turned, padded, mine, right, left, table_sem = rest[-11:]
     order = probe.shape[1]
     total_rows = cells.shape[0]
     reach = total_rows - order
@@ -109,19 +184,15 @@
     step = 64
     tile = 256
 
-    zeros[...] = jnp.zeros_like(zeros)
-    fills = []
-    for b in range(empty.shape[2] // zeros.shape[2]):
-        fill = pltpu.make_async_copy(
-            zeros, empty.at[:, :, b * zeros.shape[2] : (b + 1) * zeros.shape[2]], sem.at[b]
-        )
-        fill.start()
-        fills.append(fill)
-
+    right_copy = pltpu.make_async_copy(right_table, right, table_sem.at[0])
+    left_copy = pltpu.make_async_copy(left_table, left, table_sem.at[1])
+    right_copy.start()
+    left_copy.start()
     wide[0:total_rows, :] = cells[...].astype(jnp.float32)
     wide[total_rows:, :] = jnp.zeros((SUBLANES, 2 * order), jnp.float32)
     padded[0:reach, :] = jnp.zeros((reach, 2 * order), jnp.float32)
-    padded[reach + order :, :] = jnp.zeros((reach + SUBLANES, 2 * order), jnp.float32)
+    below = padded.shape[0] - reach - order
+    padded[reach + order :, :] = jnp.zeros((below, 2 * order), jnp.float32)
 
     @pl.loop(0, order // step)
     def _(i):
@@ -137,11 +208,13 @@
     def dot(a, b):
         return jnp.dot(a, b, preferred_element_type=jnp.float32)
 
+    right_copy.wait()
     for first in range(0, order, tile):
         here = slice(first, first + tile)
         there = slice(order + first, order + first + tile)
         half[:order, here] = dot(wave[...], right[:, here]).astype(half.dtype)
         half[order:, here] = dot(wave[...], right[:, there]).astype(half.dtype)
+    left_copy.wait()
     for first in range(0, order, tile):
         here = slice(first, first + tile)
         there = slice(order + first, order + first + tile)
@@ -175,36 +248,31 @@
             mine[line, here] = patch_real * real + patch_imag * imag
             mine[line, there] = patch_real * imag - patch_imag * real
 
-    @pl.loop(0, total_rows // step)
-    def _(i):
-        place = pl.ds(pl.multiple_of(i * step, step), step)
-        terms[place, :] = rows_from(padded, reach - first_row + i * step, step).astype(terms.dtype)
-
     count = kept.shape[0]
     side = lax.rem(me, 2)
     kept[...] = mine[pl.ds(pl.multiple_of(side * count, count), count), :]
     sent[...] = mine[pl.ds(pl.multiple_of((1 - side) * count, count), count), :].astype(sent.dtype)
-    for fill in fills:
-        fill.wait()
-
-
-def slot_terms(cells, probe, measured, dealing, rows, tile_rows, tile_cols):
+    for k, term in enumerate(terms):
+        start = reach - first_row + partner(k, paired) * own_rows
+        term[...] = rows_from(padded, start, term.shape[0]).astype(term.dtype)
+
+
+def slot_terms(cells, probe, measured, dealing, rows, owners, own_rows, tile_rows, paired):
     order = probe.shape[1]
     total_rows = cells.shape[0]
+    slots = total_rows // own_rows
     right, left = dft_tables(order)
     wide_cols = 2 * order
-    fill_cols = 2048
     bf16, f32 = jnp.bfloat16, jnp.float32
-    return pl.pallas_call(
-        slot_kernel,
-        out_shape=(
-            jax.ShapeDtypeStruct((total_rows, wide_cols), bf16),
+    *terms, kept, sent = pl.pallas_call(
+        functools.partial(slot_kernel, own_rows, paired),
+        out_shape=(jax.ShapeDtypeStruct((tile_rows, wide_cols), bf16),) * slots
+        + (
             jax.ShapeDtypeStruct((order // 2, wide_cols), f32),
             jax.ShapeDtypeStruct((order // 2, wide_cols), bf16),
-            jax.ShapeDtypeStruct((2, tile_rows, tile_cols), f32),
         ),
-        in_specs=[SMEM, SMEM, VMEM, VMEM, VMEM, VMEM, VMEM],
-        out_specs=(VMEM, VMEM, VMEM, ANY),
+        in_specs=[SMEM, SMEM, SMEM, VMEM, VMEM, VMEM, ANY, ANY],
+        out_specs=(VMEM,) * (slots + 2),
         scratch_shapes=[
             pltpu.VMEM((total_rows + SUBLANES, wide_cols), f32),
             pltpu.VMEM((order, wide_cols), bf16),
@@ -212,45 +280,39 @@
             pltpu.VMEM((wide_cols, order), bf16),
             pltpu.VMEM((order, wide_cols), bf16),
             pltpu.VMEM((wide_cols, order), bf16),
-            pltpu.VMEM((2 * total_rows - order + SUBLANES, wide_cols), f32),
+            pltpu.VMEM((2 * total_rows - order + tile_rows + SUBLANES, wide_cols), f32),
             pltpu.VMEM((order, wide_cols), f32),
-            pltpu.VMEM((2, tile_rows, fill_cols), f32),
-            pltpu.SemaphoreType.DMA((tile_cols // fill_cols,)),
+            pltpu.VMEM((wide_cols, wide_cols), bf16),
+            pltpu.VMEM((wide_cols, wide_cols), bf16),
+            pltpu.SemaphoreType.DMA((2,)),
         ],
         compiler_params=pltpu.CompilerParams(vmem_limit_bytes=40 * 2**20),
         cost_estimate=pl.CostEstimate(
-            flops=8 * 2 * order**3 * 2, bytes_accessed=20 * 2**20, transcendentals=order * order
+            flops=8 * 2 * order**3 * 2, bytes_accessed=8 * 2**20, transcendentals=order * order
         ),
         name="slot",
-    )(dealing, rows, cells, probe, measured, jnp.asarray(right), jnp.asarray(left))
-
-
-def block_places(dealing, cols, order, tile_cols):
-    base, _ = window_start(cols[dealing], order, tile_cols)
-    count = (order + LANES) // LANES
-    blocks = (base[:, None] // LANES + jnp.arange(count, dtype=jnp.int32)[None, :]).reshape(-1)
-    same = blocks[:, None] == blocks[None, :]
-    return blocks, jnp.argmax(same, axis=1).astype(jnp.int32)
-
-
-def place_kernel(order, dealing, cols, blocks, owners, terms, empty, out, totals, sems):
+    )(dealing, rows, owners, cells, probe, measured, jnp.asarray(right), jnp.asarray(left))
+    return terms, kept, sent
+
+
+def place_kernel(slots, order, paired, dealing, cols, blocks, owners, *rest):
+    terms, (empty, out, totals, sems) = rest[:slots], rest[slots:]
     del empty
-    slots, tile_rows = terms.shape[0], terms.shape[1]
-    tile_cols = out.shape[2]
+    tile_rows = terms[0].shape[0]
     count = (order + LANES) // LANES
     totals[...] = jnp.zeros_like(totals)
     lane = lax.broadcasted_iota(jnp.int32, (tile_rows, LANES), 1)
-
-    @pl.loop(0, slots)
-    def _(slot):
-        _, offset = window_start(cols[dealing[slot]], order, tile_cols)
+    nothing = jnp.zeros((tile_rows, LANES), jnp.float32)
+
+    for k, term in enumerate(terms):
+        slot = partner(k, paired)
+        _, offset = window_start(cols[dealing[slot]], order, out.shape[2])
         shift = lax.rem(offset, LANES)
         for part in range(2):
             turned = []
             for b in range(count - 1):
                 first = part * order + b * LANES
-                turned.append(pltpu.roll(terms[slot, :, first : first + LANES].astype(jnp.float32), shift, 1))
-            nothing = jnp.zeros_like(turned[0])
+                turned.append(pltpu.roll(term[:, first : first + LANES].astype(jnp.float32), shift, 1))
             for b in range(count):
                 before = turned[b - 1] if b else nothing
                 after = turned[b] if b < count - 1 else nothing
@@ -274,26 +336,23 @@
             copy(number).wait()
 
 
-def place_windows(terms, empty, dealing, cols, order):
-
-    slots, tile_rows = terms.shape[0], terms.shape[1]
-    tile_cols = empty.shape[2]
+def place_windows(terms, empty, blocks, owners, dealing, cols, order, paired):
+    slots, tile_rows = len(terms), terms[0].shape[0]
     count = (order + LANES) // LANES
-    blocks, owners = block_places(dealing, cols, order, tile_cols)
     return pl.pallas_call(
-        functools.partial(place_kernel, order),
+        functools.partial(place_kernel, slots, order, paired),
         out_shape=jax.ShapeDtypeStruct(empty.shape, empty.dtype),
-        in_specs=[SMEM, SMEM, SMEM, SMEM, VMEM, ANY],
+        in_specs=[SMEM, SMEM, SMEM, SMEM] + [VMEM] * slots + [ANY],
         out_specs=ANY,
         scratch_shapes=[
             pltpu.VMEM((slots * count, 2, tile_rows, LANES), jnp.float32),
             pltpu.SemaphoreType.DMA((slots * count,)),
         ],
-        input_output_aliases={5: 0},
+        input_output_aliases={4 + slots: 0},
         compiler_params=pltpu.CompilerParams(vmem_limit_bytes=24 * 2**20),
         cost_estimate=pl.CostEstimate(flops=0, bytes_accessed=6 * 2**20, transcendentals=0),
         name="place",
-    )(dealing, cols, blocks, owners, terms, empty)
+    )(dealing, cols, blocks, owners, *terms, empty)
 
 
 def strides(devices):
@@ -305,39 +364,33 @@
     return steps
 
 
-def turn(x, stride, radix, distance, devices):
-    pairs = []
-    for d in range(devices):
-        digit = d // stride % radix
-        pairs.append((d, d + ((digit + distance) % radix - digit) * stride))
-    return lax.ppermute(x, "row", pairs)
+def swap(x, distance, devices):
+    return lax.ppermute(x, "row", [(d, d ^ distance) for d in range(devices)])
 
 
 def sum_probe(kept, sent, devices, scale):
     me = lax.axis_index("row")
     steps = strides(devices)
-    total = kept + turn(sent, 1, 2, 1, devices).astype(jnp.float32)
+    total = kept + swap(sent, 1, devices).astype(jnp.float32)
     for stride, radix in steps[1:]:
         digit = me // stride % radix
         count = total.shape[0] // radix
         own = lax.dynamic_slice_in_dim(total, digit * count, count)
-        for distance in range(1, radix):
-            other = lax.rem(digit + distance, radix)
-            share = lax.dynamic_slice_in_dim(total, other * count, count).astype(jnp.bfloat16)
-            own = own + turn(share, stride, radix, distance, devices).astype(jnp.float32)
+        for k in range(1, radix):
+            share = lax.dynamic_slice_in_dim(total, lax.bitwise_xor(digit, k) * count, count)
+            own = own + swap(share.astype(jnp.bfloat16), k * stride, devices).astype(jnp.float32)
         total = own
     whole = (total * scale).astype(jnp.bfloat16)
     for stride, radix in reversed(steps):
         digit = me // stride % radix
-        shares = [whole] + [turn(whole, stride, radix, distance, devices) for distance in range(1, radix)]
-        order = [lax.rem(digit - k + radix, radix) for k in range(radix)]
-        rows = []
-        for k in range(radix):
+        shares = [whole] + [swap(whole, k * stride, devices) for k in range(1, radix)]
+        pieces = []
+        for j in range(radix):
             piece = shares[0]
-            for d in range(1, radix):
-                piece = jnp.where(order[k] == d, shares[d], piece)
-            rows.append(piece)
-        whole = jnp.concatenate(rows, axis=0)
+            for k in range(1, radix):
+                piece = jnp.where(lax.bitwise_xor(digit, k) == j, shares[k], piece)
+            pieces.append(piece)
+        whole = jnp.concatenate(pieces, axis=0)
     return whole
 
 
@@ -345,23 +398,23 @@
     order = probe.shape[1]
     devices = lax.axis_size("row")
     own_rows, tile_cols = object_field.shape[1], object_field.shape[2]
+    total_rows = devices * own_rows
     tile_rows = -(-own_rows // SUBLANES) * SUBLANES
     spare = tile_rows - own_rows
+    paired = devices <= 16 and devices & (devices - 1) == 0
     if spare:
         object_field = jnp.pad(object_field, ((0, 0), (0, spare), (0, 0)))
-    pieces = fetch_windows(object_field, dealing, col_offsets, order)
+    pieces, token = fetch_windows(object_field, dealing, col_offsets, order)
     strips = lax.all_to_all(pieces, "row", split_axis=0, concat_axis=0, tiled=True)
-    cells = strips[:, :own_rows].reshape(devices * own_rows, 2 * order)
-    terms, kept, sent, empty = slot_terms(
-        cells, probe, amplitude, dealing, row_offsets, tile_rows, tile_cols
+    cells = strips[:, :own_rows].reshape(total_rows, 2 * order)
+    empty, blocks, owners = prepare(dealing, col_offsets, token, object_field.shape, order)
+    terms, kept, sent = slot_terms(
+        cells, probe, amplitude, dealing, row_offsets, owners, own_rows, tile_rows, paired
     )
-    outgoing = terms.reshape(devices, own_rows, 2 * order)
-    if spare:
-        outgoing = jnp.pad(outgoing, ((0, 0), (0, spare), (0, 0)))
-    arrived = lax.all_to_all(outgoing, "row", split_axis=0, concat_axis=0, tiled=True)
+    terms = exchange(terms, paired)
     whole = sum_probe(kept, sent, devices, 1.0 / dealing.shape[0]).astype(jnp.float32)
     probe_grad = jnp.stack([whole[:, :order], whole[:, order:]])
-    object_grad = place_windows(arrived, empty, dealing, col_offsets, order)
+    object_grad = place_windows(terms, empty, blocks, owners, dealing, col_offsets, order, paired)
     if spare:
         object_grad = object_grad[:, :own_rows]
     return (object_grad, probe_grad)

time: 119 us -> 145 us (1.22)
  blocking collectives: 36.9 us -> 0 us
  waiting for transfers between devices: 35.3 us -> 67.1 us
  starting transfers between devices: 19.2 us -> 37.4 us
  local copies, waits for them, and re-layouts: 6.35 us -> 14 us
  Pallas kernels: 16.8 us -> 22.8 us
    all_to_all x1 -> x0, blocking collectives: 36.9 us -> none  [body(): lax.all_to_all(pieces, 'row', split_axis=0, concat_axis=0, tiled=True)]
    ppermute x10 -> x25, starting transfers between devices: 11.5 us -> 30.7 us  [the longest x15 19.9 us: exchange(): lax.ppermute(items[k], 'row', [(d, d ^ k) for d in range(devices)])]
    ppermute x10 -> x25, waiting for transfers between devices: 25.2 us -> 42.4 us  [the longest x10 22.7 us: swap(): return lax.ppermute(x, 'row', [(d, d ^ distance) for d in range(devices)])]
    all_to_all x1, waiting for transfers between devices: 10.1 us -> 24.7 us  [body(): lax.all_to_all(pieces, 'row', split_axis=0, concat_axis=0, tiled=True)]
    unnamed x20 -> x74, local copies, waits for them, and re-layouts: 5.32 us -> 13.7 us
    pallas_call x3 -> x4, Pallas kernels: 16.8 us -> 22.8 us  [the longest x1 8.27 us: slot_terms(): pl.pallas_call(functools.partial(slot_kernel, own_rows, paired), out_shap...]
  transfers between devices with their start and end apart: 11 -> 26, of which waited for: 7 -> 16; matrix products, arithmetic and copies ran while one was open for 3% -> 0% of each run, Pallas kernels for 0% -> 7%
where the time goes in v6:
time: 145 us
  waiting for transfers between devices  67.1 us (46%)
  starting transfers between devices  37.4 us (26%)
  Pallas kernels  22.8 us (16%)
  local copies, waits for them, and re-layouts  14 us (10%)
  other arithmetic  2.45 us (2%)
    all_to_all x1, waiting for transfers between devices, body(): lax.all_to_all(pieces, 'row', split_axis=0, concat_axis=0, tiled=True)  24.7 us
    ppermute x10, waiting for transfers between devices, swap(): return lax.ppermute(x, 'row', [(d, d ^ distance) for d in range(devices)])  22.7 us
    ppermute x15, starting transfers between devices, exchange(): lax.ppermute(items[k], 'row', [(d, d ^ k) for d in range(devices)])  19.9 us
    ppermute x15, waiting for transfers between devices, exchange(): lax.ppermute(items[k], 'row', [(d, d ^ k) for d in range(devices)])  19.7 us
    unnamed x74, local copies, waits for them, and re-layouts  13.7 us
    ppermute x10, starting transfers between devices, swap(): return lax.ppermute(x, 'row', [(d, d ^ distance) for d in range(devices)])  10.8 us
    pallas_call x1, Pallas kernels, slot_terms(): pl.pallas_call(functools.partial(slot_kernel, own_rows, paired), out_shap...  8.27 us
    all_to_all x1, starting transfers between devices, body(): lax.all_to_all(pieces, 'row', split_axis=0, concat_axis=0, tiled=True)  6.7 us
  transfers between devices with their start and end apart: 26, of which 16 were waited for; matrix products, arithmetic and copies ran while one was open for 0% of the time, Pallas kernels for 7%

profile of v6, /device:TPU:15, one launch (start us, length us, event | category | flops | bytes accessed | tf_op | source)
XLA Modules:
  0.0 144.8 jit_solution(1910941547136733559)
XLA Ops:
  0.6 4.6 %fetch.1 = (bf16[16,40,1024]{2,1,0:T(8,128)(2,1)}, s32[1]{0:T(128)}) custom-call(s32[16]{0:T(128)} %dealing.7, s32[16]{0:T(128)} %cols.5, f32[2,40,32768]{2,1,0:T(8,128)} %tile.1), custom_call_target="tpu_custom_call" | custom-call | bytes 6291456 | tf_op jit(solution)/shard_map/fetch/pallas_call | solution.py:89
  5.3 6.7 %all-to-all-start = ((bf16[16,40,1024]{2,1,0:T(8,128)(2,1)}), bf16[16,40,1024]{2,1,0:T(8,128)(2,1)S(1)}, u32[]{:S(2)}, u32[]{:S(2)}) async-start(bf16[16,40,1024]{2,1,0:T(8,128)(2,1)} %get-tuple-element.28), calls=%async_computation | async-start | bytes 2621440 | tf_op jit(solution)/shard_map/all_to_all | solution.py:408
  12.0 5.9 %prepare.1 = (f32[2,40,32768]{2,1,0:T(8,128)}, s32[80]{0:T(128)S(1)}, s32[80]{0:T(128)S(1)}) custom-call(s32[16]{0:T(128)S(1)} %copy-done, s32[16]{0:T(128)S(1)} %copy-done.1, s32[1]{0:T(128)} %get-tuple-element.25.token), custom_call_target="tpu_custom_call" | custom-call | bytes 11534336 | tf_op jit(solution)/shard_map/prepare/pallas_call | solution.py:144
  17.9 24.7 %all-to-all-done = bf16[16,40,1024]{2,1,0:T(8,128)(2,1)S(1)} async-done(((bf16[16,40,1024]{2,1,0:T(8,128)(2,1)}), bf16[16,40,1024]{2,1,0:T(8,128)(2,1)S(1)}, u32[]{:S(2)}, u32[]{:S(2)}) %all-to-all-start) | async-done | bytes 1310752 | tf_op jit(solution)/shard_map/all_to_all | solution.py:408
  42.6 1.0 copy-done.3
  43.6 1.6 %copy-done.35 = bf16[1024,1024]{1,0:T(8,128)(2,1)S(1)} copy-done((bf16[1024,1024]{1,0:T(8,128)(2,1)S(1)}, bf16[1024,1024]{1,0:T(8,128)(2,1)}, u32[]{:S(2)}) %copy-start.35) | copy-done | bytes 2097176
  45.2 1.6 %copy-done.36 = bf16[1024,1024]{1,0:T(8,128)(2,1)S(1)} copy-done((bf16[1024,1024]{1,0:T(8,128)(2,1)S(1)}, bf16[1024,1024]{1,0:T(8,128)(2,1)}, u32[]{:S(2)}) %copy-start.36) | copy-done | bytes 2097176
  46.8 8.3 %slot.1 = (bf16[40,1024]{1,0:T(8,128)(2,1)S(1)}, bf16[40,1024]{1,0:T(8,128)(2,1)S(1)}, bf16[40,1024]{1,0:T(8,128)(2,1)S(1)}, bf16[40,1024]{1,0:T(8,128)(2,1)S(1)...) custom-call(s32[16]{0:T(128)S(1)} %copy-done, ...), custom_call_target="tpu_custom_call" | custom-call | flops 4294967296 | bytes 8388608 | tf_op jit(solution)/shard_map/slot/pallas_call | solution.py:267
  55.1 0.6 copy-done.4
  55.7 0.6 copy-done.6
  56.3 0.6 copy-done.8
  57.0 0.6 copy-done.10
  57.6 0.6 copy-done.12
  58.2 0.6 copy-done.14
  58.9 0.6 copy-done.16
  59.5 0.6 copy-done.18
  60.1 0.6 copy-done.20
  60.7 0.6 copy-done.22
  61.4 0.6 copy-done.24
  62.0 0.6 copy-done.26
  62.6 0.6 copy-done.28
  63.3 0.6 copy-done.30
  63.9 0.6 copy-done.32
  64.7 1.9 %collective-permute-done.15 = bf16[256,1024]{1,0:T(8,128)(2,1)S(1)} collective-permute-done((bf16[256,1024]{1,0:T(8,128)(2,1)}, bf16[256,1024]{1,0:T(8,128)(2,1)S(1)}, u32[]{:S(2)}, u32[]{:S(2)}) %collective-permute-start.15) | collective-permute-done | bytes 524320 | tf_op jit(solution)/shard_map/ppermute | solution.py:368
  67.0 7.6 %collective-permute-done.16 = bf16[128,1024]{1,0:T(8,128)(2,1)S(1)} collective-permute-done((bf16[128,1024]{1,0:T(8,128)(2,1)S(1)}, bf16[128,1024]{1,0:T(8,128)(2,1)S(1)}, u32[]{:S(2)}, u32[]{:S(2)}) %collective-permute-start.16) | collective-permute-done | bytes 262176 | tf_op jit(solution)/shard_map/ppermute | solution.py:368
  74.9 0.4 collective-permute-start.19
  75.3 0.8 collective-permute-start.18
  76.1 1.5 %collective-permute-start.17 = (bf16[32,1024]{1,0:T(8,128)(2,1)S(1)}, bf16[32,1024]{1,0:T(8,128)(2,1)S(1)}, u32[]{:S(2)}, u32[]{:S(2)}) collective-permute-start(bf16[32,1024]{1,0:T(8,128)(2,1)S(1)} %get-tuple-element.54), channel_id=1, source_target_pairs={{0,4},{1,5},{2,6},{3,7},{4,0},{5,1},{6,2},{7,3},{8,12},{9,13},{10,... | collective-permute-start | bytes 196616 | tf_op jit(solution)/shard_map/ppermute | solution.py:368
  77.6 2.5 %collective-permute-done.19 = bf16[32,1024]{1,0:T(8,128)(2,1)S(1)} collective-permute-done((bf16[32,1024]{1,0:T(8,128)(2,1)S(1)}, bf16[32,1024]{1,0:T(8,128)(2,1)S(1)}, u32[]{:S(2)}, u32[]{:S(2)}) %collective-permute-start.19) | collective-permute-done | bytes 65568 | tf_op jit(solution)/shard_map/ppermute | solution.py:368
  80.2 1.1 collective-permute-done.17
  81.3 0.9 collective-permute-start.20
  82.2 3.4 %collective-permute-start.21 = (bf16[32,1024]{1,0:T(8,128)(2,1)S(1)}, bf16[32,1024]{1,0:T(8,128)(2,1)S(1)}, u32[]{:S(2)}, u32[]{:S(2)}) collective-permute-start(bf16[32,1024]{1,0:T(8,128)(2,1)S(1)} %multiply_convert_fusion), channel_id=1, source_target_pairs={{0,8},{1,9},{2,10},{3,11},{4,12},{5,13},{6,14},{7,15},{8,0},{9,1},... | collective-permute-start | bytes 196616 | tf_op jit(solution)/shard_map/ppermute | solution.py:368
  85.6 2.4 %collective-permute-done.21 = bf16[32,1024]{1,0:T(8,128)(2,1)S(1)} collective-permute-done((bf16[32,1024]{1,0:T(8,128)(2,1)S(1)}, bf16[32,1024]{1,0:T(8,128)(2,1)S(1)}, u32[]{:S(2)}, u32[]{:S(2)}) %collective-permute-start.21) | collective-permute-done | bytes 65568 | tf_op jit(solution)/shard_map/ppermute | solution.py:368
  88.1 1.7 %collective-permute-done.22 = bf16[32,1024]{1,0:T(8,128)(2,1)S(1)} collective-permute-done((bf16[32,1024]{1,0:T(8,128)(2,1)S(1)}, bf16[32,1024]{1,0:T(8,128)(2,1)S(1)}, u32[]{:S(2)}, u32[]{:S(2)}) %collective-permute-start.22) | collective-permute-done | bytes 65568 | tf_op jit(solution)/shard_map/ppermute | solution.py:368
  89.8 0.6 collective-permute-start.23
  90.4 5.4 %collective-permute-done.23 = bf16[128,1024]{1,0:T(8,128)(2,1)S(1)} collective-permute-done((bf16[128,1024]{1,0:T(8,128)(2,1)S(1)}, bf16[128,1024]{1,0:T(8,128)(2,1)S(1)}, u32[]{:S(2)}, u32[]{:S(2)}) %collective-permute-start.23) | collective-permute-done | bytes 262176 | tf_op jit(solution)/shard_map/ppermute | solution.py:368
  96.0 2.8 %collective-permute-start.24 = (bf16[256,1024]{1,0:T(8,128)(2,1)S(1)}, bf16[256,1024]{1,0:T(8,128)(2,1)S(1)}, u32[]{:S(2)}, u32[]{:S(2)}) collective-permute-start(bf16[256,1024]{1,0:T(8,128)(2,1)S(1)} %pad_maximum_fusion.1), channel_id=1, source_target_pairs={{0,1},{1,0},{2,3},{3,2},{4,5},{5,4},{6,7},{7,6},{8,9},{9,8},{10,11... | collective-permute-start | bytes 1572872 | tf_op jit(solution)/shard_map/ppermute | solution.py:368
  98.9 0.5 collective-permute-start.1
  99.5 1.5 %collective-permute-start.2 = (bf16[40,1024]{1,0:T(8,128)(2,1)S(1)}, bf16[40,1024]{1,0:T(8,128)(2,1)S(1)}, u32[]{:S(2)}, u32[]{:S(2)}) collective-permute-start(bf16[40,1024]{1,0:T(8,128)(2,1)S(1)} %copy-done.29), channel_id=1, source_target_pairs={{0,3},{1,2},{2,1},{3,0},{4,7},{5,6},{6,5},{7,4},{8,11},{9,10},{10,... | collective-permute-start | bytes 245768 | tf_op jit(solution)/shard_map/ppermute | solution.py:168
  101.0 0.6 collective-permute-start.3
  101.6 0.8 collective-permute-start.4
  102.4 1.5 %collective-permute-start.5 = (bf16[40,1024]{1,0:T(8,128)(2,1)S(1)}, bf16[40,1024]{1,0:T(8,128)(2,1)S(1)}, u32[]{:S(2)}, u32[]{:S(2)}) collective-permute-start(bf16[40,1024]{1,0:T(8,128)(2,1)S(1)} %copy-done.23), channel_id=1, source_target_pairs={{0,6},{1,7},{2,4},{3,5},{4,2},{5,3},{6,0},{7,1},{8,14},{9,15},{10,... | collective-permute-start | bytes 245768 | tf_op jit(solution)/shard_map/ppermute | solution.py:168
  103.9 1.2 collective-permute-done.2.rest_3_
  105.2 1.8 %collective-permute-start.6 = (bf16[40,1024]{1,0:T(8,128)(2,1)S(1)}, bf16[40,1024]{1,0:T(8,128)(2,1)S(1)}, u32[]{:S(2)}, u32[]{:S(2)}) collective-permute-start(bf16[40,1024]{1,0:T(8,128)(2,1)S(1)} %copy-done.21), channel_id=1, source_target_pairs={{0,7},{1,6},{2,5},{3,4},{4,3},{5,2},{6,1},{7,0},{8,15},{9,14},{10,... | collective-permute-start | bytes 245768 | tf_op jit(solution)/shard_map/ppermute | solution.py:168
  107.0 0.3 collective-permute-start.7
  107.3 2.3 %collective-permute-start.8 = (bf16[40,1024]{1,0:T(8,128)(2,1)S(1)}, bf16[40,1024]{1,0:T(8,128)(2,1)S(1)}, u32[]{:S(2)}, u32[]{:S(2)}) collective-permute-start(bf16[40,1024]{1,0:T(8,128)(2,1)S(1)} %copy-done.17), channel_id=1, source_target_pairs={{0,9},{1,8},{2,11},{3,10},{4,13},{5,12},{6,15},{7,14},{8,1},{9,0},... | collective-permute-start | bytes 245768 | tf_op jit(solution)/shard_map/ppermute | solution.py:168
  109.6 1.1 collective-permute-start.9
  110.7 3.3 %collective-permute-start.10 = (bf16[40,1024]{1,0:T(8,128)(2,1)S(1)}, bf16[40,1024]{1,0:T(8,128)(2,1)S(1)}, u32[]{:S(2)}, u32[]{:S(2)}) collective-permute-start(bf16[40,1024]{1,0:T(8,128)(2,1)S(1)} %copy-done.13), channel_id=1, source_target_pairs={{0,11},{1,10},{2,9},{3,8},{4,15},{5,14},{6,13},{7,12},{8,3},{9,2},... | collective-permute-start | bytes 245768 | tf_op jit(solution)/shard_map/ppermute | solution.py:168
  114.0 1.4 collective-permute-start.11
  115.4 4.0 %collective-permute-done.8.rest_9_ = bf16[40,1024]{1,0:T(8,128)(2,1)S(1)} collective-permute-done((bf16[40,1024]{1,0:T(8,128)(2,1)S(1)}, bf16[40,1024]{1,0:T(8,128)(2,1)S(1)}, u32[]{:S(2)}, u32[]{:S(2)}) %collective-permute-start.8) | collective-permute-done | bytes 81952 | tf_op jit(solution)/shard_map/ppermute | solution.py:168
  119.3 1.1 collective-permute-start.12
  120.4 0.6 collective-permute-done.9.rest_10_
  121.1 1.6 %collective-permute-start.13 = (bf16[40,1024]{1,0:T(8,128)(2,1)S(1)}, bf16[40,1024]{1,0:T(8,128)(2,1)S(1)}, u32[]{:S(2)}, u32[]{:S(2)}) collective-permute-start(bf16[40,1024]{1,0:T(8,128)(2,1)S(1)} %copy-done.7), channel_id=1, source_target_pairs={{0,14},{1,15},{2,12},{3,13},{4,10},{5,11},{6,8},{7,9},{8,6},{9,7},... | collective-permute-start | bytes 245768 | tf_op jit(solution)/shard_map/ppermute | solution.py:168
  122.7 1.0 collective-permute-done.10.rest_11_
  123.7 2.0 %collective-permute-start.14 = (bf16[40,1024]{1,0:T(8,128)(2,1)S(1)}, bf16[40,1024]{1,0:T(8,128)(2,1)S(1)}, u32[]{:S(2)}, u32[]{:S(2)}) collective-permute-start(bf16[40,1024]{1,0:T(8,128)(2,1)S(1)} %copy-done.5), channel_id=1, source_target_pairs={{0,15},{1,14},{2,13},{3,12},{4,11},{5,10},{6,9},{7,8},{8,7},{9,6},... | collective-permute-start | bytes 245768 | tf_op jit(solution)/shard_map/ppermute | solution.py:168
  125.7 5.7 %collective-permute-done.11.rest_12_ = bf16[40,1024]{1,0:T(8,128)(2,1)S(1)} collective-permute-done((bf16[40,1024]{1,0:T(8,128)(2,1)S(1)}, bf16[40,1024]{1,0:T(8,128)(2,1)S(1)}, u32[]{:S(2)}, u32[]{:S(2)}) %collective-permute-start.11) | collective-permute-done | bytes 81952 | tf_op jit(solution)/shard_map/ppermute | solution.py:168
  131.4 2.6 %collective-permute-done.12.rest_13_ = bf16[40,1024]{1,0:T(8,128)(2,1)S(1)} collective-permute-done((bf16[40,1024]{1,0:T(8,128)(2,1)S(1)}, bf16[40,1024]{1,0:T(8,128)(2,1)S(1)}, u32[]{:S(2)}, u32[]{:S(2)}) %collective-permute-start.12) | collective-permute-done | bytes 81952 | tf_op jit(solution)/shard_map/ppermute | solution.py:168
  134.0 3.2 %collective-permute-done.13.rest_14_ = bf16[40,1024]{1,0:T(8,128)(2,1)S(1)} collective-permute-done((bf16[40,1024]{1,0:T(8,128)(2,1)S(1)}, bf16[40,1024]{1,0:T(8,128)(2,1)S(1)}, u32[]{:S(2)}, u32[]{:S(2)}) %collective-permute-start.13) | collective-permute-done | bytes 81952 | tf_op jit(solution)/shard_map/ppermute | solution.py:168
  137.2 1.4 collective-permute-done.14.rest_15_
  138.6 4.0 %place.1 = f32[2,40,32768]{2,1,0:T(8,128)} custom-call(s32[16]{0:T(128)S(1)} %copy-done, s32[16]{0:T(128)S(1)} %copy-done.1, s32[80]{0:T(128)S(1)} %get-tuple-element.26.blocks, s32[80]{0:T(128)S(1)} %get-tuple-element.27.owners, bf16[40,1024]{1,0:T(8,128)(2,1)S(1)} %get-tuple-element.29.rest_0_, ...), custom_call_target="tpu_custom_call", output_to_operand_aliasing={{}: (20, {})} | custom-call | bytes 6291456 | tf_op jit(solution)/shard_map/place/pallas_call | solution.py:342
  142.6 0.2 broadcast_select_fusion.1
  142.9 0.2 maximum_convert_fusion
  143.1 0.2 slice_bitcast_fusion.1
  143.4 1.5 %pad_maximum_fusion = f32[2,512,512]{2,1,0:T(8,128)} fusion(f32[1,512,512]{2,1,0:T(8,128)S(1)} %get-tuple-element.49, f32[1,512,512]{2,1,0:T(8,128)S(1)} %get-tuple-element.48), kind=kLoop, calls=%fused_computation | loop fusion | flops 524288 | bytes 4194304 | tf_op jit(solution)/shard_map/stack | solution.py:416
  (79 shorter events, 1.1 us)
Async XLA Ops:
  5.2 6.7 %copy-start = (s32[16]{0:T(128)S(1)}, s32[16]{0:T(128)}, u32[]{:S(2)}) copy-start(s32[16]{0:T(128)} %dealing.7) | copy-start | bytes 196
  5.3 6.7 %copy-start.1 = (s32[16]{0:T(128)S(1)}, s32[16]{0:T(128)}, u32[]{:S(2)}) copy-start(s32[16]{0:T(128)} %cols.5) | copy-start | bytes 196
  5.3 37.3 %copy-start.2 = (bf16[2,512,512]{2,1,0:T(8,128)(2,1)S(1)}, bf16[2,512,512]{2,1,0:T(8,128)(2,1)}, u32[]{:S(2)}) copy-start(bf16[2,512,512]{2,1,0:T(8,128)(2,1)} %probe.1) | copy-start | bytes 3145732
  5.3 37.3 %copy-start.34 = (s32[16]{0:T(128)S(1)}, s32[16]{0:T(128)}, u32[]{:S(2)}) copy-start(s32[16]{0:T(128)} %rows.1) | copy-start | bytes 196
  5.3 37.3 %all-to-all-start = ((bf16[16,40,1024]{2,1,0:T(8,128)(2,1)}), bf16[16,40,1024]{2,1,0:T(8,128)(2,1)S(1)}, u32[]{:S(2)}, u32[]{:S(2)}) async-start(bf16[16,40,1024]{2,1,0:T(8,128)(2,1)} %get-tuple-element.28), calls=%async_computation | async-start | bytes 2621440 | tf_op jit(solution)/shard_map/all_to_all | solution.py:408
  42.6 1.0 copy-start.3
  43.6 1.6 %copy-start.35 = (bf16[1024,1024]{1,0:T(8,128)(2,1)S(1)}, bf16[1024,1024]{1,0:T(8,128)(2,1)}, u32[]{:S(2)}) copy-start(bf16[1024,1024]{1,0:T(8,128)(2,1)} %constant.81.clone.right_table) | copy-start | bytes 6291460
  45.2 1.6 %copy-start.36 = (bf16[1024,1024]{1,0:T(8,128)(2,1)S(1)}, bf16[1024,1024]{1,0:T(8,128)(2,1)}, u32[]{:S(2)}) copy-start(bf16[1024,1024]{1,0:T(8,128)(2,1)} %constant.82.clone.left_table) | copy-start | bytes 6291460
  55.1 0.6 copy-start.4
  55.7 0.6 copy-start.6
  56.3 0.6 copy-start.8
  57.0 0.6 copy-start.10
  57.6 0.6 copy-start.12
  58.2 0.6 copy-start.14
  58.9 0.6 copy-start.16
  59.5 0.6 copy-start.18
  60.1 0.6 copy-start.20
  60.7 0.6 copy-start.22
  61.4 0.6 copy-start.24
  62.0 0.6 copy-start.26
  62.6 0.6 copy-start.28
  63.3 0.6 copy-start.30
  63.9 0.6 copy-start.32
  64.5 2.1 %collective-permute-start.15 = (bf16[256,1024]{1,0:T(8,128)(2,1)}, bf16[256,1024]{1,0:T(8,128)(2,1)S(1)}, u32[]{:S(2)}, u32[]{:S(2)}) collective-permute-start(bf16[256,1024]{1,0:T(8,128)(2,1)} %get-tuple-element.47), channel_id=1, source_target_pairs={{0,1},{1,0},{2,3},{3,2},{4,5},{5,4},{6,7},{7,6},{8,9},{9,8},{10,11... | collective-permute-start | bytes 1572872 | tf_op jit(solution)/shard_map/ppermute | solution.py:368
  66.9 7.8 %collective-permute-start.16 = (bf16[128,1024]{1,0:T(8,128)(2,1)S(1)}, bf16[128,1024]{1,0:T(8,128)(2,1)S(1)}, u32[]{:S(2)}, u32[]{:S(2)}) collective-permute-start(bf16[128,1024]{1,0:T(8,128)(2,1)S(1)} %dynamic-slice_convert_fusion), channel_id=1, source_target_pairs={{0,2},{1,3},{2,0},{3,1},{4,6},{5,7},{6,4},{7,5},{8,10},{9,11},{10,... | collective-permute-start | bytes 786440 | tf_op jit(solution)/shard_map/ppermute | solution.py:368
  74.7 24.1 %copy-start.33 = (bf16[40,1024]{1,0:T(8,128)(2,1)S(1)}, bf16[40,1024]{1,0:T(8,128)(2,1)}, u32[]{:S(2)}) copy-start(bf16[40,1024]{1,0:T(8,128)(2,1)} %copy-done.32) | copy-start | bytes 245764
  74.7 24.2 %copy-start.31 = (bf16[40,1024]{1,0:T(8,128)(2,1)S(1)}, bf16[40,1024]{1,0:T(8,128)(2,1)}, u32[]{:S(2)}) copy-start(bf16[40,1024]{1,0:T(8,128)(2,1)} %copy-done.30) | copy-start | bytes 245764
  74.7 24.7 %copy-start.29 = (bf16[40,1024]{1,0:T(8,128)(2,1)S(1)}, bf16[40,1024]{1,0:T(8,128)(2,1)}, u32[]{:S(2)}) copy-start(bf16[40,1024]{1,0:T(8,128)(2,1)} %copy-done.28) | copy-start | bytes 245764
  74.7 26.3 %copy-start.27 = (bf16[40,1024]{1,0:T(8,128)(2,1)S(1)}, bf16[40,1024]{1,0:T(8,128)(2,1)}, u32[]{:S(2)}) copy-start(bf16[40,1024]{1,0:T(8,128)(2,1)} %copy-done.26) | copy-start | bytes 245764
  74.7 26.9 %copy-start.25 = (bf16[40,1024]{1,0:T(8,128)(2,1)S(1)}, bf16[40,1024]{1,0:T(8,128)(2,1)}, u32[]{:S(2)}) copy-start(bf16[40,1024]{1,0:T(8,128)(2,1)} %copy-done.24) | copy-start | bytes 245764
  74.8 27.7 %copy-start.23 = (bf16[40,1024]{1,0:T(8,128)(2,1)S(1)}, bf16[40,1024]{1,0:T(8,128)(2,1)}, u32[]{:S(2)}) copy-start(bf16[40,1024]{1,0:T(8,128)(2,1)} %copy-done.22) | copy-start | bytes 245764
  74.8 30.4 %copy-start.21 = (bf16[40,1024]{1,0:T(8,128)(2,1)S(1)}, bf16[40,1024]{1,0:T(8,128)(2,1)}, u32[]{:S(2)}) copy-start(bf16[40,1024]{1,0:T(8,128)(2,1)} %copy-done.20) | copy-start | bytes 245764
  74.8 32.2 %copy-start.19 = (bf16[40,1024]{1,0:T(8,128)(2,1)S(1)}, bf16[40,1024]{1,0:T(8,128)(2,1)}, u32[]{:S(2)}) copy-start(bf16[40,1024]{1,0:T(8,128)(2,1)} %copy-done.18) | copy-start | bytes 245764
  74.8 32.5 %copy-start.17 = (bf16[40,1024]{1,0:T(8,128)(2,1)S(1)}, bf16[40,1024]{1,0:T(8,128)(2,1)}, u32[]{:S(2)}) copy-start(bf16[40,1024]{1,0:T(8,128)(2,1)} %copy-done.16) | copy-start | bytes 245764
  74.8 34.8 %copy-start.15 = (bf16[40,1024]{1,0:T(8,128)(2,1)S(1)}, bf16[40,1024]{1,0:T(8,128)(2,1)}, u32[]{:S(2)}) copy-start(bf16[40,1024]{1,0:T(8,128)(2,1)} %copy-done.14) | copy-start | bytes 245764
  74.8 35.9 %copy-start.13 = (bf16[40,1024]{1,0:T(8,128)(2,1)S(1)}, bf16[40,1024]{1,0:T(8,128)(2,1)}, u32[]{:S(2)}) copy-start(bf16[40,1024]{1,0:T(8,128)(2,1)} %copy-done.12) | copy-start | bytes 245764
  74.8 39.2 %copy-start.11 = (bf16[40,1024]{1,0:T(8,128)(2,1)S(1)}, bf16[40,1024]{1,0:T(8,128)(2,1)}, u32[]{:S(2)}) copy-start(bf16[40,1024]{1,0:T(8,128)(2,1)} %copy-done.10) | copy-start | bytes 245764
  74.8 44.5 %copy-start.9 = (bf16[40,1024]{1,0:T(8,128)(2,1)S(1)}, bf16[40,1024]{1,0:T(8,128)(2,1)}, u32[]{:S(2)}) copy-start(bf16[40,1024]{1,0:T(8,128)(2,1)} %copy-done.8) | copy-start | bytes 245764
  74.8 46.2 %copy-start.7 = (bf16[40,1024]{1,0:T(8,128)(2,1)S(1)}, bf16[40,1024]{1,0:T(8,128)(2,1)}, u32[]{:S(2)}) copy-start(bf16[40,1024]{1,0:T(8,128)(2,1)} %copy-done.6) | copy-start | bytes 245764
  74.8 48.9 %copy-start.5 = (bf16[40,1024]{1,0:T(8,128)(2,1)S(1)}, bf16[40,1024]{1,0:T(8,128)(2,1)}, u32[]{:S(2)}) copy-start(bf16[40,1024]{1,0:T(8,128)(2,1)} %copy-done.4) | copy-start | bytes 245764
  74.9 5.3 %collective-permute-start.19 = (bf16[32,1024]{1,0:T(8,128)(2,1)S(1)}, bf16[32,1024]{1,0:T(8,128)(2,1)S(1)}, u32[]{:S(2)}, u32[]{:S(2)}) collective-permute-start(bf16[32,1024]{1,0:T(8,128)(2,1)S(1)} %get-tuple-element.55), channel_id=1, source_target_pairs={{0,12},{1,13},{2,14},{3,15},{4,8},{5,9},{6,10},{7,11},{8,4},{9,5},... | collective-permute-start | bytes 196616 | tf_op jit(solution)/shard_map/ppermute | solution.py:368
  75.3 4.8 %collective-permute-start.18 = (bf16[32,1024]{1,0:T(8,128)(2,1)S(1)}, bf16[32,1024]{1,0:T(8,128)(2,1)S(1)}, u32[]{:S(2)}, u32[]{:S(2)}) collective-permute-start(bf16[32,1024]{1,0:T(8,128)(2,1)S(1)} %get-tuple-element.56), channel_id=1, source_target_pairs={{0,8},{1,9},{2,10},{3,11},{4,12},{5,13},{6,14},{7,15},{8,0},{9,1},... | collective-permute-start | bytes 196616 | tf_op jit(solution)/shard_map/ppermute | solution.py:368
  76.1 5.1 %collective-permute-start.17 = (bf16[32,1024]{1,0:T(8,128)(2,1)S(1)}, bf16[32,1024]{1,0:T(8,128)(2,1)S(1)}, u32[]{:S(2)}, u32[]{:S(2)}) collective-permute-start(bf16[32,1024]{1,0:T(8,128)(2,1)S(1)} %get-tuple-element.54), channel_id=1, source_target_pairs={{0,4},{1,5},{2,6},{3,7},{4,0},{5,1},{6,2},{7,3},{8,12},{9,13},{10,... | collective-permute-start | bytes 196616 | tf_op jit(solution)/shard_map/ppermute | solution.py:368
  81.3 4.4 %collective-permute-start.20 = (bf16[32,1024]{1,0:T(8,128)(2,1)S(1)}, bf16[32,1024]{1,0:T(8,128)(2,1)S(1)}, u32[]{:S(2)}, u32[]{:S(2)}) collective-permute-start(bf16[32,1024]{1,0:T(8,128)(2,1)S(1)} %multiply_convert_fusion), channel_id=1, source_target_pairs={{0,12},{1,13},{2,14},{3,15},{4,8},{5,9},{6,10},{7,11},{8,4},{9,5},... | collective-permute-start | bytes 196616 | tf_op jit(solution)/shard_map/ppermute | solution.py:368
  82.2 5.9 %collective-permute-start.21 = (bf16[32,1024]{1,0:T(8,128)(2,1)S(1)}, bf16[32,1024]{1,0:T(8,128)(2,1)S(1)}, u32[]{:S(2)}, u32[]{:S(2)}) collective-permute-start(bf16[32,1024]{1,0:T(8,128)(2,1)S(1)} %multiply_convert_fusion), channel_id=1, source_target_pairs={{0,8},{1,9},{2,10},{3,11},{4,12},{5,13},{6,14},{7,15},{8,0},{9,1},... | collective-permute-start | bytes 196616 | tf_op jit(solution)/shard_map/ppermute | solution.py:368
  85.6 4.1 %collective-permute-start.22 = (bf16[32,1024]{1,0:T(8,128)(2,1)S(1)}, bf16[32,1024]{1,0:T(8,128)(2,1)S(1)}, u32[]{:S(2)}, u32[]{:S(2)}) collective-permute-start(bf16[32,1024]{1,0:T(8,128)(2,1)S(1)} %multiply_convert_fusion), channel_id=1, source_target_pairs={{0,4},{1,5},{2,6},{3,7},{4,0},{5,1},{6,2},{7,3},{8,12},{9,13},{10,... | collective-permute-start | bytes 196616 | tf_op jit(solution)/shard_map/ppermute | solution.py:368
  89.8 6.0 %collective-permute-start.23 = (bf16[128,1024]{1,0:T(8,128)(2,1)S(1)}, bf16[128,1024]{1,0:T(8,128)(2,1)S(1)}, u32[]{:S(2)}, u32[]{:S(2)}) collective-permute-start(bf16[128,1024]{1,0:T(8,128)(2,1)S(1)} %pad_maximum_fusion.2), channel_id=1, source_target_pairs={{0,2},{1,3},{2,0},{3,1},{4,6},{5,7},{6,4},{7,5},{8,10},{9,11},{10,... | collective-permute-start | bytes 786440 | tf_op jit(solution)/shard_map/ppermute | solution.py:368
  96.0 46.6 %collective-permute-start.24 = (bf16[256,1024]{1,0:T(8,128)(2,1)S(1)}, bf16[256,1024]{1,0:T(8,128)(2,1)S(1)}, u32[]{:S(2)}, u32[]{:S(2)}) collective-permute-start(bf16[256,1024]{1,0:T(8,128)(2,1)S(1)} %pad_maximum_fusion.1), channel_id=1, source_target_pairs={{0,1},{1,0},{2,3},{3,2},{4,5},{5,4},{6,7},{7,6},{8,9},{9,8},{10,11... | collective-permute-start | bytes 1572872 | tf_op jit(solution)/shard_map/ppermute | solution.py:368
  98.8 2.8 %collective-permute-start = (bf16[40,1024]{1,0:T(8,128)(2,1)S(1)}, bf16[40,1024]{1,0:T(8,128)(2,1)S(1)}, u32[]{:S(2)}, u32[]{:S(2)}) collective-permute-start(bf16[40,1024]{1,0:T(8,128)(2,1)S(1)} %copy-done.33), channel_id=1, source_target_pairs={{0,1},{1,0},{2,3},{3,2},{4,5},{5,4},{6,7},{7,6},{8,9},{9,8},{10,11... | collective-permute-start | bytes 245768 | tf_op jit(solution)/shard_map/ppermute | solution.py:168
  98.9 3.5 %collective-permute-start.1 = (bf16[40,1024]{1,0:T(8,128)(2,1)S(1)}, bf16[40,1024]{1,0:T(8,128)(2,1)S(1)}, u32[]{:S(2)}, u32[]{:S(2)}) collective-permute-start(bf16[40,1024]{1,0:T(8,128)(2,1)S(1)} %copy-done.31), channel_id=1, source_target_pairs={{0,2},{1,3},{2,0},{3,1},{4,6},{5,7},{6,4},{7,5},{8,10},{9,11},{10,... | collective-permute-start | bytes 245768 | tf_op jit(solution)/shard_map/ppermute | solution.py:168
  99.5 5.7 %collective-permute-start.2 = (bf16[40,1024]{1,0:T(8,128)(2,1)S(1)}, bf16[40,1024]{1,0:T(8,128)(2,1)S(1)}, u32[]{:S(2)}, u32[]{:S(2)}) collective-permute-start(bf16[40,1024]{1,0:T(8,128)(2,1)S(1)} %copy-done.29), channel_id=1, source_target_pairs={{0,3},{1,2},{2,1},{3,0},{4,7},{5,6},{6,5},{7,4},{8,11},{9,10},{10,... | collective-permute-start | bytes 245768 | tf_op jit(solution)/shard_map/ppermute | solution.py:168
  101.0 6.0 %collective-permute-start.3 = (bf16[40,1024]{1,0:T(8,128)(2,1)S(1)}, bf16[40,1024]{1,0:T(8,128)(2,1)S(1)}, u32[]{:S(2)}, u32[]{:S(2)}) collective-permute-start(bf16[40,1024]{1,0:T(8,128)(2,1)S(1)} %copy-done.27), channel_id=1, source_target_pairs={{0,4},{1,5},{2,6},{3,7},{4,0},{5,1},{6,2},{7,3},{8,12},{9,13},{10,... | collective-permute-start | bytes 245768 | tf_op jit(solution)/shard_map/ppermute | solution.py:168
  101.6 5.7 %collective-permute-start.4 = (bf16[40,1024]{1,0:T(8,128)(2,1)S(1)}, bf16[40,1024]{1,0:T(8,128)(2,1)S(1)}, u32[]{:S(2)}, u32[]{:S(2)}) collective-permute-start(bf16[40,1024]{1,0:T(8,128)(2,1)S(1)} %copy-done.25), channel_id=1, source_target_pairs={{0,5},{1,4},{2,7},{3,6},{4,1},{5,0},{6,3},{7,2},{8,13},{9,12},{10,... | collective-permute-start | bytes 245768 | tf_op jit(solution)/shard_map/ppermute | solution.py:168
  102.4 7.2 %collective-permute-start.5 = (bf16[40,1024]{1,0:T(8,128)(2,1)S(1)}, bf16[40,1024]{1,0:T(8,128)(2,1)S(1)}, u32[]{:S(2)}, u32[]{:S(2)}) collective-permute-start(bf16[40,1024]{1,0:T(8,128)(2,1)S(1)} %copy-done.23), channel_id=1, source_target_pairs={{0,6},{1,7},{2,4},{3,5},{4,2},{5,3},{6,0},{7,1},{8,14},{9,15},{10,... | collective-permute-start | bytes 245768 | tf_op jit(solution)/shard_map/ppermute | solution.py:168
  105.2 5.5 %collective-permute-start.6 = (bf16[40,1024]{1,0:T(8,128)(2,1)S(1)}, bf16[40,1024]{1,0:T(8,128)(2,1)S(1)}, u32[]{:S(2)}, u32[]{:S(2)}) collective-permute-start(bf16[40,1024]{1,0:T(8,128)(2,1)S(1)} %copy-done.21), channel_id=1, source_target_pairs={{0,7},{1,6},{2,5},{3,4},{4,3},{5,2},{6,1},{7,0},{8,15},{9,14},{10,... | collective-permute-start | bytes 245768 | tf_op jit(solution)/shard_map/ppermute | solution.py:168
  107.0 7.0 %collective-permute-start.7 = (bf16[40,1024]{1,0:T(8,128)(2,1)S(1)}, bf16[40,1024]{1,0:T(8,128)(2,1)S(1)}, u32[]{:S(2)}, u32[]{:S(2)}) collective-permute-start(bf16[40,1024]{1,0:T(8,128)(2,1)S(1)} %copy-done.19), channel_id=1, source_target_pairs={{0,8},{1,9},{2,10},{3,11},{4,12},{5,13},{6,14},{7,15},{8,0},{9,1},... | collective-permute-start | bytes 245768 | tf_op jit(solution)/shard_map/ppermute | solution.py:168
  107.3 12.0 %collective-permute-start.8 = (bf16[40,1024]{1,0:T(8,128)(2,1)S(1)}, bf16[40,1024]{1,0:T(8,128)(2,1)S(1)}, u32[]{:S(2)}, u32[]{:S(2)}) collective-permute-start(bf16[40,1024]{1,0:T(8,128)(2,1)S(1)} %copy-done.17), channel_id=1, source_target_pairs={{0,9},{1,8},{2,11},{3,10},{4,13},{5,12},{6,15},{7,14},{8,1},{9,0},... | collective-permute-start | bytes 245768 | tf_op jit(solution)/shard_map/ppermute | solution.py:168
  109.6 11.5 %collective-permute-start.9 = (bf16[40,1024]{1,0:T(8,128)(2,1)S(1)}, bf16[40,1024]{1,0:T(8,128)(2,1)S(1)}, u32[]{:S(2)}, u32[]{:S(2)}) collective-permute-start(bf16[40,1024]{1,0:T(8,128)(2,1)S(1)} %copy-done.15), channel_id=1, source_target_pairs={{0,10},{1,11},{2,8},{3,9},{4,14},{5,15},{6,12},{7,13},{8,2},{9,3},... | collective-permute-start | bytes 245768 | tf_op jit(solution)/shard_map/ppermute | solution.py:168
  110.7 13.0 %collective-permute-start.10 = (bf16[40,1024]{1,0:T(8,128)(2,1)S(1)}, bf16[40,1024]{1,0:T(8,128)(2,1)S(1)}, u32[]{:S(2)}, u32[]{:S(2)}) collective-permute-start(bf16[40,1024]{1,0:T(8,128)(2,1)S(1)} %copy-done.13), channel_id=1, source_target_pairs={{0,11},{1,10},{2,9},{3,8},{4,15},{5,14},{6,13},{7,12},{8,3},{9,2},... | collective-permute-start | bytes 245768 | tf_op jit(solution)/shard_map/ppermute | solution.py:168
  114.0 17.4 %collective-permute-start.11 = (bf16[40,1024]{1,0:T(8,128)(2,1)S(1)}, bf16[40,1024]{1,0:T(8,128)(2,1)S(1)}, u32[]{:S(2)}, u32[]{:S(2)}) collective-permute-start(bf16[40,1024]{1,0:T(8,128)(2,1)S(1)} %copy-done.11), channel_id=1, source_target_pairs={{0,12},{1,13},{2,14},{3,15},{4,8},{5,9},{6,10},{7,11},{8,4},{9,5},... | collective-permute-start | bytes 245768 | tf_op jit(solution)/shard_map/ppermute | solution.py:168
  119.3 14.7 %collective-permute-start.12 = (bf16[40,1024]{1,0:T(8,128)(2,1)S(1)}, bf16[40,1024]{1,0:T(8,128)(2,1)S(1)}, u32[]{:S(2)}, u32[]{:S(2)}) collective-permute-start(bf16[40,1024]{1,0:T(8,128)(2,1)S(1)} %copy-done.9), channel_id=1, source_target_pairs={{0,13},{1,12},{2,15},{3,14},{4,9},{5,8},{6,11},{7,10},{8,5},{9,4},... | collective-permute-start | bytes 245768 | tf_op jit(solution)/shard_map/ppermute | solution.py:168
  121.1 16.1 %collective-permute-start.13 = (bf16[40,1024]{1,0:T(8,128)(2,1)S(1)}, bf16[40,1024]{1,0:T(8,128)(2,1)S(1)}, u32[]{:S(2)}, u32[]{:S(2)}) collective-permute-start(bf16[40,1024]{1,0:T(8,128)(2,1)S(1)} %copy-done.7), channel_id=1, source_target_pairs={{0,14},{1,15},{2,12},{3,13},{4,10},{5,11},{6,8},{7,9},{8,6},{9,7},... | collective-permute-start | bytes 245768 | tf_op jit(solution)/shard_map/ppermute | solution.py:168
  123.7 14.9 %collective-permute-start.14 = (bf16[40,1024]{1,0:T(8,128)(2,1)S(1)}, bf16[40,1024]{1,0:T(8,128)(2,1)S(1)}, u32[]{:S(2)}, u32[]{:S(2)}) collective-permute-start(bf16[40,1024]{1,0:T(8,128)(2,1)S(1)} %copy-done.5), channel_id=1, source_target_pairs={{0,15},{1,14},{2,13},{3,12},{4,11},{5,10},{6,9},{7,8},{8,7},{9,6},... | collective-permute-start | bytes 245768 | tf_op jit(solution)/shard_map/ppermute | solution.py:168

commit v7 on v6

--- a/solution.py
+++ b/solution.py
@@ -44,10 +44,6 @@
     sub = lax.broadcasted_iota(jnp.int32, (1, SUBLANES, width), 1)
     picked = jnp.where(sub < SUBLANES - rest, turned[:-1], turned[1:])
     return picked.reshape(count, width)
-
-
-def partner(k, paired):
-    return lax.bitwise_xor(lax.axis_index("row"), k) if paired else k
 
 
 def fetch_kernel(order, dealing, cols, tile, out, token, held, sems):
@@ -161,24 +157,14 @@
     )(dealing, cols, token)
 
 
-def exchange(items, paired):
-    if paired:
-        devices = len(items)
-        return [items[0]] + [
-            lax.ppermute(items[k], "row", [(d, d ^ k) for d in range(devices)])
-            for k in range(1, devices)
-        ]
-    arrived = lax.all_to_all(jnp.stack(items), "row", split_axis=0, concat_axis=0, tiled=True)
-    return [arrived[k] for k in range(len(items))]
-
-
-def slot_kernel(own_rows, paired, dealing, rows, owners, cells, probe, measured, right_table, left_table, *rest):
+def slot_kernel(
+    dealing, rows, owners, cells, probe, measured, right_table, left_table,
+    term, kept, sent,
+    wide, patch, wave, half, resid, turned, mine, right, left, table_sem,
+):
     del owners
-    *terms, kept, sent = rest[:-11]
-    wide, patch, wave, half, resid, turned, padded, mine, right, left, table_sem = rest[-11:]
     order = probe.shape[1]
     total_rows = cells.shape[0]
-    reach = total_rows - order
     me = lax.axis_index("row")
     first_row = rows[dealing[me]]
     step = 64
@@ -190,10 +176,6 @@
     left_copy.start()
     wide[0:total_rows, :] = cells[...].astype(jnp.float32)
     wide[total_rows:, :] = jnp.zeros((SUBLANES, 2 * order), jnp.float32)
-    padded[0:reach, :] = jnp.zeros((reach, 2 * order), jnp.float32)
-    below = padded.shape[0] - reach - order
-    padded[reach + order :, :] = jnp.zeros((below, 2 * order), jnp.float32)
-
     @pl.loop(0, order // step)
     def _(i):
         place = pl.ds(pl.multiple_of(i * step, step), step)
@@ -240,9 +222,8 @@
             imag = dot(right[order + top : order + top + tile, :], turned[:, here])
             probe_real = probe[0, line, here].astype(jnp.float32)
             probe_imag = probe[1, line, here].astype(jnp.float32)
-            down = slice(reach + top, reach + top + tile)
-            padded[down, here] = probe_real * real + probe_imag * imag
-            padded[down, there] = probe_real * imag - probe_imag * real
+            term[line, here] = (probe_real * real + probe_imag * imag).astype(term.dtype)
+            term[line, there] = (probe_real * imag - probe_imag * real).astype(term.dtype)
             patch_real = patch[line, here].astype(jnp.float32)
             patch_imag = patch[line, there].astype(jnp.float32)
             mine[line, here] = patch_real * real + patch_imag * imag
@@ -252,27 +233,22 @@
     side = lax.rem(me, 2)
     kept[...] = mine[pl.ds(pl.multiple_of(side * count, count), count), :]
     sent[...] = mine[pl.ds(pl.multiple_of((1 - side) * count, count), count), :].astype(sent.dtype)
-    for k, term in enumerate(terms):
-        start = reach - first_row + partner(k, paired) * own_rows
-        term[...] = rows_from(padded, start, term.shape[0]).astype(term.dtype)
-
-
-def slot_terms(cells, probe, measured, dealing, rows, owners, own_rows, tile_rows, paired):
+
+def slot_terms(cells, probe, measured, dealing, rows, owners):
     order = probe.shape[1]
     total_rows = cells.shape[0]
-    slots = total_rows // own_rows
     right, left = dft_tables(order)
     wide_cols = 2 * order
     bf16, f32 = jnp.bfloat16, jnp.float32
-    *terms, kept, sent = pl.pallas_call(
-        functools.partial(slot_kernel, own_rows, paired),
-        out_shape=(jax.ShapeDtypeStruct((tile_rows, wide_cols), bf16),) * slots
-        + (
+    return pl.pallas_call(
+        slot_kernel,
+        out_shape=(
+            jax.ShapeDtypeStruct((order, wide_cols), bf16),
             jax.ShapeDtypeStruct((order // 2, wide_cols), f32),
             jax.ShapeDtypeStruct((order // 2, wide_cols), bf16),
         ),
         in_specs=[SMEM, SMEM, SMEM, VMEM, VMEM, VMEM, ANY, ANY],
-        out_specs=(VMEM,) * (slots + 2),
+        out_specs=(VMEM,) * 3,
         scratch_shapes=[
             pltpu.VMEM((total_rows + SUBLANES, wide_cols), f32),
             pltpu.VMEM((order, wide_cols), bf16),
@@ -280,39 +256,64 @@
             pltpu.VMEM((wide_cols, order), bf16),
             pltpu.VMEM((order, wide_cols), bf16),
             pltpu.VMEM((wide_cols, order), bf16),
-            pltpu.VMEM((2 * total_rows - order + tile_rows + SUBLANES, wide_cols), f32),
             pltpu.VMEM((order, wide_cols), f32),
             pltpu.VMEM((wide_cols, wide_cols), bf16),
             pltpu.VMEM((wide_cols, wide_cols), bf16),
             pltpu.SemaphoreType.DMA((2,)),
         ],
-        compiler_params=pltpu.CompilerParams(vmem_limit_bytes=40 * 2**20),
+        compiler_params=pltpu.CompilerParams(vmem_limit_bytes=54 * 2**20),
         cost_estimate=pl.CostEstimate(
             flops=8 * 2 * order**3 * 2, bytes_accessed=8 * 2**20, transcendentals=order * order
         ),
         name="slot",
     )(dealing, rows, owners, cells, probe, measured, jnp.asarray(right), jnp.asarray(left))
-    return terms, kept, sent
-
-
-def place_kernel(slots, order, paired, dealing, cols, blocks, owners, *rest):
-    terms, (empty, out, totals, sems) = rest[:slots], rest[slots:]
+
+
+def pack_kernel(reach, own_rows, dealing, rows, term, out, padded):
+    order = term.shape[0]
+    first_row = rows[dealing[lax.axis_index("row")]]
+    below = padded.shape[0] - reach - order
+    padded[0:reach, :] = jnp.zeros((reach, padded.shape[1]), jnp.float32)
+    padded[reach : reach + order, :] = term[...].astype(jnp.float32)
+    padded[reach + order :, :] = jnp.zeros((below, padded.shape[1]), jnp.float32)
+
+    @pl.loop(0, out.shape[0], unroll=2)
+    def _(k):
+        out[k] = rows_from(padded, reach - first_row + k * own_rows, out.shape[1]).astype(out.dtype)
+
+
+def pack_rows(term, dealing, rows, slots, own_rows, tile_rows):
+    order, width = term.shape
+    reach = slots * own_rows - order
+    return pl.pallas_call(
+        functools.partial(pack_kernel, reach, own_rows),
+        out_shape=jax.ShapeDtypeStruct((slots, tile_rows, width), jnp.bfloat16),
+        in_specs=[SMEM, SMEM, VMEM],
+        out_specs=VMEM,
+        scratch_shapes=[pltpu.VMEM((2 * reach + order + tile_rows + SUBLANES, width), jnp.float32)],
+        compiler_params=pltpu.CompilerParams(vmem_limit_bytes=16 * 2**20),
+        cost_estimate=pl.CostEstimate(flops=0, bytes_accessed=3 * 2**20, transcendentals=0),
+        name="pack",
+    )(dealing, rows, term)
+
+
+def place_kernel(order, dealing, cols, blocks, owners, terms, empty, out, totals, sems):
     del empty
-    tile_rows = terms[0].shape[0]
+    slots, tile_rows = terms.shape[0], terms.shape[1]
     count = (order + LANES) // LANES
     totals[...] = jnp.zeros_like(totals)
     lane = lax.broadcasted_iota(jnp.int32, (tile_rows, LANES), 1)
     nothing = jnp.zeros((tile_rows, LANES), jnp.float32)
 
-    for k, term in enumerate(terms):
-        slot = partner(k, paired)
+    @pl.loop(0, slots, unroll=4)
+    def _(slot):
         _, offset = window_start(cols[dealing[slot]], order, out.shape[2])
         shift = lax.rem(offset, LANES)
         for part in range(2):
             turned = []
             for b in range(count - 1):
                 first = part * order + b * LANES
-                turned.append(pltpu.roll(term[:, first : first + LANES].astype(jnp.float32), shift, 1))
+                turned.append(pltpu.roll(terms[slot, :, first : first + LANES].astype(jnp.float32), shift, 1))
             for b in range(count):
                 before = turned[b - 1] if b else nothing
                 after = turned[b] if b < count - 1 else nothing
@@ -336,23 +337,23 @@
             copy(number).wait()
 
 
-def place_windows(terms, empty, blocks, owners, dealing, cols, order, paired):
-    slots, tile_rows = len(terms), terms[0].shape[0]
+def place_windows(terms, empty, blocks, owners, dealing, cols, order):
+    slots, tile_rows = terms.shape[0], terms.shape[1]
     count = (order + LANES) // LANES
     return pl.pallas_call(
-        functools.partial(place_kernel, slots, order, paired),
+        functools.partial(place_kernel, order),
         out_shape=jax.ShapeDtypeStruct(empty.shape, empty.dtype),
-        in_specs=[SMEM, SMEM, SMEM, SMEM] + [VMEM] * slots + [ANY],
+        in_specs=[SMEM, SMEM, SMEM, SMEM, VMEM, ANY],
         out_specs=ANY,
         scratch_shapes=[
             pltpu.VMEM((slots * count, 2, tile_rows, LANES), jnp.float32),
             pltpu.SemaphoreType.DMA((slots * count,)),
         ],
-        input_output_aliases={4 + slots: 0},
+        input_output_aliases={5: 0},
         compiler_params=pltpu.CompilerParams(vmem_limit_bytes=24 * 2**20),
         cost_estimate=pl.CostEstimate(flops=0, bytes_accessed=6 * 2**20, transcendentals=0),
         name="place",
-    )(dealing, cols, blocks, owners, *terms, empty)
+    )(dealing, cols, blocks, owners, terms, empty)
 
 
 def strides(devices):
@@ -368,19 +369,26 @@
     return lax.ppermute(x, "row", [(d, d ^ distance) for d in range(devices)])
 
 
-def sum_probe(kept, sent, devices, scale):
+def sum_probe(kept, sent, devices):
+    me = lax.axis_index("row")
+    total = kept + swap(sent, 1, devices).astype(jnp.float32)
+    parts = [1 << k for k in range(1, devices.bit_length() - 1)]
+    orders = (parts[:1] + parts[:0:-1], parts[1:2] + parts[:1] + parts[2:])
+    sets = jnp.split(total, 2)
+    for step in range(len(parts)):
+        for number, order in enumerate(orders):
+            digit = me // order[step] % 2
+            count = sets[number].shape[0] // 2
+            own = lax.dynamic_slice_in_dim(sets[number], digit * count, count)
+            other = lax.dynamic_slice_in_dim(sets[number], (1 - digit) * count, count)
+            sets[number] = own + swap(other.astype(jnp.bfloat16), order[step], devices).astype(jnp.float32)
+    return jnp.concatenate(sets), orders
+
+
+def join(whole, orders, devices):
     me = lax.axis_index("row")
     steps = strides(devices)
-    total = kept + swap(sent, 1, devices).astype(jnp.float32)
-    for stride, radix in steps[1:]:
-        digit = me // stride % radix
-        count = total.shape[0] // radix
-        own = lax.dynamic_slice_in_dim(total, digit * count, count)
-        for k in range(1, radix):
-            share = lax.dynamic_slice_in_dim(total, lax.bitwise_xor(digit, k) * count, count)
-            own = own + swap(share.astype(jnp.bfloat16), k * stride, devices).astype(jnp.float32)
-        total = own
-    whole = (total * scale).astype(jnp.bfloat16)
+    count, width = whole.shape[0] // 2, whole.shape[1]
     for stride, radix in reversed(steps):
         digit = me // stride % radix
         shares = [whole] + [swap(whole, k * stride, devices) for k in range(1, radix)]
@@ -391,7 +399,16 @@
                 piece = jnp.where(lax.bitwise_xor(digit, k) == j, shares[k], piece)
             pieces.append(piece)
         whole = jnp.concatenate(pieces, axis=0)
-    return whole
+    axes = []
+    for stride, radix in steps:
+        axes += [2 * stride, stride] if radix == 4 else [stride]
+    whole = whole.reshape([2] * len(axes) + [2, count, width])
+    sets = []
+    for number, order in enumerate(orders):
+        one = lax.index_in_dim(whole, number, len(axes), keepdims=False)
+        one = one.transpose([0] + [axes.index(part) for part in order] + [len(axes), len(axes) + 1])
+        sets.append(one.reshape(2, -1, width))
+    return jnp.concatenate(sets, axis=1).reshape(-1, width)
 
 
 def body(object_field, probe, amplitude, row_offsets, col_offsets, dealing):
@@ -401,20 +418,21 @@
     total_rows = devices * own_rows
     tile_rows = -(-own_rows // SUBLANES) * SUBLANES
     spare = tile_rows - own_rows
-    paired = devices <= 16 and devices & (devices - 1) == 0
     if spare:
         object_field = jnp.pad(object_field, ((0, 0), (0, spare), (0, 0)))
     pieces, token = fetch_windows(object_field, dealing, col_offsets, order)
     strips = lax.all_to_all(pieces, "row", split_axis=0, concat_axis=0, tiled=True)
     cells = strips[:, :own_rows].reshape(total_rows, 2 * order)
     empty, blocks, owners = prepare(dealing, col_offsets, token, object_field.shape, order)
-    terms, kept, sent = slot_terms(
-        cells, probe, amplitude, dealing, row_offsets, owners, own_rows, tile_rows, paired
-    )
-    terms = exchange(terms, paired)
-    whole = sum_probe(kept, sent, devices, 1.0 / dealing.shape[0]).astype(jnp.float32)
+    term, kept, sent = slot_terms(cells, probe, amplitude, dealing, row_offsets, owners)
+    total, orders = sum_probe(kept, sent, devices)
+    terms = pack_rows(term, dealing, row_offsets, devices, own_rows, tile_rows)
+    terms, total = lax.optimization_barrier((terms, total))
+    arrived = lax.all_to_all(terms, "row", split_axis=0, concat_axis=0, tiled=True)
+    share = (total * (1.0 / dealing.shape[0])).astype(jnp.bfloat16)
+    whole = join(share, orders, devices).astype(jnp.float32)
     probe_grad = jnp.stack([whole[:, :order], whole[:, order:]])
-    object_grad = place_windows(terms, empty, blocks, owners, dealing, col_offsets, order, paired)
+    object_grad = place_windows(arrived, empty, blocks, owners, dealing, col_offsets, order)
     if spare:
         object_grad = object_grad[:, :own_rows]
     return (object_grad, probe_grad)

time: 145 us -> 126 us (0.87)
  local copies, waits for them, and re-layouts: 14 us -> 2.13 us
  starting transfers between devices: 37.4 us -> 26.4 us
  Pallas kernels: 22.8 us -> 27.1 us
  waiting for transfers between devices: 67.1 us -> 64.6 us
  other arithmetic: 2.45 us -> 3.99 us
    all_to_all x0 -> x1, waiting for transfers between devices: none -> 25.6 us  [body(): lax.all_to_all(terms, 'row', split_axis=0, concat_axis=0, tiled=True)]
    ppermute x15 -> x0, starting transfers between devices: 19.9 us -> none  [exchange(): lax.ppermute(items[k], 'row', [(d, d ^ k) for d in range(devices)])]
    ppermute x15 -> x0, waiting for transfers between devices: 19.7 us -> none  [exchange(): lax.ppermute(items[k], 'row', [(d, d ^ k) for d in range(devices)])]
    unnamed x74 -> x17, local copies, waits for them, and re-layouts: 13.7 us -> 1.63 us
    all_to_all x0 -> x1, starting transfers between devices: none -> 10.5 us  [body(): lax.all_to_all(terms, 'row', split_axis=0, concat_axis=0, tiled=True)]
    ppermute x10 -> x12, waiting for transfers between devices: 22.7 us -> 14.8 us  [swap(): return lax.ppermute(x, 'row', [(d, d ^ distance) for d in range(devices)])]
    pallas_call x2 -> x3, Pallas kernels: 12.3 us -> 16.7 us  [the longest x1 10.3 us: slot_terms(): pl.pallas_call(slot_kernel, out_shape=(jax.ShapeDtypeStruct((order, wide_...]
    ppermute x10 -> x12, starting transfers between devices: 10.8 us -> 9.39 us  [swap(): return lax.ppermute(x, 'row', [(d, d ^ distance) for d in range(devices)])]
  transfers between devices with their start and end apart: 26 -> 14, of which waited for: 16 -> 10; matrix products, arithmetic and copies ran while one was open for 0% -> 2% of each run, Pallas kernels for 7% -> 6%
where the time goes in v7:
time: 126 us; the launch traced here: 125 us
  waiting for transfers between devices  64.6 us (51%)
  Pallas kernels  27.1 us (22%)
  starting transfers between devices  26.4 us (21%)
  other arithmetic  3.99 us (3%)
  local copies, waits for them, and re-layouts  2.13 us (2%)
    all_to_all x1, waiting for transfers between devices, body(): lax.all_to_all(terms, 'row', split_axis=0, concat_axis=0, tiled=True)  25.6 us
    all_to_all x1, waiting for transfers between devices, body(): lax.all_to_all(pieces, 'row', split_axis=0, concat_axis=0, tiled=True)  24.2 us
    ppermute x12, waiting for transfers between devices, swap(): return lax.ppermute(x, 'row', [(d, d ^ distance) for d in range(devices)])  14.8 us
    all_to_all x1, starting transfers between devices, body(): lax.all_to_all(terms, 'row', split_axis=0, concat_axis=0, tiled=True)  10.5 us
    pallas_call x1, Pallas kernels, slot_terms(): pl.pallas_call(slot_kernel, out_shape=(jax.ShapeDtypeStruct((order, wide_...  10.3 us
    ppermute x12, starting transfers between devices, swap(): return lax.ppermute(x, 'row', [(d, d ^ distance) for d in range(devices)])  9.39 us
    all_to_all x1, starting transfers between devices, body(): lax.all_to_all(pieces, 'row', split_axis=0, concat_axis=0, tiled=True)  6.57 us
    pallas_call x1, Pallas kernels, prepare(): pl.pallas_call(functools.partial(prepare_kernel, order), out_shape=(jax.S...  5.81 us
  transfers between devices with their start and end apart: 14, of which 10 were waited for; matrix products, arithmetic and copies ran while one was open for 2% of the time, Pallas kernels for 6%

profile of v7, /device:TPU:15, one launch (start us, length us, event | category | flops | bytes accessed | tf_op | source)
XLA Modules:
  0.0 125.3 jit_solution(9180734492645701198)
XLA Ops:
  0.6 4.6 %fetch.1 = (bf16[16,40,1024]{2,1,0:T(8,128)(2,1)}, s32[1]{0:T(128)}) custom-call(s32[16]{0:T(128)} %dealing.9, s32[16]{0:T(128)} %cols.5, f32[2,40,32768]{2,1,0:T(8,128)} %tile.1), custom_call_target="tpu_custom_call" | custom-call | bytes 6291456 | tf_op jit(solution)/shard_map/fetch/pallas_call | solution.py:85
  5.2 0.0 copy-start.1
  5.3 0.0 copy-start.3
  5.3 6.6 %all-to-all-start = ((bf16[16,40,1024]{2,1,0:T(8,128)(2,1)}), bf16[16,40,1024]{2,1,0:T(8,128)(2,1)S(1)}, u32[]{:S(2)}, u32[]{:S(2)}) async-start(bf16[16,40,1024]{2,1,0:T(8,128)(2,1)} %get-tuple-element.15), calls=%async_computation | async-start | bytes 2621440 | tf_op jit(solution)/shard_map/all_to_all | solution.py:424
  11.8 0.0 copy-done.1
  11.8 0.0 copy-done.3
  11.9 5.8 %prepare.1 = (f32[2,40,32768]{2,1,0:T(8,128)}, s32[80]{0:T(128)S(1)}, s32[80]{0:T(128)S(1)}) custom-call(s32[16]{0:T(128)S(1)} %copy-done.1, s32[16]{0:T(128)S(1)} %copy-done.3, s32[1]{0:T(128)} %get-tuple-element.12.token), custom_call_target="tpu_custom_call" | custom-call | bytes 11534336 | tf_op jit(solution)/shard_map/prepare/pallas_call | solution.py:140
  17.7 0.0 copy-start.4
  17.7 0.5 copy-done.4
  18.2 24.2 %all-to-all-done = bf16[16,40,1024]{2,1,0:T(8,128)(2,1)S(1)} async-done(((bf16[16,40,1024]{2,1,0:T(8,128)(2,1)}), bf16[16,40,1024]{2,1,0:T(8,128)(2,1)S(1)}, u32[]{:S(2)}, u32[]{:S(2)}) %all-to-all-start) | async-done | bytes 1310752 | tf_op jit(solution)/shard_map/all_to_all | solution.py:424
  42.4 0.0 copy-start.7
  42.4 1.1 copy-done.7
  43.5 10.3 %slot.1 = (bf16[512,1024]{1,0:T(8,128)(2,1)}, f32[256,1024]{1,0:T(8,128)}, bf16[256,1024]{1,0:T(8,128)(2,1)}) custom-call(s32[16]{0:T(128)} %dealing.9, s32[16]{0:T(128)} %rows.3, s32[80]{0:T(128)} %copy-done.4, bf16[640,1024]{1,0:T(8,128)(2,1)} %bitcast.18, bf16[2,512,512]{2,1,0:T(8,128)(2,1)} %probe.1, bf16[1,512,512]{2,1,0:T(8,128)(2,1)} %measured.1, ...), custom_call_target="tpu_custom_call" | custom-call | flops 4294967296 | bytes 8388608 | tf_op jit(solution)/shard_map/slot/pallas_call | solution.py:243
  53.7 0.3 collective-permute-start
  54.0 1.9 %collective-permute-done = bf16[256,1024]{1,0:T(8,128)(2,1)S(1)} collective-permute-done((bf16[256,1024]{1,0:T(8,128)(2,1)}, bf16[256,1024]{1,0:T(8,128)(2,1)S(1)}, u32[]{:S(2)}, u32[]{:S(2)}) %collective-permute-start) | collective-permute-done | bytes 524320 | tf_op jit(solution)/shard_map/ppermute | solution.py:369
  55.9 0.0 copy-start
  55.9 0.0 copy-start.2
  55.9 0.0 copy-start.6
  55.9 1.5 %convert_add_fusion = f32[256,1024]{1,0:T(8,128)S(1)} fusion(f32[256,1024]{1,0:T(8,128)} %get-tuple-element.17, bf16[256,1024]{1,0:T(8,128)(2,1)S(1)} %collective-permute-done), kind=kLoop, calls=%fused_computation.6 | loop fusion | flops 524288 | bytes 2621440 | tf_op jit(solution)/shard_map/add | solution.py:374
  57.4 0.1 fusion.1
  57.5 0.1 collective-permute-start.4
  57.7 0.0 copy-done
  57.7 0.0 copy-done.2
  57.8 0.0 copy-done.6
  57.8 2.2 %pack.1 = bf16[16,40,1024]{2,1,0:T(8,128)(2,1)} custom-call(s32[16]{0:T(128)S(1)} %copy-done.2, s32[16]{0:T(128)S(1)} %copy-done.6, bf16[512,1024]{1,0:T(8,128)(2,1)S(1)} %copy-done), custom_call_target="tpu_custom_call" | custom-call | bytes 3145728 | tf_op jit(solution)/shard_map/pack/pallas_call | solution.py:288
  60.0 0.1 collective-permute-start.1
  60.1 2.4 %collective-permute-done.4 = bf16[64,1024]{1,0:T(8,128)(2,1)S(1)} collective-permute-done((bf16[64,1024]{1,0:T(8,128)(2,1)S(1)}, bf16[64,1024]{1,0:T(8,128)(2,1)S(1)}, u32[]{:S(2)}, u32[]{:S(2)}) %collective-permute-start.4) | collective-permute-done | bytes 131104 | tf_op jit(solution)/shard_map/ppermute | solution.py:369
  62.6 0.1 collective-permute-start.5
  62.6 2.3 %collective-permute-done.1 = bf16[64,1024]{1,0:T(8,128)(2,1)S(1)} collective-permute-done((bf16[64,1024]{1,0:T(8,128)(2,1)S(1)}, bf16[64,1024]{1,0:T(8,128)(2,1)S(1)}, u32[]{:S(2)}, u32[]{:S(2)}) %collective-permute-start.1) | collective-permute-done | bytes 131104 | tf_op jit(solution)/shard_map/ppermute | solution.py:369
  65.0 1.1 collective-permute-start.2
  66.1 0.0 collective-permute-done.5
  66.2 1.4 %collective-permute-start.6 = (bf16[16,1024]{1,0:T(8,128)(2,1)S(1)}, bf16[16,1024]{1,0:T(8,128)(2,1)S(1)}, u32[]{:S(2)}, u32[]{:S(2)}) collective-permute-start(bf16[16,1024]{1,0:T(8,128)(2,1)S(1)} %dynamic-slice_convert_fusion.4), channel_id=1, source_target_pairs={{0,8},{1,9},{2,10},{3,11},{4,12},{5,13},{6,14},{7,15},{8,0},{9,1},... | collective-permute-start | bytes 98312 | tf_op jit(solution)/shard_map/ppermute | solution.py:369
  67.5 1.6 %collective-permute-done.2 = bf16[32,1024]{1,0:T(8,128)(2,1)S(1)} collective-permute-done((bf16[32,1024]{1,0:T(8,128)(2,1)S(1)}, bf16[32,1024]{1,0:T(8,128)(2,1)S(1)}, u32[]{:S(2)}, u32[]{:S(2)}) %collective-permute-start.2) | collective-permute-done | bytes 65568 | tf_op jit(solution)/shard_map/ppermute | solution.py:369
  69.2 2.0 %collective-permute-start.3 = (bf16[16,1024]{1,0:T(8,128)(2,1)S(1)}, bf16[16,1024]{1,0:T(8,128)(2,1)S(1)}, u32[]{:S(2)}, u32[]{:S(2)}) collective-permute-start(bf16[16,1024]{1,0:T(8,128)(2,1)S(1)} %dynamic-slice_convert_fusion.5), channel_id=1, source_target_pairs={{0,4},{1,5},{2,6},{3,7},{4,0},{5,1},{6,2},{7,3},{8,12},{9,13},{10,... | collective-permute-start | bytes 98312 | tf_op jit(solution)/shard_map/ppermute | solution.py:369
  71.2 0.0 collective-permute-done.6
  71.3 1.6 %collective-permute-done.3 = bf16[16,1024]{1,0:T(8,128)(2,1)S(1)} collective-permute-done((bf16[16,1024]{1,0:T(8,128)(2,1)S(1)}, bf16[16,1024]{1,0:T(8,128)(2,1)S(1)}, u32[]{:S(2)}, u32[]{:S(2)}) %collective-permute-start.3) | collective-permute-done | bytes 32800 | tf_op jit(solution)/shard_map/ppermute | solution.py:369
  72.9 0.1 collective-permute-start.7
  73.0 3.3 %collective-permute-start.8 = (bf16[32,1024]{1,0:T(8,128)(2,1)S(1)}, bf16[32,1024]{1,0:T(8,128)(2,1)S(1)}, u32[]{:S(2)}, u32[]{:S(2)}) collective-permute-start(bf16[32,1024]{1,0:T(8,128)(2,1)S(1)} %multiply_convert_fusion), channel_id=1, source_target_pairs={{0,8},{1,9},{2,10},{3,11},{4,12},{5,13},{6,14},{7,15},{8,0},{9,1},... | collective-permute-start | bytes 196616 | tf_op jit(solution)/shard_map/ppermute | solution.py:369
  76.3 0.0 collective-permute-start.9
  76.3 0.0 collective-permute-done.7
  76.3 2.4 %collective-permute-done.8 = bf16[32,1024]{1,0:T(8,128)(2,1)S(1)} collective-permute-done((bf16[32,1024]{1,0:T(8,128)(2,1)S(1)}, bf16[32,1024]{1,0:T(8,128)(2,1)S(1)}, u32[]{:S(2)}, u32[]{:S(2)}) %collective-permute-start.8) | collective-permute-done | bytes 65568 | tf_op jit(solution)/shard_map/ppermute | solution.py:369
  78.8 1.0 collective-permute-done.9
  79.8 0.2 collective-permute-start.10
  80.0 10.5 %all-to-all-start.1 = ((bf16[16,40,1024]{2,1,0:T(8,128)(2,1)}), bf16[16,40,1024]{2,1,0:T(8,128)(2,1)S(1)}, u32[]{:S(2)}, u32[]{:S(2)}) async-start(bf16[16,40,1024]{2,1,0:T(8,128)(2,1)} %pack.1), calls=%async_computation.1 | async-start | bytes 2621440 | tf_op jit(solution)/shard_map/all_to_all | solution.py:431
  90.5 0.0 collective-permute-done.10
  90.5 0.1 broadcast_select_fusion.3
  90.7 0.7 collective-permute-start.11
  91.4 1.5 %collective-permute-done.11 = bf16[256,1024]{1,0:T(8,128)(2,1)S(1)} collective-permute-done((bf16[256,1024]{1,0:T(8,128)(2,1)S(1)}, bf16[256,1024]{1,0:T(8,128)(2,1)S(1)}, u32[]{:S(2)}, u32[]{:S(2)}) %collective-permute-start.11) | collective-permute-done | bytes 524320 | tf_op jit(solution)/shard_map/ppermute | solution.py:369
  92.9 0.2 broadcast_select_fusion.1
  93.2 0.1 pad_maximum_fusion.1
  93.2 0.1 fusion
  93.4 0.1 pad_maximum_fusion.2
  93.5 0.3 bitcast_convert_fusion
  93.8 0.2 slice_bitcast_fusion.1
  94.0 0.0 copy-start.5
  94.0 1.5 %pad_maximum_fusion = f32[2,512,512]{2,1,0:T(8,128)} fusion(f32[1,512,512]{2,1,0:T(8,128)S(1)} %get-tuple-element.23, f32[1,512,512]{2,1,0:T(8,128)S(1)} %get-tuple-element.22), kind=kLoop, calls=%fused_computation | loop fusion | flops 524288 | bytes 4194304 | tf_op jit(solution)/shard_map/stack | solution.py:434
  95.5 25.6 %all-to-all-done.1.terms = bf16[16,40,1024]{2,1,0:T(8,128)(2,1)S(1)} async-done(((bf16[16,40,1024]{2,1,0:T(8,128)(2,1)}), bf16[16,40,1024]{2,1,0:T(8,128)(2,1)S(1)}, u32[]{:S(2)}, u32[]{:S(2)}) %all-to-all-start.1) | async-done | bytes 1310752 | tf_op jit(solution)/shard_map/all_to_all | solution.py:431
  121.1 0.0 copy-done.5
  121.1 4.2 %place.1 = f32[2,40,32768]{2,1,0:T(8,128)} custom-call(s32[16]{0:T(128)S(1)} %copy-done.2, s32[16]{0:T(128)S(1)} %copy-done.3, s32[80]{0:T(128)S(1)} %get-tuple-element.13.blocks, s32[80]{0:T(128)S(1)} %copy-done.5, bf16[16,40,1024]{2,1,0:T(8,128)(2,1)S(1)} %all-to-all-done.1.terms, ...), custom_call_target="tpu_custom_call", output_to_operand_aliasing={{}: (5, {})} | custom-call | bytes 6291456 | tf_op jit(solution)/shard_map/place/pallas_call | solution.py:343
  (18 shorter events, 0.4 us)
Async XLA Ops:
  5.2 6.6 %copy-start.1 = (s32[16]{0:T(128)S(1)}, s32[16]{0:T(128)}, u32[]{:S(2)}) copy-start(s32[16]{0:T(128)} %dealing.9) | copy-start | bytes 196
  5.3 6.6 %copy-start.3 = (s32[16]{0:T(128)S(1)}, s32[16]{0:T(128)}, u32[]{:S(2)}) copy-start(s32[16]{0:T(128)} %cols.5) | copy-start | bytes 196
  5.3 37.1 %all-to-all-start = ((bf16[16,40,1024]{2,1,0:T(8,128)(2,1)}), bf16[16,40,1024]{2,1,0:T(8,128)(2,1)S(1)}, u32[]{:S(2)}, u32[]{:S(2)}) async-start(bf16[16,40,1024]{2,1,0:T(8,128)(2,1)} %get-tuple-element.15), calls=%async_computation | async-start | bytes 2621440 | tf_op jit(solution)/shard_map/all_to_all | solution.py:424
  17.7 0.5 copy-start.4
  42.4 1.1 copy-start.7
  53.7 2.2 %collective-permute-start = (bf16[256,1024]{1,0:T(8,128)(2,1)}, bf16[256,1024]{1,0:T(8,128)(2,1)S(1)}, u32[]{:S(2)}, u32[]{:S(2)}) collective-permute-start(bf16[256,1024]{1,0:T(8,128)(2,1)} %get-tuple-element.18), channel_id=1, source_target_pairs={{0,1},{1,0},{2,3},{3,2},{4,5},{5,4},{6,7},{7,6},{8,9},{9,8},{10,11... | collective-permute-start | bytes 1572872 | tf_op jit(solution)/shard_map/ppermute | solution.py:369
  55.9 1.8 %copy-start = (bf16[512,1024]{1,0:T(8,128)(2,1)S(1)}, bf16[512,1024]{1,0:T(8,128)(2,1)}, u32[]{:S(2)}) copy-start(bf16[512,1024]{1,0:T(8,128)(2,1)} %get-tuple-element.16.term) | copy-start | bytes 3145732
  55.9 1.8 %copy-start.2 = (s32[16]{0:T(128)S(1)}, s32[16]{0:T(128)}, u32[]{:S(2)}) copy-start(s32[16]{0:T(128)} %dealing.9) | copy-start | bytes 196
  55.9 1.8 %copy-start.6 = (s32[16]{0:T(128)S(1)}, s32[16]{0:T(128)}, u32[]{:S(2)}) copy-start(s32[16]{0:T(128)} %rows.3) | copy-start | bytes 196
  57.5 5.0 %collective-permute-start.4 = (bf16[64,1024]{1,0:T(8,128)(2,1)S(1)}, bf16[64,1024]{1,0:T(8,128)(2,1)S(1)}, u32[]{:S(2)}, u32[]{:S(2)}) collective-permute-start(bf16[64,1024]{1,0:T(8,128)(2,1)S(1)} %dynamic-slice_convert_fusion), channel_id=1, source_target_pairs={{0,4},{1,5},{2,6},{3,7},{4,0},{5,1},{6,2},{7,3},{8,12},{9,13},{10,... | collective-permute-start | bytes 393224 | tf_op jit(solution)/shard_map/ppermute | solution.py:369
  60.0 5.0 %collective-permute-start.1 = (bf16[64,1024]{1,0:T(8,128)(2,1)S(1)}, bf16[64,1024]{1,0:T(8,128)(2,1)S(1)}, u32[]{:S(2)}, u32[]{:S(2)}) collective-permute-start(bf16[64,1024]{1,0:T(8,128)(2,1)S(1)} %dynamic-slice_convert_fusion.1), channel_id=1, source_target_pairs={{0,2},{1,3},{2,0},{3,1},{4,6},{5,7},{6,4},{7,5},{8,10},{9,11},{10,... | collective-permute-start | bytes 393224 | tf_op jit(solution)/shard_map/ppermute | solution.py:369
  62.6 3.6 %collective-permute-start.5 = (bf16[32,1024]{1,0:T(8,128)(2,1)S(1)}, bf16[32,1024]{1,0:T(8,128)(2,1)S(1)}, u32[]{:S(2)}, u32[]{:S(2)}) collective-permute-start(bf16[32,1024]{1,0:T(8,128)(2,1)S(1)} %dynamic-slice_convert_fusion.2), channel_id=1, source_target_pairs={{0,2},{1,3},{2,0},{3,1},{4,6},{5,7},{6,4},{7,5},{8,10},{9,11},{10,... | collective-permute-start | bytes 196616 | tf_op jit(solution)/shard_map/ppermute | solution.py:369
  65.0 4.2 %collective-permute-start.2 = (bf16[32,1024]{1,0:T(8,128)(2,1)S(1)}, bf16[32,1024]{1,0:T(8,128)(2,1)S(1)}, u32[]{:S(2)}, u32[]{:S(2)}) collective-permute-start(bf16[32,1024]{1,0:T(8,128)(2,1)S(1)} %dynamic-slice_convert_fusion.3), channel_id=1, source_target_pairs={{0,8},{1,9},{2,10},{3,11},{4,12},{5,13},{6,14},{7,15},{8,0},{9,1},... | collective-permute-start | bytes 196616 | tf_op jit(solution)/shard_map/ppermute | solution.py:369
  66.2 5.1 %collective-permute-start.6 = (bf16[16,1024]{1,0:T(8,128)(2,1)S(1)}, bf16[16,1024]{1,0:T(8,128)(2,1)S(1)}, u32[]{:S(2)}, u32[]{:S(2)}) collective-permute-start(bf16[16,1024]{1,0:T(8,128)(2,1)S(1)} %dynamic-slice_convert_fusion.4), channel_id=1, source_target_pairs={{0,8},{1,9},{2,10},{3,11},{4,12},{5,13},{6,14},{7,15},{8,0},{9,1},... | collective-permute-start | bytes 98312 | tf_op jit(solution)/shard_map/ppermute | solution.py:369
  69.2 3.6 %collective-permute-start.3 = (bf16[16,1024]{1,0:T(8,128)(2,1)S(1)}, bf16[16,1024]{1,0:T(8,128)(2,1)S(1)}, u32[]{:S(2)}, u32[]{:S(2)}) collective-permute-start(bf16[16,1024]{1,0:T(8,128)(2,1)S(1)} %dynamic-slice_convert_fusion.5), channel_id=1, source_target_pairs={{0,4},{1,5},{2,6},{3,7},{4,0},{5,1},{6,2},{7,3},{8,12},{9,13},{10,... | collective-permute-start | bytes 98312 | tf_op jit(solution)/shard_map/ppermute | solution.py:369
  72.9 3.4 %collective-permute-start.7 = (bf16[32,1024]{1,0:T(8,128)(2,1)S(1)}, bf16[32,1024]{1,0:T(8,128)(2,1)S(1)}, u32[]{:S(2)}, u32[]{:S(2)}) collective-permute-start(bf16[32,1024]{1,0:T(8,128)(2,1)S(1)} %multiply_convert_fusion), channel_id=1, source_target_pairs={{0,12},{1,13},{2,14},{3,15},{4,8},{5,9},{6,10},{7,11},{8,4},{9,5},... | collective-permute-start | bytes 196616 | tf_op jit(solution)/shard_map/ppermute | solution.py:369
  73.0 5.8 %collective-permute-start.8 = (bf16[32,1024]{1,0:T(8,128)(2,1)S(1)}, bf16[32,1024]{1,0:T(8,128)(2,1)S(1)}, u32[]{:S(2)}, u32[]{:S(2)}) collective-permute-start(bf16[32,1024]{1,0:T(8,128)(2,1)S(1)} %multiply_convert_fusion), channel_id=1, source_target_pairs={{0,8},{1,9},{2,10},{3,11},{4,12},{5,13},{6,14},{7,15},{8,0},{9,1},... | collective-permute-start | bytes 196616 | tf_op jit(solution)/shard_map/ppermute | solution.py:369
  76.3 3.4 %collective-permute-start.9 = (bf16[32,1024]{1,0:T(8,128)(2,1)S(1)}, bf16[32,1024]{1,0:T(8,128)(2,1)S(1)}, u32[]{:S(2)}, u32[]{:S(2)}) collective-permute-start(bf16[32,1024]{1,0:T(8,128)(2,1)S(1)} %multiply_convert_fusion), channel_id=1, source_target_pairs={{0,4},{1,5},{2,6},{3,7},{4,0},{5,1},{6,2},{7,3},{8,12},{9,13},{10,... | collective-permute-start | bytes 196616 | tf_op jit(solution)/shard_map/ppermute | solution.py:369
  79.8 10.7 %collective-permute-start.10 = (bf16[128,1024]{1,0:T(8,128)(2,1)S(1)}, bf16[128,1024]{1,0:T(8,128)(2,1)S(1)}, u32[]{:S(2)}, u32[]{:S(2)}) collective-permute-start(bf16[128,1024]{1,0:T(8,128)(2,1)S(1)} %pad_maximum_fusion.4), channel_id=1, source_target_pairs={{0,2},{1,3},{2,0},{3,1},{4,6},{5,7},{6,4},{7,5},{8,10},{9,11},{10,... | collective-permute-start | bytes 786440 | tf_op jit(solution)/shard_map/ppermute | solution.py:369
  80.0 41.0 %all-to-all-start.1 = ((bf16[16,40,1024]{2,1,0:T(8,128)(2,1)}), bf16[16,40,1024]{2,1,0:T(8,128)(2,1)S(1)}, u32[]{:S(2)}, u32[]{:S(2)}) async-start(bf16[16,40,1024]{2,1,0:T(8,128)(2,1)} %pack.1), calls=%async_computation.1 | async-start | bytes 2621440 | tf_op jit(solution)/shard_map/all_to_all | solution.py:431
  90.7 2.2 %collective-permute-start.11 = (bf16[256,1024]{1,0:T(8,128)(2,1)S(1)}, bf16[256,1024]{1,0:T(8,128)(2,1)S(1)}, u32[]{:S(2)}, u32[]{:S(2)}) collective-permute-start(bf16[256,1024]{1,0:T(8,128)(2,1)S(1)} %pad_maximum_fusion.3), channel_id=1, source_target_pairs={{0,1},{1,0},{2,3},{3,2},{4,5},{5,4},{6,7},{7,6},{8,9},{9,8},{10,11... | collective-permute-start | bytes 1572872 | tf_op jit(solution)/shard_map/ppermute | solution.py:369
  94.0 27.1 %copy-start.5 = (s32[80]{0:T(128)S(1)}, s32[80]{0:T(128)}, u32[]{:S(2)}) copy-start(s32[80]{0:T(128)} %copy-done.4) | copy-start | bytes 964

commit v8 on v7

--- a/solution.py
+++ b/solution.py
@@ -100,8 +100,18 @@
     )(dealing, cols, tile)
 
 
-def prepare_kernel(order, dealing, cols, token, empty, blocks, owners, table, zeros, sems):
+def prepare_kernel(
+    order, dealing, cols, token, right_table, left_table,
+    empty, blocks, owners, right, left,
+    table, zeros, sems, table_sems,
+):
     del token
+    loads = [
+        pltpu.make_async_copy(right_table, right, table_sems.at[0]),
+        pltpu.make_async_copy(left_table, left, table_sems.at[1]),
+    ]
+    for load in loads:
+        load.start()
     count = (order + LANES) // LANES
     slots = dealing.shape[0]
     tile_cols = empty.shape[2]
@@ -129,40 +139,44 @@
             owners[number] = owner
             table[block] = owner
 
-    for fill in fills:
-        fill.wait()
+    for copy in loads + fills:
+        copy.wait()
 
 
 def prepare(dealing, cols, token, tile_shape, order):
     slots = dealing.shape[0]
     numbers = slots * (order + LANES) // LANES
     fill_cols = 2048
+    right, left = dft_tables(order)
+    table = jax.ShapeDtypeStruct(right.shape, jnp.bfloat16)
     return pl.pallas_call(
         functools.partial(prepare_kernel, order),
         out_shape=(
             jax.ShapeDtypeStruct(tile_shape, jnp.float32),
             jax.ShapeDtypeStruct((numbers,), jnp.int32),
             jax.ShapeDtypeStruct((numbers,), jnp.int32),
+            table,
+            table,
         ),
-        in_specs=[SMEM, SMEM, SMEM],
-        out_specs=(ANY, SMEM, SMEM),
+        in_specs=[SMEM, SMEM, SMEM, ANY, ANY],
+        out_specs=(ANY, SMEM, SMEM, VMEM, VMEM),
         scratch_shapes=[
             pltpu.SMEM((tile_shape[2] // LANES,), jnp.int32),
             pltpu.VMEM(tile_shape[:2] + (fill_cols,), jnp.float32),
             pltpu.SemaphoreType.DMA((tile_shape[2] // fill_cols,)),
+            pltpu.SemaphoreType.DMA((2,)),
         ],
-        compiler_params=pltpu.CompilerParams(vmem_limit_bytes=8 * 2**20),
+        compiler_params=pltpu.CompilerParams(vmem_limit_bytes=16 * 2**20),
         cost_estimate=pl.CostEstimate(flops=0, bytes_accessed=11 * 2**20, transcendentals=0),
         name="prepare",
-    )(dealing, cols, token)
+    )(dealing, cols, token, jnp.asarray(right), jnp.asarray(left))
 
 
 def slot_kernel(
-    dealing, rows, owners, cells, probe, measured, right_table, left_table,
+    dealing, rows, cells, probe, measured, right, left,
     term, kept, sent,
-    wide, patch, wave, half, resid, turned, mine, right, left, table_sem,
+    wide, patch, wave, half, resid, turned, mine,
 ):
-    del owners
     order = probe.shape[1]
     total_rows = cells.shape[0]
     me = lax.axis_index("row")
@@ -170,10 +184,6 @@
     step = 64
     tile = 256
 
-    right_copy = pltpu.make_async_copy(right_table, right, table_sem.at[0])
-    left_copy = pltpu.make_async_copy(left_table, left, table_sem.at[1])
-    right_copy.start()
-    left_copy.start()
     wide[0:total_rows, :] = cells[...].astype(jnp.float32)
     wide[total_rows:, :] = jnp.zeros((SUBLANES, 2 * order), jnp.float32)
     @pl.loop(0, order // step)
@@ -190,13 +200,11 @@
     def dot(a, b):
         return jnp.dot(a, b, preferred_element_type=jnp.float32)
 
-    right_copy.wait()
     for first in range(0, order, tile):
         here = slice(first, first + tile)
         there = slice(order + first, order + first + tile)
         half[:order, here] = dot(wave[...], right[:, here]).astype(half.dtype)
         half[order:, here] = dot(wave[...], right[:, there]).astype(half.dtype)
-    left_copy.wait()
     for first in range(0, order, tile):
         here = slice(first, first + tile)
         there = slice(order + first, order + first + tile)
@@ -234,10 +242,9 @@
     kept[...] = mine[pl.ds(pl.multiple_of(side * count, count), count), :]
     sent[...] = mine[pl.ds(pl.multiple_of((1 - side) * count, count), count), :].astype(sent.dtype)
 
-def slot_terms(cells, probe, measured, dealing, rows, owners):
+def slot_terms(cells, probe, measured, dealing, rows, right, left):
     order = probe.shape[1]
     total_rows = cells.shape[0]
-    right, left = dft_tables(order)
     wide_cols = 2 * order
     bf16, f32 = jnp.bfloat16, jnp.float32
     return pl.pallas_call(
@@ -247,7 +254,7 @@
             jax.ShapeDtypeStruct((order // 2, wide_cols), f32),
             jax.ShapeDtypeStruct((order // 2, wide_cols), bf16),
         ),
-        in_specs=[SMEM, SMEM, SMEM, VMEM, VMEM, VMEM, ANY, ANY],
+        in_specs=[SMEM, SMEM, VMEM, VMEM, VMEM, VMEM, VMEM],
         out_specs=(VMEM,) * 3,
         scratch_shapes=[
             pltpu.VMEM((total_rows + SUBLANES, wide_cols), f32),
@@ -257,16 +264,13 @@
             pltpu.VMEM((order, wide_cols), bf16),
             pltpu.VMEM((wide_cols, order), bf16),
             pltpu.VMEM((order, wide_cols), f32),
-            pltpu.VMEM((wide_cols, wide_cols), bf16),
-            pltpu.VMEM((wide_cols, wide_cols), bf16),
-            pltpu.SemaphoreType.DMA((2,)),
         ],
-        compiler_params=pltpu.CompilerParams(vmem_limit_bytes=54 * 2**20),
+        compiler_params=pltpu.CompilerParams(vmem_limit_bytes=40 * 2**20),
         cost_estimate=pl.CostEstimate(
             flops=8 * 2 * order**3 * 2, bytes_accessed=8 * 2**20, transcendentals=order * order
         ),
         name="slot",
-    )(dealing, rows, owners, cells, probe, measured, jnp.asarray(right), jnp.asarray(left))
+    )(dealing, rows, cells, probe, measured, right, left)
 
 
 def pack_kernel(reach, own_rows, dealing, rows, term, out, padded):
@@ -369,27 +373,60 @@
     return lax.ppermute(x, "row", [(d, d ^ distance) for d in range(devices)])
 
 
+def share_index(device, steps):
+    index = 0
+    for stride, radix in steps[1:]:
+        index = index * radix + device // stride % radix
+    return index
+
+
+def share_kernel(steps, kept, met, own, *shares):
+    me = lax.axis_index("row")
+    count = own.shape[0]
+
+    def rows(device):
+        place = pl.ds(pl.multiple_of(share_index(device, steps) * count, count), count)
+        return kept[place, :] + met[place, :].astype(jnp.float32)
+
+    own[...] = rows(me)
+    for k, share in enumerate(shares, 1):
+        share[...] = rows(lax.bitwise_xor(me, 2 * k)).astype(share.dtype)
+
+
 def sum_probe(kept, sent, devices):
     me = lax.axis_index("row")
-    total = kept + swap(sent, 1, devices).astype(jnp.float32)
-    parts = [1 << k for k in range(1, devices.bit_length() - 1)]
-    orders = (parts[:1] + parts[:0:-1], parts[1:2] + parts[:1] + parts[2:])
-    sets = jnp.split(total, 2)
-    for step in range(len(parts)):
-        for number, order in enumerate(orders):
-            digit = me // order[step] % 2
-            count = sets[number].shape[0] // 2
-            own = lax.dynamic_slice_in_dim(sets[number], digit * count, count)
-            other = lax.dynamic_slice_in_dim(sets[number], (1 - digit) * count, count)
-            sets[number] = own + swap(other.astype(jnp.bfloat16), order[step], devices).astype(jnp.float32)
-    return jnp.concatenate(sets), orders
-
-
-def join(whole, orders, devices):
+    steps = strides(devices)
+    met = swap(sent, 1, devices)
+    if devices <= 16:
+        chips = devices // 2
+        count, width = kept.shape[0] // chips, kept.shape[1]
+        total, *shares = pl.pallas_call(
+            functools.partial(share_kernel, steps),
+            out_shape=(jax.ShapeDtypeStruct((count, width), jnp.float32),)
+            + (jax.ShapeDtypeStruct((count, width), jnp.bfloat16),) * (chips - 1),
+            in_specs=[VMEM, VMEM],
+            out_specs=(VMEM,) * chips,
+            cost_estimate=pl.CostEstimate(flops=0, bytes_accessed=2 * 2**20, transcendentals=0),
+            name="share",
+        )(kept, met)
+        for k, share in enumerate(shares, 1):
+            total = total + swap(share, 2 * k, devices).astype(jnp.float32)
+        return total
+    total = kept + met.astype(jnp.float32)
+    for stride, radix in steps[1:]:
+        digit = me // stride % radix
+        count = total.shape[0] // radix
+        own = lax.dynamic_slice_in_dim(total, digit * count, count)
+        for k in range(1, radix):
+            share = lax.dynamic_slice_in_dim(total, lax.bitwise_xor(digit, k) * count, count)
+            own = own + swap(share.astype(jnp.bfloat16), k * stride, devices).astype(jnp.float32)
+        total = own
+    return total
+
+
+def join(whole, devices):
     me = lax.axis_index("row")
-    steps = strides(devices)
-    count, width = whole.shape[0] // 2, whole.shape[1]
-    for stride, radix in reversed(steps):
+    for stride, radix in reversed(strides(devices)):
         digit = me // stride % radix
         shares = [whole] + [swap(whole, k * stride, devices) for k in range(1, radix)]
         pieces = []
@@ -399,16 +436,7 @@
                 piece = jnp.where(lax.bitwise_xor(digit, k) == j, shares[k], piece)
             pieces.append(piece)
         whole = jnp.concatenate(pieces, axis=0)
-    axes = []
-    for stride, radix in steps:
-        axes += [2 * stride, stride] if radix == 4 else [stride]
-    whole = whole.reshape([2] * len(axes) + [2, count, width])
-    sets = []
-    for number, order in enumerate(orders):
-        one = lax.index_in_dim(whole, number, len(axes), keepdims=False)
-        one = one.transpose([0] + [axes.index(part) for part in order] + [len(axes), len(axes) + 1])
-        sets.append(one.reshape(2, -1, width))
-    return jnp.concatenate(sets, axis=1).reshape(-1, width)
+    return whole
 
 
 def body(object_field, probe, amplitude, row_offsets, col_offsets, dealing):
@@ -423,14 +451,13 @@
     pieces, token = fetch_windows(object_field, dealing, col_offsets, order)
     strips = lax.all_to_all(pieces, "row", split_axis=0, concat_axis=0, tiled=True)
     cells = strips[:, :own_rows].reshape(total_rows, 2 * order)
-    empty, blocks, owners = prepare(dealing, col_offsets, token, object_field.shape, order)
-    term, kept, sent = slot_terms(cells, probe, amplitude, dealing, row_offsets, owners)
-    total, orders = sum_probe(kept, sent, devices)
+    empty, blocks, owners, right, left = prepare(dealing, col_offsets, token, object_field.shape, order)
+    term, kept, sent = slot_terms(cells, probe, amplitude, dealing, row_offsets, right, left)
+    total = sum_probe(kept, sent, devices)
     terms = pack_rows(term, dealing, row_offsets, devices, own_rows, tile_rows)
-    terms, total = lax.optimization_barrier((terms, total))
     arrived = lax.all_to_all(terms, "row", split_axis=0, concat_axis=0, tiled=True)
     share = (total * (1.0 / dealing.shape[0])).astype(jnp.bfloat16)
-    whole = join(share, orders, devices).astype(jnp.float32)
+    whole = join(share, devices).astype(jnp.float32)
     probe_grad = jnp.stack([whole[:, :order], whole[:, order:]])
     object_grad = place_windows(arrived, empty, blocks, owners, dealing, col_offsets, order)
     if spare:

time: 126 us -> 125 us (level)
  waiting for transfers between devices: 64.6 us -> 54.8 us
  local copies, waits for them, and re-layouts: 2.13 us -> 11.7 us
    all_to_all x1, waiting for transfers between devices: 25.6 us -> 10.1 us  [body(): lax.all_to_all(terms, 'row', split_axis=0, concat_axis=0, tiled=True)]
    ppermute x12 -> x13, waiting for transfers between devices: 14.8 us -> 24.7 us  [swap(): return lax.ppermute(x, 'row', [(d, d ^ distance) for d in range(devices)])]
    unnamed x17 -> x26, local copies, waits for them, and re-layouts: 1.63 us -> 11.5 us
    all_to_all x1, waiting for transfers between devices: 24.2 us -> 20.1 us  [body(): lax.all_to_all(pieces, 'row', split_axis=0, concat_axis=0, tiled=True)]
    pallas_call x1, Pallas kernels: 10.3 us -> 6.72 us  [slot_terms(): pl.pallas_call(slot_kernel, out_shape=(jax.ShapeDtypeStruct((order, wide_...]
    ppermute x12 -> x13, starting transfers between devices: 9.39 us -> 12.3 us  [swap(): return lax.ppermute(x, 'row', [(d, d ^ distance) for d in range(devices)])]
    pallas_call x0 -> x1, Pallas kernels: none -> 2.3 us  [sum_probe(): pl.pallas_call(functools.partial(share_kernel, steps), out_shape=(jax.Sha...]
    all_to_all x1, starting transfers between devices: 10.5 us -> 8.34 us  [body(): lax.all_to_all(terms, 'row', split_axis=0, concat_axis=0, tiled=True)]
  transfers between devices with their start and end apart: 14 -> 15, of which waited for: 10 -> 10; matrix products, arithmetic and copies ran while one was open for 2% -> 2% of each run, Pallas kernels for 6% -> 7%
where the time goes in v8:
time: 125 us; the launch traced here: 124 us
  waiting for transfers between devices  54.8 us (44%)
  starting transfers between devices  27.3 us (22%)
  Pallas kernels  26.3 us (21%)
  local copies, waits for them, and re-layouts  11.7 us (9%)
  other arithmetic  3.15 us (3%)
    ppermute x13, waiting for transfers between devices, swap(): return lax.ppermute(x, 'row', [(d, d ^ distance) for d in range(devices)])  24.7 us
    all_to_all x1, waiting for transfers between devices, body(): lax.all_to_all(pieces, 'row', split_axis=0, concat_axis=0, tiled=True)  20.1 us
    ppermute x13, starting transfers between devices, swap(): return lax.ppermute(x, 'row', [(d, d ^ distance) for d in range(devices)])  12.3 us
    unnamed x26, local copies, waits for them, and re-layouts  11.5 us
    all_to_all x1, waiting for transfers between devices, body(): lax.all_to_all(terms, 'row', split_axis=0, concat_axis=0, tiled=True)  10.1 us
    all_to_all x1, starting transfers between devices, body(): lax.all_to_all(terms, 'row', split_axis=0, concat_axis=0, tiled=True)  8.34 us
    pallas_call x1, Pallas kernels, slot_terms(): pl.pallas_call(slot_kernel, out_shape=(jax.ShapeDtypeStruct((order, wide_...  6.72 us
    all_to_all x1, starting transfers between devices, body(): lax.all_to_all(pieces, 'row', split_axis=0, concat_axis=0, tiled=True)  6.7 us
  transfers between devices with their start and end apart: 15, of which 10 were waited for; matrix products, arithmetic and copies ran while one was open for 2% of the time, Pallas kernels for 7%

profile of v8, /device:TPU:15, one launch (start us, length us, event | category | flops | bytes accessed | tf_op | source)
XLA Modules:
  0.0 124.0 jit_solution(17320609168895230990)
XLA Ops:
  0.6 4.6 %fetch.1 = (bf16[16,40,1024]{2,1,0:T(8,128)(2,1)}, s32[1]{0:T(128)}) custom-call(s32[16]{0:T(128)} %dealing.9, s32[16]{0:T(128)} %cols.5, f32[2,40,32768]{2,1,0:T(8,128)} %tile.1), custom_call_target="tpu_custom_call" | custom-call | bytes 6291456 | tf_op jit(solution)/shard_map/fetch/pallas_call | solution.py:85
  5.2 0.0 copy-start
  5.3 0.0 copy-start.3
  5.3 0.0 copy-start.4
  5.3 6.7 %all-to-all-start = ((bf16[16,40,1024]{2,1,0:T(8,128)(2,1)}), bf16[16,40,1024]{2,1,0:T(8,128)(2,1)S(1)}, u32[]{:S(2)}, u32[]{:S(2)}) async-start(bf16[16,40,1024]{2,1,0:T(8,128)(2,1)} %get-tuple-element.23), calls=%async_computation | async-start | bytes 2621440 | tf_op jit(solution)/shard_map/all_to_all | solution.py:452
  12.0 0.0 copy-done
  12.0 0.0 copy-done.3
  12.0 0.0 copy-done.4
  12.0 0.0 copy-start.1
  12.0 1.6 %copy-done.1 = bf16[1024,1024]{1,0:T(8,128)(2,1)S(1)} copy-done((bf16[1024,1024]{1,0:T(8,128)(2,1)S(1)}, bf16[1024,1024]{1,0:T(8,128)(2,1)}, u32[]{:S(2)}) %copy-start.1) | copy-done | bytes 2097176
  13.6 0.0 copy-start.5
  13.6 6.2 %prepare.1 = (f32[2,40,32768]{2,1,0:T(8,128)}, s32[80]{0:T(128)S(1)}, s32[80]{0:T(128)S(1)}, bf16[1024,1024]{1,0:T(8,128)(2,1)S(1)}, bf16[1024,1024]{1,0:T(8,128)(2,1)S(1)}) custom-call(s32[16]{0:T(128)S(1)} %copy-done.3, s32[16]{0:T(128)S(1)} %copy-done.4, s32[1]{0:T(128)} %get-tuple-element.20.token, bf16[1024,1024]{1,0:T(8,128)(2,1)S(1)} %copy-done, ...), custom_call_target="tpu_custom_call" | custom-call | bytes 11534336 | tf_op jit(solution)/shard_map/prepare/pallas_call | solution.py:152
  19.8 0.0 copy-start.6
  19.8 1.3 %copy-done.6 = bf16[1024,1024]{1,0:T(8,128)(2,1)} copy-done((bf16[1024,1024]{1,0:T(8,128)(2,1)}, bf16[1024,1024]{1,0:T(8,128)(2,1)S(1)}, u32[]{:S(2)}) %copy-start.6) | copy-done | bytes 2097176
  21.1 0.0 copy-start.8
  21.1 1.4 %copy-done.8 = bf16[1024,1024]{1,0:T(8,128)(2,1)} copy-done((bf16[1024,1024]{1,0:T(8,128)(2,1)}, bf16[1024,1024]{1,0:T(8,128)(2,1)S(1)}, u32[]{:S(2)}) %copy-start.8) | copy-done | bytes 2097176
  22.5 20.1 %all-to-all-done = bf16[16,40,1024]{2,1,0:T(8,128)(2,1)S(1)} async-done(((bf16[16,40,1024]{2,1,0:T(8,128)(2,1)}), bf16[16,40,1024]{2,1,0:T(8,128)(2,1)S(1)}, u32[]{:S(2)}, u32[]{:S(2)}) %all-to-all-start) | async-done | bytes 1310752 | tf_op jit(solution)/shard_map/all_to_all | solution.py:452
  42.5 0.0 copy-done.5
  42.5 0.0 copy-start.7
  42.5 1.6 %copy-done.7 = bf16[1024,1024]{1,0:T(8,128)(2,1)S(1)} copy-done((bf16[1024,1024]{1,0:T(8,128)(2,1)S(1)}, bf16[1024,1024]{1,0:T(8,128)(2,1)}, u32[]{:S(2)}) %copy-start.7) | copy-done | bytes 2097176
  44.1 1.6 %copy-done.9 = bf16[1024,1024]{1,0:T(8,128)(2,1)S(1)} copy-done((bf16[1024,1024]{1,0:T(8,128)(2,1)S(1)}, bf16[1024,1024]{1,0:T(8,128)(2,1)}, u32[]{:S(2)}) %copy-start.9) | copy-done | bytes 2097176
  45.7 1.2 copy-done.10
  47.0 1.0 copy-done.11
  48.0 6.7 %slot.1 = (bf16[512,1024]{1,0:T(8,128)(2,1)S(1)}, f32[256,1024]{1,0:T(8,128)S(1)}, bf16[256,1024]{1,0:T(8,128)(2,1)S(1)}) custom-call(s32[16]{0:T(128)S(1)} %copy-done.3, s32[16]{0:T(128)S(1)} %copy-done.5, bf16[640,1024]{1,0:T(8,128)(2,1)S(1)} %bitcast.5, bf16[2,512,512]{2,1,0:T(8,128)(2,1)S(1)} %copy-done.10, bf16[1,512,512]{2,1,0:T(8,128)(2,1)S(1)} %copy-done.11, ...), custom_call_target="tpu_custom_call" | custom-call | flops 4294967296 | bytes 8388608 | tf_op jit(solution)/shard_map/slot/pallas_call | solution.py:250
  54.7 0.0 copy-start.2
  54.7 1.0 copy-done.2
  55.7 0.2 collective-permute-start
  55.9 1.7 %collective-permute-done.met = bf16[256,1024]{1,0:T(8,128)(2,1)S(1)} collective-permute-done((bf16[256,1024]{1,0:T(8,128)(2,1)S(1)}, bf16[256,1024]{1,0:T(8,128)(2,1)S(1)}, u32[]{:S(2)}, u32[]{:S(2)}) %collective-permute-start) | collective-permute-done | bytes 524320 | tf_op jit(solution)/shard_map/ppermute | solution.py:373
  57.6 0.8 copy-done.12
  58.4 2.3 %share.1 = (f32[32,1024]{1,0:T(8,128)}, bf16[32,1024]{1,0:T(8,128)(2,1)}, bf16[32,1024]{1,0:T(8,128)(2,1)}, bf16[32,1024]{1,0:T(8,128)(2,1)}, bf16[32,1024]{1,0:...) custom-call(f32[256,1024]{1,0:T(8,128)} %copy-done.2, ...), custom_call_target="tpu_custom_call" | custom-call | bytes 2097152 | tf_op jit(solution)/shard_map/share/pallas_call | solution.py:403
  60.7 1.4 %collective-permute-start.7 = (bf16[32,1024]{1,0:T(8,128)(2,1)}, bf16[32,1024]{1,0:T(8,128)(2,1)S(1)}, u32[]{:S(2)}, u32[]{:S(2)}) collective-permute-start(bf16[32,1024]{1,0:T(8,128)(2,1)} %get-tuple-element.37), channel_id=1, source_target_pairs={{0,14},{1,15},{2,12},{3,13},{4,10},{5,11},{6,8},{7,9},{8,6},{9,7},... | collective-permute-start | bytes 196616 | tf_op jit(solution)/shard_map/ppermute | solution.py:373
  62.1 0.0 collective-permute-start.6
  62.1 3.8 %collective-permute-start.5 = (bf16[32,1024]{1,0:T(8,128)(2,1)}, bf16[32,1024]{1,0:T(8,128)(2,1)S(1)}, u32[]{:S(2)}, u32[]{:S(2)}) collective-permute-start(bf16[32,1024]{1,0:T(8,128)(2,1)} %get-tuple-element.35), channel_id=1, source_target_pairs={{0,10},{1,11},{2,8},{3,9},{4,14},{5,15},{6,12},{7,13},{8,2},{9,3},... | collective-permute-start | bytes 196616 | tf_op jit(solution)/shard_map/ppermute | solution.py:373
  65.9 0.0 collective-permute-start.4
  65.9 0.3 collective-permute-start.3
  66.3 2.2 %collective-permute-done.7 = bf16[32,1024]{1,0:T(8,128)(2,1)S(1)} collective-permute-done((bf16[32,1024]{1,0:T(8,128)(2,1)}, bf16[32,1024]{1,0:T(8,128)(2,1)S(1)}, u32[]{:S(2)}, u32[]{:S(2)}) %collective-permute-start.7) | collective-permute-done | bytes 65568 | tf_op jit(solution)/shard_map/ppermute | solution.py:373
  68.4 0.0 collective-permute-start.2
  68.4 2.4 %collective-permute-done.6 = bf16[32,1024]{1,0:T(8,128)(2,1)S(1)} collective-permute-done((bf16[32,1024]{1,0:T(8,128)(2,1)}, bf16[32,1024]{1,0:T(8,128)(2,1)S(1)}, u32[]{:S(2)}, u32[]{:S(2)}) %collective-permute-start.6) | collective-permute-done | bytes 65568 | tf_op jit(solution)/shard_map/ppermute | solution.py:373
  70.9 0.0 collective-permute-start.1
  70.9 1.2 collective-permute-done.5
  72.0 1.4 %collective-permute-done.4 = bf16[32,1024]{1,0:T(8,128)(2,1)S(1)} collective-permute-done((bf16[32,1024]{1,0:T(8,128)(2,1)}, bf16[32,1024]{1,0:T(8,128)(2,1)S(1)}, u32[]{:S(2)}, u32[]{:S(2)}) %collective-permute-start.4) | collective-permute-done | bytes 65568 | tf_op jit(solution)/shard_map/ppermute | solution.py:373
  73.4 0.0 collective-permute-done.3
  73.4 0.0 collective-permute-done.2
  73.4 0.8 collective-permute-done.1
  74.2 1.0 multiply_convert_fusion
  75.2 1.9 %collective-permute-start.8 = (bf16[32,1024]{1,0:T(8,128)(2,1)S(1)}, bf16[32,1024]{1,0:T(8,128)(2,1)S(1)}, u32[]{:S(2)}, u32[]{:S(2)}) collective-permute-start(bf16[32,1024]{1,0:T(8,128)(2,1)S(1)} %multiply_convert_fusion), channel_id=1, source_target_pairs={{0,12},{1,13},{2,14},{3,15},{4,8},{5,9},{6,10},{7,11},{8,4},{9,5},... | collective-permute-start | bytes 196616 | tf_op jit(solution)/shard_map/ppermute | solution.py:373
  77.0 1.7 %collective-permute-start.9 = (bf16[32,1024]{1,0:T(8,128)(2,1)S(1)}, bf16[32,1024]{1,0:T(8,128)(2,1)S(1)}, u32[]{:S(2)}, u32[]{:S(2)}) collective-permute-start(bf16[32,1024]{1,0:T(8,128)(2,1)S(1)} %multiply_convert_fusion), channel_id=1, source_target_pairs={{0,8},{1,9},{2,10},{3,11},{4,12},{5,13},{6,14},{7,15},{8,0},{9,1},... | collective-permute-start | bytes 196616 | tf_op jit(solution)/shard_map/ppermute | solution.py:373
  78.7 0.0 collective-permute-start.10
  78.7 2.2 %pack.1 = bf16[16,40,1024]{2,1,0:T(8,128)(2,1)} custom-call(s32[16]{0:T(128)S(1)} %copy-done.3, s32[16]{0:T(128)S(1)} %copy-done.5, bf16[512,1024]{1,0:T(8,128)(2,1)S(1)} %get-tuple-element.26.term), custom_call_target="tpu_custom_call" | custom-call | bytes 3145728 | tf_op jit(solution)/shard_map/pack/pallas_call | solution.py:292
  80.9 8.3 %all-to-all-start.1 = ((bf16[16,40,1024]{2,1,0:T(8,128)(2,1)}), bf16[16,40,1024]{2,1,0:T(8,128)(2,1)S(1)}, u32[]{:S(2)}, u32[]{:S(2)}) async-start(bf16[16,40,1024]{2,1,0:T(8,128)(2,1)} %pack.1), calls=%async_computation.1 | async-start | bytes 2621440 | tf_op jit(solution)/shard_map/all_to_all | solution.py:458
  89.2 0.0 collective-permute-done.8
  89.2 0.0 collective-permute-done.9
  89.2 0.0 collective-permute-done.10
  89.3 0.3 collective-permute-start.11
  89.7 13.5 %collective-permute-done.11 = bf16[128,1024]{1,0:T(8,128)(2,1)S(1)} collective-permute-done((bf16[128,1024]{1,0:T(8,128)(2,1)S(1)}, bf16[128,1024]{1,0:T(8,128)(2,1)S(1)}, u32[]{:S(2)}, u32[]{:S(2)}) %collective-permute-start.11) | collective-permute-done | bytes 262176 | tf_op jit(solution)/shard_map/ppermute | solution.py:373
  103.2 0.1 broadcast_select_fusion.3
  103.4 2.6 %collective-permute-start.12 = (bf16[256,1024]{1,0:T(8,128)(2,1)S(1)}, bf16[256,1024]{1,0:T(8,128)(2,1)S(1)}, u32[]{:S(2)}, u32[]{:S(2)}) collective-permute-start(bf16[256,1024]{1,0:T(8,128)(2,1)S(1)} %pad_maximum_fusion.1), channel_id=1, source_target_pairs={{0,1},{1,0},{2,3},{3,2},{4,5},{5,4},{6,7},{7,6},{8,9},{9,8},{10,11... | collective-permute-start | bytes 1572872 | tf_op jit(solution)/shard_map/ppermute | solution.py:373
  106.0 1.5 %collective-permute-done.12 = bf16[256,1024]{1,0:T(8,128)(2,1)S(1)} collective-permute-done((bf16[256,1024]{1,0:T(8,128)(2,1)S(1)}, bf16[256,1024]{1,0:T(8,128)(2,1)S(1)}, u32[]{:S(2)}, u32[]{:S(2)}) %collective-permute-start.12) | collective-permute-done | bytes 524320 | tf_op jit(solution)/shard_map/ppermute | solution.py:373
  107.5 0.2 broadcast_select_fusion.1
  107.8 0.2 maximum_convert_fusion
  108.0 0.2 slice_bitcast_fusion.1
  108.2 1.5 %pad_maximum_fusion = f32[2,512,512]{2,1,0:T(8,128)} fusion(f32[1,512,512]{2,1,0:T(8,128)S(1)} %get-tuple-element.39, f32[1,512,512]{2,1,0:T(8,128)S(1)} %get-tuple-element.38), kind=kLoop, calls=%fused_computation | loop fusion | flops 524288 | bytes 4194304 | tf_op jit(solution)/shard_map/stack | solution.py:461
  109.7 10.1 %all-to-all-done.1.terms = bf16[16,40,1024]{2,1,0:T(8,128)(2,1)S(1)} async-done(((bf16[16,40,1024]{2,1,0:T(8,128)(2,1)}), bf16[16,40,1024]{2,1,0:T(8,128)(2,1)S(1)}, u32[]{:S(2)}, u32[]{:S(2)}) %all-to-all-start.1) | async-done | bytes 1310752 | tf_op jit(solution)/shard_map/all_to_all | solution.py:458
  119.8 4.2 %place.1 = f32[2,40,32768]{2,1,0:T(8,128)} custom-call(s32[16]{0:T(128)S(1)} %copy-done.3, s32[16]{0:T(128)S(1)} %copy-done.4, s32[80]{0:T(128)S(1)} %get-tuple-element.21.blocks, s32[80]{0:T(128)S(1)} %get-tuple-element.22.owners, bf16[16,40,1024]{2,1,0:T(8,128)(2,1)S(1)} %all-to-all-done.1.terms, ...), custom_call_target="tpu_custom_call", output_to_operand_aliasing={{}: (5, {})} | custom-call | bytes 6291456 | tf_op jit(solution)/shard_map/place/pallas_call | solution.py:347
  (7 shorter events, 0.1 us)
Async XLA Ops:
  5.2 6.7 %copy-start = (bf16[1024,1024]{1,0:T(8,128)(2,1)S(1)}, bf16[1024,1024]{1,0:T(8,128)(2,1)}, u32[]{:S(2)}) copy-start(bf16[1024,1024]{1,0:T(8,128)(2,1)} %constant.67.clone.right_table) | copy-start | bytes 6291460
  5.3 6.7 %copy-start.3 = (s32[16]{0:T(128)S(1)}, s32[16]{0:T(128)}, u32[]{:S(2)}) copy-start(s32[16]{0:T(128)} %dealing.9) | copy-start | bytes 196
  5.3 6.7 %copy-start.4 = (s32[16]{0:T(128)S(1)}, s32[16]{0:T(128)}, u32[]{:S(2)}) copy-start(s32[16]{0:T(128)} %cols.5) | copy-start | bytes 196
  5.3 37.3 %all-to-all-start = ((bf16[16,40,1024]{2,1,0:T(8,128)(2,1)}), bf16[16,40,1024]{2,1,0:T(8,128)(2,1)S(1)}, u32[]{:S(2)}, u32[]{:S(2)}) async-start(bf16[16,40,1024]{2,1,0:T(8,128)(2,1)} %get-tuple-element.23), calls=%async_computation | async-start | bytes 2621440 | tf_op jit(solution)/shard_map/all_to_all | solution.py:452
  12.0 1.6 %copy-start.1 = (bf16[1024,1024]{1,0:T(8,128)(2,1)S(1)}, bf16[1024,1024]{1,0:T(8,128)(2,1)}, u32[]{:S(2)}) copy-start(bf16[1024,1024]{1,0:T(8,128)(2,1)} %constant.68.clone.left_table) | copy-start | bytes 6291460
  13.6 28.9 %copy-start.5 = (s32[16]{0:T(128)S(1)}, s32[16]{0:T(128)}, u32[]{:S(2)}) copy-start(s32[16]{0:T(128)} %rows.3) | copy-start | bytes 196
  19.8 1.3 %copy-start.6 = (bf16[1024,1024]{1,0:T(8,128)(2,1)}, bf16[1024,1024]{1,0:T(8,128)(2,1)S(1)}, u32[]{:S(2)}) copy-start(bf16[1024,1024]{1,0:T(8,128)(2,1)S(1)} %get-tuple-element.24.right) | copy-start | bytes 6291460
  21.1 1.4 %copy-start.8 = (bf16[1024,1024]{1,0:T(8,128)(2,1)}, bf16[1024,1024]{1,0:T(8,128)(2,1)S(1)}, u32[]{:S(2)}) copy-start(bf16[1024,1024]{1,0:T(8,128)(2,1)S(1)} %get-tuple-element.25.left) | copy-start | bytes 6291460
  42.5 1.6 %copy-start.7 = (bf16[1024,1024]{1,0:T(8,128)(2,1)S(1)}, bf16[1024,1024]{1,0:T(8,128)(2,1)}, u32[]{:S(2)}) copy-start(bf16[1024,1024]{1,0:T(8,128)(2,1)} %copy-done.6) | copy-start | bytes 6291460
  44.1 1.6 %copy-start.9 = (bf16[1024,1024]{1,0:T(8,128)(2,1)S(1)}, bf16[1024,1024]{1,0:T(8,128)(2,1)}, u32[]{:S(2)}) copy-start(bf16[1024,1024]{1,0:T(8,128)(2,1)} %copy-done.8) | copy-start | bytes 6291460
  45.7 1.2 copy-start.10
  47.0 1.0 copy-start.11
  54.7 1.0 copy-start.2
  55.7 1.9 %collective-permute-start = (bf16[256,1024]{1,0:T(8,128)(2,1)S(1)}, bf16[256,1024]{1,0:T(8,128)(2,1)S(1)}, u32[]{:S(2)}, u32[]{:S(2)}) collective-permute-start(bf16[256,1024]{1,0:T(8,128)(2,1)S(1)} %get-tuple-element.29), channel_id=1, source_target_pairs={{0,1},{1,0},{2,3},{3,2},{4,5},{5,4},{6,7},{7,6},{8,9},{9,8},{10,11... | collective-permute-start | bytes 1572872 | tf_op jit(solution)/shard_map/ppermute | solution.py:373
  57.6 0.8 copy-start.12
  60.7 7.7 %collective-permute-start.7 = (bf16[32,1024]{1,0:T(8,128)(2,1)}, bf16[32,1024]{1,0:T(8,128)(2,1)S(1)}, u32[]{:S(2)}, u32[]{:S(2)}) collective-permute-start(bf16[32,1024]{1,0:T(8,128)(2,1)} %get-tuple-element.37), channel_id=1, source_target_pairs={{0,14},{1,15},{2,12},{3,13},{4,10},{5,11},{6,8},{7,9},{8,6},{9,7},... | collective-permute-start | bytes 196616 | tf_op jit(solution)/shard_map/ppermute | solution.py:373
  62.1 8.8 %collective-permute-start.6 = (bf16[32,1024]{1,0:T(8,128)(2,1)}, bf16[32,1024]{1,0:T(8,128)(2,1)S(1)}, u32[]{:S(2)}, u32[]{:S(2)}) collective-permute-start(bf16[32,1024]{1,0:T(8,128)(2,1)} %get-tuple-element.36), channel_id=1, source_target_pairs={{0,12},{1,13},{2,14},{3,15},{4,8},{5,9},{6,10},{7,11},{8,4},{9,5},... | collective-permute-start | bytes 196616 | tf_op jit(solution)/shard_map/ppermute | solution.py:373
  62.1 9.9 %collective-permute-start.5 = (bf16[32,1024]{1,0:T(8,128)(2,1)}, bf16[32,1024]{1,0:T(8,128)(2,1)S(1)}, u32[]{:S(2)}, u32[]{:S(2)}) collective-permute-start(bf16[32,1024]{1,0:T(8,128)(2,1)} %get-tuple-element.35), channel_id=1, source_target_pairs={{0,10},{1,11},{2,8},{3,9},{4,14},{5,15},{6,12},{7,13},{8,2},{9,3},... | collective-permute-start | bytes 196616 | tf_op jit(solution)/shard_map/ppermute | solution.py:373
  65.9 7.5 %collective-permute-start.4 = (bf16[32,1024]{1,0:T(8,128)(2,1)}, bf16[32,1024]{1,0:T(8,128)(2,1)S(1)}, u32[]{:S(2)}, u32[]{:S(2)}) collective-permute-start(bf16[32,1024]{1,0:T(8,128)(2,1)} %get-tuple-element.34), channel_id=1, source_target_pairs={{0,8},{1,9},{2,10},{3,11},{4,12},{5,13},{6,14},{7,15},{8,0},{9,1},... | collective-permute-start | bytes 196616 | tf_op jit(solution)/shard_map/ppermute | solution.py:373
  65.9 7.5 %collective-permute-start.3 = (bf16[32,1024]{1,0:T(8,128)(2,1)}, bf16[32,1024]{1,0:T(8,128)(2,1)S(1)}, u32[]{:S(2)}, u32[]{:S(2)}) collective-permute-start(bf16[32,1024]{1,0:T(8,128)(2,1)} %get-tuple-element.33), channel_id=1, source_target_pairs={{0,6},{1,7},{2,4},{3,5},{4,2},{5,3},{6,0},{7,1},{8,14},{9,15},{10,... | collective-permute-start | bytes 196616 | tf_op jit(solution)/shard_map/ppermute | solution.py:373
  68.4 5.0 %collective-permute-start.2 = (bf16[32,1024]{1,0:T(8,128)(2,1)}, bf16[32,1024]{1,0:T(8,128)(2,1)S(1)}, u32[]{:S(2)}, u32[]{:S(2)}) collective-permute-start(bf16[32,1024]{1,0:T(8,128)(2,1)} %get-tuple-element.32), channel_id=1, source_target_pairs={{0,4},{1,5},{2,6},{3,7},{4,0},{5,1},{6,2},{7,3},{8,12},{9,13},{10,... | collective-permute-start | bytes 196616 | tf_op jit(solution)/shard_map/ppermute | solution.py:373
  70.9 3.3 %collective-permute-start.1 = (bf16[32,1024]{1,0:T(8,128)(2,1)}, bf16[32,1024]{1,0:T(8,128)(2,1)S(1)}, u32[]{:S(2)}, u32[]{:S(2)}) collective-permute-start(bf16[32,1024]{1,0:T(8,128)(2,1)} %get-tuple-element.31), channel_id=1, source_target_pairs={{0,2},{1,3},{2,0},{3,1},{4,6},{5,7},{6,4},{7,5},{8,10},{9,11},{10,... | collective-permute-start | bytes 196616 | tf_op jit(solution)/shard_map/ppermute | solution.py:373
  75.2 14.1 %collective-permute-start.8 = (bf16[32,1024]{1,0:T(8,128)(2,1)S(1)}, bf16[32,1024]{1,0:T(8,128)(2,1)S(1)}, u32[]{:S(2)}, u32[]{:S(2)}) collective-permute-start(bf16[32,1024]{1,0:T(8,128)(2,1)S(1)} %multiply_convert_fusion), channel_id=1, source_target_pairs={{0,12},{1,13},{2,14},{3,15},{4,8},{5,9},{6,10},{7,11},{8,4},{9,5},... | collective-permute-start | bytes 196616 | tf_op jit(solution)/shard_map/ppermute | solution.py:373
  77.0 12.2 %collective-permute-start.9 = (bf16[32,1024]{1,0:T(8,128)(2,1)S(1)}, bf16[32,1024]{1,0:T(8,128)(2,1)S(1)}, u32[]{:S(2)}, u32[]{:S(2)}) collective-permute-start(bf16[32,1024]{1,0:T(8,128)(2,1)S(1)} %multiply_convert_fusion), channel_id=1, source_target_pairs={{0,8},{1,9},{2,10},{3,11},{4,12},{5,13},{6,14},{7,15},{8,0},{9,1},... | collective-permute-start | bytes 196616 | tf_op jit(solution)/shard_map/ppermute | solution.py:373
  78.7 10.6 %collective-permute-start.10 = (bf16[32,1024]{1,0:T(8,128)(2,1)S(1)}, bf16[32,1024]{1,0:T(8,128)(2,1)S(1)}, u32[]{:S(2)}, u32[]{:S(2)}) collective-permute-start(bf16[32,1024]{1,0:T(8,128)(2,1)S(1)} %multiply_convert_fusion), channel_id=1, source_target_pairs={{0,4},{1,5},{2,6},{3,7},{4,0},{5,1},{6,2},{7,3},{8,12},{9,13},{10,... | collective-permute-start | bytes 196616 | tf_op jit(solution)/shard_map/ppermute | solution.py:373
  80.9 38.9 %all-to-all-start.1 = ((bf16[16,40,1024]{2,1,0:T(8,128)(2,1)}), bf16[16,40,1024]{2,1,0:T(8,128)(2,1)S(1)}, u32[]{:S(2)}, u32[]{:S(2)}) async-start(bf16[16,40,1024]{2,1,0:T(8,128)(2,1)} %pack.1), calls=%async_computation.1 | async-start | bytes 2621440 | tf_op jit(solution)/shard_map/all_to_all | solution.py:458
  89.3 13.9 %collective-permute-start.11 = (bf16[128,1024]{1,0:T(8,128)(2,1)S(1)}, bf16[128,1024]{1,0:T(8,128)(2,1)S(1)}, u32[]{:S(2)}, u32[]{:S(2)}) collective-permute-start(bf16[128,1024]{1,0:T(8,128)(2,1)S(1)} %pad_maximum_fusion.2), channel_id=1, source_target_pairs={{0,2},{1,3},{2,0},{3,1},{4,6},{5,7},{6,4},{7,5},{8,10},{9,11},{10,... | collective-permute-start | bytes 786440 | tf_op jit(solution)/shard_map/ppermute | solution.py:373
  103.4 4.2 %collective-permute-start.12 = (bf16[256,1024]{1,0:T(8,128)(2,1)S(1)}, bf16[256,1024]{1,0:T(8,128)(2,1)S(1)}, u32[]{:S(2)}, u32[]{:S(2)}) collective-permute-start(bf16[256,1024]{1,0:T(8,128)(2,1)S(1)} %pad_maximum_fusion.1), channel_id=1, source_target_pairs={{0,1},{1,0},{2,3},{3,2},{4,5},{5,4},{6,7},{7,6},{8,9},{9,8},{10,11... | collective-permute-start | bytes 1572872 | tf_op jit(solution)/shard_map/ppermute | solution.py:373

commit v9 on v7

--- a/solution.py
+++ b/solution.py
@@ -100,7 +100,7 @@
     )(dealing, cols, tile)
 
 
-def prepare_kernel(order, dealing, cols, token, empty, blocks, owners, table, zeros, sems):
+def prepare_kernel(order, dealing, cols, token, empty, blocks, owners, lasts, table, zeros, sems):
     del token
     count = (order + LANES) // LANES
     slots = dealing.shape[0]
@@ -128,6 +128,7 @@
             owner = jnp.where(known < 0, number, known)
             owners[number] = owner
             table[block] = owner
+            lasts[owner] = slot
 
     for fill in fills:
         fill.wait()
@@ -143,9 +144,10 @@
             jax.ShapeDtypeStruct(tile_shape, jnp.float32),
             jax.ShapeDtypeStruct((numbers,), jnp.int32),
             jax.ShapeDtypeStruct((numbers,), jnp.int32),
+            jax.ShapeDtypeStruct((numbers,), jnp.int32),
         ),
         in_specs=[SMEM, SMEM, SMEM],
-        out_specs=(ANY, SMEM, SMEM),
+        out_specs=(ANY, SMEM, SMEM, SMEM),
         scratch_shapes=[
             pltpu.SMEM((tile_shape[2] // LANES,), jnp.int32),
             pltpu.VMEM(tile_shape[:2] + (fill_cols,), jnp.float32),
@@ -158,11 +160,17 @@
 
 
 def slot_kernel(
-    dealing, rows, owners, cells, probe, measured, right_table, left_table,
-    term, kept, sent,
-    wide, patch, wave, half, resid, turned, mine, right, left, table_sem,
+    dealing, rows, *rest
 ):
-    del owners
+    sources, (term, kept, sent), rest = rest[:5], rest[5:8], rest[8:]
+    (cells, probe, right, measured, left), rest = rest[:5], rest[5:]
+    wide, patch, wave, half, resid, turned, mine, sems = rest
+    loads = [
+        pltpu.make_async_copy(source, held, sems.at[k])
+        for k, (source, held) in enumerate(zip(sources, (cells, probe, right, measured, left)))
+    ]
+    for load in loads:
+        load.start()
     order = probe.shape[1]
     total_rows = cells.shape[0]
     me = lax.axis_index("row")
@@ -170,12 +178,11 @@
     step = 64
     tile = 256
 
-    right_copy = pltpu.make_async_copy(right_table, right, table_sem.at[0])
-    left_copy = pltpu.make_async_copy(left_table, left, table_sem.at[1])
-    right_copy.start()
-    left_copy.start()
+    loads[0].wait()
     wide[0:total_rows, :] = cells[...].astype(jnp.float32)
     wide[total_rows:, :] = jnp.zeros((SUBLANES, 2 * order), jnp.float32)
+    loads[1].wait()
+
     @pl.loop(0, order // step)
     def _(i):
         place = pl.ds(pl.multiple_of(i * step, step), step)
@@ -190,13 +197,14 @@
     def dot(a, b):
         return jnp.dot(a, b, preferred_element_type=jnp.float32)
 
-    right_copy.wait()
+    loads[2].wait()
     for first in range(0, order, tile):
         here = slice(first, first + tile)
         there = slice(order + first, order + first + tile)
         half[:order, here] = dot(wave[...], right[:, here]).astype(half.dtype)
         half[order:, here] = dot(wave[...], right[:, there]).astype(half.dtype)
-    left_copy.wait()
+    loads[3].wait()
+    loads[4].wait()
     for first in range(0, order, tile):
         here = slice(first, first + tile)
         there = slice(order + first, order + first + tile)
@@ -234,12 +242,13 @@
     kept[...] = mine[pl.ds(pl.multiple_of(side * count, count), count), :]
     sent[...] = mine[pl.ds(pl.multiple_of((1 - side) * count, count), count), :].astype(sent.dtype)
 
-def slot_terms(cells, probe, measured, dealing, rows, owners):
+def slot_terms(cells, probe, measured, dealing, rows):
     order = probe.shape[1]
     total_rows = cells.shape[0]
     right, left = dft_tables(order)
     wide_cols = 2 * order
     bf16, f32 = jnp.bfloat16, jnp.float32
+    sources = (cells, probe, jnp.asarray(right), measured, jnp.asarray(left))
     return pl.pallas_call(
         slot_kernel,
         out_shape=(
@@ -247,9 +256,10 @@
             jax.ShapeDtypeStruct((order // 2, wide_cols), f32),
             jax.ShapeDtypeStruct((order // 2, wide_cols), bf16),
         ),
-        in_specs=[SMEM, SMEM, SMEM, VMEM, VMEM, VMEM, ANY, ANY],
+        in_specs=[SMEM, SMEM] + [ANY] * len(sources),
         out_specs=(VMEM,) * 3,
-        scratch_shapes=[
+        scratch_shapes=[pltpu.VMEM(source.shape, bf16) for source in sources]
+        + [
             pltpu.VMEM((total_rows + SUBLANES, wide_cols), f32),
             pltpu.VMEM((order, wide_cols), bf16),
             pltpu.VMEM((order, wide_cols), bf16),
@@ -257,16 +267,14 @@
             pltpu.VMEM((order, wide_cols), bf16),
             pltpu.VMEM((wide_cols, order), bf16),
             pltpu.VMEM((order, wide_cols), f32),
-            pltpu.VMEM((wide_cols, wide_cols), bf16),
-            pltpu.VMEM((wide_cols, wide_cols), bf16),
-            pltpu.SemaphoreType.DMA((2,)),
+            pltpu.SemaphoreType.DMA((len(sources),)),
         ],
         compiler_params=pltpu.CompilerParams(vmem_limit_bytes=54 * 2**20),
         cost_estimate=pl.CostEstimate(
             flops=8 * 2 * order**3 * 2, bytes_accessed=8 * 2**20, transcendentals=order * order
         ),
         name="slot",
-    )(dealing, rows, owners, cells, probe, measured, jnp.asarray(right), jnp.asarray(left))
+    )(dealing, rows, *sources)
 
 
 def pack_kernel(reach, own_rows, dealing, rows, term, out, padded):
@@ -297,7 +305,7 @@
     )(dealing, rows, term)
 
 
-def place_kernel(order, dealing, cols, blocks, owners, terms, empty, out, totals, sems):
+def place_kernel(order, dealing, cols, blocks, owners, lasts, terms, empty, out, totals, sems):
     del empty
     slots, tile_rows = terms.shape[0], terms.shape[1]
     count = (order + LANES) // LANES
@@ -305,7 +313,11 @@
     lane = lax.broadcasted_iota(jnp.int32, (tile_rows, LANES), 1)
     nothing = jnp.zeros((tile_rows, LANES), jnp.float32)
 
-    @pl.loop(0, slots, unroll=4)
+    def copy(number):
+        place = pl.multiple_of(blocks[number] * LANES, LANES)
+        return pltpu.make_async_copy(totals.at[number], out.at[:, :, pl.ds(place, LANES)], sems.at[number])
+
+    @pl.loop(0, slots)
     def _(slot):
         _, offset = window_start(cols[dealing[slot]], order, out.shape[2])
         shift = lax.rem(offset, LANES)
@@ -319,16 +331,12 @@
                 after = turned[b] if b < count - 1 else nothing
                 owner = owners[slot * count + b]
                 totals[owner, part] += jnp.where(lane < offset, before, after)
-
-    def copy(number):
-        place = pl.multiple_of(blocks[number] * LANES, LANES)
-        return pltpu.make_async_copy(totals.at[number], out.at[:, :, pl.ds(place, LANES)], sems.at[number])
-
-    @pl.loop(0, slots * count)
-    def _(number):
-        @pl.when(owners[number] == number)
-        def _():
-            copy(number).start()
+        for b in range(count):
+            owner = owners[slot * count + b]
+
+            @pl.when(lasts[owner] == slot)
+            def _():
+                copy(owner).start()
 
     @pl.loop(0, slots * count)
     def _(number):
@@ -337,23 +345,23 @@
             copy(number).wait()
 
 
-def place_windows(terms, empty, blocks, owners, dealing, cols, order):
+def place_windows(terms, empty, blocks, owners, lasts, dealing, cols, order):
     slots, tile_rows = terms.shape[0], terms.shape[1]
     count = (order + LANES) // LANES
     return pl.pallas_call(
         functools.partial(place_kernel, order),
         out_shape=jax.ShapeDtypeStruct(empty.shape, empty.dtype),
-        in_specs=[SMEM, SMEM, SMEM, SMEM, VMEM, ANY],
+        in_specs=[SMEM, SMEM, SMEM, SMEM, SMEM, VMEM, ANY],
         out_specs=ANY,
         scratch_shapes=[
             pltpu.VMEM((slots * count, 2, tile_rows, LANES), jnp.float32),
             pltpu.SemaphoreType.DMA((slots * count,)),
         ],
-        input_output_aliases={5: 0},
+        input_output_aliases={6: 0},
         compiler_params=pltpu.CompilerParams(vmem_limit_bytes=24 * 2**20),
         cost_estimate=pl.CostEstimate(flops=0, bytes_accessed=6 * 2**20, transcendentals=0),
         name="place",
-    )(dealing, cols, blocks, owners, terms, empty)
+    )(dealing, cols, blocks, owners, lasts, terms, empty)
 
 
 def strides(devices):
@@ -372,24 +380,20 @@
 def sum_probe(kept, sent, devices):
     me = lax.axis_index("row")
     total = kept + swap(sent, 1, devices).astype(jnp.float32)
-    parts = [1 << k for k in range(1, devices.bit_length() - 1)]
-    orders = (parts[:1] + parts[:0:-1], parts[1:2] + parts[:1] + parts[2:])
-    sets = jnp.split(total, 2)
-    for step in range(len(parts)):
-        for number, order in enumerate(orders):
-            digit = me // order[step] % 2
-            count = sets[number].shape[0] // 2
-            own = lax.dynamic_slice_in_dim(sets[number], digit * count, count)
-            other = lax.dynamic_slice_in_dim(sets[number], (1 - digit) * count, count)
-            sets[number] = own + swap(other.astype(jnp.bfloat16), order[step], devices).astype(jnp.float32)
-    return jnp.concatenate(sets), orders
-
-
-def join(whole, orders, devices):
+    for stride, radix in strides(devices)[1:]:
+        digit = me // stride % radix
+        count = total.shape[0] // radix
+        own = lax.dynamic_slice_in_dim(total, digit * count, count)
+        for k in range(1, radix):
+            share = lax.dynamic_slice_in_dim(total, lax.bitwise_xor(digit, k) * count, count)
+            own = own + swap(share.astype(jnp.bfloat16), k * stride, devices).astype(jnp.float32)
+        total = own
+    return total
+
+
+def join(whole, devices):
     me = lax.axis_index("row")
-    steps = strides(devices)
-    count, width = whole.shape[0] // 2, whole.shape[1]
-    for stride, radix in reversed(steps):
+    for stride, radix in reversed(strides(devices)):
         digit = me // stride % radix
         shares = [whole] + [swap(whole, k * stride, devices) for k in range(1, radix)]
         pieces = []
@@ -399,16 +403,7 @@
                 piece = jnp.where(lax.bitwise_xor(digit, k) == j, shares[k], piece)
             pieces.append(piece)
         whole = jnp.concatenate(pieces, axis=0)
-    axes = []
-    for stride, radix in steps:
-        axes += [2 * stride, stride] if radix == 4 else [stride]
-    whole = whole.reshape([2] * len(axes) + [2, count, width])
-    sets = []
-    for number, order in enumerate(orders):
-        one = lax.index_in_dim(whole, number, len(axes), keepdims=False)
-        one = one.transpose([0] + [axes.index(part) for part in order] + [len(axes), len(axes) + 1])
-        sets.append(one.reshape(2, -1, width))
-    return jnp.concatenate(sets, axis=1).reshape(-1, width)
+    return whole
 
 
 def body(object_field, probe, amplitude, row_offsets, col_offsets, dealing):
@@ -423,16 +418,18 @@
     pieces, token = fetch_windows(object_field, dealing, col_offsets, order)
     strips = lax.all_to_all(pieces, "row", split_axis=0, concat_axis=0, tiled=True)
     cells = strips[:, :own_rows].reshape(total_rows, 2 * order)
-    empty, blocks, owners = prepare(dealing, col_offsets, token, object_field.shape, order)
-    term, kept, sent = slot_terms(cells, probe, amplitude, dealing, row_offsets, owners)
-    total, orders = sum_probe(kept, sent, devices)
+    empty, blocks, owners, lasts = prepare(dealing, col_offsets, token, object_field.shape, order)
+    term, kept, sent = slot_terms(cells, probe, amplitude, dealing, row_offsets)
+    total = sum_probe(kept, sent, devices)
     terms = pack_rows(term, dealing, row_offsets, devices, own_rows, tile_rows)
     terms, total = lax.optimization_barrier((terms, total))
     arrived = lax.all_to_all(terms, "row", split_axis=0, concat_axis=0, tiled=True)
     share = (total * (1.0 / dealing.shape[0])).astype(jnp.bfloat16)
-    whole = join(share, orders, devices).astype(jnp.float32)
+    whole = join(share, devices).astype(jnp.float32)
     probe_grad = jnp.stack([whole[:, :order], whole[:, order:]])
-    object_grad = place_windows(arrived, empty, blocks, owners, dealing, col_offsets, order)
+    object_grad = place_windows(
+        arrived, empty, blocks, owners, lasts, dealing, col_offsets, order
+    )
     if spare:
         object_grad = object_grad[:, :own_rows]
     return (object_grad, probe_grad)

time: 126 us -> 119 us (0.944)
  blocking collectives: 0 us -> 37.1 us
  waiting for transfers between devices: 64.6 us -> 29.7 us
  starting transfers between devices: 26.4 us -> 19.5 us
  local copies, waits for them, and re-layouts: 2.13 us -> 0.29 us
    all_to_all x0 -> x1, blocking collectives: none -> 37.1 us  [body(): lax.all_to_all(pieces, 'row', split_axis=0, concat_axis=0, tiled=True)]
    all_to_all x1 -> x0, waiting for transfers between devices: 24.2 us -> none  [body(): lax.all_to_all(pieces, 'row', split_axis=0, concat_axis=0, tiled=True)]
    all_to_all x1, waiting for transfers between devices: 25.6 us -> 5.69 us  [body(): lax.all_to_all(terms, 'row', split_axis=0, concat_axis=0, tiled=True)]
    ppermute x12 -> x10, waiting for transfers between devices: 14.8 us -> 24 us  [swap(): return lax.ppermute(x, 'row', [(d, d ^ distance) for d in range(devices)])]
    all_to_all x1 -> x0, starting transfers between devices: 6.57 us -> none  [body(): lax.all_to_all(pieces, 'row', split_axis=0, concat_axis=0, tiled=True)]
    all_to_all x1, starting transfers between devices: 10.5 us -> 7.42 us  [body(): lax.all_to_all(terms, 'row', split_axis=0, concat_axis=0, tiled=True)]
    ppermute x12 -> x10, starting transfers between devices: 9.39 us -> 12.1 us  [swap(): return lax.ppermute(x, 'row', [(d, d ^ distance) for d in range(devices)])]
    unnamed x17 -> x8, local copies, waits for them, and re-layouts: 1.63 us -> 0.01 us
  transfers between devices with their start and end apart: 14 -> 11, of which waited for: 10 -> 6; matrix products, arithmetic and copies ran while one was open for 2% -> 2% of each run, Pallas kernels for 6% -> 7%
where the time goes in v9:
time: 119 us
  blocking collectives  37.1 us (31%)
  waiting for transfers between devices  29.7 us (25%)
  Pallas kernels  27.5 us (23%)
  starting transfers between devices  19.5 us (16%)
  other arithmetic  3.75 us (3%)
    all_to_all x1, blocking collectives, body(): lax.all_to_all(pieces, 'row', split_axis=0, concat_axis=0, tiled=True)  37.1 us
    ppermute x10, waiting for transfers between devices, swap(): return lax.ppermute(x, 'row', [(d, d ^ distance) for d in range(devices)])  24 us
    ppermute x10, starting transfers between devices, swap(): return lax.ppermute(x, 'row', [(d, d ^ distance) for d in range(devices)])  12.1 us
    pallas_call x1, Pallas kernels, slot_terms(): pl.pallas_call(slot_kernel, out_shape=(jax.ShapeDtypeStruct((order, wide_...  9.9 us
    all_to_all x1, starting transfers between devices, body(): lax.all_to_all(terms, 'row', split_axis=0, concat_axis=0, tiled=True)  7.42 us
    pallas_call x1, Pallas kernels, prepare(): pl.pallas_call(functools.partial(prepare_kernel, order), out_shape=(jax.S...  5.93 us
    all_to_all x1, waiting for transfers between devices, body(): lax.all_to_all(terms, 'row', split_axis=0, concat_axis=0, tiled=True)  5.69 us
    pallas_call x1, Pallas kernels, place_windows(): pl.pallas_call(functools.partial(place_kernel, order), out_shape=jax.Shap...  4.88 us
  transfers between devices with their start and end apart: 11, of which 6 were waited for; matrix products, arithmetic and copies ran while one was open for 2% of the time, Pallas kernels for 7%

profile of v9, /device:TPU:15, one launch (start us, length us, event | category | flops | bytes accessed | tf_op | source)
XLA Modules:
  0.0 118.7 jit_solution(2980341257756319403)
XLA Ops:
  0.6 4.6 %fetch.1 = (bf16[16,40,1024]{2,1,0:T(8,128)(2,1)}, s32[1]{0:T(128)}) custom-call(s32[16]{0:T(128)} %dealing.9, s32[16]{0:T(128)} %cols.5, f32[2,40,32768]{2,1,0:T(8,128)} %tile.1), custom_call_target="tpu_custom_call" | custom-call | bytes 6291456 | tf_op jit(solution)/shard_map/fetch/pallas_call | solution.py:85
  5.2 37.1 %all_to_all.10 = bf16[16,40,1024]{2,1,0:T(8,128)(2,1)} all-to-all(bf16[16,40,1024]{2,1,0:T(8,128)(2,1)} %get-tuple-element.17), channel_id=1, replica_groups=mesh['groups'=2,'row'=16] {'row'}, dimensions={0} | all-to-all | bytes 2621440 | tf_op jit(solution)/shard_map/all_to_all | solution.py:419
  42.4 9.9 %slot.1 = (bf16[512,1024]{1,0:T(8,128)(2,1)}, f32[256,1024]{1,0:T(8,128)}, bf16[256,1024]{1,0:T(8,128)(2,1)}) custom-call(s32[16]{0:T(128)} %dealing.9, s32[16]{0:T(128)} %rows.3, bf16[640,1024]{1,0:T(8,128)(2,1)} %bitcast.5, bf16[2,512,512]{2,1,0:T(8,128)(2,1)} %rest_1_.1, bf16[1024,1024]{1,0:T(8,128)(2,1)} %constant.81.clone.rest_2_, ...), custom_call_target="tpu_custom_call" | custom-call | flops 4294967296 | bytes 8388608 | tf_op jit(solution)/shard_map/slot/pallas_call | solution.py:252
  52.3 0.3 collective-permute-start
  52.6 1.9 %collective-permute-done = bf16[256,1024]{1,0:T(8,128)(2,1)S(1)} collective-permute-done((bf16[256,1024]{1,0:T(8,128)(2,1)}, bf16[256,1024]{1,0:T(8,128)(2,1)S(1)}, u32[]{:S(2)}, u32[]{:S(2)}) %collective-permute-start) | collective-permute-done | bytes 524320 | tf_op jit(solution)/shard_map/ppermute | solution.py:377
  54.5 0.0 copy-start
  54.5 0.0 copy-start.1
  54.5 0.0 copy-start.3
  54.5 1.5 %convert_add_fusion = f32[256,1024]{1,0:T(8,128)S(1)} fusion(f32[256,1024]{1,0:T(8,128)} %get-tuple-element.19, bf16[256,1024]{1,0:T(8,128)(2,1)S(1)} %collective-permute-done), kind=kLoop, calls=%fused_computation.4 | loop fusion | flops 524288 | bytes 2621440 | tf_op jit(solution)/shard_map/add | solution.py:382
  56.0 1.1 collective-permute-start.1
  57.1 6.7 %collective-permute-done.1 = bf16[128,1024]{1,0:T(8,128)(2,1)S(1)} collective-permute-done((bf16[128,1024]{1,0:T(8,128)(2,1)S(1)}, bf16[128,1024]{1,0:T(8,128)(2,1)S(1)}, u32[]{:S(2)}, u32[]{:S(2)}) %collective-permute-start.1) | collective-permute-done | bytes 262176 | tf_op jit(solution)/shard_map/ppermute | solution.py:377
  63.8 0.1 convert_add_fusion.1
  63.9 0.5 collective-permute-start.4
  64.4 2.6 %collective-permute-start.3 = (bf16[32,1024]{1,0:T(8,128)(2,1)S(1)}, bf16[32,1024]{1,0:T(8,128)(2,1)S(1)}, u32[]{:S(2)}, u32[]{:S(2)}) collective-permute-start(bf16[32,1024]{1,0:T(8,128)(2,1)S(1)} %get-tuple-element.32), channel_id=1, source_target_pairs={{0,8},{1,9},{2,10},{3,11},{4,12},{5,13},{6,14},{7,15},{8,0},{9,1},... | collective-permute-start | bytes 196616 | tf_op jit(solution)/shard_map/ppermute | solution.py:377
  66.9 0.0 collective-permute-start.2
  66.9 0.0 copy-done
  66.9 0.0 copy-done.1
  66.9 0.0 copy-done.3
  66.9 2.2 %pack.1 = bf16[16,40,1024]{2,1,0:T(8,128)(2,1)} custom-call(s32[16]{0:T(128)S(1)} %copy-done.1, s32[16]{0:T(128)S(1)} %copy-done.3, bf16[512,1024]{1,0:T(8,128)(2,1)S(1)} %copy-done), custom_call_target="tpu_custom_call" | custom-call | bytes 3145728 | tf_op jit(solution)/shard_map/pack/pallas_call | solution.py:296
  69.1 0.0 collective-permute-done.4
  69.1 1.7 %collective-permute-done.3 = bf16[32,1024]{1,0:T(8,128)(2,1)S(1)} collective-permute-done((bf16[32,1024]{1,0:T(8,128)(2,1)S(1)}, bf16[32,1024]{1,0:T(8,128)(2,1)S(1)}, u32[]{:S(2)}, u32[]{:S(2)}) %collective-permute-start.3) | collective-permute-done | bytes 65568 | tf_op jit(solution)/shard_map/ppermute | solution.py:377
  70.8 0.1 collective-permute-done.2
  71.0 0.8 collective-permute-start.5
  71.8 4.0 %collective-permute-start.6 = (bf16[32,1024]{1,0:T(8,128)(2,1)S(1)}, bf16[32,1024]{1,0:T(8,128)(2,1)S(1)}, u32[]{:S(2)}, u32[]{:S(2)}) collective-permute-start(bf16[32,1024]{1,0:T(8,128)(2,1)S(1)} %multiply_convert_fusion), channel_id=1, source_target_pairs={{0,8},{1,9},{2,10},{3,11},{4,12},{5,13},{6,14},{7,15},{8,0},{9,1},... | collective-permute-start | bytes 196616 | tf_op jit(solution)/shard_map/ppermute | solution.py:377
  75.8 0.0 collective-permute-start.7
  75.9 7.4 %all-to-all-start.1 = ((bf16[16,40,1024]{2,1,0:T(8,128)(2,1)}), bf16[16,40,1024]{2,1,0:T(8,128)(2,1)S(1)}, u32[]{:S(2)}, u32[]{:S(2)}) async-start(bf16[16,40,1024]{2,1,0:T(8,128)(2,1)} %pack.1), calls=%async_computation.1 | async-start | bytes 2621440 | tf_op jit(solution)/shard_map/all_to_all | solution.py:426
  83.3 0.0 copy-start.2
  83.3 0.0 collective-permute-done.5
  83.3 0.0 collective-permute-done.6
  83.3 0.0 collective-permute-done.7
  83.4 0.3 collective-permute-start.8
  83.8 13.6 %collective-permute-done.8 = bf16[128,1024]{1,0:T(8,128)(2,1)S(1)} collective-permute-done((bf16[128,1024]{1,0:T(8,128)(2,1)S(1)}, bf16[128,1024]{1,0:T(8,128)(2,1)S(1)}, u32[]{:S(2)}, u32[]{:S(2)}) %collective-permute-start.8) | collective-permute-done | bytes 262176 | tf_op jit(solution)/shard_map/ppermute | solution.py:377
  97.3 0.1 broadcast_select_fusion.3
  97.5 2.5 %collective-permute-start.9 = (bf16[256,1024]{1,0:T(8,128)(2,1)S(1)}, bf16[256,1024]{1,0:T(8,128)(2,1)S(1)}, u32[]{:S(2)}, u32[]{:S(2)}) collective-permute-start(bf16[256,1024]{1,0:T(8,128)(2,1)S(1)} %pad_maximum_fusion.1), channel_id=1, source_target_pairs={{0,1},{1,0},{2,3},{3,2},{4,5},{5,4},{6,7},{7,6},{8,9},{9,8},{10,11... | collective-permute-start | bytes 1572872 | tf_op jit(solution)/shard_map/ppermute | solution.py:377
  100.0 0.0 copy-done.2
  100.0 5.9 %prepare.1 = (f32[2,40,32768]{2,1,0:T(8,128)}, s32[80]{0:T(128)S(1)}, s32[80]{0:T(128)S(1)}, s32[80]{0:T(128)S(1)}) custom-call(s32[16]{0:T(128)S(1)} %copy-done.1, s32[16]{0:T(128)S(1)} %copy-done.2, s32[1]{0:T(128)} %get-tuple-element.13.token), custom_call_target="tpu_custom_call" | custom-call | bytes 11534336 | tf_op jit(solution)/shard_map/prepare/pallas_call | solution.py:141
  106.0 0.0 collective-permute-done.9
  106.0 0.2 broadcast_select_fusion.1
  106.2 0.2 maximum_convert_fusion
  106.5 0.2 slice_bitcast_fusion.1
  106.7 1.5 %pad_maximum_fusion = f32[2,512,512]{2,1,0:T(8,128)} fusion(f32[1,512,512]{2,1,0:T(8,128)S(1)} %get-tuple-element.25, f32[1,512,512]{2,1,0:T(8,128)S(1)} %get-tuple-element.24), kind=kLoop, calls=%fused_computation | loop fusion | flops 524288 | bytes 4194304 | tf_op jit(solution)/shard_map/stack | solution.py:429
  108.2 5.7 %all-to-all-done.1.terms = bf16[16,40,1024]{2,1,0:T(8,128)(2,1)S(1)} async-done(((bf16[16,40,1024]{2,1,0:T(8,128)(2,1)}), bf16[16,40,1024]{2,1,0:T(8,128)(2,1)S(1)}, u32[]{:S(2)}, u32[]{:S(2)}) %all-to-all-start.1) | async-done | bytes 1310752 | tf_op jit(solution)/shard_map/all_to_all | solution.py:426
  113.9 4.9 %place.1 = f32[2,40,32768]{2,1,0:T(8,128)} custom-call(s32[16]{0:T(128)S(1)} %copy-done.1, s32[16]{0:T(128)S(1)} %copy-done.2, s32[80]{0:T(128)S(1)} %get-tuple-element.14.blocks, s32[80]{0:T(128)S(1)} %get-tuple-element.15.owners, s32[80]{0:T(128)S(1)} %get-tuple-element.16.lasts, ...), custom_call_target="tpu_custom_call", output_to_operand_aliasing={{}: (6, {})} | custom-call | bytes 6291456 | tf_op jit(solution)/shard_map/place/pallas_call | solution.py:351
  (7 shorter events, 0.2 us)
Async XLA Ops:
  52.3 2.2 %collective-permute-start = (bf16[256,1024]{1,0:T(8,128)(2,1)}, bf16[256,1024]{1,0:T(8,128)(2,1)S(1)}, u32[]{:S(2)}, u32[]{:S(2)}) collective-permute-start(bf16[256,1024]{1,0:T(8,128)(2,1)} %get-tuple-element.20), channel_id=1, source_target_pairs={{0,1},{1,0},{2,3},{3,2},{4,5},{5,4},{6,7},{7,6},{8,9},{9,8},{10,11... | collective-permute-start | bytes 1572872 | tf_op jit(solution)/shard_map/ppermute | solution.py:377
  54.5 12.4 %copy-start = (bf16[512,1024]{1,0:T(8,128)(2,1)S(1)}, bf16[512,1024]{1,0:T(8,128)(2,1)}, u32[]{:S(2)}) copy-start(bf16[512,1024]{1,0:T(8,128)(2,1)} %get-tuple-element.18.term) | copy-start | bytes 3145732
  54.5 12.4 %copy-start.1 = (s32[16]{0:T(128)S(1)}, s32[16]{0:T(128)}, u32[]{:S(2)}) copy-start(s32[16]{0:T(128)} %dealing.9) | copy-start | bytes 196
  54.5 12.5 %copy-start.3 = (s32[16]{0:T(128)S(1)}, s32[16]{0:T(128)}, u32[]{:S(2)}) copy-start(s32[16]{0:T(128)} %rows.3) | copy-start | bytes 196
  56.0 7.8 %collective-permute-start.1 = (bf16[128,1024]{1,0:T(8,128)(2,1)S(1)}, bf16[128,1024]{1,0:T(8,128)(2,1)S(1)}, u32[]{:S(2)}, u32[]{:S(2)}) collective-permute-start(bf16[128,1024]{1,0:T(8,128)(2,1)S(1)} %dynamic-slice_convert_fusion), channel_id=1, source_target_pairs={{0,2},{1,3},{2,0},{3,1},{4,6},{5,7},{6,4},{7,5},{8,10},{9,11},{10,... | collective-permute-start | bytes 786440 | tf_op jit(solution)/shard_map/ppermute | solution.py:377
  63.9 5.3 %collective-permute-start.4 = (bf16[32,1024]{1,0:T(8,128)(2,1)S(1)}, bf16[32,1024]{1,0:T(8,128)(2,1)S(1)}, u32[]{:S(2)}, u32[]{:S(2)}) collective-permute-start(bf16[32,1024]{1,0:T(8,128)(2,1)S(1)} %get-tuple-element.31), channel_id=1, source_target_pairs={{0,12},{1,13},{2,14},{3,15},{4,8},{5,9},{6,10},{7,11},{8,4},{9,5},... | collective-permute-start | bytes 196616 | tf_op jit(solution)/shard_map/ppermute | solution.py:377
  64.4 6.4 %collective-permute-start.3 = (bf16[32,1024]{1,0:T(8,128)(2,1)S(1)}, bf16[32,1024]{1,0:T(8,128)(2,1)S(1)}, u32[]{:S(2)}, u32[]{:S(2)}) collective-permute-start(bf16[32,1024]{1,0:T(8,128)(2,1)S(1)} %get-tuple-element.32), channel_id=1, source_target_pairs={{0,8},{1,9},{2,10},{3,11},{4,12},{5,13},{6,14},{7,15},{8,0},{9,1},... | collective-permute-start | bytes 196616 | tf_op jit(solution)/shard_map/ppermute | solution.py:377
  66.9 4.0 %collective-permute-start.2 = (bf16[32,1024]{1,0:T(8,128)(2,1)S(1)}, bf16[32,1024]{1,0:T(8,128)(2,1)S(1)}, u32[]{:S(2)}, u32[]{:S(2)}) collective-permute-start(bf16[32,1024]{1,0:T(8,128)(2,1)S(1)} %get-tuple-element.30), channel_id=1, source_target_pairs={{0,4},{1,5},{2,6},{3,7},{4,0},{5,1},{6,2},{7,3},{8,12},{9,13},{10,... | collective-permute-start | bytes 196616 | tf_op jit(solution)/shard_map/ppermute | solution.py:377
  71.0 12.3 %collective-permute-start.5 = (bf16[32,1024]{1,0:T(8,128)(2,1)S(1)}, bf16[32,1024]{1,0:T(8,128)(2,1)S(1)}, u32[]{:S(2)}, u32[]{:S(2)}) collective-permute-start(bf16[32,1024]{1,0:T(8,128)(2,1)S(1)} %multiply_convert_fusion), channel_id=1, source_target_pairs={{0,12},{1,13},{2,14},{3,15},{4,8},{5,9},{6,10},{7,11},{8,4},{9,5},... | collective-permute-start | bytes 196616 | tf_op jit(solution)/shard_map/ppermute | solution.py:377
  71.8 11.5 %collective-permute-start.6 = (bf16[32,1024]{1,0:T(8,128)(2,1)S(1)}, bf16[32,1024]{1,0:T(8,128)(2,1)S(1)}, u32[]{:S(2)}, u32[]{:S(2)}) collective-permute-start(bf16[32,1024]{1,0:T(8,128)(2,1)S(1)} %multiply_convert_fusion), channel_id=1, source_target_pairs={{0,8},{1,9},{2,10},{3,11},{4,12},{5,13},{6,14},{7,15},{8,0},{9,1},... | collective-permute-start | bytes 196616 | tf_op jit(solution)/shard_map/ppermute | solution.py:377
  75.8 7.5 %collective-permute-start.7 = (bf16[32,1024]{1,0:T(8,128)(2,1)S(1)}, bf16[32,1024]{1,0:T(8,128)(2,1)S(1)}, u32[]{:S(2)}, u32[]{:S(2)}) collective-permute-start(bf16[32,1024]{1,0:T(8,128)(2,1)S(1)} %multiply_convert_fusion), channel_id=1, source_target_pairs={{0,4},{1,5},{2,6},{3,7},{4,0},{5,1},{6,2},{7,3},{8,12},{9,13},{10,... | collective-permute-start | bytes 196616 | tf_op jit(solution)/shard_map/ppermute | solution.py:377
  75.9 38.0 %all-to-all-start.1 = ((bf16[16,40,1024]{2,1,0:T(8,128)(2,1)}), bf16[16,40,1024]{2,1,0:T(8,128)(2,1)S(1)}, u32[]{:S(2)}, u32[]{:S(2)}) async-start(bf16[16,40,1024]{2,1,0:T(8,128)(2,1)} %pack.1), calls=%async_computation.1 | async-start | bytes 2621440 | tf_op jit(solution)/shard_map/all_to_all | solution.py:426
  83.3 16.7 %copy-start.2 = (s32[16]{0:T(128)S(1)}, s32[16]{0:T(128)}, u32[]{:S(2)}) copy-start(s32[16]{0:T(128)} %cols.5) | copy-start | bytes 196
  83.4 13.9 %collective-permute-start.8 = (bf16[128,1024]{1,0:T(8,128)(2,1)S(1)}, bf16[128,1024]{1,0:T(8,128)(2,1)S(1)}, u32[]{:S(2)}, u32[]{:S(2)}) collective-permute-start(bf16[128,1024]{1,0:T(8,128)(2,1)S(1)} %pad_maximum_fusion.2), channel_id=1, source_target_pairs={{0,2},{1,3},{2,0},{3,1},{4,6},{5,7},{6,4},{7,5},{8,10},{9,11},{10,... | collective-permute-start | bytes 786440 | tf_op jit(solution)/shard_map/ppermute | solution.py:377
  97.5 8.4 %collective-permute-start.9 = (bf16[256,1024]{1,0:T(8,128)(2,1)S(1)}, bf16[256,1024]{1,0:T(8,128)(2,1)S(1)}, u32[]{:S(2)}, u32[]{:S(2)}) collective-permute-start(bf16[256,1024]{1,0:T(8,128)(2,1)S(1)} %pad_maximum_fusion.1), channel_id=1, source_target_pairs={{0,1},{1,0},{2,3},{3,2},{4,5},{5,4},{6,7},{7,6},{8,9},{9,8},{10,11... | collective-permute-start | bytes 1572872 | tf_op jit(solution)/shard_map/ppermute | solution.py:377

commit v10 on v7

--- a/solution.py
+++ b/solution.py
@@ -152,15 +152,15 @@
             pltpu.SemaphoreType.DMA((tile_shape[2] // fill_cols,)),
         ],
         compiler_params=pltpu.CompilerParams(vmem_limit_bytes=8 * 2**20),
-        cost_estimate=pl.CostEstimate(flops=0, bytes_accessed=11 * 2**20, transcendentals=0),
+        cost_estimate=pl.CostEstimate(flops=0, bytes_accessed=110 * 2**20, transcendentals=0),
         name="prepare",
     )(dealing, cols, token)
 
 
 def slot_kernel(
-    dealing, rows, owners, cells, probe, measured, right_table, left_table,
+    dealing, rows, owners, cells, probe, measured, right, left,
     term, kept, sent,
-    wide, patch, wave, half, resid, turned, mine, right, left, table_sem,
+    wide, patch, wave, half, resid, turned, mine,
 ):
     del owners
     order = probe.shape[1]
@@ -170,10 +170,6 @@
     step = 64
     tile = 256
 
-    right_copy = pltpu.make_async_copy(right_table, right, table_sem.at[0])
-    left_copy = pltpu.make_async_copy(left_table, left, table_sem.at[1])
-    right_copy.start()
-    left_copy.start()
     wide[0:total_rows, :] = cells[...].astype(jnp.float32)
     wide[total_rows:, :] = jnp.zeros((SUBLANES, 2 * order), jnp.float32)
     @pl.loop(0, order // step)
@@ -190,13 +186,11 @@
     def dot(a, b):
         return jnp.dot(a, b, preferred_element_type=jnp.float32)
 
-    right_copy.wait()
     for first in range(0, order, tile):
         here = slice(first, first + tile)
         there = slice(order + first, order + first + tile)
         half[:order, here] = dot(wave[...], right[:, here]).astype(half.dtype)
         half[order:, here] = dot(wave[...], right[:, there]).astype(half.dtype)
-    left_copy.wait()
     for first in range(0, order, tile):
         here = slice(first, first + tile)
         there = slice(order + first, order + first + tile)
@@ -237,8 +231,8 @@
 def slot_terms(cells, probe, measured, dealing, rows, owners):
     order = probe.shape[1]
     total_rows = cells.shape[0]
+    wide_cols = 2 * order
     right, left = dft_tables(order)
-    wide_cols = 2 * order
     bf16, f32 = jnp.bfloat16, jnp.float32
     return pl.pallas_call(
         slot_kernel,
@@ -247,7 +241,7 @@
             jax.ShapeDtypeStruct((order // 2, wide_cols), f32),
             jax.ShapeDtypeStruct((order // 2, wide_cols), bf16),
         ),
-        in_specs=[SMEM, SMEM, SMEM, VMEM, VMEM, VMEM, ANY, ANY],
+        in_specs=[SMEM, SMEM, SMEM, VMEM, VMEM, VMEM, VMEM, VMEM],
         out_specs=(VMEM,) * 3,
         scratch_shapes=[
             pltpu.VMEM((total_rows + SUBLANES, wide_cols), f32),
@@ -257,11 +251,8 @@
             pltpu.VMEM((order, wide_cols), bf16),
             pltpu.VMEM((wide_cols, order), bf16),
             pltpu.VMEM((order, wide_cols), f32),
-            pltpu.VMEM((wide_cols, wide_cols), bf16),
-            pltpu.VMEM((wide_cols, wide_cols), bf16),
-            pltpu.SemaphoreType.DMA((2,)),
         ],
-        compiler_params=pltpu.CompilerParams(vmem_limit_bytes=54 * 2**20),
+        compiler_params=pltpu.CompilerParams(vmem_limit_bytes=40 * 2**20),
         cost_estimate=pl.CostEstimate(
             flops=8 * 2 * order**3 * 2, bytes_accessed=8 * 2**20, transcendentals=order * order
         ),
@@ -372,24 +363,20 @@
 def sum_probe(kept, sent, devices):
     me = lax.axis_index("row")
     total = kept + swap(sent, 1, devices).astype(jnp.float32)
-    parts = [1 << k for k in range(1, devices.bit_length() - 1)]
-    orders = (parts[:1] + parts[:0:-1], parts[1:2] + parts[:1] + parts[2:])
-    sets = jnp.split(total, 2)
-    for step in range(len(parts)):
-        for number, order in enumerate(orders):
-            digit = me // order[step] % 2
-            count = sets[number].shape[0] // 2
-            own = lax.dynamic_slice_in_dim(sets[number], digit * count, count)
-            other = lax.dynamic_slice_in_dim(sets[number], (1 - digit) * count, count)
-            sets[number] = own + swap(other.astype(jnp.bfloat16), order[step], devices).astype(jnp.float32)
-    return jnp.concatenate(sets), orders
-
-
-def join(whole, orders, devices):
+    for stride, radix in strides(devices)[1:]:
+        digit = me // stride % radix
+        count = total.shape[0] // radix
+        own = lax.dynamic_slice_in_dim(total, digit * count, count)
+        for k in range(1, radix):
+            share = lax.dynamic_slice_in_dim(total, lax.bitwise_xor(digit, k) * count, count)
+            own = own + swap(share.astype(jnp.bfloat16), k * stride, devices).astype(jnp.float32)
+        total = own
+    return total
+
+
+def join(whole, devices):
     me = lax.axis_index("row")
-    steps = strides(devices)
-    count, width = whole.shape[0] // 2, whole.shape[1]
-    for stride, radix in reversed(steps):
+    for stride, radix in reversed(strides(devices)):
         digit = me // stride % radix
         shares = [whole] + [swap(whole, k * stride, devices) for k in range(1, radix)]
         pieces = []
@@ -399,16 +386,7 @@
                 piece = jnp.where(lax.bitwise_xor(digit, k) == j, shares[k], piece)
             pieces.append(piece)
         whole = jnp.concatenate(pieces, axis=0)
-    axes = []
-    for stride, radix in steps:
-        axes += [2 * stride, stride] if radix == 4 else [stride]
-    whole = whole.reshape([2] * len(axes) + [2, count, width])
-    sets = []
-    for number, order in enumerate(orders):
-        one = lax.index_in_dim(whole, number, len(axes), keepdims=False)
-        one = one.transpose([0] + [axes.index(part) for part in order] + [len(axes), len(axes) + 1])
-        sets.append(one.reshape(2, -1, width))
-    return jnp.concatenate(sets, axis=1).reshape(-1, width)
+    return whole
 
 
 def body(object_field, probe, amplitude, row_offsets, col_offsets, dealing):
@@ -425,12 +403,12 @@
     cells = strips[:, :own_rows].reshape(total_rows, 2 * order)
     empty, blocks, owners = prepare(dealing, col_offsets, token, object_field.shape, order)
     term, kept, sent = slot_terms(cells, probe, amplitude, dealing, row_offsets, owners)
-    total, orders = sum_probe(kept, sent, devices)
+    total = sum_probe(kept, sent, devices)
     terms = pack_rows(term, dealing, row_offsets, devices, own_rows, tile_rows)
     terms, total = lax.optimization_barrier((terms, total))
     arrived = lax.all_to_all(terms, "row", split_axis=0, concat_axis=0, tiled=True)
     share = (total * (1.0 / dealing.shape[0])).astype(jnp.bfloat16)
-    whole = join(share, orders, devices).astype(jnp.float32)
+    whole = join(share, devices).astype(jnp.float32)
     probe_grad = jnp.stack([whole[:, :order], whole[:, order:]])
     object_grad = place_windows(arrived, empty, blocks, owners, dealing, col_offsets, order)
     if spare:

time: 126 us -> 120 us (0.952)
  waiting for transfers between devices: 64.6 us -> 60.9 us
  local copies, waits for them, and re-layouts: 2.13 us -> 5.73 us
  Pallas kernels: 27.1 us -> 24.5 us
  starting transfers between devices: 26.4 us -> 24.5 us
    all_to_all x1, waiting for transfers between devices: 25.6 us -> 10.1 us  [body(): lax.all_to_all(terms, 'row', split_axis=0, concat_axis=0, tiled=True)]
    ppermute x12 -> x10, waiting for transfers between devices: 14.8 us -> 26.1 us  [swap(): return lax.ppermute(x, 'row', [(d, d ^ distance) for d in range(devices)])]
    unnamed x17 -> x14, local copies, waits for them, and re-layouts: 1.63 us -> 5.47 us
    all_to_all x1, starting transfers between devices: 10.5 us -> 7.49 us  [body(): lax.all_to_all(terms, 'row', split_axis=0, concat_axis=0, tiled=True)]
    pallas_call x1, Pallas kernels: 10.3 us -> 7.51 us  [slot_terms(): pl.pallas_call(slot_kernel, out_shape=(jax.ShapeDtypeStruct((order, wide_...]
    ppermute x12 -> x10, starting transfers between devices: 9.39 us -> 10.3 us  [swap(): return lax.ppermute(x, 'row', [(d, d ^ distance) for d in range(devices)])]
  transfers between devices with their start and end apart: 14 -> 12, of which waited for: 10 -> 8; matrix products, arithmetic and copies ran while one was open for 2% -> 2% of each run, Pallas kernels for 6% -> 7%
where the time goes in v10:
time: 120 us
  waiting for transfers between devices  60.9 us (51%)
  Pallas kernels  24.5 us (20%)
  starting transfers between devices  24.5 us (20%)
  local copies, waits for them, and re-layouts  5.73 us (5%)
  other arithmetic  3.5 us (3%)
    ppermute x10, waiting for transfers between devices, swap(): return lax.ppermute(x, 'row', [(d, d ^ distance) for d in range(devices)])  26.1 us
    all_to_all x1, waiting for transfers between devices, body(): lax.all_to_all(pieces, 'row', split_axis=0, concat_axis=0, tiled=True)  24.6 us
    ppermute x10, starting transfers between devices, swap(): return lax.ppermute(x, 'row', [(d, d ^ distance) for d in range(devices)])  10.3 us
    all_to_all x1, waiting for transfers between devices, body(): lax.all_to_all(terms, 'row', split_axis=0, concat_axis=0, tiled=True)  10.1 us
    pallas_call x1, Pallas kernels, slot_terms(): pl.pallas_call(slot_kernel, out_shape=(jax.ShapeDtypeStruct((order, wide_...  7.51 us
    all_to_all x1, starting transfers between devices, body(): lax.all_to_all(terms, 'row', split_axis=0, concat_axis=0, tiled=True)  7.49 us
    all_to_all x1, starting transfers between devices, body(): lax.all_to_all(pieces, 'row', split_axis=0, concat_axis=0, tiled=True)  6.7 us
    pallas_call x1, Pallas kernels, prepare(): pl.pallas_call(functools.partial(prepare_kernel, order), out_shape=(jax.S...  5.93 us
  transfers between devices with their start and end apart: 12, of which 8 were waited for; matrix products, arithmetic and copies ran while one was open for 2% of the time, Pallas kernels for 7%

profile of v10, /device:TPU:15, one launch (start us, length us, event | category | flops | bytes accessed | tf_op | source)
XLA Modules:
  0.0 120.0 jit_solution(5164498336331897036)
XLA Ops:
  0.6 4.6 %fetch.1 = (bf16[16,40,1024]{2,1,0:T(8,128)(2,1)}, s32[1]{0:T(128)}) custom-call(s32[16]{0:T(128)} %dealing.9, s32[16]{0:T(128)} %cols.5, f32[2,40,32768]{2,1,0:T(8,128)} %tile.1), custom_call_target="tpu_custom_call" | custom-call | bytes 6291456 | tf_op jit(solution)/shard_map/fetch/pallas_call | solution.py:85
  5.2 0.0 copy-start
  5.3 0.0 copy-start.1
  5.3 0.0 copy-start.2
  5.3 6.7 %all-to-all-start = ((bf16[16,40,1024]{2,1,0:T(8,128)(2,1)}), bf16[16,40,1024]{2,1,0:T(8,128)(2,1)S(1)}, u32[]{:S(2)}, u32[]{:S(2)}) async-start(bf16[16,40,1024]{2,1,0:T(8,128)(2,1)} %get-tuple-element.15), calls=%async_computation | async-start | bytes 2621440 | tf_op jit(solution)/shard_map/all_to_all | solution.py:402
  12.0 0.0 copy-done
  12.0 0.0 copy-done.1
  12.0 5.9 %prepare.1 = (f32[2,40,32768]{2,1,0:T(8,128)}, s32[80]{0:T(128)S(1)}, s32[80]{0:T(128)S(1)}) custom-call(s32[16]{0:T(128)S(1)} %copy-done, s32[16]{0:T(128)S(1)} %copy-done.1, s32[1]{0:T(128)} %get-tuple-element.12.token), custom_call_target="tpu_custom_call" | custom-call | bytes 115343360 | tf_op jit(solution)/shard_map/prepare/pallas_call | solution.py:140
  17.9 24.6 %all-to-all-done = bf16[16,40,1024]{2,1,0:T(8,128)(2,1)S(1)} async-done(((bf16[16,40,1024]{2,1,0:T(8,128)(2,1)}), bf16[16,40,1024]{2,1,0:T(8,128)(2,1)S(1)}, u32[]{:S(2)}, u32[]{:S(2)}) %all-to-all-start) | async-done | bytes 1310752 | tf_op jit(solution)/shard_map/all_to_all | solution.py:402
  42.5 0.0 copy-done.2
  42.6 0.0 copy-start.3
  42.6 1.2 %copy-done.3 = bf16[2,512,512]{2,1,0:T(8,128)(2,1)S(1)} copy-done((bf16[2,512,512]{2,1,0:T(8,128)(2,1)S(1)}, bf16[2,512,512]{2,1,0:T(8,128)(2,1)}, u32[]{:S(2)}) %copy-start.3) | copy-done | bytes 1048600
  43.8 0.0 copy-start.4
  43.8 1.0 copy-done.4
  44.8 0.0 copy-start.5
  44.8 1.6 %copy-done.5 = bf16[1024,1024]{1,0:T(8,128)(2,1)S(1)} copy-done((bf16[1024,1024]{1,0:T(8,128)(2,1)S(1)}, bf16[1024,1024]{1,0:T(8,128)(2,1)}, u32[]{:S(2)}) %copy-start.5) | copy-done | bytes 2097176
  46.4 0.0 copy-start.6
  46.4 1.6 %copy-done.6 = bf16[1024,1024]{1,0:T(8,128)(2,1)S(1)} copy-done((bf16[1024,1024]{1,0:T(8,128)(2,1)S(1)}, bf16[1024,1024]{1,0:T(8,128)(2,1)}, u32[]{:S(2)}) %copy-start.6) | copy-done | bytes 2097176
  48.0 7.5 %slot.1 = (bf16[512,1024]{1,0:T(8,128)(2,1)S(1)}, f32[256,1024]{1,0:T(8,128)S(1)}, bf16[256,1024]{1,0:T(8,128)(2,1)}) custom-call(s32[16]{0:T(128)S(1)} %copy-done, s32[16]{0:T(128)S(1)} %copy-done.2, s32[80]{0:T(128)S(1)} %get-tuple-element.14.owners, bf16[640,1024]{1,0:T(8,128)(2,1)S(1)} %bitcast.5, bf16[2,512,512]{2,1,0:T(8,128)(2,1)S(1)} %copy-done.3, ...), custom_call_target="tpu_custom_call" | custom-call | flops 4294967296 | bytes 8388608 | tf_op jit(solution)/shard_map/slot/pallas_call | solution.py:237
  55.5 0.2 collective-permute-start
  55.7 2.0 %collective-permute-done = bf16[256,1024]{1,0:T(8,128)(2,1)} collective-permute-done((bf16[256,1024]{1,0:T(8,128)(2,1)}, bf16[256,1024]{1,0:T(8,128)(2,1)}, u32[]{:S(2)}, u32[]{:S(2)}) %collective-permute-start) | collective-permute-done | bytes 524320 | tf_op jit(solution)/shard_map/ppermute | solution.py:360
  57.8 1.2 %convert_add_fusion = f32[256,1024]{1,0:T(8,128)S(1)} fusion(f32[256,1024]{1,0:T(8,128)S(1)} %get-tuple-element.17, bf16[256,1024]{1,0:T(8,128)(2,1)} %collective-permute-done), kind=kLoop, calls=%fused_computation.4 | loop fusion | flops 524288 | bytes 2621440 | tf_op jit(solution)/shard_map/add | solution.py:365
  59.0 0.1 collective-permute-start.1
  59.2 7.6 %collective-permute-done.1 = bf16[128,1024]{1,0:T(8,128)(2,1)S(1)} collective-permute-done((bf16[128,1024]{1,0:T(8,128)(2,1)S(1)}, bf16[128,1024]{1,0:T(8,128)(2,1)S(1)}, u32[]{:S(2)}, u32[]{:S(2)}) %collective-permute-start.1) | collective-permute-done | bytes 262176 | tf_op jit(solution)/shard_map/ppermute | solution.py:360
  66.8 0.1 convert_add_fusion.1
  66.9 0.4 collective-permute-start.4
  67.3 0.8 collective-permute-start.3
  68.1 1.5 %collective-permute-start.2 = (bf16[32,1024]{1,0:T(8,128)(2,1)S(1)}, bf16[32,1024]{1,0:T(8,128)(2,1)S(1)}, u32[]{:S(2)}, u32[]{:S(2)}) collective-permute-start(bf16[32,1024]{1,0:T(8,128)(2,1)S(1)} %get-tuple-element.28), channel_id=1, source_target_pairs={{0,4},{1,5},{2,6},{3,7},{4,0},{5,1},{6,2},{7,3},{8,12},{9,13},{10,... | collective-permute-start | bytes 196616 | tf_op jit(solution)/shard_map/ppermute | solution.py:360
  69.6 2.2 %pack.1 = bf16[16,40,1024]{2,1,0:T(8,128)(2,1)} custom-call(s32[16]{0:T(128)S(1)} %copy-done, s32[16]{0:T(128)S(1)} %copy-done.2, bf16[512,1024]{1,0:T(8,128)(2,1)S(1)} %get-tuple-element.16.term), custom_call_target="tpu_custom_call" | custom-call | bytes 3145728 | tf_op jit(solution)/shard_map/pack/pallas_call | solution.py:279
  71.8 0.3 collective-permute-done.4
  72.2 0.0 collective-permute-done.3
  72.2 1.1 collective-permute-done.2
  73.3 0.9 collective-permute-start.5
  74.2 3.4 %collective-permute-start.6 = (bf16[32,1024]{1,0:T(8,128)(2,1)S(1)}, bf16[32,1024]{1,0:T(8,128)(2,1)S(1)}, u32[]{:S(2)}, u32[]{:S(2)}) collective-permute-start(bf16[32,1024]{1,0:T(8,128)(2,1)S(1)} %multiply_convert_fusion), channel_id=1, source_target_pairs={{0,8},{1,9},{2,10},{3,11},{4,12},{5,13},{6,14},{7,15},{8,0},{9,1},... | collective-permute-start | bytes 196616 | tf_op jit(solution)/shard_map/ppermute | solution.py:360
  77.7 0.0 collective-permute-start.7
  77.7 7.5 %all-to-all-start.1 = ((bf16[16,40,1024]{2,1,0:T(8,128)(2,1)}), bf16[16,40,1024]{2,1,0:T(8,128)(2,1)S(1)}, u32[]{:S(2)}, u32[]{:S(2)}) async-start(bf16[16,40,1024]{2,1,0:T(8,128)(2,1)} %pack.1), calls=%async_computation.1 | async-start | bytes 2621440 | tf_op jit(solution)/shard_map/all_to_all | solution.py:409
  85.1 0.0 collective-permute-done.5
  85.2 0.0 collective-permute-done.6
  85.2 0.0 collective-permute-done.7
  85.3 0.3 collective-permute-start.8
  85.6 13.5 %collective-permute-done.8 = bf16[128,1024]{1,0:T(8,128)(2,1)S(1)} collective-permute-done((bf16[128,1024]{1,0:T(8,128)(2,1)S(1)}, bf16[128,1024]{1,0:T(8,128)(2,1)S(1)}, u32[]{:S(2)}, u32[]{:S(2)}) %collective-permute-start.8) | collective-permute-done | bytes 262176 | tf_op jit(solution)/shard_map/ppermute | solution.py:360
  99.1 0.1 broadcast_select_fusion.3
  99.3 2.6 %collective-permute-start.9 = (bf16[256,1024]{1,0:T(8,128)(2,1)S(1)}, bf16[256,1024]{1,0:T(8,128)(2,1)S(1)}, u32[]{:S(2)}, u32[]{:S(2)}) collective-permute-start(bf16[256,1024]{1,0:T(8,128)(2,1)S(1)} %pad_maximum_fusion.1), channel_id=1, source_target_pairs={{0,1},{1,0},{2,3},{3,2},{4,5},{5,4},{6,7},{7,6},{8,9},{9,8},{10,11... | collective-permute-start | bytes 1572872 | tf_op jit(solution)/shard_map/ppermute | solution.py:360
  101.9 1.5 %collective-permute-done.9 = bf16[256,1024]{1,0:T(8,128)(2,1)S(1)} collective-permute-done((bf16[256,1024]{1,0:T(8,128)(2,1)S(1)}, bf16[256,1024]{1,0:T(8,128)(2,1)S(1)}, u32[]{:S(2)}, u32[]{:S(2)}) %collective-permute-start.9) | collective-permute-done | bytes 524320 | tf_op jit(solution)/shard_map/ppermute | solution.py:360
  103.4 0.2 broadcast_select_fusion.1
  103.7 0.2 maximum_convert_fusion
  103.9 0.2 slice_bitcast_fusion.1
  104.1 1.5 %pad_maximum_fusion = f32[2,512,512]{2,1,0:T(8,128)} fusion(f32[1,512,512]{2,1,0:T(8,128)S(1)} %get-tuple-element.23, f32[1,512,512]{2,1,0:T(8,128)S(1)} %get-tuple-element.22), kind=kLoop, calls=%fused_computation | loop fusion | flops 524288 | bytes 4194304 | tf_op jit(solution)/shard_map/stack | solution.py:412
  105.6 10.1 %all-to-all-done.1.terms = bf16[16,40,1024]{2,1,0:T(8,128)(2,1)S(1)} async-done(((bf16[16,40,1024]{2,1,0:T(8,128)(2,1)}), bf16[16,40,1024]{2,1,0:T(8,128)(2,1)S(1)}, u32[]{:S(2)}, u32[]{:S(2)}) %all-to-all-start.1) | async-done | bytes 1310752 | tf_op jit(solution)/shard_map/all_to_all | solution.py:409
  115.7 4.2 %place.1 = f32[2,40,32768]{2,1,0:T(8,128)} custom-call(s32[16]{0:T(128)S(1)} %copy-done, s32[16]{0:T(128)S(1)} %copy-done.1, s32[80]{0:T(128)S(1)} %get-tuple-element.13.blocks, s32[80]{0:T(128)S(1)} %get-tuple-element.14.owners, bf16[16,40,1024]{2,1,0:T(8,128)(2,1)S(1)} %all-to-all-done.1.terms, ...), custom_call_target="tpu_custom_call", output_to_operand_aliasing={{}: (5, {})} | custom-call | bytes 6291456 | tf_op jit(solution)/shard_map/place/pallas_call | solution.py:334
  (7 shorter events, 0.2 us)
Async XLA Ops:
  5.2 6.7 %copy-start = (s32[16]{0:T(128)S(1)}, s32[16]{0:T(128)}, u32[]{:S(2)}) copy-start(s32[16]{0:T(128)} %dealing.9) | copy-start | bytes 196
  5.3 6.7 %copy-start.1 = (s32[16]{0:T(128)S(1)}, s32[16]{0:T(128)}, u32[]{:S(2)}) copy-start(s32[16]{0:T(128)} %cols.5) | copy-start | bytes 196
  5.3 37.3 %copy-start.2 = (s32[16]{0:T(128)S(1)}, s32[16]{0:T(128)}, u32[]{:S(2)}) copy-start(s32[16]{0:T(128)} %rows.3) | copy-start | bytes 196
  5.3 37.3 %all-to-all-start = ((bf16[16,40,1024]{2,1,0:T(8,128)(2,1)}), bf16[16,40,1024]{2,1,0:T(8,128)(2,1)S(1)}, u32[]{:S(2)}, u32[]{:S(2)}) async-start(bf16[16,40,1024]{2,1,0:T(8,128)(2,1)} %get-tuple-element.15), calls=%async_computation | async-start | bytes 2621440 | tf_op jit(solution)/shard_map/all_to_all | solution.py:402
  42.6 1.2 %copy-start.3 = (bf16[2,512,512]{2,1,0:T(8,128)(2,1)S(1)}, bf16[2,512,512]{2,1,0:T(8,128)(2,1)}, u32[]{:S(2)}) copy-start(bf16[2,512,512]{2,1,0:T(8,128)(2,1)} %probe.1) | copy-start | bytes 3145732
  43.8 1.0 copy-start.4
  44.8 1.6 %copy-start.5 = (bf16[1024,1024]{1,0:T(8,128)(2,1)S(1)}, bf16[1024,1024]{1,0:T(8,128)(2,1)}, u32[]{:S(2)}) copy-start(bf16[1024,1024]{1,0:T(8,128)(2,1)} %constant.81.clone.right) | copy-start | bytes 6291460
  46.4 1.6 %copy-start.6 = (bf16[1024,1024]{1,0:T(8,128)(2,1)S(1)}, bf16[1024,1024]{1,0:T(8,128)(2,1)}, u32[]{:S(2)}) copy-start(bf16[1024,1024]{1,0:T(8,128)(2,1)} %constant.82.clone.left) | copy-start | bytes 6291460
  55.5 2.3 %collective-permute-start = (bf16[256,1024]{1,0:T(8,128)(2,1)}, bf16[256,1024]{1,0:T(8,128)(2,1)}, u32[]{:S(2)}, u32[]{:S(2)}) collective-permute-start(bf16[256,1024]{1,0:T(8,128)(2,1)} %get-tuple-element.18), channel_id=1, source_target_pairs={{0,1},{1,0},{2,3},{3,2},{4,5},{5,4},{6,7},{7,6},{8,9},{9,8},{10,11... | collective-permute-start | bytes 1572872 | tf_op jit(solution)/shard_map/ppermute | solution.py:360
  59.0 7.8 %collective-permute-start.1 = (bf16[128,1024]{1,0:T(8,128)(2,1)S(1)}, bf16[128,1024]{1,0:T(8,128)(2,1)S(1)}, u32[]{:S(2)}, u32[]{:S(2)}) collective-permute-start(bf16[128,1024]{1,0:T(8,128)(2,1)S(1)} %dynamic-slice_convert_fusion), channel_id=1, source_target_pairs={{0,2},{1,3},{2,0},{3,1},{4,6},{5,7},{6,4},{7,5},{8,10},{9,11},{10,... | collective-permute-start | bytes 786440 | tf_op jit(solution)/shard_map/ppermute | solution.py:360
  66.9 5.2 %collective-permute-start.4 = (bf16[32,1024]{1,0:T(8,128)(2,1)S(1)}, bf16[32,1024]{1,0:T(8,128)(2,1)S(1)}, u32[]{:S(2)}, u32[]{:S(2)}) collective-permute-start(bf16[32,1024]{1,0:T(8,128)(2,1)S(1)} %get-tuple-element.29), channel_id=1, source_target_pairs={{0,12},{1,13},{2,14},{3,15},{4,8},{5,9},{6,10},{7,11},{8,4},{9,5},... | collective-permute-start | bytes 196616 | tf_op jit(solution)/shard_map/ppermute | solution.py:360
  67.3 4.8 %collective-permute-start.3 = (bf16[32,1024]{1,0:T(8,128)(2,1)S(1)}, bf16[32,1024]{1,0:T(8,128)(2,1)S(1)}, u32[]{:S(2)}, u32[]{:S(2)}) collective-permute-start(bf16[32,1024]{1,0:T(8,128)(2,1)S(1)} %get-tuple-element.30), channel_id=1, source_target_pairs={{0,8},{1,9},{2,10},{3,11},{4,12},{5,13},{6,14},{7,15},{8,0},{9,1},... | collective-permute-start | bytes 196616 | tf_op jit(solution)/shard_map/ppermute | solution.py:360
  68.1 5.1 %collective-permute-start.2 = (bf16[32,1024]{1,0:T(8,128)(2,1)S(1)}, bf16[32,1024]{1,0:T(8,128)(2,1)S(1)}, u32[]{:S(2)}, u32[]{:S(2)}) collective-permute-start(bf16[32,1024]{1,0:T(8,128)(2,1)S(1)} %get-tuple-element.28), channel_id=1, source_target_pairs={{0,4},{1,5},{2,6},{3,7},{4,0},{5,1},{6,2},{7,3},{8,12},{9,13},{10,... | collective-permute-start | bytes 196616 | tf_op jit(solution)/shard_map/ppermute | solution.py:360
  73.3 11.8 %collective-permute-start.5 = (bf16[32,1024]{1,0:T(8,128)(2,1)S(1)}, bf16[32,1024]{1,0:T(8,128)(2,1)S(1)}, u32[]{:S(2)}, u32[]{:S(2)}) collective-permute-start(bf16[32,1024]{1,0:T(8,128)(2,1)S(1)} %multiply_convert_fusion), channel_id=1, source_target_pairs={{0,12},{1,13},{2,14},{3,15},{4,8},{5,9},{6,10},{7,11},{8,4},{9,5},... | collective-permute-start | bytes 196616 | tf_op jit(solution)/shard_map/ppermute | solution.py:360
  74.2 10.9 %collective-permute-start.6 = (bf16[32,1024]{1,0:T(8,128)(2,1)S(1)}, bf16[32,1024]{1,0:T(8,128)(2,1)S(1)}, u32[]{:S(2)}, u32[]{:S(2)}) collective-permute-start(bf16[32,1024]{1,0:T(8,128)(2,1)S(1)} %multiply_convert_fusion), channel_id=1, source_target_pairs={{0,8},{1,9},{2,10},{3,11},{4,12},{5,13},{6,14},{7,15},{8,0},{9,1},... | collective-permute-start | bytes 196616 | tf_op jit(solution)/shard_map/ppermute | solution.py:360
  77.7 7.5 %collective-permute-start.7 = (bf16[32,1024]{1,0:T(8,128)(2,1)S(1)}, bf16[32,1024]{1,0:T(8,128)(2,1)S(1)}, u32[]{:S(2)}, u32[]{:S(2)}) collective-permute-start(bf16[32,1024]{1,0:T(8,128)(2,1)S(1)} %multiply_convert_fusion), channel_id=1, source_target_pairs={{0,4},{1,5},{2,6},{3,7},{4,0},{5,1},{6,2},{7,3},{8,12},{9,13},{10,... | collective-permute-start | bytes 196616 | tf_op jit(solution)/shard_map/ppermute | solution.py:360
  77.7 38.1 %all-to-all-start.1 = ((bf16[16,40,1024]{2,1,0:T(8,128)(2,1)}), bf16[16,40,1024]{2,1,0:T(8,128)(2,1)S(1)}, u32[]{:S(2)}, u32[]{:S(2)}) async-start(bf16[16,40,1024]{2,1,0:T(8,128)(2,1)} %pack.1), calls=%async_computation.1 | async-start | bytes 2621440 | tf_op jit(solution)/shard_map/all_to_all | solution.py:409
  85.3 13.9 %collective-permute-start.8 = (bf16[128,1024]{1,0:T(8,128)(2,1)S(1)}, bf16[128,1024]{1,0:T(8,128)(2,1)S(1)}, u32[]{:S(2)}, u32[]{:S(2)}) collective-permute-start(bf16[128,1024]{1,0:T(8,128)(2,1)S(1)} %pad_maximum_fusion.2), channel_id=1, source_target_pairs={{0,2},{1,3},{2,0},{3,1},{4,6},{5,7},{6,4},{7,5},{8,10},{9,11},{10,... | collective-permute-start | bytes 786440 | tf_op jit(solution)/shard_map/ppermute | solution.py:360
  99.3 4.2 %collective-permute-start.9 = (bf16[256,1024]{1,0:T(8,128)(2,1)S(1)}, bf16[256,1024]{1,0:T(8,128)(2,1)S(1)}, u32[]{:S(2)}, u32[]{:S(2)}) collective-permute-start(bf16[256,1024]{1,0:T(8,128)(2,1)S(1)} %pad_maximum_fusion.1), channel_id=1, source_target_pairs={{0,1},{1,0},{2,3},{3,2},{4,5},{5,4},{6,7},{7,6},{8,9},{9,8},{10,11... | collective-permute-start | bytes 1572872 | tf_op jit(solution)/shard_map/ppermute | solution.py:360

commit v11 on v10

--- a/solution.py
+++ b/solution.py
@@ -69,13 +69,13 @@
         shift = lax.rem(LANES - lax.rem(offset, LANES), LANES)
         for part in range(2):
             turned = [
-                pltpu.roll(held[slot, part, :, b * LANES : (b + 1) * LANES], shift, 1)
+                pltpu.roll(held[slot, part, :, b * LANES : (b + 1) * LANES].astype(out.dtype), shift, 1)
                 for b in range(span // LANES)
             ]
             for b in range(order // LANES):
                 first = part * order + b * LANES
                 cells = jnp.where(lane < LANES - offset, turned[b], turned[b + 1])
-                out[slot, :, first : first + LANES] = cells.astype(out.dtype)
+                out[slot, :, first : first + LANES] = cells
 
 
 def fetch_windows(tile, dealing, cols, order):
@@ -100,14 +100,34 @@
     )(dealing, cols, tile)
 
 
-def prepare_kernel(order, dealing, cols, token, empty, blocks, owners, table, zeros, sems):
+def stock_places(stock, order):
+    return (
+        stock.at[0:order, 0:order],
+        stock.at[0:order, order : 2 * order],
+        stock.at[order : 3 * order, :],
+        stock.at[3 * order : 4 * order, 0:order],
+        stock.at[4 * order : 6 * order, :],
+    )
+
+
+def prepare_kernel(
+    order, dealing, cols, token, right, left, probe, measured,
+    empty, blocks, owners, stock,
+    table, zeros, sems, stock_sems,
+):
     del token
+    places = stock_places(stock, order)
+    sources = (probe.at[0], probe.at[1], right, measured.at[0], left)
+    fills = []
+    for k, (source, place) in enumerate(zip(sources, places)):
+        fill = pltpu.make_async_copy(source, place, stock_sems.at[k])
+        fill.start()
+        fills.append(fill)
     count = (order + LANES) // LANES
     slots = dealing.shape[0]
     tile_cols = empty.shape[2]
     width = zeros.shape[2]
     zeros[...] = jnp.zeros_like(zeros)
-    fills = []
     for b in range(tile_cols // width):
         fill = pltpu.make_async_copy(zeros, empty.at[:, :, b * width : (b + 1) * width], sems.at[b])
         fill.start()
@@ -133,7 +153,9 @@
         fill.wait()
 
 
-def prepare(dealing, cols, token, tile_shape, order):
+def prepare(dealing, cols, token, probe, measured, tile_shape):
+    order = probe.shape[1]
+    right, left = dft_tables(order)
     slots = dealing.shape[0]
     numbers = slots * (order + LANES) // LANES
     fill_cols = 2048
@@ -143,27 +165,36 @@
             jax.ShapeDtypeStruct(tile_shape, jnp.float32),
             jax.ShapeDtypeStruct((numbers,), jnp.int32),
             jax.ShapeDtypeStruct((numbers,), jnp.int32),
+            jax.ShapeDtypeStruct((28 * order, 2 * order), jnp.bfloat16),
         ),
-        in_specs=[SMEM, SMEM, SMEM],
-        out_specs=(ANY, SMEM, SMEM),
+        in_specs=[SMEM, SMEM, SMEM, ANY, ANY, ANY, ANY],
+        out_specs=(ANY, SMEM, SMEM, ANY),
         scratch_shapes=[
             pltpu.SMEM((tile_shape[2] // LANES,), jnp.int32),
             pltpu.VMEM(tile_shape[:2] + (fill_cols,), jnp.float32),
             pltpu.SemaphoreType.DMA((tile_shape[2] // fill_cols,)),
+            pltpu.SemaphoreType.DMA((5,)),
         ],
         compiler_params=pltpu.CompilerParams(vmem_limit_bytes=8 * 2**20),
         cost_estimate=pl.CostEstimate(flops=0, bytes_accessed=110 * 2**20, transcendentals=0),
         name="prepare",
-    )(dealing, cols, token)
+    )(dealing, cols, token, jnp.asarray(right), jnp.asarray(left), probe, measured)
 
 
 def slot_kernel(
-    dealing, rows, owners, cells, probe, measured, right, left,
+    dealing, rows, owners, cells, stock,
     term, kept, sent,
-    wide, patch, wave, half, resid, turned, mine,
+    wide, patch, wave, half, resid, turned, mine, probe, right, measured, left, sems,
 ):
     del owners
-    order = probe.shape[1]
+    order = term.shape[0]
+    targets = (probe.at[0], probe.at[1], right, measured, left)
+    loads = [
+        pltpu.make_async_copy(source, target, sems.at[k])
+        for k, (source, target) in enumerate(zip(stock_places(stock, order), targets))
+    ]
+    for load in loads:
+        load.start()
     total_rows = cells.shape[0]
     me = lax.axis_index("row")
     first_row = rows[dealing[me]]
@@ -172,6 +203,9 @@
 
     wide[0:total_rows, :] = cells[...].astype(jnp.float32)
     wide[total_rows:, :] = jnp.zeros((SUBLANES, 2 * order), jnp.float32)
+    loads[0].wait()
+    loads[1].wait()
+
     @pl.loop(0, order // step)
     def _(i):
         place = pl.ds(pl.multiple_of(i * step, step), step)
@@ -186,11 +220,14 @@
     def dot(a, b):
         return jnp.dot(a, b, preferred_element_type=jnp.float32)
 
+    loads[2].wait()
     for first in range(0, order, tile):
         here = slice(first, first + tile)
         there = slice(order + first, order + first + tile)
         half[:order, here] = dot(wave[...], right[:, here]).astype(half.dtype)
         half[order:, here] = dot(wave[...], right[:, there]).astype(half.dtype)
+    loads[3].wait()
+    loads[4].wait()
     for first in range(0, order, tile):
         here = slice(first, first + tile)
         there = slice(order + first, order + first + tile)
@@ -199,7 +236,7 @@
             real = dot(left[line, :], half[:, here])
             imag = dot(left[order + top : order + top + tile, :], half[:, here])
             inverse = jnp.minimum(lax.rsqrt(real * real + imag * imag), 1.0 / MAG_FLOOR)
-            shrink = 1.0 - measured[0, line, here].astype(jnp.float32) * inverse
+            shrink = 1.0 - measured[line, here].astype(jnp.float32) * inverse
             resid[line, here] = (real * shrink).astype(resid.dtype)
             resid[line, there] = (imag * shrink).astype(resid.dtype)
     for first in range(0, order, tile):
@@ -228,11 +265,9 @@
     kept[...] = mine[pl.ds(pl.multiple_of(side * count, count), count), :]
     sent[...] = mine[pl.ds(pl.multiple_of((1 - side) * count, count), count), :].astype(sent.dtype)
 
-def slot_terms(cells, probe, measured, dealing, rows, owners):
-    order = probe.shape[1]
+def slot_terms(cells, stock, dealing, rows, owners, order):
     total_rows = cells.shape[0]
     wide_cols = 2 * order
-    right, left = dft_tables(order)
     bf16, f32 = jnp.bfloat16, jnp.float32
     return pl.pallas_call(
         slot_kernel,
@@ -241,7 +276,7 @@
             jax.ShapeDtypeStruct((order // 2, wide_cols), f32),
             jax.ShapeDtypeStruct((order // 2, wide_cols), bf16),
         ),
-        in_specs=[SMEM, SMEM, SMEM, VMEM, VMEM, VMEM, VMEM, VMEM],
+        in_specs=[SMEM, SMEM, SMEM, VMEM, ANY],
         out_specs=(VMEM,) * 3,
         scratch_shapes=[
             pltpu.VMEM((total_rows + SUBLANES, wide_cols), f32),
@@ -251,13 +286,18 @@
             pltpu.VMEM((order, wide_cols), bf16),
             pltpu.VMEM((wide_cols, order), bf16),
             pltpu.VMEM((order, wide_cols), f32),
+            pltpu.VMEM((2, order, order), bf16),
+            pltpu.VMEM((wide_cols, wide_cols), bf16),
+            pltpu.VMEM((order, order), bf16),
+            pltpu.VMEM((wide_cols, wide_cols), bf16),
+            pltpu.SemaphoreType.DMA((5,)),
         ],
         compiler_params=pltpu.CompilerParams(vmem_limit_bytes=40 * 2**20),
         cost_estimate=pl.CostEstimate(
             flops=8 * 2 * order**3 * 2, bytes_accessed=8 * 2**20, transcendentals=order * order
         ),
         name="slot",
-    )(dealing, rows, owners, cells, probe, measured, jnp.asarray(right), jnp.asarray(left))
+    )(dealing, rows, owners, cells, stock)
 
 
 def pack_kernel(reach, own_rows, dealing, rows, term, out, padded):
@@ -304,7 +344,7 @@
             turned = []
             for b in range(count - 1):
                 first = part * order + b * LANES
-                turned.append(pltpu.roll(terms[slot, :, first : first + LANES].astype(jnp.float32), shift, 1))
+                turned.append(pltpu.roll(terms[slot, :, first : first + LANES], shift, 1).astype(jnp.float32))
             for b in range(count):
                 before = turned[b - 1] if b else nothing
                 after = turned[b] if b < count - 1 else nothing
@@ -361,22 +401,22 @@
 
 
 def sum_probe(kept, sent, devices):
-    me = lax.axis_index("row")
-    total = kept + swap(sent, 1, devices).astype(jnp.float32)
-    for stride, radix in strides(devices)[1:]:
-        digit = me // stride % radix
-        count = total.shape[0] // radix
-        own = lax.dynamic_slice_in_dim(total, digit * count, count)
-        for k in range(1, radix):
-            share = lax.dynamic_slice_in_dim(total, lax.bitwise_xor(digit, k) * count, count)
-            own = own + swap(share.astype(jnp.bfloat16), k * stride, devices).astype(jnp.float32)
-        total = own
-    return total
+    chips = devices // 2
+    total = (kept + swap(sent, 1, devices).astype(jnp.float32)).astype(jnp.bfloat16)
+    groups = [list(range(core, devices, 2)) for core in range(2)]
+    count = total.shape[0] // chips
+    shares = lax.all_to_all(
+        total.reshape(chips, count, -1), "row", split_axis=0, concat_axis=0, tiled=True, axis_index_groups=groups
+    )
+    return jnp.sum(shares.astype(jnp.float32), axis=0)
 
 
 def join(whole, devices):
     me = lax.axis_index("row")
-    for stride, radix in reversed(strides(devices)):
+    rows, width = whole.shape
+    steps = strides(devices)
+    axes = [*range(len(steps) - 1), 0]
+    for axis, (stride, radix) in zip(axes, reversed(steps)):
         digit = me // stride % radix
         shares = [whole] + [swap(whole, k * stride, devices) for k in range(1, radix)]
         pieces = []
@@ -385,8 +425,8 @@
             for k in range(1, radix):
                 piece = jnp.where(lax.bitwise_xor(digit, k) == j, shares[k], piece)
             pieces.append(piece)
-        whole = jnp.concatenate(pieces, axis=0)
-    return whole
+        whole = jnp.stack(pieces, axis=axis)
+    return whole.reshape(devices * rows, width)
 
 
 def body(object_field, probe, amplitude, row_offsets, col_offsets, dealing):
@@ -401,8 +441,10 @@
     pieces, token = fetch_windows(object_field, dealing, col_offsets, order)
     strips = lax.all_to_all(pieces, "row", split_axis=0, concat_axis=0, tiled=True)
     cells = strips[:, :own_rows].reshape(total_rows, 2 * order)
-    empty, blocks, owners = prepare(dealing, col_offsets, token, object_field.shape, order)
-    term, kept, sent = slot_terms(cells, probe, amplitude, dealing, row_offsets, owners)
+    empty, blocks, owners, stock = prepare(
+        dealing, col_offsets, token, probe, amplitude, object_field.shape
+    )
+    term, kept, sent = slot_terms(cells, stock, dealing, row_offsets, owners, order)
     total = sum_probe(kept, sent, devices)
     terms = pack_rows(term, dealing, row_offsets, devices, own_rows, tile_rows)
     terms, total = lax.optimization_barrier((terms, total))

time: 120 us -> 117 us (0.975)
  waiting for transfers between devices: 60.9 us -> 47.2 us
  local copies, waits for them, and re-layouts: 5.73 us -> 13.7 us
  starting transfers between devices: 24.5 us -> 25.9 us
    all_to_all x1, waiting for transfers between devices: 24.6 us -> 10.5 us  [body(): lax.all_to_all(pieces, 'row', split_axis=0, concat_axis=0, tiled=True)]
    all_to_all x0 -> x1, waiting for transfers between devices: none -> 9.78 us  [sum_probe(): lax.all_to_all(total.reshape(chips, count, -1), 'row', split_axis=0, conc...]
    ppermute x10 -> x6, waiting for transfers between devices: 26.1 us -> 16.7 us  [swap(): return lax.ppermute(x, 'row', [(d, d ^ distance) for d in range(devices)])]
    unnamed x14 -> x16, local copies, waits for them, and re-layouts: 5.47 us -> 13.6 us
    all_to_all x0 -> x1, starting transfers between devices: none -> 4.44 us  [sum_probe(): lax.all_to_all(total.reshape(chips, count, -1), 'row', split_axis=0, conc...]
    ppermute x10 -> x6, starting transfers between devices: 10.3 us -> 7.55 us  [swap(): return lax.ppermute(x, 'row', [(d, d ^ distance) for d in range(devices)])]
    add x3 -> x0, other arithmetic: 1.31 us -> none  [the longest x1 1.22 us: sum_probe(): total = kept + swap(sent, 1, devices).astype(jnp.float32)]
  transfers between devices with their start and end apart: 12 -> 9, of which waited for: 8 -> 6; matrix products, arithmetic and copies ran while one was open for 2% -> 2% of each run, Pallas kernels for 7% -> 7%
where the time goes in v11:
time: 117 us; the launch traced here: 116 us
  waiting for transfers between devices  47.2 us (40%)
  starting transfers between devices  25.9 us (22%)
  Pallas kernels  25.5 us (22%)
  local copies, waits for them, and re-layouts  13.7 us (12%)
  other arithmetic  3.2 us (3%)
    ppermute x6, waiting for transfers between devices, swap(): return lax.ppermute(x, 'row', [(d, d ^ distance) for d in range(devices)])  16.7 us
    unnamed x16, local copies, waits for them, and re-layouts  13.6 us
    all_to_all x1, waiting for transfers between devices, body(): lax.all_to_all(pieces, 'row', split_axis=0, concat_axis=0, tiled=True)  10.5 us
    all_to_all x1, waiting for transfers between devices, body(): lax.all_to_all(terms, 'row', split_axis=0, concat_axis=0, tiled=True)  10.1 us
    all_to_all x1, waiting for transfers between devices, sum_probe(): lax.all_to_all(total.reshape(chips, count, -1), 'row', split_axis=0, conc...  9.78 us
    pallas_call x1, Pallas kernels, slot_terms(): pl.pallas_call(slot_kernel, out_shape=(jax.ShapeDtypeStruct((order, wide_...  7.93 us
    ppermute x6, starting transfers between devices, swap(): return lax.ppermute(x, 'row', [(d, d ^ distance) for d in range(devices)])  7.55 us
    all_to_all x1, starting transfers between devices, body(): lax.all_to_all(terms, 'row', split_axis=0, concat_axis=0, tiled=True)  7.2 us
  transfers between devices with their start and end apart: 9, of which 6 were waited for; matrix products, arithmetic and copies ran while one was open for 2% of the time, Pallas kernels for 7%

profile of v11, /device:TPU:15, one launch (start us, length us, event | category | flops | bytes accessed | tf_op | source)
XLA Modules:
  0.0 116.3 jit_solution(4859254145293712596)
XLA Ops:
  0.6 4.7 %fetch.1 = (bf16[16,40,1024]{2,1,0:T(8,128)(2,1)}, s32[1]{0:T(128)}) custom-call(s32[16]{0:T(128)} %dealing.9, s32[16]{0:T(128)} %cols.5, f32[2,40,32768]{2,1,0:T(8,128)} %tile.1), custom_call_target="tpu_custom_call" | custom-call | bytes 6291456 | tf_op jit(solution)/shard_map/fetch/pallas_call | solution.py:85
  5.3 0.0 copy-start.1
  5.3 0.0 copy-start.5
  5.3 0.0 copy-start.6
  5.3 6.7 %all-to-all-start = ((bf16[16,40,1024]{2,1,0:T(8,128)(2,1)}), bf16[16,40,1024]{2,1,0:T(8,128)(2,1)S(1)}, u32[]{:S(2)}, u32[]{:S(2)}) async-start(bf16[16,40,1024]{2,1,0:T(8,128)(2,1)} %get-tuple-element.16), calls=%async_computation | async-start | bytes 2621440 | tf_op jit(solution)/shard_map/all_to_all | solution.py:442
  12.0 0.0 copy-done.1
  12.0 0.0 copy-done.5
  12.1 0.0 copy-done.6
  12.1 0.0 copy-start.2
  12.1 1.6 %copy-done.2 = bf16[1024,1024]{1,0:T(8,128)(2,1)S(1)} copy-done((bf16[1024,1024]{1,0:T(8,128)(2,1)S(1)}, bf16[1024,1024]{1,0:T(8,128)(2,1)}, u32[]{:S(2)}) %copy-start.2) | copy-done | bytes 2097176
  13.7 0.0 copy-start.3
  13.7 1.2 %copy-done.3 = bf16[2,512,512]{2,1,0:T(8,128)(2,1)S(1)} copy-done((bf16[2,512,512]{2,1,0:T(8,128)(2,1)S(1)}, bf16[2,512,512]{2,1,0:T(8,128)(2,1)}, u32[]{:S(2)}) %copy-start.3) | copy-done | bytes 1048600
  14.9 0.0 copy-start.4
  14.9 1.0 copy-done.4
  15.9 0.0 copy-start.7
  15.9 6.4 %prepare.1 = (f32[2,40,32768]{2,1,0:T(8,128)}, s32[80]{0:T(128)S(1)}, s32[80]{0:T(128)S(1)}, bf16[14336,1024]{1,0:T(8,128)(2,1)S(1)}) custom-call(s32[16]{0:T(128)S(1)} %copy-done.5, s32[16]{0:T(128)S(1)} %copy-done.6, s32[1]{0:T(128)} %get-tuple-element.13.token, bf16[1024,1024]{1,0:T(8,128)(2,1)S(1)} %copy-done.1, bf16[1024,1024]{1,0:T(8,128)(2,1)S(1)} %copy-done.2, ...), custom_call_target="tpu_custom_call" | custom-call | bytes 115343360 | tf_op jit(solution)/shard_map/prepare/pallas_call | solution.py:162
  22.4 0.0 copy-start
  22.4 9.7 %copy-done = bf16[14336,1024]{1,0:T(8,128)(2,1)} copy-done((bf16[14336,1024]{1,0:T(8,128)(2,1)}, bf16[14336,1024]{1,0:T(8,128)(2,1)S(1)}, u32[]{:S(2)}) %copy-start) | copy-done | bytes 29360152
  32.1 10.5 %all-to-all-done = bf16[16,40,1024]{2,1,0:T(8,128)(2,1)S(1)} async-done(((bf16[16,40,1024]{2,1,0:T(8,128)(2,1)}), bf16[16,40,1024]{2,1,0:T(8,128)(2,1)S(1)}, u32[]{:S(2)}, u32[]{:S(2)}) %all-to-all-start) | async-done | bytes 1310752 | tf_op jit(solution)/shard_map/all_to_all | solution.py:442
  42.6 0.0 copy-done.7
  42.6 7.9 %slot.1 = (bf16[512,1024]{1,0:T(8,128)(2,1)S(1)}, f32[256,1024]{1,0:T(8,128)S(1)}, bf16[256,1024]{1,0:T(8,128)(2,1)S(1)}) custom-call(s32[16]{0:T(128)S(1)} %copy-done.5, s32[16]{0:T(128)S(1)} %copy-done.7, s32[80]{0:T(128)S(1)} %get-tuple-element.15.owners, bf16[640,1024]{1,0:T(8,128)(2,1)S(1)} %bitcast.27, bf16[14336,1024]{1,0:T(8,128)(2,1)} %copy-done), custom_call_target="tpu_custom_call" | custom-call | flops 4294967296 | bytes 8388608 | tf_op jit(solution)/shard_map/slot/pallas_call | solution.py:272
  50.5 0.3 collective-permute-start
  50.8 1.7 %collective-permute-done = bf16[256,1024]{1,0:T(8,128)(2,1)S(1)} collective-permute-done((bf16[256,1024]{1,0:T(8,128)(2,1)S(1)}, bf16[256,1024]{1,0:T(8,128)(2,1)S(1)}, u32[]{:S(2)}, u32[]{:S(2)}) %collective-permute-start) | collective-permute-done | bytes 524320 | tf_op jit(solution)/shard_map/ppermute | solution.py:400
  52.5 1.0 add_convert_fusion
  53.5 4.4 %all-to-all-start.1 = ((bf16[8,32,1024]{2,1,0:T(8,128)(2,1)}), bf16[8,32,1024]{2,1,0:T(8,128)(2,1)S(1)}, u32[]{:S(2)}, u32[]{:S(2)}) async-start(bf16[8,32,1024]{2,1,0:T(8,128)(2,1)} %bitcast.1), calls=%async_computation.1 | async-start | bytes 1048576 | tf_op jit(solution)/shard_map/all_to_all | solution.py:408
  57.9 2.2 %pack.1 = bf16[16,40,1024]{2,1,0:T(8,128)(2,1)} custom-call(s32[16]{0:T(128)S(1)} %copy-done.5, s32[16]{0:T(128)S(1)} %copy-done.7, bf16[512,1024]{1,0:T(8,128)(2,1)S(1)} %get-tuple-element.18.term), custom_call_target="tpu_custom_call" | custom-call | bytes 3145728 | tf_op jit(solution)/shard_map/pack/pallas_call | solution.py:319
  60.1 9.8 %all-to-all-done.1 = bf16[8,32,1024]{2,1,0:T(8,128)(2,1)S(1)} async-done(((bf16[8,32,1024]{2,1,0:T(8,128)(2,1)}), bf16[8,32,1024]{2,1,0:T(8,128)(2,1)S(1)}, u32[]{:S(2)}, u32[]{:S(2)}) %all-to-all-start.1) | async-done | bytes 524320 | tf_op jit(solution)/shard_map/all_to_all | solution.py:408
  69.9 0.1 convert_reduce_fusion
  70.0 0.4 collective-permute-start.1
  70.4 3.9 %collective-permute-start.2 = (bf16[32,1024]{1,0:T(8,128)(2,1)S(1)}, bf16[32,1024]{1,0:T(8,128)(2,1)S(1)}, u32[]{:S(2)}, u32[]{:S(2)}) collective-permute-start(bf16[32,1024]{1,0:T(8,128)(2,1)S(1)} %multiply_convert_fusion), channel_id=1, source_target_pairs={{0,8},{1,9},{2,10},{3,11},{4,12},{5,13},{6,14},{7,15},{8,0},{9,1},... | collective-permute-start | bytes 196616 | tf_op jit(solution)/shard_map/ppermute | solution.py:400
  74.3 0.0 collective-permute-start.3
  74.3 7.2 %all-to-all-start.2 = ((bf16[16,40,1024]{2,1,0:T(8,128)(2,1)}), bf16[16,40,1024]{2,1,0:T(8,128)(2,1)S(1)}, u32[]{:S(2)}, u32[]{:S(2)}) async-start(bf16[16,40,1024]{2,1,0:T(8,128)(2,1)} %pack.1), calls=%async_computation.2 | async-start | bytes 2621440 | tf_op jit(solution)/shard_map/all_to_all | solution.py:451
  81.5 0.0 collective-permute-done.1
  81.5 0.0 collective-permute-done.2
  81.5 0.0 collective-permute-done.3
  81.6 0.3 collective-permute-start.4
  82.0 13.5 %collective-permute-done.4 = bf16[4,32,1024]{2,1,0:T(8,128)(2,1)S(1)} collective-permute-done((bf16[4,32,1024]{2,1,0:T(8,128)(2,1)S(1)}, bf16[4,32,1024]{2,1,0:T(8,128)(2,1)S(1)}, u32[]{:S(2)}, u32[]{:S(2)}) %collective-permute-start.4) | collective-permute-done | bytes 262176 | tf_op jit(solution)/shard_map/ppermute | solution.py:400
  95.5 0.1 select_bitcast_fusion.3
  95.5 0.1 pad_maximum_fusion.2
  95.6 2.6 %collective-permute-start.5 = (bf16[4,2,32,1024]{3,2,1,0:T(8,128)(2,1)S(1)}, bf16[4,2,32,1024]{3,2,1,0:T(8,128)(2,1)S(1)}, u32[]{:S(2)}, u32[]{:S(2)}) collective-permute-start(bf16[4,2,32,1024]{3,2,1,0:T(8,128)(2,1)S(1)} %pad_maximum_fusion.2), channel_id=1, source_target_pairs={{0,1},{1,0},{2,3},{3,2},{4,5},{5,4},{6,7},{7,6},{8,9},{9,8},{10,11... | collective-permute-start | bytes 1572872 | tf_op jit(solution)/shard_map/ppermute | solution.py:400
  98.2 1.5 %collective-permute-done.5 = bf16[4,2,32,1024]{3,2,1,0:T(8,128)(2,1)S(1)} collective-permute-done((bf16[4,2,32,1024]{3,2,1,0:T(8,128)(2,1)S(1)}, bf16[4,2,32,1024]{3,2,1,0:T(8,128)(2,1)S(1)}, u32[]{:S(2)}, u32[]{:S(2)}) %collective-permute-start.5) | collective-permute-done | bytes 524320 | tf_op jit(solution)/shard_map/ppermute | solution.py:400
  99.7 0.1 select_bitcast_fusion.1
  99.8 0.1 pad_maximum_fusion.1
  99.9 0.3 bitcast_convert_fusion
  100.2 0.2 slice_bitcast_fusion.1
  100.4 1.5 %pad_maximum_fusion = f32[2,512,512]{2,1,0:T(8,128)} fusion(f32[1,512,512]{2,1,0:T(8,128)S(1)} %get-tuple-element.25, f32[1,512,512]{2,1,0:T(8,128)S(1)} %get-tuple-element.24), kind=kLoop, calls=%fused_computation | loop fusion | flops 524288 | bytes 4194304 | tf_op jit(solution)/shard_map/stack | solution.py:454
  101.9 10.1 %all-to-all-done.2.terms = bf16[16,40,1024]{2,1,0:T(8,128)(2,1)S(1)} async-done(((bf16[16,40,1024]{2,1,0:T(8,128)(2,1)}), bf16[16,40,1024]{2,1,0:T(8,128)(2,1)S(1)}, u32[]{:S(2)}, u32[]{:S(2)}) %all-to-all-start.2) | async-done | bytes 1310752 | tf_op jit(solution)/shard_map/all_to_all | solution.py:451
  112.1 4.2 %place.1 = f32[2,40,32768]{2,1,0:T(8,128)} custom-call(s32[16]{0:T(128)S(1)} %copy-done.5, s32[16]{0:T(128)S(1)} %copy-done.6, s32[80]{0:T(128)S(1)} %get-tuple-element.14.blocks, s32[80]{0:T(128)S(1)} %get-tuple-element.15.owners, bf16[16,40,1024]{2,1,0:T(8,128)(2,1)S(1)} %all-to-all-done.2.terms, ...), custom_call_target="tpu_custom_call", output_to_operand_aliasing={{}: (5, {})} | custom-call | bytes 6291456 | tf_op jit(solution)/shard_map/place/pallas_call | solution.py:374
  (3 shorter events, 0.1 us)
Async XLA Ops:
  5.3 6.7 %copy-start.1 = (bf16[1024,1024]{1,0:T(8,128)(2,1)S(1)}, bf16[1024,1024]{1,0:T(8,128)(2,1)}, u32[]{:S(2)}) copy-start(bf16[1024,1024]{1,0:T(8,128)(2,1)} %constant.69.clone.right) | copy-start | bytes 6291460
  5.3 6.7 %copy-start.5 = (s32[16]{0:T(128)S(1)}, s32[16]{0:T(128)}, u32[]{:S(2)}) copy-start(s32[16]{0:T(128)} %dealing.9) | copy-start | bytes 196
  5.3 6.7 %copy-start.6 = (s32[16]{0:T(128)S(1)}, s32[16]{0:T(128)}, u32[]{:S(2)}) copy-start(s32[16]{0:T(128)} %cols.5) | copy-start | bytes 196
  5.3 37.3 %all-to-all-start = ((bf16[16,40,1024]{2,1,0:T(8,128)(2,1)}), bf16[16,40,1024]{2,1,0:T(8,128)(2,1)S(1)}, u32[]{:S(2)}, u32[]{:S(2)}) async-start(bf16[16,40,1024]{2,1,0:T(8,128)(2,1)} %get-tuple-element.16), calls=%async_computation | async-start | bytes 2621440 | tf_op jit(solution)/shard_map/all_to_all | solution.py:442
  12.1 1.6 %copy-start.2 = (bf16[1024,1024]{1,0:T(8,128)(2,1)S(1)}, bf16[1024,1024]{1,0:T(8,128)(2,1)}, u32[]{:S(2)}) copy-start(bf16[1024,1024]{1,0:T(8,128)(2,1)} %constant.70.clone.left) | copy-start | bytes 6291460
  13.7 1.2 %copy-start.3 = (bf16[2,512,512]{2,1,0:T(8,128)(2,1)S(1)}, bf16[2,512,512]{2,1,0:T(8,128)(2,1)}, u32[]{:S(2)}) copy-start(bf16[2,512,512]{2,1,0:T(8,128)(2,1)} %probe.1) | copy-start | bytes 3145732
  14.9 1.0 copy-start.4
  15.9 26.7 %copy-start.7 = (s32[16]{0:T(128)S(1)}, s32[16]{0:T(128)}, u32[]{:S(2)}) copy-start(s32[16]{0:T(128)} %rows.3) | copy-start | bytes 196
  22.4 9.7 %copy-start = (bf16[14336,1024]{1,0:T(8,128)(2,1)}, bf16[14336,1024]{1,0:T(8,128)(2,1)S(1)}, u32[]{:S(2)}) copy-start(bf16[14336,1024]{1,0:T(8,128)(2,1)S(1)} %get-tuple-element.17.stock) | copy-start | bytes 88080384
  50.5 2.0 %collective-permute-start = (bf16[256,1024]{1,0:T(8,128)(2,1)S(1)}, bf16[256,1024]{1,0:T(8,128)(2,1)S(1)}, u32[]{:S(2)}, u32[]{:S(2)}) collective-permute-start(bf16[256,1024]{1,0:T(8,128)(2,1)S(1)} %get-tuple-element.20), channel_id=1, source_target_pairs={{0,1},{1,0},{2,3},{3,2},{4,5},{5,4},{6,7},{7,6},{8,9},{9,8},{10,11... | collective-permute-start | bytes 1572872 | tf_op jit(solution)/shard_map/ppermute | solution.py:400
  53.5 16.4 %all-to-all-start.1 = ((bf16[8,32,1024]{2,1,0:T(8,128)(2,1)}), bf16[8,32,1024]{2,1,0:T(8,128)(2,1)S(1)}, u32[]{:S(2)}, u32[]{:S(2)}) async-start(bf16[8,32,1024]{2,1,0:T(8,128)(2,1)} %bitcast.1), calls=%async_computation.1 | async-start | bytes 1048576 | tf_op jit(solution)/shard_map/all_to_all | solution.py:408
  70.0 11.5 %collective-permute-start.1 = (bf16[32,1024]{1,0:T(8,128)(2,1)S(1)}, bf16[32,1024]{1,0:T(8,128)(2,1)S(1)}, u32[]{:S(2)}, u32[]{:S(2)}) collective-permute-start(bf16[32,1024]{1,0:T(8,128)(2,1)S(1)} %multiply_convert_fusion), channel_id=1, source_target_pairs={{0,12},{1,13},{2,14},{3,15},{4,8},{5,9},{6,10},{7,11},{8,4},{9,5},... | collective-permute-start | bytes 196616 | tf_op jit(solution)/shard_map/ppermute | solution.py:400
  70.4 11.1 %collective-permute-start.2 = (bf16[32,1024]{1,0:T(8,128)(2,1)S(1)}, bf16[32,1024]{1,0:T(8,128)(2,1)S(1)}, u32[]{:S(2)}, u32[]{:S(2)}) collective-permute-start(bf16[32,1024]{1,0:T(8,128)(2,1)S(1)} %multiply_convert_fusion), channel_id=1, source_target_pairs={{0,8},{1,9},{2,10},{3,11},{4,12},{5,13},{6,14},{7,15},{8,0},{9,1},... | collective-permute-start | bytes 196616 | tf_op jit(solution)/shard_map/ppermute | solution.py:400
  74.3 7.2 %collective-permute-start.3 = (bf16[32,1024]{1,0:T(8,128)(2,1)S(1)}, bf16[32,1024]{1,0:T(8,128)(2,1)S(1)}, u32[]{:S(2)}, u32[]{:S(2)}) collective-permute-start(bf16[32,1024]{1,0:T(8,128)(2,1)S(1)} %multiply_convert_fusion), channel_id=1, source_target_pairs={{0,4},{1,5},{2,6},{3,7},{4,0},{5,1},{6,2},{7,3},{8,12},{9,13},{10,... | collective-permute-start | bytes 196616 | tf_op jit(solution)/shard_map/ppermute | solution.py:400
  74.3 37.8 %all-to-all-start.2 = ((bf16[16,40,1024]{2,1,0:T(8,128)(2,1)}), bf16[16,40,1024]{2,1,0:T(8,128)(2,1)S(1)}, u32[]{:S(2)}, u32[]{:S(2)}) async-start(bf16[16,40,1024]{2,1,0:T(8,128)(2,1)} %pack.1), calls=%async_computation.2 | async-start | bytes 2621440 | tf_op jit(solution)/shard_map/all_to_all | solution.py:451
  81.6 13.8 %collective-permute-start.4 = (bf16[4,32,1024]{2,1,0:T(8,128)(2,1)S(1)}, bf16[4,32,1024]{2,1,0:T(8,128)(2,1)S(1)}, u32[]{:S(2)}, u32[]{:S(2)}) collective-permute-start(bf16[4,32,1024]{2,1,0:T(8,128)(2,1)S(1)} %pad_maximum_fusion.3), channel_id=1, source_target_pairs={{0,2},{1,3},{2,0},{3,1},{4,6},{5,7},{6,4},{7,5},{8,10},{9,11},{10,... | collective-permute-start | bytes 786440 | tf_op jit(solution)/shard_map/ppermute | solution.py:400
  95.6 4.2 %collective-permute-start.5 = (bf16[4,2,32,1024]{3,2,1,0:T(8,128)(2,1)S(1)}, bf16[4,2,32,1024]{3,2,1,0:T(8,128)(2,1)S(1)}, u32[]{:S(2)}, u32[]{:S(2)}) collective-permute-start(bf16[4,2,32,1024]{3,2,1,0:T(8,128)(2,1)S(1)} %pad_maximum_fusion.2), channel_id=1, source_target_pairs={{0,1},{1,0},{2,3},{3,2},{4,5},{5,4},{6,7},{7,6},{8,9},{9,8},{10,11... | collective-permute-start | bytes 1572872 | tf_op jit(solution)/shard_map/ppermute | solution.py:400

commit v12 on v11

--- a/solution.py
+++ b/solution.py
@@ -401,22 +401,22 @@
 
 
 def sum_probe(kept, sent, devices):
-    chips = devices // 2
-    total = (kept + swap(sent, 1, devices).astype(jnp.float32)).astype(jnp.bfloat16)
-    groups = [list(range(core, devices, 2)) for core in range(2)]
-    count = total.shape[0] // chips
-    shares = lax.all_to_all(
-        total.reshape(chips, count, -1), "row", split_axis=0, concat_axis=0, tiled=True, axis_index_groups=groups
-    )
-    return jnp.sum(shares.astype(jnp.float32), axis=0)
+    me = lax.axis_index("row")
+    total = kept + swap(sent, 1, devices).astype(jnp.float32)
+    for stride, radix in strides(devices)[1:]:
+        digit = me // stride % radix
+        count = total.shape[0] // radix
+        own = lax.dynamic_slice_in_dim(total, digit * count, count)
+        for k in range(1, radix):
+            share = lax.dynamic_slice_in_dim(total, lax.bitwise_xor(digit, k) * count, count)
+            own = own + swap(share.astype(jnp.bfloat16), k * stride, devices).astype(jnp.float32)
+        total = own
+    return total
 
 
 def join(whole, devices):
     me = lax.axis_index("row")
-    rows, width = whole.shape
-    steps = strides(devices)
-    axes = [*range(len(steps) - 1), 0]
-    for axis, (stride, radix) in zip(axes, reversed(steps)):
+    for stride, radix in reversed(strides(devices)):
         digit = me // stride % radix
         shares = [whole] + [swap(whole, k * stride, devices) for k in range(1, radix)]
         pieces = []
@@ -425,8 +425,8 @@
             for k in range(1, radix):
                 piece = jnp.where(lax.bitwise_xor(digit, k) == j, shares[k], piece)
             pieces.append(piece)
-        whole = jnp.stack(pieces, axis=axis)
-    return whole.reshape(devices * rows, width)
+        whole = jnp.concatenate(pieces, axis=0)
+    return whole
 
 
 def body(object_field, probe, amplitude, row_offsets, col_offsets, dealing):

time: 117 us -> 116 us (level)
  starting transfers between devices: 25.9 us -> 24.6 us
    all_to_all x1 -> x0, waiting for transfers between devices: 9.78 us -> none  [sum_probe(): lax.all_to_all(total.reshape(chips, count, -1), 'row', split_axis=0, conc...]
    ppermute x6 -> x10, waiting for transfers between devices: 16.7 us -> 26.2 us  [swap(): return lax.ppermute(x, 'row', [(d, d ^ distance) for d in range(devices)])]
    all_to_all x1 -> x0, starting transfers between devices: 4.44 us -> none  [sum_probe(): lax.all_to_all(total.reshape(chips, count, -1), 'row', split_axis=0, conc...]
    ppermute x6 -> x10, starting transfers between devices: 7.55 us -> 10.4 us  [swap(): return lax.ppermute(x, 'row', [(d, d ^ distance) for d in range(devices)])]
    add x0 -> x3, other arithmetic: none -> 1.31 us  [the longest x1 1.22 us: sum_probe(): total = kept + swap(sent, 1, devices).astype(jnp.float32)]
  transfers between devices with their start and end apart: 9 -> 12, of which waited for: 6 -> 8; matrix products, arithmetic and copies ran while one was open for 2% -> 2% of each run, Pallas kernels for 7% -> 7%
where the time goes in v12:
time: 116 us
  waiting for transfers between devices  46.8 us (40%)
  Pallas kernels  26.3 us (23%)
  starting transfers between devices  24.6 us (21%)
  local copies, waits for them, and re-layouts  13.8 us (12%)
  other arithmetic  3.5 us (3%)
    ppermute x10, waiting for transfers between devices, swap(): return lax.ppermute(x, 'row', [(d, d ^ distance) for d in range(devices)])  26.2 us
    unnamed x16, local copies, waits for them, and re-layouts  13.6 us
    all_to_all x1, waiting for transfers between devices, body(): lax.all_to_all(pieces, 'row', split_axis=0, concat_axis=0, tiled=True)  10.5 us
    ppermute x10, starting transfers between devices, swap(): return lax.ppermute(x, 'row', [(d, d ^ distance) for d in range(devices)])  10.4 us
    all_to_all x1, waiting for transfers between devices, body(): lax.all_to_all(terms, 'row', split_axis=0, concat_axis=0, tiled=True)  10.1 us
    pallas_call x1, Pallas kernels, slot_terms(): pl.pallas_call(slot_kernel, out_shape=(jax.ShapeDtypeStruct((order, wide_...  8.73 us
    all_to_all x1, starting transfers between devices, body(): lax.all_to_all(terms, 'row', split_axis=0, concat_axis=0, tiled=True)  7.48 us
    all_to_all x1, starting transfers between devices, body(): lax.all_to_all(pieces, 'row', split_axis=0, concat_axis=0, tiled=True)  6.7 us
  transfers between devices with their start and end apart: 12, of which 8 were waited for; matrix products, arithmetic and copies ran while one was open for 2% of the time, Pallas kernels for 7%

profile of v12, /device:TPU:15, one launch (start us, length us, event | category | flops | bytes accessed | tf_op | source)
XLA Modules:
  0.0 115.9 jit_solution(2350288863470716328)
XLA Ops:
  0.6 4.7 %fetch.1 = (bf16[16,40,1024]{2,1,0:T(8,128)(2,1)}, s32[1]{0:T(128)}) custom-call(s32[16]{0:T(128)} %dealing.9, s32[16]{0:T(128)} %cols.5, f32[2,40,32768]{2,1,0:T(8,128)} %tile.1), custom_call_target="tpu_custom_call" | custom-call | bytes 6291456 | tf_op jit(solution)/shard_map/fetch/pallas_call | solution.py:85
  5.3 0.0 copy-start.1
  5.3 0.0 copy-start.5
  5.3 0.0 copy-start.6
  5.3 6.7 %all-to-all-start = ((bf16[16,40,1024]{2,1,0:T(8,128)(2,1)}), bf16[16,40,1024]{2,1,0:T(8,128)(2,1)S(1)}, u32[]{:S(2)}, u32[]{:S(2)}) async-start(bf16[16,40,1024]{2,1,0:T(8,128)(2,1)} %get-tuple-element.16), calls=%async_computation | async-start | bytes 2621440 | tf_op jit(solution)/shard_map/all_to_all | solution.py:442
  12.0 0.0 copy-done.1
  12.0 0.0 copy-done.5
  12.1 0.0 copy-done.6
  12.1 0.0 copy-start.2
  12.1 1.6 %copy-done.2 = bf16[1024,1024]{1,0:T(8,128)(2,1)S(1)} copy-done((bf16[1024,1024]{1,0:T(8,128)(2,1)S(1)}, bf16[1024,1024]{1,0:T(8,128)(2,1)}, u32[]{:S(2)}) %copy-start.2) | copy-done | bytes 2097176
  13.7 0.0 copy-start.3
  13.7 1.2 %copy-done.3 = bf16[2,512,512]{2,1,0:T(8,128)(2,1)S(1)} copy-done((bf16[2,512,512]{2,1,0:T(8,128)(2,1)S(1)}, bf16[2,512,512]{2,1,0:T(8,128)(2,1)}, u32[]{:S(2)}) %copy-start.3) | copy-done | bytes 1048600
  14.9 0.0 copy-start.4
  14.9 1.0 copy-done.4
  15.9 0.0 copy-start.7
  15.9 6.4 %prepare.1 = (f32[2,40,32768]{2,1,0:T(8,128)}, s32[80]{0:T(128)S(1)}, s32[80]{0:T(128)S(1)}, bf16[14336,1024]{1,0:T(8,128)(2,1)S(1)}) custom-call(s32[16]{0:T(128)S(1)} %copy-done.5, s32[16]{0:T(128)S(1)} %copy-done.6, s32[1]{0:T(128)} %get-tuple-element.13.token, bf16[1024,1024]{1,0:T(8,128)(2,1)S(1)} %copy-done.1, bf16[1024,1024]{1,0:T(8,128)(2,1)S(1)} %copy-done.2, ...), custom_call_target="tpu_custom_call" | custom-call | bytes 115343360 | tf_op jit(solution)/shard_map/prepare/pallas_call | solution.py:162
  22.4 0.0 copy-start
  22.4 9.7 %copy-done = bf16[14336,1024]{1,0:T(8,128)(2,1)} copy-done((bf16[14336,1024]{1,0:T(8,128)(2,1)}, bf16[14336,1024]{1,0:T(8,128)(2,1)S(1)}, u32[]{:S(2)}) %copy-start) | copy-done | bytes 29360152
  32.1 10.5 %all-to-all-done = bf16[16,40,1024]{2,1,0:T(8,128)(2,1)S(1)} async-done(((bf16[16,40,1024]{2,1,0:T(8,128)(2,1)}), bf16[16,40,1024]{2,1,0:T(8,128)(2,1)S(1)}, u32[]{:S(2)}, u32[]{:S(2)}) %all-to-all-start) | async-done | bytes 1310752 | tf_op jit(solution)/shard_map/all_to_all | solution.py:442
  42.6 0.0 copy-done.7
  42.6 8.7 %slot.1 = (bf16[512,1024]{1,0:T(8,128)(2,1)S(1)}, f32[256,1024]{1,0:T(8,128)S(1)}, bf16[256,1024]{1,0:T(8,128)(2,1)}) custom-call(s32[16]{0:T(128)S(1)} %copy-done.5, s32[16]{0:T(128)S(1)} %copy-done.7, s32[80]{0:T(128)S(1)} %get-tuple-element.15.owners, bf16[640,1024]{1,0:T(8,128)(2,1)S(1)} %bitcast.5, bf16[14336,1024]{1,0:T(8,128)(2,1)} %copy-done), custom_call_target="tpu_custom_call" | custom-call | flops 4294967296 | bytes 8388608 | tf_op jit(solution)/shard_map/slot/pallas_call | solution.py:272
  51.3 0.3 collective-permute-start
  51.6 2.0 %collective-permute-done = bf16[256,1024]{1,0:T(8,128)(2,1)} collective-permute-done((bf16[256,1024]{1,0:T(8,128)(2,1)}, bf16[256,1024]{1,0:T(8,128)(2,1)}, u32[]{:S(2)}, u32[]{:S(2)}) %collective-permute-start) | collective-permute-done | bytes 524320 | tf_op jit(solution)/shard_map/ppermute | solution.py:400
  53.7 1.2 %convert_add_fusion = f32[256,1024]{1,0:T(8,128)S(1)} fusion(f32[256,1024]{1,0:T(8,128)S(1)} %get-tuple-element.19, bf16[256,1024]{1,0:T(8,128)(2,1)} %collective-permute-done), kind=kLoop, calls=%fused_computation.4 | loop fusion | flops 524288 | bytes 2621440 | tf_op jit(solution)/shard_map/add | solution.py:405
  54.9 0.1 collective-permute-start.1
  55.1 7.6 %collective-permute-done.1 = bf16[128,1024]{1,0:T(8,128)(2,1)S(1)} collective-permute-done((bf16[128,1024]{1,0:T(8,128)(2,1)S(1)}, bf16[128,1024]{1,0:T(8,128)(2,1)S(1)}, u32[]{:S(2)}, u32[]{:S(2)}) %collective-permute-start.1) | collective-permute-done | bytes 262176 | tf_op jit(solution)/shard_map/ppermute | solution.py:400
  62.7 0.1 convert_add_fusion.1
  62.8 0.4 collective-permute-start.4
  63.2 0.8 collective-permute-start.3
  64.1 1.5 %collective-permute-start.2 = (bf16[32,1024]{1,0:T(8,128)(2,1)S(1)}, bf16[32,1024]{1,0:T(8,128)(2,1)S(1)}, u32[]{:S(2)}, u32[]{:S(2)}) collective-permute-start(bf16[32,1024]{1,0:T(8,128)(2,1)S(1)} %get-tuple-element.30), channel_id=1, source_target_pairs={{0,4},{1,5},{2,6},{3,7},{4,0},{5,1},{6,2},{7,3},{8,12},{9,13},{10,... | collective-permute-start | bytes 196616 | tf_op jit(solution)/shard_map/ppermute | solution.py:400
  65.5 2.2 %pack.1 = bf16[16,40,1024]{2,1,0:T(8,128)(2,1)} custom-call(s32[16]{0:T(128)S(1)} %copy-done.5, s32[16]{0:T(128)S(1)} %copy-done.7, bf16[512,1024]{1,0:T(8,128)(2,1)S(1)} %get-tuple-element.18.term), custom_call_target="tpu_custom_call" | custom-call | bytes 3145728 | tf_op jit(solution)/shard_map/pack/pallas_call | solution.py:319
  67.7 0.3 collective-permute-done.4
  68.1 0.0 collective-permute-done.3
  68.1 1.1 collective-permute-done.2
  69.2 0.9 collective-permute-start.5
  70.1 3.4 %collective-permute-start.6 = (bf16[32,1024]{1,0:T(8,128)(2,1)S(1)}, bf16[32,1024]{1,0:T(8,128)(2,1)S(1)}, u32[]{:S(2)}, u32[]{:S(2)}) collective-permute-start(bf16[32,1024]{1,0:T(8,128)(2,1)S(1)} %multiply_convert_fusion), channel_id=1, source_target_pairs={{0,8},{1,9},{2,10},{3,11},{4,12},{5,13},{6,14},{7,15},{8,0},{9,1},... | collective-permute-start | bytes 196616 | tf_op jit(solution)/shard_map/ppermute | solution.py:400
  73.6 0.0 collective-permute-start.7
  73.6 7.5 %all-to-all-start.1 = ((bf16[16,40,1024]{2,1,0:T(8,128)(2,1)}), bf16[16,40,1024]{2,1,0:T(8,128)(2,1)S(1)}, u32[]{:S(2)}, u32[]{:S(2)}) async-start(bf16[16,40,1024]{2,1,0:T(8,128)(2,1)} %pack.1), calls=%async_computation.1 | async-start | bytes 2621440 | tf_op jit(solution)/shard_map/all_to_all | solution.py:451
  81.1 0.0 collective-permute-done.5
  81.1 0.0 collective-permute-done.6
  81.1 0.0 collective-permute-done.7
  81.2 0.3 collective-permute-start.8
  81.5 13.5 %collective-permute-done.8 = bf16[128,1024]{1,0:T(8,128)(2,1)S(1)} collective-permute-done((bf16[128,1024]{1,0:T(8,128)(2,1)S(1)}, bf16[128,1024]{1,0:T(8,128)(2,1)S(1)}, u32[]{:S(2)}, u32[]{:S(2)}) %collective-permute-start.8) | collective-permute-done | bytes 262176 | tf_op jit(solution)/shard_map/ppermute | solution.py:400
  95.0 0.1 broadcast_select_fusion.3
  95.2 2.6 %collective-permute-start.9 = (bf16[256,1024]{1,0:T(8,128)(2,1)S(1)}, bf16[256,1024]{1,0:T(8,128)(2,1)S(1)}, u32[]{:S(2)}, u32[]{:S(2)}) collective-permute-start(bf16[256,1024]{1,0:T(8,128)(2,1)S(1)} %pad_maximum_fusion.1), channel_id=1, source_target_pairs={{0,1},{1,0},{2,3},{3,2},{4,5},{5,4},{6,7},{7,6},{8,9},{9,8},{10,11... | collective-permute-start | bytes 1572872 | tf_op jit(solution)/shard_map/ppermute | solution.py:400
  97.8 1.5 %collective-permute-done.9 = bf16[256,1024]{1,0:T(8,128)(2,1)S(1)} collective-permute-done((bf16[256,1024]{1,0:T(8,128)(2,1)S(1)}, bf16[256,1024]{1,0:T(8,128)(2,1)S(1)}, u32[]{:S(2)}, u32[]{:S(2)}) %collective-permute-start.9) | collective-permute-done | bytes 524320 | tf_op jit(solution)/shard_map/ppermute | solution.py:400
  99.3 0.2 broadcast_select_fusion.1
  99.6 0.2 maximum_convert_fusion
  99.8 0.2 slice_bitcast_fusion.1
  100.0 1.5 %pad_maximum_fusion = f32[2,512,512]{2,1,0:T(8,128)} fusion(f32[1,512,512]{2,1,0:T(8,128)S(1)} %get-tuple-element.25, f32[1,512,512]{2,1,0:T(8,128)S(1)} %get-tuple-element.24), kind=kLoop, calls=%fused_computation | loop fusion | flops 524288 | bytes 4194304 | tf_op jit(solution)/shard_map/stack | solution.py:454
  101.5 10.1 %all-to-all-done.1.terms = bf16[16,40,1024]{2,1,0:T(8,128)(2,1)S(1)} async-done(((bf16[16,40,1024]{2,1,0:T(8,128)(2,1)}), bf16[16,40,1024]{2,1,0:T(8,128)(2,1)S(1)}, u32[]{:S(2)}, u32[]{:S(2)}) %all-to-all-start.1) | async-done | bytes 1310752 | tf_op jit(solution)/shard_map/all_to_all | solution.py:451
  111.6 4.2 %place.1 = f32[2,40,32768]{2,1,0:T(8,128)} custom-call(s32[16]{0:T(128)S(1)} %copy-done.5, s32[16]{0:T(128)S(1)} %copy-done.6, s32[80]{0:T(128)S(1)} %get-tuple-element.14.blocks, s32[80]{0:T(128)S(1)} %get-tuple-element.15.owners, bf16[16,40,1024]{2,1,0:T(8,128)(2,1)S(1)} %all-to-all-done.1.terms, ...), custom_call_target="tpu_custom_call", output_to_operand_aliasing={{}: (5, {})} | custom-call | bytes 6291456 | tf_op jit(solution)/shard_map/place/pallas_call | solution.py:374
  (7 shorter events, 0.2 us)
Async XLA Ops:
  5.3 6.7 %copy-start.1 = (bf16[1024,1024]{1,0:T(8,128)(2,1)S(1)}, bf16[1024,1024]{1,0:T(8,128)(2,1)}, u32[]{:S(2)}) copy-start(bf16[1024,1024]{1,0:T(8,128)(2,1)} %constant.81.clone.right) | copy-start | bytes 6291460
  5.3 6.7 %copy-start.5 = (s32[16]{0:T(128)S(1)}, s32[16]{0:T(128)}, u32[]{:S(2)}) copy-start(s32[16]{0:T(128)} %dealing.9) | copy-start | bytes 196
  5.3 6.7 %copy-start.6 = (s32[16]{0:T(128)S(1)}, s32[16]{0:T(128)}, u32[]{:S(2)}) copy-start(s32[16]{0:T(128)} %cols.5) | copy-start | bytes 196
  5.3 37.3 %all-to-all-start = ((bf16[16,40,1024]{2,1,0:T(8,128)(2,1)}), bf16[16,40,1024]{2,1,0:T(8,128)(2,1)S(1)}, u32[]{:S(2)}, u32[]{:S(2)}) async-start(bf16[16,40,1024]{2,1,0:T(8,128)(2,1)} %get-tuple-element.16), calls=%async_computation | async-start | bytes 2621440 | tf_op jit(solution)/shard_map/all_to_all | solution.py:442
  12.1 1.6 %copy-start.2 = (bf16[1024,1024]{1,0:T(8,128)(2,1)S(1)}, bf16[1024,1024]{1,0:T(8,128)(2,1)}, u32[]{:S(2)}) copy-start(bf16[1024,1024]{1,0:T(8,128)(2,1)} %constant.82.clone.left) | copy-start | bytes 6291460
  13.7 1.2 %copy-start.3 = (bf16[2,512,512]{2,1,0:T(8,128)(2,1)S(1)}, bf16[2,512,512]{2,1,0:T(8,128)(2,1)}, u32[]{:S(2)}) copy-start(bf16[2,512,512]{2,1,0:T(8,128)(2,1)} %probe.1) | copy-start | bytes 3145732
  14.9 1.0 copy-start.4
  15.9 26.7 %copy-start.7 = (s32[16]{0:T(128)S(1)}, s32[16]{0:T(128)}, u32[]{:S(2)}) copy-start(s32[16]{0:T(128)} %rows.3) | copy-start | bytes 196
  22.4 9.7 %copy-start = (bf16[14336,1024]{1,0:T(8,128)(2,1)}, bf16[14336,1024]{1,0:T(8,128)(2,1)S(1)}, u32[]{:S(2)}) copy-start(bf16[14336,1024]{1,0:T(8,128)(2,1)S(1)} %get-tuple-element.17.stock) | copy-start | bytes 88080384
  51.3 2.3 %collective-permute-start = (bf16[256,1024]{1,0:T(8,128)(2,1)}, bf16[256,1024]{1,0:T(8,128)(2,1)}, u32[]{:S(2)}, u32[]{:S(2)}) collective-permute-start(bf16[256,1024]{1,0:T(8,128)(2,1)} %get-tuple-element.20), channel_id=1, source_target_pairs={{0,1},{1,0},{2,3},{3,2},{4,5},{5,4},{6,7},{7,6},{8,9},{9,8},{10,11... | collective-permute-start | bytes 1572872 | tf_op jit(solution)/shard_map/ppermute | solution.py:400
  54.9 7.8 %collective-permute-start.1 = (bf16[128,1024]{1,0:T(8,128)(2,1)S(1)}, bf16[128,1024]{1,0:T(8,128)(2,1)S(1)}, u32[]{:S(2)}, u32[]{:S(2)}) collective-permute-start(bf16[128,1024]{1,0:T(8,128)(2,1)S(1)} %dynamic-slice_convert_fusion), channel_id=1, source_target_pairs={{0,2},{1,3},{2,0},{3,1},{4,6},{5,7},{6,4},{7,5},{8,10},{9,11},{10,... | collective-permute-start | bytes 786440 | tf_op jit(solution)/shard_map/ppermute | solution.py:400
  62.8 5.3 %collective-permute-start.4 = (bf16[32,1024]{1,0:T(8,128)(2,1)S(1)}, bf16[32,1024]{1,0:T(8,128)(2,1)S(1)}, u32[]{:S(2)}, u32[]{:S(2)}) collective-permute-start(bf16[32,1024]{1,0:T(8,128)(2,1)S(1)} %get-tuple-element.31), channel_id=1, source_target_pairs={{0,12},{1,13},{2,14},{3,15},{4,8},{5,9},{6,10},{7,11},{8,4},{9,5},... | collective-permute-start | bytes 196616 | tf_op jit(solution)/shard_map/ppermute | solution.py:400
  63.2 4.8 %collective-permute-start.3 = (bf16[32,1024]{1,0:T(8,128)(2,1)S(1)}, bf16[32,1024]{1,0:T(8,128)(2,1)S(1)}, u32[]{:S(2)}, u32[]{:S(2)}) collective-permute-start(bf16[32,1024]{1,0:T(8,128)(2,1)S(1)} %get-tuple-element.32), channel_id=1, source_target_pairs={{0,8},{1,9},{2,10},{3,11},{4,12},{5,13},{6,14},{7,15},{8,0},{9,1},... | collective-permute-start | bytes 196616 | tf_op jit(solution)/shard_map/ppermute | solution.py:400
  64.1 5.1 %collective-permute-start.2 = (bf16[32,1024]{1,0:T(8,128)(2,1)S(1)}, bf16[32,1024]{1,0:T(8,128)(2,1)S(1)}, u32[]{:S(2)}, u32[]{:S(2)}) collective-permute-start(bf16[32,1024]{1,0:T(8,128)(2,1)S(1)} %get-tuple-element.30), channel_id=1, source_target_pairs={{0,4},{1,5},{2,6},{3,7},{4,0},{5,1},{6,2},{7,3},{8,12},{9,13},{10,... | collective-permute-start | bytes 196616 | tf_op jit(solution)/shard_map/ppermute | solution.py:400
  69.2 11.8 %collective-permute-start.5 = (bf16[32,1024]{1,0:T(8,128)(2,1)S(1)}, bf16[32,1024]{1,0:T(8,128)(2,1)S(1)}, u32[]{:S(2)}, u32[]{:S(2)}) collective-permute-start(bf16[32,1024]{1,0:T(8,128)(2,1)S(1)} %multiply_convert_fusion), channel_id=1, source_target_pairs={{0,12},{1,13},{2,14},{3,15},{4,8},{5,9},{6,10},{7,11},{8,4},{9,5},... | collective-permute-start | bytes 196616 | tf_op jit(solution)/shard_map/ppermute | solution.py:400
  70.1 10.9 %collective-permute-start.6 = (bf16[32,1024]{1,0:T(8,128)(2,1)S(1)}, bf16[32,1024]{1,0:T(8,128)(2,1)S(1)}, u32[]{:S(2)}, u32[]{:S(2)}) collective-permute-start(bf16[32,1024]{1,0:T(8,128)(2,1)S(1)} %multiply_convert_fusion), channel_id=1, source_target_pairs={{0,8},{1,9},{2,10},{3,11},{4,12},{5,13},{6,14},{7,15},{8,0},{9,1},... | collective-permute-start | bytes 196616 | tf_op jit(solution)/shard_map/ppermute | solution.py:400
  73.6 7.5 %collective-permute-start.7 = (bf16[32,1024]{1,0:T(8,128)(2,1)S(1)}, bf16[32,1024]{1,0:T(8,128)(2,1)S(1)}, u32[]{:S(2)}, u32[]{:S(2)}) collective-permute-start(bf16[32,1024]{1,0:T(8,128)(2,1)S(1)} %multiply_convert_fusion), channel_id=1, source_target_pairs={{0,4},{1,5},{2,6},{3,7},{4,0},{5,1},{6,2},{7,3},{8,12},{9,13},{10,... | collective-permute-start | bytes 196616 | tf_op jit(solution)/shard_map/ppermute | solution.py:400
  73.6 38.0 %all-to-all-start.1 = ((bf16[16,40,1024]{2,1,0:T(8,128)(2,1)}), bf16[16,40,1024]{2,1,0:T(8,128)(2,1)S(1)}, u32[]{:S(2)}, u32[]{:S(2)}) async-start(bf16[16,40,1024]{2,1,0:T(8,128)(2,1)} %pack.1), calls=%async_computation.1 | async-start | bytes 2621440 | tf_op jit(solution)/shard_map/all_to_all | solution.py:451
  81.2 13.9 %collective-permute-start.8 = (bf16[128,1024]{1,0:T(8,128)(2,1)S(1)}, bf16[128,1024]{1,0:T(8,128)(2,1)S(1)}, u32[]{:S(2)}, u32[]{:S(2)}) collective-permute-start(bf16[128,1024]{1,0:T(8,128)(2,1)S(1)} %pad_maximum_fusion.2), channel_id=1, source_target_pairs={{0,2},{1,3},{2,0},{3,1},{4,6},{5,7},{6,4},{7,5},{8,10},{9,11},{10,... | collective-permute-start | bytes 786440 | tf_op jit(solution)/shard_map/ppermute | solution.py:400
  95.2 4.2 %collective-permute-start.9 = (bf16[256,1024]{1,0:T(8,128)(2,1)S(1)}, bf16[256,1024]{1,0:T(8,128)(2,1)S(1)}, u32[]{:S(2)}, u32[]{:S(2)}) collective-permute-start(bf16[256,1024]{1,0:T(8,128)(2,1)S(1)} %pad_maximum_fusion.1), channel_id=1, source_target_pairs={{0,1},{1,0},{2,3},{3,2},{4,5},{5,4},{6,7},{7,6},{8,9},{9,8},{10,11... | collective-permute-start | bytes 1572872 | tf_op jit(solution)/shard_map/ppermute | solution.py:400

commit v13 on v12

--- a/solution.py
+++ b/solution.py
@@ -46,7 +46,7 @@
     return picked.reshape(count, width)
 
 
-def fetch_kernel(order, dealing, cols, tile, out, token, held, sems):
+def fetch_kernel(order, dealing, cols, tile, out, token, held, cut, sems, out_sems):
     token[0] = dealing[0]
     slots, tile_rows = out.shape[0], out.shape[1]
     tile_cols = tile.shape[2]
@@ -61,6 +61,9 @@
         copy(slot).start()
 
     lane = lax.broadcasted_iota(jnp.int32, (tile_rows, LANES), 1)
+
+    def send(slot):
+        return pltpu.make_async_copy(cut.at[slot], out.at[slot], out_sems.at[slot])
 
     @pl.loop(0, slots, unroll=4)
     def _(slot):
@@ -75,7 +78,12 @@
             for b in range(order // LANES):
                 first = part * order + b * LANES
                 cells = jnp.where(lane < LANES - offset, turned[b], turned[b + 1])
-                out[slot, :, first : first + LANES] = cells
+                cut[slot, :, first : first + LANES] = cells
+        send(slot).start()
+
+    @pl.loop(0, slots)
+    def _(slot):
+        send(slot).wait()
 
 
 def fetch_windows(tile, dealing, cols, order):
@@ -89,9 +97,11 @@
             jax.ShapeDtypeStruct((1,), jnp.int32),
         ),
         in_specs=[SMEM, SMEM, ANY],
-        out_specs=(VMEM, SMEM),
+        out_specs=(ANY, SMEM),
         scratch_shapes=[
             pltpu.VMEM((slots, 2, tile_rows, span), jnp.float32),
+            pltpu.VMEM((slots, tile_rows, 2 * order), jnp.bfloat16),
+            pltpu.SemaphoreType.DMA((slots,)),
             pltpu.SemaphoreType.DMA((slots,)),
         ],
         compiler_params=pltpu.CompilerParams(vmem_limit_bytes=56 * 2**20),
@@ -112,8 +122,8 @@
 
 def prepare_kernel(
     order, dealing, cols, token, right, left, probe, measured,
-    empty, blocks, owners, stock,
-    table, zeros, sems, stock_sems,
+    empty, blocks, owners, single, stock,
+    table, shared, zeros, sems, stock_sems,
 ):
     del token
     places = stock_places(stock, order)
@@ -148,6 +158,15 @@
             owner = jnp.where(known < 0, number, known)
             owners[number] = owner
             table[block] = owner
+            shared[number] = jnp.where(known < 0, 0, 1)
+            shared[owner] = jnp.where(known < 0, 0, 1)
+
+    @pl.loop(0, slots)
+    def _(slot):
+        total = shared[slot * count]
+        for b in range(1, count):
+            total += shared[slot * count + b]
+        single[slot] = jnp.where(total == 0, 1, 0)
 
     for fill in fills:
         fill.wait()
@@ -165,12 +184,14 @@
             jax.ShapeDtypeStruct(tile_shape, jnp.float32),
             jax.ShapeDtypeStruct((numbers,), jnp.int32),
             jax.ShapeDtypeStruct((numbers,), jnp.int32),
+            jax.ShapeDtypeStruct((slots,), jnp.int32),
             jax.ShapeDtypeStruct((28 * order, 2 * order), jnp.bfloat16),
         ),
         in_specs=[SMEM, SMEM, SMEM, ANY, ANY, ANY, ANY],
-        out_specs=(ANY, SMEM, SMEM, ANY),
+        out_specs=(ANY, SMEM, SMEM, SMEM, ANY),
         scratch_shapes=[
             pltpu.SMEM((tile_shape[2] // LANES,), jnp.int32),
+            pltpu.SMEM((numbers,), jnp.int32),
             pltpu.VMEM(tile_shape[:2] + (fill_cols,), jnp.float32),
             pltpu.SemaphoreType.DMA((tile_shape[2] // fill_cols,)),
             pltpu.SemaphoreType.DMA((5,)),
@@ -205,27 +226,27 @@
     wide[total_rows:, :] = jnp.zeros((SUBLANES, 2 * order), jnp.float32)
     loads[0].wait()
     loads[1].wait()
-
-    @pl.loop(0, order // step)
-    def _(i):
-        place = pl.ds(pl.multiple_of(i * step, step), step)
-        found = rows_from(wide, first_row + i * step, step)
-        patch[place, :] = found.astype(patch.dtype)
-        real, imag = found[:, :order], found[:, order:]
-        probe_real = probe[0, place, :].astype(jnp.float32)
-        probe_imag = probe[1, place, :].astype(jnp.float32)
-        wave[place, :order] = (probe_real * real - probe_imag * imag).astype(wave.dtype)
-        wave[place, order:] = (probe_real * imag + probe_imag * real).astype(wave.dtype)
+    loads[2].wait()
 
     def dot(a, b):
         return jnp.dot(a, b, preferred_element_type=jnp.float32)
 
-    loads[2].wait()
-    for first in range(0, order, tile):
-        here = slice(first, first + tile)
-        there = slice(order + first, order + first + tile)
-        half[:order, here] = dot(wave[...], right[:, here]).astype(half.dtype)
-        half[order:, here] = dot(wave[...], right[:, there]).astype(half.dtype)
+    for top in range(0, order, tile):
+        for start in range(top, top + tile, step):
+            line = slice(start, start + step)
+            found = rows_from(wide, first_row + start, step)
+            patch[line, :] = found.astype(patch.dtype)
+            real, imag = found[:, :order], found[:, order:]
+            probe_real = probe[0, line, :].astype(jnp.float32)
+            probe_imag = probe[1, line, :].astype(jnp.float32)
+            wave[line, :order] = (probe_real * real - probe_imag * imag).astype(wave.dtype)
+            wave[line, order:] = (probe_real * imag + probe_imag * real).astype(wave.dtype)
+        line = slice(top, top + tile)
+        for first in range(0, order, tile):
+            here = slice(first, first + tile)
+            there = slice(order + first, order + first + tile)
+            half[line, here] = dot(wave[line, :], right[:, here]).astype(half.dtype)
+            half[order + top : order + top + tile, here] = dot(wave[line, :], right[:, there]).astype(half.dtype)
     loads[3].wait()
     loads[4].wait()
     for first in range(0, order, tile):
@@ -328,16 +349,25 @@
     )(dealing, rows, term)
 
 
-def place_kernel(order, dealing, cols, blocks, owners, terms, empty, out, totals, sems):
+def place_kernel(order, dealing, cols, blocks, owners, single, terms, empty, out, totals, sems):
     del empty
     slots, tile_rows = terms.shape[0], terms.shape[1]
     count = (order + LANES) // LANES
-    totals[...] = jnp.zeros_like(totals)
     lane = lax.broadcasted_iota(jnp.int32, (tile_rows, LANES), 1)
     nothing = jnp.zeros((tile_rows, LANES), jnp.float32)
 
-    @pl.loop(0, slots, unroll=4)
-    def _(slot):
+    def whole(slot):
+        place = pl.multiple_of(blocks[slot * count] * LANES, LANES)
+        window = out.at[:, :, pl.ds(place, count * LANES)]
+        return pltpu.make_async_copy(totals.at[slot], window, sems.at[slot * count])
+
+    def part_of(slot, b):
+        number = slot * count + b
+        place = pl.multiple_of(blocks[number] * LANES, LANES)
+        held = totals.at[slot, :, :, b * LANES : (b + 1) * LANES]
+        return pltpu.make_async_copy(held, out.at[:, :, pl.ds(place, LANES)], sems.at[number])
+
+    def add(slot):
         _, offset = window_start(cols[dealing[slot]], order, out.shape[2])
         shift = lax.rem(offset, LANES)
         for part in range(2):
@@ -348,43 +378,65 @@
             for b in range(count):
                 before = turned[b - 1] if b else nothing
                 after = turned[b] if b < count - 1 else nothing
+                term = jnp.where(lane < offset, before, after)
                 owner = owners[slot * count + b]
-                totals[owner, part] += jnp.where(lane < offset, before, after)
-
-    def copy(number):
-        place = pl.multiple_of(blocks[number] * LANES, LANES)
-        return pltpu.make_async_copy(totals.at[number], out.at[:, :, pl.ds(place, LANES)], sems.at[number])
-
-    @pl.loop(0, slots * count)
-    def _(number):
-        @pl.when(owners[number] == number)
+                holder = lax.div(owner, count)
+                here = pl.ds(pl.multiple_of((owner - holder * count) * LANES, LANES), LANES)
+                held = totals[holder, part, :, here]
+                totals[holder, part, :, here] = jnp.where(owner == slot * count + b, term, held + term)
+
+    half = slots // 2
+    for low, high in ((0, half), (half, slots)):
+
+        @pl.loop(low, high, unroll=4)
+        def _(slot):
+            add(slot)
+
+        @pl.loop(low, high)
+        def _(slot):
+            @pl.when(single[slot] == 1)
+            def _():
+                whole(slot).start()
+
+    def finish(slot, act):
+        @pl.when(single[slot] == 0)
         def _():
-            copy(number).start()
-
-    @pl.loop(0, slots * count)
-    def _(number):
-        @pl.when(owners[number] == number)
+            for b in range(count):
+
+                @pl.when(owners[slot * count + b] == slot * count + b)
+                def _():
+                    act(part_of(slot, b))
+
+    @pl.loop(0, slots)
+    def _(slot):
+        finish(slot, lambda copy: copy.start())
+
+    @pl.loop(0, slots)
+    def _(slot):
+        @pl.when(single[slot] == 1)
         def _():
-            copy(number).wait()
-
-
-def place_windows(terms, empty, blocks, owners, dealing, cols, order):
+            whole(slot).wait()
+
+        finish(slot, lambda copy: copy.wait())
+
+
+def place_windows(terms, empty, blocks, owners, single, dealing, cols, order):
     slots, tile_rows = terms.shape[0], terms.shape[1]
     count = (order + LANES) // LANES
     return pl.pallas_call(
         functools.partial(place_kernel, order),
         out_shape=jax.ShapeDtypeStruct(empty.shape, empty.dtype),
-        in_specs=[SMEM, SMEM, SMEM, SMEM, VMEM, ANY],
+        in_specs=[SMEM, SMEM, SMEM, SMEM, SMEM, VMEM, ANY],
         out_specs=ANY,
         scratch_shapes=[
-            pltpu.VMEM((slots * count, 2, tile_rows, LANES), jnp.float32),
+            pltpu.VMEM((slots, 2, tile_rows, count * LANES), jnp.float32),
             pltpu.SemaphoreType.DMA((slots * count,)),
         ],
-        input_output_aliases={5: 0},
+        input_output_aliases={6: 0},
         compiler_params=pltpu.CompilerParams(vmem_limit_bytes=24 * 2**20),
         cost_estimate=pl.CostEstimate(flops=0, bytes_accessed=6 * 2**20, transcendentals=0),
         name="place",
-    )(dealing, cols, blocks, owners, terms, empty)
+    )(dealing, cols, blocks, owners, single, terms, empty)
 
 
 def strides(devices):
@@ -441,7 +493,7 @@
     pieces, token = fetch_windows(object_field, dealing, col_offsets, order)
     strips = lax.all_to_all(pieces, "row", split_axis=0, concat_axis=0, tiled=True)
     cells = strips[:, :own_rows].reshape(total_rows, 2 * order)
-    empty, blocks, owners, stock = prepare(
+    empty, blocks, owners, single, stock = prepare(
         dealing, col_offsets, token, probe, amplitude, object_field.shape
     )
     term, kept, sent = slot_terms(cells, stock, dealing, row_offsets, owners, order)
@@ -452,7 +504,7 @@
     share = (total * (1.0 / dealing.shape[0])).astype(jnp.bfloat16)
     whole = join(share, devices).astype(jnp.float32)
     probe_grad = jnp.stack([whole[:, :order], whole[:, order:]])
-    object_grad = place_windows(arrived, empty, blocks, owners, dealing, col_offsets, order)
+    object_grad = place_windows(arrived, empty, blocks, owners, single, dealing, col_offsets, order)
     if spare:
         object_grad = object_grad[:, :own_rows]
     return (object_grad, probe_grad)

time: 116 us -> 117 us (level)
  no operation moved by 1% of the time
where the time goes in v13:
time: 117 us; the launch traced here: 116 us
  waiting for transfers between devices  46.8 us (40%)
  Pallas kernels  26.8 us (23%)
  starting transfers between devices  24.6 us (21%)
  local copies, waits for them, and re-layouts  13.8 us (12%)
  other arithmetic  3.5 us (3%)
    ppermute x10, waiting for transfers between devices, swap(): return lax.ppermute(x, 'row', [(d, d ^ distance) for d in range(devices)])  26.1 us
    unnamed x16, local copies, waits for them, and re-layouts  13.6 us
    all_to_all x1, waiting for transfers between devices, body(): lax.all_to_all(pieces, 'row', split_axis=0, concat_axis=0, tiled=True)  10.6 us
    ppermute x10, starting transfers between devices, swap(): return lax.ppermute(x, 'row', [(d, d ^ distance) for d in range(devices)])  10.4 us
    all_to_all x1, waiting for transfers between devices, body(): lax.all_to_all(terms, 'row', split_axis=0, concat_axis=0, tiled=True)  10.1 us
    pallas_call x1, Pallas kernels, slot_terms(): pl.pallas_call(slot_kernel, out_shape=(jax.ShapeDtypeStruct((order, wide_...  8.83 us
    all_to_all x1, starting transfers between devices, body(): lax.all_to_all(terms, 'row', split_axis=0, concat_axis=0, tiled=True)  7.49 us
    all_to_all x1, starting transfers between devices, body(): lax.all_to_all(pieces, 'row', split_axis=0, concat_axis=0, tiled=True)  6.7 us
  transfers between devices with their start and end apart: 12, of which 8 were waited for; matrix products, arithmetic and copies ran while one was open for 2% of the time, Pallas kernels for 7%

profile of v13, /device:TPU:15, one launch (start us, length us, event | category | flops | bytes accessed | tf_op | source)
XLA Modules:
  0.0 116.4 jit_solution(8950095933606104155)
XLA Ops:
  0.6 4.9 %fetch.1 = (bf16[16,40,1024]{2,1,0:T(8,128)(2,1)}, s32[1]{0:T(128)}) custom-call(s32[16]{0:T(128)} %dealing.9, s32[16]{0:T(128)} %cols.5, f32[2,40,32768]{2,1,0:T(8,128)} %tile.1), custom_call_target="tpu_custom_call" | custom-call | bytes 6291456 | tf_op jit(solution)/shard_map/fetch/pallas_call | solution.py:93
  5.5 0.0 copy-start.1
  5.6 0.0 copy-start.5
  5.6 0.0 copy-start.6
  5.6 6.7 %all-to-all-start = ((bf16[16,40,1024]{2,1,0:T(8,128)(2,1)}), bf16[16,40,1024]{2,1,0:T(8,128)(2,1)S(1)}, u32[]{:S(2)}, u32[]{:S(2)}) async-start(bf16[16,40,1024]{2,1,0:T(8,128)(2,1)} %get-tuple-element.18), calls=%async_computation | async-start | bytes 2621440 | tf_op jit(solution)/shard_map/all_to_all | solution.py:494
  12.3 0.0 copy-done.1
  12.3 0.0 copy-done.5
  12.3 0.0 copy-done.6
  12.3 0.0 copy-start.2
  12.3 1.6 %copy-done.2 = bf16[1024,1024]{1,0:T(8,128)(2,1)S(1)} copy-done((bf16[1024,1024]{1,0:T(8,128)(2,1)S(1)}, bf16[1024,1024]{1,0:T(8,128)(2,1)}, u32[]{:S(2)}) %copy-start.2) | copy-done | bytes 2097176
  13.9 0.0 copy-start.3
  13.9 1.2 %copy-done.3 = bf16[2,512,512]{2,1,0:T(8,128)(2,1)S(1)} copy-done((bf16[2,512,512]{2,1,0:T(8,128)(2,1)S(1)}, bf16[2,512,512]{2,1,0:T(8,128)(2,1)}, u32[]{:S(2)}) %copy-start.3) | copy-done | bytes 1048600
  15.1 0.0 copy-start.4
  15.1 1.0 copy-done.4
  16.2 0.0 copy-start.7
  16.2 6.4 %prepare.1 = (f32[2,40,32768]{2,1,0:T(8,128)}, s32[80]{0:T(128)S(1)}, s32[80]{0:T(128)S(1)}, s32[16]{0:T(128)S(1)}, bf16[14336,1024]{1,0:T(8,128)(2,1)S(1)}) custom-call(s32[16]{0:T(128)S(1)} %copy-done.5, s32[16]{0:T(128)S(1)} %copy-done.6, s32[1]{0:T(128)} %get-tuple-element.14.token, bf16[1024,1024]{1,0:T(8,128)(2,1)S(1)} %copy-done.1, ...), custom_call_target="tpu_custom_call" | custom-call | bytes 115343360 | tf_op jit(solution)/shard_map/prepare/pallas_call | solution.py:181
  22.6 0.0 copy-start
  22.6 9.7 %copy-done = bf16[14336,1024]{1,0:T(8,128)(2,1)} copy-done((bf16[14336,1024]{1,0:T(8,128)(2,1)}, bf16[14336,1024]{1,0:T(8,128)(2,1)S(1)}, u32[]{:S(2)}) %copy-start) | copy-done | bytes 29360152
  32.3 10.6 %all-to-all-done = bf16[16,40,1024]{2,1,0:T(8,128)(2,1)S(1)} async-done(((bf16[16,40,1024]{2,1,0:T(8,128)(2,1)}), bf16[16,40,1024]{2,1,0:T(8,128)(2,1)S(1)}, u32[]{:S(2)}, u32[]{:S(2)}) %all-to-all-start) | async-done | bytes 1310752 | tf_op jit(solution)/shard_map/all_to_all | solution.py:494
  42.8 0.0 copy-done.7
  42.8 8.8 %slot.1 = (bf16[512,1024]{1,0:T(8,128)(2,1)S(1)}, f32[256,1024]{1,0:T(8,128)S(1)}, bf16[256,1024]{1,0:T(8,128)(2,1)}) custom-call(s32[16]{0:T(128)S(1)} %copy-done.5, s32[16]{0:T(128)S(1)} %copy-done.7, s32[80]{0:T(128)S(1)} %get-tuple-element.16.owners, bf16[640,1024]{1,0:T(8,128)(2,1)S(1)} %bitcast.5, bf16[14336,1024]{1,0:T(8,128)(2,1)} %copy-done), custom_call_target="tpu_custom_call" | custom-call | flops 4294967296 | bytes 8388608 | tf_op jit(solution)/shard_map/slot/pallas_call | solution.py:293
  51.7 0.3 collective-permute-start
  52.0 2.0 %collective-permute-done = bf16[256,1024]{1,0:T(8,128)(2,1)} collective-permute-done((bf16[256,1024]{1,0:T(8,128)(2,1)}, bf16[256,1024]{1,0:T(8,128)(2,1)}, u32[]{:S(2)}, u32[]{:S(2)}) %collective-permute-start) | collective-permute-done | bytes 524320 | tf_op jit(solution)/shard_map/ppermute | solution.py:452
  54.0 1.2 %convert_add_fusion = f32[256,1024]{1,0:T(8,128)S(1)} fusion(f32[256,1024]{1,0:T(8,128)S(1)} %get-tuple-element.21, bf16[256,1024]{1,0:T(8,128)(2,1)} %collective-permute-done), kind=kLoop, calls=%fused_computation.4 | loop fusion | flops 524288 | bytes 2621440 | tf_op jit(solution)/shard_map/add | solution.py:457
  55.3 0.1 collective-permute-start.1
  55.4 7.6 %collective-permute-done.1 = bf16[128,1024]{1,0:T(8,128)(2,1)S(1)} collective-permute-done((bf16[128,1024]{1,0:T(8,128)(2,1)S(1)}, bf16[128,1024]{1,0:T(8,128)(2,1)S(1)}, u32[]{:S(2)}, u32[]{:S(2)}) %collective-permute-start.1) | collective-permute-done | bytes 262176 | tf_op jit(solution)/shard_map/ppermute | solution.py:452
  63.1 0.1 convert_add_fusion.1
  63.2 0.4 collective-permute-start.4
  63.6 0.8 collective-permute-start.3
  64.4 1.5 %collective-permute-start.2 = (bf16[32,1024]{1,0:T(8,128)(2,1)S(1)}, bf16[32,1024]{1,0:T(8,128)(2,1)S(1)}, u32[]{:S(2)}, u32[]{:S(2)}) collective-permute-start(bf16[32,1024]{1,0:T(8,128)(2,1)S(1)} %get-tuple-element.32), channel_id=1, source_target_pairs={{0,4},{1,5},{2,6},{3,7},{4,0},{5,1},{6,2},{7,3},{8,12},{9,13},{10,... | collective-permute-start | bytes 196616 | tf_op jit(solution)/shard_map/ppermute | solution.py:452
  65.9 2.2 %pack.1 = bf16[16,40,1024]{2,1,0:T(8,128)(2,1)} custom-call(s32[16]{0:T(128)S(1)} %copy-done.5, s32[16]{0:T(128)S(1)} %copy-done.7, bf16[512,1024]{1,0:T(8,128)(2,1)S(1)} %get-tuple-element.20.term), custom_call_target="tpu_custom_call" | custom-call | bytes 3145728 | tf_op jit(solution)/shard_map/pack/pallas_call | solution.py:340
  68.1 0.3 collective-permute-done.4
  68.4 0.0 collective-permute-done.3
  68.4 1.1 collective-permute-done.2
  69.5 0.9 collective-permute-start.5
  70.4 3.4 %collective-permute-start.6 = (bf16[32,1024]{1,0:T(8,128)(2,1)S(1)}, bf16[32,1024]{1,0:T(8,128)(2,1)S(1)}, u32[]{:S(2)}, u32[]{:S(2)}) collective-permute-start(bf16[32,1024]{1,0:T(8,128)(2,1)S(1)} %multiply_convert_fusion), channel_id=1, source_target_pairs={{0,8},{1,9},{2,10},{3,11},{4,12},{5,13},{6,14},{7,15},{8,0},{9,1},... | collective-permute-start | bytes 196616 | tf_op jit(solution)/shard_map/ppermute | solution.py:452
  73.9 0.0 collective-permute-start.7
  73.9 7.5 %all-to-all-start.1 = ((bf16[16,40,1024]{2,1,0:T(8,128)(2,1)}), bf16[16,40,1024]{2,1,0:T(8,128)(2,1)S(1)}, u32[]{:S(2)}, u32[]{:S(2)}) async-start(bf16[16,40,1024]{2,1,0:T(8,128)(2,1)} %pack.1), calls=%async_computation.1 | async-start | bytes 2621440 | tf_op jit(solution)/shard_map/all_to_all | solution.py:503
  81.4 0.0 collective-permute-done.5
  81.4 0.0 collective-permute-done.6
  81.4 0.0 collective-permute-done.7
  81.5 0.3 collective-permute-start.8
  81.8 13.5 %collective-permute-done.8 = bf16[128,1024]{1,0:T(8,128)(2,1)S(1)} collective-permute-done((bf16[128,1024]{1,0:T(8,128)(2,1)S(1)}, bf16[128,1024]{1,0:T(8,128)(2,1)S(1)}, u32[]{:S(2)}, u32[]{:S(2)}) %collective-permute-start.8) | collective-permute-done | bytes 262176 | tf_op jit(solution)/shard_map/ppermute | solution.py:452
  95.3 0.1 broadcast_select_fusion.3
  95.5 2.6 %collective-permute-start.9 = (bf16[256,1024]{1,0:T(8,128)(2,1)S(1)}, bf16[256,1024]{1,0:T(8,128)(2,1)S(1)}, u32[]{:S(2)}, u32[]{:S(2)}) collective-permute-start(bf16[256,1024]{1,0:T(8,128)(2,1)S(1)} %pad_maximum_fusion.1), channel_id=1, source_target_pairs={{0,1},{1,0},{2,3},{3,2},{4,5},{5,4},{6,7},{7,6},{8,9},{9,8},{10,11... | collective-permute-start | bytes 1572872 | tf_op jit(solution)/shard_map/ppermute | solution.py:452
  98.1 1.5 %collective-permute-done.9 = bf16[256,1024]{1,0:T(8,128)(2,1)S(1)} collective-permute-done((bf16[256,1024]{1,0:T(8,128)(2,1)S(1)}, bf16[256,1024]{1,0:T(8,128)(2,1)S(1)}, u32[]{:S(2)}, u32[]{:S(2)}) %collective-permute-start.9) | collective-permute-done | bytes 524320 | tf_op jit(solution)/shard_map/ppermute | solution.py:452
  99.7 0.2 broadcast_select_fusion.1
  99.9 0.2 maximum_convert_fusion
  100.2 0.2 slice_bitcast_fusion.1
  100.4 1.5 %pad_maximum_fusion = f32[2,512,512]{2,1,0:T(8,128)} fusion(f32[1,512,512]{2,1,0:T(8,128)S(1)} %get-tuple-element.27, f32[1,512,512]{2,1,0:T(8,128)S(1)} %get-tuple-element.26), kind=kLoop, calls=%fused_computation | loop fusion | flops 524288 | bytes 4194304 | tf_op jit(solution)/shard_map/stack | solution.py:506
  101.8 10.1 %all-to-all-done.1.terms = bf16[16,40,1024]{2,1,0:T(8,128)(2,1)S(1)} async-done(((bf16[16,40,1024]{2,1,0:T(8,128)(2,1)}), bf16[16,40,1024]{2,1,0:T(8,128)(2,1)S(1)}, u32[]{:S(2)}, u32[]{:S(2)}) %all-to-all-start.1) | async-done | bytes 1310752 | tf_op jit(solution)/shard_map/all_to_all | solution.py:503
  111.9 4.4 %place.1 = f32[2,40,32768]{2,1,0:T(8,128)} custom-call(s32[16]{0:T(128)S(1)} %copy-done.5, s32[16]{0:T(128)S(1)} %copy-done.6, s32[80]{0:T(128)S(1)} %get-tuple-element.15.blocks, s32[80]{0:T(128)S(1)} %get-tuple-element.16.owners, s32[16]{0:T(128)S(1)} %get-tuple-element.17.single, ...), custom_call_target="tpu_custom_call", output_to_operand_aliasing={{}: (6, {})} | custom-call | bytes 6291456 | tf_op jit(solution)/shard_map/place/pallas_call | solution.py:426
  (7 shorter events, 0.2 us)
Async XLA Ops:
  5.5 6.7 %copy-start.1 = (bf16[1024,1024]{1,0:T(8,128)(2,1)S(1)}, bf16[1024,1024]{1,0:T(8,128)(2,1)}, u32[]{:S(2)}) copy-start(bf16[1024,1024]{1,0:T(8,128)(2,1)} %constant.81.clone.right) | copy-start | bytes 6291460
  5.6 6.7 %copy-start.5 = (s32[16]{0:T(128)S(1)}, s32[16]{0:T(128)}, u32[]{:S(2)}) copy-start(s32[16]{0:T(128)} %dealing.9) | copy-start | bytes 196
  5.6 6.7 %copy-start.6 = (s32[16]{0:T(128)S(1)}, s32[16]{0:T(128)}, u32[]{:S(2)}) copy-start(s32[16]{0:T(128)} %cols.5) | copy-start | bytes 196
  5.6 37.3 %all-to-all-start = ((bf16[16,40,1024]{2,1,0:T(8,128)(2,1)}), bf16[16,40,1024]{2,1,0:T(8,128)(2,1)S(1)}, u32[]{:S(2)}, u32[]{:S(2)}) async-start(bf16[16,40,1024]{2,1,0:T(8,128)(2,1)} %get-tuple-element.18), calls=%async_computation | async-start | bytes 2621440 | tf_op jit(solution)/shard_map/all_to_all | solution.py:494
  12.3 1.6 %copy-start.2 = (bf16[1024,1024]{1,0:T(8,128)(2,1)S(1)}, bf16[1024,1024]{1,0:T(8,128)(2,1)}, u32[]{:S(2)}) copy-start(bf16[1024,1024]{1,0:T(8,128)(2,1)} %constant.82.clone.left) | copy-start | bytes 6291460
  13.9 1.2 %copy-start.3 = (bf16[2,512,512]{2,1,0:T(8,128)(2,1)S(1)}, bf16[2,512,512]{2,1,0:T(8,128)(2,1)}, u32[]{:S(2)}) copy-start(bf16[2,512,512]{2,1,0:T(8,128)(2,1)} %probe.1) | copy-start | bytes 3145732
  15.1 1.0 copy-start.4
  16.2 26.7 %copy-start.7 = (s32[16]{0:T(128)S(1)}, s32[16]{0:T(128)}, u32[]{:S(2)}) copy-start(s32[16]{0:T(128)} %rows.3) | copy-start | bytes 196
  22.6 9.7 %copy-start = (bf16[14336,1024]{1,0:T(8,128)(2,1)}, bf16[14336,1024]{1,0:T(8,128)(2,1)S(1)}, u32[]{:S(2)}) copy-start(bf16[14336,1024]{1,0:T(8,128)(2,1)S(1)} %get-tuple-element.19.stock) | copy-start | bytes 88080384
  51.7 2.3 %collective-permute-start = (bf16[256,1024]{1,0:T(8,128)(2,1)}, bf16[256,1024]{1,0:T(8,128)(2,1)}, u32[]{:S(2)}, u32[]{:S(2)}) collective-permute-start(bf16[256,1024]{1,0:T(8,128)(2,1)} %get-tuple-element.22), channel_id=1, source_target_pairs={{0,1},{1,0},{2,3},{3,2},{4,5},{5,4},{6,7},{7,6},{8,9},{9,8},{10,11... | collective-permute-start | bytes 1572872 | tf_op jit(solution)/shard_map/ppermute | solution.py:452
  55.3 7.8 %collective-permute-start.1 = (bf16[128,1024]{1,0:T(8,128)(2,1)S(1)}, bf16[128,1024]{1,0:T(8,128)(2,1)S(1)}, u32[]{:S(2)}, u32[]{:S(2)}) collective-permute-start(bf16[128,1024]{1,0:T(8,128)(2,1)S(1)} %dynamic-slice_convert_fusion), channel_id=1, source_target_pairs={{0,2},{1,3},{2,0},{3,1},{4,6},{5,7},{6,4},{7,5},{8,10},{9,11},{10,... | collective-permute-start | bytes 786440 | tf_op jit(solution)/shard_map/ppermute | solution.py:452
  63.2 5.2 %collective-permute-start.4 = (bf16[32,1024]{1,0:T(8,128)(2,1)S(1)}, bf16[32,1024]{1,0:T(8,128)(2,1)S(1)}, u32[]{:S(2)}, u32[]{:S(2)}) collective-permute-start(bf16[32,1024]{1,0:T(8,128)(2,1)S(1)} %get-tuple-element.33), channel_id=1, source_target_pairs={{0,12},{1,13},{2,14},{3,15},{4,8},{5,9},{6,10},{7,11},{8,4},{9,5},... | collective-permute-start | bytes 196616 | tf_op jit(solution)/shard_map/ppermute | solution.py:452
  63.6 4.8 %collective-permute-start.3 = (bf16[32,1024]{1,0:T(8,128)(2,1)S(1)}, bf16[32,1024]{1,0:T(8,128)(2,1)S(1)}, u32[]{:S(2)}, u32[]{:S(2)}) collective-permute-start(bf16[32,1024]{1,0:T(8,128)(2,1)S(1)} %get-tuple-element.34), channel_id=1, source_target_pairs={{0,8},{1,9},{2,10},{3,11},{4,12},{5,13},{6,14},{7,15},{8,0},{9,1},... | collective-permute-start | bytes 196616 | tf_op jit(solution)/shard_map/ppermute | solution.py:452
  64.4 5.1 %collective-permute-start.2 = (bf16[32,1024]{1,0:T(8,128)(2,1)S(1)}, bf16[32,1024]{1,0:T(8,128)(2,1)S(1)}, u32[]{:S(2)}, u32[]{:S(2)}) collective-permute-start(bf16[32,1024]{1,0:T(8,128)(2,1)S(1)} %get-tuple-element.32), channel_id=1, source_target_pairs={{0,4},{1,5},{2,6},{3,7},{4,0},{5,1},{6,2},{7,3},{8,12},{9,13},{10,... | collective-permute-start | bytes 196616 | tf_op jit(solution)/shard_map/ppermute | solution.py:452
  69.5 11.9 %collective-permute-start.5 = (bf16[32,1024]{1,0:T(8,128)(2,1)S(1)}, bf16[32,1024]{1,0:T(8,128)(2,1)S(1)}, u32[]{:S(2)}, u32[]{:S(2)}) collective-permute-start(bf16[32,1024]{1,0:T(8,128)(2,1)S(1)} %multiply_convert_fusion), channel_id=1, source_target_pairs={{0,12},{1,13},{2,14},{3,15},{4,8},{5,9},{6,10},{7,11},{8,4},{9,5},... | collective-permute-start | bytes 196616 | tf_op jit(solution)/shard_map/ppermute | solution.py:452
  70.4 10.9 %collective-permute-start.6 = (bf16[32,1024]{1,0:T(8,128)(2,1)S(1)}, bf16[32,1024]{1,0:T(8,128)(2,1)S(1)}, u32[]{:S(2)}, u32[]{:S(2)}) collective-permute-start(bf16[32,1024]{1,0:T(8,128)(2,1)S(1)} %multiply_convert_fusion), channel_id=1, source_target_pairs={{0,8},{1,9},{2,10},{3,11},{4,12},{5,13},{6,14},{7,15},{8,0},{9,1},... | collective-permute-start | bytes 196616 | tf_op jit(solution)/shard_map/ppermute | solution.py:452
  73.9 7.5 %collective-permute-start.7 = (bf16[32,1024]{1,0:T(8,128)(2,1)S(1)}, bf16[32,1024]{1,0:T(8,128)(2,1)S(1)}, u32[]{:S(2)}, u32[]{:S(2)}) collective-permute-start(bf16[32,1024]{1,0:T(8,128)(2,1)S(1)} %multiply_convert_fusion), channel_id=1, source_target_pairs={{0,4},{1,5},{2,6},{3,7},{4,0},{5,1},{6,2},{7,3},{8,12},{9,13},{10,... | collective-permute-start | bytes 196616 | tf_op jit(solution)/shard_map/ppermute | solution.py:452
  73.9 38.1 %all-to-all-start.1 = ((bf16[16,40,1024]{2,1,0:T(8,128)(2,1)}), bf16[16,40,1024]{2,1,0:T(8,128)(2,1)S(1)}, u32[]{:S(2)}, u32[]{:S(2)}) async-start(bf16[16,40,1024]{2,1,0:T(8,128)(2,1)} %pack.1), calls=%async_computation.1 | async-start | bytes 2621440 | tf_op jit(solution)/shard_map/all_to_all | solution.py:503
  81.5 13.9 %collective-permute-start.8 = (bf16[128,1024]{1,0:T(8,128)(2,1)S(1)}, bf16[128,1024]{1,0:T(8,128)(2,1)S(1)}, u32[]{:S(2)}, u32[]{:S(2)}) collective-permute-start(bf16[128,1024]{1,0:T(8,128)(2,1)S(1)} %pad_maximum_fusion.2), channel_id=1, source_target_pairs={{0,2},{1,3},{2,0},{3,1},{4,6},{5,7},{6,4},{7,5},{8,10},{9,11},{10,... | collective-permute-start | bytes 786440 | tf_op jit(solution)/shard_map/ppermute | solution.py:452
  95.5 4.2 %collective-permute-start.9 = (bf16[256,1024]{1,0:T(8,128)(2,1)S(1)}, bf16[256,1024]{1,0:T(8,128)(2,1)S(1)}, u32[]{:S(2)}, u32[]{:S(2)}) collective-permute-start(bf16[256,1024]{1,0:T(8,128)(2,1)S(1)} %pad_maximum_fusion.1), channel_id=1, source_target_pairs={{0,1},{1,0},{2,3},{3,2},{4,5},{5,4},{6,7},{7,6},{8,9},{9,8},{10,11... | collective-permute-start | bytes 1572872 | tf_op jit(solution)/shard_map/ppermute | solution.py:452

commit v14 on v13

--- a/solution.py
+++ b/solution.py
@@ -52,13 +52,16 @@
     tile_cols = tile.shape[2]
     span = order + LANES
 
-    def copy(slot):
+    def copy(slot, part):
         base, _ = window_start(cols[dealing[slot]], order, tile_cols)
-        return pltpu.make_async_copy(tile.at[:, :, pl.ds(base, span)], held.at[slot], sems.at[slot])
+        return pltpu.make_async_copy(
+            tile.at[part, :, pl.ds(base, span)], held.at[slot, part], sems.at[slot, part]
+        )
 
     @pl.loop(0, slots)
     def _(slot):
-        copy(slot).start()
+        copy(slot, 0).start()
+        copy(slot, 1).start()
 
     lane = lax.broadcasted_iota(jnp.int32, (tile_rows, LANES), 1)
 
@@ -67,10 +70,10 @@
 
     @pl.loop(0, slots, unroll=4)
     def _(slot):
-        copy(slot).wait()
         _, offset = window_start(cols[dealing[slot]], order, tile_cols)
         shift = lax.rem(LANES - lax.rem(offset, LANES), LANES)
         for part in range(2):
+            copy(slot, part).wait()
             turned = [
                 pltpu.roll(held[slot, part, :, b * LANES : (b + 1) * LANES].astype(out.dtype), shift, 1)
                 for b in range(span // LANES)
@@ -101,7 +104,7 @@
         scratch_shapes=[
             pltpu.VMEM((slots, 2, tile_rows, span), jnp.float32),
             pltpu.VMEM((slots, tile_rows, 2 * order), jnp.bfloat16),
-            pltpu.SemaphoreType.DMA((slots,)),
+            pltpu.SemaphoreType.DMA((slots, 2)),
             pltpu.SemaphoreType.DMA((slots,)),
         ],
         compiler_params=pltpu.CompilerParams(vmem_limit_bytes=56 * 2**20),
@@ -226,40 +229,38 @@
     wide[total_rows:, :] = jnp.zeros((SUBLANES, 2 * order), jnp.float32)
     loads[0].wait()
     loads[1].wait()
-    loads[2].wait()
+
+    @pl.loop(0, order // step)
+    def _(i):
+        place = pl.ds(pl.multiple_of(i * step, step), step)
+        found = rows_from(wide, first_row + i * step, step)
+        patch[place, :] = found.astype(patch.dtype)
+        real, imag = found[:, :order], found[:, order:]
+        probe_real = probe[0, place, :].astype(jnp.float32)
+        probe_imag = probe[1, place, :].astype(jnp.float32)
+        wave[place, :order] = (probe_real * real - probe_imag * imag).astype(wave.dtype)
+        wave[place, order:] = (probe_real * imag + probe_imag * real).astype(wave.dtype)
 
     def dot(a, b):
         return jnp.dot(a, b, preferred_element_type=jnp.float32)
 
-    for top in range(0, order, tile):
-        for start in range(top, top + tile, step):
-            line = slice(start, start + step)
-            found = rows_from(wide, first_row + start, step)
-            patch[line, :] = found.astype(patch.dtype)
-            real, imag = found[:, :order], found[:, order:]
-            probe_real = probe[0, line, :].astype(jnp.float32)
-            probe_imag = probe[1, line, :].astype(jnp.float32)
-            wave[line, :order] = (probe_real * real - probe_imag * imag).astype(wave.dtype)
-            wave[line, order:] = (probe_real * imag + probe_imag * real).astype(wave.dtype)
-        line = slice(top, top + tile)
-        for first in range(0, order, tile):
-            here = slice(first, first + tile)
-            there = slice(order + first, order + first + tile)
-            half[line, here] = dot(wave[line, :], right[:, here]).astype(half.dtype)
-            half[order + top : order + top + tile, here] = dot(wave[line, :], right[:, there]).astype(half.dtype)
+    loads[2].wait()
+    for first in range(0, order, tile):
+        here = slice(first, first + tile)
+        there = slice(order + first, order + first + tile)
+        half[:order, here] = dot(wave[...], right[:, here]).astype(half.dtype)
+        half[order:, here] = dot(wave[...], right[:, there]).astype(half.dtype)
     loads[3].wait()
     loads[4].wait()
     for first in range(0, order, tile):
         here = slice(first, first + tile)
         there = slice(order + first, order + first + tile)
-        for top in range(0, order, tile):
-            line = slice(top, top + tile)
-            real = dot(left[line, :], half[:, here])
-            imag = dot(left[order + top : order + top + tile, :], half[:, here])
-            inverse = jnp.minimum(lax.rsqrt(real * real + imag * imag), 1.0 / MAG_FLOOR)
-            shrink = 1.0 - measured[line, here].astype(jnp.float32) * inverse
-            resid[line, here] = (real * shrink).astype(resid.dtype)
-            resid[line, there] = (imag * shrink).astype(resid.dtype)
+        far = dot(left[...], half[:, here])
+        real, imag = far[:order], far[order:]
+        inverse = jnp.minimum(lax.rsqrt(real * real + imag * imag), 1.0 / MAG_FLOOR)
+        shrink = 1.0 - measured[:, here].astype(jnp.float32) * inverse
+        resid[:, here] = (real * shrink).astype(resid.dtype)
+        resid[:, there] = (imag * shrink).astype(resid.dtype)
     for first in range(0, order, tile):
         here = slice(first, first + tile)
         there = slice(order + first, order + first + tile)
@@ -268,18 +269,16 @@
     for first in range(0, order, tile):
         here = slice(first, first + tile)
         there = slice(order + first, order + first + tile)
-        for top in range(0, order, tile):
-            line = slice(top, top + tile)
-            real = dot(right[line, :], turned[:, here])
-            imag = dot(right[order + top : order + top + tile, :], turned[:, here])
-            probe_real = probe[0, line, here].astype(jnp.float32)
-            probe_imag = probe[1, line, here].astype(jnp.float32)
-            term[line, here] = (probe_real * real + probe_imag * imag).astype(term.dtype)
-            term[line, there] = (probe_real * imag - probe_imag * real).astype(term.dtype)
-            patch_real = patch[line, here].astype(jnp.float32)
-            patch_imag = patch[line, there].astype(jnp.float32)
-            mine[line, here] = patch_real * real + patch_imag * imag
-            mine[line, there] = patch_real * imag - patch_imag * real
+        back = dot(right[...], turned[:, here])
+        real, imag = back[:order], back[order:]
+        probe_real = probe[0, :, here].astype(jnp.float32)
+        probe_imag = probe[1, :, here].astype(jnp.float32)
+        term[:, here] = (probe_real * real + probe_imag * imag).astype(term.dtype)
+        term[:, there] = (probe_real * imag - probe_imag * real).astype(term.dtype)
+        patch_real = patch[:, here].astype(jnp.float32)
+        patch_imag = patch[:, there].astype(jnp.float32)
+        mine[:, here] = patch_real * real + patch_imag * imag
+        mine[:, there] = patch_real * imag - patch_imag * real
 
     count = kept.shape[0]
     side = lax.rem(me, 2)

time: 117 us -> 118 us (level)
  Pallas kernels: 26.8 us -> 28.1 us
where the time goes in v14:
time: 118 us
  waiting for transfers between devices  46.8 us (40%)
  Pallas kernels  28.1 us (24%)
  starting transfers between devices  24.6 us (21%)
  local copies, waits for them, and re-layouts  13.8 us (12%)
  other arithmetic  3.5 us (3%)
    ppermute x10, waiting for transfers between devices, swap(): return lax.ppermute(x, 'row', [(d, d ^ distance) for d in range(devices)])  26.1 us
    unnamed x16, local copies, waits for them, and re-layouts  13.6 us
    all_to_all x1, waiting for transfers between devices, body(): lax.all_to_all(pieces, 'row', split_axis=0, concat_axis=0, tiled=True)  10.6 us
    ppermute x10, starting transfers between devices, swap(): return lax.ppermute(x, 'row', [(d, d ^ distance) for d in range(devices)])  10.4 us
    all_to_all x1, waiting for transfers between devices, body(): lax.all_to_all(terms, 'row', split_axis=0, concat_axis=0, tiled=True)  10.1 us
    pallas_call x1, Pallas kernels, slot_terms(): pl.pallas_call(slot_kernel, out_shape=(jax.ShapeDtypeStruct((order, wide_...  9.2 us
    all_to_all x1, starting transfers between devices, body(): lax.all_to_all(terms, 'row', split_axis=0, concat_axis=0, tiled=True)  7.49 us
    all_to_all x1, starting transfers between devices, body(): lax.all_to_all(pieces, 'row', split_axis=0, concat_axis=0, tiled=True)  6.7 us
  transfers between devices with their start and end apart: 12, of which 8 were waited for; matrix products, arithmetic and copies ran while one was open for 2% of the time, Pallas kernels for 7%

profile of v14, /device:TPU:15, one launch (start us, length us, event | category | flops | bytes accessed | tf_op | source)
XLA Modules:
  0.0 117.7 jit_solution(13955775729835214484)
XLA Ops:
  0.6 6.0 %fetch.1 = (bf16[16,40,1024]{2,1,0:T(8,128)(2,1)}, s32[1]{0:T(128)}) custom-call(s32[16]{0:T(128)} %dealing.9, s32[16]{0:T(128)} %cols.5, f32[2,40,32768]{2,1,0:T(8,128)} %tile.1), custom_call_target="tpu_custom_call" | custom-call | bytes 6291456 | tf_op jit(solution)/shard_map/fetch/pallas_call | solution.py:96
  6.6 0.0 copy-start.1
  6.7 0.0 copy-start.5
  6.7 0.0 copy-start.6
  6.7 6.7 %all-to-all-start = ((bf16[16,40,1024]{2,1,0:T(8,128)(2,1)}), bf16[16,40,1024]{2,1,0:T(8,128)(2,1)S(1)}, u32[]{:S(2)}, u32[]{:S(2)}) async-start(bf16[16,40,1024]{2,1,0:T(8,128)(2,1)} %get-tuple-element.18), calls=%async_computation | async-start | bytes 2621440 | tf_op jit(solution)/shard_map/all_to_all | solution.py:493
  13.4 0.0 copy-done.1
  13.4 0.0 copy-done.5
  13.4 0.0 copy-done.6
  13.4 0.0 copy-start.2
  13.4 1.6 %copy-done.2 = bf16[1024,1024]{1,0:T(8,128)(2,1)S(1)} copy-done((bf16[1024,1024]{1,0:T(8,128)(2,1)S(1)}, bf16[1024,1024]{1,0:T(8,128)(2,1)}, u32[]{:S(2)}) %copy-start.2) | copy-done | bytes 2097176
  15.0 0.0 copy-start.3
  15.0 1.2 %copy-done.3 = bf16[2,512,512]{2,1,0:T(8,128)(2,1)S(1)} copy-done((bf16[2,512,512]{2,1,0:T(8,128)(2,1)S(1)}, bf16[2,512,512]{2,1,0:T(8,128)(2,1)}, u32[]{:S(2)}) %copy-start.3) | copy-done | bytes 1048600
  16.2 0.0 copy-start.4
  16.2 1.0 copy-done.4
  17.3 0.0 copy-start.7
  17.3 6.4 %prepare.1 = (f32[2,40,32768]{2,1,0:T(8,128)}, s32[80]{0:T(128)S(1)}, s32[80]{0:T(128)S(1)}, s32[16]{0:T(128)S(1)}, bf16[14336,1024]{1,0:T(8,128)(2,1)S(1)}) custom-call(s32[16]{0:T(128)S(1)} %copy-done.5, s32[16]{0:T(128)S(1)} %copy-done.6, s32[1]{0:T(128)} %get-tuple-element.14.token, bf16[1024,1024]{1,0:T(8,128)(2,1)S(1)} %copy-done.1, ...), custom_call_target="tpu_custom_call" | custom-call | bytes 115343360 | tf_op jit(solution)/shard_map/prepare/pallas_call | solution.py:184
  23.7 0.0 copy-start
  23.7 9.7 %copy-done = bf16[14336,1024]{1,0:T(8,128)(2,1)} copy-done((bf16[14336,1024]{1,0:T(8,128)(2,1)}, bf16[14336,1024]{1,0:T(8,128)(2,1)S(1)}, u32[]{:S(2)}) %copy-start) | copy-done | bytes 29360152
  33.4 10.6 %all-to-all-done = bf16[16,40,1024]{2,1,0:T(8,128)(2,1)S(1)} async-done(((bf16[16,40,1024]{2,1,0:T(8,128)(2,1)}), bf16[16,40,1024]{2,1,0:T(8,128)(2,1)S(1)}, u32[]{:S(2)}, u32[]{:S(2)}) %all-to-all-start) | async-done | bytes 1310752 | tf_op jit(solution)/shard_map/all_to_all | solution.py:493
  44.0 0.0 copy-done.7
  44.0 9.2 %slot.1 = (bf16[512,1024]{1,0:T(8,128)(2,1)S(1)}, f32[256,1024]{1,0:T(8,128)S(1)}, bf16[256,1024]{1,0:T(8,128)(2,1)}) custom-call(s32[16]{0:T(128)S(1)} %copy-done.5, s32[16]{0:T(128)S(1)} %copy-done.7, s32[80]{0:T(128)S(1)} %get-tuple-element.16.owners, bf16[640,1024]{1,0:T(8,128)(2,1)S(1)} %bitcast.5, bf16[14336,1024]{1,0:T(8,128)(2,1)} %copy-done), custom_call_target="tpu_custom_call" | custom-call | flops 4294967296 | bytes 8388608 | tf_op jit(solution)/shard_map/slot/pallas_call | solution.py:292
  53.2 0.3 collective-permute-start
  53.4 2.0 %collective-permute-done = bf16[256,1024]{1,0:T(8,128)(2,1)} collective-permute-done((bf16[256,1024]{1,0:T(8,128)(2,1)}, bf16[256,1024]{1,0:T(8,128)(2,1)}, u32[]{:S(2)}, u32[]{:S(2)}) %collective-permute-start) | collective-permute-done | bytes 524320 | tf_op jit(solution)/shard_map/ppermute | solution.py:451
  55.5 1.2 %convert_add_fusion = f32[256,1024]{1,0:T(8,128)S(1)} fusion(f32[256,1024]{1,0:T(8,128)S(1)} %get-tuple-element.21, bf16[256,1024]{1,0:T(8,128)(2,1)} %collective-permute-done), kind=kLoop, calls=%fused_computation.4 | loop fusion | flops 524288 | bytes 2621440 | tf_op jit(solution)/shard_map/add | solution.py:456
  56.8 0.1 collective-permute-start.1
  56.9 7.6 %collective-permute-done.1 = bf16[128,1024]{1,0:T(8,128)(2,1)S(1)} collective-permute-done((bf16[128,1024]{1,0:T(8,128)(2,1)S(1)}, bf16[128,1024]{1,0:T(8,128)(2,1)S(1)}, u32[]{:S(2)}, u32[]{:S(2)}) %collective-permute-start.1) | collective-permute-done | bytes 262176 | tf_op jit(solution)/shard_map/ppermute | solution.py:451
  64.5 0.1 convert_add_fusion.1
  64.6 0.4 collective-permute-start.4
  65.1 0.8 collective-permute-start.3
  65.9 1.5 %collective-permute-start.2 = (bf16[32,1024]{1,0:T(8,128)(2,1)S(1)}, bf16[32,1024]{1,0:T(8,128)(2,1)S(1)}, u32[]{:S(2)}, u32[]{:S(2)}) collective-permute-start(bf16[32,1024]{1,0:T(8,128)(2,1)S(1)} %get-tuple-element.32), channel_id=1, source_target_pairs={{0,4},{1,5},{2,6},{3,7},{4,0},{5,1},{6,2},{7,3},{8,12},{9,13},{10,... | collective-permute-start | bytes 196616 | tf_op jit(solution)/shard_map/ppermute | solution.py:451
  67.3 2.2 %pack.1 = bf16[16,40,1024]{2,1,0:T(8,128)(2,1)} custom-call(s32[16]{0:T(128)S(1)} %copy-done.5, s32[16]{0:T(128)S(1)} %copy-done.7, bf16[512,1024]{1,0:T(8,128)(2,1)S(1)} %get-tuple-element.20.term), custom_call_target="tpu_custom_call" | custom-call | bytes 3145728 | tf_op jit(solution)/shard_map/pack/pallas_call | solution.py:339
  69.5 0.3 collective-permute-done.4
  69.9 0.0 collective-permute-done.3
  69.9 1.1 collective-permute-done.2
  71.0 0.9 collective-permute-start.5
  71.9 3.4 %collective-permute-start.6 = (bf16[32,1024]{1,0:T(8,128)(2,1)S(1)}, bf16[32,1024]{1,0:T(8,128)(2,1)S(1)}, u32[]{:S(2)}, u32[]{:S(2)}) collective-permute-start(bf16[32,1024]{1,0:T(8,128)(2,1)S(1)} %multiply_convert_fusion), channel_id=1, source_target_pairs={{0,8},{1,9},{2,10},{3,11},{4,12},{5,13},{6,14},{7,15},{8,0},{9,1},... | collective-permute-start | bytes 196616 | tf_op jit(solution)/shard_map/ppermute | solution.py:451
  75.4 0.0 collective-permute-start.7
  75.4 7.5 %all-to-all-start.1 = ((bf16[16,40,1024]{2,1,0:T(8,128)(2,1)}), bf16[16,40,1024]{2,1,0:T(8,128)(2,1)S(1)}, u32[]{:S(2)}, u32[]{:S(2)}) async-start(bf16[16,40,1024]{2,1,0:T(8,128)(2,1)} %pack.1), calls=%async_computation.1 | async-start | bytes 2621440 | tf_op jit(solution)/shard_map/all_to_all | solution.py:502
  82.9 0.0 collective-permute-done.5
  82.9 0.0 collective-permute-done.6
  82.9 0.0 collective-permute-done.7
  83.0 0.3 collective-permute-start.8
  83.3 13.5 %collective-permute-done.8 = bf16[128,1024]{1,0:T(8,128)(2,1)S(1)} collective-permute-done((bf16[128,1024]{1,0:T(8,128)(2,1)S(1)}, bf16[128,1024]{1,0:T(8,128)(2,1)S(1)}, u32[]{:S(2)}, u32[]{:S(2)}) %collective-permute-start.8) | collective-permute-done | bytes 262176 | tf_op jit(solution)/shard_map/ppermute | solution.py:451
  96.8 0.1 broadcast_select_fusion.3
  97.0 2.6 %collective-permute-start.9 = (bf16[256,1024]{1,0:T(8,128)(2,1)S(1)}, bf16[256,1024]{1,0:T(8,128)(2,1)S(1)}, u32[]{:S(2)}, u32[]{:S(2)}) collective-permute-start(bf16[256,1024]{1,0:T(8,128)(2,1)S(1)} %pad_maximum_fusion.1), channel_id=1, source_target_pairs={{0,1},{1,0},{2,3},{3,2},{4,5},{5,4},{6,7},{7,6},{8,9},{9,8},{10,11... | collective-permute-start | bytes 1572872 | tf_op jit(solution)/shard_map/ppermute | solution.py:451
  99.6 1.5 %collective-permute-done.9 = bf16[256,1024]{1,0:T(8,128)(2,1)S(1)} collective-permute-done((bf16[256,1024]{1,0:T(8,128)(2,1)S(1)}, bf16[256,1024]{1,0:T(8,128)(2,1)S(1)}, u32[]{:S(2)}, u32[]{:S(2)}) %collective-permute-start.9) | collective-permute-done | bytes 524320 | tf_op jit(solution)/shard_map/ppermute | solution.py:451
  101.1 0.2 broadcast_select_fusion.1
  101.4 0.2 maximum_convert_fusion
  101.6 0.2 slice_bitcast_fusion.1
  101.8 1.5 %pad_maximum_fusion = f32[2,512,512]{2,1,0:T(8,128)} fusion(f32[1,512,512]{2,1,0:T(8,128)S(1)} %get-tuple-element.27, f32[1,512,512]{2,1,0:T(8,128)S(1)} %get-tuple-element.26), kind=kLoop, calls=%fused_computation | loop fusion | flops 524288 | bytes 4194304 | tf_op jit(solution)/shard_map/stack | solution.py:505
  103.3 10.1 %all-to-all-done.1.terms = bf16[16,40,1024]{2,1,0:T(8,128)(2,1)S(1)} async-done(((bf16[16,40,1024]{2,1,0:T(8,128)(2,1)}), bf16[16,40,1024]{2,1,0:T(8,128)(2,1)S(1)}, u32[]{:S(2)}, u32[]{:S(2)}) %all-to-all-start.1) | async-done | bytes 1310752 | tf_op jit(solution)/shard_map/all_to_all | solution.py:502
  113.4 4.3 %place.1 = f32[2,40,32768]{2,1,0:T(8,128)} custom-call(s32[16]{0:T(128)S(1)} %copy-done.5, s32[16]{0:T(128)S(1)} %copy-done.6, s32[80]{0:T(128)S(1)} %get-tuple-element.15.blocks, s32[80]{0:T(128)S(1)} %get-tuple-element.16.owners, s32[16]{0:T(128)S(1)} %get-tuple-element.17.single, ...), custom_call_target="tpu_custom_call", output_to_operand_aliasing={{}: (6, {})} | custom-call | bytes 6291456 | tf_op jit(solution)/shard_map/place/pallas_call | solution.py:425
  (7 shorter events, 0.2 us)
Async XLA Ops:
  6.6 6.7 %copy-start.1 = (bf16[1024,1024]{1,0:T(8,128)(2,1)S(1)}, bf16[1024,1024]{1,0:T(8,128)(2,1)}, u32[]{:S(2)}) copy-start(bf16[1024,1024]{1,0:T(8,128)(2,1)} %constant.81.clone.right) | copy-start | bytes 6291460
  6.7 6.7 %copy-start.5 = (s32[16]{0:T(128)S(1)}, s32[16]{0:T(128)}, u32[]{:S(2)}) copy-start(s32[16]{0:T(128)} %dealing.9) | copy-start | bytes 196
  6.7 6.7 %copy-start.6 = (s32[16]{0:T(128)S(1)}, s32[16]{0:T(128)}, u32[]{:S(2)}) copy-start(s32[16]{0:T(128)} %cols.5) | copy-start | bytes 196
  6.7 37.3 %all-to-all-start = ((bf16[16,40,1024]{2,1,0:T(8,128)(2,1)}), bf16[16,40,1024]{2,1,0:T(8,128)(2,1)S(1)}, u32[]{:S(2)}, u32[]{:S(2)}) async-start(bf16[16,40,1024]{2,1,0:T(8,128)(2,1)} %get-tuple-element.18), calls=%async_computation | async-start | bytes 2621440 | tf_op jit(solution)/shard_map/all_to_all | solution.py:493
  13.4 1.6 %copy-start.2 = (bf16[1024,1024]{1,0:T(8,128)(2,1)S(1)}, bf16[1024,1024]{1,0:T(8,128)(2,1)}, u32[]{:S(2)}) copy-start(bf16[1024,1024]{1,0:T(8,128)(2,1)} %constant.82.clone.left) | copy-start | bytes 6291460
  15.0 1.2 %copy-start.3 = (bf16[2,512,512]{2,1,0:T(8,128)(2,1)S(1)}, bf16[2,512,512]{2,1,0:T(8,128)(2,1)}, u32[]{:S(2)}) copy-start(bf16[2,512,512]{2,1,0:T(8,128)(2,1)} %probe.1) | copy-start | bytes 3145732
  16.2 1.0 copy-start.4
  17.3 26.7 %copy-start.7 = (s32[16]{0:T(128)S(1)}, s32[16]{0:T(128)}, u32[]{:S(2)}) copy-start(s32[16]{0:T(128)} %rows.3) | copy-start | bytes 196
  23.7 9.7 %copy-start = (bf16[14336,1024]{1,0:T(8,128)(2,1)}, bf16[14336,1024]{1,0:T(8,128)(2,1)S(1)}, u32[]{:S(2)}) copy-start(bf16[14336,1024]{1,0:T(8,128)(2,1)S(1)} %get-tuple-element.19.stock) | copy-start | bytes 88080384
  53.2 2.3 %collective-permute-start = (bf16[256,1024]{1,0:T(8,128)(2,1)}, bf16[256,1024]{1,0:T(8,128)(2,1)}, u32[]{:S(2)}, u32[]{:S(2)}) collective-permute-start(bf16[256,1024]{1,0:T(8,128)(2,1)} %get-tuple-element.22), channel_id=1, source_target_pairs={{0,1},{1,0},{2,3},{3,2},{4,5},{5,4},{6,7},{7,6},{8,9},{9,8},{10,11... | collective-permute-start | bytes 1572872 | tf_op jit(solution)/shard_map/ppermute | solution.py:451
  56.8 7.8 %collective-permute-start.1 = (bf16[128,1024]{1,0:T(8,128)(2,1)S(1)}, bf16[128,1024]{1,0:T(8,128)(2,1)S(1)}, u32[]{:S(2)}, u32[]{:S(2)}) collective-permute-start(bf16[128,1024]{1,0:T(8,128)(2,1)S(1)} %dynamic-slice_convert_fusion), channel_id=1, source_target_pairs={{0,2},{1,3},{2,0},{3,1},{4,6},{5,7},{6,4},{7,5},{8,10},{9,11},{10,... | collective-permute-start | bytes 786440 | tf_op jit(solution)/shard_map/ppermute | solution.py:451
  64.6 5.2 %collective-permute-start.4 = (bf16[32,1024]{1,0:T(8,128)(2,1)S(1)}, bf16[32,1024]{1,0:T(8,128)(2,1)S(1)}, u32[]{:S(2)}, u32[]{:S(2)}) collective-permute-start(bf16[32,1024]{1,0:T(8,128)(2,1)S(1)} %get-tuple-element.33), channel_id=1, source_target_pairs={{0,12},{1,13},{2,14},{3,15},{4,8},{5,9},{6,10},{7,11},{8,4},{9,5},... | collective-permute-start | bytes 196616 | tf_op jit(solution)/shard_map/ppermute | solution.py:451
  65.1 4.8 %collective-permute-start.3 = (bf16[32,1024]{1,0:T(8,128)(2,1)S(1)}, bf16[32,1024]{1,0:T(8,128)(2,1)S(1)}, u32[]{:S(2)}, u32[]{:S(2)}) collective-permute-start(bf16[32,1024]{1,0:T(8,128)(2,1)S(1)} %get-tuple-element.34), channel_id=1, source_target_pairs={{0,8},{1,9},{2,10},{3,11},{4,12},{5,13},{6,14},{7,15},{8,0},{9,1},... | collective-permute-start | bytes 196616 | tf_op jit(solution)/shard_map/ppermute | solution.py:451
  65.9 5.1 %collective-permute-start.2 = (bf16[32,1024]{1,0:T(8,128)(2,1)S(1)}, bf16[32,1024]{1,0:T(8,128)(2,1)S(1)}, u32[]{:S(2)}, u32[]{:S(2)}) collective-permute-start(bf16[32,1024]{1,0:T(8,128)(2,1)S(1)} %get-tuple-element.32), channel_id=1, source_target_pairs={{0,4},{1,5},{2,6},{3,7},{4,0},{5,1},{6,2},{7,3},{8,12},{9,13},{10,... | collective-permute-start | bytes 196616 | tf_op jit(solution)/shard_map/ppermute | solution.py:451
  71.0 11.8 %collective-permute-start.5 = (bf16[32,1024]{1,0:T(8,128)(2,1)S(1)}, bf16[32,1024]{1,0:T(8,128)(2,1)S(1)}, u32[]{:S(2)}, u32[]{:S(2)}) collective-permute-start(bf16[32,1024]{1,0:T(8,128)(2,1)S(1)} %multiply_convert_fusion), channel_id=1, source_target_pairs={{0,12},{1,13},{2,14},{3,15},{4,8},{5,9},{6,10},{7,11},{8,4},{9,5},... | collective-permute-start | bytes 196616 | tf_op jit(solution)/shard_map/ppermute | solution.py:451
  71.9 10.9 %collective-permute-start.6 = (bf16[32,1024]{1,0:T(8,128)(2,1)S(1)}, bf16[32,1024]{1,0:T(8,128)(2,1)S(1)}, u32[]{:S(2)}, u32[]{:S(2)}) collective-permute-start(bf16[32,1024]{1,0:T(8,128)(2,1)S(1)} %multiply_convert_fusion), channel_id=1, source_target_pairs={{0,8},{1,9},{2,10},{3,11},{4,12},{5,13},{6,14},{7,15},{8,0},{9,1},... | collective-permute-start | bytes 196616 | tf_op jit(solution)/shard_map/ppermute | solution.py:451
  75.4 7.5 %collective-permute-start.7 = (bf16[32,1024]{1,0:T(8,128)(2,1)S(1)}, bf16[32,1024]{1,0:T(8,128)(2,1)S(1)}, u32[]{:S(2)}, u32[]{:S(2)}) collective-permute-start(bf16[32,1024]{1,0:T(8,128)(2,1)S(1)} %multiply_convert_fusion), channel_id=1, source_target_pairs={{0,4},{1,5},{2,6},{3,7},{4,0},{5,1},{6,2},{7,3},{8,12},{9,13},{10,... | collective-permute-start | bytes 196616 | tf_op jit(solution)/shard_map/ppermute | solution.py:451
  75.4 38.1 %all-to-all-start.1 = ((bf16[16,40,1024]{2,1,0:T(8,128)(2,1)}), bf16[16,40,1024]{2,1,0:T(8,128)(2,1)S(1)}, u32[]{:S(2)}, u32[]{:S(2)}) async-start(bf16[16,40,1024]{2,1,0:T(8,128)(2,1)} %pack.1), calls=%async_computation.1 | async-start | bytes 2621440 | tf_op jit(solution)/shard_map/all_to_all | solution.py:502
  83.0 13.9 %collective-permute-start.8 = (bf16[128,1024]{1,0:T(8,128)(2,1)S(1)}, bf16[128,1024]{1,0:T(8,128)(2,1)S(1)}, u32[]{:S(2)}, u32[]{:S(2)}) collective-permute-start(bf16[128,1024]{1,0:T(8,128)(2,1)S(1)} %pad_maximum_fusion.2), channel_id=1, source_target_pairs={{0,2},{1,3},{2,0},{3,1},{4,6},{5,7},{6,4},{7,5},{8,10},{9,11},{10,... | collective-permute-start | bytes 786440 | tf_op jit(solution)/shard_map/ppermute | solution.py:451
  97.0 4.2 %collective-permute-start.9 = (bf16[256,1024]{1,0:T(8,128)(2,1)S(1)}, bf16[256,1024]{1,0:T(8,128)(2,1)S(1)}, u32[]{:S(2)}, u32[]{:S(2)}) collective-permute-start(bf16[256,1024]{1,0:T(8,128)(2,1)S(1)} %pad_maximum_fusion.1), channel_id=1, source_target_pairs={{0,1},{1,0},{2,3},{3,2},{4,5},{5,4},{6,7},{7,6},{8,9},{9,8},{10,11... | collective-permute-start | bytes 1572872 | tf_op jit(solution)/shard_map/ppermute | solution.py:451

commit v15 on v12

--- a/solution.py
+++ b/solution.py
@@ -17,16 +17,12 @@
 ANY = pl.BlockSpec(memory_space=pl.ANY)
 
 
-def dft_tables(order):
+def dft_table(order):
     indices = np.arange(order, dtype=np.int32)
     phases = indices[:, None] * indices[None, :] % order
     angles = phases.astype(np.float32) * np.float32(2.0 * math.pi / order)
     factor = np.float32(1.0 / math.sqrt(order))
-    real_part = np.cos(angles) * factor
-    imag_part = -np.sin(angles) * factor
-    right_table = np.block([[real_part, imag_part], [-imag_part, real_part]])
-    left_table = np.block([[real_part, -imag_part], [imag_part, real_part]])
-    return right_table.astype(jnp.bfloat16), left_table.astype(jnp.bfloat16)
+    return np.concatenate([np.cos(angles) * factor, -np.sin(angles) * factor], axis=1).astype(jnp.bfloat16)
 
 
 def window_start(column, order, tile_cols):
@@ -104,20 +100,19 @@
     return (
         stock.at[0:order, 0:order],
         stock.at[0:order, order : 2 * order],
-        stock.at[order : 3 * order, :],
-        stock.at[3 * order : 4 * order, 0:order],
-        stock.at[4 * order : 6 * order, :],
+        stock.at[order : 2 * order, :],
+        stock.at[2 * order : 3 * order, 0:order],
     )
 
 
 def prepare_kernel(
-    order, dealing, cols, token, right, left, probe, measured,
+    order, dealing, cols, token, table_in, probe, measured,
     empty, blocks, owners, stock,
     table, zeros, sems, stock_sems,
 ):
     del token
     places = stock_places(stock, order)
-    sources = (probe.at[0], probe.at[1], right, measured.at[0], left)
+    sources = (probe.at[0], probe.at[1], table_in, measured.at[0])
     fills = []
     for k, (source, place) in enumerate(zip(sources, places)):
         fill = pltpu.make_async_copy(source, place, stock_sems.at[k])
@@ -155,7 +150,6 @@
 
 def prepare(dealing, cols, token, probe, measured, tile_shape):
     order = probe.shape[1]
-    right, left = dft_tables(order)
     slots = dealing.shape[0]
     numbers = slots * (order + LANES) // LANES
     fill_cols = 2048
@@ -167,31 +161,32 @@
             jax.ShapeDtypeStruct((numbers,), jnp.int32),
             jax.ShapeDtypeStruct((28 * order, 2 * order), jnp.bfloat16),
         ),
-        in_specs=[SMEM, SMEM, SMEM, ANY, ANY, ANY, ANY],
+        in_specs=[SMEM, SMEM, SMEM, ANY, ANY, ANY],
         out_specs=(ANY, SMEM, SMEM, ANY),
         scratch_shapes=[
             pltpu.SMEM((tile_shape[2] // LANES,), jnp.int32),
             pltpu.VMEM(tile_shape[:2] + (fill_cols,), jnp.float32),
             pltpu.SemaphoreType.DMA((tile_shape[2] // fill_cols,)),
-            pltpu.SemaphoreType.DMA((5,)),
+            pltpu.SemaphoreType.DMA((4,)),
         ],
         compiler_params=pltpu.CompilerParams(vmem_limit_bytes=8 * 2**20),
         cost_estimate=pl.CostEstimate(flops=0, bytes_accessed=110 * 2**20, transcendentals=0),
         name="prepare",
-    )(dealing, cols, token, jnp.asarray(right), jnp.asarray(left), probe, measured)
+    )(dealing, cols, token, jnp.asarray(dft_table(order)), probe, measured)
 
 
 def slot_kernel(
     dealing, rows, owners, cells, stock,
     term, kept, sent,
-    wide, patch, wave, half, resid, turned, mine, probe, right, measured, left, sems,
+    wide, patch, wave, half, resid, turned, mine, probe, table, minus, measured, sems,
 ):
     del owners
     order = term.shape[0]
-    targets = (probe.at[0], probe.at[1], right, measured, left)
+    places = stock_places(stock, order)
+    targets = (probe.at[0], probe.at[1], table, measured)
     loads = [
         pltpu.make_async_copy(source, target, sems.at[k])
-        for k, (source, target) in enumerate(zip(stock_places(stock, order), targets))
+        for k, (source, target) in enumerate(zip(places, targets))
     ]
     for load in loads:
         load.start()
@@ -217,40 +212,46 @@
         wave[place, :order] = (probe_real * real - probe_imag * imag).astype(wave.dtype)
         wave[place, order:] = (probe_real * imag + probe_imag * real).astype(wave.dtype)
 
-    def dot(a, b):
-        return jnp.dot(a, b, preferred_element_type=jnp.float32)
-
     loads[2].wait()
+    minus[...] = -table[:, order:]
+    cos, sin = table.at[:, :order], table.at[:, order:]
+    first_half, second_half = slice(0, order), slice(order, 2 * order)
+
+    def dots(a, b, c, d):
+        one = jnp.dot(a, b, preferred_element_type=jnp.float32)
+        return one + jnp.dot(c, d, preferred_element_type=jnp.float32)
+
     for first in range(0, order, tile):
         here = slice(first, first + tile)
-        there = slice(order + first, order + first + tile)
-        half[:order, here] = dot(wave[...], right[:, here]).astype(half.dtype)
-        half[order:, here] = dot(wave[...], right[:, there]).astype(half.dtype)
+        real, imag = wave[:, first_half], wave[:, second_half]
+        half[first_half, here] = dots(real, cos[:, here], imag, minus[:, here]).astype(half.dtype)
+        half[second_half, here] = dots(real, sin[:, here], imag, cos[:, here]).astype(half.dtype)
     loads[3].wait()
-    loads[4].wait()
     for first in range(0, order, tile):
         here = slice(first, first + tile)
         there = slice(order + first, order + first + tile)
         for top in range(0, order, tile):
             line = slice(top, top + tile)
-            real = dot(left[line, :], half[:, here])
-            imag = dot(left[order + top : order + top + tile, :], half[:, here])
+            half_real, half_imag = half[first_half, here], half[second_half, here]
+            real = dots(cos[line, :], half_real, minus[line, :], half_imag)
+            imag = dots(sin[line, :], half_real, cos[line, :], half_imag)
             inverse = jnp.minimum(lax.rsqrt(real * real + imag * imag), 1.0 / MAG_FLOOR)
             shrink = 1.0 - measured[line, here].astype(jnp.float32) * inverse
             resid[line, here] = (real * shrink).astype(resid.dtype)
             resid[line, there] = (imag * shrink).astype(resid.dtype)
     for first in range(0, order, tile):
         here = slice(first, first + tile)
-        there = slice(order + first, order + first + tile)
-        turned[:order, here] = dot(resid[...], left[:, here]).astype(turned.dtype)
-        turned[order:, here] = dot(resid[...], left[:, there]).astype(turned.dtype)
+        real, imag = resid[:, first_half], resid[:, second_half]
+        turned[first_half, here] = dots(real, cos[:, here], imag, sin[:, here]).astype(turned.dtype)
+        turned[second_half, here] = dots(real, minus[:, here], imag, cos[:, here]).astype(turned.dtype)
     for first in range(0, order, tile):
         here = slice(first, first + tile)
         there = slice(order + first, order + first + tile)
         for top in range(0, order, tile):
             line = slice(top, top + tile)
-            real = dot(right[line, :], turned[:, here])
-            imag = dot(right[order + top : order + top + tile, :], turned[:, here])
+            turned_real, turned_imag = turned[first_half, here], turned[second_half, here]
+            real = dots(cos[line, :], turned_real, sin[line, :], turned_imag)
+            imag = dots(minus[line, :], turned_real, cos[line, :], turned_imag)
             probe_real = probe[0, line, here].astype(jnp.float32)
             probe_imag = probe[1, line, here].astype(jnp.float32)
             term[line, here] = (probe_real * real + probe_imag * imag).astype(term.dtype)
@@ -287,10 +288,10 @@
             pltpu.VMEM((wide_cols, order), bf16),
             pltpu.VMEM((order, wide_cols), f32),
             pltpu.VMEM((2, order, order), bf16),
-            pltpu.VMEM((wide_cols, wide_cols), bf16),
+            pltpu.VMEM((order, wide_cols), bf16),
             pltpu.VMEM((order, order), bf16),
-            pltpu.VMEM((wide_cols, wide_cols), bf16),
-            pltpu.SemaphoreType.DMA((5,)),
+            pltpu.VMEM((order, order), bf16),
+            pltpu.SemaphoreType.DMA((4,)),
         ],
         compiler_params=pltpu.CompilerParams(vmem_limit_bytes=40 * 2**20),
         cost_estimate=pl.CostEstimate(

time: 116 us -> 116 us (level)
  waiting for transfers between devices: 46.8 us -> 49.8 us
  local copies, waits for them, and re-layouts: 13.8 us -> 11 us
    all_to_all x1, waiting for transfers between devices: 10.5 us -> 13.5 us  [body(): lax.all_to_all(pieces, 'row', split_axis=0, concat_axis=0, tiled=True)]
    unnamed x16 -> x14, local copies, waits for them, and re-layouts: 13.6 us -> 10.7 us
where the time goes in v15:
time: 116 us
  waiting for transfers between devices  49.8 us (43%)
  Pallas kernels  25.9 us (22%)
  starting transfers between devices  24.6 us (21%)
  local copies, waits for them, and re-layouts  11 us (9%)
  other arithmetic  3.5 us (3%)
    ppermute x10, waiting for transfers between devices, swap(): return lax.ppermute(x, 'row', [(d, d ^ distance) for d in range(devices)])  26.2 us
    all_to_all x1, waiting for transfers between devices, body(): lax.all_to_all(pieces, 'row', split_axis=0, concat_axis=0, tiled=True)  13.5 us
    unnamed x14, local copies, waits for them, and re-layouts  10.7 us
    ppermute x10, starting transfers between devices, swap(): return lax.ppermute(x, 'row', [(d, d ^ distance) for d in range(devices)])  10.4 us
    all_to_all x1, waiting for transfers between devices, body(): lax.all_to_all(terms, 'row', split_axis=0, concat_axis=0, tiled=True)  10.1 us
    pallas_call x1, Pallas kernels, slot_terms(): pl.pallas_call(slot_kernel, out_shape=(jax.ShapeDtypeStruct((order, wide_...  8.59 us
    all_to_all x1, starting transfers between devices, body(): lax.all_to_all(terms, 'row', split_axis=0, concat_axis=0, tiled=True)  7.48 us
    all_to_all x1, starting transfers between devices, body(): lax.all_to_all(pieces, 'row', split_axis=0, concat_axis=0, tiled=True)  6.7 us
  transfers between devices with their start and end apart: 12, of which 8 were waited for; matrix products, arithmetic and copies ran while one was open for 2% of the time, Pallas kernels for 7%

profile of v15, /device:TPU:15, one launch (start us, length us, event | category | flops | bytes accessed | tf_op | source)
XLA Modules:
  0.0 115.7 jit_solution(2878006418742760494)
XLA Ops:
  0.6 4.7 %fetch.1 = (bf16[16,40,1024]{2,1,0:T(8,128)(2,1)}, s32[1]{0:T(128)}) custom-call(s32[16]{0:T(128)} %dealing.9, s32[16]{0:T(128)} %cols.5, f32[2,40,32768]{2,1,0:T(8,128)} %tile.1), custom_call_target="tpu_custom_call" | custom-call | bytes 6291456 | tf_op jit(solution)/shard_map/fetch/pallas_call | solution.py:81
  5.3 0.0 copy-start.1
  5.3 0.0 copy-start.2
  5.3 0.0 copy-start.4
  5.3 0.0 copy-start.5
  5.4 0.0 copy-start.6
  5.4 6.7 %all-to-all-start = ((bf16[16,40,1024]{2,1,0:T(8,128)(2,1)}), bf16[16,40,1024]{2,1,0:T(8,128)(2,1)S(1)}, u32[]{:S(2)}, u32[]{:S(2)}) async-start(bf16[16,40,1024]{2,1,0:T(8,128)(2,1)} %get-tuple-element.16), calls=%async_computation | async-start | bytes 2621440 | tf_op jit(solution)/shard_map/all_to_all | solution.py:443
  12.1 0.0 copy-done.1
  12.1 0.0 copy-done.2
  12.1 0.0 copy-done.4
  12.1 0.0 copy-done.5
  12.1 0.0 copy-start.3
  12.1 1.0 copy-done.3
  13.1 6.2 %prepare.1 = (f32[2,40,32768]{2,1,0:T(8,128)}, s32[80]{0:T(128)S(1)}, s32[80]{0:T(128)S(1)}, bf16[14336,1024]{1,0:T(8,128)(2,1)S(1)}) custom-call(s32[16]{0:T(128)S(1)} %copy-done.4, s32[16]{0:T(128)S(1)} %copy-done.5, s32[1]{0:T(128)} %get-tuple-element.13.token, bf16[512,1024]{1,0:T(8,128)(2,1)S(1)} %copy-done.2, bf16[2,512,512]{2,1,0:T(8,128)(2,1)S(1)} %copy-done.1, ...), custom_call_target="tpu_custom_call" | custom-call | bytes 115343360 | tf_op jit(solution)/shard_map/prepare/pallas_call | solution.py:156
  19.4 0.0 copy-start
  19.4 9.7 %copy-done = bf16[14336,1024]{1,0:T(8,128)(2,1)} copy-done((bf16[14336,1024]{1,0:T(8,128)(2,1)}, bf16[14336,1024]{1,0:T(8,128)(2,1)S(1)}, u32[]{:S(2)}) %copy-start) | copy-done | bytes 29360152
  29.1 13.5 %all-to-all-done = bf16[16,40,1024]{2,1,0:T(8,128)(2,1)S(1)} async-done(((bf16[16,40,1024]{2,1,0:T(8,128)(2,1)}), bf16[16,40,1024]{2,1,0:T(8,128)(2,1)S(1)}, u32[]{:S(2)}, u32[]{:S(2)}) %all-to-all-start) | async-done | bytes 1310752 | tf_op jit(solution)/shard_map/all_to_all | solution.py:443
  42.6 0.0 copy-done.6
  42.6 8.6 %slot.1 = (bf16[512,1024]{1,0:T(8,128)(2,1)S(1)}, f32[256,1024]{1,0:T(8,128)S(1)}, bf16[256,1024]{1,0:T(8,128)(2,1)}) custom-call(s32[16]{0:T(128)S(1)} %copy-done.4, s32[16]{0:T(128)S(1)} %copy-done.6, s32[80]{0:T(128)S(1)} %get-tuple-element.15.owners, bf16[640,1024]{1,0:T(8,128)(2,1)S(1)} %bitcast.5, bf16[14336,1024]{1,0:T(8,128)(2,1)} %copy-done), custom_call_target="tpu_custom_call" | custom-call | flops 4294967296 | bytes 8388608 | tf_op jit(solution)/shard_map/slot/pallas_call | solution.py:273
  51.2 0.3 collective-permute-start
  51.5 2.0 %collective-permute-done = bf16[256,1024]{1,0:T(8,128)(2,1)} collective-permute-done((bf16[256,1024]{1,0:T(8,128)(2,1)}, bf16[256,1024]{1,0:T(8,128)(2,1)}, u32[]{:S(2)}, u32[]{:S(2)}) %collective-permute-start) | collective-permute-done | bytes 524320 | tf_op jit(solution)/shard_map/ppermute | solution.py:401
  53.5 1.2 %convert_add_fusion = f32[256,1024]{1,0:T(8,128)S(1)} fusion(f32[256,1024]{1,0:T(8,128)S(1)} %get-tuple-element.19, bf16[256,1024]{1,0:T(8,128)(2,1)} %collective-permute-done), kind=kLoop, calls=%fused_computation.4 | loop fusion | flops 524288 | bytes 2621440 | tf_op jit(solution)/shard_map/add | solution.py:406
  54.8 0.1 collective-permute-start.1
  55.0 7.6 %collective-permute-done.1 = bf16[128,1024]{1,0:T(8,128)(2,1)S(1)} collective-permute-done((bf16[128,1024]{1,0:T(8,128)(2,1)S(1)}, bf16[128,1024]{1,0:T(8,128)(2,1)S(1)}, u32[]{:S(2)}, u32[]{:S(2)}) %collective-permute-start.1) | collective-permute-done | bytes 262176 | tf_op jit(solution)/shard_map/ppermute | solution.py:401
  62.6 0.1 convert_add_fusion.1
  62.7 0.4 collective-permute-start.4
  63.1 0.8 collective-permute-start.3
  63.9 1.5 %collective-permute-start.2 = (bf16[32,1024]{1,0:T(8,128)(2,1)S(1)}, bf16[32,1024]{1,0:T(8,128)(2,1)S(1)}, u32[]{:S(2)}, u32[]{:S(2)}) collective-permute-start(bf16[32,1024]{1,0:T(8,128)(2,1)S(1)} %get-tuple-element.30), channel_id=1, source_target_pairs={{0,4},{1,5},{2,6},{3,7},{4,0},{5,1},{6,2},{7,3},{8,12},{9,13},{10,... | collective-permute-start | bytes 196616 | tf_op jit(solution)/shard_map/ppermute | solution.py:401
  65.4 2.2 %pack.1 = bf16[16,40,1024]{2,1,0:T(8,128)(2,1)} custom-call(s32[16]{0:T(128)S(1)} %copy-done.4, s32[16]{0:T(128)S(1)} %copy-done.6, bf16[512,1024]{1,0:T(8,128)(2,1)S(1)} %get-tuple-element.18.term), custom_call_target="tpu_custom_call" | custom-call | bytes 3145728 | tf_op jit(solution)/shard_map/pack/pallas_call | solution.py:320
  67.6 0.3 collective-permute-done.4
  68.0 0.0 collective-permute-done.3
  68.0 1.1 collective-permute-done.2
  69.1 0.9 collective-permute-start.5
  70.0 3.4 %collective-permute-start.6 = (bf16[32,1024]{1,0:T(8,128)(2,1)S(1)}, bf16[32,1024]{1,0:T(8,128)(2,1)S(1)}, u32[]{:S(2)}, u32[]{:S(2)}) collective-permute-start(bf16[32,1024]{1,0:T(8,128)(2,1)S(1)} %multiply_convert_fusion), channel_id=1, source_target_pairs={{0,8},{1,9},{2,10},{3,11},{4,12},{5,13},{6,14},{7,15},{8,0},{9,1},... | collective-permute-start | bytes 196616 | tf_op jit(solution)/shard_map/ppermute | solution.py:401
  73.4 0.0 collective-permute-start.7
  73.5 7.5 %all-to-all-start.1 = ((bf16[16,40,1024]{2,1,0:T(8,128)(2,1)}), bf16[16,40,1024]{2,1,0:T(8,128)(2,1)S(1)}, u32[]{:S(2)}, u32[]{:S(2)}) async-start(bf16[16,40,1024]{2,1,0:T(8,128)(2,1)} %pack.1), calls=%async_computation.1 | async-start | bytes 2621440 | tf_op jit(solution)/shard_map/all_to_all | solution.py:452
  80.9 0.0 collective-permute-done.5
  80.9 0.0 collective-permute-done.6
  80.9 0.0 collective-permute-done.7
  81.0 0.3 collective-permute-start.8
  81.4 13.5 %collective-permute-done.8 = bf16[128,1024]{1,0:T(8,128)(2,1)S(1)} collective-permute-done((bf16[128,1024]{1,0:T(8,128)(2,1)S(1)}, bf16[128,1024]{1,0:T(8,128)(2,1)S(1)}, u32[]{:S(2)}, u32[]{:S(2)}) %collective-permute-start.8) | collective-permute-done | bytes 262176 | tf_op jit(solution)/shard_map/ppermute | solution.py:401
  94.9 0.1 broadcast_select_fusion.3
  95.1 2.6 %collective-permute-start.9 = (bf16[256,1024]{1,0:T(8,128)(2,1)S(1)}, bf16[256,1024]{1,0:T(8,128)(2,1)S(1)}, u32[]{:S(2)}, u32[]{:S(2)}) collective-permute-start(bf16[256,1024]{1,0:T(8,128)(2,1)S(1)} %pad_maximum_fusion.1), channel_id=1, source_target_pairs={{0,1},{1,0},{2,3},{3,2},{4,5},{5,4},{6,7},{7,6},{8,9},{9,8},{10,11... | collective-permute-start | bytes 1572872 | tf_op jit(solution)/shard_map/ppermute | solution.py:401
  97.7 1.5 %collective-permute-done.9 = bf16[256,1024]{1,0:T(8,128)(2,1)S(1)} collective-permute-done((bf16[256,1024]{1,0:T(8,128)(2,1)S(1)}, bf16[256,1024]{1,0:T(8,128)(2,1)S(1)}, u32[]{:S(2)}, u32[]{:S(2)}) %collective-permute-start.9) | collective-permute-done | bytes 524320 | tf_op jit(solution)/shard_map/ppermute | solution.py:401
  99.2 0.2 broadcast_select_fusion.1
  99.5 0.2 maximum_convert_fusion
  99.7 0.2 slice_bitcast_fusion.1
  99.9 1.5 %pad_maximum_fusion = f32[2,512,512]{2,1,0:T(8,128)} fusion(f32[1,512,512]{2,1,0:T(8,128)S(1)} %get-tuple-element.25, f32[1,512,512]{2,1,0:T(8,128)S(1)} %get-tuple-element.24), kind=kLoop, calls=%fused_computation | loop fusion | flops 524288 | bytes 4194304 | tf_op jit(solution)/shard_map/stack | solution.py:455
  101.4 10.1 %all-to-all-done.1.terms = bf16[16,40,1024]{2,1,0:T(8,128)(2,1)S(1)} async-done(((bf16[16,40,1024]{2,1,0:T(8,128)(2,1)}), bf16[16,40,1024]{2,1,0:T(8,128)(2,1)S(1)}, u32[]{:S(2)}, u32[]{:S(2)}) %all-to-all-start.1) | async-done | bytes 1310752 | tf_op jit(solution)/shard_map/all_to_all | solution.py:452
  111.5 4.2 %place.1 = f32[2,40,32768]{2,1,0:T(8,128)} custom-call(s32[16]{0:T(128)S(1)} %copy-done.4, s32[16]{0:T(128)S(1)} %copy-done.5, s32[80]{0:T(128)S(1)} %get-tuple-element.14.blocks, s32[80]{0:T(128)S(1)} %get-tuple-element.15.owners, bf16[16,40,1024]{2,1,0:T(8,128)(2,1)S(1)} %all-to-all-done.1.terms, ...), custom_call_target="tpu_custom_call", output_to_operand_aliasing={{}: (5, {})} | custom-call | bytes 6291456 | tf_op jit(solution)/shard_map/place/pallas_call | solution.py:375
  (7 shorter events, 0.2 us)
Async XLA Ops:
  5.3 6.8 %copy-start.1 = (bf16[2,512,512]{2,1,0:T(8,128)(2,1)S(1)}, bf16[2,512,512]{2,1,0:T(8,128)(2,1)}, u32[]{:S(2)}) copy-start(bf16[2,512,512]{2,1,0:T(8,128)(2,1)} %probe.1) | copy-start | bytes 3145732
  5.3 6.8 %copy-start.2 = (bf16[512,1024]{1,0:T(8,128)(2,1)S(1)}, bf16[512,1024]{1,0:T(8,128)(2,1)}, u32[]{:S(2)}) copy-start(bf16[512,1024]{1,0:T(8,128)(2,1)} %constant.79.clone.table_in) | copy-start | bytes 3145732
  5.3 6.8 %copy-start.4 = (s32[16]{0:T(128)S(1)}, s32[16]{0:T(128)}, u32[]{:S(2)}) copy-start(s32[16]{0:T(128)} %dealing.9) | copy-start | bytes 196
  5.3 6.8 %copy-start.5 = (s32[16]{0:T(128)S(1)}, s32[16]{0:T(128)}, u32[]{:S(2)}) copy-start(s32[16]{0:T(128)} %cols.5) | copy-start | bytes 196
  5.4 37.3 %copy-start.6 = (s32[16]{0:T(128)S(1)}, s32[16]{0:T(128)}, u32[]{:S(2)}) copy-start(s32[16]{0:T(128)} %rows.3) | copy-start | bytes 196
  5.4 37.3 %all-to-all-start = ((bf16[16,40,1024]{2,1,0:T(8,128)(2,1)}), bf16[16,40,1024]{2,1,0:T(8,128)(2,1)S(1)}, u32[]{:S(2)}, u32[]{:S(2)}) async-start(bf16[16,40,1024]{2,1,0:T(8,128)(2,1)} %get-tuple-element.16), calls=%async_computation | async-start | bytes 2621440 | tf_op jit(solution)/shard_map/all_to_all | solution.py:443
  12.1 1.0 copy-start.3
  19.4 9.7 %copy-start = (bf16[14336,1024]{1,0:T(8,128)(2,1)}, bf16[14336,1024]{1,0:T(8,128)(2,1)S(1)}, u32[]{:S(2)}) copy-start(bf16[14336,1024]{1,0:T(8,128)(2,1)S(1)} %get-tuple-element.17.stock) | copy-start | bytes 88080384
  51.2 2.3 %collective-permute-start = (bf16[256,1024]{1,0:T(8,128)(2,1)}, bf16[256,1024]{1,0:T(8,128)(2,1)}, u32[]{:S(2)}, u32[]{:S(2)}) collective-permute-start(bf16[256,1024]{1,0:T(8,128)(2,1)} %get-tuple-element.20), channel_id=1, source_target_pairs={{0,1},{1,0},{2,3},{3,2},{4,5},{5,4},{6,7},{7,6},{8,9},{9,8},{10,11... | collective-permute-start | bytes 1572872 | tf_op jit(solution)/shard_map/ppermute | solution.py:401
  54.8 7.8 %collective-permute-start.1 = (bf16[128,1024]{1,0:T(8,128)(2,1)S(1)}, bf16[128,1024]{1,0:T(8,128)(2,1)S(1)}, u32[]{:S(2)}, u32[]{:S(2)}) collective-permute-start(bf16[128,1024]{1,0:T(8,128)(2,1)S(1)} %dynamic-slice_convert_fusion), channel_id=1, source_target_pairs={{0,2},{1,3},{2,0},{3,1},{4,6},{5,7},{6,4},{7,5},{8,10},{9,11},{10,... | collective-permute-start | bytes 786440 | tf_op jit(solution)/shard_map/ppermute | solution.py:401
  62.7 5.3 %collective-permute-start.4 = (bf16[32,1024]{1,0:T(8,128)(2,1)S(1)}, bf16[32,1024]{1,0:T(8,128)(2,1)S(1)}, u32[]{:S(2)}, u32[]{:S(2)}) collective-permute-start(bf16[32,1024]{1,0:T(8,128)(2,1)S(1)} %get-tuple-element.31), channel_id=1, source_target_pairs={{0,12},{1,13},{2,14},{3,15},{4,8},{5,9},{6,10},{7,11},{8,4},{9,5},... | collective-permute-start | bytes 196616 | tf_op jit(solution)/shard_map/ppermute | solution.py:401
  63.1 4.8 %collective-permute-start.3 = (bf16[32,1024]{1,0:T(8,128)(2,1)S(1)}, bf16[32,1024]{1,0:T(8,128)(2,1)S(1)}, u32[]{:S(2)}, u32[]{:S(2)}) collective-permute-start(bf16[32,1024]{1,0:T(8,128)(2,1)S(1)} %get-tuple-element.32), channel_id=1, source_target_pairs={{0,8},{1,9},{2,10},{3,11},{4,12},{5,13},{6,14},{7,15},{8,0},{9,1},... | collective-permute-start | bytes 196616 | tf_op jit(solution)/shard_map/ppermute | solution.py:401
  63.9 5.1 %collective-permute-start.2 = (bf16[32,1024]{1,0:T(8,128)(2,1)S(1)}, bf16[32,1024]{1,0:T(8,128)(2,1)S(1)}, u32[]{:S(2)}, u32[]{:S(2)}) collective-permute-start(bf16[32,1024]{1,0:T(8,128)(2,1)S(1)} %get-tuple-element.30), channel_id=1, source_target_pairs={{0,4},{1,5},{2,6},{3,7},{4,0},{5,1},{6,2},{7,3},{8,12},{9,13},{10,... | collective-permute-start | bytes 196616 | tf_op jit(solution)/shard_map/ppermute | solution.py:401
  69.1 11.8 %collective-permute-start.5 = (bf16[32,1024]{1,0:T(8,128)(2,1)S(1)}, bf16[32,1024]{1,0:T(8,128)(2,1)S(1)}, u32[]{:S(2)}, u32[]{:S(2)}) collective-permute-start(bf16[32,1024]{1,0:T(8,128)(2,1)S(1)} %multiply_convert_fusion), channel_id=1, source_target_pairs={{0,12},{1,13},{2,14},{3,15},{4,8},{5,9},{6,10},{7,11},{8,4},{9,5},... | collective-permute-start | bytes 196616 | tf_op jit(solution)/shard_map/ppermute | solution.py:401
  70.0 10.9 %collective-permute-start.6 = (bf16[32,1024]{1,0:T(8,128)(2,1)S(1)}, bf16[32,1024]{1,0:T(8,128)(2,1)S(1)}, u32[]{:S(2)}, u32[]{:S(2)}) collective-permute-start(bf16[32,1024]{1,0:T(8,128)(2,1)S(1)} %multiply_convert_fusion), channel_id=1, source_target_pairs={{0,8},{1,9},{2,10},{3,11},{4,12},{5,13},{6,14},{7,15},{8,0},{9,1},... | collective-permute-start | bytes 196616 | tf_op jit(solution)/shard_map/ppermute | solution.py:401
  73.4 7.5 %collective-permute-start.7 = (bf16[32,1024]{1,0:T(8,128)(2,1)S(1)}, bf16[32,1024]{1,0:T(8,128)(2,1)S(1)}, u32[]{:S(2)}, u32[]{:S(2)}) collective-permute-start(bf16[32,1024]{1,0:T(8,128)(2,1)S(1)} %multiply_convert_fusion), channel_id=1, source_target_pairs={{0,4},{1,5},{2,6},{3,7},{4,0},{5,1},{6,2},{7,3},{8,12},{9,13},{10,... | collective-permute-start | bytes 196616 | tf_op jit(solution)/shard_map/ppermute | solution.py:401
  73.5 38.0 %all-to-all-start.1 = ((bf16[16,40,1024]{2,1,0:T(8,128)(2,1)}), bf16[16,40,1024]{2,1,0:T(8,128)(2,1)S(1)}, u32[]{:S(2)}, u32[]{:S(2)}) async-start(bf16[16,40,1024]{2,1,0:T(8,128)(2,1)} %pack.1), calls=%async_computation.1 | async-start | bytes 2621440 | tf_op jit(solution)/shard_map/all_to_all | solution.py:452
  81.0 13.9 %collective-permute-start.8 = (bf16[128,1024]{1,0:T(8,128)(2,1)S(1)}, bf16[128,1024]{1,0:T(8,128)(2,1)S(1)}, u32[]{:S(2)}, u32[]{:S(2)}) collective-permute-start(bf16[128,1024]{1,0:T(8,128)(2,1)S(1)} %pad_maximum_fusion.2), channel_id=1, source_target_pairs={{0,2},{1,3},{2,0},{3,1},{4,6},{5,7},{6,4},{7,5},{8,10},{9,11},{10,... | collective-permute-start | bytes 786440 | tf_op jit(solution)/shard_map/ppermute | solution.py:401
  95.1 4.2 %collective-permute-start.9 = (bf16[256,1024]{1,0:T(8,128)(2,1)S(1)}, bf16[256,1024]{1,0:T(8,128)(2,1)S(1)}, u32[]{:S(2)}, u32[]{:S(2)}) collective-permute-start(bf16[256,1024]{1,0:T(8,128)(2,1)S(1)} %pad_maximum_fusion.1), channel_id=1, source_target_pairs={{0,1},{1,0},{2,3},{3,2},{4,5},{5,4},{6,7},{7,6},{8,9},{9,8},{10,11... | collective-permute-start | bytes 1572872 | tf_op jit(solution)/shard_map/ppermute | solution.py:401

commit v16 on v15

--- a/solution.py
+++ b/solution.py
@@ -159,7 +159,7 @@
             jax.ShapeDtypeStruct(tile_shape, jnp.float32),
             jax.ShapeDtypeStruct((numbers,), jnp.int32),
             jax.ShapeDtypeStruct((numbers,), jnp.int32),
-            jax.ShapeDtypeStruct((28 * order, 2 * order), jnp.bfloat16),
+            jax.ShapeDtypeStruct((48 * order, 2 * order), jnp.bfloat16),
         ),
         in_specs=[SMEM, SMEM, SMEM, ANY, ANY, ANY],
         out_specs=(ANY, SMEM, SMEM, ANY),
@@ -198,14 +198,19 @@
 
     wide[0:total_rows, :] = cells[...].astype(jnp.float32)
     wide[total_rows:, :] = jnp.zeros((SUBLANES, 2 * order), jnp.float32)
+
+    @pl.loop(0, order // step, unroll=2)
+    def _(i):
+        place = pl.ds(pl.multiple_of(i * step, step), step)
+        patch[place, :] = rows_from(wide, first_row + i * step, step).astype(patch.dtype)
+
     loads[0].wait()
     loads[1].wait()
 
-    @pl.loop(0, order // step)
+    @pl.loop(0, order // step, unroll=2)
     def _(i):
         place = pl.ds(pl.multiple_of(i * step, step), step)
-        found = rows_from(wide, first_row + i * step, step)
-        patch[place, :] = found.astype(patch.dtype)
+        found = patch[place, :].astype(jnp.float32)
         real, imag = found[:, :order], found[:, order:]
         probe_real = probe[0, place, :].astype(jnp.float32)
         probe_imag = probe[1, place, :].astype(jnp.float32)
@@ -293,7 +298,7 @@
             pltpu.VMEM((order, order), bf16),
             pltpu.SemaphoreType.DMA((4,)),
         ],
-        compiler_params=pltpu.CompilerParams(vmem_limit_bytes=40 * 2**20),
+        compiler_params=pltpu.CompilerParams(vmem_limit_bytes=24 * 2**20),
         cost_estimate=pl.CostEstimate(
             flops=8 * 2 * order**3 * 2, bytes_accessed=8 * 2**20, transcendentals=order * order
         ),
@@ -323,7 +328,7 @@
         in_specs=[SMEM, SMEM, VMEM],
         out_specs=VMEM,
         scratch_shapes=[pltpu.VMEM((2 * reach + order + tile_rows + SUBLANES, width), jnp.float32)],
-        compiler_params=pltpu.CompilerParams(vmem_limit_bytes=16 * 2**20),
+        compiler_params=pltpu.CompilerParams(vmem_limit_bytes=8 * 2**20),
         cost_estimate=pl.CostEstimate(flops=0, bytes_accessed=3 * 2**20, transcendentals=0),
         name="pack",
     )(dealing, rows, term)
@@ -382,7 +387,7 @@
             pltpu.SemaphoreType.DMA((slots * count,)),
         ],
         input_output_aliases={5: 0},
-        compiler_params=pltpu.CompilerParams(vmem_limit_bytes=24 * 2**20),
+        compiler_params=pltpu.CompilerParams(vmem_limit_bytes=12 * 2**20),
         cost_estimate=pl.CostEstimate(flops=0, bytes_accessed=6 * 2**20, transcendentals=0),
         name="place",
     )(dealing, cols, blocks, owners, terms, empty)

time: 116 us -> 116 us (level)
  local copies, waits for them, and re-layouts: 11 us -> 1.33 us
  waiting for transfers between devices: 49.8 us -> 59 us
    unnamed x14 -> x12, local copies, waits for them, and re-layouts: 10.7 us -> 1.07 us
    all_to_all x1, waiting for transfers between devices: 13.5 us -> 22.7 us  [body(): lax.all_to_all(pieces, 'row', split_axis=0, concat_axis=0, tiled=True)]
  transfers between devices with their start and end apart: 12 -> 12, of which waited for: 8 -> 8; matrix products, arithmetic and copies ran while one was open for 2% -> 2% of each run, Pallas kernels for 7% -> 8%
where the time goes in v16:
time: 116 us
  waiting for transfers between devices  59 us (51%)
  Pallas kernels  26.2 us (23%)
  starting transfers between devices  24.6 us (21%)
  other arithmetic  3.5 us (3%)
  local copies, waits for them, and re-layouts  1.33 us (1%)
    ppermute x10, waiting for transfers between devices, swap(): return lax.ppermute(x, 'row', [(d, d ^ distance) for d in range(devices)])  26.2 us
    all_to_all x1, waiting for transfers between devices, body(): lax.all_to_all(pieces, 'row', split_axis=0, concat_axis=0, tiled=True)  22.7 us
    ppermute x10, starting transfers between devices, swap(): return lax.ppermute(x, 'row', [(d, d ^ distance) for d in range(devices)])  10.4 us
    all_to_all x1, waiting for transfers between devices, body(): lax.all_to_all(terms, 'row', split_axis=0, concat_axis=0, tiled=True)  10.1 us
    pallas_call x1, Pallas kernels, slot_terms(): pl.pallas_call(slot_kernel, out_shape=(jax.ShapeDtypeStruct((order, wide_...  8.37 us
    all_to_all x1, starting transfers between devices, body(): lax.all_to_all(terms, 'row', split_axis=0, concat_axis=0, tiled=True)  7.48 us
    pallas_call x1, Pallas kernels, prepare(): pl.pallas_call(functools.partial(prepare_kernel, order), out_shape=(jax.S...  6.76 us
    all_to_all x1, starting transfers between devices, body(): lax.all_to_all(pieces, 'row', split_axis=0, concat_axis=0, tiled=True)  6.7 us
  transfers between devices with their start and end apart: 12, of which 8 were waited for; matrix products, arithmetic and copies ran while one was open for 2% of the time, Pallas kernels for 8%

profile of v16, /device:TPU:15, one launch (start us, length us, event | category | flops | bytes accessed | tf_op | source)
XLA Modules:
  0.0 115.5 jit_solution(1534902231566071013)
XLA Ops:
  0.6 4.7 %fetch.1 = (bf16[16,40,1024]{2,1,0:T(8,128)(2,1)}, s32[1]{0:T(128)}) custom-call(s32[16]{0:T(128)} %dealing.9, s32[16]{0:T(128)} %cols.5, f32[2,40,32768]{2,1,0:T(8,128)} %tile.1), custom_call_target="tpu_custom_call" | custom-call | bytes 6291456 | tf_op jit(solution)/shard_map/fetch/pallas_call | solution.py:81
  5.3 0.0 copy-start
  5.3 0.0 copy-start.1
  5.3 0.0 copy-start.3
  5.3 0.0 copy-start.4
  5.4 0.0 copy-start.5
  5.4 6.7 %all-to-all-start = ((bf16[16,40,1024]{2,1,0:T(8,128)(2,1)}), bf16[16,40,1024]{2,1,0:T(8,128)(2,1)S(1)}, u32[]{:S(2)}, u32[]{:S(2)}) async-start(bf16[16,40,1024]{2,1,0:T(8,128)(2,1)} %get-tuple-element.16), calls=%async_computation | async-start | bytes 2621440 | tf_op jit(solution)/shard_map/all_to_all | solution.py:448
  12.1 0.0 copy-done
  12.1 0.0 copy-done.1
  12.1 0.0 copy-done.3
  12.1 0.0 copy-done.4
  12.1 0.0 copy-start.2
  12.1 1.0 copy-done.2
  13.1 6.8 %prepare.1 = (f32[2,40,32768]{2,1,0:T(8,128)}, s32[80]{0:T(128)S(1)}, s32[80]{0:T(128)S(1)}, bf16[24576,1024]{1,0:T(8,128)(2,1)}) custom-call(s32[16]{0:T(128)S(1)} %copy-done.3, s32[16]{0:T(128)S(1)} %copy-done.4, s32[1]{0:T(128)} %get-tuple-element.13.token, bf16[512,1024]{1,0:T(8,128)(2,1)S(1)} %copy-done.1, bf16[2,512,512]{2,1,0:T(8,128)(2,1)S(1)} %copy-done, ...), custom_call_target="tpu_custom_call" | custom-call | bytes 115343360 | tf_op jit(solution)/shard_map/prepare/pallas_call | solution.py:156
  19.9 22.7 %all-to-all-done = bf16[16,40,1024]{2,1,0:T(8,128)(2,1)S(1)} async-done(((bf16[16,40,1024]{2,1,0:T(8,128)(2,1)}), bf16[16,40,1024]{2,1,0:T(8,128)(2,1)S(1)}, u32[]{:S(2)}, u32[]{:S(2)}) %all-to-all-start) | async-done | bytes 1310752 | tf_op jit(solution)/shard_map/all_to_all | solution.py:448
  42.6 0.0 copy-done.5
  42.6 8.4 %slot.1 = (bf16[512,1024]{1,0:T(8,128)(2,1)S(1)}, f32[256,1024]{1,0:T(8,128)S(1)}, bf16[256,1024]{1,0:T(8,128)(2,1)}) custom-call(s32[16]{0:T(128)S(1)} %copy-done.3, s32[16]{0:T(128)S(1)} %copy-done.5, s32[80]{0:T(128)S(1)} %get-tuple-element.15.owners, bf16[640,1024]{1,0:T(8,128)(2,1)S(1)} %bitcast.5, bf16[24576,1024]{1,0:T(8,128)(2,1)} %get-tuple-element.17.stock), custom_call_target="tpu_custom_call" | custom-call | flops 4294967296 | bytes 8388608 | tf_op jit(solution)/shard_map/slot/pallas_call | solution.py:278
  51.0 0.3 collective-permute-start
  51.3 2.0 %collective-permute-done = bf16[256,1024]{1,0:T(8,128)(2,1)} collective-permute-done((bf16[256,1024]{1,0:T(8,128)(2,1)}, bf16[256,1024]{1,0:T(8,128)(2,1)}, u32[]{:S(2)}, u32[]{:S(2)}) %collective-permute-start) | collective-permute-done | bytes 524320 | tf_op jit(solution)/shard_map/ppermute | solution.py:406
  53.3 1.2 %convert_add_fusion = f32[256,1024]{1,0:T(8,128)S(1)} fusion(f32[256,1024]{1,0:T(8,128)S(1)} %get-tuple-element.19, bf16[256,1024]{1,0:T(8,128)(2,1)} %collective-permute-done), kind=kLoop, calls=%fused_computation.4 | loop fusion | flops 524288 | bytes 2621440 | tf_op jit(solution)/shard_map/add | solution.py:411
  54.6 0.1 collective-permute-start.1
  54.7 7.6 %collective-permute-done.1 = bf16[128,1024]{1,0:T(8,128)(2,1)S(1)} collective-permute-done((bf16[128,1024]{1,0:T(8,128)(2,1)S(1)}, bf16[128,1024]{1,0:T(8,128)(2,1)S(1)}, u32[]{:S(2)}, u32[]{:S(2)}) %collective-permute-start.1) | collective-permute-done | bytes 262176 | tf_op jit(solution)/shard_map/ppermute | solution.py:406
  62.4 0.1 convert_add_fusion.1
  62.5 0.4 collective-permute-start.4
  62.9 0.8 collective-permute-start.3
  63.7 1.5 %collective-permute-start.2 = (bf16[32,1024]{1,0:T(8,128)(2,1)S(1)}, bf16[32,1024]{1,0:T(8,128)(2,1)S(1)}, u32[]{:S(2)}, u32[]{:S(2)}) collective-permute-start(bf16[32,1024]{1,0:T(8,128)(2,1)S(1)} %get-tuple-element.30), channel_id=1, source_target_pairs={{0,4},{1,5},{2,6},{3,7},{4,0},{5,1},{6,2},{7,3},{8,12},{9,13},{10,... | collective-permute-start | bytes 196616 | tf_op jit(solution)/shard_map/ppermute | solution.py:406
  65.2 2.2 %pack.1 = bf16[16,40,1024]{2,1,0:T(8,128)(2,1)} custom-call(s32[16]{0:T(128)S(1)} %copy-done.3, s32[16]{0:T(128)S(1)} %copy-done.5, bf16[512,1024]{1,0:T(8,128)(2,1)S(1)} %get-tuple-element.18.term), custom_call_target="tpu_custom_call" | custom-call | bytes 3145728 | tf_op jit(solution)/shard_map/pack/pallas_call | solution.py:325
  67.4 0.3 collective-permute-done.4
  67.7 0.0 collective-permute-done.3
  67.7 1.1 collective-permute-done.2
  68.9 0.9 collective-permute-start.5
  69.8 3.4 %collective-permute-start.6 = (bf16[32,1024]{1,0:T(8,128)(2,1)S(1)}, bf16[32,1024]{1,0:T(8,128)(2,1)S(1)}, u32[]{:S(2)}, u32[]{:S(2)}) collective-permute-start(bf16[32,1024]{1,0:T(8,128)(2,1)S(1)} %multiply_convert_fusion), channel_id=1, source_target_pairs={{0,8},{1,9},{2,10},{3,11},{4,12},{5,13},{6,14},{7,15},{8,0},{9,1},... | collective-permute-start | bytes 196616 | tf_op jit(solution)/shard_map/ppermute | solution.py:406
  73.2 0.0 collective-permute-start.7
  73.2 7.5 %all-to-all-start.1 = ((bf16[16,40,1024]{2,1,0:T(8,128)(2,1)}), bf16[16,40,1024]{2,1,0:T(8,128)(2,1)S(1)}, u32[]{:S(2)}, u32[]{:S(2)}) async-start(bf16[16,40,1024]{2,1,0:T(8,128)(2,1)} %pack.1), calls=%async_computation.1 | async-start | bytes 2621440 | tf_op jit(solution)/shard_map/all_to_all | solution.py:457
  80.7 0.0 collective-permute-done.5
  80.7 0.0 collective-permute-done.6
  80.7 0.0 collective-permute-done.7
  80.8 0.3 collective-permute-start.8
  81.2 13.5 %collective-permute-done.8 = bf16[128,1024]{1,0:T(8,128)(2,1)S(1)} collective-permute-done((bf16[128,1024]{1,0:T(8,128)(2,1)S(1)}, bf16[128,1024]{1,0:T(8,128)(2,1)S(1)}, u32[]{:S(2)}, u32[]{:S(2)}) %collective-permute-start.8) | collective-permute-done | bytes 262176 | tf_op jit(solution)/shard_map/ppermute | solution.py:406
  94.7 0.1 broadcast_select_fusion.3
  94.9 2.6 %collective-permute-start.9 = (bf16[256,1024]{1,0:T(8,128)(2,1)S(1)}, bf16[256,1024]{1,0:T(8,128)(2,1)S(1)}, u32[]{:S(2)}, u32[]{:S(2)}) collective-permute-start(bf16[256,1024]{1,0:T(8,128)(2,1)S(1)} %pad_maximum_fusion.1), channel_id=1, source_target_pairs={{0,1},{1,0},{2,3},{3,2},{4,5},{5,4},{6,7},{7,6},{8,9},{9,8},{10,11... | collective-permute-start | bytes 1572872 | tf_op jit(solution)/shard_map/ppermute | solution.py:406
  97.5 1.5 %collective-permute-done.9 = bf16[256,1024]{1,0:T(8,128)(2,1)S(1)} collective-permute-done((bf16[256,1024]{1,0:T(8,128)(2,1)S(1)}, bf16[256,1024]{1,0:T(8,128)(2,1)S(1)}, u32[]{:S(2)}, u32[]{:S(2)}) %collective-permute-start.9) | collective-permute-done | bytes 524320 | tf_op jit(solution)/shard_map/ppermute | solution.py:406
  99.0 0.2 broadcast_select_fusion.1
  99.3 0.2 maximum_convert_fusion
  99.5 0.2 slice_bitcast_fusion.1
  99.7 1.5 %pad_maximum_fusion = f32[2,512,512]{2,1,0:T(8,128)} fusion(f32[1,512,512]{2,1,0:T(8,128)S(1)} %get-tuple-element.25, f32[1,512,512]{2,1,0:T(8,128)S(1)} %get-tuple-element.24), kind=kLoop, calls=%fused_computation | loop fusion | flops 524288 | bytes 4194304 | tf_op jit(solution)/shard_map/stack | solution.py:460
  101.2 10.1 %all-to-all-done.1.terms = bf16[16,40,1024]{2,1,0:T(8,128)(2,1)S(1)} async-done(((bf16[16,40,1024]{2,1,0:T(8,128)(2,1)}), bf16[16,40,1024]{2,1,0:T(8,128)(2,1)S(1)}, u32[]{:S(2)}, u32[]{:S(2)}) %all-to-all-start.1) | async-done | bytes 1310752 | tf_op jit(solution)/shard_map/all_to_all | solution.py:457
  111.3 4.2 %place.1 = f32[2,40,32768]{2,1,0:T(8,128)} custom-call(s32[16]{0:T(128)S(1)} %copy-done.3, s32[16]{0:T(128)S(1)} %copy-done.4, s32[80]{0:T(128)S(1)} %get-tuple-element.14.blocks, s32[80]{0:T(128)S(1)} %get-tuple-element.15.owners, bf16[16,40,1024]{2,1,0:T(8,128)(2,1)S(1)} %all-to-all-done.1.terms, ...), custom_call_target="tpu_custom_call", output_to_operand_aliasing={{}: (5, {})} | custom-call | bytes 6291456 | tf_op jit(solution)/shard_map/place/pallas_call | solution.py:380
  (7 shorter events, 0.2 us)
Async XLA Ops:
  5.3 6.8 %copy-start = (bf16[2,512,512]{2,1,0:T(8,128)(2,1)S(1)}, bf16[2,512,512]{2,1,0:T(8,128)(2,1)}, u32[]{:S(2)}) copy-start(bf16[2,512,512]{2,1,0:T(8,128)(2,1)} %probe.1) | copy-start | bytes 3145732
  5.3 6.8 %copy-start.1 = (bf16[512,1024]{1,0:T(8,128)(2,1)S(1)}, bf16[512,1024]{1,0:T(8,128)(2,1)}, u32[]{:S(2)}) copy-start(bf16[512,1024]{1,0:T(8,128)(2,1)} %constant.79.clone.table_in) | copy-start | bytes 3145732
  5.3 6.8 %copy-start.3 = (s32[16]{0:T(128)S(1)}, s32[16]{0:T(128)}, u32[]{:S(2)}) copy-start(s32[16]{0:T(128)} %dealing.9) | copy-start | bytes 196
  5.3 6.8 %copy-start.4 = (s32[16]{0:T(128)S(1)}, s32[16]{0:T(128)}, u32[]{:S(2)}) copy-start(s32[16]{0:T(128)} %cols.5) | copy-start | bytes 196
  5.4 37.3 %copy-start.5 = (s32[16]{0:T(128)S(1)}, s32[16]{0:T(128)}, u32[]{:S(2)}) copy-start(s32[16]{0:T(128)} %rows.3) | copy-start | bytes 196
  5.4 37.3 %all-to-all-start = ((bf16[16,40,1024]{2,1,0:T(8,128)(2,1)}), bf16[16,40,1024]{2,1,0:T(8,128)(2,1)S(1)}, u32[]{:S(2)}, u32[]{:S(2)}) async-start(bf16[16,40,1024]{2,1,0:T(8,128)(2,1)} %get-tuple-element.16), calls=%async_computation | async-start | bytes 2621440 | tf_op jit(solution)/shard_map/all_to_all | solution.py:448
  12.1 1.0 copy-start.2
  51.0 2.3 %collective-permute-start = (bf16[256,1024]{1,0:T(8,128)(2,1)}, bf16[256,1024]{1,0:T(8,128)(2,1)}, u32[]{:S(2)}, u32[]{:S(2)}) collective-permute-start(bf16[256,1024]{1,0:T(8,128)(2,1)} %get-tuple-element.20), channel_id=1, source_target_pairs={{0,1},{1,0},{2,3},{3,2},{4,5},{5,4},{6,7},{7,6},{8,9},{9,8},{10,11... | collective-permute-start | bytes 1572872 | tf_op jit(solution)/shard_map/ppermute | solution.py:406
  54.6 7.8 %collective-permute-start.1 = (bf16[128,1024]{1,0:T(8,128)(2,1)S(1)}, bf16[128,1024]{1,0:T(8,128)(2,1)S(1)}, u32[]{:S(2)}, u32[]{:S(2)}) collective-permute-start(bf16[128,1024]{1,0:T(8,128)(2,1)S(1)} %dynamic-slice_convert_fusion), channel_id=1, source_target_pairs={{0,2},{1,3},{2,0},{3,1},{4,6},{5,7},{6,4},{7,5},{8,10},{9,11},{10,... | collective-permute-start | bytes 786440 | tf_op jit(solution)/shard_map/ppermute | solution.py:406
  62.5 5.2 %collective-permute-start.4 = (bf16[32,1024]{1,0:T(8,128)(2,1)S(1)}, bf16[32,1024]{1,0:T(8,128)(2,1)S(1)}, u32[]{:S(2)}, u32[]{:S(2)}) collective-permute-start(bf16[32,1024]{1,0:T(8,128)(2,1)S(1)} %get-tuple-element.31), channel_id=1, source_target_pairs={{0,12},{1,13},{2,14},{3,15},{4,8},{5,9},{6,10},{7,11},{8,4},{9,5},... | collective-permute-start | bytes 196616 | tf_op jit(solution)/shard_map/ppermute | solution.py:406
  62.9 4.8 %collective-permute-start.3 = (bf16[32,1024]{1,0:T(8,128)(2,1)S(1)}, bf16[32,1024]{1,0:T(8,128)(2,1)S(1)}, u32[]{:S(2)}, u32[]{:S(2)}) collective-permute-start(bf16[32,1024]{1,0:T(8,128)(2,1)S(1)} %get-tuple-element.32), channel_id=1, source_target_pairs={{0,8},{1,9},{2,10},{3,11},{4,12},{5,13},{6,14},{7,15},{8,0},{9,1},... | collective-permute-start | bytes 196616 | tf_op jit(solution)/shard_map/ppermute | solution.py:406
  63.7 5.1 %collective-permute-start.2 = (bf16[32,1024]{1,0:T(8,128)(2,1)S(1)}, bf16[32,1024]{1,0:T(8,128)(2,1)S(1)}, u32[]{:S(2)}, u32[]{:S(2)}) collective-permute-start(bf16[32,1024]{1,0:T(8,128)(2,1)S(1)} %get-tuple-element.30), channel_id=1, source_target_pairs={{0,4},{1,5},{2,6},{3,7},{4,0},{5,1},{6,2},{7,3},{8,12},{9,13},{10,... | collective-permute-start | bytes 196616 | tf_op jit(solution)/shard_map/ppermute | solution.py:406
  68.9 11.8 %collective-permute-start.5 = (bf16[32,1024]{1,0:T(8,128)(2,1)S(1)}, bf16[32,1024]{1,0:T(8,128)(2,1)S(1)}, u32[]{:S(2)}, u32[]{:S(2)}) collective-permute-start(bf16[32,1024]{1,0:T(8,128)(2,1)S(1)} %multiply_convert_fusion), channel_id=1, source_target_pairs={{0,12},{1,13},{2,14},{3,15},{4,8},{5,9},{6,10},{7,11},{8,4},{9,5},... | collective-permute-start | bytes 196616 | tf_op jit(solution)/shard_map/ppermute | solution.py:406
  69.8 10.9 %collective-permute-start.6 = (bf16[32,1024]{1,0:T(8,128)(2,1)S(1)}, bf16[32,1024]{1,0:T(8,128)(2,1)S(1)}, u32[]{:S(2)}, u32[]{:S(2)}) collective-permute-start(bf16[32,1024]{1,0:T(8,128)(2,1)S(1)} %multiply_convert_fusion), channel_id=1, source_target_pairs={{0,8},{1,9},{2,10},{3,11},{4,12},{5,13},{6,14},{7,15},{8,0},{9,1},... | collective-permute-start | bytes 196616 | tf_op jit(solution)/shard_map/ppermute | solution.py:406
  73.2 7.5 %collective-permute-start.7 = (bf16[32,1024]{1,0:T(8,128)(2,1)S(1)}, bf16[32,1024]{1,0:T(8,128)(2,1)S(1)}, u32[]{:S(2)}, u32[]{:S(2)}) collective-permute-start(bf16[32,1024]{1,0:T(8,128)(2,1)S(1)} %multiply_convert_fusion), channel_id=1, source_target_pairs={{0,4},{1,5},{2,6},{3,7},{4,0},{5,1},{6,2},{7,3},{8,12},{9,13},{10,... | collective-permute-start | bytes 196616 | tf_op jit(solution)/shard_map/ppermute | solution.py:406
  73.2 38.0 %all-to-all-start.1 = ((bf16[16,40,1024]{2,1,0:T(8,128)(2,1)}), bf16[16,40,1024]{2,1,0:T(8,128)(2,1)S(1)}, u32[]{:S(2)}, u32[]{:S(2)}) async-start(bf16[16,40,1024]{2,1,0:T(8,128)(2,1)} %pack.1), calls=%async_computation.1 | async-start | bytes 2621440 | tf_op jit(solution)/shard_map/all_to_all | solution.py:457
  80.8 13.9 %collective-permute-start.8 = (bf16[128,1024]{1,0:T(8,128)(2,1)S(1)}, bf16[128,1024]{1,0:T(8,128)(2,1)S(1)}, u32[]{:S(2)}, u32[]{:S(2)}) collective-permute-start(bf16[128,1024]{1,0:T(8,128)(2,1)S(1)} %pad_maximum_fusion.2), channel_id=1, source_target_pairs={{0,2},{1,3},{2,0},{3,1},{4,6},{5,7},{6,4},{7,5},{8,10},{9,11},{10,... | collective-permute-start | bytes 786440 | tf_op jit(solution)/shard_map/ppermute | solution.py:406
  94.9 4.2 %collective-permute-start.9 = (bf16[256,1024]{1,0:T(8,128)(2,1)S(1)}, bf16[256,1024]{1,0:T(8,128)(2,1)S(1)}, u32[]{:S(2)}, u32[]{:S(2)}) collective-permute-start(bf16[256,1024]{1,0:T(8,128)(2,1)S(1)} %pad_maximum_fusion.1), channel_id=1, source_target_pairs={{0,1},{1,0},{2,3},{3,2},{4,5},{5,4},{6,7},{7,6},{8,9},{9,8},{10,11... | collective-permute-start | bytes 1572872 | tf_op jit(solution)/shard_map/ppermute | solution.py:406

commit v17 on v16

--- a/solution.py
+++ b/solution.py
@@ -42,7 +42,7 @@
     return picked.reshape(count, width)
 
 
-def fetch_kernel(order, dealing, cols, tile, out, token, held, sems):
+def fetch_kernel(order, dealing, cols, tile, out, token, held, cut, sems, out_sems):
     token[0] = dealing[0]
     slots, tile_rows = out.shape[0], out.shape[1]
     tile_cols = tile.shape[2]
@@ -58,8 +58,7 @@
 
     lane = lax.broadcasted_iota(jnp.int32, (tile_rows, LANES), 1)
 
-    @pl.loop(0, slots, unroll=4)
-    def _(slot):
+    def cut_slot(slot):
         copy(slot).wait()
         _, offset = window_start(cols[dealing[slot]], order, tile_cols)
         shift = lax.rem(LANES - lax.rem(offset, LANES), LANES)
@@ -70,8 +69,22 @@
             ]
             for b in range(order // LANES):
                 first = part * order + b * LANES
-                cells = jnp.where(lane < LANES - offset, turned[b], turned[b + 1])
-                out[slot, :, first : first + LANES] = cells
+                cut[slot, :, first : first + LANES] = jnp.where(lane < LANES - offset, turned[b], turned[b + 1])
+
+    group = slots // out_sems.shape[0]
+    sends = []
+    for g in range(out_sems.shape[0]):
+
+        @pl.loop(g * group, (g + 1) * group, unroll=4)
+        def _(slot):
+            cut_slot(slot)
+
+        here = slice(g * group, (g + 1) * group)
+        send = pltpu.make_async_copy(cut.at[here], out.at[here], out_sems.at[g])
+        send.start()
+        sends.append(send)
+    for send in sends:
+        send.wait()
 
 
 def fetch_windows(tile, dealing, cols, order):
@@ -85,10 +98,12 @@
             jax.ShapeDtypeStruct((1,), jnp.int32),
         ),
         in_specs=[SMEM, SMEM, ANY],
-        out_specs=(VMEM, SMEM),
+        out_specs=(ANY, SMEM),
         scratch_shapes=[
             pltpu.VMEM((slots, 2, tile_rows, span), jnp.float32),
+            pltpu.VMEM((slots, tile_rows, 2 * order), jnp.bfloat16),
             pltpu.SemaphoreType.DMA((slots,)),
+            pltpu.SemaphoreType.DMA((4,)),
         ],
         compiler_params=pltpu.CompilerParams(vmem_limit_bytes=56 * 2**20),
         cost_estimate=pl.CostEstimate(flops=0, bytes_accessed=6 * 2**20, transcendentals=0),
@@ -182,8 +197,8 @@
 ):
     del owners
     order = term.shape[0]
-    places = stock_places(stock, order)
-    targets = (probe.at[0], probe.at[1], table, measured)
+    places = (stock.at[0:order, :],) + stock_places(stock, order)[2:]
+    targets = (probe, table, measured)
     loads = [
         pltpu.make_async_copy(source, target, sems.at[k])
         for k, (source, target) in enumerate(zip(places, targets))
@@ -205,19 +220,18 @@
         patch[place, :] = rows_from(wide, first_row + i * step, step).astype(patch.dtype)
 
     loads[0].wait()
-    loads[1].wait()
 
     @pl.loop(0, order // step, unroll=2)
     def _(i):
         place = pl.ds(pl.multiple_of(i * step, step), step)
         found = patch[place, :].astype(jnp.float32)
         real, imag = found[:, :order], found[:, order:]
-        probe_real = probe[0, place, :].astype(jnp.float32)
-        probe_imag = probe[1, place, :].astype(jnp.float32)
+        probe_real = probe[place, :order].astype(jnp.float32)
+        probe_imag = probe[place, order:].astype(jnp.float32)
         wave[place, :order] = (probe_real * real - probe_imag * imag).astype(wave.dtype)
         wave[place, order:] = (probe_real * imag + probe_imag * real).astype(wave.dtype)
 
-    loads[2].wait()
+    loads[1].wait()
     minus[...] = -table[:, order:]
     cos, sin = table.at[:, :order], table.at[:, order:]
     first_half, second_half = slice(0, order), slice(order, 2 * order)
@@ -231,7 +245,7 @@
         real, imag = wave[:, first_half], wave[:, second_half]
         half[first_half, here] = dots(real, cos[:, here], imag, minus[:, here]).astype(half.dtype)
         half[second_half, here] = dots(real, sin[:, here], imag, cos[:, here]).astype(half.dtype)
-    loads[3].wait()
+    loads[2].wait()
     for first in range(0, order, tile):
         here = slice(first, first + tile)
         there = slice(order + first, order + first + tile)
@@ -257,8 +271,8 @@
             turned_real, turned_imag = turned[first_half, here], turned[second_half, here]
             real = dots(cos[line, :], turned_real, sin[line, :], turned_imag)
             imag = dots(minus[line, :], turned_real, cos[line, :], turned_imag)
-            probe_real = probe[0, line, here].astype(jnp.float32)
-            probe_imag = probe[1, line, here].astype(jnp.float32)
+            probe_real = probe[line, here].astype(jnp.float32)
+            probe_imag = probe[line, there].astype(jnp.float32)
             term[line, here] = (probe_real * real + probe_imag * imag).astype(term.dtype)
             term[line, there] = (probe_real * imag - probe_imag * real).astype(term.dtype)
             patch_real = patch[line, here].astype(jnp.float32)
@@ -292,11 +306,11 @@
             pltpu.VMEM((order, wide_cols), bf16),
             pltpu.VMEM((wide_cols, order), bf16),
             pltpu.VMEM((order, wide_cols), f32),
-            pltpu.VMEM((2, order, order), bf16),
+            pltpu.VMEM((order, wide_cols), bf16),
             pltpu.VMEM((order, wide_cols), bf16),
             pltpu.VMEM((order, order), bf16),
             pltpu.VMEM((order, order), bf16),
-            pltpu.SemaphoreType.DMA((4,)),
+            pltpu.SemaphoreType.DMA((3,)),
         ],
         compiler_params=pltpu.CompilerParams(vmem_limit_bytes=24 * 2**20),
         cost_estimate=pl.CostEstimate(
@@ -408,16 +422,24 @@
 
 def sum_probe(kept, sent, devices):
     me = lax.axis_index("row")
-    total = kept + swap(sent, 1, devices).astype(jnp.float32)
+    addends = [kept, swap(sent, 1, devices)]
+
+    def rows(index, count):
+        found = [lax.dynamic_slice_in_dim(x, index * count, count).astype(jnp.float32) for x in addends]
+        return found[0] + found[1]
+
     for stride, radix in strides(devices)[1:]:
         digit = me // stride % radix
-        count = total.shape[0] // radix
-        own = lax.dynamic_slice_in_dim(total, digit * count, count)
+        count = addends[0].shape[0] // radix
+        met = []
         for k in range(1, radix):
-            share = lax.dynamic_slice_in_dim(total, lax.bitwise_xor(digit, k) * count, count)
-            own = own + swap(share.astype(jnp.bfloat16), k * stride, devices).astype(jnp.float32)
-        total = own
-    return total
+            share = rows(lax.bitwise_xor(digit, k), count).astype(jnp.bfloat16)
+            met.append(swap(share, k * stride, devices))
+        own = rows(digit, count)
+        for one in met[:-1]:
+            own = own + one.astype(jnp.float32)
+        addends = [own, met[-1]]
+    return addends[0] + addends[1].astype(jnp.float32)
 
 
 def join(whole, devices):

time: 116 us -> 115 us (level)
    add x3 -> x1, other arithmetic: 1.31 us -> 0.04 us  [sum_probe(): return addends[0] + addends[1].astype(jnp.float32)]
where the time goes in v17:
time: 115 us; the launch traced here: 114 us
  waiting for transfers between devices  58.9 us (51%)
  Pallas kernels  26.4 us (23%)
  starting transfers between devices  24.6 us (21%)
  other arithmetic  2.4 us (2%)
  local copies, waits for them, and re-layouts  1.26 us (1%)
    ppermute x10, waiting for transfers between devices, swap(): return lax.ppermute(x, 'row', [(d, d ^ distance) for d in range(devices)])  26 us
    all_to_all x1, waiting for transfers between devices, body(): lax.all_to_all(pieces, 'row', split_axis=0, concat_axis=0, tiled=True)  22.8 us
    ppermute x10, starting transfers between devices, swap(): return lax.ppermute(x, 'row', [(d, d ^ distance) for d in range(devices)])  10.4 us
    all_to_all x1, waiting for transfers between devices, body(): lax.all_to_all(terms, 'row', split_axis=0, concat_axis=0, tiled=True)  10.1 us
    pallas_call x1, Pallas kernels, slot_terms(): pl.pallas_call(slot_kernel, out_shape=(jax.ShapeDtypeStruct((order, wide_...  8.39 us
    all_to_all x1, starting transfers between devices, body(): lax.all_to_all(terms, 'row', split_axis=0, concat_axis=0, tiled=True)  7.49 us
    all_to_all x1, starting transfers between devices, body(): lax.all_to_all(pieces, 'row', split_axis=0, concat_axis=0, tiled=True)  6.7 us
    pallas_call x1, Pallas kernels, prepare(): pl.pallas_call(functools.partial(prepare_kernel, order), out_shape=(jax.S...  6.69 us
  transfers between devices with their start and end apart: 12, of which 8 were waited for; matrix products, arithmetic and copies ran while one was open for 2% of the time, Pallas kernels for 8%

profile of v17, /device:TPU:15, one launch (start us, length us, event | category | flops | bytes accessed | tf_op | source)
XLA Modules:
  0.0 114.4 jit_solution(3548218188933994927)
XLA Ops:
  0.6 4.9 %fetch.1 = (bf16[16,40,1024]{2,1,0:T(8,128)(2,1)}, s32[1]{0:T(128)}) custom-call(s32[16]{0:T(128)} %dealing.9, s32[16]{0:T(128)} %cols.5, f32[2,40,32768]{2,1,0:T(8,128)} %tile.1), custom_call_target="tpu_custom_call" | custom-call | bytes 6291456 | tf_op jit(solution)/shard_map/fetch/pallas_call | solution.py:94
  5.5 0.0 copy-start
  5.5 0.0 copy-start.1
  5.5 0.0 copy-start.3
  5.6 0.0 copy-start.4
  5.6 0.0 copy-start.5
  5.6 6.7 %all-to-all-start = ((bf16[16,40,1024]{2,1,0:T(8,128)(2,1)}), bf16[16,40,1024]{2,1,0:T(8,128)(2,1)S(1)}, u32[]{:S(2)}, u32[]{:S(2)}) async-start(bf16[16,40,1024]{2,1,0:T(8,128)(2,1)} %get-tuple-element.16), calls=%async_computation | async-start | bytes 2621440 | tf_op jit(solution)/shard_map/all_to_all | solution.py:470
  12.3 0.0 copy-done
  12.3 0.0 copy-done.1
  12.3 0.0 copy-done.3
  12.3 0.0 copy-done.4
  12.3 0.0 copy-start.2
  12.3 1.0 copy-done.2
  13.4 6.7 %prepare.1 = (f32[2,40,32768]{2,1,0:T(8,128)}, s32[80]{0:T(128)S(1)}, s32[80]{0:T(128)S(1)}, bf16[24576,1024]{1,0:T(8,128)(2,1)}) custom-call(s32[16]{0:T(128)S(1)} %copy-done.3, s32[16]{0:T(128)S(1)} %copy-done.4, s32[1]{0:T(128)} %get-tuple-element.13.token, bf16[512,1024]{1,0:T(8,128)(2,1)S(1)} %copy-done.1, bf16[2,512,512]{2,1,0:T(8,128)(2,1)S(1)} %copy-done, ...), custom_call_target="tpu_custom_call" | custom-call | bytes 115343360 | tf_op jit(solution)/shard_map/prepare/pallas_call | solution.py:171
  20.1 22.8 %all-to-all-done = bf16[16,40,1024]{2,1,0:T(8,128)(2,1)S(1)} async-done(((bf16[16,40,1024]{2,1,0:T(8,128)(2,1)}), bf16[16,40,1024]{2,1,0:T(8,128)(2,1)S(1)}, u32[]{:S(2)}, u32[]{:S(2)}) %all-to-all-start) | async-done | bytes 1310752 | tf_op jit(solution)/shard_map/all_to_all | solution.py:470
  42.8 0.0 copy-done.5
  42.9 8.4 %slot.1 = (bf16[512,1024]{1,0:T(8,128)(2,1)S(1)}, f32[256,1024]{1,0:T(8,128)S(1)}, bf16[256,1024]{1,0:T(8,128)(2,1)}) custom-call(s32[16]{0:T(128)S(1)} %copy-done.3, s32[16]{0:T(128)S(1)} %copy-done.5, s32[80]{0:T(128)S(1)} %get-tuple-element.15.owners, bf16[640,1024]{1,0:T(8,128)(2,1)S(1)} %bitcast.5, bf16[24576,1024]{1,0:T(8,128)(2,1)} %get-tuple-element.17.stock), custom_call_target="tpu_custom_call" | custom-call | flops 4294967296 | bytes 8388608 | tf_op jit(solution)/shard_map/slot/pallas_call | solution.py:292
  51.2 0.3 collective-permute-start
  51.5 1.9 %collective-permute-done = bf16[256,1024]{1,0:T(8,128)(2,1)S(1)} collective-permute-done((bf16[256,1024]{1,0:T(8,128)(2,1)}, bf16[256,1024]{1,0:T(8,128)(2,1)S(1)}, u32[]{:S(2)}, u32[]{:S(2)}) %collective-permute-start) | collective-permute-done | bytes 524320 | tf_op jit(solution)/shard_map/ppermute | solution.py:420
  53.4 0.1 add_convert_fusion
  53.6 0.1 collective-permute-start.1
  53.7 7.6 %collective-permute-done.1 = bf16[128,1024]{1,0:T(8,128)(2,1)S(1)} collective-permute-done((bf16[128,1024]{1,0:T(8,128)(2,1)S(1)}, bf16[128,1024]{1,0:T(8,128)(2,1)S(1)}, u32[]{:S(2)}, u32[]{:S(2)}) %collective-permute-start.1) | collective-permute-done | bytes 262176 | tf_op jit(solution)/shard_map/ppermute | solution.py:420
  61.4 0.4 collective-permute-start.4
  61.8 0.8 collective-permute-start.3
  62.6 1.5 %collective-permute-start.2 = (bf16[32,1024]{1,0:T(8,128)(2,1)S(1)}, bf16[32,1024]{1,0:T(8,128)(2,1)S(1)}, u32[]{:S(2)}, u32[]{:S(2)}) collective-permute-start(bf16[32,1024]{1,0:T(8,128)(2,1)S(1)} %get-tuple-element.30), channel_id=1, source_target_pairs={{0,4},{1,5},{2,6},{3,7},{4,0},{5,1},{6,2},{7,3},{8,12},{9,13},{10,... | collective-permute-start | bytes 196616 | tf_op jit(solution)/shard_map/ppermute | solution.py:420
  64.1 2.2 %pack.1 = bf16[16,40,1024]{2,1,0:T(8,128)(2,1)} custom-call(s32[16]{0:T(128)S(1)} %copy-done.3, s32[16]{0:T(128)S(1)} %copy-done.5, bf16[512,1024]{1,0:T(8,128)(2,1)S(1)} %get-tuple-element.18.term), custom_call_target="tpu_custom_call" | custom-call | bytes 3145728 | tf_op jit(solution)/shard_map/pack/pallas_call | solution.py:339
  66.3 0.3 collective-permute-done.4
  66.6 0.0 collective-permute-done.3
  66.6 1.1 collective-permute-done.2
  67.8 0.9 collective-permute-start.5
  68.7 3.4 %collective-permute-start.6 = (bf16[32,1024]{1,0:T(8,128)(2,1)S(1)}, bf16[32,1024]{1,0:T(8,128)(2,1)S(1)}, u32[]{:S(2)}, u32[]{:S(2)}) collective-permute-start(bf16[32,1024]{1,0:T(8,128)(2,1)S(1)} %multiply_convert_fusion), channel_id=1, source_target_pairs={{0,8},{1,9},{2,10},{3,11},{4,12},{5,13},{6,14},{7,15},{8,0},{9,1},... | collective-permute-start | bytes 196616 | tf_op jit(solution)/shard_map/ppermute | solution.py:420
  72.1 0.0 collective-permute-start.7
  72.1 7.5 %all-to-all-start.1 = ((bf16[16,40,1024]{2,1,0:T(8,128)(2,1)}), bf16[16,40,1024]{2,1,0:T(8,128)(2,1)S(1)}, u32[]{:S(2)}, u32[]{:S(2)}) async-start(bf16[16,40,1024]{2,1,0:T(8,128)(2,1)} %pack.1), calls=%async_computation.1 | async-start | bytes 2621440 | tf_op jit(solution)/shard_map/all_to_all | solution.py:479
  79.6 0.0 collective-permute-done.5
  79.6 0.0 collective-permute-done.6
  79.6 0.0 collective-permute-done.7
  79.7 0.3 collective-permute-start.8
  80.1 13.5 %collective-permute-done.8 = bf16[128,1024]{1,0:T(8,128)(2,1)S(1)} collective-permute-done((bf16[128,1024]{1,0:T(8,128)(2,1)S(1)}, bf16[128,1024]{1,0:T(8,128)(2,1)S(1)}, u32[]{:S(2)}, u32[]{:S(2)}) %collective-permute-start.8) | collective-permute-done | bytes 262176 | tf_op jit(solution)/shard_map/ppermute | solution.py:420
  93.6 0.1 broadcast_select_fusion.3
  93.8 2.6 %collective-permute-start.9 = (bf16[256,1024]{1,0:T(8,128)(2,1)S(1)}, bf16[256,1024]{1,0:T(8,128)(2,1)S(1)}, u32[]{:S(2)}, u32[]{:S(2)}) collective-permute-start(bf16[256,1024]{1,0:T(8,128)(2,1)S(1)} %pad_maximum_fusion.1), channel_id=1, source_target_pairs={{0,1},{1,0},{2,3},{3,2},{4,5},{5,4},{6,7},{7,6},{8,9},{9,8},{10,11... | collective-permute-start | bytes 1572872 | tf_op jit(solution)/shard_map/ppermute | solution.py:420
  96.4 1.5 %collective-permute-done.9 = bf16[256,1024]{1,0:T(8,128)(2,1)S(1)} collective-permute-done((bf16[256,1024]{1,0:T(8,128)(2,1)S(1)}, bf16[256,1024]{1,0:T(8,128)(2,1)S(1)}, u32[]{:S(2)}, u32[]{:S(2)}) %collective-permute-start.9) | collective-permute-done | bytes 524320 | tf_op jit(solution)/shard_map/ppermute | solution.py:420
  97.9 0.2 broadcast_select_fusion.1
  98.2 0.2 maximum_convert_fusion
  98.4 0.2 slice_bitcast_fusion.1
  98.6 1.5 %pad_maximum_fusion = f32[2,512,512]{2,1,0:T(8,128)} fusion(f32[1,512,512]{2,1,0:T(8,128)S(1)} %get-tuple-element.25, f32[1,512,512]{2,1,0:T(8,128)S(1)} %get-tuple-element.24), kind=kLoop, calls=%fused_computation | loop fusion | flops 524288 | bytes 4194304 | tf_op jit(solution)/shard_map/stack | solution.py:482
  100.1 10.1 %all-to-all-done.1.terms = bf16[16,40,1024]{2,1,0:T(8,128)(2,1)S(1)} async-done(((bf16[16,40,1024]{2,1,0:T(8,128)(2,1)}), bf16[16,40,1024]{2,1,0:T(8,128)(2,1)S(1)}, u32[]{:S(2)}, u32[]{:S(2)}) %all-to-all-start.1) | async-done | bytes 1310752 | tf_op jit(solution)/shard_map/all_to_all | solution.py:479
  110.2 4.2 %place.1 = f32[2,40,32768]{2,1,0:T(8,128)} custom-call(s32[16]{0:T(128)S(1)} %copy-done.3, s32[16]{0:T(128)S(1)} %copy-done.4, s32[80]{0:T(128)S(1)} %get-tuple-element.14.blocks, s32[80]{0:T(128)S(1)} %get-tuple-element.15.owners, bf16[16,40,1024]{2,1,0:T(8,128)(2,1)S(1)} %all-to-all-done.1.terms, ...), custom_call_target="tpu_custom_call", output_to_operand_aliasing={{}: (5, {})} | custom-call | bytes 6291456 | tf_op jit(solution)/shard_map/place/pallas_call | solution.py:394
  (6 shorter events, 0.2 us)
Async XLA Ops:
  5.5 6.8 %copy-start = (bf16[2,512,512]{2,1,0:T(8,128)(2,1)S(1)}, bf16[2,512,512]{2,1,0:T(8,128)(2,1)}, u32[]{:S(2)}) copy-start(bf16[2,512,512]{2,1,0:T(8,128)(2,1)} %probe.1) | copy-start | bytes 3145732
  5.5 6.8 %copy-start.1 = (bf16[512,1024]{1,0:T(8,128)(2,1)S(1)}, bf16[512,1024]{1,0:T(8,128)(2,1)}, u32[]{:S(2)}) copy-start(bf16[512,1024]{1,0:T(8,128)(2,1)} %constant.79.clone.table_in) | copy-start | bytes 3145732
  5.5 6.8 %copy-start.3 = (s32[16]{0:T(128)S(1)}, s32[16]{0:T(128)}, u32[]{:S(2)}) copy-start(s32[16]{0:T(128)} %dealing.9) | copy-start | bytes 196
  5.6 6.8 %copy-start.4 = (s32[16]{0:T(128)S(1)}, s32[16]{0:T(128)}, u32[]{:S(2)}) copy-start(s32[16]{0:T(128)} %cols.5) | copy-start | bytes 196
  5.6 37.3 %copy-start.5 = (s32[16]{0:T(128)S(1)}, s32[16]{0:T(128)}, u32[]{:S(2)}) copy-start(s32[16]{0:T(128)} %rows.3) | copy-start | bytes 196
  5.6 37.3 %all-to-all-start = ((bf16[16,40,1024]{2,1,0:T(8,128)(2,1)}), bf16[16,40,1024]{2,1,0:T(8,128)(2,1)S(1)}, u32[]{:S(2)}, u32[]{:S(2)}) async-start(bf16[16,40,1024]{2,1,0:T(8,128)(2,1)} %get-tuple-element.16), calls=%async_computation | async-start | bytes 2621440 | tf_op jit(solution)/shard_map/all_to_all | solution.py:470
  12.3 1.0 copy-start.2
  51.2 2.2 %collective-permute-start = (bf16[256,1024]{1,0:T(8,128)(2,1)}, bf16[256,1024]{1,0:T(8,128)(2,1)S(1)}, u32[]{:S(2)}, u32[]{:S(2)}) collective-permute-start(bf16[256,1024]{1,0:T(8,128)(2,1)} %get-tuple-element.20), channel_id=1, source_target_pairs={{0,1},{1,0},{2,3},{3,2},{4,5},{5,4},{6,7},{7,6},{8,9},{9,8},{10,11... | collective-permute-start | bytes 1572872 | tf_op jit(solution)/shard_map/ppermute | solution.py:420
  53.6 7.8 %collective-permute-start.1 = (bf16[128,1024]{1,0:T(8,128)(2,1)S(1)}, bf16[128,1024]{1,0:T(8,128)(2,1)S(1)}, u32[]{:S(2)}, u32[]{:S(2)}) collective-permute-start(bf16[128,1024]{1,0:T(8,128)(2,1)S(1)} %get-tuple-element.26), channel_id=1, source_target_pairs={{0,2},{1,3},{2,0},{3,1},{4,6},{5,7},{6,4},{7,5},{8,10},{9,11},{10,... | collective-permute-start | bytes 786440 | tf_op jit(solution)/shard_map/ppermute | solution.py:420
  61.4 5.2 %collective-permute-start.4 = (bf16[32,1024]{1,0:T(8,128)(2,1)S(1)}, bf16[32,1024]{1,0:T(8,128)(2,1)S(1)}, u32[]{:S(2)}, u32[]{:S(2)}) collective-permute-start(bf16[32,1024]{1,0:T(8,128)(2,1)S(1)} %get-tuple-element.31), channel_id=1, source_target_pairs={{0,12},{1,13},{2,14},{3,15},{4,8},{5,9},{6,10},{7,11},{8,4},{9,5},... | collective-permute-start | bytes 196616 | tf_op jit(solution)/shard_map/ppermute | solution.py:420
  61.8 4.8 %collective-permute-start.3 = (bf16[32,1024]{1,0:T(8,128)(2,1)S(1)}, bf16[32,1024]{1,0:T(8,128)(2,1)S(1)}, u32[]{:S(2)}, u32[]{:S(2)}) collective-permute-start(bf16[32,1024]{1,0:T(8,128)(2,1)S(1)} %get-tuple-element.32), channel_id=1, source_target_pairs={{0,8},{1,9},{2,10},{3,11},{4,12},{5,13},{6,14},{7,15},{8,0},{9,1},... | collective-permute-start | bytes 196616 | tf_op jit(solution)/shard_map/ppermute | solution.py:420
  62.6 5.1 %collective-permute-start.2 = (bf16[32,1024]{1,0:T(8,128)(2,1)S(1)}, bf16[32,1024]{1,0:T(8,128)(2,1)S(1)}, u32[]{:S(2)}, u32[]{:S(2)}) collective-permute-start(bf16[32,1024]{1,0:T(8,128)(2,1)S(1)} %get-tuple-element.30), channel_id=1, source_target_pairs={{0,4},{1,5},{2,6},{3,7},{4,0},{5,1},{6,2},{7,3},{8,12},{9,13},{10,... | collective-permute-start | bytes 196616 | tf_op jit(solution)/shard_map/ppermute | solution.py:420
  67.8 11.8 %collective-permute-start.5 = (bf16[32,1024]{1,0:T(8,128)(2,1)S(1)}, bf16[32,1024]{1,0:T(8,128)(2,1)S(1)}, u32[]{:S(2)}, u32[]{:S(2)}) collective-permute-start(bf16[32,1024]{1,0:T(8,128)(2,1)S(1)} %multiply_convert_fusion), channel_id=1, source_target_pairs={{0,12},{1,13},{2,14},{3,15},{4,8},{5,9},{6,10},{7,11},{8,4},{9,5},... | collective-permute-start | bytes 196616 | tf_op jit(solution)/shard_map/ppermute | solution.py:420
  68.7 10.9 %collective-permute-start.6 = (bf16[32,1024]{1,0:T(8,128)(2,1)S(1)}, bf16[32,1024]{1,0:T(8,128)(2,1)S(1)}, u32[]{:S(2)}, u32[]{:S(2)}) collective-permute-start(bf16[32,1024]{1,0:T(8,128)(2,1)S(1)} %multiply_convert_fusion), channel_id=1, source_target_pairs={{0,8},{1,9},{2,10},{3,11},{4,12},{5,13},{6,14},{7,15},{8,0},{9,1},... | collective-permute-start | bytes 196616 | tf_op jit(solution)/shard_map/ppermute | solution.py:420
  72.1 7.5 %collective-permute-start.7 = (bf16[32,1024]{1,0:T(8,128)(2,1)S(1)}, bf16[32,1024]{1,0:T(8,128)(2,1)S(1)}, u32[]{:S(2)}, u32[]{:S(2)}) collective-permute-start(bf16[32,1024]{1,0:T(8,128)(2,1)S(1)} %multiply_convert_fusion), channel_id=1, source_target_pairs={{0,4},{1,5},{2,6},{3,7},{4,0},{5,1},{6,2},{7,3},{8,12},{9,13},{10,... | collective-permute-start | bytes 196616 | tf_op jit(solution)/shard_map/ppermute | solution.py:420
  72.1 38.1 %all-to-all-start.1 = ((bf16[16,40,1024]{2,1,0:T(8,128)(2,1)}), bf16[16,40,1024]{2,1,0:T(8,128)(2,1)S(1)}, u32[]{:S(2)}, u32[]{:S(2)}) async-start(bf16[16,40,1024]{2,1,0:T(8,128)(2,1)} %pack.1), calls=%async_computation.1 | async-start | bytes 2621440 | tf_op jit(solution)/shard_map/all_to_all | solution.py:479
  79.7 13.9 %collective-permute-start.8 = (bf16[128,1024]{1,0:T(8,128)(2,1)S(1)}, bf16[128,1024]{1,0:T(8,128)(2,1)S(1)}, u32[]{:S(2)}, u32[]{:S(2)}) collective-permute-start(bf16[128,1024]{1,0:T(8,128)(2,1)S(1)} %pad_maximum_fusion.2), channel_id=1, source_target_pairs={{0,2},{1,3},{2,0},{3,1},{4,6},{5,7},{6,4},{7,5},{8,10},{9,11},{10,... | collective-permute-start | bytes 786440 | tf_op jit(solution)/shard_map/ppermute | solution.py:420
  93.8 4.2 %collective-permute-start.9 = (bf16[256,1024]{1,0:T(8,128)(2,1)S(1)}, bf16[256,1024]{1,0:T(8,128)(2,1)S(1)}, u32[]{:S(2)}, u32[]{:S(2)}) collective-permute-start(bf16[256,1024]{1,0:T(8,128)(2,1)S(1)} %pad_maximum_fusion.1), channel_id=1, source_target_pairs={{0,1},{1,0},{2,3},{3,2},{4,5},{5,4},{6,7},{7,6},{8,9},{9,8},{10,11... | collective-permute-start | bytes 1572872 | tf_op jit(solution)/shard_map/ppermute | solution.py:420

commit v18 on v17

--- a/solution.py
+++ b/solution.py
@@ -42,7 +42,7 @@
     return picked.reshape(count, width)
 
 
-def fetch_kernel(order, dealing, cols, tile, out, token, held, cut, sems, out_sems):
+def fetch_kernel(order, dealing, cols, tile, out, token, held, sems):
     token[0] = dealing[0]
     slots, tile_rows = out.shape[0], out.shape[1]
     tile_cols = tile.shape[2]
@@ -58,7 +58,8 @@
 
     lane = lax.broadcasted_iota(jnp.int32, (tile_rows, LANES), 1)
 
-    def cut_slot(slot):
+    @pl.loop(0, slots, unroll=4)
+    def _(slot):
         copy(slot).wait()
         _, offset = window_start(cols[dealing[slot]], order, tile_cols)
         shift = lax.rem(LANES - lax.rem(offset, LANES), LANES)
@@ -69,22 +70,8 @@
             ]
             for b in range(order // LANES):
                 first = part * order + b * LANES
-                cut[slot, :, first : first + LANES] = jnp.where(lane < LANES - offset, turned[b], turned[b + 1])
-
-    group = slots // out_sems.shape[0]
-    sends = []
-    for g in range(out_sems.shape[0]):
-
-        @pl.loop(g * group, (g + 1) * group, unroll=4)
-        def _(slot):
-            cut_slot(slot)
-
-        here = slice(g * group, (g + 1) * group)
-        send = pltpu.make_async_copy(cut.at[here], out.at[here], out_sems.at[g])
-        send.start()
-        sends.append(send)
-    for send in sends:
-        send.wait()
+                cells = jnp.where(lane < LANES - offset, turned[b], turned[b + 1])
+                out[slot, :, first : first + LANES] = cells
 
 
 def fetch_windows(tile, dealing, cols, order):
@@ -98,12 +85,10 @@
             jax.ShapeDtypeStruct((1,), jnp.int32),
         ),
         in_specs=[SMEM, SMEM, ANY],
-        out_specs=(ANY, SMEM),
+        out_specs=(VMEM, SMEM),
         scratch_shapes=[
             pltpu.VMEM((slots, 2, tile_rows, span), jnp.float32),
-            pltpu.VMEM((slots, tile_rows, 2 * order), jnp.bfloat16),
             pltpu.SemaphoreType.DMA((slots,)),
-            pltpu.SemaphoreType.DMA((4,)),
         ],
         compiler_params=pltpu.CompilerParams(vmem_limit_bytes=56 * 2**20),
         cost_estimate=pl.CostEstimate(flops=0, bytes_accessed=6 * 2**20, transcendentals=0),
@@ -193,7 +178,7 @@
 def slot_kernel(
     dealing, rows, owners, cells, stock,
     term, kept, sent,
-    wide, patch, wave, half, resid, turned, mine, probe, table, minus, measured, sems,
+    wide, patch, wave, half, resid, turned, leaving, probe, table, minus, measured, sems, leave_sem,
 ):
     del owners
     order = term.shape[0]
@@ -263,27 +248,29 @@
         real, imag = resid[:, first_half], resid[:, second_half]
         turned[first_half, here] = dots(real, cos[:, here], imag, sin[:, here]).astype(turned.dtype)
         turned[second_half, here] = dots(real, minus[:, here], imag, cos[:, here]).astype(turned.dtype)
-    for first in range(0, order, tile):
-        here = slice(first, first + tile)
-        there = slice(order + first, order + first + tile)
-        for top in range(0, order, tile):
-            line = slice(top, top + tile)
+    count = order // 2
+    side = lax.rem(me, 2)
+    for number, target in ((1 - side, leaving), (side, kept)):
+        line = pl.ds(pl.multiple_of(number * count, count), count)
+        for first in range(0, order, tile):
+            here = slice(first, first + tile)
+            there = slice(order + first, order + first + tile)
             turned_real, turned_imag = turned[first_half, here], turned[second_half, here]
             real = dots(cos[line, :], turned_real, sin[line, :], turned_imag)
             imag = dots(minus[line, :], turned_real, cos[line, :], turned_imag)
+            patch_real = patch[line, here].astype(jnp.float32)
+            patch_imag = patch[line, there].astype(jnp.float32)
+            target[:, here] = (patch_real * real + patch_imag * imag).astype(target.dtype)
+            target[:, there] = (patch_real * imag - patch_imag * real).astype(target.dtype)
             probe_real = probe[line, here].astype(jnp.float32)
             probe_imag = probe[line, there].astype(jnp.float32)
             term[line, here] = (probe_real * real + probe_imag * imag).astype(term.dtype)
             term[line, there] = (probe_real * imag - probe_imag * real).astype(term.dtype)
-            patch_real = patch[line, here].astype(jnp.float32)
-            patch_imag = patch[line, there].astype(jnp.float32)
-            mine[line, here] = patch_real * real + patch_imag * imag
-            mine[line, there] = patch_real * imag - patch_imag * real
-
-    count = kept.shape[0]
-    side = lax.rem(me, 2)
-    kept[...] = mine[pl.ds(pl.multiple_of(side * count, count), count), :]
-    sent[...] = mine[pl.ds(pl.multiple_of((1 - side) * count, count), count), :].astype(sent.dtype)
+        if target is leaving:
+            leave = pltpu.make_async_copy(leaving, sent, leave_sem.at[0])
+            leave.start()
+    leave.wait()
+
 
 def slot_terms(cells, stock, dealing, rows, owners, order):
     total_rows = cells.shape[0]
@@ -297,7 +284,7 @@
             jax.ShapeDtypeStruct((order // 2, wide_cols), bf16),
         ),
         in_specs=[SMEM, SMEM, SMEM, VMEM, ANY],
-        out_specs=(VMEM,) * 3,
+        out_specs=(VMEM, VMEM, ANY),
         scratch_shapes=[
             pltpu.VMEM((total_rows + SUBLANES, wide_cols), f32),
             pltpu.VMEM((order, wide_cols), bf16),
@@ -305,12 +292,13 @@
             pltpu.VMEM((wide_cols, order), bf16),
             pltpu.VMEM((order, wide_cols), bf16),
             pltpu.VMEM((wide_cols, order), bf16),
-            pltpu.VMEM((order, wide_cols), f32),
+            pltpu.VMEM((order // 2, wide_cols), bf16),
             pltpu.VMEM((order, wide_cols), bf16),
             pltpu.VMEM((order, wide_cols), bf16),
             pltpu.VMEM((order, order), bf16),
             pltpu.VMEM((order, order), bf16),
             pltpu.SemaphoreType.DMA((3,)),
+            pltpu.SemaphoreType.DMA((1,)),
         ],
         compiler_params=pltpu.CompilerParams(vmem_limit_bytes=24 * 2**20),
         cost_estimate=pl.CostEstimate(

time: 115 us -> 114 us (level)
  Pallas kernels: 26.4 us -> 25.2 us
where the time goes in v18:
time: 114 us; the launch traced here: 113 us
  waiting for transfers between devices  58.9 us (52%)
  Pallas kernels  25.2 us (22%)
  starting transfers between devices  24.6 us (22%)
  other arithmetic  2.4 us (2%)
  local copies, waits for them, and re-layouts  1.26 us (1%)
    ppermute x10, waiting for transfers between devices, swap(): return lax.ppermute(x, 'row', [(d, d ^ distance) for d in range(devices)])  26 us
    all_to_all x1, waiting for transfers between devices, body(): lax.all_to_all(pieces, 'row', split_axis=0, concat_axis=0, tiled=True)  22.8 us
    ppermute x10, starting transfers between devices, swap(): return lax.ppermute(x, 'row', [(d, d ^ distance) for d in range(devices)])  10.4 us
    all_to_all x1, waiting for transfers between devices, body(): lax.all_to_all(terms, 'row', split_axis=0, concat_axis=0, tiled=True)  10.1 us
    all_to_all x1, starting transfers between devices, body(): lax.all_to_all(terms, 'row', split_axis=0, concat_axis=0, tiled=True)  7.49 us
    pallas_call x1, Pallas kernels, slot_terms(): pl.pallas_call(slot_kernel, out_shape=(jax.ShapeDtypeStruct((order, wide_...  7.4 us
    all_to_all x1, starting transfers between devices, body(): lax.all_to_all(pieces, 'row', split_axis=0, concat_axis=0, tiled=True)  6.7 us
    pallas_call x1, Pallas kernels, prepare(): pl.pallas_call(functools.partial(prepare_kernel, order), out_shape=(jax.S...  6.69 us
  transfers between devices with their start and end apart: 12, of which 8 were waited for; matrix products, arithmetic and copies ran while one was open for 2% of the time, Pallas kernels for 8%

profile of v18, /device:TPU:15, one launch (start us, length us, event | category | flops | bytes accessed | tf_op | source)
XLA Modules:
  0.0 113.2 jit_solution(17770311996482102748)
XLA Ops:
  0.6 4.7 %fetch.1 = (bf16[16,40,1024]{2,1,0:T(8,128)(2,1)}, s32[1]{0:T(128)}) custom-call(s32[16]{0:T(128)} %dealing.9, s32[16]{0:T(128)} %cols.5, f32[2,40,32768]{2,1,0:T(8,128)} %tile.1), custom_call_target="tpu_custom_call" | custom-call | bytes 6291456 | tf_op jit(solution)/shard_map/fetch/pallas_call | solution.py:81
  5.3 0.0 copy-start
  5.3 0.0 copy-start.1
  5.3 0.0 copy-start.3
  5.3 0.0 copy-start.4
  5.4 0.0 copy-start.5
  5.4 6.7 %all-to-all-start = ((bf16[16,40,1024]{2,1,0:T(8,128)(2,1)}), bf16[16,40,1024]{2,1,0:T(8,128)(2,1)S(1)}, u32[]{:S(2)}, u32[]{:S(2)}) async-start(bf16[16,40,1024]{2,1,0:T(8,128)(2,1)} %get-tuple-element.16), calls=%async_computation | async-start | bytes 2621440 | tf_op jit(solution)/shard_map/all_to_all | solution.py:458
  12.1 0.0 copy-done
  12.1 0.0 copy-done.1
  12.1 0.0 copy-done.3
  12.1 0.0 copy-done.4
  12.1 0.0 copy-start.2
  12.1 1.0 copy-done.2
  13.1 6.7 %prepare.1 = (f32[2,40,32768]{2,1,0:T(8,128)}, s32[80]{0:T(128)S(1)}, s32[80]{0:T(128)S(1)}, bf16[24576,1024]{1,0:T(8,128)(2,1)}) custom-call(s32[16]{0:T(128)S(1)} %copy-done.3, s32[16]{0:T(128)S(1)} %copy-done.4, s32[1]{0:T(128)} %get-tuple-element.13.token, bf16[512,1024]{1,0:T(8,128)(2,1)S(1)} %copy-done.1, bf16[2,512,512]{2,1,0:T(8,128)(2,1)S(1)} %copy-done, ...), custom_call_target="tpu_custom_call" | custom-call | bytes 115343360 | tf_op jit(solution)/shard_map/prepare/pallas_call | solution.py:156
  19.8 22.8 %all-to-all-done = bf16[16,40,1024]{2,1,0:T(8,128)(2,1)S(1)} async-done(((bf16[16,40,1024]{2,1,0:T(8,128)(2,1)}), bf16[16,40,1024]{2,1,0:T(8,128)(2,1)S(1)}, u32[]{:S(2)}, u32[]{:S(2)}) %all-to-all-start) | async-done | bytes 1310752 | tf_op jit(solution)/shard_map/all_to_all | solution.py:458
  42.6 0.0 copy-done.5
  42.6 7.4 %slot.1 = (bf16[512,1024]{1,0:T(8,128)(2,1)S(1)}, f32[256,1024]{1,0:T(8,128)S(1)}, bf16[256,1024]{1,0:T(8,128)(2,1)}) custom-call(s32[16]{0:T(128)S(1)} %copy-done.3, s32[16]{0:T(128)S(1)} %copy-done.5, s32[80]{0:T(128)S(1)} %get-tuple-element.15.owners, bf16[640,1024]{1,0:T(8,128)(2,1)S(1)} %bitcast.5, bf16[24576,1024]{1,0:T(8,128)(2,1)} %get-tuple-element.17.stock), custom_call_target="tpu_custom_call" | custom-call | flops 4294967296 | bytes 8388608 | tf_op jit(solution)/shard_map/slot/pallas_call | solution.py:279
  50.0 0.3 collective-permute-start
  50.3 1.9 %collective-permute-done = bf16[256,1024]{1,0:T(8,128)(2,1)S(1)} collective-permute-done((bf16[256,1024]{1,0:T(8,128)(2,1)}, bf16[256,1024]{1,0:T(8,128)(2,1)S(1)}, u32[]{:S(2)}, u32[]{:S(2)}) %collective-permute-start) | collective-permute-done | bytes 524320 | tf_op jit(solution)/shard_map/ppermute | solution.py:408
  52.2 0.1 add_convert_fusion
  52.4 0.1 collective-permute-start.1
  52.5 7.6 %collective-permute-done.1 = bf16[128,1024]{1,0:T(8,128)(2,1)S(1)} collective-permute-done((bf16[128,1024]{1,0:T(8,128)(2,1)S(1)}, bf16[128,1024]{1,0:T(8,128)(2,1)S(1)}, u32[]{:S(2)}, u32[]{:S(2)}) %collective-permute-start.1) | collective-permute-done | bytes 262176 | tf_op jit(solution)/shard_map/ppermute | solution.py:408
  60.2 0.4 collective-permute-start.4
  60.6 0.8 collective-permute-start.3
  61.4 1.5 %collective-permute-start.2 = (bf16[32,1024]{1,0:T(8,128)(2,1)S(1)}, bf16[32,1024]{1,0:T(8,128)(2,1)S(1)}, u32[]{:S(2)}, u32[]{:S(2)}) collective-permute-start(bf16[32,1024]{1,0:T(8,128)(2,1)S(1)} %get-tuple-element.30), channel_id=1, source_target_pairs={{0,4},{1,5},{2,6},{3,7},{4,0},{5,1},{6,2},{7,3},{8,12},{9,13},{10,... | collective-permute-start | bytes 196616 | tf_op jit(solution)/shard_map/ppermute | solution.py:408
  62.9 2.2 %pack.1 = bf16[16,40,1024]{2,1,0:T(8,128)(2,1)} custom-call(s32[16]{0:T(128)S(1)} %copy-done.3, s32[16]{0:T(128)S(1)} %copy-done.5, bf16[512,1024]{1,0:T(8,128)(2,1)S(1)} %get-tuple-element.18.term), custom_call_target="tpu_custom_call" | custom-call | bytes 3145728 | tf_op jit(solution)/shard_map/pack/pallas_call | solution.py:327
  65.1 0.3 collective-permute-done.4
  65.4 0.0 collective-permute-done.3
  65.4 1.1 collective-permute-done.2
  66.6 0.9 collective-permute-start.5
  67.5 3.4 %collective-permute-start.6 = (bf16[32,1024]{1,0:T(8,128)(2,1)S(1)}, bf16[32,1024]{1,0:T(8,128)(2,1)S(1)}, u32[]{:S(2)}, u32[]{:S(2)}) collective-permute-start(bf16[32,1024]{1,0:T(8,128)(2,1)S(1)} %multiply_convert_fusion), channel_id=1, source_target_pairs={{0,8},{1,9},{2,10},{3,11},{4,12},{5,13},{6,14},{7,15},{8,0},{9,1},... | collective-permute-start | bytes 196616 | tf_op jit(solution)/shard_map/ppermute | solution.py:408
  70.9 0.0 collective-permute-start.7
  70.9 7.5 %all-to-all-start.1 = ((bf16[16,40,1024]{2,1,0:T(8,128)(2,1)}), bf16[16,40,1024]{2,1,0:T(8,128)(2,1)S(1)}, u32[]{:S(2)}, u32[]{:S(2)}) async-start(bf16[16,40,1024]{2,1,0:T(8,128)(2,1)} %pack.1), calls=%async_computation.1 | async-start | bytes 2621440 | tf_op jit(solution)/shard_map/all_to_all | solution.py:467
  78.4 0.0 collective-permute-done.5
  78.4 0.0 collective-permute-done.6
  78.4 0.0 collective-permute-done.7
  78.5 0.3 collective-permute-start.8
  78.9 13.5 %collective-permute-done.8 = bf16[128,1024]{1,0:T(8,128)(2,1)S(1)} collective-permute-done((bf16[128,1024]{1,0:T(8,128)(2,1)S(1)}, bf16[128,1024]{1,0:T(8,128)(2,1)S(1)}, u32[]{:S(2)}, u32[]{:S(2)}) %collective-permute-start.8) | collective-permute-done | bytes 262176 | tf_op jit(solution)/shard_map/ppermute | solution.py:408
  92.4 0.1 broadcast_select_fusion.3
  92.5 2.6 %collective-permute-start.9 = (bf16[256,1024]{1,0:T(8,128)(2,1)S(1)}, bf16[256,1024]{1,0:T(8,128)(2,1)S(1)}, u32[]{:S(2)}, u32[]{:S(2)}) collective-permute-start(bf16[256,1024]{1,0:T(8,128)(2,1)S(1)} %pad_maximum_fusion.1), channel_id=1, source_target_pairs={{0,1},{1,0},{2,3},{3,2},{4,5},{5,4},{6,7},{7,6},{8,9},{9,8},{10,11... | collective-permute-start | bytes 1572872 | tf_op jit(solution)/shard_map/ppermute | solution.py:408
  95.2 1.5 %collective-permute-done.9 = bf16[256,1024]{1,0:T(8,128)(2,1)S(1)} collective-permute-done((bf16[256,1024]{1,0:T(8,128)(2,1)S(1)}, bf16[256,1024]{1,0:T(8,128)(2,1)S(1)}, u32[]{:S(2)}, u32[]{:S(2)}) %collective-permute-start.9) | collective-permute-done | bytes 524320 | tf_op jit(solution)/shard_map/ppermute | solution.py:408
  96.7 0.2 broadcast_select_fusion.1
  96.9 0.2 maximum_convert_fusion
  97.2 0.2 slice_bitcast_fusion.1
  97.4 1.5 %pad_maximum_fusion = f32[2,512,512]{2,1,0:T(8,128)} fusion(f32[1,512,512]{2,1,0:T(8,128)S(1)} %get-tuple-element.25, f32[1,512,512]{2,1,0:T(8,128)S(1)} %get-tuple-element.24), kind=kLoop, calls=%fused_computation | loop fusion | flops 524288 | bytes 4194304 | tf_op jit(solution)/shard_map/stack | solution.py:470
  98.9 10.1 %all-to-all-done.1.terms = bf16[16,40,1024]{2,1,0:T(8,128)(2,1)S(1)} async-done(((bf16[16,40,1024]{2,1,0:T(8,128)(2,1)}), bf16[16,40,1024]{2,1,0:T(8,128)(2,1)S(1)}, u32[]{:S(2)}, u32[]{:S(2)}) %all-to-all-start.1) | async-done | bytes 1310752 | tf_op jit(solution)/shard_map/all_to_all | solution.py:467
  109.0 4.2 %place.1 = f32[2,40,32768]{2,1,0:T(8,128)} custom-call(s32[16]{0:T(128)S(1)} %copy-done.3, s32[16]{0:T(128)S(1)} %copy-done.4, s32[80]{0:T(128)S(1)} %get-tuple-element.14.blocks, s32[80]{0:T(128)S(1)} %get-tuple-element.15.owners, bf16[16,40,1024]{2,1,0:T(8,128)(2,1)S(1)} %all-to-all-done.1.terms, ...), custom_call_target="tpu_custom_call", output_to_operand_aliasing={{}: (5, {})} | custom-call | bytes 6291456 | tf_op jit(solution)/shard_map/place/pallas_call | solution.py:382
  (6 shorter events, 0.2 us)
Async XLA Ops:
  5.3 6.8 %copy-start = (bf16[2,512,512]{2,1,0:T(8,128)(2,1)S(1)}, bf16[2,512,512]{2,1,0:T(8,128)(2,1)}, u32[]{:S(2)}) copy-start(bf16[2,512,512]{2,1,0:T(8,128)(2,1)} %probe.1) | copy-start | bytes 3145732
  5.3 6.8 %copy-start.1 = (bf16[512,1024]{1,0:T(8,128)(2,1)S(1)}, bf16[512,1024]{1,0:T(8,128)(2,1)}, u32[]{:S(2)}) copy-start(bf16[512,1024]{1,0:T(8,128)(2,1)} %constant.79.clone.table_in) | copy-start | bytes 3145732
  5.3 6.8 %copy-start.3 = (s32[16]{0:T(128)S(1)}, s32[16]{0:T(128)}, u32[]{:S(2)}) copy-start(s32[16]{0:T(128)} %dealing.9) | copy-start | bytes 196
  5.3 6.8 %copy-start.4 = (s32[16]{0:T(128)S(1)}, s32[16]{0:T(128)}, u32[]{:S(2)}) copy-start(s32[16]{0:T(128)} %cols.5) | copy-start | bytes 196
  5.4 37.3 %copy-start.5 = (s32[16]{0:T(128)S(1)}, s32[16]{0:T(128)}, u32[]{:S(2)}) copy-start(s32[16]{0:T(128)} %rows.3) | copy-start | bytes 196
  5.4 37.3 %all-to-all-start = ((bf16[16,40,1024]{2,1,0:T(8,128)(2,1)}), bf16[16,40,1024]{2,1,0:T(8,128)(2,1)S(1)}, u32[]{:S(2)}, u32[]{:S(2)}) async-start(bf16[16,40,1024]{2,1,0:T(8,128)(2,1)} %get-tuple-element.16), calls=%async_computation | async-start | bytes 2621440 | tf_op jit(solution)/shard_map/all_to_all | solution.py:458
  12.1 1.0 copy-start.2
  50.0 2.2 %collective-permute-start = (bf16[256,1024]{1,0:T(8,128)(2,1)}, bf16[256,1024]{1,0:T(8,128)(2,1)S(1)}, u32[]{:S(2)}, u32[]{:S(2)}) collective-permute-start(bf16[256,1024]{1,0:T(8,128)(2,1)} %get-tuple-element.20), channel_id=1, source_target_pairs={{0,1},{1,0},{2,3},{3,2},{4,5},{5,4},{6,7},{7,6},{8,9},{9,8},{10,11... | collective-permute-start | bytes 1572872 | tf_op jit(solution)/shard_map/ppermute | solution.py:408
  52.4 7.8 %collective-permute-start.1 = (bf16[128,1024]{1,0:T(8,128)(2,1)S(1)}, bf16[128,1024]{1,0:T(8,128)(2,1)S(1)}, u32[]{:S(2)}, u32[]{:S(2)}) collective-permute-start(bf16[128,1024]{1,0:T(8,128)(2,1)S(1)} %get-tuple-element.26), channel_id=1, source_target_pairs={{0,2},{1,3},{2,0},{3,1},{4,6},{5,7},{6,4},{7,5},{8,10},{9,11},{10,... | collective-permute-start | bytes 786440 | tf_op jit(solution)/shard_map/ppermute | solution.py:408
  60.2 5.2 %collective-permute-start.4 = (bf16[32,1024]{1,0:T(8,128)(2,1)S(1)}, bf16[32,1024]{1,0:T(8,128)(2,1)S(1)}, u32[]{:S(2)}, u32[]{:S(2)}) collective-permute-start(bf16[32,1024]{1,0:T(8,128)(2,1)S(1)} %get-tuple-element.31), channel_id=1, source_target_pairs={{0,12},{1,13},{2,14},{3,15},{4,8},{5,9},{6,10},{7,11},{8,4},{9,5},... | collective-permute-start | bytes 196616 | tf_op jit(solution)/shard_map/ppermute | solution.py:408
  60.6 4.8 %collective-permute-start.3 = (bf16[32,1024]{1,0:T(8,128)(2,1)S(1)}, bf16[32,1024]{1,0:T(8,128)(2,1)S(1)}, u32[]{:S(2)}, u32[]{:S(2)}) collective-permute-start(bf16[32,1024]{1,0:T(8,128)(2,1)S(1)} %get-tuple-element.32), channel_id=1, source_target_pairs={{0,8},{1,9},{2,10},{3,11},{4,12},{5,13},{6,14},{7,15},{8,0},{9,1},... | collective-permute-start | bytes 196616 | tf_op jit(solution)/shard_map/ppermute | solution.py:408
  61.4 5.1 %collective-permute-start.2 = (bf16[32,1024]{1,0:T(8,128)(2,1)S(1)}, bf16[32,1024]{1,0:T(8,128)(2,1)S(1)}, u32[]{:S(2)}, u32[]{:S(2)}) collective-permute-start(bf16[32,1024]{1,0:T(8,128)(2,1)S(1)} %get-tuple-element.30), channel_id=1, source_target_pairs={{0,4},{1,5},{2,6},{3,7},{4,0},{5,1},{6,2},{7,3},{8,12},{9,13},{10,... | collective-permute-start | bytes 196616 | tf_op jit(solution)/shard_map/ppermute | solution.py:408
  66.6 11.9 %collective-permute-start.5 = (bf16[32,1024]{1,0:T(8,128)(2,1)S(1)}, bf16[32,1024]{1,0:T(8,128)(2,1)S(1)}, u32[]{:S(2)}, u32[]{:S(2)}) collective-permute-start(bf16[32,1024]{1,0:T(8,128)(2,1)S(1)} %multiply_convert_fusion), channel_id=1, source_target_pairs={{0,12},{1,13},{2,14},{3,15},{4,8},{5,9},{6,10},{7,11},{8,4},{9,5},... | collective-permute-start | bytes 196616 | tf_op jit(solution)/shard_map/ppermute | solution.py:408
  67.5 10.9 %collective-permute-start.6 = (bf16[32,1024]{1,0:T(8,128)(2,1)S(1)}, bf16[32,1024]{1,0:T(8,128)(2,1)S(1)}, u32[]{:S(2)}, u32[]{:S(2)}) collective-permute-start(bf16[32,1024]{1,0:T(8,128)(2,1)S(1)} %multiply_convert_fusion), channel_id=1, source_target_pairs={{0,8},{1,9},{2,10},{3,11},{4,12},{5,13},{6,14},{7,15},{8,0},{9,1},... | collective-permute-start | bytes 196616 | tf_op jit(solution)/shard_map/ppermute | solution.py:408
  70.9 7.5 %collective-permute-start.7 = (bf16[32,1024]{1,0:T(8,128)(2,1)S(1)}, bf16[32,1024]{1,0:T(8,128)(2,1)S(1)}, u32[]{:S(2)}, u32[]{:S(2)}) collective-permute-start(bf16[32,1024]{1,0:T(8,128)(2,1)S(1)} %multiply_convert_fusion), channel_id=1, source_target_pairs={{0,4},{1,5},{2,6},{3,7},{4,0},{5,1},{6,2},{7,3},{8,12},{9,13},{10,... | collective-permute-start | bytes 196616 | tf_op jit(solution)/shard_map/ppermute | solution.py:408
  70.9 38.1 %all-to-all-start.1 = ((bf16[16,40,1024]{2,1,0:T(8,128)(2,1)}), bf16[16,40,1024]{2,1,0:T(8,128)(2,1)S(1)}, u32[]{:S(2)}, u32[]{:S(2)}) async-start(bf16[16,40,1024]{2,1,0:T(8,128)(2,1)} %pack.1), calls=%async_computation.1 | async-start | bytes 2621440 | tf_op jit(solution)/shard_map/all_to_all | solution.py:467
  78.5 13.9 %collective-permute-start.8 = (bf16[128,1024]{1,0:T(8,128)(2,1)S(1)}, bf16[128,1024]{1,0:T(8,128)(2,1)S(1)}, u32[]{:S(2)}, u32[]{:S(2)}) collective-permute-start(bf16[128,1024]{1,0:T(8,128)(2,1)S(1)} %pad_maximum_fusion.2), channel_id=1, source_target_pairs={{0,2},{1,3},{2,0},{3,1},{4,6},{5,7},{6,4},{7,5},{8,10},{9,11},{10,... | collective-permute-start | bytes 786440 | tf_op jit(solution)/shard_map/ppermute | solution.py:408
  92.5 4.2 %collective-permute-start.9 = (bf16[256,1024]{1,0:T(8,128)(2,1)S(1)}, bf16[256,1024]{1,0:T(8,128)(2,1)S(1)}, u32[]{:S(2)}, u32[]{:S(2)}) collective-permute-start(bf16[256,1024]{1,0:T(8,128)(2,1)S(1)} %pad_maximum_fusion.1), channel_id=1, source_target_pairs={{0,1},{1,0},{2,3},{3,2},{4,5},{5,4},{6,7},{7,6},{8,9},{9,8},{10,11... | collective-permute-start | bytes 1572872 | tf_op jit(solution)/shard_map/ppermute | solution.py:408

commit v19 on v18

--- a/solution.py
+++ b/solution.py
@@ -340,7 +340,6 @@
     del empty
     slots, tile_rows = terms.shape[0], terms.shape[1]
     count = (order + LANES) // LANES
-    totals[...] = jnp.zeros_like(totals)
     lane = lax.broadcasted_iota(jnp.int32, (tile_rows, LANES), 1)
     nothing = jnp.zeros((tile_rows, LANES), jnp.float32)
 
@@ -353,11 +352,14 @@
             for b in range(count - 1):
                 first = part * order + b * LANES
                 turned.append(pltpu.roll(terms[slot, :, first : first + LANES], shift, 1).astype(jnp.float32))
+            holders = [owners[slot * count + b] for b in range(count)]
+            held = [totals[holder, part] for holder in holders]
             for b in range(count):
                 before = turned[b - 1] if b else nothing
                 after = turned[b] if b < count - 1 else nothing
-                owner = owners[slot * count + b]
-                totals[owner, part] += jnp.where(lane < offset, before, after)
+                term = jnp.where(lane < offset, before, after)
+                first_one = holders[b] == slot * count + b
+                totals[holders[b], part] = jnp.where(first_one, term, held[b] + term)
 
     def copy(number):
         place = pl.multiple_of(blocks[number] * LANES, LANES)
@@ -410,29 +412,46 @@
 
 def sum_probe(kept, sent, devices):
     me = lax.axis_index("row")
-    addends = [kept, swap(sent, 1, devices)]
-
-    def rows(index, count):
-        found = [lax.dynamic_slice_in_dim(x, index * count, count).astype(jnp.float32) for x in addends]
+
+    def rows(addends, first, count):
+        found = [lax.dynamic_slice_in_dim(x, first, count).astype(jnp.float32) for x in addends]
         return found[0] + found[1]
 
-    for stride, radix in strides(devices)[1:]:
-        digit = me // stride % radix
-        count = addends[0].shape[0] // radix
-        met = []
-        for k in range(1, radix):
-            share = rows(lax.bitwise_xor(digit, k), count).astype(jnp.bfloat16)
-            met.append(swap(share, k * stride, devices))
-        own = rows(digit, count)
-        for one in met[:-1]:
-            own = own + one.astype(jnp.float32)
-        addends = [own, met[-1]]
-    return addends[0] + addends[1].astype(jnp.float32)
+    halves = [kept, swap(sent, 1, devices)]
+    (stride, radix), *later = strides(devices)[1:]
+    digit = me // stride % radix
+    count = kept.shape[0] // (2 * radix)
+    other = lax.rem(digit + 1, 2)
+    met = [
+        swap(rows(halves, (other * 2 + number) * count, count).astype(jnp.bfloat16), stride, devices)
+        for number in range(2)
+    ]
+    totals = []
+    for number in range(2):
+        addends = [rows(halves, (digit * 2 + number) * count, count), met[number]]
+        for stride, radix in later:
+            digit_here = me // stride % radix
+            share_rows = addends[0].shape[0] // radix
+            arrived = []
+            for k in range(1, radix):
+                share = rows(addends, lax.bitwise_xor(digit_here, k) * share_rows, share_rows)
+                arrived.append(swap(share.astype(jnp.bfloat16), k * stride, devices))
+            own = rows(addends, digit_here * share_rows, share_rows)
+            for one in arrived[:-1]:
+                own = own + one.astype(jnp.float32)
+            addends = [own, arrived[-1]]
+        totals.append(addends[0] + addends[1].astype(jnp.float32))
+    return jnp.concatenate(totals)
 
 
 def join(whole, devices):
     me = lax.axis_index("row")
-    for stride, radix in reversed(strides(devices)):
+    rows, width = whole.shape
+    steps = strides(devices)
+    for stride, radix in reversed(steps):
+        if stride == steps[1][0]:
+            sets = whole.reshape(-1, 2, rows // 2, width)
+            whole = jnp.concatenate([sets[:, 0].reshape(-1, width), sets[:, 1].reshape(-1, width)])
         digit = me // stride % radix
         shares = [whole] + [swap(whole, k * stride, devices) for k in range(1, radix)]
         pieces = []

time: 114 us -> 114 us (level)
  starting transfers between devices: 24.6 us -> 31 us
  waiting for transfers between devices: 58.9 us -> 53 us
    ppermute x10 -> x14, waiting for transfers between devices: 26 us -> 20.1 us  [swap(): return lax.ppermute(x, 'row', [(d, d ^ distance) for d in range(devices)])]
    ppermute x10 -> x14, starting transfers between devices: 10.4 us -> 15 us  [swap(): return lax.ppermute(x, 'row', [(d, d ^ distance) for d in range(devices)])]
    all_to_all x1, starting transfers between devices: 7.49 us -> 9.31 us  [body(): lax.all_to_all(terms, 'row', split_axis=0, concat_axis=0, tiled=True)]
  transfers between devices with their start and end apart: 12 -> 16, of which waited for: 8 -> 9; matrix products, arithmetic and copies ran while one was open for 2% -> 2% of each run, Pallas kernels for 8% -> 8%
where the time goes in v19:
time: 114 us; the launch traced here: 113 us
  waiting for transfers between devices  53 us (46%)
  starting transfers between devices  31 us (27%)
  Pallas kernels  24.8 us (22%)
  other arithmetic  2.45 us (2%)
  local copies, waits for them, and re-layouts  1.29 us (1%)
    all_to_all x1, waiting for transfers between devices, body(): lax.all_to_all(pieces, 'row', split_axis=0, concat_axis=0, tiled=True)  22.7 us
    ppermute x14, waiting for transfers between devices, swap(): return lax.ppermute(x, 'row', [(d, d ^ distance) for d in range(devices)])  20.1 us
    ppermute x14, starting transfers between devices, swap(): return lax.ppermute(x, 'row', [(d, d ^ distance) for d in range(devices)])  15 us
    all_to_all x1, waiting for transfers between devices, body(): lax.all_to_all(terms, 'row', split_axis=0, concat_axis=0, tiled=True)  10.1 us
    all_to_all x1, starting transfers between devices, body(): lax.all_to_all(terms, 'row', split_axis=0, concat_axis=0, tiled=True)  9.31 us
    pallas_call x1, Pallas kernels, slot_terms(): pl.pallas_call(slot_kernel, out_shape=(jax.ShapeDtypeStruct((order, wide_...  7.41 us
    pallas_call x1, Pallas kernels, prepare(): pl.pallas_call(functools.partial(prepare_kernel, order), out_shape=(jax.S...  6.75 us
    all_to_all x1, starting transfers between devices, body(): lax.all_to_all(pieces, 'row', split_axis=0, concat_axis=0, tiled=True)  6.7 us
  transfers between devices with their start and end apart: 16, of which 9 were waited for; matrix products, arithmetic and copies ran while one was open for 2% of the time, Pallas kernels for 8%

profile of v19, /device:TPU:15, one launch (start us, length us, event | category | flops | bytes accessed | tf_op | source)
XLA Modules:
  0.0 113.4 jit_solution(13271246656499504301)
XLA Ops:
  0.6 4.7 %fetch.1 = (bf16[16,40,1024]{2,1,0:T(8,128)(2,1)}, s32[1]{0:T(128)}) custom-call(s32[16]{0:T(128)} %dealing.9, s32[16]{0:T(128)} %cols.5, f32[2,40,32768]{2,1,0:T(8,128)} %tile.1), custom_call_target="tpu_custom_call" | custom-call | bytes 6291456 | tf_op jit(solution)/shard_map/fetch/pallas_call | solution.py:81
  5.3 0.0 copy-start
  5.3 0.0 copy-start.1
  5.3 0.0 copy-start.3
  5.3 0.0 copy-start.4
  5.4 0.0 copy-start.5
  5.4 6.7 %all-to-all-start = ((bf16[16,40,1024]{2,1,0:T(8,128)(2,1)}), bf16[16,40,1024]{2,1,0:T(8,128)(2,1)S(1)}, u32[]{:S(2)}, u32[]{:S(2)}) async-start(bf16[16,40,1024]{2,1,0:T(8,128)(2,1)} %get-tuple-element.16), calls=%async_computation | async-start | bytes 2621440 | tf_op jit(solution)/shard_map/all_to_all | solution.py:477
  12.1 0.0 copy-done
  12.1 0.0 copy-done.1
  12.1 0.0 copy-done.3
  12.1 0.0 copy-done.4
  12.1 0.0 copy-start.2
  12.1 1.0 copy-done.2
  13.1 6.7 %prepare.1 = (f32[2,40,32768]{2,1,0:T(8,128)}, s32[80]{0:T(128)S(1)}, s32[80]{0:T(128)S(1)}, bf16[24576,1024]{1,0:T(8,128)(2,1)}) custom-call(s32[16]{0:T(128)S(1)} %copy-done.3, s32[16]{0:T(128)S(1)} %copy-done.4, s32[1]{0:T(128)} %get-tuple-element.13.token, bf16[512,1024]{1,0:T(8,128)(2,1)S(1)} %copy-done.1, bf16[2,512,512]{2,1,0:T(8,128)(2,1)S(1)} %copy-done, ...), custom_call_target="tpu_custom_call" | custom-call | bytes 115343360 | tf_op jit(solution)/shard_map/prepare/pallas_call | solution.py:156
  19.9 22.7 %all-to-all-done = bf16[16,40,1024]{2,1,0:T(8,128)(2,1)S(1)} async-done(((bf16[16,40,1024]{2,1,0:T(8,128)(2,1)}), bf16[16,40,1024]{2,1,0:T(8,128)(2,1)S(1)}, u32[]{:S(2)}, u32[]{:S(2)}) %all-to-all-start) | async-done | bytes 1310752 | tf_op jit(solution)/shard_map/all_to_all | solution.py:477
  42.6 0.0 copy-done.5
  42.6 7.4 %slot.1 = (bf16[512,1024]{1,0:T(8,128)(2,1)S(1)}, f32[256,1024]{1,0:T(8,128)S(1)}, bf16[256,1024]{1,0:T(8,128)(2,1)}) custom-call(s32[16]{0:T(128)S(1)} %copy-done.3, s32[16]{0:T(128)S(1)} %copy-done.5, s32[80]{0:T(128)S(1)} %get-tuple-element.15.owners, bf16[640,1024]{1,0:T(8,128)(2,1)S(1)} %bitcast.8, bf16[24576,1024]{1,0:T(8,128)(2,1)} %get-tuple-element.17.stock), custom_call_target="tpu_custom_call" | custom-call | flops 4294967296 | bytes 8388608 | tf_op jit(solution)/shard_map/slot/pallas_call | solution.py:279
  50.0 0.3 collective-permute-start
  50.3 1.9 %collective-permute-done = bf16[256,1024]{1,0:T(8,128)(2,1)S(1)} collective-permute-done((bf16[256,1024]{1,0:T(8,128)(2,1)}, bf16[256,1024]{1,0:T(8,128)(2,1)S(1)}, u32[]{:S(2)}, u32[]{:S(2)}) %collective-permute-start) | collective-permute-done | bytes 524320 | tf_op jit(solution)/shard_map/ppermute | solution.py:410
  52.2 0.1 add_convert_fusion.1
  52.4 0.1 collective-permute-start.5
  52.5 1.5 %collective-permute-start.1 = (bf16[64,1024]{1,0:T(8,128)(2,1)S(1)}, bf16[64,1024]{1,0:T(8,128)(2,1)S(1)}, u32[]{:S(2)}, u32[]{:S(2)}) collective-permute-start(bf16[64,1024]{1,0:T(8,128)(2,1)S(1)} %get-tuple-element.26), channel_id=1, source_target_pairs={{0,2},{1,3},{2,0},{3,1},{4,6},{5,7},{6,4},{7,5},{8,10},{9,11},{10,... | collective-permute-start | bytes 393224 | tf_op jit(solution)/shard_map/ppermute | solution.py:410
  53.9 2.2 %pack.1 = bf16[16,40,1024]{2,1,0:T(8,128)(2,1)} custom-call(s32[16]{0:T(128)S(1)} %copy-done.3, s32[16]{0:T(128)S(1)} %copy-done.5, bf16[512,1024]{1,0:T(8,128)(2,1)S(1)} %get-tuple-element.18.term), custom_call_target="tpu_custom_call" | custom-call | bytes 3145728 | tf_op jit(solution)/shard_map/pack/pallas_call | solution.py:327
  56.1 1.2 %collective-permute-done.5 = bf16[64,1024]{1,0:T(8,128)(2,1)S(1)} collective-permute-done((bf16[64,1024]{1,0:T(8,128)(2,1)S(1)}, bf16[64,1024]{1,0:T(8,128)(2,1)S(1)}, u32[]{:S(2)}, u32[]{:S(2)}) %collective-permute-start.5) | collective-permute-done | bytes 131104 | tf_op jit(solution)/shard_map/ppermute | solution.py:410
  57.3 0.4 collective-permute-start.8
  57.8 0.8 collective-permute-start.7
  58.6 1.5 %collective-permute-start.6 = (bf16[16,1024]{1,0:T(8,128)(2,1)S(1)}, bf16[16,1024]{1,0:T(8,128)(2,1)S(1)}, u32[]{:S(2)}, u32[]{:S(2)}) collective-permute-start(bf16[16,1024]{1,0:T(8,128)(2,1)S(1)} %get-tuple-element.37), channel_id=1, source_target_pairs={{0,4},{1,5},{2,6},{3,7},{4,0},{5,1},{6,2},{7,3},{8,12},{9,13},{10,... | collective-permute-start | bytes 98312 | tf_op jit(solution)/shard_map/ppermute | solution.py:410
  60.1 0.1 collective-permute-done.1
  60.2 0.8 collective-permute-start.4
  60.9 1.3 %collective-permute-start.3 = (bf16[16,1024]{1,0:T(8,128)(2,1)S(1)}, bf16[16,1024]{1,0:T(8,128)(2,1)S(1)}, u32[]{:S(2)}, u32[]{:S(2)}) collective-permute-start(bf16[16,1024]{1,0:T(8,128)(2,1)S(1)} %get-tuple-element.36), channel_id=1, source_target_pairs={{0,8},{1,9},{2,10},{3,11},{4,12},{5,13},{6,14},{7,15},{8,0},{9,1},... | collective-permute-start | bytes 98312 | tf_op jit(solution)/shard_map/ppermute | solution.py:410
  62.2 0.0 collective-permute-done.8
  62.2 1.1 collective-permute-start.2
  63.3 0.0 collective-permute-done.7
  63.3 0.0 collective-permute-done.6
  63.4 0.0 collective-permute-done.4
  63.4 1.4 %collective-permute-done.3 = bf16[16,1024]{1,0:T(8,128)(2,1)S(1)} collective-permute-done((bf16[16,1024]{1,0:T(8,128)(2,1)S(1)}, bf16[16,1024]{1,0:T(8,128)(2,1)S(1)}, u32[]{:S(2)}, u32[]{:S(2)}) %collective-permute-start.3) | collective-permute-done | bytes 32800 | tf_op jit(solution)/shard_map/ppermute | solution.py:410
  64.7 0.6 collective-permute-done.2
  65.4 2.0 %collective-permute-start.9 = (bf16[32,1024]{1,0:T(8,128)(2,1)S(1)}, bf16[32,1024]{1,0:T(8,128)(2,1)S(1)}, u32[]{:S(2)}, u32[]{:S(2)}) collective-permute-start(bf16[32,1024]{1,0:T(8,128)(2,1)S(1)} %multiply_convert_fusion), channel_id=1, source_target_pairs={{0,12},{1,13},{2,14},{3,15},{4,8},{5,9},{6,10},{7,11},{8,4},{9,5},... | collective-permute-start | bytes 196616 | tf_op jit(solution)/shard_map/ppermute | solution.py:410
  67.4 2.3 %collective-permute-start.10 = (bf16[32,1024]{1,0:T(8,128)(2,1)S(1)}, bf16[32,1024]{1,0:T(8,128)(2,1)S(1)}, u32[]{:S(2)}, u32[]{:S(2)}) collective-permute-start(bf16[32,1024]{1,0:T(8,128)(2,1)S(1)} %multiply_convert_fusion), channel_id=1, source_target_pairs={{0,8},{1,9},{2,10},{3,11},{4,12},{5,13},{6,14},{7,15},{8,0},{9,1},... | collective-permute-start | bytes 196616 | tf_op jit(solution)/shard_map/ppermute | solution.py:410
  69.7 0.0 collective-permute-start.11
  69.7 9.3 %all-to-all-start.1 = ((bf16[16,40,1024]{2,1,0:T(8,128)(2,1)}), bf16[16,40,1024]{2,1,0:T(8,128)(2,1)S(1)}, u32[]{:S(2)}, u32[]{:S(2)}) async-start(bf16[16,40,1024]{2,1,0:T(8,128)(2,1)} %pack.1), calls=%async_computation.1 | async-start | bytes 2621440 | tf_op jit(solution)/shard_map/all_to_all | solution.py:486
  79.0 0.0 collective-permute-done.9
  79.0 0.0 collective-permute-done.10
  79.0 0.0 collective-permute-done.11
  79.2 0.3 collective-permute-start.12
  79.5 13.5 %collective-permute-done.12 = bf16[128,1024]{1,0:T(8,128)(2,1)S(1)} collective-permute-done((bf16[128,1024]{1,0:T(8,128)(2,1)S(1)}, bf16[128,1024]{1,0:T(8,128)(2,1)S(1)}, u32[]{:S(2)}, u32[]{:S(2)}) %collective-permute-start.12) | collective-permute-done | bytes 262176 | tf_op jit(solution)/shard_map/ppermute | solution.py:410
  93.0 0.1 broadcast_select_fusion.3
  93.2 2.6 %collective-permute-start.13 = (bf16[256,1024]{1,0:T(8,128)(2,1)S(1)}, bf16[256,1024]{1,0:T(8,128)(2,1)S(1)}, u32[]{:S(2)}, u32[]{:S(2)}) collective-permute-start(bf16[256,1024]{1,0:T(8,128)(2,1)S(1)} %pad_maximum_fusion.1), channel_id=1, source_target_pairs={{0,1},{1,0},{2,3},{3,2},{4,5},{5,4},{6,7},{7,6},{8,9},{9,8},{10,11... | collective-permute-start | bytes 1572872 | tf_op jit(solution)/shard_map/ppermute | solution.py:410
  95.8 1.5 %collective-permute-done.13 = bf16[256,1024]{1,0:T(8,128)(2,1)S(1)} collective-permute-done((bf16[256,1024]{1,0:T(8,128)(2,1)S(1)}, bf16[256,1024]{1,0:T(8,128)(2,1)S(1)}, u32[]{:S(2)}, u32[]{:S(2)}) %collective-permute-start.13) | collective-permute-done | bytes 524320 | tf_op jit(solution)/shard_map/ppermute | solution.py:410
  97.3 0.2 broadcast_select_fusion.1
  97.6 0.2 maximum_convert_fusion
  97.8 0.2 slice_bitcast_fusion.1
  98.0 1.5 %pad_maximum_fusion = f32[2,512,512]{2,1,0:T(8,128)} fusion(f32[1,512,512]{2,1,0:T(8,128)S(1)} %get-tuple-element.25, f32[1,512,512]{2,1,0:T(8,128)S(1)} %get-tuple-element.24), kind=kLoop, calls=%fused_computation | loop fusion | flops 524288 | bytes 4194304 | tf_op jit(solution)/shard_map/stack | solution.py:489
  99.5 10.1 %all-to-all-done.1.terms = bf16[16,40,1024]{2,1,0:T(8,128)(2,1)S(1)} async-done(((bf16[16,40,1024]{2,1,0:T(8,128)(2,1)}), bf16[16,40,1024]{2,1,0:T(8,128)(2,1)S(1)}, u32[]{:S(2)}, u32[]{:S(2)}) %all-to-all-start.1) | async-done | bytes 1310752 | tf_op jit(solution)/shard_map/all_to_all | solution.py:486
  109.6 3.8 %place.1 = f32[2,40,32768]{2,1,0:T(8,128)} custom-call(s32[16]{0:T(128)S(1)} %copy-done.3, s32[16]{0:T(128)S(1)} %copy-done.4, s32[80]{0:T(128)S(1)} %get-tuple-element.14.blocks, s32[80]{0:T(128)S(1)} %get-tuple-element.15.owners, bf16[16,40,1024]{2,1,0:T(8,128)(2,1)S(1)} %all-to-all-done.1.terms, ...), custom_call_target="tpu_custom_call", output_to_operand_aliasing={{}: (5, {})} | custom-call | bytes 6291456 | tf_op jit(solution)/shard_map/place/pallas_call | solution.py:384
  (11 shorter events, 0.3 us)
Async XLA Ops:
  5.3 6.8 %copy-start = (bf16[2,512,512]{2,1,0:T(8,128)(2,1)S(1)}, bf16[2,512,512]{2,1,0:T(8,128)(2,1)}, u32[]{:S(2)}) copy-start(bf16[2,512,512]{2,1,0:T(8,128)(2,1)} %probe.1) | copy-start | bytes 3145732
  5.3 6.8 %copy-start.1 = (bf16[512,1024]{1,0:T(8,128)(2,1)S(1)}, bf16[512,1024]{1,0:T(8,128)(2,1)}, u32[]{:S(2)}) copy-start(bf16[512,1024]{1,0:T(8,128)(2,1)} %constant.88.clone.table_in) | copy-start | bytes 3145732
  5.3 6.8 %copy-start.3 = (s32[16]{0:T(128)S(1)}, s32[16]{0:T(128)}, u32[]{:S(2)}) copy-start(s32[16]{0:T(128)} %dealing.9) | copy-start | bytes 196
  5.3 6.8 %copy-start.4 = (s32[16]{0:T(128)S(1)}, s32[16]{0:T(128)}, u32[]{:S(2)}) copy-start(s32[16]{0:T(128)} %cols.5) | copy-start | bytes 196
  5.4 37.3 %copy-start.5 = (s32[16]{0:T(128)S(1)}, s32[16]{0:T(128)}, u32[]{:S(2)}) copy-start(s32[16]{0:T(128)} %rows.3) | copy-start | bytes 196
  5.4 37.3 %all-to-all-start = ((bf16[16,40,1024]{2,1,0:T(8,128)(2,1)}), bf16[16,40,1024]{2,1,0:T(8,128)(2,1)S(1)}, u32[]{:S(2)}, u32[]{:S(2)}) async-start(bf16[16,40,1024]{2,1,0:T(8,128)(2,1)} %get-tuple-element.16), calls=%async_computation | async-start | bytes 2621440 | tf_op jit(solution)/shard_map/all_to_all | solution.py:477
  12.1 1.0 copy-start.2
  50.0 2.2 %collective-permute-start = (bf16[256,1024]{1,0:T(8,128)(2,1)}, bf16[256,1024]{1,0:T(8,128)(2,1)S(1)}, u32[]{:S(2)}, u32[]{:S(2)}) collective-permute-start(bf16[256,1024]{1,0:T(8,128)(2,1)} %get-tuple-element.20), channel_id=1, source_target_pairs={{0,1},{1,0},{2,3},{3,2},{4,5},{5,4},{6,7},{7,6},{8,9},{9,8},{10,11... | collective-permute-start | bytes 1572872 | tf_op jit(solution)/shard_map/ppermute | solution.py:410
  52.4 4.9 %collective-permute-start.5 = (bf16[64,1024]{1,0:T(8,128)(2,1)S(1)}, bf16[64,1024]{1,0:T(8,128)(2,1)S(1)}, u32[]{:S(2)}, u32[]{:S(2)}) collective-permute-start(bf16[64,1024]{1,0:T(8,128)(2,1)S(1)} %get-tuple-element.27), channel_id=1, source_target_pairs={{0,2},{1,3},{2,0},{3,1},{4,6},{5,7},{6,4},{7,5},{8,10},{9,11},{10,... | collective-permute-start | bytes 393224 | tf_op jit(solution)/shard_map/ppermute | solution.py:410
  52.5 7.7 %collective-permute-start.1 = (bf16[64,1024]{1,0:T(8,128)(2,1)S(1)}, bf16[64,1024]{1,0:T(8,128)(2,1)S(1)}, u32[]{:S(2)}, u32[]{:S(2)}) collective-permute-start(bf16[64,1024]{1,0:T(8,128)(2,1)S(1)} %get-tuple-element.26), channel_id=1, source_target_pairs={{0,2},{1,3},{2,0},{3,1},{4,6},{5,7},{6,4},{7,5},{8,10},{9,11},{10,... | collective-permute-start | bytes 393224 | tf_op jit(solution)/shard_map/ppermute | solution.py:410
  57.3 4.9 %collective-permute-start.8 = (bf16[16,1024]{1,0:T(8,128)(2,1)S(1)}, bf16[16,1024]{1,0:T(8,128)(2,1)S(1)}, u32[]{:S(2)}, u32[]{:S(2)}) collective-permute-start(bf16[16,1024]{1,0:T(8,128)(2,1)S(1)} %get-tuple-element.38), channel_id=1, source_target_pairs={{0,12},{1,13},{2,14},{3,15},{4,8},{5,9},{6,10},{7,11},{8,4},{9,5},... | collective-permute-start | bytes 98312 | tf_op jit(solution)/shard_map/ppermute | solution.py:410
  57.8 5.5 %collective-permute-start.7 = (bf16[16,1024]{1,0:T(8,128)(2,1)S(1)}, bf16[16,1024]{1,0:T(8,128)(2,1)S(1)}, u32[]{:S(2)}, u32[]{:S(2)}) collective-permute-start(bf16[16,1024]{1,0:T(8,128)(2,1)S(1)} %get-tuple-element.39), channel_id=1, source_target_pairs={{0,8},{1,9},{2,10},{3,11},{4,12},{5,13},{6,14},{7,15},{8,0},{9,1},... | collective-permute-start | bytes 98312 | tf_op jit(solution)/shard_map/ppermute | solution.py:410
  58.6 4.8 %collective-permute-start.6 = (bf16[16,1024]{1,0:T(8,128)(2,1)S(1)}, bf16[16,1024]{1,0:T(8,128)(2,1)S(1)}, u32[]{:S(2)}, u32[]{:S(2)}) collective-permute-start(bf16[16,1024]{1,0:T(8,128)(2,1)S(1)} %get-tuple-element.37), channel_id=1, source_target_pairs={{0,4},{1,5},{2,6},{3,7},{4,0},{5,1},{6,2},{7,3},{8,12},{9,13},{10,... | collective-permute-start | bytes 98312 | tf_op jit(solution)/shard_map/ppermute | solution.py:410
  60.2 3.2 %collective-permute-start.4 = (bf16[16,1024]{1,0:T(8,128)(2,1)S(1)}, bf16[16,1024]{1,0:T(8,128)(2,1)S(1)}, u32[]{:S(2)}, u32[]{:S(2)}) collective-permute-start(bf16[16,1024]{1,0:T(8,128)(2,1)S(1)} %get-tuple-element.35), channel_id=1, source_target_pairs={{0,12},{1,13},{2,14},{3,15},{4,8},{5,9},{6,10},{7,11},{8,4},{9,5},... | collective-permute-start | bytes 98312 | tf_op jit(solution)/shard_map/ppermute | solution.py:410
  60.9 3.8 %collective-permute-start.3 = (bf16[16,1024]{1,0:T(8,128)(2,1)S(1)}, bf16[16,1024]{1,0:T(8,128)(2,1)S(1)}, u32[]{:S(2)}, u32[]{:S(2)}) collective-permute-start(bf16[16,1024]{1,0:T(8,128)(2,1)S(1)} %get-tuple-element.36), channel_id=1, source_target_pairs={{0,8},{1,9},{2,10},{3,11},{4,12},{5,13},{6,14},{7,15},{8,0},{9,1},... | collective-permute-start | bytes 98312 | tf_op jit(solution)/shard_map/ppermute | solution.py:410
  62.2 3.1 %collective-permute-start.2 = (bf16[16,1024]{1,0:T(8,128)(2,1)S(1)}, bf16[16,1024]{1,0:T(8,128)(2,1)S(1)}, u32[]{:S(2)}, u32[]{:S(2)}) collective-permute-start(bf16[16,1024]{1,0:T(8,128)(2,1)S(1)} %get-tuple-element.34), channel_id=1, source_target_pairs={{0,4},{1,5},{2,6},{3,7},{4,0},{5,1},{6,2},{7,3},{8,12},{9,13},{10,... | collective-permute-start | bytes 98312 | tf_op jit(solution)/shard_map/ppermute | solution.py:410
  65.4 13.7 %collective-permute-start.9 = (bf16[32,1024]{1,0:T(8,128)(2,1)S(1)}, bf16[32,1024]{1,0:T(8,128)(2,1)S(1)}, u32[]{:S(2)}, u32[]{:S(2)}) collective-permute-start(bf16[32,1024]{1,0:T(8,128)(2,1)S(1)} %multiply_convert_fusion), channel_id=1, source_target_pairs={{0,12},{1,13},{2,14},{3,15},{4,8},{5,9},{6,10},{7,11},{8,4},{9,5},... | collective-permute-start | bytes 196616 | tf_op jit(solution)/shard_map/ppermute | solution.py:410
  67.4 11.6 %collective-permute-start.10 = (bf16[32,1024]{1,0:T(8,128)(2,1)S(1)}, bf16[32,1024]{1,0:T(8,128)(2,1)S(1)}, u32[]{:S(2)}, u32[]{:S(2)}) collective-permute-start(bf16[32,1024]{1,0:T(8,128)(2,1)S(1)} %multiply_convert_fusion), channel_id=1, source_target_pairs={{0,8},{1,9},{2,10},{3,11},{4,12},{5,13},{6,14},{7,15},{8,0},{9,1},... | collective-permute-start | bytes 196616 | tf_op jit(solution)/shard_map/ppermute | solution.py:410
  69.7 9.3 %collective-permute-start.11 = (bf16[32,1024]{1,0:T(8,128)(2,1)S(1)}, bf16[32,1024]{1,0:T(8,128)(2,1)S(1)}, u32[]{:S(2)}, u32[]{:S(2)}) collective-permute-start(bf16[32,1024]{1,0:T(8,128)(2,1)S(1)} %multiply_convert_fusion), channel_id=1, source_target_pairs={{0,4},{1,5},{2,6},{3,7},{4,0},{5,1},{6,2},{7,3},{8,12},{9,13},{10,... | collective-permute-start | bytes 196616 | tf_op jit(solution)/shard_map/ppermute | solution.py:410
  69.7 39.9 %all-to-all-start.1 = ((bf16[16,40,1024]{2,1,0:T(8,128)(2,1)}), bf16[16,40,1024]{2,1,0:T(8,128)(2,1)S(1)}, u32[]{:S(2)}, u32[]{:S(2)}) async-start(bf16[16,40,1024]{2,1,0:T(8,128)(2,1)} %pack.1), calls=%async_computation.1 | async-start | bytes 2621440 | tf_op jit(solution)/shard_map/all_to_all | solution.py:486
  79.2 13.8 %collective-permute-start.12 = (bf16[128,1024]{1,0:T(8,128)(2,1)S(1)}, bf16[128,1024]{1,0:T(8,128)(2,1)S(1)}, u32[]{:S(2)}, u32[]{:S(2)}) collective-permute-start(bf16[128,1024]{1,0:T(8,128)(2,1)S(1)} %pad_maximum_fusion.3), channel_id=1, source_target_pairs={{0,2},{1,3},{2,0},{3,1},{4,6},{5,7},{6,4},{7,5},{8,10},{9,11},{10,... | collective-permute-start | bytes 786440 | tf_op jit(solution)/shard_map/ppermute | solution.py:410
  93.2 4.2 %collective-permute-start.13 = (bf16[256,1024]{1,0:T(8,128)(2,1)S(1)}, bf16[256,1024]{1,0:T(8,128)(2,1)S(1)}, u32[]{:S(2)}, u32[]{:S(2)}) collective-permute-start(bf16[256,1024]{1,0:T(8,128)(2,1)S(1)} %pad_maximum_fusion.1), channel_id=1, source_target_pairs={{0,1},{1,0},{2,3},{3,2},{4,5},{5,4},{6,7},{7,6},{8,9},{9,8},{10,11... | collective-permute-start | bytes 1572872 | tf_op jit(solution)/shard_map/ppermute | solution.py:410

commit v20 on v18

--- a/solution.py
+++ b/solution.py
@@ -340,7 +340,6 @@
     del empty
     slots, tile_rows = terms.shape[0], terms.shape[1]
     count = (order + LANES) // LANES
-    totals[...] = jnp.zeros_like(totals)
     lane = lax.broadcasted_iota(jnp.int32, (tile_rows, LANES), 1)
     nothing = jnp.zeros((tile_rows, LANES), jnp.float32)
 
@@ -353,11 +352,14 @@
             for b in range(count - 1):
                 first = part * order + b * LANES
                 turned.append(pltpu.roll(terms[slot, :, first : first + LANES], shift, 1).astype(jnp.float32))
+            holders = [owners[slot * count + b] for b in range(count)]
+            held = [totals[holder, part] for holder in holders]
             for b in range(count):
                 before = turned[b - 1] if b else nothing
                 after = turned[b] if b < count - 1 else nothing
-                owner = owners[slot * count + b]
-                totals[owner, part] += jnp.where(lane < offset, before, after)
+                term = jnp.where(lane < offset, before, after)
+                first_one = holders[b] == slot * count + b
+                totals[holders[b], part] = jnp.where(first_one, term, held[b] + term)
 
     def copy(number):
         place = pl.multiple_of(blocks[number] * LANES, LANES)
@@ -420,7 +422,7 @@
         digit = me // stride % radix
         count = addends[0].shape[0] // radix
         met = []
-        for k in range(1, radix):
+        for k in range(radix - 1, 0, -1):
             share = rows(lax.bitwise_xor(digit, k), count).astype(jnp.bfloat16)
             met.append(swap(share, k * stride, devices))
         own = rows(digit, count)
@@ -434,10 +436,10 @@
     me = lax.axis_index("row")
     for stride, radix in reversed(strides(devices)):
         digit = me // stride % radix
-        shares = [whole] + [swap(whole, k * stride, devices) for k in range(1, radix)]
+        shares = {k: swap(whole, k * stride, devices) for k in range(radix - 1, 0, -1)}
         pieces = []
         for j in range(radix):
-            piece = shares[0]
+            piece = whole
             for k in range(1, radix):
                 piece = jnp.where(lax.bitwise_xor(digit, k) == j, shares[k], piece)
             pieces.append(piece)

time: 114 us -> 114 us (level)
  waiting for transfers between devices: 58.9 us -> 60.1 us
    ppermute x10, starting transfers between devices: 10.4 us -> 8.73 us  [swap(): return lax.ppermute(x, 'row', [(d, d ^ distance) for d in range(devices)])]
    ppermute x10, waiting for transfers between devices: 26 us -> 27.2 us  [swap(): return lax.ppermute(x, 'row', [(d, d ^ distance) for d in range(devices)])]
  transfers between devices with their start and end apart: 12 -> 12, of which waited for: 8 -> 7; matrix products, arithmetic and copies ran while one was open for 2% -> 2% of each run, Pallas kernels for 8% -> 8%
where the time goes in v20:
time: 114 us; the launch traced here: 113 us
  waiting for transfers between devices  60.1 us (53%)
  Pallas kernels  24.8 us (22%)
  starting transfers between devices  23.8 us (21%)
  other arithmetic  2.4 us (2%)
  local copies, waits for them, and re-layouts  1.26 us (1%)
    ppermute x10, waiting for transfers between devices, swap(): return lax.ppermute(x, 'row', [(d, d ^ distance) for d in range(devices)])  27.2 us
    all_to_all x1, waiting for transfers between devices, body(): lax.all_to_all(pieces, 'row', split_axis=0, concat_axis=0, tiled=True)  22.8 us
    all_to_all x1, waiting for transfers between devices, body(): lax.all_to_all(terms, 'row', split_axis=0, concat_axis=0, tiled=True)  10.1 us
    ppermute x10, starting transfers between devices, swap(): return lax.ppermute(x, 'row', [(d, d ^ distance) for d in range(devices)])  8.73 us
    all_to_all x1, starting transfers between devices, body(): lax.all_to_all(terms, 'row', split_axis=0, concat_axis=0, tiled=True)  8.36 us
    pallas_call x1, Pallas kernels, slot_terms(): pl.pallas_call(slot_kernel, out_shape=(jax.ShapeDtypeStruct((order, wide_...  7.4 us
    all_to_all x1, starting transfers between devices, body(): lax.all_to_all(pieces, 'row', split_axis=0, concat_axis=0, tiled=True)  6.7 us
    pallas_call x1, Pallas kernels, prepare(): pl.pallas_call(functools.partial(prepare_kernel, order), out_shape=(jax.S...  6.69 us
  transfers between devices with their start and end apart: 12, of which 7 were waited for; matrix products, arithmetic and copies ran while one was open for 2% of the time, Pallas kernels for 8%

profile of v20, /device:TPU:15, one launch (start us, length us, event | category | flops | bytes accessed | tf_op | source)
XLA Modules:
  0.0 113.2 jit_solution(14262285727381862744)
XLA Ops:
  0.6 4.7 %fetch.1 = (bf16[16,40,1024]{2,1,0:T(8,128)(2,1)}, s32[1]{0:T(128)}) custom-call(s32[16]{0:T(128)} %dealing.9, s32[16]{0:T(128)} %cols.5, f32[2,40,32768]{2,1,0:T(8,128)} %tile.1), custom_call_target="tpu_custom_call" | custom-call | bytes 6291456 | tf_op jit(solution)/shard_map/fetch/pallas_call | solution.py:81
  5.3 0.0 copy-start
  5.3 0.0 copy-start.1
  5.3 0.0 copy-start.3
  5.3 0.0 copy-start.4
  5.4 0.0 copy-start.5
  5.4 6.7 %all-to-all-start = ((bf16[16,40,1024]{2,1,0:T(8,128)(2,1)}), bf16[16,40,1024]{2,1,0:T(8,128)(2,1)S(1)}, u32[]{:S(2)}, u32[]{:S(2)}) async-start(bf16[16,40,1024]{2,1,0:T(8,128)(2,1)} %get-tuple-element.16), calls=%async_computation | async-start | bytes 2621440 | tf_op jit(solution)/shard_map/all_to_all | solution.py:460
  12.1 0.0 copy-done
  12.1 0.0 copy-done.1
  12.1 0.0 copy-done.3
  12.1 0.0 copy-done.4
  12.1 0.0 copy-start.2
  12.1 1.0 copy-done.2
  13.1 6.7 %prepare.1 = (f32[2,40,32768]{2,1,0:T(8,128)}, s32[80]{0:T(128)S(1)}, s32[80]{0:T(128)S(1)}, bf16[24576,1024]{1,0:T(8,128)(2,1)}) custom-call(s32[16]{0:T(128)S(1)} %copy-done.3, s32[16]{0:T(128)S(1)} %copy-done.4, s32[1]{0:T(128)} %get-tuple-element.13.token, bf16[512,1024]{1,0:T(8,128)(2,1)S(1)} %copy-done.1, bf16[2,512,512]{2,1,0:T(8,128)(2,1)S(1)} %copy-done, ...), custom_call_target="tpu_custom_call" | custom-call | bytes 115343360 | tf_op jit(solution)/shard_map/prepare/pallas_call | solution.py:156
  19.8 22.8 %all-to-all-done = bf16[16,40,1024]{2,1,0:T(8,128)(2,1)S(1)} async-done(((bf16[16,40,1024]{2,1,0:T(8,128)(2,1)}), bf16[16,40,1024]{2,1,0:T(8,128)(2,1)S(1)}, u32[]{:S(2)}, u32[]{:S(2)}) %all-to-all-start) | async-done | bytes 1310752 | tf_op jit(solution)/shard_map/all_to_all | solution.py:460
  42.6 0.0 copy-done.5
  42.6 7.4 %slot.1 = (bf16[512,1024]{1,0:T(8,128)(2,1)S(1)}, f32[256,1024]{1,0:T(8,128)S(1)}, bf16[256,1024]{1,0:T(8,128)(2,1)}) custom-call(s32[16]{0:T(128)S(1)} %copy-done.3, s32[16]{0:T(128)S(1)} %copy-done.5, s32[80]{0:T(128)S(1)} %get-tuple-element.15.owners, bf16[640,1024]{1,0:T(8,128)(2,1)S(1)} %bitcast.5, bf16[24576,1024]{1,0:T(8,128)(2,1)} %get-tuple-element.17.stock), custom_call_target="tpu_custom_call" | custom-call | flops 4294967296 | bytes 8388608 | tf_op jit(solution)/shard_map/slot/pallas_call | solution.py:279
  50.0 0.3 collective-permute-start
  50.3 1.9 %collective-permute-done = bf16[256,1024]{1,0:T(8,128)(2,1)S(1)} collective-permute-done((bf16[256,1024]{1,0:T(8,128)(2,1)}, bf16[256,1024]{1,0:T(8,128)(2,1)S(1)}, u32[]{:S(2)}, u32[]{:S(2)}) %collective-permute-start) | collective-permute-done | bytes 524320 | tf_op jit(solution)/shard_map/ppermute | solution.py:410
  52.2 0.1 add_convert_fusion
  52.4 0.1 collective-permute-start.1
  52.5 7.6 %collective-permute-done.1 = bf16[128,1024]{1,0:T(8,128)(2,1)S(1)} collective-permute-done((bf16[128,1024]{1,0:T(8,128)(2,1)S(1)}, bf16[128,1024]{1,0:T(8,128)(2,1)S(1)}, u32[]{:S(2)}, u32[]{:S(2)}) %collective-permute-start.1) | collective-permute-done | bytes 262176 | tf_op jit(solution)/shard_map/ppermute | solution.py:410
  60.2 0.1 collective-permute-start.4
  60.3 1.5 %collective-permute-start.3 = (bf16[32,1024]{1,0:T(8,128)(2,1)S(1)}, bf16[32,1024]{1,0:T(8,128)(2,1)S(1)}, u32[]{:S(2)}, u32[]{:S(2)}) collective-permute-start(bf16[32,1024]{1,0:T(8,128)(2,1)S(1)} %get-tuple-element.32), channel_id=1, source_target_pairs={{0,8},{1,9},{2,10},{3,11},{4,12},{5,13},{6,14},{7,15},{8,0},{9,1},... | collective-permute-start | bytes 196616 | tf_op jit(solution)/shard_map/ppermute | solution.py:410
  61.8 1.1 collective-permute-start.2
  62.9 2.2 %pack.1 = bf16[16,40,1024]{2,1,0:T(8,128)(2,1)} custom-call(s32[16]{0:T(128)S(1)} %copy-done.3, s32[16]{0:T(128)S(1)} %copy-done.5, bf16[512,1024]{1,0:T(8,128)(2,1)S(1)} %get-tuple-element.18.term), custom_call_target="tpu_custom_call" | custom-call | bytes 3145728 | tf_op jit(solution)/shard_map/pack/pallas_call | solution.py:327
  65.1 0.0 collective-permute-done.4
  65.1 0.0 collective-permute-done.3
  65.1 2.6 %collective-permute-done.2 = bf16[32,1024]{1,0:T(8,128)(2,1)S(1)} collective-permute-done((bf16[32,1024]{1,0:T(8,128)(2,1)S(1)}, bf16[32,1024]{1,0:T(8,128)(2,1)S(1)}, u32[]{:S(2)}, u32[]{:S(2)}) %collective-permute-start.2) | collective-permute-done | bytes 65568 | tf_op jit(solution)/shard_map/ppermute | solution.py:410
  67.7 1.2 %collective-permute-start.5 = (bf16[32,1024]{1,0:T(8,128)(2,1)S(1)}, bf16[32,1024]{1,0:T(8,128)(2,1)S(1)}, u32[]{:S(2)}, u32[]{:S(2)}) collective-permute-start(bf16[32,1024]{1,0:T(8,128)(2,1)S(1)} %multiply_convert_fusion), channel_id=1, source_target_pairs={{0,12},{1,13},{2,14},{3,15},{4,8},{5,9},{6,10},{7,11},{8,4},{9,5},... | collective-permute-start | bytes 196616 | tf_op jit(solution)/shard_map/ppermute | solution.py:410
  69.0 1.0 collective-permute-start.6
  70.0 0.5 collective-permute-start.7
  70.4 8.4 %all-to-all-start.1 = ((bf16[16,40,1024]{2,1,0:T(8,128)(2,1)}), bf16[16,40,1024]{2,1,0:T(8,128)(2,1)S(1)}, u32[]{:S(2)}, u32[]{:S(2)}) async-start(bf16[16,40,1024]{2,1,0:T(8,128)(2,1)} %pack.1), calls=%async_computation.1 | async-start | bytes 2621440 | tf_op jit(solution)/shard_map/all_to_all | solution.py:469
  78.8 0.0 collective-permute-done.5
  78.8 0.0 collective-permute-done.6
  78.8 0.0 collective-permute-done.7
  78.9 0.3 collective-permute-start.8
  79.3 13.5 %collective-permute-done.8 = bf16[128,1024]{1,0:T(8,128)(2,1)S(1)} collective-permute-done((bf16[128,1024]{1,0:T(8,128)(2,1)S(1)}, bf16[128,1024]{1,0:T(8,128)(2,1)S(1)}, u32[]{:S(2)}, u32[]{:S(2)}) %collective-permute-start.8) | collective-permute-done | bytes 262176 | tf_op jit(solution)/shard_map/ppermute | solution.py:410
  92.8 0.1 broadcast_select_fusion.3
  92.9 2.6 %collective-permute-start.9 = (bf16[256,1024]{1,0:T(8,128)(2,1)S(1)}, bf16[256,1024]{1,0:T(8,128)(2,1)S(1)}, u32[]{:S(2)}, u32[]{:S(2)}) collective-permute-start(bf16[256,1024]{1,0:T(8,128)(2,1)S(1)} %pad_maximum_fusion.1), channel_id=1, source_target_pairs={{0,1},{1,0},{2,3},{3,2},{4,5},{5,4},{6,7},{7,6},{8,9},{9,8},{10,11... | collective-permute-start | bytes 1572872 | tf_op jit(solution)/shard_map/ppermute | solution.py:410
  95.6 1.5 %collective-permute-done.9 = bf16[256,1024]{1,0:T(8,128)(2,1)S(1)} collective-permute-done((bf16[256,1024]{1,0:T(8,128)(2,1)S(1)}, bf16[256,1024]{1,0:T(8,128)(2,1)S(1)}, u32[]{:S(2)}, u32[]{:S(2)}) %collective-permute-start.9) | collective-permute-done | bytes 524320 | tf_op jit(solution)/shard_map/ppermute | solution.py:410
  97.1 0.2 broadcast_select_fusion.1
  97.3 0.2 maximum_convert_fusion
  97.6 0.2 slice_bitcast_fusion.1
  97.8 1.5 %pad_maximum_fusion = f32[2,512,512]{2,1,0:T(8,128)} fusion(f32[1,512,512]{2,1,0:T(8,128)S(1)} %get-tuple-element.25, f32[1,512,512]{2,1,0:T(8,128)S(1)} %get-tuple-element.24), kind=kLoop, calls=%fused_computation | loop fusion | flops 524288 | bytes 4194304 | tf_op jit(solution)/shard_map/stack | solution.py:472
  99.3 10.1 %all-to-all-done.1.terms = bf16[16,40,1024]{2,1,0:T(8,128)(2,1)S(1)} async-done(((bf16[16,40,1024]{2,1,0:T(8,128)(2,1)}), bf16[16,40,1024]{2,1,0:T(8,128)(2,1)S(1)}, u32[]{:S(2)}, u32[]{:S(2)}) %all-to-all-start.1) | async-done | bytes 1310752 | tf_op jit(solution)/shard_map/all_to_all | solution.py:469
  109.4 3.8 %place.1 = f32[2,40,32768]{2,1,0:T(8,128)} custom-call(s32[16]{0:T(128)S(1)} %copy-done.3, s32[16]{0:T(128)S(1)} %copy-done.4, s32[80]{0:T(128)S(1)} %get-tuple-element.14.blocks, s32[80]{0:T(128)S(1)} %get-tuple-element.15.owners, bf16[16,40,1024]{2,1,0:T(8,128)(2,1)S(1)} %all-to-all-done.1.terms, ...), custom_call_target="tpu_custom_call", output_to_operand_aliasing={{}: (5, {})} | custom-call | bytes 6291456 | tf_op jit(solution)/shard_map/place/pallas_call | solution.py:384
  (6 shorter events, 0.2 us)
Async XLA Ops:
  5.3 6.8 %copy-start = (bf16[2,512,512]{2,1,0:T(8,128)(2,1)S(1)}, bf16[2,512,512]{2,1,0:T(8,128)(2,1)}, u32[]{:S(2)}) copy-start(bf16[2,512,512]{2,1,0:T(8,128)(2,1)} %probe.1) | copy-start | bytes 3145732
  5.3 6.8 %copy-start.1 = (bf16[512,1024]{1,0:T(8,128)(2,1)S(1)}, bf16[512,1024]{1,0:T(8,128)(2,1)}, u32[]{:S(2)}) copy-start(bf16[512,1024]{1,0:T(8,128)(2,1)} %constant.79.clone.table_in) | copy-start | bytes 3145732
  5.3 6.8 %copy-start.3 = (s32[16]{0:T(128)S(1)}, s32[16]{0:T(128)}, u32[]{:S(2)}) copy-start(s32[16]{0:T(128)} %dealing.9) | copy-start | bytes 196
  5.3 6.8 %copy-start.4 = (s32[16]{0:T(128)S(1)}, s32[16]{0:T(128)}, u32[]{:S(2)}) copy-start(s32[16]{0:T(128)} %cols.5) | copy-start | bytes 196
  5.4 37.3 %copy-start.5 = (s32[16]{0:T(128)S(1)}, s32[16]{0:T(128)}, u32[]{:S(2)}) copy-start(s32[16]{0:T(128)} %rows.3) | copy-start | bytes 196
  5.4 37.3 %all-to-all-start = ((bf16[16,40,1024]{2,1,0:T(8,128)(2,1)}), bf16[16,40,1024]{2,1,0:T(8,128)(2,1)S(1)}, u32[]{:S(2)}, u32[]{:S(2)}) async-start(bf16[16,40,1024]{2,1,0:T(8,128)(2,1)} %get-tuple-element.16), calls=%async_computation | async-start | bytes 2621440 | tf_op jit(solution)/shard_map/all_to_all | solution.py:460
  12.1 1.0 copy-start.2
  50.0 2.2 %collective-permute-start = (bf16[256,1024]{1,0:T(8,128)(2,1)}, bf16[256,1024]{1,0:T(8,128)(2,1)S(1)}, u32[]{:S(2)}, u32[]{:S(2)}) collective-permute-start(bf16[256,1024]{1,0:T(8,128)(2,1)} %get-tuple-element.20), channel_id=1, source_target_pairs={{0,1},{1,0},{2,3},{3,2},{4,5},{5,4},{6,7},{7,6},{8,9},{9,8},{10,11... | collective-permute-start | bytes 1572872 | tf_op jit(solution)/shard_map/ppermute | solution.py:410
  52.4 7.8 %collective-permute-start.1 = (bf16[128,1024]{1,0:T(8,128)(2,1)S(1)}, bf16[128,1024]{1,0:T(8,128)(2,1)S(1)}, u32[]{:S(2)}, u32[]{:S(2)}) collective-permute-start(bf16[128,1024]{1,0:T(8,128)(2,1)S(1)} %get-tuple-element.26), channel_id=1, source_target_pairs={{0,2},{1,3},{2,0},{3,1},{4,6},{5,7},{6,4},{7,5},{8,10},{9,11},{10,... | collective-permute-start | bytes 786440 | tf_op jit(solution)/shard_map/ppermute | solution.py:410
  60.2 4.9 %collective-permute-start.4 = (bf16[32,1024]{1,0:T(8,128)(2,1)S(1)}, bf16[32,1024]{1,0:T(8,128)(2,1)S(1)}, u32[]{:S(2)}, u32[]{:S(2)}) collective-permute-start(bf16[32,1024]{1,0:T(8,128)(2,1)S(1)} %get-tuple-element.31), channel_id=1, source_target_pairs={{0,4},{1,5},{2,6},{3,7},{4,0},{5,1},{6,2},{7,3},{8,12},{9,13},{10,... | collective-permute-start | bytes 196616 | tf_op jit(solution)/shard_map/ppermute | solution.py:410
  60.3 4.8 %collective-permute-start.3 = (bf16[32,1024]{1,0:T(8,128)(2,1)S(1)}, bf16[32,1024]{1,0:T(8,128)(2,1)S(1)}, u32[]{:S(2)}, u32[]{:S(2)}) collective-permute-start(bf16[32,1024]{1,0:T(8,128)(2,1)S(1)} %get-tuple-element.32), channel_id=1, source_target_pairs={{0,8},{1,9},{2,10},{3,11},{4,12},{5,13},{6,14},{7,15},{8,0},{9,1},... | collective-permute-start | bytes 196616 | tf_op jit(solution)/shard_map/ppermute | solution.py:410
  61.8 5.9 %collective-permute-start.2 = (bf16[32,1024]{1,0:T(8,128)(2,1)S(1)}, bf16[32,1024]{1,0:T(8,128)(2,1)S(1)}, u32[]{:S(2)}, u32[]{:S(2)}) collective-permute-start(bf16[32,1024]{1,0:T(8,128)(2,1)S(1)} %get-tuple-element.30), channel_id=1, source_target_pairs={{0,12},{1,13},{2,14},{3,15},{4,8},{5,9},{6,10},{7,11},{8,4},{9,5},... | collective-permute-start | bytes 196616 | tf_op jit(solution)/shard_map/ppermute | solution.py:410
  67.7 11.1 %collective-permute-start.5 = (bf16[32,1024]{1,0:T(8,128)(2,1)S(1)}, bf16[32,1024]{1,0:T(8,128)(2,1)S(1)}, u32[]{:S(2)}, u32[]{:S(2)}) collective-permute-start(bf16[32,1024]{1,0:T(8,128)(2,1)S(1)} %multiply_convert_fusion), channel_id=1, source_target_pairs={{0,12},{1,13},{2,14},{3,15},{4,8},{5,9},{6,10},{7,11},{8,4},{9,5},... | collective-permute-start | bytes 196616 | tf_op jit(solution)/shard_map/ppermute | solution.py:410
  69.0 9.9 %collective-permute-start.6 = (bf16[32,1024]{1,0:T(8,128)(2,1)S(1)}, bf16[32,1024]{1,0:T(8,128)(2,1)S(1)}, u32[]{:S(2)}, u32[]{:S(2)}) collective-permute-start(bf16[32,1024]{1,0:T(8,128)(2,1)S(1)} %multiply_convert_fusion), channel_id=1, source_target_pairs={{0,8},{1,9},{2,10},{3,11},{4,12},{5,13},{6,14},{7,15},{8,0},{9,1},... | collective-permute-start | bytes 196616 | tf_op jit(solution)/shard_map/ppermute | solution.py:410
  70.0 8.9 %collective-permute-start.7 = (bf16[32,1024]{1,0:T(8,128)(2,1)S(1)}, bf16[32,1024]{1,0:T(8,128)(2,1)S(1)}, u32[]{:S(2)}, u32[]{:S(2)}) collective-permute-start(bf16[32,1024]{1,0:T(8,128)(2,1)S(1)} %multiply_convert_fusion), channel_id=1, source_target_pairs={{0,4},{1,5},{2,6},{3,7},{4,0},{5,1},{6,2},{7,3},{8,12},{9,13},{10,... | collective-permute-start | bytes 196616 | tf_op jit(solution)/shard_map/ppermute | solution.py:410
  70.4 38.9 %all-to-all-start.1 = ((bf16[16,40,1024]{2,1,0:T(8,128)(2,1)}), bf16[16,40,1024]{2,1,0:T(8,128)(2,1)S(1)}, u32[]{:S(2)}, u32[]{:S(2)}) async-start(bf16[16,40,1024]{2,1,0:T(8,128)(2,1)} %pack.1), calls=%async_computation.1 | async-start | bytes 2621440 | tf_op jit(solution)/shard_map/all_to_all | solution.py:469
  78.9 13.9 %collective-permute-start.8 = (bf16[128,1024]{1,0:T(8,128)(2,1)S(1)}, bf16[128,1024]{1,0:T(8,128)(2,1)S(1)}, u32[]{:S(2)}, u32[]{:S(2)}) collective-permute-start(bf16[128,1024]{1,0:T(8,128)(2,1)S(1)} %pad_maximum_fusion.2), channel_id=1, source_target_pairs={{0,2},{1,3},{2,0},{3,1},{4,6},{5,7},{6,4},{7,5},{8,10},{9,11},{10,... | collective-permute-start | bytes 786440 | tf_op jit(solution)/shard_map/ppermute | solution.py:410
  92.9 4.2 %collective-permute-start.9 = (bf16[256,1024]{1,0:T(8,128)(2,1)S(1)}, bf16[256,1024]{1,0:T(8,128)(2,1)S(1)}, u32[]{:S(2)}, u32[]{:S(2)}) collective-permute-start(bf16[256,1024]{1,0:T(8,128)(2,1)S(1)} %pad_maximum_fusion.1), channel_id=1, source_target_pairs={{0,1},{1,0},{2,3},{3,2},{4,5},{5,4},{6,7},{7,6},{8,9},{9,8},{10,11... | collective-permute-start | bytes 1572872 | tf_op jit(solution)/shard_map/ppermute | solution.py:410

commit v21 on v20

--- a/solution.py
+++ b/solution.py
@@ -225,11 +225,9 @@
         one = jnp.dot(a, b, preferred_element_type=jnp.float32)
         return one + jnp.dot(c, d, preferred_element_type=jnp.float32)
 
-    for first in range(0, order, tile):
-        here = slice(first, first + tile)
-        real, imag = wave[:, first_half], wave[:, second_half]
-        half[first_half, here] = dots(real, cos[:, here], imag, minus[:, here]).astype(half.dtype)
-        half[second_half, here] = dots(real, sin[:, here], imag, cos[:, here]).astype(half.dtype)
+    real, imag = wave[:, first_half], wave[:, second_half]
+    half[first_half, :] = dots(real, cos[...], imag, minus[...]).astype(half.dtype)
+    half[second_half, :] = dots(real, sin[...], imag, cos[...]).astype(half.dtype)
     loads[2].wait()
     for first in range(0, order, tile):
         here = slice(first, first + tile)
@@ -243,11 +241,9 @@
             shrink = 1.0 - measured[line, here].astype(jnp.float32) * inverse
             resid[line, here] = (real * shrink).astype(resid.dtype)
             resid[line, there] = (imag * shrink).astype(resid.dtype)
-    for first in range(0, order, tile):
-        here = slice(first, first + tile)
-        real, imag = resid[:, first_half], resid[:, second_half]
-        turned[first_half, here] = dots(real, cos[:, here], imag, sin[:, here]).astype(turned.dtype)
-        turned[second_half, here] = dots(real, minus[:, here], imag, cos[:, here]).astype(turned.dtype)
+    real, imag = resid[:, first_half], resid[:, second_half]
+    turned[first_half, :] = dots(real, cos[...], imag, sin[...]).astype(turned.dtype)
+    turned[second_half, :] = dots(real, minus[...], imag, cos[...]).astype(turned.dtype)
     count = order // 2
     side = lax.rem(me, 2)
     for number, target in ((1 - side, leaving), (side, kept)):
@@ -422,7 +418,7 @@
         digit = me // stride % radix
         count = addends[0].shape[0] // radix
         met = []
-        for k in range(radix - 1, 0, -1):
+        for k in range(1, radix):
             share = rows(lax.bitwise_xor(digit, k), count).astype(jnp.bfloat16)
             met.append(swap(share, k * stride, devices))
         own = rows(digit, count)
@@ -436,10 +432,10 @@
     me = lax.axis_index("row")
     for stride, radix in reversed(strides(devices)):
         digit = me // stride % radix
-        shares = {k: swap(whole, k * stride, devices) for k in range(radix - 1, 0, -1)}
+        shares = [whole] + [swap(whole, k * stride, devices) for k in range(1, radix)]
         pieces = []
         for j in range(radix):
-            piece = whole
+            piece = shares[0]
             for k in range(1, radix):
                 piece = jnp.where(lax.bitwise_xor(digit, k) == j, shares[k], piece)
             pieces.append(piece)

time: 114 us -> 113 us (level)
  waiting for transfers between devices: 60.1 us -> 58.9 us
    ppermute x10, starting transfers between devices: 8.73 us -> 10.4 us  [swap(): return lax.ppermute(x, 'row', [(d, d ^ distance) for d in range(devices)])]
    ppermute x10, waiting for transfers between devices: 27.2 us -> 26 us  [swap(): return lax.ppermute(x, 'row', [(d, d ^ distance) for d in range(devices)])]
  transfers between devices with their start and end apart: 12 -> 12, of which waited for: 7 -> 8; matrix products, arithmetic and copies ran while one was open for 2% -> 2% of each run, Pallas kernels for 8% -> 8%
where the time goes in v21:
time: 113 us
  waiting for transfers between devices  58.9 us (52%)
  Pallas kernels  24.8 us (22%)
  starting transfers between devices  24.6 us (22%)
  other arithmetic  2.4 us (2%)
  local copies, waits for them, and re-layouts  1.26 us (1%)
    ppermute x10, waiting for transfers between devices, swap(): return lax.ppermute(x, 'row', [(d, d ^ distance) for d in range(devices)])  26 us
    all_to_all x1, waiting for transfers between devices, body(): lax.all_to_all(pieces, 'row', split_axis=0, concat_axis=0, tiled=True)  22.8 us
    ppermute x10, starting transfers between devices, swap(): return lax.ppermute(x, 'row', [(d, d ^ distance) for d in range(devices)])  10.4 us
    all_to_all x1, waiting for transfers between devices, body(): lax.all_to_all(terms, 'row', split_axis=0, concat_axis=0, tiled=True)  10.1 us
    all_to_all x1, starting transfers between devices, body(): lax.all_to_all(terms, 'row', split_axis=0, concat_axis=0, tiled=True)  7.49 us
    pallas_call x1, Pallas kernels, slot_terms(): pl.pallas_call(slot_kernel, out_shape=(jax.ShapeDtypeStruct((order, wide_...  7.47 us
    all_to_all x1, starting transfers between devices, body(): lax.all_to_all(pieces, 'row', split_axis=0, concat_axis=0, tiled=True)  6.7 us
    pallas_call x1, Pallas kernels, prepare(): pl.pallas_call(functools.partial(prepare_kernel, order), out_shape=(jax.S...  6.69 us
  transfers between devices with their start and end apart: 12, of which 8 were waited for; matrix products, arithmetic and copies ran while one was open for 2% of the time, Pallas kernels for 8%

profile of v21, /device:TPU:15, one launch (start us, length us, event | category | flops | bytes accessed | tf_op | source)
XLA Modules:
  0.0 112.9 jit_solution(5761912818641786910)
XLA Ops:
  0.6 4.7 %fetch.1 = (bf16[16,40,1024]{2,1,0:T(8,128)(2,1)}, s32[1]{0:T(128)}) custom-call(s32[16]{0:T(128)} %dealing.9, s32[16]{0:T(128)} %cols.5, f32[2,40,32768]{2,1,0:T(8,128)} %tile.1), custom_call_target="tpu_custom_call" | custom-call | bytes 6291456 | tf_op jit(solution)/shard_map/fetch/pallas_call | solution.py:81
  5.3 0.0 copy-start
  5.3 0.0 copy-start.1
  5.3 0.0 copy-start.3
  5.3 0.0 copy-start.4
  5.4 0.0 copy-start.5
  5.4 6.7 %all-to-all-start = ((bf16[16,40,1024]{2,1,0:T(8,128)(2,1)}), bf16[16,40,1024]{2,1,0:T(8,128)(2,1)S(1)}, u32[]{:S(2)}, u32[]{:S(2)}) async-start(bf16[16,40,1024]{2,1,0:T(8,128)(2,1)} %get-tuple-element.16), calls=%async_computation | async-start | bytes 2621440 | tf_op jit(solution)/shard_map/all_to_all | solution.py:456
  12.1 0.0 copy-done
  12.1 0.0 copy-done.1
  12.1 0.0 copy-done.3
  12.1 0.0 copy-done.4
  12.1 0.0 copy-start.2
  12.1 1.0 copy-done.2
  13.1 6.7 %prepare.1 = (f32[2,40,32768]{2,1,0:T(8,128)}, s32[80]{0:T(128)S(1)}, s32[80]{0:T(128)S(1)}, bf16[24576,1024]{1,0:T(8,128)(2,1)}) custom-call(s32[16]{0:T(128)S(1)} %copy-done.3, s32[16]{0:T(128)S(1)} %copy-done.4, s32[1]{0:T(128)} %get-tuple-element.13.token, bf16[512,1024]{1,0:T(8,128)(2,1)S(1)} %copy-done.1, bf16[2,512,512]{2,1,0:T(8,128)(2,1)S(1)} %copy-done, ...), custom_call_target="tpu_custom_call" | custom-call | bytes 115343360 | tf_op jit(solution)/shard_map/prepare/pallas_call | solution.py:156
  19.8 22.8 %all-to-all-done = bf16[16,40,1024]{2,1,0:T(8,128)(2,1)S(1)} async-done(((bf16[16,40,1024]{2,1,0:T(8,128)(2,1)}), bf16[16,40,1024]{2,1,0:T(8,128)(2,1)S(1)}, u32[]{:S(2)}, u32[]{:S(2)}) %all-to-all-start) | async-done | bytes 1310752 | tf_op jit(solution)/shard_map/all_to_all | solution.py:456
  42.6 0.0 copy-done.5
  42.6 7.5 %slot.1 = (bf16[512,1024]{1,0:T(8,128)(2,1)S(1)}, f32[256,1024]{1,0:T(8,128)S(1)}, bf16[256,1024]{1,0:T(8,128)(2,1)}) custom-call(s32[16]{0:T(128)S(1)} %copy-done.3, s32[16]{0:T(128)S(1)} %copy-done.5, s32[80]{0:T(128)S(1)} %get-tuple-element.15.owners, bf16[640,1024]{1,0:T(8,128)(2,1)S(1)} %bitcast.5, bf16[24576,1024]{1,0:T(8,128)(2,1)} %get-tuple-element.17.stock), custom_call_target="tpu_custom_call" | custom-call | flops 4294967296 | bytes 8388608 | tf_op jit(solution)/shard_map/slot/pallas_call | solution.py:275
  50.1 0.3 collective-permute-start
  50.4 1.9 %collective-permute-done = bf16[256,1024]{1,0:T(8,128)(2,1)S(1)} collective-permute-done((bf16[256,1024]{1,0:T(8,128)(2,1)}, bf16[256,1024]{1,0:T(8,128)(2,1)S(1)}, u32[]{:S(2)}, u32[]{:S(2)}) %collective-permute-start) | collective-permute-done | bytes 524320 | tf_op jit(solution)/shard_map/ppermute | solution.py:406
  52.3 0.1 add_convert_fusion
  52.4 0.1 collective-permute-start.1
  52.6 7.6 %collective-permute-done.1 = bf16[128,1024]{1,0:T(8,128)(2,1)S(1)} collective-permute-done((bf16[128,1024]{1,0:T(8,128)(2,1)S(1)}, bf16[128,1024]{1,0:T(8,128)(2,1)S(1)}, u32[]{:S(2)}, u32[]{:S(2)}) %collective-permute-start.1) | collective-permute-done | bytes 262176 | tf_op jit(solution)/shard_map/ppermute | solution.py:406
  60.2 0.4 collective-permute-start.4
  60.7 0.8 collective-permute-start.3
  61.5 1.5 %collective-permute-start.2 = (bf16[32,1024]{1,0:T(8,128)(2,1)S(1)}, bf16[32,1024]{1,0:T(8,128)(2,1)S(1)}, u32[]{:S(2)}, u32[]{:S(2)}) collective-permute-start(bf16[32,1024]{1,0:T(8,128)(2,1)S(1)} %get-tuple-element.30), channel_id=1, source_target_pairs={{0,4},{1,5},{2,6},{3,7},{4,0},{5,1},{6,2},{7,3},{8,12},{9,13},{10,... | collective-permute-start | bytes 196616 | tf_op jit(solution)/shard_map/ppermute | solution.py:406
  63.0 2.2 %pack.1 = bf16[16,40,1024]{2,1,0:T(8,128)(2,1)} custom-call(s32[16]{0:T(128)S(1)} %copy-done.3, s32[16]{0:T(128)S(1)} %copy-done.5, bf16[512,1024]{1,0:T(8,128)(2,1)S(1)} %get-tuple-element.18.term), custom_call_target="tpu_custom_call" | custom-call | bytes 3145728 | tf_op jit(solution)/shard_map/pack/pallas_call | solution.py:323
  65.2 0.3 collective-permute-done.4
  65.5 0.0 collective-permute-done.3
  65.5 1.1 collective-permute-done.2
  66.6 0.9 collective-permute-start.5
  67.6 3.4 %collective-permute-start.6 = (bf16[32,1024]{1,0:T(8,128)(2,1)S(1)}, bf16[32,1024]{1,0:T(8,128)(2,1)S(1)}, u32[]{:S(2)}, u32[]{:S(2)}) collective-permute-start(bf16[32,1024]{1,0:T(8,128)(2,1)S(1)} %multiply_convert_fusion), channel_id=1, source_target_pairs={{0,8},{1,9},{2,10},{3,11},{4,12},{5,13},{6,14},{7,15},{8,0},{9,1},... | collective-permute-start | bytes 196616 | tf_op jit(solution)/shard_map/ppermute | solution.py:406
  71.0 0.0 collective-permute-start.7
  71.0 7.5 %all-to-all-start.1 = ((bf16[16,40,1024]{2,1,0:T(8,128)(2,1)}), bf16[16,40,1024]{2,1,0:T(8,128)(2,1)S(1)}, u32[]{:S(2)}, u32[]{:S(2)}) async-start(bf16[16,40,1024]{2,1,0:T(8,128)(2,1)} %pack.1), calls=%async_computation.1 | async-start | bytes 2621440 | tf_op jit(solution)/shard_map/all_to_all | solution.py:465
  78.5 0.0 collective-permute-done.5
  78.5 0.0 collective-permute-done.6
  78.5 0.0 collective-permute-done.7
  78.6 0.3 collective-permute-start.8
  78.9 13.5 %collective-permute-done.8 = bf16[128,1024]{1,0:T(8,128)(2,1)S(1)} collective-permute-done((bf16[128,1024]{1,0:T(8,128)(2,1)S(1)}, bf16[128,1024]{1,0:T(8,128)(2,1)S(1)}, u32[]{:S(2)}, u32[]{:S(2)}) %collective-permute-start.8) | collective-permute-done | bytes 262176 | tf_op jit(solution)/shard_map/ppermute | solution.py:406
  92.5 0.1 broadcast_select_fusion.3
  92.6 2.6 %collective-permute-start.9 = (bf16[256,1024]{1,0:T(8,128)(2,1)S(1)}, bf16[256,1024]{1,0:T(8,128)(2,1)S(1)}, u32[]{:S(2)}, u32[]{:S(2)}) collective-permute-start(bf16[256,1024]{1,0:T(8,128)(2,1)S(1)} %pad_maximum_fusion.1), channel_id=1, source_target_pairs={{0,1},{1,0},{2,3},{3,2},{4,5},{5,4},{6,7},{7,6},{8,9},{9,8},{10,11... | collective-permute-start | bytes 1572872 | tf_op jit(solution)/shard_map/ppermute | solution.py:406
  95.2 1.5 %collective-permute-done.9 = bf16[256,1024]{1,0:T(8,128)(2,1)S(1)} collective-permute-done((bf16[256,1024]{1,0:T(8,128)(2,1)S(1)}, bf16[256,1024]{1,0:T(8,128)(2,1)S(1)}, u32[]{:S(2)}, u32[]{:S(2)}) %collective-permute-start.9) | collective-permute-done | bytes 524320 | tf_op jit(solution)/shard_map/ppermute | solution.py:406
  96.8 0.2 broadcast_select_fusion.1
  97.0 0.2 maximum_convert_fusion
  97.3 0.2 slice_bitcast_fusion.1
  97.5 1.5 %pad_maximum_fusion = f32[2,512,512]{2,1,0:T(8,128)} fusion(f32[1,512,512]{2,1,0:T(8,128)S(1)} %get-tuple-element.25, f32[1,512,512]{2,1,0:T(8,128)S(1)} %get-tuple-element.24), kind=kLoop, calls=%fused_computation | loop fusion | flops 524288 | bytes 4194304 | tf_op jit(solution)/shard_map/stack | solution.py:468
  99.0 10.1 %all-to-all-done.1.terms = bf16[16,40,1024]{2,1,0:T(8,128)(2,1)S(1)} async-done(((bf16[16,40,1024]{2,1,0:T(8,128)(2,1)}), bf16[16,40,1024]{2,1,0:T(8,128)(2,1)S(1)}, u32[]{:S(2)}, u32[]{:S(2)}) %all-to-all-start.1) | async-done | bytes 1310752 | tf_op jit(solution)/shard_map/all_to_all | solution.py:465
  109.1 3.8 %place.1 = f32[2,40,32768]{2,1,0:T(8,128)} custom-call(s32[16]{0:T(128)S(1)} %copy-done.3, s32[16]{0:T(128)S(1)} %copy-done.4, s32[80]{0:T(128)S(1)} %get-tuple-element.14.blocks, s32[80]{0:T(128)S(1)} %get-tuple-element.15.owners, bf16[16,40,1024]{2,1,0:T(8,128)(2,1)S(1)} %all-to-all-done.1.terms, ...), custom_call_target="tpu_custom_call", output_to_operand_aliasing={{}: (5, {})} | custom-call | bytes 6291456 | tf_op jit(solution)/shard_map/place/pallas_call | solution.py:380
  (6 shorter events, 0.2 us)
Async XLA Ops:
  5.3 6.8 %copy-start = (bf16[2,512,512]{2,1,0:T(8,128)(2,1)S(1)}, bf16[2,512,512]{2,1,0:T(8,128)(2,1)}, u32[]{:S(2)}) copy-start(bf16[2,512,512]{2,1,0:T(8,128)(2,1)} %probe.1) | copy-start | bytes 3145732
  5.3 6.8 %copy-start.1 = (bf16[512,1024]{1,0:T(8,128)(2,1)S(1)}, bf16[512,1024]{1,0:T(8,128)(2,1)}, u32[]{:S(2)}) copy-start(bf16[512,1024]{1,0:T(8,128)(2,1)} %constant.79.clone.table_in) | copy-start | bytes 3145732
  5.3 6.8 %copy-start.3 = (s32[16]{0:T(128)S(1)}, s32[16]{0:T(128)}, u32[]{:S(2)}) copy-start(s32[16]{0:T(128)} %dealing.9) | copy-start | bytes 196
  5.3 6.8 %copy-start.4 = (s32[16]{0:T(128)S(1)}, s32[16]{0:T(128)}, u32[]{:S(2)}) copy-start(s32[16]{0:T(128)} %cols.5) | copy-start | bytes 196
  5.4 37.3 %copy-start.5 = (s32[16]{0:T(128)S(1)}, s32[16]{0:T(128)}, u32[]{:S(2)}) copy-start(s32[16]{0:T(128)} %rows.3) | copy-start | bytes 196
  5.4 37.3 %all-to-all-start = ((bf16[16,40,1024]{2,1,0:T(8,128)(2,1)}), bf16[16,40,1024]{2,1,0:T(8,128)(2,1)S(1)}, u32[]{:S(2)}, u32[]{:S(2)}) async-start(bf16[16,40,1024]{2,1,0:T(8,128)(2,1)} %get-tuple-element.16), calls=%async_computation | async-start | bytes 2621440 | tf_op jit(solution)/shard_map/all_to_all | solution.py:456
  12.1 1.0 copy-start.2
  50.1 2.2 %collective-permute-start = (bf16[256,1024]{1,0:T(8,128)(2,1)}, bf16[256,1024]{1,0:T(8,128)(2,1)S(1)}, u32[]{:S(2)}, u32[]{:S(2)}) collective-permute-start(bf16[256,1024]{1,0:T(8,128)(2,1)} %get-tuple-element.20), channel_id=1, source_target_pairs={{0,1},{1,0},{2,3},{3,2},{4,5},{5,4},{6,7},{7,6},{8,9},{9,8},{10,11... | collective-permute-start | bytes 1572872 | tf_op jit(solution)/shard_map/ppermute | solution.py:406
  52.4 7.8 %collective-permute-start.1 = (bf16[128,1024]{1,0:T(8,128)(2,1)S(1)}, bf16[128,1024]{1,0:T(8,128)(2,1)S(1)}, u32[]{:S(2)}, u32[]{:S(2)}) collective-permute-start(bf16[128,1024]{1,0:T(8,128)(2,1)S(1)} %get-tuple-element.26), channel_id=1, source_target_pairs={{0,2},{1,3},{2,0},{3,1},{4,6},{5,7},{6,4},{7,5},{8,10},{9,11},{10,... | collective-permute-start | bytes 786440 | tf_op jit(solution)/shard_map/ppermute | solution.py:406
  60.2 5.2 %collective-permute-start.4 = (bf16[32,1024]{1,0:T(8,128)(2,1)S(1)}, bf16[32,1024]{1,0:T(8,128)(2,1)S(1)}, u32[]{:S(2)}, u32[]{:S(2)}) collective-permute-start(bf16[32,1024]{1,0:T(8,128)(2,1)S(1)} %get-tuple-element.31), channel_id=1, source_target_pairs={{0,12},{1,13},{2,14},{3,15},{4,8},{5,9},{6,10},{7,11},{8,4},{9,5},... | collective-permute-start | bytes 196616 | tf_op jit(solution)/shard_map/ppermute | solution.py:406
  60.7 4.8 %collective-permute-start.3 = (bf16[32,1024]{1,0:T(8,128)(2,1)S(1)}, bf16[32,1024]{1,0:T(8,128)(2,1)S(1)}, u32[]{:S(2)}, u32[]{:S(2)}) collective-permute-start(bf16[32,1024]{1,0:T(8,128)(2,1)S(1)} %get-tuple-element.32), channel_id=1, source_target_pairs={{0,8},{1,9},{2,10},{3,11},{4,12},{5,13},{6,14},{7,15},{8,0},{9,1},... | collective-permute-start | bytes 196616 | tf_op jit(solution)/shard_map/ppermute | solution.py:406
  61.5 5.1 %collective-permute-start.2 = (bf16[32,1024]{1,0:T(8,128)(2,1)S(1)}, bf16[32,1024]{1,0:T(8,128)(2,1)S(1)}, u32[]{:S(2)}, u32[]{:S(2)}) collective-permute-start(bf16[32,1024]{1,0:T(8,128)(2,1)S(1)} %get-tuple-element.30), channel_id=1, source_target_pairs={{0,4},{1,5},{2,6},{3,7},{4,0},{5,1},{6,2},{7,3},{8,12},{9,13},{10,... | collective-permute-start | bytes 196616 | tf_op jit(solution)/shard_map/ppermute | solution.py:406
  66.6 11.8 %collective-permute-start.5 = (bf16[32,1024]{1,0:T(8,128)(2,1)S(1)}, bf16[32,1024]{1,0:T(8,128)(2,1)S(1)}, u32[]{:S(2)}, u32[]{:S(2)}) collective-permute-start(bf16[32,1024]{1,0:T(8,128)(2,1)S(1)} %multiply_convert_fusion), channel_id=1, source_target_pairs={{0,12},{1,13},{2,14},{3,15},{4,8},{5,9},{6,10},{7,11},{8,4},{9,5},... | collective-permute-start | bytes 196616 | tf_op jit(solution)/shard_map/ppermute | solution.py:406
  67.6 10.9 %collective-permute-start.6 = (bf16[32,1024]{1,0:T(8,128)(2,1)S(1)}, bf16[32,1024]{1,0:T(8,128)(2,1)S(1)}, u32[]{:S(2)}, u32[]{:S(2)}) collective-permute-start(bf16[32,1024]{1,0:T(8,128)(2,1)S(1)} %multiply_convert_fusion), channel_id=1, source_target_pairs={{0,8},{1,9},{2,10},{3,11},{4,12},{5,13},{6,14},{7,15},{8,0},{9,1},... | collective-permute-start | bytes 196616 | tf_op jit(solution)/shard_map/ppermute | solution.py:406
  71.0 7.5 %collective-permute-start.7 = (bf16[32,1024]{1,0:T(8,128)(2,1)S(1)}, bf16[32,1024]{1,0:T(8,128)(2,1)S(1)}, u32[]{:S(2)}, u32[]{:S(2)}) collective-permute-start(bf16[32,1024]{1,0:T(8,128)(2,1)S(1)} %multiply_convert_fusion), channel_id=1, source_target_pairs={{0,4},{1,5},{2,6},{3,7},{4,0},{5,1},{6,2},{7,3},{8,12},{9,13},{10,... | collective-permute-start | bytes 196616 | tf_op jit(solution)/shard_map/ppermute | solution.py:406
  71.0 38.1 %all-to-all-start.1 = ((bf16[16,40,1024]{2,1,0:T(8,128)(2,1)}), bf16[16,40,1024]{2,1,0:T(8,128)(2,1)S(1)}, u32[]{:S(2)}, u32[]{:S(2)}) async-start(bf16[16,40,1024]{2,1,0:T(8,128)(2,1)} %pack.1), calls=%async_computation.1 | async-start | bytes 2621440 | tf_op jit(solution)/shard_map/all_to_all | solution.py:465
  78.6 13.9 %collective-permute-start.8 = (bf16[128,1024]{1,0:T(8,128)(2,1)S(1)}, bf16[128,1024]{1,0:T(8,128)(2,1)S(1)}, u32[]{:S(2)}, u32[]{:S(2)}) collective-permute-start(bf16[128,1024]{1,0:T(8,128)(2,1)S(1)} %pad_maximum_fusion.2), channel_id=1, source_target_pairs={{0,2},{1,3},{2,0},{3,1},{4,6},{5,7},{6,4},{7,5},{8,10},{9,11},{10,... | collective-permute-start | bytes 786440 | tf_op jit(solution)/shard_map/ppermute | solution.py:406
  92.6 4.2 %collective-permute-start.9 = (bf16[256,1024]{1,0:T(8,128)(2,1)S(1)}, bf16[256,1024]{1,0:T(8,128)(2,1)S(1)}, u32[]{:S(2)}, u32[]{:S(2)}) collective-permute-start(bf16[256,1024]{1,0:T(8,128)(2,1)S(1)} %pad_maximum_fusion.1), channel_id=1, source_target_pairs={{0,1},{1,0},{2,3},{3,2},{4,5},{5,4},{6,7},{7,6},{8,9},{9,8},{10,11... | collective-permute-start | bytes 1572872 | tf_op jit(solution)/shard_map/ppermute | solution.py:406

commit v22 on v21

--- a/solution.py
+++ b/solution.py
@@ -106,8 +106,8 @@
 
 
 def prepare_kernel(
-    order, dealing, cols, token, table_in, probe, measured,
-    empty, blocks, owners, stock,
+    order, dealing, rows, cols, token, table_in, probe, measured,
+    empty, starts, info, stock,
     table, zeros, sems, stock_sems,
 ):
     del token
@@ -134,21 +134,23 @@
 
     @pl.loop(0, slots)
     def _(slot):
-        base, _ = window_start(cols[dealing[slot]], order, tile_cols)
+        base, offset = window_start(cols[dealing[slot]], order, tile_cols)
+        starts[slot] = rows[dealing[slot]]
+        info[2 * slots * count + slot] = offset
         for b in range(count):
             number = slot * count + b
             block = base // LANES + b
-            blocks[number] = block
+            info[number] = block
             known = table[block]
             owner = jnp.where(known < 0, number, known)
-            owners[number] = owner
+            info[slots * count + number] = owner
             table[block] = owner
 
     for fill in fills:
         fill.wait()
 
 
-def prepare(dealing, cols, token, probe, measured, tile_shape):
+def prepare(dealing, rows, cols, token, probe, measured, tile_shape):
     order = probe.shape[1]
     slots = dealing.shape[0]
     numbers = slots * (order + LANES) // LANES
@@ -157,11 +159,11 @@
         functools.partial(prepare_kernel, order),
         out_shape=(
             jax.ShapeDtypeStruct(tile_shape, jnp.float32),
-            jax.ShapeDtypeStruct((numbers,), jnp.int32),
-            jax.ShapeDtypeStruct((numbers,), jnp.int32),
+            jax.ShapeDtypeStruct((slots,), jnp.int32),
+            jax.ShapeDtypeStruct((2 * numbers + slots,), jnp.int32),
             jax.ShapeDtypeStruct((48 * order, 2 * order), jnp.bfloat16),
         ),
-        in_specs=[SMEM, SMEM, SMEM, ANY, ANY, ANY],
+        in_specs=[SMEM, SMEM, SMEM, SMEM, ANY, ANY, ANY],
         out_specs=(ANY, SMEM, SMEM, ANY),
         scratch_shapes=[
             pltpu.SMEM((tile_shape[2] // LANES,), jnp.int32),
@@ -172,15 +174,14 @@
         compiler_params=pltpu.CompilerParams(vmem_limit_bytes=8 * 2**20),
         cost_estimate=pl.CostEstimate(flops=0, bytes_accessed=110 * 2**20, transcendentals=0),
         name="prepare",
-    )(dealing, cols, token, jnp.asarray(dft_table(order)), probe, measured)
+    )(dealing, rows, cols, token, jnp.asarray(dft_table(order)), probe, measured)
 
 
 def slot_kernel(
-    dealing, rows, owners, cells, stock,
+    starts, cells, stock,
     term, kept, sent,
     wide, patch, wave, half, resid, turned, leaving, probe, table, minus, measured, sems, leave_sem,
 ):
-    del owners
     order = term.shape[0]
     places = (stock.at[0:order, :],) + stock_places(stock, order)[2:]
     targets = (probe, table, measured)
@@ -192,7 +193,7 @@
         load.start()
     total_rows = cells.shape[0]
     me = lax.axis_index("row")
-    first_row = rows[dealing[me]]
+    first_row = starts[me]
     step = 64
     tile = 256
 
@@ -268,7 +269,7 @@
     leave.wait()
 
 
-def slot_terms(cells, stock, dealing, rows, owners, order):
+def slot_terms(cells, stock, starts, order):
     total_rows = cells.shape[0]
     wide_cols = 2 * order
     bf16, f32 = jnp.bfloat16, jnp.float32
@@ -279,7 +280,7 @@
             jax.ShapeDtypeStruct((order // 2, wide_cols), f32),
             jax.ShapeDtypeStruct((order // 2, wide_cols), bf16),
         ),
-        in_specs=[SMEM, SMEM, SMEM, VMEM, ANY],
+        in_specs=[SMEM, VMEM, ANY],
         out_specs=(VMEM, VMEM, ANY),
         scratch_shapes=[
             pltpu.VMEM((total_rows + SUBLANES, wide_cols), f32),
@@ -301,12 +302,12 @@
             flops=8 * 2 * order**3 * 2, bytes_accessed=8 * 2**20, transcendentals=order * order
         ),
         name="slot",
-    )(dealing, rows, owners, cells, stock)
-
-
-def pack_kernel(reach, own_rows, dealing, rows, term, out, padded):
+    )(starts, cells, stock)
+
+
+def pack_kernel(reach, own_rows, starts, term, out, padded):
     order = term.shape[0]
-    first_row = rows[dealing[lax.axis_index("row")]]
+    first_row = starts[lax.axis_index("row")]
     below = padded.shape[0] - reach - order
     padded[0:reach, :] = jnp.zeros((reach, padded.shape[1]), jnp.float32)
     padded[reach : reach + order, :] = term[...].astype(jnp.float32)
@@ -317,22 +318,22 @@
         out[k] = rows_from(padded, reach - first_row + k * own_rows, out.shape[1]).astype(out.dtype)
 
 
-def pack_rows(term, dealing, rows, slots, own_rows, tile_rows):
+def pack_rows(term, starts, slots, own_rows, tile_rows):
     order, width = term.shape
     reach = slots * own_rows - order
     return pl.pallas_call(
         functools.partial(pack_kernel, reach, own_rows),
         out_shape=jax.ShapeDtypeStruct((slots, tile_rows, width), jnp.bfloat16),
-        in_specs=[SMEM, SMEM, VMEM],
+        in_specs=[SMEM, VMEM],
         out_specs=VMEM,
         scratch_shapes=[pltpu.VMEM((2 * reach + order + tile_rows + SUBLANES, width), jnp.float32)],
         compiler_params=pltpu.CompilerParams(vmem_limit_bytes=8 * 2**20),
         cost_estimate=pl.CostEstimate(flops=0, bytes_accessed=3 * 2**20, transcendentals=0),
         name="pack",
-    )(dealing, rows, term)
-
-
-def place_kernel(order, dealing, cols, blocks, owners, terms, empty, out, totals, sems):
+    )(starts, term)
+
+
+def place_kernel(order, info, terms, empty, out, totals, sems):
     del empty
     slots, tile_rows = terms.shape[0], terms.shape[1]
     count = (order + LANES) // LANES
@@ -341,14 +342,14 @@
 
     @pl.loop(0, slots, unroll=4)
     def _(slot):
-        _, offset = window_start(cols[dealing[slot]], order, out.shape[2])
+        offset = info[2 * slots * count + slot]
         shift = lax.rem(offset, LANES)
         for part in range(2):
             turned = []
             for b in range(count - 1):
                 first = part * order + b * LANES
                 turned.append(pltpu.roll(terms[slot, :, first : first + LANES], shift, 1).astype(jnp.float32))
-            holders = [owners[slot * count + b] for b in range(count)]
+            holders = [info[slots * count + slot * count + b] for b in range(count)]
             held = [totals[holder, part] for holder in holders]
             for b in range(count):
                 before = turned[b - 1] if b else nothing
@@ -358,39 +359,39 @@
                 totals[holders[b], part] = jnp.where(first_one, term, held[b] + term)
 
     def copy(number):
-        place = pl.multiple_of(blocks[number] * LANES, LANES)
+        place = pl.multiple_of(info[number] * LANES, LANES)
         return pltpu.make_async_copy(totals.at[number], out.at[:, :, pl.ds(place, LANES)], sems.at[number])
 
     @pl.loop(0, slots * count)
     def _(number):
-        @pl.when(owners[number] == number)
+        @pl.when(info[slots * count + number] == number)
         def _():
             copy(number).start()
 
     @pl.loop(0, slots * count)
     def _(number):
-        @pl.when(owners[number] == number)
+        @pl.when(info[slots * count + number] == number)
         def _():
             copy(number).wait()
 
 
-def place_windows(terms, empty, blocks, owners, dealing, cols, order):
+def place_windows(terms, empty, info, order):
     slots, tile_rows = terms.shape[0], terms.shape[1]
     count = (order + LANES) // LANES
     return pl.pallas_call(
         functools.partial(place_kernel, order),
         out_shape=jax.ShapeDtypeStruct(empty.shape, empty.dtype),
-        in_specs=[SMEM, SMEM, SMEM, SMEM, VMEM, ANY],
+        in_specs=[SMEM, VMEM, ANY],
         out_specs=ANY,
         scratch_shapes=[
             pltpu.VMEM((slots * count, 2, tile_rows, LANES), jnp.float32),
             pltpu.SemaphoreType.DMA((slots * count,)),
         ],
-        input_output_aliases={5: 0},
+        input_output_aliases={2: 0},
         compiler_params=pltpu.CompilerParams(vmem_limit_bytes=12 * 2**20),
         cost_estimate=pl.CostEstimate(flops=0, bytes_accessed=6 * 2**20, transcendentals=0),
         name="place",
-    )(dealing, cols, blocks, owners, terms, empty)
+    )(info, terms, empty)
 
 
 def strides(devices):
@@ -455,18 +456,18 @@
     pieces, token = fetch_windows(object_field, dealing, col_offsets, order)
     strips = lax.all_to_all(pieces, "row", split_axis=0, concat_axis=0, tiled=True)
     cells = strips[:, :own_rows].reshape(total_rows, 2 * order)
-    empty, blocks, owners, stock = prepare(
-        dealing, col_offsets, token, probe, amplitude, object_field.shape
+    empty, starts, info, stock = prepare(
+        dealing, row_offsets, col_offsets, token, probe, amplitude, object_field.shape
     )
-    term, kept, sent = slot_terms(cells, stock, dealing, row_offsets, owners, order)
+    term, kept, sent = slot_terms(cells, stock, starts, order)
     total = sum_probe(kept, sent, devices)
-    terms = pack_rows(term, dealing, row_offsets, devices, own_rows, tile_rows)
+    terms = pack_rows(term, starts, devices, own_rows, tile_rows)
     terms, total = lax.optimization_barrier((terms, total))
     arrived = lax.all_to_all(terms, "row", split_axis=0, concat_axis=0, tiled=True)
     share = (total * (1.0 / dealing.shape[0])).astype(jnp.bfloat16)
     whole = join(share, devices).astype(jnp.float32)
     probe_grad = jnp.stack([whole[:, :order], whole[:, order:]])
-    object_grad = place_windows(arrived, empty, blocks, owners, dealing, col_offsets, order)
+    object_grad = place_windows(arrived, empty, info, order)
     if spare:
         object_grad = object_grad[:, :own_rows]
     return (object_grad, probe_grad)

time: 113 us -> 113 us (level)
  no operation moved by 1% of the time
where the time goes in v22:
time: 113 us
  waiting for transfers between devices  58.9 us (52%)
  Pallas kernels  24.9 us (22%)
  starting transfers between devices  24.6 us (22%)
  other arithmetic  2.4 us (2%)
  local copies, waits for them, and re-layouts  1.26 us (1%)
    ppermute x10, waiting for transfers between devices, swap(): return lax.ppermute(x, 'row', [(d, d ^ distance) for d in range(devices)])  26 us
    all_to_all x1, waiting for transfers between devices, body(): lax.all_to_all(pieces, 'row', split_axis=0, concat_axis=0, tiled=True)  22.8 us
    ppermute x10, starting transfers between devices, swap(): return lax.ppermute(x, 'row', [(d, d ^ distance) for d in range(devices)])  10.4 us
    all_to_all x1, waiting for transfers between devices, body(): lax.all_to_all(terms, 'row', split_axis=0, concat_axis=0, tiled=True)  10.1 us
    all_to_all x1, starting transfers between devices, body(): lax.all_to_all(terms, 'row', split_axis=0, concat_axis=0, tiled=True)  7.48 us
    pallas_call x1, Pallas kernels, slot_terms(): pl.pallas_call(slot_kernel, out_shape=(jax.ShapeDtypeStruct((order, wide_...  7.46 us
    pallas_call x1, Pallas kernels, prepare(): pl.pallas_call(functools.partial(prepare_kernel, order), out_shape=(jax.S...  6.7 us
    all_to_all x1, starting transfers between devices, body(): lax.all_to_all(pieces, 'row', split_axis=0, concat_axis=0, tiled=True)  6.7 us
  transfers between devices with their start and end apart: 12, of which 8 were waited for; matrix products, arithmetic and copies ran while one was open for 2% of the time, Pallas kernels for 8%

profile of v22, /device:TPU:15, one launch (start us, length us, event | category | flops | bytes accessed | tf_op | source)
XLA Modules:
  0.0 112.9 jit_solution(12087314142060576713)
XLA Ops:
  0.6 4.7 %fetch.1 = (bf16[16,40,1024]{2,1,0:T(8,128)(2,1)}, s32[1]{0:T(128)}) custom-call(s32[16]{0:T(128)} %dealing.3, s32[16]{0:T(128)} %cols.3, f32[2,40,32768]{2,1,0:T(8,128)} %tile.1), custom_call_target="tpu_custom_call" | custom-call | bytes 6291456 | tf_op jit(solution)/shard_map/fetch/pallas_call | solution.py:81
  5.3 0.0 copy-start
  5.3 0.0 copy-start.1
  5.3 0.0 copy-start.3
  5.3 0.0 copy-start.4
  5.4 0.0 copy-start.5
  5.4 6.7 %all-to-all-start = ((bf16[16,40,1024]{2,1,0:T(8,128)(2,1)}), bf16[16,40,1024]{2,1,0:T(8,128)(2,1)S(1)}, u32[]{:S(2)}, u32[]{:S(2)}) async-start(bf16[16,40,1024]{2,1,0:T(8,128)(2,1)} %get-tuple-element.16), calls=%async_computation | async-start | bytes 2621440 | tf_op jit(solution)/shard_map/all_to_all | solution.py:457
  12.1 0.0 copy-done
  12.1 0.0 copy-done.1
  12.1 0.0 copy-done.3
  12.1 0.0 copy-done.4
  12.1 0.0 copy-done.5
  12.1 0.0 copy-start.2
  12.1 1.0 copy-done.2
  13.2 6.7 %prepare.1 = (f32[2,40,32768]{2,1,0:T(8,128)}, s32[16]{0:T(128)S(1)}, s32[176]{0:T(256)S(1)}, bf16[24576,1024]{1,0:T(8,128)(2,1)}) custom-call(s32[16]{0:T(128)S(1)} %copy-done.3, s32[16]{0:T(128)S(1)} %copy-done.5, s32[16]{0:T(128)S(1)} %copy-done.4, s32[1]{0:T(128)} %get-tuple-element.13.token, bf16[512,1024]{1,0:T(8,128)(2,1)S(1)} %copy-done.1, ...), custom_call_target="tpu_custom_call" | custom-call | bytes 115343360 | tf_op jit(solution)/shard_map/prepare/pallas_call | solution.py:158
  19.9 22.8 %all-to-all-done = bf16[16,40,1024]{2,1,0:T(8,128)(2,1)S(1)} async-done(((bf16[16,40,1024]{2,1,0:T(8,128)(2,1)}), bf16[16,40,1024]{2,1,0:T(8,128)(2,1)S(1)}, u32[]{:S(2)}, u32[]{:S(2)}) %all-to-all-start) | async-done | bytes 1310752 | tf_op jit(solution)/shard_map/all_to_all | solution.py:457
  42.6 7.5 %slot.1 = (bf16[512,1024]{1,0:T(8,128)(2,1)S(1)}, f32[256,1024]{1,0:T(8,128)S(1)}, bf16[256,1024]{1,0:T(8,128)(2,1)}) custom-call(s32[16]{0:T(128)S(1)} %get-tuple-element.15.starts, bf16[640,1024]{1,0:T(8,128)(2,1)S(1)} %bitcast.5, bf16[24576,1024]{1,0:T(8,128)(2,1)} %get-tuple-element.17.stock), custom_call_target="tpu_custom_call" | custom-call | flops 4294967296 | bytes 8388608 | tf_op jit(solution)/shard_map/slot/pallas_call | solution.py:276
  50.1 0.3 collective-permute-start
  50.4 1.9 %collective-permute-done = bf16[256,1024]{1,0:T(8,128)(2,1)S(1)} collective-permute-done((bf16[256,1024]{1,0:T(8,128)(2,1)}, bf16[256,1024]{1,0:T(8,128)(2,1)S(1)}, u32[]{:S(2)}, u32[]{:S(2)}) %collective-permute-start) | collective-permute-done | bytes 524320 | tf_op jit(solution)/shard_map/ppermute | solution.py:407
  52.3 0.1 add_convert_fusion
  52.4 0.1 collective-permute-start.1
  52.5 7.6 %collective-permute-done.1 = bf16[128,1024]{1,0:T(8,128)(2,1)S(1)} collective-permute-done((bf16[128,1024]{1,0:T(8,128)(2,1)S(1)}, bf16[128,1024]{1,0:T(8,128)(2,1)S(1)}, u32[]{:S(2)}, u32[]{:S(2)}) %collective-permute-start.1) | collective-permute-done | bytes 262176 | tf_op jit(solution)/shard_map/ppermute | solution.py:407
  60.2 0.4 collective-permute-start.4
  60.7 0.8 collective-permute-start.3
  61.5 1.5 %collective-permute-start.2 = (bf16[32,1024]{1,0:T(8,128)(2,1)S(1)}, bf16[32,1024]{1,0:T(8,128)(2,1)S(1)}, u32[]{:S(2)}, u32[]{:S(2)}) collective-permute-start(bf16[32,1024]{1,0:T(8,128)(2,1)S(1)} %get-tuple-element.30), channel_id=1, source_target_pairs={{0,4},{1,5},{2,6},{3,7},{4,0},{5,1},{6,2},{7,3},{8,12},{9,13},{10,... | collective-permute-start | bytes 196616 | tf_op jit(solution)/shard_map/ppermute | solution.py:407
  62.9 2.2 %pack.1 = bf16[16,40,1024]{2,1,0:T(8,128)(2,1)} custom-call(s32[16]{0:T(128)S(1)} %get-tuple-element.15.starts, bf16[512,1024]{1,0:T(8,128)(2,1)S(1)} %get-tuple-element.18.term), custom_call_target="tpu_custom_call" | custom-call | bytes 3145728 | tf_op jit(solution)/shard_map/pack/pallas_call | solution.py:324
  65.1 0.4 collective-permute-done.4
  65.5 0.0 collective-permute-done.3
  65.5 1.1 collective-permute-done.2
  66.6 0.9 collective-permute-start.5
  67.6 3.4 %collective-permute-start.6 = (bf16[32,1024]{1,0:T(8,128)(2,1)S(1)}, bf16[32,1024]{1,0:T(8,128)(2,1)S(1)}, u32[]{:S(2)}, u32[]{:S(2)}) collective-permute-start(bf16[32,1024]{1,0:T(8,128)(2,1)S(1)} %multiply_convert_fusion), channel_id=1, source_target_pairs={{0,8},{1,9},{2,10},{3,11},{4,12},{5,13},{6,14},{7,15},{8,0},{9,1},... | collective-permute-start | bytes 196616 | tf_op jit(solution)/shard_map/ppermute | solution.py:407
  71.0 0.0 collective-permute-start.7
  71.0 7.5 %all-to-all-start.1 = ((bf16[16,40,1024]{2,1,0:T(8,128)(2,1)}), bf16[16,40,1024]{2,1,0:T(8,128)(2,1)S(1)}, u32[]{:S(2)}, u32[]{:S(2)}) async-start(bf16[16,40,1024]{2,1,0:T(8,128)(2,1)} %pack.1), calls=%async_computation.1 | async-start | bytes 2621440 | tf_op jit(solution)/shard_map/all_to_all | solution.py:466
  78.5 0.0 collective-permute-done.5
  78.5 0.0 collective-permute-done.6
  78.5 0.0 collective-permute-done.7
  78.6 0.3 collective-permute-start.8
  78.9 13.5 %collective-permute-done.8 = bf16[128,1024]{1,0:T(8,128)(2,1)S(1)} collective-permute-done((bf16[128,1024]{1,0:T(8,128)(2,1)S(1)}, bf16[128,1024]{1,0:T(8,128)(2,1)S(1)}, u32[]{:S(2)}, u32[]{:S(2)}) %collective-permute-start.8) | collective-permute-done | bytes 262176 | tf_op jit(solution)/shard_map/ppermute | solution.py:407
  92.5 0.1 broadcast_select_fusion.3
  92.6 2.6 %collective-permute-start.9 = (bf16[256,1024]{1,0:T(8,128)(2,1)S(1)}, bf16[256,1024]{1,0:T(8,128)(2,1)S(1)}, u32[]{:S(2)}, u32[]{:S(2)}) collective-permute-start(bf16[256,1024]{1,0:T(8,128)(2,1)S(1)} %pad_maximum_fusion.1), channel_id=1, source_target_pairs={{0,1},{1,0},{2,3},{3,2},{4,5},{5,4},{6,7},{7,6},{8,9},{9,8},{10,11... | collective-permute-start | bytes 1572872 | tf_op jit(solution)/shard_map/ppermute | solution.py:407
  95.2 1.5 %collective-permute-done.9 = bf16[256,1024]{1,0:T(8,128)(2,1)S(1)} collective-permute-done((bf16[256,1024]{1,0:T(8,128)(2,1)S(1)}, bf16[256,1024]{1,0:T(8,128)(2,1)S(1)}, u32[]{:S(2)}, u32[]{:S(2)}) %collective-permute-start.9) | collective-permute-done | bytes 524320 | tf_op jit(solution)/shard_map/ppermute | solution.py:407
  96.8 0.2 broadcast_select_fusion.1
  97.0 0.2 maximum_convert_fusion
  97.3 0.2 slice_bitcast_fusion.1
  97.5 1.5 %pad_maximum_fusion = f32[2,512,512]{2,1,0:T(8,128)} fusion(f32[1,512,512]{2,1,0:T(8,128)S(1)} %get-tuple-element.25, f32[1,512,512]{2,1,0:T(8,128)S(1)} %get-tuple-element.24), kind=kLoop, calls=%fused_computation | loop fusion | flops 524288 | bytes 4194304 | tf_op jit(solution)/shard_map/stack | solution.py:469
  99.0 10.1 %all-to-all-done.1.terms = bf16[16,40,1024]{2,1,0:T(8,128)(2,1)S(1)} async-done(((bf16[16,40,1024]{2,1,0:T(8,128)(2,1)}), bf16[16,40,1024]{2,1,0:T(8,128)(2,1)S(1)}, u32[]{:S(2)}, u32[]{:S(2)}) %all-to-all-start.1) | async-done | bytes 1310752 | tf_op jit(solution)/shard_map/all_to_all | solution.py:466
  109.0 3.8 %place.1 = f32[2,40,32768]{2,1,0:T(8,128)} custom-call(s32[176]{0:T(256)S(1)} %get-tuple-element.14.info, bf16[16,40,1024]{2,1,0:T(8,128)(2,1)S(1)} %all-to-all-done.1.terms, f32[2,40,32768]{2,1,0:T(8,128)} %get-tuple-element.22.empty), custom_call_target="tpu_custom_call", output_to_operand_aliasing={{}: (2, {})} | custom-call | bytes 6291456 | tf_op jit(solution)/shard_map/place/pallas_call | solution.py:381
  (6 shorter events, 0.2 us)
Async XLA Ops:
  5.3 6.8 %copy-start = (bf16[2,512,512]{2,1,0:T(8,128)(2,1)S(1)}, bf16[2,512,512]{2,1,0:T(8,128)(2,1)}, u32[]{:S(2)}) copy-start(bf16[2,512,512]{2,1,0:T(8,128)(2,1)} %probe.1) | copy-start | bytes 3145732
  5.3 6.8 %copy-start.1 = (bf16[512,1024]{1,0:T(8,128)(2,1)S(1)}, bf16[512,1024]{1,0:T(8,128)(2,1)}, u32[]{:S(2)}) copy-start(bf16[512,1024]{1,0:T(8,128)(2,1)} %constant.79.clone.table_in) | copy-start | bytes 3145732
  5.3 6.8 %copy-start.3 = (s32[16]{0:T(128)S(1)}, s32[16]{0:T(128)}, u32[]{:S(2)}) copy-start(s32[16]{0:T(128)} %dealing.3) | copy-start | bytes 196
  5.3 6.8 %copy-start.4 = (s32[16]{0:T(128)S(1)}, s32[16]{0:T(128)}, u32[]{:S(2)}) copy-start(s32[16]{0:T(128)} %cols.3) | copy-start | bytes 196
  5.4 6.7 %copy-start.5 = (s32[16]{0:T(128)S(1)}, s32[16]{0:T(128)}, u32[]{:S(2)}) copy-start(s32[16]{0:T(128)} %rows.1) | copy-start | bytes 196
  5.4 37.3 %all-to-all-start = ((bf16[16,40,1024]{2,1,0:T(8,128)(2,1)}), bf16[16,40,1024]{2,1,0:T(8,128)(2,1)S(1)}, u32[]{:S(2)}, u32[]{:S(2)}) async-start(bf16[16,40,1024]{2,1,0:T(8,128)(2,1)} %get-tuple-element.16), calls=%async_computation | async-start | bytes 2621440 | tf_op jit(solution)/shard_map/all_to_all | solution.py:457
  12.1 1.0 copy-start.2
  50.1 2.2 %collective-permute-start = (bf16[256,1024]{1,0:T(8,128)(2,1)}, bf16[256,1024]{1,0:T(8,128)(2,1)S(1)}, u32[]{:S(2)}, u32[]{:S(2)}) collective-permute-start(bf16[256,1024]{1,0:T(8,128)(2,1)} %get-tuple-element.20), channel_id=1, source_target_pairs={{0,1},{1,0},{2,3},{3,2},{4,5},{5,4},{6,7},{7,6},{8,9},{9,8},{10,11... | collective-permute-start | bytes 1572872 | tf_op jit(solution)/shard_map/ppermute | solution.py:407
  52.4 7.8 %collective-permute-start.1 = (bf16[128,1024]{1,0:T(8,128)(2,1)S(1)}, bf16[128,1024]{1,0:T(8,128)(2,1)S(1)}, u32[]{:S(2)}, u32[]{:S(2)}) collective-permute-start(bf16[128,1024]{1,0:T(8,128)(2,1)S(1)} %get-tuple-element.26), channel_id=1, source_target_pairs={{0,2},{1,3},{2,0},{3,1},{4,6},{5,7},{6,4},{7,5},{8,10},{9,11},{10,... | collective-permute-start | bytes 786440 | tf_op jit(solution)/shard_map/ppermute | solution.py:407
  60.2 5.3 %collective-permute-start.4 = (bf16[32,1024]{1,0:T(8,128)(2,1)S(1)}, bf16[32,1024]{1,0:T(8,128)(2,1)S(1)}, u32[]{:S(2)}, u32[]{:S(2)}) collective-permute-start(bf16[32,1024]{1,0:T(8,128)(2,1)S(1)} %get-tuple-element.31), channel_id=1, source_target_pairs={{0,12},{1,13},{2,14},{3,15},{4,8},{5,9},{6,10},{7,11},{8,4},{9,5},... | collective-permute-start | bytes 196616 | tf_op jit(solution)/shard_map/ppermute | solution.py:407
  60.7 4.8 %collective-permute-start.3 = (bf16[32,1024]{1,0:T(8,128)(2,1)S(1)}, bf16[32,1024]{1,0:T(8,128)(2,1)S(1)}, u32[]{:S(2)}, u32[]{:S(2)}) collective-permute-start(bf16[32,1024]{1,0:T(8,128)(2,1)S(1)} %get-tuple-element.32), channel_id=1, source_target_pairs={{0,8},{1,9},{2,10},{3,11},{4,12},{5,13},{6,14},{7,15},{8,0},{9,1},... | collective-permute-start | bytes 196616 | tf_op jit(solution)/shard_map/ppermute | solution.py:407
  61.5 5.1 %collective-permute-start.2 = (bf16[32,1024]{1,0:T(8,128)(2,1)S(1)}, bf16[32,1024]{1,0:T(8,128)(2,1)S(1)}, u32[]{:S(2)}, u32[]{:S(2)}) collective-permute-start(bf16[32,1024]{1,0:T(8,128)(2,1)S(1)} %get-tuple-element.30), channel_id=1, source_target_pairs={{0,4},{1,5},{2,6},{3,7},{4,0},{5,1},{6,2},{7,3},{8,12},{9,13},{10,... | collective-permute-start | bytes 196616 | tf_op jit(solution)/shard_map/ppermute | solution.py:407
  66.6 11.8 %collective-permute-start.5 = (bf16[32,1024]{1,0:T(8,128)(2,1)S(1)}, bf16[32,1024]{1,0:T(8,128)(2,1)S(1)}, u32[]{:S(2)}, u32[]{:S(2)}) collective-permute-start(bf16[32,1024]{1,0:T(8,128)(2,1)S(1)} %multiply_convert_fusion), channel_id=1, source_target_pairs={{0,12},{1,13},{2,14},{3,15},{4,8},{5,9},{6,10},{7,11},{8,4},{9,5},... | collective-permute-start | bytes 196616 | tf_op jit(solution)/shard_map/ppermute | solution.py:407
  67.6 10.9 %collective-permute-start.6 = (bf16[32,1024]{1,0:T(8,128)(2,1)S(1)}, bf16[32,1024]{1,0:T(8,128)(2,1)S(1)}, u32[]{:S(2)}, u32[]{:S(2)}) collective-permute-start(bf16[32,1024]{1,0:T(8,128)(2,1)S(1)} %multiply_convert_fusion), channel_id=1, source_target_pairs={{0,8},{1,9},{2,10},{3,11},{4,12},{5,13},{6,14},{7,15},{8,0},{9,1},... | collective-permute-start | bytes 196616 | tf_op jit(solution)/shard_map/ppermute | solution.py:407
  71.0 7.5 %collective-permute-start.7 = (bf16[32,1024]{1,0:T(8,128)(2,1)S(1)}, bf16[32,1024]{1,0:T(8,128)(2,1)S(1)}, u32[]{:S(2)}, u32[]{:S(2)}) collective-permute-start(bf16[32,1024]{1,0:T(8,128)(2,1)S(1)} %multiply_convert_fusion), channel_id=1, source_target_pairs={{0,4},{1,5},{2,6},{3,7},{4,0},{5,1},{6,2},{7,3},{8,12},{9,13},{10,... | collective-permute-start | bytes 196616 | tf_op jit(solution)/shard_map/ppermute | solution.py:407
  71.0 38.0 %all-to-all-start.1 = ((bf16[16,40,1024]{2,1,0:T(8,128)(2,1)}), bf16[16,40,1024]{2,1,0:T(8,128)(2,1)S(1)}, u32[]{:S(2)}, u32[]{:S(2)}) async-start(bf16[16,40,1024]{2,1,0:T(8,128)(2,1)} %pack.1), calls=%async_computation.1 | async-start | bytes 2621440 | tf_op jit(solution)/shard_map/all_to_all | solution.py:466
  78.6 13.9 %collective-permute-start.8 = (bf16[128,1024]{1,0:T(8,128)(2,1)S(1)}, bf16[128,1024]{1,0:T(8,128)(2,1)S(1)}, u32[]{:S(2)}, u32[]{:S(2)}) collective-permute-start(bf16[128,1024]{1,0:T(8,128)(2,1)S(1)} %pad_maximum_fusion.2), channel_id=1, source_target_pairs={{0,2},{1,3},{2,0},{3,1},{4,6},{5,7},{6,4},{7,5},{8,10},{9,11},{10,... | collective-permute-start | bytes 786440 | tf_op jit(solution)/shard_map/ppermute | solution.py:407
  92.6 4.2 %collective-permute-start.9 = (bf16[256,1024]{1,0:T(8,128)(2,1)S(1)}, bf16[256,1024]{1,0:T(8,128)(2,1)S(1)}, u32[]{:S(2)}, u32[]{:S(2)}) collective-permute-start(bf16[256,1024]{1,0:T(8,128)(2,1)S(1)} %pad_maximum_fusion.1), channel_id=1, source_target_pairs={{0,1},{1,0},{2,3},{3,2},{4,5},{5,4},{6,7},{7,6},{8,9},{9,8},{10,11... | collective-permute-start | bytes 1572872 | tf_op jit(solution)/shard_map/ppermute | solution.py:407

commit v23 on v22

--- a/solution.py
+++ b/solution.py
@@ -52,13 +52,13 @@
         base, _ = window_start(cols[dealing[slot]], order, tile_cols)
         return pltpu.make_async_copy(tile.at[:, :, pl.ds(base, span)], held.at[slot], sems.at[slot])
 
-    @pl.loop(0, slots)
+    @pl.loop(0, slots, unroll=8)
     def _(slot):
         copy(slot).start()
 
     lane = lax.broadcasted_iota(jnp.int32, (tile_rows, LANES), 1)
 
-    @pl.loop(0, slots, unroll=4)
+    @pl.loop(0, slots, unroll=8)
     def _(slot):
         copy(slot).wait()
         _, offset = window_start(cols[dealing[slot]], order, tile_cols)
@@ -340,7 +340,7 @@
     lane = lax.broadcasted_iota(jnp.int32, (tile_rows, LANES), 1)
     nothing = jnp.zeros((tile_rows, LANES), jnp.float32)
 
-    @pl.loop(0, slots, unroll=4)
+    @pl.loop(0, slots, unroll=8)
     def _(slot):
         offset = info[2 * slots * count + slot]
         shift = lax.rem(offset, LANES)

time: 113 us -> 113 us (level)
  no operation moved by 1% of the time
where the time goes in v23:
time: 113 us
  waiting for transfers between devices  58.9 us (52%)
  Pallas kernels  24.8 us (22%)
  starting transfers between devices  24.6 us (22%)
  other arithmetic  2.4 us (2%)
  local copies, waits for them, and re-layouts  1.26 us (1%)
    ppermute x10, waiting for transfers between devices, swap(): return lax.ppermute(x, 'row', [(d, d ^ distance) for d in range(devices)])  26 us
    all_to_all x1, waiting for transfers between devices, body(): lax.all_to_all(pieces, 'row', split_axis=0, concat_axis=0, tiled=True)  22.8 us
    ppermute x10, starting transfers between devices, swap(): return lax.ppermute(x, 'row', [(d, d ^ distance) for d in range(devices)])  10.4 us
    all_to_all x1, waiting for transfers between devices, body(): lax.all_to_all(terms, 'row', split_axis=0, concat_axis=0, tiled=True)  10.1 us
    all_to_all x1, starting transfers between devices, body(): lax.all_to_all(terms, 'row', split_axis=0, concat_axis=0, tiled=True)  7.49 us
    pallas_call x1, Pallas kernels, slot_terms(): pl.pallas_call(slot_kernel, out_shape=(jax.ShapeDtypeStruct((order, wide_...  7.46 us
    pallas_call x1, Pallas kernels, prepare(): pl.pallas_call(functools.partial(prepare_kernel, order), out_shape=(jax.S...  6.7 us
    all_to_all x1, starting transfers between devices, body(): lax.all_to_all(pieces, 'row', split_axis=0, concat_axis=0, tiled=True)  6.7 us
  transfers between devices with their start and end apart: 12, of which 8 were waited for; matrix products, arithmetic and copies ran while one was open for 2% of the time, Pallas kernels for 8%

profile of v23, /device:TPU:15, one launch (start us, length us, event | category | flops | bytes accessed | tf_op | source)
XLA Modules:
  0.0 112.8 jit_solution(1490434052980933230)
XLA Ops:
  0.6 4.7 %fetch.1 = (bf16[16,40,1024]{2,1,0:T(8,128)(2,1)}, s32[1]{0:T(128)}) custom-call(s32[16]{0:T(128)} %dealing.3, s32[16]{0:T(128)} %cols.3, f32[2,40,32768]{2,1,0:T(8,128)} %tile.1), custom_call_target="tpu_custom_call" | custom-call | bytes 6291456 | tf_op jit(solution)/shard_map/fetch/pallas_call | solution.py:81
  5.3 0.0 copy-start
  5.3 0.0 copy-start.1
  5.3 0.0 copy-start.3
  5.3 0.0 copy-start.4
  5.4 0.0 copy-start.5
  5.4 6.7 %all-to-all-start = ((bf16[16,40,1024]{2,1,0:T(8,128)(2,1)}), bf16[16,40,1024]{2,1,0:T(8,128)(2,1)S(1)}, u32[]{:S(2)}, u32[]{:S(2)}) async-start(bf16[16,40,1024]{2,1,0:T(8,128)(2,1)} %get-tuple-element.16), calls=%async_computation | async-start | bytes 2621440 | tf_op jit(solution)/shard_map/all_to_all | solution.py:457
  12.1 0.0 copy-done
  12.1 0.0 copy-done.1
  12.1 0.0 copy-done.3
  12.1 0.0 copy-done.4
  12.1 0.0 copy-done.5
  12.1 0.0 copy-start.2
  12.1 1.0 copy-done.2
  13.2 6.7 %prepare.1 = (f32[2,40,32768]{2,1,0:T(8,128)}, s32[16]{0:T(128)S(1)}, s32[176]{0:T(256)S(1)}, bf16[24576,1024]{1,0:T(8,128)(2,1)}) custom-call(s32[16]{0:T(128)S(1)} %copy-done.3, s32[16]{0:T(128)S(1)} %copy-done.5, s32[16]{0:T(128)S(1)} %copy-done.4, s32[1]{0:T(128)} %get-tuple-element.13.token, bf16[512,1024]{1,0:T(8,128)(2,1)S(1)} %copy-done.1, ...), custom_call_target="tpu_custom_call" | custom-call | bytes 115343360 | tf_op jit(solution)/shard_map/prepare/pallas_call | solution.py:158
  19.9 22.8 %all-to-all-done = bf16[16,40,1024]{2,1,0:T(8,128)(2,1)S(1)} async-done(((bf16[16,40,1024]{2,1,0:T(8,128)(2,1)}), bf16[16,40,1024]{2,1,0:T(8,128)(2,1)S(1)}, u32[]{:S(2)}, u32[]{:S(2)}) %all-to-all-start) | async-done | bytes 1310752 | tf_op jit(solution)/shard_map/all_to_all | solution.py:457
  42.6 7.5 %slot.1 = (bf16[512,1024]{1,0:T(8,128)(2,1)S(1)}, f32[256,1024]{1,0:T(8,128)S(1)}, bf16[256,1024]{1,0:T(8,128)(2,1)}) custom-call(s32[16]{0:T(128)S(1)} %get-tuple-element.15.starts, bf16[640,1024]{1,0:T(8,128)(2,1)S(1)} %bitcast.5, bf16[24576,1024]{1,0:T(8,128)(2,1)} %get-tuple-element.17.stock), custom_call_target="tpu_custom_call" | custom-call | flops 4294967296 | bytes 8388608 | tf_op jit(solution)/shard_map/slot/pallas_call | solution.py:276
  50.1 0.3 collective-permute-start
  50.4 1.9 %collective-permute-done = bf16[256,1024]{1,0:T(8,128)(2,1)S(1)} collective-permute-done((bf16[256,1024]{1,0:T(8,128)(2,1)}, bf16[256,1024]{1,0:T(8,128)(2,1)S(1)}, u32[]{:S(2)}, u32[]{:S(2)}) %collective-permute-start) | collective-permute-done | bytes 524320 | tf_op jit(solution)/shard_map/ppermute | solution.py:407
  52.3 0.1 add_convert_fusion
  52.4 0.1 collective-permute-start.1
  52.6 7.6 %collective-permute-done.1 = bf16[128,1024]{1,0:T(8,128)(2,1)S(1)} collective-permute-done((bf16[128,1024]{1,0:T(8,128)(2,1)S(1)}, bf16[128,1024]{1,0:T(8,128)(2,1)S(1)}, u32[]{:S(2)}, u32[]{:S(2)}) %collective-permute-start.1) | collective-permute-done | bytes 262176 | tf_op jit(solution)/shard_map/ppermute | solution.py:407
  60.2 0.4 collective-permute-start.4
  60.7 0.8 collective-permute-start.3
  61.5 1.5 %collective-permute-start.2 = (bf16[32,1024]{1,0:T(8,128)(2,1)S(1)}, bf16[32,1024]{1,0:T(8,128)(2,1)S(1)}, u32[]{:S(2)}, u32[]{:S(2)}) collective-permute-start(bf16[32,1024]{1,0:T(8,128)(2,1)S(1)} %get-tuple-element.30), channel_id=1, source_target_pairs={{0,4},{1,5},{2,6},{3,7},{4,0},{5,1},{6,2},{7,3},{8,12},{9,13},{10,... | collective-permute-start | bytes 196616 | tf_op jit(solution)/shard_map/ppermute | solution.py:407
  63.0 2.2 %pack.1 = bf16[16,40,1024]{2,1,0:T(8,128)(2,1)} custom-call(s32[16]{0:T(128)S(1)} %get-tuple-element.15.starts, bf16[512,1024]{1,0:T(8,128)(2,1)S(1)} %get-tuple-element.18.term), custom_call_target="tpu_custom_call" | custom-call | bytes 3145728 | tf_op jit(solution)/shard_map/pack/pallas_call | solution.py:324
  65.1 0.3 collective-permute-done.4
  65.5 0.0 collective-permute-done.3
  65.5 1.1 collective-permute-done.2
  66.6 0.9 collective-permute-start.5
  67.6 3.4 %collective-permute-start.6 = (bf16[32,1024]{1,0:T(8,128)(2,1)S(1)}, bf16[32,1024]{1,0:T(8,128)(2,1)S(1)}, u32[]{:S(2)}, u32[]{:S(2)}) collective-permute-start(bf16[32,1024]{1,0:T(8,128)(2,1)S(1)} %multiply_convert_fusion), channel_id=1, source_target_pairs={{0,8},{1,9},{2,10},{3,11},{4,12},{5,13},{6,14},{7,15},{8,0},{9,1},... | collective-permute-start | bytes 196616 | tf_op jit(solution)/shard_map/ppermute | solution.py:407
  71.0 0.0 collective-permute-start.7
  71.0 7.5 %all-to-all-start.1 = ((bf16[16,40,1024]{2,1,0:T(8,128)(2,1)}), bf16[16,40,1024]{2,1,0:T(8,128)(2,1)S(1)}, u32[]{:S(2)}, u32[]{:S(2)}) async-start(bf16[16,40,1024]{2,1,0:T(8,128)(2,1)} %pack.1), calls=%async_computation.1 | async-start | bytes 2621440 | tf_op jit(solution)/shard_map/all_to_all | solution.py:466
  78.5 0.0 collective-permute-done.5
  78.5 0.0 collective-permute-done.6
  78.5 0.0 collective-permute-done.7
  78.6 0.3 collective-permute-start.8
  78.9 13.5 %collective-permute-done.8 = bf16[128,1024]{1,0:T(8,128)(2,1)S(1)} collective-permute-done((bf16[128,1024]{1,0:T(8,128)(2,1)S(1)}, bf16[128,1024]{1,0:T(8,128)(2,1)S(1)}, u32[]{:S(2)}, u32[]{:S(2)}) %collective-permute-start.8) | collective-permute-done | bytes 262176 | tf_op jit(solution)/shard_map/ppermute | solution.py:407
  92.4 0.1 broadcast_select_fusion.3
  92.6 2.6 %collective-permute-start.9 = (bf16[256,1024]{1,0:T(8,128)(2,1)S(1)}, bf16[256,1024]{1,0:T(8,128)(2,1)S(1)}, u32[]{:S(2)}, u32[]{:S(2)}) collective-permute-start(bf16[256,1024]{1,0:T(8,128)(2,1)S(1)} %pad_maximum_fusion.1), channel_id=1, source_target_pairs={{0,1},{1,0},{2,3},{3,2},{4,5},{5,4},{6,7},{7,6},{8,9},{9,8},{10,11... | collective-permute-start | bytes 1572872 | tf_op jit(solution)/shard_map/ppermute | solution.py:407
  95.2 1.5 %collective-permute-done.9 = bf16[256,1024]{1,0:T(8,128)(2,1)S(1)} collective-permute-done((bf16[256,1024]{1,0:T(8,128)(2,1)S(1)}, bf16[256,1024]{1,0:T(8,128)(2,1)S(1)}, u32[]{:S(2)}, u32[]{:S(2)}) %collective-permute-start.9) | collective-permute-done | bytes 524320 | tf_op jit(solution)/shard_map/ppermute | solution.py:407
  96.8 0.2 broadcast_select_fusion.1
  97.0 0.2 maximum_convert_fusion
  97.3 0.2 slice_bitcast_fusion.1
  97.5 1.5 %pad_maximum_fusion = f32[2,512,512]{2,1,0:T(8,128)} fusion(f32[1,512,512]{2,1,0:T(8,128)S(1)} %get-tuple-element.25, f32[1,512,512]{2,1,0:T(8,128)S(1)} %get-tuple-element.24), kind=kLoop, calls=%fused_computation | loop fusion | flops 524288 | bytes 4194304 | tf_op jit(solution)/shard_map/stack | solution.py:469
  98.9 10.1 %all-to-all-done.1.terms = bf16[16,40,1024]{2,1,0:T(8,128)(2,1)S(1)} async-done(((bf16[16,40,1024]{2,1,0:T(8,128)(2,1)}), bf16[16,40,1024]{2,1,0:T(8,128)(2,1)S(1)}, u32[]{:S(2)}, u32[]{:S(2)}) %all-to-all-start.1) | async-done | bytes 1310752 | tf_op jit(solution)/shard_map/all_to_all | solution.py:466
  109.0 3.7 %place.1 = f32[2,40,32768]{2,1,0:T(8,128)} custom-call(s32[176]{0:T(256)S(1)} %get-tuple-element.14.info, bf16[16,40,1024]{2,1,0:T(8,128)(2,1)S(1)} %all-to-all-done.1.terms, f32[2,40,32768]{2,1,0:T(8,128)} %get-tuple-element.22.empty), custom_call_target="tpu_custom_call", output_to_operand_aliasing={{}: (2, {})} | custom-call | bytes 6291456 | tf_op jit(solution)/shard_map/place/pallas_call | solution.py:381
  (6 shorter events, 0.2 us)
Async XLA Ops:
  5.3 6.8 %copy-start = (bf16[2,512,512]{2,1,0:T(8,128)(2,1)S(1)}, bf16[2,512,512]{2,1,0:T(8,128)(2,1)}, u32[]{:S(2)}) copy-start(bf16[2,512,512]{2,1,0:T(8,128)(2,1)} %probe.1) | copy-start | bytes 3145732
  5.3 6.8 %copy-start.1 = (bf16[512,1024]{1,0:T(8,128)(2,1)S(1)}, bf16[512,1024]{1,0:T(8,128)(2,1)}, u32[]{:S(2)}) copy-start(bf16[512,1024]{1,0:T(8,128)(2,1)} %constant.79.clone.table_in) | copy-start | bytes 3145732
  5.3 6.8 %copy-start.3 = (s32[16]{0:T(128)S(1)}, s32[16]{0:T(128)}, u32[]{:S(2)}) copy-start(s32[16]{0:T(128)} %dealing.3) | copy-start | bytes 196
  5.3 6.8 %copy-start.4 = (s32[16]{0:T(128)S(1)}, s32[16]{0:T(128)}, u32[]{:S(2)}) copy-start(s32[16]{0:T(128)} %cols.3) | copy-start | bytes 196
  5.4 6.7 %copy-start.5 = (s32[16]{0:T(128)S(1)}, s32[16]{0:T(128)}, u32[]{:S(2)}) copy-start(s32[16]{0:T(128)} %rows.1) | copy-start | bytes 196
  5.4 37.3 %all-to-all-start = ((bf16[16,40,1024]{2,1,0:T(8,128)(2,1)}), bf16[16,40,1024]{2,1,0:T(8,128)(2,1)S(1)}, u32[]{:S(2)}, u32[]{:S(2)}) async-start(bf16[16,40,1024]{2,1,0:T(8,128)(2,1)} %get-tuple-element.16), calls=%async_computation | async-start | bytes 2621440 | tf_op jit(solution)/shard_map/all_to_all | solution.py:457
  12.1 1.0 copy-start.2
  50.1 2.2 %collective-permute-start = (bf16[256,1024]{1,0:T(8,128)(2,1)}, bf16[256,1024]{1,0:T(8,128)(2,1)S(1)}, u32[]{:S(2)}, u32[]{:S(2)}) collective-permute-start(bf16[256,1024]{1,0:T(8,128)(2,1)} %get-tuple-element.20), channel_id=1, source_target_pairs={{0,1},{1,0},{2,3},{3,2},{4,5},{5,4},{6,7},{7,6},{8,9},{9,8},{10,11... | collective-permute-start | bytes 1572872 | tf_op jit(solution)/shard_map/ppermute | solution.py:407
  52.4 7.8 %collective-permute-start.1 = (bf16[128,1024]{1,0:T(8,128)(2,1)S(1)}, bf16[128,1024]{1,0:T(8,128)(2,1)S(1)}, u32[]{:S(2)}, u32[]{:S(2)}) collective-permute-start(bf16[128,1024]{1,0:T(8,128)(2,1)S(1)} %get-tuple-element.26), channel_id=1, source_target_pairs={{0,2},{1,3},{2,0},{3,1},{4,6},{5,7},{6,4},{7,5},{8,10},{9,11},{10,... | collective-permute-start | bytes 786440 | tf_op jit(solution)/shard_map/ppermute | solution.py:407
  60.2 5.2 %collective-permute-start.4 = (bf16[32,1024]{1,0:T(8,128)(2,1)S(1)}, bf16[32,1024]{1,0:T(8,128)(2,1)S(1)}, u32[]{:S(2)}, u32[]{:S(2)}) collective-permute-start(bf16[32,1024]{1,0:T(8,128)(2,1)S(1)} %get-tuple-element.31), channel_id=1, source_target_pairs={{0,12},{1,13},{2,14},{3,15},{4,8},{5,9},{6,10},{7,11},{8,4},{9,5},... | collective-permute-start | bytes 196616 | tf_op jit(solution)/shard_map/ppermute | solution.py:407
  60.7 4.8 %collective-permute-start.3 = (bf16[32,1024]{1,0:T(8,128)(2,1)S(1)}, bf16[32,1024]{1,0:T(8,128)(2,1)S(1)}, u32[]{:S(2)}, u32[]{:S(2)}) collective-permute-start(bf16[32,1024]{1,0:T(8,128)(2,1)S(1)} %get-tuple-element.32), channel_id=1, source_target_pairs={{0,8},{1,9},{2,10},{3,11},{4,12},{5,13},{6,14},{7,15},{8,0},{9,1},... | collective-permute-start | bytes 196616 | tf_op jit(solution)/shard_map/ppermute | solution.py:407
  61.5 5.1 %collective-permute-start.2 = (bf16[32,1024]{1,0:T(8,128)(2,1)S(1)}, bf16[32,1024]{1,0:T(8,128)(2,1)S(1)}, u32[]{:S(2)}, u32[]{:S(2)}) collective-permute-start(bf16[32,1024]{1,0:T(8,128)(2,1)S(1)} %get-tuple-element.30), channel_id=1, source_target_pairs={{0,4},{1,5},{2,6},{3,7},{4,0},{5,1},{6,2},{7,3},{8,12},{9,13},{10,... | collective-permute-start | bytes 196616 | tf_op jit(solution)/shard_map/ppermute | solution.py:407
  66.6 11.8 %collective-permute-start.5 = (bf16[32,1024]{1,0:T(8,128)(2,1)S(1)}, bf16[32,1024]{1,0:T(8,128)(2,1)S(1)}, u32[]{:S(2)}, u32[]{:S(2)}) collective-permute-start(bf16[32,1024]{1,0:T(8,128)(2,1)S(1)} %multiply_convert_fusion), channel_id=1, source_target_pairs={{0,12},{1,13},{2,14},{3,15},{4,8},{5,9},{6,10},{7,11},{8,4},{9,5},... | collective-permute-start | bytes 196616 | tf_op jit(solution)/shard_map/ppermute | solution.py:407
  67.6 10.9 %collective-permute-start.6 = (bf16[32,1024]{1,0:T(8,128)(2,1)S(1)}, bf16[32,1024]{1,0:T(8,128)(2,1)S(1)}, u32[]{:S(2)}, u32[]{:S(2)}) collective-permute-start(bf16[32,1024]{1,0:T(8,128)(2,1)S(1)} %multiply_convert_fusion), channel_id=1, source_target_pairs={{0,8},{1,9},{2,10},{3,11},{4,12},{5,13},{6,14},{7,15},{8,0},{9,1},... | collective-permute-start | bytes 196616 | tf_op jit(solution)/shard_map/ppermute | solution.py:407
  71.0 7.5 %collective-permute-start.7 = (bf16[32,1024]{1,0:T(8,128)(2,1)S(1)}, bf16[32,1024]{1,0:T(8,128)(2,1)S(1)}, u32[]{:S(2)}, u32[]{:S(2)}) collective-permute-start(bf16[32,1024]{1,0:T(8,128)(2,1)S(1)} %multiply_convert_fusion), channel_id=1, source_target_pairs={{0,4},{1,5},{2,6},{3,7},{4,0},{5,1},{6,2},{7,3},{8,12},{9,13},{10,... | collective-permute-start | bytes 196616 | tf_op jit(solution)/shard_map/ppermute | solution.py:407
  71.0 38.1 %all-to-all-start.1 = ((bf16[16,40,1024]{2,1,0:T(8,128)(2,1)}), bf16[16,40,1024]{2,1,0:T(8,128)(2,1)S(1)}, u32[]{:S(2)}, u32[]{:S(2)}) async-start(bf16[16,40,1024]{2,1,0:T(8,128)(2,1)} %pack.1), calls=%async_computation.1 | async-start | bytes 2621440 | tf_op jit(solution)/shard_map/all_to_all | solution.py:466
  78.6 13.9 %collective-permute-start.8 = (bf16[128,1024]{1,0:T(8,128)(2,1)S(1)}, bf16[128,1024]{1,0:T(8,128)(2,1)S(1)}, u32[]{:S(2)}, u32[]{:S(2)}) collective-permute-start(bf16[128,1024]{1,0:T(8,128)(2,1)S(1)} %pad_maximum_fusion.2), channel_id=1, source_target_pairs={{0,2},{1,3},{2,0},{3,1},{4,6},{5,7},{6,4},{7,5},{8,10},{9,11},{10,... | collective-permute-start | bytes 786440 | tf_op jit(solution)/shard_map/ppermute | solution.py:407
  92.6 4.2 %collective-permute-start.9 = (bf16[256,1024]{1,0:T(8,128)(2,1)S(1)}, bf16[256,1024]{1,0:T(8,128)(2,1)S(1)}, u32[]{:S(2)}, u32[]{:S(2)}) collective-permute-start(bf16[256,1024]{1,0:T(8,128)(2,1)S(1)} %pad_maximum_fusion.1), channel_id=1, source_target_pairs={{0,1},{1,0},{2,3},{3,2},{4,5},{5,4},{6,7},{7,6},{8,9},{9,8},{10,11... | collective-permute-start | bytes 1572872 | tf_op jit(solution)/shard_map/ppermute | solution.py:407

commit v24 on v21

--- a/solution.py
+++ b/solution.py
@@ -430,17 +430,20 @@
 
 def join(whole, devices):
     me = lax.axis_index("row")
-    for stride, radix in reversed(strides(devices)):
-        digit = me // stride % radix
-        shares = [whole] + [swap(whole, k * stride, devices) for k in range(1, radix)]
-        pieces = []
-        for j in range(radix):
-            piece = shares[0]
-            for k in range(1, radix):
-                piece = jnp.where(lax.bitwise_xor(digit, k) == j, shares[k], piece)
-            pieces.append(piece)
-        whole = jnp.concatenate(pieces, axis=0)
-    return whole
+    rows, width = whole.shape
+    places = []
+    for stride, radix in strides(devices):
+        places += [2 * stride, stride] if radix == 4 else [stride]
+    far = max(places)
+    order = [far] + places[1:2] + [part for part in places[2:] if part != far] + places[:1]
+    done = []
+    for part in order:
+        met = swap(whole, part, devices)
+        high = me // part % 2 == 1
+        axis = sum(places.index(one) < places.index(part) for one in done)
+        whole = jnp.stack([jnp.where(high, met, whole), jnp.where(high, whole, met)], axis=axis)
+        done.append(part)
+    return whole.reshape(devices * rows, width)
 
 
 def body(object_field, probe, amplitude, row_offsets, col_offsets, dealing):

time: 113 us -> 120 us (1.062)
  the two profiles are of different devices: /device:TPU:15 before, /device:TPU:0 now
where the time goes in v24:
time: 120 us; the launch traced here: 119 us
  waiting for transfers between devices  65.3 us (54%)
  Pallas kernels  24.8 us (21%)
  starting transfers between devices  24.8 us (21%)
  other arithmetic  2.1 us (2%)
  local copies, waits for them, and re-layouts  1.5 us (1%)
    ppermute x9, waiting for transfers between devices, swap(): return lax.ppermute(x, 'row', [(d, d ^ distance) for d in range(devices)])  45.7 us
    all_to_all x1, waiting for transfers between devices, body(): lax.all_to_all(pieces, 'row', split_axis=0, concat_axis=0, tiled=True)  19.6 us
    ppermute x9, starting transfers between devices, swap(): return lax.ppermute(x, 'row', [(d, d ^ distance) for d in range(devices)])  13.5 us
    all_to_all x1, starting transfers between devices, body(): lax.all_to_all(pieces, 'row', split_axis=0, concat_axis=0, tiled=True)  7.53 us
    pallas_call x1, Pallas kernels, slot_terms(): pl.pallas_call(slot_kernel, out_shape=(jax.ShapeDtypeStruct((order, wide_...  7.47 us
    pallas_call x1, Pallas kernels, prepare(): pl.pallas_call(functools.partial(prepare_kernel, order), out_shape=(jax.S...  6.69 us
    pallas_call x1, Pallas kernels, fetch_windows(): pl.pallas_call(functools.partial(fetch_kernel, order), out_shape=(jax.Sha...  4.67 us
    pallas_call x1, Pallas kernels, place_windows(): pl.pallas_call(functools.partial(place_kernel, order), out_shape=jax.Shap...  3.81 us
  transfers between devices with their start and end apart: 11, of which 7 were waited for; matrix products, arithmetic and copies ran while one was open for 2% of the time, Pallas kernels for 7%

profile of v24, /device:TPU:0, one launch (start us, length us, event | category | flops | bytes accessed | tf_op | source)
XLA Modules:
  0.0 119.4 jit_solution(11558307347468676413)
XLA Ops:
  0.6 4.7 %fetch.1 = (bf16[16,40,1024]{2,1,0:T(8,128)(2,1)}, s32[1]{0:T(128)}) custom-call(s32[16]{0:T(128)} %dealing.9, s32[16]{0:T(128)} %cols.5, f32[2,40,32768]{2,1,0:T(8,128)} %tile.1), custom_call_target="tpu_custom_call" | custom-call | bytes 6291456 | tf_op jit(solution)/shard_map/fetch/pallas_call | solution.py:81
  5.3 0.0 copy-start
  5.3 0.0 copy-start.1
  5.3 0.0 copy-start.3
  5.3 0.0 copy-start.4
  5.4 0.0 copy-start.5
  5.4 7.5 %all-to-all-start = ((bf16[16,40,1024]{2,1,0:T(8,128)(2,1)}), bf16[16,40,1024]{2,1,0:T(8,128)(2,1)S(1)}, u32[]{:S(2)}, u32[]{:S(2)}) async-start(bf16[16,40,1024]{2,1,0:T(8,128)(2,1)} %get-tuple-element.16), calls=%async_computation | async-start | bytes 2621440 | tf_op jit(solution)/shard_map/all_to_all | solution.py:459
  12.9 0.0 copy-done
  12.9 0.0 copy-done.1
  12.9 0.0 copy-done.3
  12.9 0.0 copy-done.4
  12.9 0.0 copy-start.2
  13.0 1.0 copy-done.2
  14.0 6.7 %prepare.1 = (f32[2,40,32768]{2,1,0:T(8,128)}, s32[80]{0:T(128)S(1)}, s32[80]{0:T(128)S(1)}, bf16[24576,1024]{1,0:T(8,128)(2,1)}) custom-call(s32[16]{0:T(128)S(1)} %copy-done.3, s32[16]{0:T(128)S(1)} %copy-done.4, s32[1]{0:T(128)} %get-tuple-element.13.token, bf16[512,1024]{1,0:T(8,128)(2,1)S(1)} %copy-done.1, bf16[2,512,512]{2,1,0:T(8,128)(2,1)S(1)} %copy-done, ...), custom_call_target="tpu_custom_call" | custom-call | bytes 115343360 | tf_op jit(solution)/shard_map/prepare/pallas_call | solution.py:156
  20.7 19.6 %all-to-all-done = bf16[16,40,1024]{2,1,0:T(8,128)(2,1)S(1)} async-done(((bf16[16,40,1024]{2,1,0:T(8,128)(2,1)}), bf16[16,40,1024]{2,1,0:T(8,128)(2,1)S(1)}, u32[]{:S(2)}, u32[]{:S(2)}) %all-to-all-start) | async-done | bytes 1310752 | tf_op jit(solution)/shard_map/all_to_all | solution.py:459
  40.3 0.0 copy-done.5
  40.3 7.5 %slot.1 = (bf16[512,1024]{1,0:T(8,128)(2,1)S(1)}, f32[256,1024]{1,0:T(8,128)S(1)}, bf16[256,1024]{1,0:T(8,128)(2,1)}) custom-call(s32[16]{0:T(128)S(1)} %copy-done.3, s32[16]{0:T(128)S(1)} %copy-done.5, s32[80]{0:T(128)S(1)} %get-tuple-element.15.owners, bf16[640,1024]{1,0:T(8,128)(2,1)S(1)} %bitcast.22, bf16[24576,1024]{1,0:T(8,128)(2,1)} %get-tuple-element.17.stock), custom_call_target="tpu_custom_call" | custom-call | flops 4294967296 | bytes 8388608 | tf_op jit(solution)/shard_map/slot/pallas_call | solution.py:275
  47.8 0.8 collective-permute-start
  48.6 1.7 %collective-permute-done = bf16[256,1024]{1,0:T(8,128)(2,1)S(1)} collective-permute-done((bf16[256,1024]{1,0:T(8,128)(2,1)}, bf16[256,1024]{1,0:T(8,128)(2,1)S(1)}, u32[]{:S(2)}, u32[]{:S(2)}) %collective-permute-start) | collective-permute-done | bytes 524320 | tf_op jit(solution)/shard_map/ppermute | solution.py:406
  50.4 0.1 add_convert_fusion
  50.5 2.4 %collective-permute-start.1 = (bf16[128,1024]{1,0:T(8,128)(2,1)S(1)}, bf16[128,1024]{1,0:T(8,128)(2,1)S(1)}, u32[]{:S(2)}, u32[]{:S(2)}) collective-permute-start(bf16[128,1024]{1,0:T(8,128)(2,1)S(1)} %get-tuple-element.26), channel_id=1, source_target_pairs={{0,2},{1,3},{2,0},{3,1},{4,6},{5,7},{6,4},{7,5},{8,10},{9,11},{10,... | collective-permute-start | bytes 786440 | tf_op jit(solution)/shard_map/ppermute | solution.py:406
  52.9 6.8 %collective-permute-done.1 = bf16[128,1024]{1,0:T(8,128)(2,1)S(1)} collective-permute-done((bf16[128,1024]{1,0:T(8,128)(2,1)S(1)}, bf16[128,1024]{1,0:T(8,128)(2,1)S(1)}, u32[]{:S(2)}, u32[]{:S(2)}) %collective-permute-start.1) | collective-permute-done | bytes 262176 | tf_op jit(solution)/shard_map/ppermute | solution.py:406
  59.8 4.5 %collective-permute-start.4 = (bf16[32,1024]{1,0:T(8,128)(2,1)S(1)}, bf16[32,1024]{1,0:T(8,128)(2,1)S(1)}, u32[]{:S(2)}, u32[]{:S(2)}) collective-permute-start(bf16[32,1024]{1,0:T(8,128)(2,1)S(1)} %get-tuple-element.31), channel_id=1, source_target_pairs={{0,12},{1,13},{2,14},{3,15},{4,8},{5,9},{6,10},{7,11},{8,4},{9,5},... | collective-permute-start | bytes 196616 | tf_op jit(solution)/shard_map/ppermute | solution.py:406
  64.3 0.7 collective-permute-start.3
  64.9 0.5 collective-permute-start.2
  65.4 2.2 %pack.1 = bf16[16,40,1024]{2,1,0:T(8,128)(2,1)} custom-call(s32[16]{0:T(128)S(1)} %copy-done.3, s32[16]{0:T(128)S(1)} %copy-done.5, bf16[512,1024]{1,0:T(8,128)(2,1)S(1)} %get-tuple-element.18.term), custom_call_target="tpu_custom_call" | custom-call | bytes 3145728 | tf_op jit(solution)/shard_map/pack/pallas_call | solution.py:323
  67.6 0.0 collective-permute-done.4
  67.6 2.9 %collective-permute-done.3 = bf16[32,1024]{1,0:T(8,128)(2,1)S(1)} collective-permute-done((bf16[32,1024]{1,0:T(8,128)(2,1)S(1)}, bf16[32,1024]{1,0:T(8,128)(2,1)S(1)}, u32[]{:S(2)}, u32[]{:S(2)}) %collective-permute-start.3) | collective-permute-done | bytes 65568 | tf_op jit(solution)/shard_map/ppermute | solution.py:406
  70.5 0.0 collective-permute-done.2
  70.6 1.2 %collective-permute-start.5 = (bf16[32,1024]{1,0:T(8,128)(2,1)S(1)}, bf16[32,1024]{1,0:T(8,128)(2,1)S(1)}, u32[]{:S(2)}, u32[]{:S(2)}) collective-permute-start(bf16[32,1024]{1,0:T(8,128)(2,1)S(1)} %multiply_convert_fusion), channel_id=1, source_target_pairs={{0,8},{1,9},{2,10},{3,11},{4,12},{5,13},{6,14},{7,15},{8,0},{9,1},... | collective-permute-start | bytes 196616 | tf_op jit(solution)/shard_map/ppermute | solution.py:406
  71.8 4.5 %collective-permute-done.5 = bf16[32,1024]{1,0:T(8,128)(2,1)S(1)} collective-permute-done((bf16[32,1024]{1,0:T(8,128)(2,1)S(1)}, bf16[32,1024]{1,0:T(8,128)(2,1)S(1)}, u32[]{:S(2)}, u32[]{:S(2)}) %collective-permute-start.5) | collective-permute-done | bytes 65568 | tf_op jit(solution)/shard_map/ppermute | solution.py:406
  76.4 1.5 %collective-permute-start.6 = (bf16[2,32,1024]{2,1,0:T(8,128)(2,1)S(1)}, bf16[2,32,1024]{2,1,0:T(8,128)(2,1)S(1)}, u32[]{:S(2)}, u32[]{:S(2)}) collective-permute-start(bf16[2,32,1024]{2,1,0:T(8,128)(2,1)S(1)} %pad_maximum_fusion.3), channel_id=1, source_target_pairs={{0,2},{1,3},{2,0},{3,1},{4,6},{5,7},{6,4},{7,5},{8,10},{9,11},{10,... | collective-permute-start | bytes 393224 | tf_op jit(solution)/shard_map/ppermute | solution.py:406
  77.9 3.7 %all-to-all-start.1 = ((bf16[16,40,1024]{2,1,0:T(8,128)(2,1)}), bf16[16,40,1024]{2,1,0:T(8,128)(2,1)S(1)}, u32[]{:S(2)}, u32[]{:S(2)}) async-start(bf16[16,40,1024]{2,1,0:T(8,128)(2,1)} %pack.1), calls=%async_computation.1 | async-start | bytes 2621440 | tf_op jit(solution)/shard_map/all_to_all | solution.py:468
  81.6 0.0 collective-permute-done.6
  81.7 1.9 %collective-permute-start.7 = (bf16[2,2,32,1024]{3,2,1,0:T(8,128)(2,1)S(1)}, bf16[2,2,32,1024]{3,2,1,0:T(8,128)(2,1)S(1)}, u32[]{:S(2)}, u32[]{:S(2)}) collective-permute-start(bf16[2,2,32,1024]{3,2,1,0:T(8,128)(2,1)S(1)} %pad_maximum_fusion.2), channel_id=1, source_target_pairs={{0,4},{1,5},{2,6},{3,7},{4,0},{5,1},{6,2},{7,3},{8,12},{9,13},{10,... | collective-permute-start | bytes 786440 | tf_op jit(solution)/shard_map/ppermute | solution.py:406
  83.6 27.7 %collective-permute-done.7 = bf16[2,2,32,1024]{3,2,1,0:T(8,128)(2,1)S(1)} collective-permute-done((bf16[2,2,32,1024]{3,2,1,0:T(8,128)(2,1)S(1)}, bf16[2,2,32,1024]{3,2,1,0:T(8,128)(2,1)S(1)}, u32[]{:S(2)}, u32[]{:S(2)}) %collective-permute-start.7) | collective-permute-done | bytes 262176 | tf_op jit(solution)/shard_map/ppermute | solution.py:406
  111.4 0.1 pad_maximum_fusion.1
  111.5 0.1 collective-permute-start.8
  111.5 1.9 %collective-permute-done.8 = bf16[2,2,2,32,1024]{4,3,1,0,2:T(8,128)(2,1)S(1)} collective-permute-done((bf16[2,2,2,32,1024]{4,3,1,0,2:T(8,128)(2,1)S(1)}, bf16[2,2,2,32,1024]{4,3,1,0,2:T(8,128)(2,1)S(1)}, u32[]{:S(2)}, u32[]{:S(2)}) %collective-permute-start.8) | collective-permute-done | bytes 524320 | tf_op jit(solution)/shard_map/ppermute | solution.py:406
  113.4 0.1 select_bitcast_fusion.1
  113.5 0.1 maximum_convert_fusion
  113.7 0.2 copy.10
  113.9 0.2 slice_bitcast_fusion.1
  114.1 1.5 %pad_maximum_fusion = f32[2,512,512]{2,1,0:T(8,128)} fusion(f32[1,512,512]{2,1,0:T(8,128)S(1)} %get-tuple-element.25, f32[1,512,512]{2,1,0:T(8,128)S(1)} %get-tuple-element.24), kind=kLoop, calls=%fused_computation | loop fusion | flops 524288 | bytes 4194304 | tf_op jit(solution)/shard_map/stack | solution.py:471
  115.6 0.0 all-to-all-done.1.terms
  115.6 3.8 %place.1 = f32[2,40,32768]{2,1,0:T(8,128)} custom-call(s32[16]{0:T(128)S(1)} %copy-done.3, s32[16]{0:T(128)S(1)} %copy-done.4, s32[80]{0:T(128)S(1)} %get-tuple-element.14.blocks, s32[80]{0:T(128)S(1)} %get-tuple-element.15.owners, bf16[16,40,1024]{2,1,0:T(8,128)(2,1)S(1)} %all-to-all-done.1.terms, ...), custom_call_target="tpu_custom_call", output_to_operand_aliasing={{}: (5, {})} | custom-call | bytes 6291456 | tf_op jit(solution)/shard_map/place/pallas_call | solution.py:380
  (8 shorter events, 0.2 us)
Async XLA Ops:
  5.3 7.6 %copy-start = (bf16[2,512,512]{2,1,0:T(8,128)(2,1)S(1)}, bf16[2,512,512]{2,1,0:T(8,128)(2,1)}, u32[]{:S(2)}) copy-start(bf16[2,512,512]{2,1,0:T(8,128)(2,1)} %probe.1) | copy-start | bytes 3145732
  5.3 7.6 %copy-start.1 = (bf16[512,1024]{1,0:T(8,128)(2,1)S(1)}, bf16[512,1024]{1,0:T(8,128)(2,1)}, u32[]{:S(2)}) copy-start(bf16[512,1024]{1,0:T(8,128)(2,1)} %constant.95.clone.table_in) | copy-start | bytes 3145732
  5.3 7.6 %copy-start.3 = (s32[16]{0:T(128)S(1)}, s32[16]{0:T(128)}, u32[]{:S(2)}) copy-start(s32[16]{0:T(128)} %dealing.9) | copy-start | bytes 196
  5.3 7.6 %copy-start.4 = (s32[16]{0:T(128)S(1)}, s32[16]{0:T(128)}, u32[]{:S(2)}) copy-start(s32[16]{0:T(128)} %cols.5) | copy-start | bytes 196
  5.4 35.0 %copy-start.5 = (s32[16]{0:T(128)S(1)}, s32[16]{0:T(128)}, u32[]{:S(2)}) copy-start(s32[16]{0:T(128)} %rows.3) | copy-start | bytes 196
  5.4 35.0 %all-to-all-start = ((bf16[16,40,1024]{2,1,0:T(8,128)(2,1)}), bf16[16,40,1024]{2,1,0:T(8,128)(2,1)S(1)}, u32[]{:S(2)}, u32[]{:S(2)}) async-start(bf16[16,40,1024]{2,1,0:T(8,128)(2,1)} %get-tuple-element.16), calls=%async_computation | async-start | bytes 2621440 | tf_op jit(solution)/shard_map/all_to_all | solution.py:459
  12.9 1.0 copy-start.2
  47.8 2.6 %collective-permute-start = (bf16[256,1024]{1,0:T(8,128)(2,1)}, bf16[256,1024]{1,0:T(8,128)(2,1)S(1)}, u32[]{:S(2)}, u32[]{:S(2)}) collective-permute-start(bf16[256,1024]{1,0:T(8,128)(2,1)} %get-tuple-element.20), channel_id=1, source_target_pairs={{0,1},{1,0},{2,3},{3,2},{4,5},{5,4},{6,7},{7,6},{8,9},{9,8},{10,11... | collective-permute-start | bytes 1572872 | tf_op jit(solution)/shard_map/ppermute | solution.py:406
  50.5 9.2 %collective-permute-start.1 = (bf16[128,1024]{1,0:T(8,128)(2,1)S(1)}, bf16[128,1024]{1,0:T(8,128)(2,1)S(1)}, u32[]{:S(2)}, u32[]{:S(2)}) collective-permute-start(bf16[128,1024]{1,0:T(8,128)(2,1)S(1)} %get-tuple-element.26), channel_id=1, source_target_pairs={{0,2},{1,3},{2,0},{3,1},{4,6},{5,7},{6,4},{7,5},{8,10},{9,11},{10,... | collective-permute-start | bytes 786440 | tf_op jit(solution)/shard_map/ppermute | solution.py:406
  59.8 7.8 %collective-permute-start.4 = (bf16[32,1024]{1,0:T(8,128)(2,1)S(1)}, bf16[32,1024]{1,0:T(8,128)(2,1)S(1)}, u32[]{:S(2)}, u32[]{:S(2)}) collective-permute-start(bf16[32,1024]{1,0:T(8,128)(2,1)S(1)} %get-tuple-element.31), channel_id=1, source_target_pairs={{0,12},{1,13},{2,14},{3,15},{4,8},{5,9},{6,10},{7,11},{8,4},{9,5},... | collective-permute-start | bytes 196616 | tf_op jit(solution)/shard_map/ppermute | solution.py:406
  64.3 6.3 %collective-permute-start.3 = (bf16[32,1024]{1,0:T(8,128)(2,1)S(1)}, bf16[32,1024]{1,0:T(8,128)(2,1)S(1)}, u32[]{:S(2)}, u32[]{:S(2)}) collective-permute-start(bf16[32,1024]{1,0:T(8,128)(2,1)S(1)} %get-tuple-element.32), channel_id=1, source_target_pairs={{0,8},{1,9},{2,10},{3,11},{4,12},{5,13},{6,14},{7,15},{8,0},{9,1},... | collective-permute-start | bytes 196616 | tf_op jit(solution)/shard_map/ppermute | solution.py:406
  64.9 5.6 %collective-permute-start.2 = (bf16[32,1024]{1,0:T(8,128)(2,1)S(1)}, bf16[32,1024]{1,0:T(8,128)(2,1)S(1)}, u32[]{:S(2)}, u32[]{:S(2)}) collective-permute-start(bf16[32,1024]{1,0:T(8,128)(2,1)S(1)} %get-tuple-element.30), channel_id=1, source_target_pairs={{0,4},{1,5},{2,6},{3,7},{4,0},{5,1},{6,2},{7,3},{8,12},{9,13},{10,... | collective-permute-start | bytes 196616 | tf_op jit(solution)/shard_map/ppermute | solution.py:406
  70.6 5.7 %collective-permute-start.5 = (bf16[32,1024]{1,0:T(8,128)(2,1)S(1)}, bf16[32,1024]{1,0:T(8,128)(2,1)S(1)}, u32[]{:S(2)}, u32[]{:S(2)}) collective-permute-start(bf16[32,1024]{1,0:T(8,128)(2,1)S(1)} %multiply_convert_fusion), channel_id=1, source_target_pairs={{0,8},{1,9},{2,10},{3,11},{4,12},{5,13},{6,14},{7,15},{8,0},{9,1},... | collective-permute-start | bytes 196616 | tf_op jit(solution)/shard_map/ppermute | solution.py:406
  76.4 5.2 %collective-permute-start.6 = (bf16[2,32,1024]{2,1,0:T(8,128)(2,1)S(1)}, bf16[2,32,1024]{2,1,0:T(8,128)(2,1)S(1)}, u32[]{:S(2)}, u32[]{:S(2)}) collective-permute-start(bf16[2,32,1024]{2,1,0:T(8,128)(2,1)S(1)} %pad_maximum_fusion.3), channel_id=1, source_target_pairs={{0,2},{1,3},{2,0},{3,1},{4,6},{5,7},{6,4},{7,5},{8,10},{9,11},{10,... | collective-permute-start | bytes 393224 | tf_op jit(solution)/shard_map/ppermute | solution.py:406
  77.9 37.7 %all-to-all-start.1 = ((bf16[16,40,1024]{2,1,0:T(8,128)(2,1)}), bf16[16,40,1024]{2,1,0:T(8,128)(2,1)S(1)}, u32[]{:S(2)}, u32[]{:S(2)}) async-start(bf16[16,40,1024]{2,1,0:T(8,128)(2,1)} %pack.1), calls=%async_computation.1 | async-start | bytes 2621440 | tf_op jit(solution)/shard_map/all_to_all | solution.py:468
  81.7 29.7 %collective-permute-start.7 = (bf16[2,2,32,1024]{3,2,1,0:T(8,128)(2,1)S(1)}, bf16[2,2,32,1024]{3,2,1,0:T(8,128)(2,1)S(1)}, u32[]{:S(2)}, u32[]{:S(2)}) collective-permute-start(bf16[2,2,32,1024]{3,2,1,0:T(8,128)(2,1)S(1)} %pad_maximum_fusion.2), channel_id=1, source_target_pairs={{0,4},{1,5},{2,6},{3,7},{4,0},{5,1},{6,2},{7,3},{8,12},{9,13},{10,... | collective-permute-start | bytes 786440 | tf_op jit(solution)/shard_map/ppermute | solution.py:406
  111.5 2.0 %collective-permute-start.8 = (bf16[2,2,2,32,1024]{4,3,1,0,2:T(8,128)(2,1)S(1)}, bf16[2,2,2,32,1024]{4,3,1,0,2:T(8,128)(2,1)S(1)}, u32[]{:S(2)}, u32[]{:S(2)}) collective-permute-start(bf16[2,2,2,32,1024]{4,3,1,0,2:T(8,128)(2,1)S(1)} %pad_maximum_fusion.1), channel_id=1, source_target_pairs={{0,1},{1,0},{2,3},{3,2},{4,5},{5,4},{6,7},{7,6},{8,9},{9,8},{10,11... | collective-permute-start | bytes 1572872 | tf_op jit(solution)/shard_map/ppermute | solution.py:406

commit v25 on v21

--- a/solution.py
+++ b/solution.py
@@ -65,13 +65,13 @@
         shift = lax.rem(LANES - lax.rem(offset, LANES), LANES)
         for part in range(2):
             turned = [
-                pltpu.roll(held[slot, part, :, b * LANES : (b + 1) * LANES].astype(out.dtype), shift, 1)
+                pltpu.roll(held[slot, part, :, b * LANES : (b + 1) * LANES], shift, 1)
                 for b in range(span // LANES)
             ]
             for b in range(order // LANES):
                 first = part * order + b * LANES
                 cells = jnp.where(lane < LANES - offset, turned[b], turned[b + 1])
-                out[slot, :, first : first + LANES] = cells
+                out[slot, :, first : first + LANES] = cells.astype(out.dtype)
 
 
 def fetch_windows(tile, dealing, cols, order):
@@ -199,14 +199,14 @@
     wide[0:total_rows, :] = cells[...].astype(jnp.float32)
     wide[total_rows:, :] = jnp.zeros((SUBLANES, 2 * order), jnp.float32)
 
-    @pl.loop(0, order // step, unroll=2)
+    @pl.loop(0, order // step, unroll=4)
     def _(i):
         place = pl.ds(pl.multiple_of(i * step, step), step)
         patch[place, :] = rows_from(wide, first_row + i * step, step).astype(patch.dtype)
 
     loads[0].wait()
 
-    @pl.loop(0, order // step, unroll=2)
+    @pl.loop(0, order // step, unroll=4)
     def _(i):
         place = pl.ds(pl.multiple_of(i * step, step), step)
         found = patch[place, :].astype(jnp.float32)

time: 113 us -> 113 us (level)
  no operation moved by 1% of the time
where the time goes in v25:
time: 113 us
  waiting for transfers between devices  58.9 us (52%)
  Pallas kernels  24.8 us (22%)
  starting transfers between devices  24.6 us (22%)
  other arithmetic  2.4 us (2%)
  local copies, waits for them, and re-layouts  1.26 us (1%)
    ppermute x10, waiting for transfers between devices, swap(): return lax.ppermute(x, 'row', [(d, d ^ distance) for d in range(devices)])  26 us
    all_to_all x1, waiting for transfers between devices, body(): lax.all_to_all(pieces, 'row', split_axis=0, concat_axis=0, tiled=True)  22.8 us
    ppermute x10, starting transfers between devices, swap(): return lax.ppermute(x, 'row', [(d, d ^ distance) for d in range(devices)])  10.4 us
    all_to_all x1, waiting for transfers between devices, body(): lax.all_to_all(terms, 'row', split_axis=0, concat_axis=0, tiled=True)  10.1 us
    all_to_all x1, starting transfers between devices, body(): lax.all_to_all(terms, 'row', split_axis=0, concat_axis=0, tiled=True)  7.49 us
    pallas_call x1, Pallas kernels, slot_terms(): pl.pallas_call(slot_kernel, out_shape=(jax.ShapeDtypeStruct((order, wide_...  7.46 us
    all_to_all x1, starting transfers between devices, body(): lax.all_to_all(pieces, 'row', split_axis=0, concat_axis=0, tiled=True)  6.7 us
    pallas_call x1, Pallas kernels, prepare(): pl.pallas_call(functools.partial(prepare_kernel, order), out_shape=(jax.S...  6.69 us
  transfers between devices with their start and end apart: 12, of which 8 were waited for; matrix products, arithmetic and copies ran while one was open for 2% of the time, Pallas kernels for 8%

profile of v25, /device:TPU:15, one launch (start us, length us, event | category | flops | bytes accessed | tf_op | source)
XLA Modules:
  0.0 112.8 jit_solution(600263020134656705)
XLA Ops:
  0.6 4.6 %fetch.1 = (bf16[16,40,1024]{2,1,0:T(8,128)(2,1)}, s32[1]{0:T(128)}) custom-call(s32[16]{0:T(128)} %dealing.9, s32[16]{0:T(128)} %cols.5, f32[2,40,32768]{2,1,0:T(8,128)} %tile.1), custom_call_target="tpu_custom_call" | custom-call | bytes 6291456 | tf_op jit(solution)/shard_map/fetch/pallas_call | solution.py:81
  5.2 0.0 copy-start
  5.3 0.0 copy-start.1
  5.3 0.0 copy-start.3
  5.3 0.0 copy-start.4
  5.3 0.0 copy-start.5
  5.3 6.7 %all-to-all-start = ((bf16[16,40,1024]{2,1,0:T(8,128)(2,1)}), bf16[16,40,1024]{2,1,0:T(8,128)(2,1)S(1)}, u32[]{:S(2)}, u32[]{:S(2)}) async-start(bf16[16,40,1024]{2,1,0:T(8,128)(2,1)} %get-tuple-element.16), calls=%async_computation | async-start | bytes 2621440 | tf_op jit(solution)/shard_map/all_to_all | solution.py:456
  12.0 0.0 copy-done
  12.0 0.0 copy-done.1
  12.0 0.0 copy-done.3
  12.0 0.0 copy-done.4
  12.0 0.0 copy-start.2
  12.1 1.0 copy-done.2
  13.1 6.7 %prepare.1 = (f32[2,40,32768]{2,1,0:T(8,128)}, s32[80]{0:T(128)S(1)}, s32[80]{0:T(128)S(1)}, bf16[24576,1024]{1,0:T(8,128)(2,1)}) custom-call(s32[16]{0:T(128)S(1)} %copy-done.3, s32[16]{0:T(128)S(1)} %copy-done.4, s32[1]{0:T(128)} %get-tuple-element.13.token, bf16[512,1024]{1,0:T(8,128)(2,1)S(1)} %copy-done.1, bf16[2,512,512]{2,1,0:T(8,128)(2,1)S(1)} %copy-done, ...), custom_call_target="tpu_custom_call" | custom-call | bytes 115343360 | tf_op jit(solution)/shard_map/prepare/pallas_call | solution.py:156
  19.8 22.8 %all-to-all-done = bf16[16,40,1024]{2,1,0:T(8,128)(2,1)S(1)} async-done(((bf16[16,40,1024]{2,1,0:T(8,128)(2,1)}), bf16[16,40,1024]{2,1,0:T(8,128)(2,1)S(1)}, u32[]{:S(2)}, u32[]{:S(2)}) %all-to-all-start) | async-done | bytes 1310752 | tf_op jit(solution)/shard_map/all_to_all | solution.py:456
  42.6 0.0 copy-done.5
  42.6 7.5 %slot.1 = (bf16[512,1024]{1,0:T(8,128)(2,1)S(1)}, f32[256,1024]{1,0:T(8,128)S(1)}, bf16[256,1024]{1,0:T(8,128)(2,1)}) custom-call(s32[16]{0:T(128)S(1)} %copy-done.3, s32[16]{0:T(128)S(1)} %copy-done.5, s32[80]{0:T(128)S(1)} %get-tuple-element.15.owners, bf16[640,1024]{1,0:T(8,128)(2,1)S(1)} %bitcast.5, bf16[24576,1024]{1,0:T(8,128)(2,1)} %get-tuple-element.17.stock), custom_call_target="tpu_custom_call" | custom-call | flops 4294967296 | bytes 8388608 | tf_op jit(solution)/shard_map/slot/pallas_call | solution.py:275
  50.0 0.3 collective-permute-start
  50.3 1.9 %collective-permute-done = bf16[256,1024]{1,0:T(8,128)(2,1)S(1)} collective-permute-done((bf16[256,1024]{1,0:T(8,128)(2,1)}, bf16[256,1024]{1,0:T(8,128)(2,1)S(1)}, u32[]{:S(2)}, u32[]{:S(2)}) %collective-permute-start) | collective-permute-done | bytes 524320 | tf_op jit(solution)/shard_map/ppermute | solution.py:406
  52.2 0.1 add_convert_fusion
  52.4 0.1 collective-permute-start.1
  52.5 7.6 %collective-permute-done.1 = bf16[128,1024]{1,0:T(8,128)(2,1)S(1)} collective-permute-done((bf16[128,1024]{1,0:T(8,128)(2,1)S(1)}, bf16[128,1024]{1,0:T(8,128)(2,1)S(1)}, u32[]{:S(2)}, u32[]{:S(2)}) %collective-permute-start.1) | collective-permute-done | bytes 262176 | tf_op jit(solution)/shard_map/ppermute | solution.py:406
  60.2 0.4 collective-permute-start.4
  60.6 0.8 collective-permute-start.3
  61.4 1.5 %collective-permute-start.2 = (bf16[32,1024]{1,0:T(8,128)(2,1)S(1)}, bf16[32,1024]{1,0:T(8,128)(2,1)S(1)}, u32[]{:S(2)}, u32[]{:S(2)}) collective-permute-start(bf16[32,1024]{1,0:T(8,128)(2,1)S(1)} %get-tuple-element.30), channel_id=1, source_target_pairs={{0,4},{1,5},{2,6},{3,7},{4,0},{5,1},{6,2},{7,3},{8,12},{9,13},{10,... | collective-permute-start | bytes 196616 | tf_op jit(solution)/shard_map/ppermute | solution.py:406
  62.9 2.2 %pack.1 = bf16[16,40,1024]{2,1,0:T(8,128)(2,1)} custom-call(s32[16]{0:T(128)S(1)} %copy-done.3, s32[16]{0:T(128)S(1)} %copy-done.5, bf16[512,1024]{1,0:T(8,128)(2,1)S(1)} %get-tuple-element.18.term), custom_call_target="tpu_custom_call" | custom-call | bytes 3145728 | tf_op jit(solution)/shard_map/pack/pallas_call | solution.py:323
  65.1 0.3 collective-permute-done.4
  65.4 0.0 collective-permute-done.3
  65.4 1.1 collective-permute-done.2
  66.6 0.9 collective-permute-start.5
  67.5 3.4 %collective-permute-start.6 = (bf16[32,1024]{1,0:T(8,128)(2,1)S(1)}, bf16[32,1024]{1,0:T(8,128)(2,1)S(1)}, u32[]{:S(2)}, u32[]{:S(2)}) collective-permute-start(bf16[32,1024]{1,0:T(8,128)(2,1)S(1)} %multiply_convert_fusion), channel_id=1, source_target_pairs={{0,8},{1,9},{2,10},{3,11},{4,12},{5,13},{6,14},{7,15},{8,0},{9,1},... | collective-permute-start | bytes 196616 | tf_op jit(solution)/shard_map/ppermute | solution.py:406
  70.9 0.0 collective-permute-start.7
  70.9 7.5 %all-to-all-start.1 = ((bf16[16,40,1024]{2,1,0:T(8,128)(2,1)}), bf16[16,40,1024]{2,1,0:T(8,128)(2,1)S(1)}, u32[]{:S(2)}, u32[]{:S(2)}) async-start(bf16[16,40,1024]{2,1,0:T(8,128)(2,1)} %pack.1), calls=%async_computation.1 | async-start | bytes 2621440 | tf_op jit(solution)/shard_map/all_to_all | solution.py:465
  78.4 0.0 collective-permute-done.5
  78.4 0.0 collective-permute-done.6
  78.4 0.0 collective-permute-done.7
  78.5 0.3 collective-permute-start.8
  78.9 13.5 %collective-permute-done.8 = bf16[128,1024]{1,0:T(8,128)(2,1)S(1)} collective-permute-done((bf16[128,1024]{1,0:T(8,128)(2,1)S(1)}, bf16[128,1024]{1,0:T(8,128)(2,1)S(1)}, u32[]{:S(2)}, u32[]{:S(2)}) %collective-permute-start.8) | collective-permute-done | bytes 262176 | tf_op jit(solution)/shard_map/ppermute | solution.py:406
  92.4 0.1 broadcast_select_fusion.3
  92.6 2.6 %collective-permute-start.9 = (bf16[256,1024]{1,0:T(8,128)(2,1)S(1)}, bf16[256,1024]{1,0:T(8,128)(2,1)S(1)}, u32[]{:S(2)}, u32[]{:S(2)}) collective-permute-start(bf16[256,1024]{1,0:T(8,128)(2,1)S(1)} %pad_maximum_fusion.1), channel_id=1, source_target_pairs={{0,1},{1,0},{2,3},{3,2},{4,5},{5,4},{6,7},{7,6},{8,9},{9,8},{10,11... | collective-permute-start | bytes 1572872 | tf_op jit(solution)/shard_map/ppermute | solution.py:406
  95.2 1.5 %collective-permute-done.9 = bf16[256,1024]{1,0:T(8,128)(2,1)S(1)} collective-permute-done((bf16[256,1024]{1,0:T(8,128)(2,1)S(1)}, bf16[256,1024]{1,0:T(8,128)(2,1)S(1)}, u32[]{:S(2)}, u32[]{:S(2)}) %collective-permute-start.9) | collective-permute-done | bytes 524320 | tf_op jit(solution)/shard_map/ppermute | solution.py:406
  96.7 0.2 broadcast_select_fusion.1
  97.0 0.2 maximum_convert_fusion
  97.2 0.2 slice_bitcast_fusion.1
  97.4 1.5 %pad_maximum_fusion = f32[2,512,512]{2,1,0:T(8,128)} fusion(f32[1,512,512]{2,1,0:T(8,128)S(1)} %get-tuple-element.25, f32[1,512,512]{2,1,0:T(8,128)S(1)} %get-tuple-element.24), kind=kLoop, calls=%fused_computation | loop fusion | flops 524288 | bytes 4194304 | tf_op jit(solution)/shard_map/stack | solution.py:468
  98.9 10.1 %all-to-all-done.1.terms = bf16[16,40,1024]{2,1,0:T(8,128)(2,1)S(1)} async-done(((bf16[16,40,1024]{2,1,0:T(8,128)(2,1)}), bf16[16,40,1024]{2,1,0:T(8,128)(2,1)S(1)}, u32[]{:S(2)}, u32[]{:S(2)}) %all-to-all-start.1) | async-done | bytes 1310752 | tf_op jit(solution)/shard_map/all_to_all | solution.py:465
  109.0 3.8 %place.1 = f32[2,40,32768]{2,1,0:T(8,128)} custom-call(s32[16]{0:T(128)S(1)} %copy-done.3, s32[16]{0:T(128)S(1)} %copy-done.4, s32[80]{0:T(128)S(1)} %get-tuple-element.14.blocks, s32[80]{0:T(128)S(1)} %get-tuple-element.15.owners, bf16[16,40,1024]{2,1,0:T(8,128)(2,1)S(1)} %all-to-all-done.1.terms, ...), custom_call_target="tpu_custom_call", output_to_operand_aliasing={{}: (5, {})} | custom-call | bytes 6291456 | tf_op jit(solution)/shard_map/place/pallas_call | solution.py:380
  (6 shorter events, 0.2 us)
Async XLA Ops:
  5.2 6.8 %copy-start = (bf16[2,512,512]{2,1,0:T(8,128)(2,1)S(1)}, bf16[2,512,512]{2,1,0:T(8,128)(2,1)}, u32[]{:S(2)}) copy-start(bf16[2,512,512]{2,1,0:T(8,128)(2,1)} %probe.1) | copy-start | bytes 3145732
  5.3 6.8 %copy-start.1 = (bf16[512,1024]{1,0:T(8,128)(2,1)S(1)}, bf16[512,1024]{1,0:T(8,128)(2,1)}, u32[]{:S(2)}) copy-start(bf16[512,1024]{1,0:T(8,128)(2,1)} %constant.79.clone.table_in) | copy-start | bytes 3145732
  5.3 6.8 %copy-start.3 = (s32[16]{0:T(128)S(1)}, s32[16]{0:T(128)}, u32[]{:S(2)}) copy-start(s32[16]{0:T(128)} %dealing.9) | copy-start | bytes 196
  5.3 6.8 %copy-start.4 = (s32[16]{0:T(128)S(1)}, s32[16]{0:T(128)}, u32[]{:S(2)}) copy-start(s32[16]{0:T(128)} %cols.5) | copy-start | bytes 196
  5.3 37.3 %copy-start.5 = (s32[16]{0:T(128)S(1)}, s32[16]{0:T(128)}, u32[]{:S(2)}) copy-start(s32[16]{0:T(128)} %rows.3) | copy-start | bytes 196
  5.3 37.3 %all-to-all-start = ((bf16[16,40,1024]{2,1,0:T(8,128)(2,1)}), bf16[16,40,1024]{2,1,0:T(8,128)(2,1)S(1)}, u32[]{:S(2)}, u32[]{:S(2)}) async-start(bf16[16,40,1024]{2,1,0:T(8,128)(2,1)} %get-tuple-element.16), calls=%async_computation | async-start | bytes 2621440 | tf_op jit(solution)/shard_map/all_to_all | solution.py:456
  12.0 1.0 copy-start.2
  50.0 2.2 %collective-permute-start = (bf16[256,1024]{1,0:T(8,128)(2,1)}, bf16[256,1024]{1,0:T(8,128)(2,1)S(1)}, u32[]{:S(2)}, u32[]{:S(2)}) collective-permute-start(bf16[256,1024]{1,0:T(8,128)(2,1)} %get-tuple-element.20), channel_id=1, source_target_pairs={{0,1},{1,0},{2,3},{3,2},{4,5},{5,4},{6,7},{7,6},{8,9},{9,8},{10,11... | collective-permute-start | bytes 1572872 | tf_op jit(solution)/shard_map/ppermute | solution.py:406
  52.4 7.8 %collective-permute-start.1 = (bf16[128,1024]{1,0:T(8,128)(2,1)S(1)}, bf16[128,1024]{1,0:T(8,128)(2,1)S(1)}, u32[]{:S(2)}, u32[]{:S(2)}) collective-permute-start(bf16[128,1024]{1,0:T(8,128)(2,1)S(1)} %get-tuple-element.26), channel_id=1, source_target_pairs={{0,2},{1,3},{2,0},{3,1},{4,6},{5,7},{6,4},{7,5},{8,10},{9,11},{10,... | collective-permute-start | bytes 786440 | tf_op jit(solution)/shard_map/ppermute | solution.py:406
  60.2 5.2 %collective-permute-start.4 = (bf16[32,1024]{1,0:T(8,128)(2,1)S(1)}, bf16[32,1024]{1,0:T(8,128)(2,1)S(1)}, u32[]{:S(2)}, u32[]{:S(2)}) collective-permute-start(bf16[32,1024]{1,0:T(8,128)(2,1)S(1)} %get-tuple-element.31), channel_id=1, source_target_pairs={{0,12},{1,13},{2,14},{3,15},{4,8},{5,9},{6,10},{7,11},{8,4},{9,5},... | collective-permute-start | bytes 196616 | tf_op jit(solution)/shard_map/ppermute | solution.py:406
  60.6 4.8 %collective-permute-start.3 = (bf16[32,1024]{1,0:T(8,128)(2,1)S(1)}, bf16[32,1024]{1,0:T(8,128)(2,1)S(1)}, u32[]{:S(2)}, u32[]{:S(2)}) collective-permute-start(bf16[32,1024]{1,0:T(8,128)(2,1)S(1)} %get-tuple-element.32), channel_id=1, source_target_pairs={{0,8},{1,9},{2,10},{3,11},{4,12},{5,13},{6,14},{7,15},{8,0},{9,1},... | collective-permute-start | bytes 196616 | tf_op jit(solution)/shard_map/ppermute | solution.py:406
  61.4 5.1 %collective-permute-start.2 = (bf16[32,1024]{1,0:T(8,128)(2,1)S(1)}, bf16[32,1024]{1,0:T(8,128)(2,1)S(1)}, u32[]{:S(2)}, u32[]{:S(2)}) collective-permute-start(bf16[32,1024]{1,0:T(8,128)(2,1)S(1)} %get-tuple-element.30), channel_id=1, source_target_pairs={{0,4},{1,5},{2,6},{3,7},{4,0},{5,1},{6,2},{7,3},{8,12},{9,13},{10,... | collective-permute-start | bytes 196616 | tf_op jit(solution)/shard_map/ppermute | solution.py:406
  66.6 11.8 %collective-permute-start.5 = (bf16[32,1024]{1,0:T(8,128)(2,1)S(1)}, bf16[32,1024]{1,0:T(8,128)(2,1)S(1)}, u32[]{:S(2)}, u32[]{:S(2)}) collective-permute-start(bf16[32,1024]{1,0:T(8,128)(2,1)S(1)} %multiply_convert_fusion), channel_id=1, source_target_pairs={{0,12},{1,13},{2,14},{3,15},{4,8},{5,9},{6,10},{7,11},{8,4},{9,5},... | collective-permute-start | bytes 196616 | tf_op jit(solution)/shard_map/ppermute | solution.py:406
  67.5 10.9 %collective-permute-start.6 = (bf16[32,1024]{1,0:T(8,128)(2,1)S(1)}, bf16[32,1024]{1,0:T(8,128)(2,1)S(1)}, u32[]{:S(2)}, u32[]{:S(2)}) collective-permute-start(bf16[32,1024]{1,0:T(8,128)(2,1)S(1)} %multiply_convert_fusion), channel_id=1, source_target_pairs={{0,8},{1,9},{2,10},{3,11},{4,12},{5,13},{6,14},{7,15},{8,0},{9,1},... | collective-permute-start | bytes 196616 | tf_op jit(solution)/shard_map/ppermute | solution.py:406
  70.9 7.5 %collective-permute-start.7 = (bf16[32,1024]{1,0:T(8,128)(2,1)S(1)}, bf16[32,1024]{1,0:T(8,128)(2,1)S(1)}, u32[]{:S(2)}, u32[]{:S(2)}) collective-permute-start(bf16[32,1024]{1,0:T(8,128)(2,1)S(1)} %multiply_convert_fusion), channel_id=1, source_target_pairs={{0,4},{1,5},{2,6},{3,7},{4,0},{5,1},{6,2},{7,3},{8,12},{9,13},{10,... | collective-permute-start | bytes 196616 | tf_op jit(solution)/shard_map/ppermute | solution.py:406
  70.9 38.1 %all-to-all-start.1 = ((bf16[16,40,1024]{2,1,0:T(8,128)(2,1)}), bf16[16,40,1024]{2,1,0:T(8,128)(2,1)S(1)}, u32[]{:S(2)}, u32[]{:S(2)}) async-start(bf16[16,40,1024]{2,1,0:T(8,128)(2,1)} %pack.1), calls=%async_computation.1 | async-start | bytes 2621440 | tf_op jit(solution)/shard_map/all_to_all | solution.py:465
  78.5 13.9 %collective-permute-start.8 = (bf16[128,1024]{1,0:T(8,128)(2,1)S(1)}, bf16[128,1024]{1,0:T(8,128)(2,1)S(1)}, u32[]{:S(2)}, u32[]{:S(2)}) collective-permute-start(bf16[128,1024]{1,0:T(8,128)(2,1)S(1)} %pad_maximum_fusion.2), channel_id=1, source_target_pairs={{0,2},{1,3},{2,0},{3,1},{4,6},{5,7},{6,4},{7,5},{8,10},{9,11},{10,... | collective-permute-start | bytes 786440 | tf_op jit(solution)/shard_map/ppermute | solution.py:406
  92.6 4.2 %collective-permute-start.9 = (bf16[256,1024]{1,0:T(8,128)(2,1)S(1)}, bf16[256,1024]{1,0:T(8,128)(2,1)S(1)}, u32[]{:S(2)}, u32[]{:S(2)}) collective-permute-start(bf16[256,1024]{1,0:T(8,128)(2,1)S(1)} %pad_maximum_fusion.1), channel_id=1, source_target_pairs={{0,1},{1,0},{2,3},{3,2},{4,5},{5,4},{6,7},{7,6},{8,9},{9,8},{10,11... | collective-permute-start | bytes 1572872 | tf_op jit(solution)/shard_map/ppermute | solution.py:406
